TPU v7x, 32 devices: a whole 2x2x4 slice. The times are simulated.
32 devices in a mesh: groups: 2 (over y), owner: 16 (over z, x, core).
Axes of the slice: x: 2, y: 2, z: 4, core: 2. Of those that a mesh axis runs over, the one named last changes fastest.
Arguments:
- hidden: bfloat16 [4096, 8192], P(('groups', 'owner')), parts along dimension 0, may hold values from -6 to 6
- adapter_id: int32 [4096], P(('groups', 'owner')), parts along dimension 0, may hold values from 0 to 31, as said below
- adapter_slot: int32 [64], P('groups'), parts along dimension 0, may hold values from 0 to 31, as said below
- cache_len: int32 [4096], P(('groups', 'owner')), parts along dimension 0, may hold values from 2 to 16, as said below
- base_q: bfloat16 [4096, 4096], P(('groups', 'owner')), parts along dimension 0, may hold values from -6 to 6
- kv_cache: bfloat16 [4096, 2, 16, 512], P(('groups', 'owner')), parts along dimension 0, may hold values from -160 to 160
- a_maps: bfloat16 [8192, 2048], P(None, 'owner'), may hold values from -0.0625 to 0.0625
- b_maps: bfloat16 [2048, 4096], P('owner'), may hold values from -0.75 to 0.75
Outputs:
- attended: bfloat16 [4096, 4096], P(('groups', 'owner')), parts along dimension 0
There are 2 independent parts, one for each index of `groups`. A program takes and returns all parts, laid end to end along the dimension named above; an argument that names none is the same for every part. Nothing has to cross between parts.
Inputs may be any that keep to these rules, and one draw needn't show every extreme that they name: `adapter_id`: each replica's owners hold the slots in blocks of 2: owner o holds slots o * 2 to o * 2 + 1. Within the 128 rows of one device, at most 8 rows name adapters whose slots lie in one owner's block; in every draw some owner receives exactly 8 rows from every device. `adapter_slot`: A permutation of the slots. `cache_len`: each device's rows include one with 16 cached positions.
All inputs are finite; a program needn't handle non-finite values.
Results may differ from a plain program's by a relative error of at most 0.0071.
Values may be sent and summed in bfloat16 or wider, within the bound.
No kernel may reach another device: no remote copies, remote signals or barrier semaphores. Data moves between devices by JAX's collectives and lax.ppermute only.
A program may use at most 64 MiB of HBM per device.

v0:
```python
import jax
import jax.numpy as jnp
from jax import lax
from jax.sharding import PartitionSpec as P

HEAD = 128
KVH = 4
RANK = 64


SCALE = 2.0


def split_heads(query, kv_cache):
    rows = query.shape[0]
    context = kv_cache.shape[2]
    group = query.shape[1] // (KVH * HEAD)
    keys = kv_cache[:, 0].reshape(rows, context, KVH, HEAD)
    return (query.reshape(rows, KVH, group, HEAD), keys)


def head_scores(query, kv_cache):
    query_heads, keys = split_heads(query, kv_cache)
    return jnp.einsum("rkgd,rtkd->rkgt", query_heads, keys, preferred_element_type=jnp.float32)


def finish_rows(scores, kv_cache, cache_len, width):
    rows = kv_cache.shape[0]
    context = kv_cache.shape[2]
    values = kv_cache[:, 1].reshape(rows, context, KVH, HEAD)
    scores = scores * (1.0 / jnp.sqrt(jnp.float32(HEAD)))
    live = (
        jnp.arange(context, dtype=jnp.int32)[None, None, None, :] < cache_len[:, None, None, None]
    )
    scores = jnp.where(live, scores, -jnp.inf)
    top = jnp.max(scores, axis=-1, keepdims=True)
    expo = jnp.where(live, jnp.exp(scores - top), 0.0)
    probs = (expo / jnp.sum(expo, axis=-1, keepdims=True)).astype(jnp.bfloat16)
    out = jnp.einsum("rkgt,rtkd->rkgd", probs, values, preferred_element_type=jnp.float32)
    return out.reshape(rows, width).astype(jnp.bfloat16)


def on_device(hidden, adapter_id, adapter_slot, cache_len, base_q, kv_cache, a_maps, b_maps):
    owners = lax.axis_size("owner")
    rows, width = hidden.shape
    held = a_maps.shape[1] // RANK
    slot_count = max(2, 2 * ((rows + 2 * owners - 1) // (2 * owners)))
    bins = owners * slot_count
    every_slot = jnp.arange(adapter_slot.shape[0], dtype=jnp.int32)
    slot = jnp.sum(
        jnp.where(adapter_id[:, None] == every_slot[None, :], adapter_slot[None, :], 0), axis=1
    )
    owner_of = slot // held
    local = slot % held
    owner_hits = (owner_of[:, None] == jnp.arange(owners, dtype=jnp.int32)[None, :]).astype(
        jnp.int32
    )
    before = jnp.cumsum(owner_hits, axis=0) - owner_hits
    place = jnp.sum(before * owner_hits, axis=1)
    flat_bin = owner_of * slot_count + place
    routed = flat_bin[:, None] == jnp.arange(bins, dtype=jnp.int32)[None, :]
    routed_mat = routed.astype(jnp.bfloat16)
    packed = lax.dot_general(
        routed_mat, hidden, (((0,), (0,)), ((), ())), preferred_element_type=jnp.float32
    )
    packed = packed.astype(jnp.bfloat16).reshape(owners, slot_count, width)
    labels = jnp.sum(jnp.where(routed, local[:, None] + 1, 0), axis=0) - 1
    labels = labels.reshape(owners, slot_count)
    column_owner = jnp.arange(a_maps.shape[1], dtype=jnp.int32) // RANK
    arrived = lax.all_to_all(packed, "owner", split_axis=0, concat_axis=0, tiled=True)
    arrived_labels = lax.all_to_all(labels, "owner", split_axis=0, concat_axis=0, tiled=True)
    count = arrived.shape[1]
    flat_rows = arrived.reshape(owners * count, width)
    low = jnp.dot(flat_rows, a_maps, preferred_element_type=jnp.float32)
    keep = column_owner[None, :] == arrived_labels.reshape(owners * count)[:, None]
    low = jnp.where(keep, low, 0.0).astype(jnp.bfloat16)
    change = (SCALE * jnp.dot(low, b_maps, preferred_element_type=jnp.float32)).astype(jnp.bfloat16)
    change = change.reshape(owners, count, b_maps.shape[1])
    returned = lax.all_to_all(change, "owner", split_axis=0, concat_axis=0, tiled=True)
    returned = returned.reshape(bins, b_maps.shape[1])
    delta = jnp.dot(routed_mat, returned, preferred_element_type=jnp.float32).astype(jnp.bfloat16)
    scores = head_scores(base_q, kv_cache) + head_scores(delta, kv_cache)
    return finish_rows(scores, kv_cache, cache_len, base_q.shape[1])


def solution(mesh):
    return jax.shard_map(
        on_device,
        mesh=mesh,
        in_specs=(
            P(("groups", "owner"), None),
            P(("groups", "owner")),
            P("groups"),
            P(("groups", "owner")),
            P(("groups", "owner"), None),
            P(("groups", "owner"), None, None, None),
            P(None, "owner"),
            P("owner", None),
        ),
        out_specs=P(("groups", "owner"), None),
        check_vma=False,
    )
```

profile of v0, /device:TPU:0, one launch (start us, length us, event | category | flops | bytes accessed | tf_op | source)
XLA Modules:
  0.0 117.0 jit_solution(15113428999064336963)
XLA Ops:
  0.0 0.0 copy-start
  0.0 0.9 select_reduce_fusion.2
  0.9 0.1 fusion.17
  1.0 0.2 reduce_window_sum.11
  1.2 0.2 select_reduce_fusion.1
  1.4 0.1 select_reduce_fusion
  1.5 0.7 sub.31
  2.2 7.4 %all-to-all-start = ((s32[16,1,8]{2,1,0:T(1,128)}), s32[16,1,8]{2,1,0:T(1,128)S(1)}, u32[]{:S(2)}, u32[]{:S(2)}) async-start(s32[16,1,8]{2,1,0:T(1,128)} %bitcast.1), calls=%async_computation | async-start | bytes 16384 | tf_op jit(solution)/shard_map/all_to_all | solution.py:71
  9.6 0.0 copy-done
  9.6 2.1 %fusion.1 = bf16[16,8,8192]{2,1,0:T(8,128)(2,1)} fusion(bf16[128,8192]{1,0:T(8,128)(2,1)S(1)} %copy-done, s32[128]{0:T(128)S(1)} %multiply_add_fusion), kind=kOutput, calls=%fused_computation.2 | convolution fusion | flops 269500416 | bytes 4194816 | tf_op jit(solution)/shard_map/dot_general | solution.py:63
  11.7 0.0 copy-start.1
  11.7 4.2 %all-to-all-done = s32[16,1,8]{2,1,0:T(1,128)S(1)} async-done(((s32[16,1,8]{2,1,0:T(1,128)}), s32[16,1,8]{2,1,0:T(1,128)S(1)}, u32[]{:S(2)}, u32[]{:S(2)}) %all-to-all-start) | async-done | bytes 544 | tf_op jit(solution)/shard_map/all_to_all | solution.py:71
  15.9 4.4 %all-to-all-start.1 = ((bf16[16,8,8192]{2,1,0:T(8,128)(2,1)}), bf16[16,8,8192]{2,1,0:T(8,128)(2,1)}, u32[]{:S(2)}, u32[]{:S(2)}) async-start(bf16[16,8,8192]{2,1,0:T(8,128)(2,1)} %fusion.1), calls=%async_computation.1 | async-start | bytes 4194304 | tf_op jit(solution)/shard_map/all_to_all | solution.py:70
  20.3 0.5 broadcast.168
  20.9 0.7 reduce.3
  21.5 0.1 eq.66
  21.6 39.8 %all-to-all-done.1 = bf16[16,8,8192]{2,1,0:T(8,128)(2,1)} async-done(((bf16[16,8,8192]{2,1,0:T(8,128)(2,1)}), bf16[16,8,8192]{2,1,0:T(8,128)(2,1)}, u32[]{:S(2)}, u32[]{:S(2)}) %all-to-all-start.1) | async-done | bytes 2097184 | tf_op jit(solution)/shard_map/all_to_all | solution.py:70
  61.4 0.0 copy-done.1
  61.4 4.3 %fusion.3 = bf16[16,8,4096]{2,1,0:T(8,128)(2,1)} fusion(bf16[128,4096]{1,0:T(8,128)(2,1)S(1)} %copy-done.1, bf16[8192,128]{1,0:T(8,128)(2,1)} %param.14, bf16[16,8,8192]{2,1,0:T(8,128)(2,1)} %all-to-all-done.1, s32[128]{0:T(128)S(1)} %and_select_fusion.1, s32[128]{0:T(128)S(1)} %eq.66), kind=kOutput, calls=%fused_computation.6 | convolution fusion | flops 403750912 | bytes 6292480 | tf_op jit(solution)/shard_map/dot_general | solution.py:77
  65.7 11.2 %all-to-all-start.2 = ((bf16[16,8,4096]{2,1,0:T(8,128)(2,1)}), bf16[16,8,4096]{2,1,0:T(8,128)(2,1)}, u32[]{:S(2)}, u32[]{:S(2)}) async-start(bf16[16,8,4096]{2,1,0:T(8,128)(2,1)} %fusion.3), calls=%async_computation.2 | async-start | bytes 2097152 | tf_op jit(solution)/shard_map/all_to_all | solution.py:79
  76.9 1.4 %copy.28 = bf16[16,8,32,128]{3,2,1,0:T(8,128)(2,1)S(1)} copy(bf16[16,8,32,128]{3,1,2,0:T(8,128)(2,1)} %bitcast.43) | data formatting | bytes 2097152
  78.4 4.6 %fusion.26 = (bf16[128,1,16,512]{3,2,1,0:T(8,128)(2,1)}, bf16[128,1,16,512]{3,2,1,0:T(8,128)(2,1)}) fusion(bf16[128,2,16,512]{3,2,1,0:T(8,128)(2,1)} %param.13), kind=kLoop, calls=%fused_computation.46 | loop fusion | bytes 8388608 | tf_op jit(solution)/shard_map/slice | solution.py:18
  83.0 4.6 %copy.26 = bf16[128,1,16,512]{0,3,2,1:T(8,128)(2,1)} copy(bf16[128,1,16,512]{3,2,1,0:T(8,128)(2,1)} %get-tuple-element.5) | data formatting | bytes 4194304
  87.6 4.6 %copy.21 = bf16[128,16,4,128]{3,1,2,0:T(8,128)(2,1)} copy(bf16[128,16,4,128]{0,3,2,1:T(8,128)(2,1)} %bitcast.39) | data formatting | bytes 4194304 | tf_op jit(solution)/shard_map/reshape;squeeze | solution.py:18
  92.2 4.6 %copy.27 = bf16[128,1,16,512]{0,3,2,1:T(8,128)(2,1)} copy(bf16[128,1,16,512]{3,2,1,0:T(8,128)(2,1)} %get-tuple-element.6) | data formatting | bytes 4194304
  96.8 0.0 copy-start.2
  96.8 4.6 %copy.25 = bf16[128,16,4,128]{3,1,2,0:T(8,128)(2,1)} copy(bf16[128,16,4,128]{0,3,2,1:T(8,128)(2,1)} %bitcast.40) | data formatting | bytes 4194304 | tf_op jit(solution)/shard_map/reshape;squeeze | solution.py:30
  101.4 0.0 copy-done.2
  101.4 0.1 iota_compare_fusion.4
  101.4 4.1 %fusion.28 = f32[128,4,8,16]{3,2,1,0:T(8,128)} fusion(bf16[128,4,8,128]{3,2,1,0:T(8,128)(2,1)S(1)} %bitcast.41, bf16[128,16,4,128]{3,1,2,0:T(8,128)(2,1)} %copy.21), kind=kOutput, calls=%fused_computation.48 | convolution fusion | flops 16777216 | bytes 3407872 | tf_op jit(solution)/shard_map/rkgd,rtkd->rkgt/dot_general | solution.py:24
  105.6 0.0 all-to-all-done.2
  105.6 1.7 %fusion.6 = bf16[16,8,32,128]{3,1,2,0:T(8,128)(2,1)S(1)} fusion(bf16[16,8,4096]{2,1,0:T(8,128)(2,1)} %all-to-all-done.2, s32[128]{0:T(128)S(1)} %multiply_add_fusion), kind=kOutput, calls=%fused_computation.13 | convolution fusion | flops 134758400 | bytes 2097664 | tf_op jit(solution)/shard_map/dot_general | solution.py:81
  107.3 0.2 copy.29
  107.5 4.9 %fusion.27 = (f32[128,4,8]{2,1,0:T(4,128)S(1)}, f32[128,4,8,16]{3,2,1,0:T(8,128)}) fusion(pred[128,16]{1,0:T(8,128)(4,1)S(1)} %iota_compare_fusion.4, f32[128,4,8,16]{3,2,1,0:T(8,128)} %fusion.28, bf16[128,4,8,128]{3,2,1,0:T(8,128)(2,1)S(1)} %bitcast.42, bf16[128,16,4,128]{3,1,2,0:T(8,128)(2,1)} %copy.21), kind=kOutput, calls=%fused_computation.47 | convolution fusion | flops 17170448 | bytes 3688448 | tf_op jit(solution)/shard_map/sub | solution.py:37
  112.5 3.1 %convolution_convert_fusion.2 = bf16[128,4,8,128]{3,2,1,0:T(8,128)(2,1)S(1)} fusion(bf16[128,16,4,128]{3,1,2,0:T(8,128)(2,1)} %copy.25, f32[128,4,8,16]{3,2,1,0:T(8,128)} %get-tuple-element.10, f32[128,4,8]{2,1,0:T(4,128)S(1)} %get-tuple-element.9), kind=kOutput, calls=%fused_computation.12 | convolution fusion | flops 17432576 | bytes 3424256 | tf_op jit(solution)/shard_map/rkgt,rtkd->rkgd/dot_general | solution.py:39
  115.6 1.4 %copy.32 = bf16[16,8,32,128]{3,1,2,0:T(8,128)(2,1)} copy(bf16[16,8,32,128]{3,2,1,0:T(8,128)(2,1)S(1)} %bitcast.44) | data formatting | bytes 2097152
  (4 shorter events, 0.0 us)
Async XLA Ops:
  0.0 9.6 %copy-start = (bf16[128,8192]{1,0:T(8,128)(2,1)S(1)}, bf16[128,8192]{1,0:T(8,128)(2,1)}, u32[]{:S(2)}) copy-start(bf16[128,8192]{1,0:T(8,128)(2,1)} %param.8) | copy-start | bytes 6291460
  2.2 13.7 %all-to-all-start = ((s32[16,1,8]{2,1,0:T(1,128)}), s32[16,1,8]{2,1,0:T(1,128)S(1)}, u32[]{:S(2)}, u32[]{:S(2)}) async-start(s32[16,1,8]{2,1,0:T(1,128)} %bitcast.1), calls=%async_computation | async-start | bytes 16384 | tf_op jit(solution)/shard_map/all_to_all | solution.py:71
  11.7 49.7 %copy-start.1 = (bf16[128,4096]{1,0:T(8,128)(2,1)S(1)}, bf16[128,4096]{1,0:T(8,128)(2,1)}, u32[]{:S(2)}) copy-start(bf16[128,4096]{1,0:T(8,128)(2,1)} %param.15) | copy-start | bytes 3145732
  15.9 45.5 %all-to-all-start.1 = ((bf16[16,8,8192]{2,1,0:T(8,128)(2,1)}), bf16[16,8,8192]{2,1,0:T(8,128)(2,1)}, u32[]{:S(2)}, u32[]{:S(2)}) async-start(bf16[16,8,8192]{2,1,0:T(8,128)(2,1)} %fusion.1), calls=%async_computation.1 | async-start | bytes 4194304 | tf_op jit(solution)/shard_map/all_to_all | solution.py:70
  65.7 39.9 %all-to-all-start.2 = ((bf16[16,8,4096]{2,1,0:T(8,128)(2,1)}), bf16[16,8,4096]{2,1,0:T(8,128)(2,1)}, u32[]{:S(2)}, u32[]{:S(2)}) async-start(bf16[16,8,4096]{2,1,0:T(8,128)(2,1)} %fusion.3), calls=%async_computation.2 | async-start | bytes 2097152 | tf_op jit(solution)/shard_map/all_to_all | solution.py:79
  96.8 4.6 %copy-start.2 = (s32[128]{0:T(128)S(1)}, s32[128]{0:T(128)}, u32[]{:S(2)}) copy-start(s32[128]{0:T(128)} %param.11) | copy-start | bytes 1540
where the time goes:
time: 118 us; the launch traced here: 117 us
  waiting for transfers between devices  44 us (37%)
  local copies, waits for them, and re-layouts  27.4 us (23%)
  starting transfers between devices  23 us (19%)
  matrix products  20.2 us (17%)
  other arithmetic  2.24 us (2%)
    all_to_all x1, waiting for transfers between devices, on_device(): lax.all_to_all(packed, 'owner', split_axis=0, concat_axis=0, tiled=True)  39.8 us
    unnamed x11, local copies, waits for them, and re-layouts  12.2 us
    all_to_all x1, starting transfers between devices, on_device(): lax.all_to_all(change, 'owner', split_axis=0, concat_axis=0, tiled=True)  11.2 us
    all_to_all x1, starting transfers between devices, on_device(): lax.all_to_all(labels, 'owner', split_axis=0, concat_axis=0, tiled=True)  7.36 us
    sub x1, matrix products, finish_rows(): expo = jnp.where(live, jnp.exp(scores - top), 0.0)  4.95 us
    another operation x1, local copies, waits for them, and re-layouts, split_heads(): keys = kv_cache[:, 0].reshape(rows, context, KVH, HEAD)  4.64 us
    slice x1, local copies, waits for them, and re-layouts, split_heads(): keys = kv_cache[:, 0].reshape(rows, context, KVH, HEAD)  4.62 us
    another operation x1, local copies, waits for them, and re-layouts, finish_rows(): values = kv_cache[:, 1].reshape(rows, context, KVH, HEAD)  4.58 us
  transfers between devices with their start and end apart: 3, of which 2 were waited for; matrix products, arithmetic and copies ran while one was open for 27% of the time, Pallas kernels for 0%

commit v1 on v0

v1 whole, which is shorter than its diff:
```python
import functools

import jax
import jax.numpy as jnp
from jax import lax
from jax.experimental import pallas as pl
from jax.experimental.pallas import tpu as pltpu
from jax.sharding import PartitionSpec as P

HEAD = 128
KVH = 4
RANK = 64
LANES = 128
SCALE = 2.0
ROWS_STEP = 16


def routing(owners, slot_count, held, slots_ref, ids_ref):
    ids = ids_ref[...]
    rows = ids.shape[1]

    def look(s, slot):
        return jnp.where(ids == s, slots_ref[s], slot)

    slot = lax.fori_loop(0, slots_ref.shape[0], look, jnp.zeros_like(ids), unroll=8)
    owner = lax.div(slot, held)
    local = slot - owner * held
    hits = owner == lax.broadcasted_iota(jnp.int32, (owners, rows), 0)
    earlier = lax.broadcasted_iota(jnp.int32, (rows, rows), 0) < lax.broadcasted_iota(
        jnp.int32, (rows, rows), 1
    )
    before = jnp.dot(
        hits.astype(jnp.bfloat16), earlier.astype(jnp.bfloat16), preferred_element_type=jnp.float32
    )
    place = jnp.sum(jnp.where(hits, before, 0.0), axis=0, keepdims=True).astype(jnp.int32)
    bins = owner * slot_count + place
    routed = bins == lax.broadcasted_iota(jnp.int32, (owners * slot_count, rows), 0)
    label = jnp.sum(jnp.where(routed, local.astype(jnp.float32), 0.0), axis=1, keepdims=True)
    return routed.astype(jnp.bfloat16), label


def pack_kernel(owners, slot_count, held, slots_ref, ids_ref, hidden_ref, packed_ref, routed_ref, label_ref):
    step = pl.program_id(0)

    @pl.when(step == 0)
    def _():
        routed, label = routing(owners, slot_count, held, slots_ref, ids_ref)
        routed_ref[...] = routed
        label_ref[...] = jnp.broadcast_to(label, label_ref.shape)

    packed_ref[...] = jnp.dot(
        routed_ref[...], hidden_ref[...], preferred_element_type=jnp.float32
    ).astype(packed_ref.dtype)

    @pl.when(step == pl.num_programs(0) - 1)
    def _():
        packed_ref[:, packed_ref.shape[1] - LANES :] = label_ref[...].astype(packed_ref.dtype)


def pack(hidden, adapter_id, adapter_slot, owners, slot_count, held):
    rows, width = hidden.shape
    bins = owners * slot_count
    total = width + LANES
    steps = next(n for n in range(4, total // LANES + 1) if total % (n * LANES) == 0)
    block = total // steps
    return pl.pallas_call(
        functools.partial(pack_kernel, owners, slot_count, held),
        grid=(steps,),
        in_specs=[
            pl.BlockSpec(memory_space=pltpu.SMEM),
            pl.BlockSpec((1, rows), lambda i: (0, 0)),
            pl.BlockSpec((rows, block), lambda i: (0, i)),
        ],
        out_specs=[
            pl.BlockSpec((bins, block), lambda i: (0, i)),
            pl.BlockSpec((bins, rows), lambda i: (0, 0)),
        ],
        out_shape=[
            jax.ShapeDtypeStruct((bins, total), hidden.dtype),
            jax.ShapeDtypeStruct((bins, rows), jnp.bfloat16),
        ],
        scratch_shapes=[pltpu.VMEM((bins, LANES), jnp.float32)],
        compiler_params=pltpu.CompilerParams(vmem_limit_bytes=16 * 2**20),
        name="pack",
    )(adapter_slot, adapter_id.reshape(1, rows), hidden)


def adapt_kernel(chunk, arrived_ref, a_ref, b_ref, change_ref, held_ref, sems):
    width = a_ref.shape[0]
    spans = [(c, min(chunk, width + LANES - c)) for c in range(0, width + LANES, chunk)]
    copies = [
        pltpu.make_async_copy(
            arrived_ref.at[:, pl.ds(at, size)], held_ref.at[:, pl.ds(at, size)], sems.at[i]
        )
        for i, (at, size) in enumerate(spans)
    ]
    for copy in copies:
        copy.start()
    low = jnp.zeros((arrived_ref.shape[0], a_ref.shape[1]), jnp.float32)
    for copy, (at, size) in zip(copies, spans):
        copy.wait()
        size = min(size, width - at)
        if size > 0:
            low += jnp.dot(
                held_ref[:, at : at + size],
                a_ref[at : at + size, :],
                preferred_element_type=jnp.float32,
            )
    label = held_ref[:, width:].astype(jnp.float32)[:, :1].astype(jnp.int32)
    column = lax.broadcasted_iota(jnp.int32, low.shape, 1) // RANK
    low = jnp.where(column == label, low, 0.0).astype(jnp.bfloat16)
    out_width = b_ref.shape[1]
    piece = min(1024, out_width)
    for at in range(0, out_width, piece):
        change_ref[:, at : at + piece] = (
            SCALE
            * jnp.dot(low, b_ref[:, at : at + piece], preferred_element_type=jnp.float32)
        ).astype(change_ref.dtype)


def adapt(arrived, a_maps, b_maps):
    bins = arrived.shape[0]
    chunk = 2048
    chunks = -(-arrived.shape[1] // chunk)
    return pl.pallas_call(
        functools.partial(adapt_kernel, chunk),
        in_specs=[
            pl.BlockSpec(memory_space=pl.ANY),
            pl.BlockSpec(memory_space=pltpu.VMEM),
            pl.BlockSpec(memory_space=pltpu.VMEM),
        ],
        out_specs=pl.BlockSpec(memory_space=pltpu.VMEM),
        out_shape=jax.ShapeDtypeStruct((bins, b_maps.shape[1]), jnp.bfloat16),
        scratch_shapes=[
            pltpu.VMEM(arrived.shape, arrived.dtype),
            pltpu.SemaphoreType.DMA((chunks,)),
        ],
        compiler_params=pltpu.CompilerParams(vmem_limit_bytes=24 * 2**20),
        name="adapt",
    )(arrived, a_maps, b_maps)


def attend_kernel(context, routed_ref, returned_ref, base_ref, kv_ref, len_ref, out_ref, delta_ref):
    rows, width = base_ref.shape
    group = width // (KVH * HEAD)
    span = group * HEAD
    step = ROWS_STEP
    cells = step * context
    for k in range(KVH):
        delta_ref[:, k * span : (k + 1) * span] = lax.dot_general(
            routed_ref[...],
            returned_ref[:, k * span : (k + 1) * span],
            (((0,), (0,)), ((), ())),
            preferred_element_type=jnp.float32,
        ).astype(delta_ref.dtype)
    lane = lax.broadcasted_iota(jnp.int32, (group * step, cells), 1)
    line = lax.broadcasted_iota(jnp.int32, (group * step, cells), 0)
    own = lane // context == lax.rem(line, step)
    position = lax.rem(lane, context)
    factor = 1.0 / jnp.sqrt(jnp.float32(HEAD))

    def tall(ref, at, k):
        return jnp.concatenate(
            [
                ref[pl.ds(at, step), (k * group + g) * HEAD : (k * group + g + 1) * HEAD]
                for g in range(group)
            ],
            axis=0,
        )

    def rows_step(i, carry):
        at = pl.multiple_of(i * step, step)
        live = own & (position < len_ref[pl.ds(i, 1), :])
        for k in range(KVH):
            keys = kv_ref[pl.ds(at, step), 0, :, k * HEAD : (k + 1) * HEAD].reshape(cells, HEAD)
            values = kv_ref[pl.ds(at, step), 1, :, k * HEAD : (k + 1) * HEAD].reshape(cells, HEAD)
            query = jnp.concatenate([tall(base_ref, at, k), tall(delta_ref, at, k)], axis=1)
            scores = lax.dot_general(
                query,
                jnp.concatenate([keys, keys], axis=1),
                (((1,), (1,)), ((), ())),
                preferred_element_type=jnp.float32,
            )
            scores = jnp.where(live, scores * factor, -jnp.inf)
            expo = jnp.exp(scores - jnp.max(scores, axis=1, keepdims=True))
            probs = (expo * (1.0 / jnp.sum(expo, axis=1, keepdims=True))).astype(jnp.bfloat16)
            out = jnp.dot(probs, values, preferred_element_type=jnp.float32).astype(out_ref.dtype)
            for g in range(group):
                out_ref[
                    pl.ds(at, step), (k * group + g) * HEAD : (k * group + g + 1) * HEAD
                ] = out[g * step : (g + 1) * step, :]
        return carry

    lax.fori_loop(0, rows // step, rows_step, 0)


def attend(routed, returned, base_q, kv_cache, cache_len):
    rows = base_q.shape[0]
    context = kv_cache.shape[2]
    lens = jnp.repeat(cache_len, context).reshape(rows // ROWS_STEP, ROWS_STEP * context)
    return pl.pallas_call(
        functools.partial(attend_kernel, context),
        in_specs=[pl.BlockSpec(memory_space=pltpu.VMEM)] * 5,
        out_specs=pl.BlockSpec(memory_space=pltpu.VMEM),
        out_shape=jax.ShapeDtypeStruct(base_q.shape, jnp.bfloat16),
        scratch_shapes=[pltpu.VMEM(base_q.shape, jnp.bfloat16)],
        compiler_params=pltpu.CompilerParams(vmem_limit_bytes=24 * 2**20),
        name="attend",
    )(routed, returned, base_q, kv_cache, lens)


def on_device(hidden, adapter_id, adapter_slot, cache_len, base_q, kv_cache, a_maps, b_maps):
    owners = lax.axis_size("owner")
    rows = hidden.shape[0]
    held = a_maps.shape[1] // RANK
    slot_count = max(2, 2 * ((rows + 2 * owners - 1) // (2 * owners)))
    bins = owners * slot_count
    packed, routed = pack(hidden, adapter_id, adapter_slot, owners, slot_count, held)
    packed = packed.reshape(owners, slot_count, packed.shape[1])
    arrived = lax.all_to_all(packed, "owner", split_axis=0, concat_axis=0, tiled=True)
    change = adapt(arrived.reshape(bins, arrived.shape[2]), a_maps, b_maps)
    change = change.reshape(owners, slot_count, change.shape[1])
    returned = lax.all_to_all(change, "owner", split_axis=0, concat_axis=0, tiled=True)
    return attend(routed, returned.reshape(bins, returned.shape[2]), base_q, kv_cache, cache_len)


def solution(mesh):
    return jax.shard_map(
        on_device,
        mesh=mesh,
        in_specs=(
            P(("groups", "owner"), None),
            P(("groups", "owner")),
            P("groups"),
            P(("groups", "owner")),
            P(("groups", "owner"), None),
            P(("groups", "owner"), None, None, None),
            P(None, "owner"),
            P("owner", None),
        ),
        out_specs=P(("groups", "owner"), None),
        check_vma=False,
    )
```

time: 118 us -> 109 us (0.924)
  blocking collectives: 0 us -> 57.9 us
  local copies, waits for them, and re-layouts: 27.4 us -> 5.36 us
  waiting for transfers between devices: 44 us -> 22.6 us
  matrix products: 20.2 us -> 0 us
  starting transfers between devices: 23 us -> 3.8 us
  Pallas kernels: 0 us -> 17.7 us
  other arithmetic: 2.24 us -> 0 us
    all_to_all x0 -> x1, blocking collectives: none -> 57.9 us  [on_device(): lax.all_to_all(packed, 'owner', split_axis=0, concat_axis=0, tiled=True)]
    all_to_all x2 -> x0, waiting for transfers between devices: 44 us -> none  [the longest x1 39.8 us: on_device(): lax.all_to_all(packed, 'owner', split_axis=0, concat_axis=0, tiled=True)]
    all_to_all x1, waiting for transfers between devices: 0.01 us -> 22.6 us  [on_device(): lax.all_to_all(change, 'owner', split_axis=0, concat_axis=0, tiled=True)]
    pallas_call x0 -> x3, Pallas kernels: none -> 17.7 us  [the longest x1 12.3 us: attend(): pl.pallas_call(functools.partial(attend_kernel, context), in_specs=[pl.Bl...]
    dot_general x5 -> x0, matrix products: 15.3 us -> none  [the longest x1 4.26 us: on_device(): jnp.dot(low, b_maps, preferred_element_type=jnp.float32)]
    all_to_all x2 -> x0, starting transfers between devices: 11.8 us -> none  [the longest x1 7.36 us: on_device(): lax.all_to_all(labels, 'owner', split_axis=0, concat_axis=0, tiled=True)]
    another operation x2 -> x0, local copies, waits for them, and re-layouts: 9.21 us -> none  [the longest x1 4.64 us: split_heads(): keys = kv_cache[:, 0].reshape(rows, context, KVH, HEAD)]
    all_to_all x1, starting transfers between devices: 11.2 us -> 3.8 us  [on_device(): lax.all_to_all(change, 'owner', split_axis=0, concat_axis=0, tiled=True)]
  transfers between devices with their start and end apart: 3 -> 1, of which waited for: 2 -> 1; matrix products, arithmetic and copies ran while one was open for 27% -> 0% of each run, Pallas kernels for 0% -> 0%
where the time goes in v1:
time: 109 us; the launch traced here: 107 us
  blocking collectives  57.9 us (53%)
  waiting for transfers between devices  22.6 us (21%)
  Pallas kernels  17.7 us (16%)
  local copies, waits for them, and re-layouts  5.36 us (5%)
  starting transfers between devices  3.8 us (3%)
    all_to_all x1, blocking collectives, on_device(): lax.all_to_all(packed, 'owner', split_axis=0, concat_axis=0, tiled=True)  57.9 us
    all_to_all x1, waiting for transfers between devices, on_device(): lax.all_to_all(change, 'owner', split_axis=0, concat_axis=0, tiled=True)  22.6 us
    pallas_call x1, Pallas kernels, attend(): pl.pallas_call(functools.partial(attend_kernel, context), in_specs=[pl.Bl...  12.3 us
    unnamed x16, local copies, waits for them, and re-layouts  5.11 us
    all_to_all x1, starting transfers between devices, on_device(): lax.all_to_all(change, 'owner', split_axis=0, concat_axis=0, tiled=True)  3.8 us
    pallas_call x1, Pallas kernels, adapt(): pl.pallas_call(functools.partial(adapt_kernel, chunk), in_specs=[pl.Block...  2.75 us
    pallas_call x1, Pallas kernels, pack(): pl.pallas_call(functools.partial(pack_kernel, owners, slot_count, held),...  2.65 us
  transfers between devices with their start and end apart: 1, of which 1 were waited for; matrix products, arithmetic and copies ran while one was open for 0% of the time, Pallas kernels for 0%

profile of v1, /device:TPU:0, one launch (start us, length us, event | category | flops | bytes accessed | tf_op | source)
XLA Modules:
  0.0 107.4 jit_solution(15476295858924119039)
XLA Ops:
  0.0 0.0 copy-start.2
  0.0 1.6 %copy-done.2 = bf16[128,8192]{1,0:T(8,128)(2,1)S(1)} copy-done((bf16[128,8192]{1,0:T(8,128)(2,1)S(1)}, bf16[128,8192]{1,0:T(8,128)(2,1)}, u32[]{:S(2)}) %copy-start.2) | copy-done | bytes 2097176
  1.6 0.0 copy-start.5
  1.6 0.7 copy-done.5
  2.2 0.0 copy-start.6
  2.2 0.7 copy-done.6
  2.9 2.7 %pack.1 = (bf16[128,8320]{1,0:T(8,128)(2,1)S(1)}, bf16[128,128]{1,0:T(8,128)(2,1)S(1)}) custom-call(s32[32]{0:T(128)S(1)} %copy-done.5, s32[1,128]{1,0:T(1,128)S(1)} %bitcast.8, bf16[128,8192]{1,0:T(8,128)(2,1)S(1)} %copy-done.2), custom_call_target="tpu_custom_call" | custom-call | tf_op jit(solution)/shard_map/pack/pallas_call | solution.py:66
  5.6 0.0 copy-start.1
  5.6 0.0 copy-start.3
  5.6 57.9 %all_to_all.10 = bf16[16,8,8320]{2,1,0:T(8,128)(2,1)S(1)} all-to-all(bf16[16,8,8320]{2,1,0:T(8,128)(2,1)S(1)} %bitcast.7), channel_id=1, replica_groups=mesh['groups'=2,'owner'=16] {'owner'}, dimensions={0} | all-to-all | bytes 4259840 | tf_op jit(solution)/shard_map/all_to_all | solution.py:220
  63.5 0.0 copy-done.1
  63.5 0.0 copy-done.3
  63.5 0.0 copy-start.7
  63.5 2.7 %adapt.1 = bf16[128,4096]{1,0:T(8,128)(2,1)} custom-call(bf16[128,8320]{1,0:T(8,128)(2,1)S(1)} %bitcast.5, bf16[8192,128]{1,0:T(8,128)(2,1)S(1)} %copy-done.1, bf16[128,4096]{1,0:T(8,128)(2,1)S(1)} %copy-done.3), custom_call_target="tpu_custom_call" | custom-call | tf_op jit(solution)/shard_map/adapt/pallas_call | solution.py:125
  66.2 0.0 copy-start.4
  66.2 3.8 %all-to-all-start.1 = ((bf16[16,8,4096]{2,1,0:T(8,128)(2,1)}), bf16[16,8,4096]{2,1,0:T(8,128)(2,1)S(1)}, u32[]{:S(2)}, u32[]{:S(2)}) async-start(bf16[16,8,4096]{2,1,0:T(8,128)(2,1)} %bitcast.3), calls=%async_computation.1 | async-start | bytes 2097152 | tf_op jit(solution)/shard_map/all_to_all | solution.py:223
  70.0 0.0 copy-done.7
  70.0 0.1 broadcast_in_dim.7
  70.1 0.1 broadcast_in_dim.8
  70.2 0.1 broadcast_in_dim.9.len_ref
  70.3 22.6 %all-to-all-done.1 = bf16[16,8,4096]{2,1,0:T(8,128)(2,1)S(1)} async-done(((bf16[16,8,4096]{2,1,0:T(8,128)(2,1)}), bf16[16,8,4096]{2,1,0:T(8,128)(2,1)S(1)}, u32[]{:S(2)}, u32[]{:S(2)}) %all-to-all-start.1) | async-done | bytes 1048608 | tf_op jit(solution)/shard_map/all_to_all | solution.py:223
  92.9 0.0 copy-done.4
  92.9 0.0 copy-start
  92.9 2.2 %copy-done = bf16[128,2,16,512]{3,2,1,0:T(8,128)(2,1)S(1)} copy-done((bf16[128,2,16,512]{3,2,1,0:T(8,128)(2,1)S(1)}, bf16[128,2,16,512]{3,2,1,0:T(8,128)(2,1)}, u32[]{:S(2)}) %copy-start) | copy-done | bytes 4194328
  95.1 12.3 %attend.1 = bf16[128,4096]{1,0:T(8,128)(2,1)} custom-call(bf16[128,128]{1,0:T(8,128)(2,1)S(1)} %get-tuple-element.7.routed_ref, bf16[128,4096]{1,0:T(8,128)(2,1)S(1)} %bitcast.6, bf16[128,4096]{1,0:T(8,128)(2,1)S(1)} %copy-done.4, bf16[128,2,16,512]{3,2,1,0:T(8,128)(2,1)S(1)} %copy-done, s32[8,256]{1,0:T(8,128)S(1)} %broadcast_in_dim.9.len_ref), custom_call_target="tpu_custom_call" | custom-call | tf_op jit(solution)/shard_map/attend/pallas_call | solution.py:201
Async XLA Ops:
  0.0 1.6 %copy-start.2 = (bf16[128,8192]{1,0:T(8,128)(2,1)S(1)}, bf16[128,8192]{1,0:T(8,128)(2,1)}, u32[]{:S(2)}) copy-start(bf16[128,8192]{1,0:T(8,128)(2,1)} %hidden_ref.1) | copy-start | bytes 6291460
  1.6 0.7 copy-start.5
  2.2 0.7 copy-start.6
  5.6 57.9 %copy-start.1 = (bf16[8192,128]{1,0:T(8,128)(2,1)S(1)}, bf16[8192,128]{1,0:T(8,128)(2,1)}, u32[]{:S(2)}) copy-start(bf16[8192,128]{1,0:T(8,128)(2,1)} %a_ref.1) | copy-start | bytes 6291460
  5.6 57.9 %copy-start.3 = (bf16[128,4096]{1,0:T(8,128)(2,1)S(1)}, bf16[128,4096]{1,0:T(8,128)(2,1)}, u32[]{:S(2)}) copy-start(bf16[128,4096]{1,0:T(8,128)(2,1)} %b_ref.1) | copy-start | bytes 3145732
  63.5 6.6 %copy-start.7 = (s32[128]{0:T(128)S(1)}, s32[128]{0:T(128)}, u32[]{:S(2)}) copy-start(s32[128]{0:T(128)} %param.11) | copy-start | bytes 1540
  66.2 26.7 %copy-start.4 = (bf16[128,4096]{1,0:T(8,128)(2,1)S(1)}, bf16[128,4096]{1,0:T(8,128)(2,1)}, u32[]{:S(2)}) copy-start(bf16[128,4096]{1,0:T(8,128)(2,1)} %base_ref.1) | copy-start | bytes 3145732
  66.2 26.7 %all-to-all-start.1 = ((bf16[16,8,4096]{2,1,0:T(8,128)(2,1)}), bf16[16,8,4096]{2,1,0:T(8,128)(2,1)S(1)}, u32[]{:S(2)}, u32[]{:S(2)}) async-start(bf16[16,8,4096]{2,1,0:T(8,128)(2,1)} %bitcast.3), calls=%async_computation.1 | async-start | bytes 2097152 | tf_op jit(solution)/shard_map/all_to_all | solution.py:223
  92.9 2.2 %copy-start = (bf16[128,2,16,512]{3,2,1,0:T(8,128)(2,1)S(1)}, bf16[128,2,16,512]{3,2,1,0:T(8,128)(2,1)}, u32[]{:S(2)}) copy-start(bf16[128,2,16,512]{3,2,1,0:T(8,128)(2,1)} %kv_ref.1) | copy-start | bytes 12582916

commit v2 on v1

--- a/solution.py
+++ b/solution.py
@@ -25,6 +25,7 @@
     slot = lax.fori_loop(0, slots_ref.shape[0], look, jnp.zeros_like(ids), unroll=8)
     owner = lax.div(slot, held)
     local = slot - owner * held
+    owner = owner ^ lax.axis_index("owner")
     hits = owner == lax.broadcasted_iota(jnp.int32, (owners, rows), 0)
     earlier = lax.broadcasted_iota(jnp.int32, (rows, rows), 0) < lax.broadcasted_iota(
         jnp.int32, (rows, rows), 1
@@ -39,7 +40,8 @@
     return routed.astype(jnp.bfloat16), label
 
 
-def pack_kernel(owners, slot_count, held, slots_ref, ids_ref, hidden_ref, packed_ref, routed_ref, label_ref):
+def pack_kernel(owners, slot_count, held, slots_ref, ids_ref, hidden_ref, *refs):
+    packed_refs, (routed_ref, label_ref) = refs[:owners], refs[owners:]
     step = pl.program_id(0)
 
     @pl.when(step == 0)
@@ -48,13 +50,16 @@
         routed_ref[...] = routed
         label_ref[...] = jnp.broadcast_to(label, label_ref.shape)
 
-    packed_ref[...] = jnp.dot(
-        routed_ref[...], hidden_ref[...], preferred_element_type=jnp.float32
-    ).astype(packed_ref.dtype)
+    packed = jnp.dot(routed_ref[...], hidden_ref[...], preferred_element_type=jnp.float32)
+    for s, packed_ref in enumerate(packed_refs):
+        packed_ref[...] = packed[s * slot_count : (s + 1) * slot_count].astype(packed_ref.dtype)
 
     @pl.when(step == pl.num_programs(0) - 1)
     def _():
-        packed_ref[:, packed_ref.shape[1] - LANES :] = label_ref[...].astype(packed_ref.dtype)
+        for s, packed_ref in enumerate(packed_refs):
+            packed_ref[:, packed_ref.shape[1] - LANES :] = label_ref[
+                s * slot_count : (s + 1) * slot_count
+            ].astype(packed_ref.dtype)
 
 
 def pack(hidden, adapter_id, adapter_slot, owners, slot_count, held):
@@ -71,76 +76,63 @@
             pl.BlockSpec((1, rows), lambda i: (0, 0)),
             pl.BlockSpec((rows, block), lambda i: (0, i)),
         ],
-        out_specs=[
-            pl.BlockSpec((bins, block), lambda i: (0, i)),
-            pl.BlockSpec((bins, rows), lambda i: (0, 0)),
-        ],
-        out_shape=[
-            jax.ShapeDtypeStruct((bins, total), hidden.dtype),
-            jax.ShapeDtypeStruct((bins, rows), jnp.bfloat16),
-        ],
+        out_specs=[pl.BlockSpec((slot_count, block), lambda i: (0, i))] * owners
+        + [pl.BlockSpec((bins, rows), lambda i: (0, 0))],
+        out_shape=[jax.ShapeDtypeStruct((slot_count, total), hidden.dtype)] * owners
+        + [jax.ShapeDtypeStruct((bins, rows), jnp.bfloat16)],
         scratch_shapes=[pltpu.VMEM((bins, LANES), jnp.float32)],
         compiler_params=pltpu.CompilerParams(vmem_limit_bytes=16 * 2**20),
         name="pack",
     )(adapter_slot, adapter_id.reshape(1, rows), hidden)
 
 
-def adapt_kernel(chunk, arrived_ref, a_ref, b_ref, change_ref, held_ref, sems):
+def stack(refs, columns):
+    return jnp.concatenate([ref[:, columns].astype(jnp.float32) for ref in refs], axis=0).astype(
+        jnp.bfloat16
+    )
+
+
+def adapt_kernel(count, *refs):
+    arrived_refs, (a_ref, b_ref), change_refs = refs[:count], refs[count : count + 2], refs[count + 2 :]
     width = a_ref.shape[0]
-    spans = [(c, min(chunk, width + LANES - c)) for c in range(0, width + LANES, chunk)]
-    copies = [
-        pltpu.make_async_copy(
-            arrived_ref.at[:, pl.ds(at, size)], held_ref.at[:, pl.ds(at, size)], sems.at[i]
+    slot_count = arrived_refs[0].shape[0]
+    chunk = 2048
+    low = jnp.zeros((count * slot_count, a_ref.shape[1]), jnp.float32)
+    for at in range(0, width, chunk):
+        low += jnp.dot(
+            stack(arrived_refs, slice(at, at + chunk)),
+            a_ref[at : at + chunk, :],
+            preferred_element_type=jnp.float32,
         )
-        for i, (at, size) in enumerate(spans)
-    ]
-    for copy in copies:
-        copy.start()
-    low = jnp.zeros((arrived_ref.shape[0], a_ref.shape[1]), jnp.float32)
-    for copy, (at, size) in zip(copies, spans):
-        copy.wait()
-        size = min(size, width - at)
-        if size > 0:
-            low += jnp.dot(
-                held_ref[:, at : at + size],
-                a_ref[at : at + size, :],
-                preferred_element_type=jnp.float32,
-            )
-    label = held_ref[:, width:].astype(jnp.float32)[:, :1].astype(jnp.int32)
+    label = stack(arrived_refs, slice(width, width + LANES)).astype(jnp.float32)[:, :1]
     column = lax.broadcasted_iota(jnp.int32, low.shape, 1) // RANK
-    low = jnp.where(column == label, low, 0.0).astype(jnp.bfloat16)
+    low = jnp.where(column == label.astype(jnp.int32), low, 0.0).astype(jnp.bfloat16)
     out_width = b_ref.shape[1]
     piece = min(1024, out_width)
     for at in range(0, out_width, piece):
-        change_ref[:, at : at + piece] = (
-            SCALE
-            * jnp.dot(low, b_ref[:, at : at + piece], preferred_element_type=jnp.float32)
-        ).astype(change_ref.dtype)
+        change = SCALE * jnp.dot(low, b_ref[:, at : at + piece], preferred_element_type=jnp.float32)
+        for i, change_ref in enumerate(change_refs):
+            change_ref[:, at : at + piece] = change[i * slot_count : (i + 1) * slot_count].astype(
+                change_ref.dtype
+            )
 
 
 def adapt(arrived, a_maps, b_maps):
-    bins = arrived.shape[0]
-    chunk = 2048
-    chunks = -(-arrived.shape[1] // chunk)
+    count = len(arrived)
+    slot_count = arrived[0].shape[0]
     return pl.pallas_call(
-        functools.partial(adapt_kernel, chunk),
-        in_specs=[
-            pl.BlockSpec(memory_space=pl.ANY),
-            pl.BlockSpec(memory_space=pltpu.VMEM),
-            pl.BlockSpec(memory_space=pltpu.VMEM),
-        ],
-        out_specs=pl.BlockSpec(memory_space=pltpu.VMEM),
-        out_shape=jax.ShapeDtypeStruct((bins, b_maps.shape[1]), jnp.bfloat16),
-        scratch_shapes=[
-            pltpu.VMEM(arrived.shape, arrived.dtype),
-            pltpu.SemaphoreType.DMA((chunks,)),
-        ],
-        compiler_params=pltpu.CompilerParams(vmem_limit_bytes=24 * 2**20),
+        functools.partial(adapt_kernel, count),
+        in_specs=[pl.BlockSpec(memory_space=pltpu.VMEM)] * (count + 2),
+        out_specs=[pl.BlockSpec(memory_space=pltpu.VMEM)] * count,
+        out_shape=[jax.ShapeDtypeStruct((slot_count, b_maps.shape[1]), jnp.bfloat16)] * count,
+        compiler_params=pltpu.CompilerParams(vmem_limit_bytes=16 * 2**20),
         name="adapt",
-    )(arrived, a_maps, b_maps)
-
-
-def attend_kernel(context, routed_ref, returned_ref, base_ref, kv_ref, len_ref, out_ref, delta_ref):
+    )(*arrived, a_maps, b_maps)
+
+
+def attend_kernel(owners, context, *refs):
+    returned_refs = refs[:owners]
+    routed_ref, base_ref, kv_ref, len_ref, out_ref, delta_ref = refs[owners:]
     rows, width = base_ref.shape
     group = width // (KVH * HEAD)
     span = group * HEAD
@@ -149,7 +141,7 @@
     for k in range(KVH):
         delta_ref[:, k * span : (k + 1) * span] = lax.dot_general(
             routed_ref[...],
-            returned_ref[:, k * span : (k + 1) * span],
+            stack(returned_refs, slice(k * span, (k + 1) * span)),
             (((0,), (0,)), ((), ())),
             preferred_element_type=jnp.float32,
         ).astype(delta_ref.dtype)
@@ -199,14 +191,14 @@
     context = kv_cache.shape[2]
     lens = jnp.repeat(cache_len, context).reshape(rows // ROWS_STEP, ROWS_STEP * context)
     return pl.pallas_call(
-        functools.partial(attend_kernel, context),
-        in_specs=[pl.BlockSpec(memory_space=pltpu.VMEM)] * 5,
+        functools.partial(attend_kernel, len(returned), context),
+        in_specs=[pl.BlockSpec(memory_space=pltpu.VMEM)] * (len(returned) + 4),
         out_specs=pl.BlockSpec(memory_space=pltpu.VMEM),
         out_shape=jax.ShapeDtypeStruct(base_q.shape, jnp.bfloat16),
         scratch_shapes=[pltpu.VMEM(base_q.shape, jnp.bfloat16)],
         compiler_params=pltpu.CompilerParams(vmem_limit_bytes=24 * 2**20),
         name="attend",
-    )(routed, returned, base_q, kv_cache, lens)
+    )(*returned, routed, base_q, kv_cache, lens)
 
 
 def on_device(hidden, adapter_id, adapter_slot, cache_len, base_q, kv_cache, a_maps, b_maps):
@@ -214,14 +206,23 @@
     rows = hidden.shape[0]
     held = a_maps.shape[1] // RANK
     slot_count = max(2, 2 * ((rows + 2 * owners - 1) // (2 * owners)))
-    bins = owners * slot_count
-    packed, routed = pack(hidden, adapter_id, adapter_slot, owners, slot_count, held)
-    packed = packed.reshape(owners, slot_count, packed.shape[1])
-    arrived = lax.all_to_all(packed, "owner", split_axis=0, concat_axis=0, tiled=True)
-    change = adapt(arrived.reshape(bins, arrived.shape[2]), a_maps, b_maps)
-    change = change.reshape(owners, slot_count, change.shape[1])
-    returned = lax.all_to_all(change, "owner", split_axis=0, concat_axis=0, tiled=True)
-    return attend(routed, returned.reshape(bins, returned.shape[2]), base_q, kv_cache, cache_len)
+    *packed, routed = pack(hidden, adapter_id, adapter_slot, owners, slot_count, held)
+    send = functools.partial(exchange, owners)
+    quarter = max(1, owners // 4)
+    groups = [range(at, at + quarter) for at in range(0, owners, quarter)]
+    groups = groups[2:] + groups[1::-1]
+    arrived = {s: send(s, packed[s]) for group in groups for s in group}
+    returned = [None] * owners
+    for group in groups[::-1]:
+        for s, change in zip(group, adapt([arrived[s] for s in group], a_maps, b_maps)):
+            returned[s] = send(s, change)
+    return attend(routed, returned, base_q, kv_cache, cache_len)
+
+
+def exchange(owners, s, message):
+    if s == 0:
+        return message
+    return lax.ppermute(message, "owner", [(i, i ^ s) for i in range(owners)])
 
 
 def solution(mesh):

time: 109 us -> 112 us (1.028); the launches traced: 107 us -> 112 us
  blocking collectives: 57.9 us -> 0 us
  starting transfers between devices: 3.8 us -> 60.8 us
  waiting for transfers between devices: 22.6 us -> 26.5 us
  local copies, waits for them, and re-layouts: 5.36 us -> 6.73 us
    ppermute x0 -> x30, starting transfers between devices: none -> 60.8 us  [exchange(): return lax.ppermute(message, 'owner', [(i, i ^ s) for i in range(owners)])]
    all_to_all x1 -> x0, blocking collectives: 57.9 us -> none  [on_device(): lax.all_to_all(packed, 'owner', split_axis=0, concat_axis=0, tiled=True)]
    ppermute x0 -> x30, waiting for transfers between devices: none -> 26.5 us  [exchange(): return lax.ppermute(message, 'owner', [(i, i ^ s) for i in range(owners)])]
    all_to_all x1 -> x0, waiting for transfers between devices: 22.6 us -> none  [on_device(): lax.all_to_all(change, 'owner', split_axis=0, concat_axis=0, tiled=True)]
    all_to_all x1 -> x0, starting transfers between devices: 3.8 us -> none  [on_device(): lax.all_to_all(change, 'owner', split_axis=0, concat_axis=0, tiled=True)]
    unnamed x16 -> x18, local copies, waits for them, and re-layouts: 5.11 us -> 6.48 us
    pallas_call x2 -> x5, Pallas kernels: 15.1 us -> 15 us  [the longest x1 12.3 us: attend(): pl.pallas_call(functools.partial(attend_kernel, len(returned), context),...]
  transfers between devices with their start and end apart: 1 -> 30, of which waited for: 1 -> 17; matrix products, arithmetic and copies ran while one was open for 0% -> 0% of each run, Pallas kernels for 0% -> 2%
where the time goes in v2:
time: 112 us
  starting transfers between devices  60.8 us (54%)
  waiting for transfers between devices  26.5 us (24%)
  Pallas kernels  17.6 us (16%)
  local copies, waits for them, and re-layouts  6.73 us (6%)
    ppermute x30, starting transfers between devices, exchange(): return lax.ppermute(message, 'owner', [(i, i ^ s) for i in range(owners)])  60.8 us
    ppermute x30, waiting for transfers between devices, exchange(): return lax.ppermute(message, 'owner', [(i, i ^ s) for i in range(owners)])  26.5 us
    pallas_call x1, Pallas kernels, attend(): pl.pallas_call(functools.partial(attend_kernel, len(returned), context),...  12.3 us
    unnamed x18, local copies, waits for them, and re-layouts  6.48 us
    pallas_call x4, Pallas kernels, adapt(): pl.pallas_call(functools.partial(adapt_kernel, count), in_specs=[pl.Block...  2.72 us
    pallas_call x1, Pallas kernels, pack(): pl.pallas_call(functools.partial(pack_kernel, owners, slot_count, held),...  2.55 us
  transfers between devices with their start and end apart: 30, of which 17 were waited for; matrix products, arithmetic and copies ran while one was open for 0% of the time, Pallas kernels for 2%

profile of v2, /device:TPU:0, one launch (start us, length us, event | category | flops | bytes accessed | tf_op | source)
XLA Modules:
  0.0 111.8 jit_solution(10940985413938552127)
XLA Ops:
  0.0 1.7 %copy-done.4 = bf16[128,8192]{1,0:T(8,128)(2,1)S(1)} copy-done((bf16[128,8192]{1,0:T(8,128)(2,1)S(1)}, bf16[128,8192]{1,0:T(8,128)(2,1)}, u32[]{:S(2)}) %copy-start.4) | copy-done | bytes 2097176
  1.7 0.7 copy-done.6
  2.4 0.7 copy-done.7
  3.1 2.6 %pack.1 = (bf16[8,8320]{1,0:T(8,128)(2,1)S(1)}, bf16[8,8320]{1,0:T(8,128)(2,1)S(1)}, bf16[8,8320]{1,0:T(8,128)(2,1)S(1)}, bf16[8,8320]{1,0:T(8,128)(2,1)S(1)}, b...) custom-call(s32[32]{0:T(128)S(1)} %copy-done.6, ...), custom_call_target="tpu_custom_call" | custom-call | tf_op jit(solution)/shard_map/pack/pallas_call | solution.py:71
  5.6 5.1 %collective-permute-start.22 = (bf16[8,8320]{1,0:T(8,128)(2,1)S(1)}, bf16[8,8320]{1,0:T(8,128)(2,1)S(1)}, u32[]{:S(2)}, u32[]{:S(2)}) collective-permute-start(bf16[8,8320]{1,0:T(8,128)(2,1)S(1)} %get-tuple-element.62), channel_id=1, source_target_pairs={{0,12},{1,13},{2,14},{3,15},{4,8},{5,9},{6,10},{7,11},{8,4},{9,5},... | collective-permute-start | bytes 399368 | tf_op jit(solution)/shard_map/ppermute | solution.py:225
  10.7 3.9 %collective-permute-start.24 = (bf16[8,8320]{1,0:T(8,128)(2,1)S(1)}, bf16[8,8320]{1,0:T(8,128)(2,1)S(1)}, u32[]{:S(2)}, u32[]{:S(2)}) collective-permute-start(bf16[8,8320]{1,0:T(8,128)(2,1)S(1)} %get-tuple-element.64), channel_id=1, source_target_pairs={{0,14},{1,15},{2,12},{3,13},{4,10},{5,11},{6,8},{7,9},{8,6},{9,7},... | collective-permute-start | bytes 399368 | tf_op jit(solution)/shard_map/ppermute | solution.py:225
  14.6 0.6 collective-permute-start.25
  15.2 2.6 %collective-permute-start.15 = (bf16[8,8320]{1,0:T(8,128)(2,1)S(1)}, bf16[8,8320]{1,0:T(8,128)(2,1)S(1)}, u32[]{:S(2)}, u32[]{:S(2)}) collective-permute-start(bf16[8,8320]{1,0:T(8,128)(2,1)S(1)} %get-tuple-element.55), channel_id=1, source_target_pairs={{0,9},{1,8},{2,11},{3,10},{4,13},{5,12},{6,15},{7,14},{8,1},{9,0},... | collective-permute-start | bytes 399368 | tf_op jit(solution)/shard_map/ppermute | solution.py:225
  17.8 0.6 collective-permute-done.23.refs_1_
  18.5 14.9 %collective-permute-start.16 = (bf16[8,8320]{1,0:T(8,128)(2,1)S(1)}, bf16[8,8320]{1,0:T(8,128)(2,1)S(1)}, u32[]{:S(2)}, u32[]{:S(2)}) collective-permute-start(bf16[8,8320]{1,0:T(8,128)(2,1)S(1)} %get-tuple-element.56), channel_id=1, source_target_pairs={{0,10},{1,11},{2,8},{3,9},{4,14},{5,15},{6,12},{7,13},{8,2},{9,3},... | collective-permute-start | bytes 399368 | tf_op jit(solution)/shard_map/ppermute | solution.py:225
  33.4 2.4 %collective-permute-start.17 = (bf16[8,8320]{1,0:T(8,128)(2,1)S(1)}, bf16[8,8320]{1,0:T(8,128)(2,1)S(1)}, u32[]{:S(2)}, u32[]{:S(2)}) collective-permute-start(bf16[8,8320]{1,0:T(8,128)(2,1)S(1)} %get-tuple-element.57), channel_id=1, source_target_pairs={{0,11},{1,10},{2,9},{3,8},{4,15},{5,14},{6,13},{7,12},{8,3},{9,2},... | collective-permute-start | bytes 399368 | tf_op jit(solution)/shard_map/ppermute | solution.py:225
  35.8 8.3 %collective-permute-start.6 = (bf16[8,8320]{1,0:T(8,128)(2,1)S(1)}, bf16[8,8320]{1,0:T(8,128)(2,1)S(1)}, u32[]{:S(2)}, u32[]{:S(2)}) collective-permute-start(bf16[8,8320]{1,0:T(8,128)(2,1)S(1)} %get-tuple-element.46), channel_id=1, source_target_pairs={{0,4},{1,5},{2,6},{3,7},{4,0},{5,1},{6,2},{7,3},{8,12},{9,13},{10,... | collective-permute-start | bytes 399368 | tf_op jit(solution)/shard_map/ppermute | solution.py:225
  44.2 4.5 %collective-permute-done.14.refs_0_ = bf16[8,8320]{1,0:T(8,128)(2,1)S(1)} collective-permute-done((bf16[8,8320]{1,0:T(8,128)(2,1)S(1)}, bf16[8,8320]{1,0:T(8,128)(2,1)S(1)}, u32[]{:S(2)}, u32[]{:S(2)}) %collective-permute-start.14) | collective-permute-done | bytes 133152 | tf_op jit(solution)/shard_map/ppermute | solution.py:225
  48.7 0.9 collective-permute-done.15.refs_1_
  49.6 2.7 %collective-permute-start.8 = (bf16[8,8320]{1,0:T(8,128)(2,1)S(1)}, bf16[8,8320]{1,0:T(8,128)(2,1)S(1)}, u32[]{:S(2)}, u32[]{:S(2)}) collective-permute-start(bf16[8,8320]{1,0:T(8,128)(2,1)S(1)} %get-tuple-element.48), channel_id=1, source_target_pairs={{0,6},{1,7},{2,4},{3,5},{4,2},{5,3},{6,0},{7,1},{8,14},{9,15},{10,... | collective-permute-start | bytes 399368 | tf_op jit(solution)/shard_map/ppermute | solution.py:225
  52.3 3.0 %collective-permute-done.16.refs_2_ = bf16[8,8320]{1,0:T(8,128)(2,1)S(1)} collective-permute-done((bf16[8,8320]{1,0:T(8,128)(2,1)S(1)}, bf16[8,8320]{1,0:T(8,128)(2,1)S(1)}, u32[]{:S(2)}, u32[]{:S(2)}) %collective-permute-start.16) | collective-permute-done | bytes 133152 | tf_op jit(solution)/shard_map/ppermute | solution.py:225
  55.3 0.9 collective-permute-done.17.refs_3_
  56.3 0.8 collective-permute-start
  57.1 1.6 %collective-permute-start.1 = (bf16[8,8320]{1,0:T(8,128)(2,1)S(1)}, bf16[8,8320]{1,0:T(8,128)(2,1)S(1)}, u32[]{:S(2)}, u32[]{:S(2)}) collective-permute-start(bf16[8,8320]{1,0:T(8,128)(2,1)S(1)} %get-tuple-element.40), channel_id=1, source_target_pairs={{0,2},{1,3},{2,0},{3,1},{4,6},{5,7},{6,4},{7,5},{8,10},{9,11},{10,... | collective-permute-start | bytes 399368 | tf_op jit(solution)/shard_map/ppermute | solution.py:225
  58.6 3.1 %collective-permute-done.7.refs_1_ = bf16[8,8320]{1,0:T(8,128)(2,1)S(1)} collective-permute-done((bf16[8,8320]{1,0:T(8,128)(2,1)S(1)}, bf16[8,8320]{1,0:T(8,128)(2,1)S(1)}, u32[]{:S(2)}, u32[]{:S(2)}) %collective-permute-start.7) | collective-permute-done | bytes 133152 | tf_op jit(solution)/shard_map/ppermute | solution.py:225
  61.7 1.2 %copy-done.1 = bf16[128,4096]{1,0:T(8,128)(2,1)S(1)} copy-done((bf16[128,4096]{1,0:T(8,128)(2,1)S(1)}, bf16[128,4096]{1,0:T(8,128)(2,1)}, u32[]{:S(2)}) %copy-start.1) | copy-done | bytes 1048600
  62.9 0.7 adapt.7
  63.6 0.7 adapt.6
  64.3 2.3 %collective-permute-start.26 = (bf16[8,4096]{1,0:T(8,128)(2,1)S(1)}, bf16[8,4096]{1,0:T(8,128)(2,1)S(1)}, u32[]{:S(2)}, u32[]{:S(2)}) collective-permute-start(bf16[8,4096]{1,0:T(8,128)(2,1)S(1)} %get-tuple-element.66), channel_id=1, source_target_pairs={{0,12},{1,13},{2,14},{3,15},{4,8},{5,9},{6,10},{7,11},{8,4},{9,5},... | collective-permute-start | bytes 196616 | tf_op jit(solution)/shard_map/ppermute | solution.py:225
  66.6 0.6 collective-permute-done.9.refs_3_
  67.2 1.9 %collective-permute-start.27 = (bf16[8,4096]{1,0:T(8,128)(2,1)S(1)}, bf16[8,4096]{1,0:T(8,128)(2,1)S(1)}, u32[]{:S(2)}, u32[]{:S(2)}) collective-permute-start(bf16[8,4096]{1,0:T(8,128)(2,1)S(1)} %get-tuple-element.67), channel_id=1, source_target_pairs={{0,13},{1,12},{2,15},{3,14},{4,9},{5,8},{6,11},{7,10},{8,5},{9,4},... | collective-permute-start | bytes 196616 | tf_op jit(solution)/shard_map/ppermute | solution.py:225
  69.2 1.3 %collective-permute-start.28 = (bf16[8,4096]{1,0:T(8,128)(2,1)S(1)}, bf16[8,4096]{1,0:T(8,128)(2,1)S(1)}, u32[]{:S(2)}, u32[]{:S(2)}) collective-permute-start(bf16[8,4096]{1,0:T(8,128)(2,1)S(1)} %get-tuple-element.68), channel_id=1, source_target_pairs={{0,14},{1,15},{2,12},{3,13},{4,10},{5,11},{6,8},{7,9},{8,6},{9,7},... | collective-permute-start | bytes 196616 | tf_op jit(solution)/shard_map/ppermute | solution.py:225
  70.5 3.3 %collective-permute-start.29 = (bf16[8,4096]{1,0:T(8,128)(2,1)S(1)}, bf16[8,4096]{1,0:T(8,128)(2,1)S(1)}, u32[]{:S(2)}, u32[]{:S(2)}) collective-permute-start(bf16[8,4096]{1,0:T(8,128)(2,1)S(1)} %get-tuple-element.69), channel_id=1, source_target_pairs={{0,15},{1,14},{2,13},{3,12},{4,11},{5,10},{6,9},{7,8},{8,7},{9,6},... | collective-permute-start | bytes 196616 | tf_op jit(solution)/shard_map/ppermute | solution.py:225
  73.8 0.7 adapt.5
  74.5 2.5 %collective-permute-start.19 = (bf16[8,4096]{1,0:T(8,128)(2,1)S(1)}, bf16[8,4096]{1,0:T(8,128)(2,1)S(1)}, u32[]{:S(2)}, u32[]{:S(2)}) collective-permute-start(bf16[8,4096]{1,0:T(8,128)(2,1)S(1)} %get-tuple-element.59), channel_id=1, source_target_pairs={{0,9},{1,8},{2,11},{3,10},{4,13},{5,12},{6,15},{7,14},{8,1},{9,0},... | collective-permute-start | bytes 196616 | tf_op jit(solution)/shard_map/ppermute | solution.py:225
  77.0 0.6 collective-permute-start.20
  77.6 3.2 %collective-permute-start.21 = (bf16[8,4096]{1,0:T(8,128)(2,1)S(1)}, bf16[8,4096]{1,0:T(8,128)(2,1)S(1)}, u32[]{:S(2)}, u32[]{:S(2)}) collective-permute-start(bf16[8,4096]{1,0:T(8,128)(2,1)S(1)} %get-tuple-element.61), channel_id=1, source_target_pairs={{0,11},{1,10},{2,9},{3,8},{4,15},{5,14},{6,13},{7,12},{8,3},{9,2},... | collective-permute-start | bytes 196616 | tf_op jit(solution)/shard_map/ppermute | solution.py:225
  80.8 4.5 %collective-permute-done.18.refs_8_ = bf16[8,4096]{1,0:T(8,128)(2,1)S(1)} collective-permute-done((bf16[8,4096]{1,0:T(8,128)(2,1)S(1)}, bf16[8,4096]{1,0:T(8,128)(2,1)S(1)}, u32[]{:S(2)}, u32[]{:S(2)}) %collective-permute-start.18) | collective-permute-done | bytes 65568 | tf_op jit(solution)/shard_map/ppermute | solution.py:225
  85.3 0.7 adapt.4
  86.0 0.6 collective-permute-done.19.refs_9_
  86.6 1.4 %collective-permute-start.12 = (bf16[8,4096]{1,0:T(8,128)(2,1)S(1)}, bf16[8,4096]{1,0:T(8,128)(2,1)S(1)}, u32[]{:S(2)}, u32[]{:S(2)}) collective-permute-start(bf16[8,4096]{1,0:T(8,128)(2,1)S(1)} %get-tuple-element.52), channel_id=1, source_target_pairs={{0,6},{1,7},{2,4},{3,5},{4,2},{5,3},{6,0},{7,1},{8,14},{9,15},{10,... | collective-permute-start | bytes 196616 | tf_op jit(solution)/shard_map/ppermute | solution.py:225
  88.0 0.7 collective-permute-done.20.refs_10_
  88.9 0.9 collective-permute-done.21.refs_11_
  89.9 0.7 collective-permute-done.10.refs_4_
  90.5 0.7 collective-permute-start.4
  91.2 0.5 collective-permute-done.11.refs_5_
  91.8 0.3 collective-permute-start.5
  92.3 1.2 %collective-permute-done.12.refs_6_ = bf16[8,4096]{1,0:T(8,128)(2,1)S(1)} collective-permute-done((bf16[8,4096]{1,0:T(8,128)(2,1)S(1)}, bf16[8,4096]{1,0:T(8,128)(2,1)S(1)}, u32[]{:S(2)}, u32[]{:S(2)}) %collective-permute-start.12) | collective-permute-done | bytes 65568 | tf_op jit(solution)/shard_map/ppermute | solution.py:225
  93.5 0.7 collective-permute-done.13.refs_7_
  94.3 1.8 %collective-permute-done.4.refs_2_ = bf16[8,4096]{1,0:T(8,128)(2,1)S(1)} collective-permute-done((bf16[8,4096]{1,0:T(8,128)(2,1)S(1)}, bf16[8,4096]{1,0:T(8,128)(2,1)S(1)}, u32[]{:S(2)}, u32[]{:S(2)}) %collective-permute-start.4) | collective-permute-done | bytes 65568 | tf_op jit(solution)/shard_map/ppermute | solution.py:225
  96.0 1.2 %collective-permute-done.5.refs_3_ = bf16[8,4096]{1,0:T(8,128)(2,1)S(1)} collective-permute-done((bf16[8,4096]{1,0:T(8,128)(2,1)S(1)}, bf16[8,4096]{1,0:T(8,128)(2,1)S(1)}, u32[]{:S(2)}, u32[]{:S(2)}) %collective-permute-start.5) | collective-permute-done | bytes 65568 | tf_op jit(solution)/shard_map/ppermute | solution.py:225
  97.3 2.2 %copy-done.3 = bf16[128,2,16,512]{3,2,1,0:T(8,128)(2,1)S(1)} copy-done((bf16[128,2,16,512]{3,2,1,0:T(8,128)(2,1)S(1)}, bf16[128,2,16,512]{3,2,1,0:T(8,128)(2,1)}, u32[]{:S(2)}) %copy-start.3) | copy-done | bytes 4194328
  99.4 12.3 %attend.1 = bf16[128,4096]{1,0:T(8,128)(2,1)} custom-call(bf16[8,4096]{1,0:T(8,128)(2,1)S(1)} %get-tuple-element.42.refs_0_, bf16[8,4096]{1,0:T(8,128)(2,1)S(1)} %collective-permute-done.3.refs_1_, bf16[8,4096]{1,0:T(8,128)(2,1)S(1)} %collective-permute-done.4.refs_2_, bf16[8,4096]{1,0:T(8,128)(2,1)S(1)} %collective-permute-done.5.refs_3_, ...), custom_call_target="tpu_custom_call" | custom-call | tf_op jit(solution)/shard_map/attend/pallas_call | solution.py:193
  (39 shorter events, 0.6 us)
Async XLA Ops:
  0.0 61.7 %copy-start = (bf16[8192,128]{1,0:T(8,128)(2,1)S(1)}, bf16[8192,128]{1,0:T(8,128)(2,1)}, u32[]{:S(2)}) copy-start(bf16[8192,128]{1,0:T(8,128)(2,1)} %refs_4_.7) | copy-start | bytes 6291460
  0.0 1.7 %copy-start.4 = (bf16[128,8192]{1,0:T(8,128)(2,1)S(1)}, bf16[128,8192]{1,0:T(8,128)(2,1)}, u32[]{:S(2)}) copy-start(bf16[128,8192]{1,0:T(8,128)(2,1)} %hidden_ref.1) | copy-start | bytes 6291460
  1.7 0.7 copy-start.6
  2.4 0.7 copy-start.7
  5.6 9.6 %collective-permute-start.22 = (bf16[8,8320]{1,0:T(8,128)(2,1)S(1)}, bf16[8,8320]{1,0:T(8,128)(2,1)S(1)}, u32[]{:S(2)}, u32[]{:S(2)}) collective-permute-start(bf16[8,8320]{1,0:T(8,128)(2,1)S(1)} %get-tuple-element.62), channel_id=1, source_target_pairs={{0,12},{1,13},{2,14},{3,15},{4,8},{5,9},{6,10},{7,11},{8,4},{9,5},... | collective-permute-start | bytes 399368 | tf_op jit(solution)/shard_map/ppermute | solution.py:225
  10.7 7.7 %collective-permute-start.23 = (bf16[8,8320]{1,0:T(8,128)(2,1)S(1)}, bf16[8,8320]{1,0:T(8,128)(2,1)S(1)}, u32[]{:S(2)}, u32[]{:S(2)}) collective-permute-start(bf16[8,8320]{1,0:T(8,128)(2,1)S(1)} %get-tuple-element.63), channel_id=1, source_target_pairs={{0,13},{1,12},{2,15},{3,14},{4,9},{5,8},{6,11},{7,10},{8,5},{9,4},... | collective-permute-start | bytes 399368 | tf_op jit(solution)/shard_map/ppermute | solution.py:225
  10.7 22.7 %collective-permute-start.24 = (bf16[8,8320]{1,0:T(8,128)(2,1)S(1)}, bf16[8,8320]{1,0:T(8,128)(2,1)S(1)}, u32[]{:S(2)}, u32[]{:S(2)}) collective-permute-start(bf16[8,8320]{1,0:T(8,128)(2,1)S(1)} %get-tuple-element.64), channel_id=1, source_target_pairs={{0,14},{1,15},{2,12},{3,13},{4,10},{5,11},{6,8},{7,9},{8,6},{9,7},... | collective-permute-start | bytes 399368 | tf_op jit(solution)/shard_map/ppermute | solution.py:225
  14.6 21.2 %collective-permute-start.25 = (bf16[8,8320]{1,0:T(8,128)(2,1)S(1)}, bf16[8,8320]{1,0:T(8,128)(2,1)S(1)}, u32[]{:S(2)}, u32[]{:S(2)}) collective-permute-start(bf16[8,8320]{1,0:T(8,128)(2,1)S(1)} %get-tuple-element.65), channel_id=1, source_target_pairs={{0,15},{1,14},{2,13},{3,12},{4,11},{5,10},{6,9},{7,8},{8,7},{9,6},... | collective-permute-start | bytes 399368 | tf_op jit(solution)/shard_map/ppermute | solution.py:225
  15.2 33.5 %collective-permute-start.14 = (bf16[8,8320]{1,0:T(8,128)(2,1)S(1)}, bf16[8,8320]{1,0:T(8,128)(2,1)S(1)}, u32[]{:S(2)}, u32[]{:S(2)}) collective-permute-start(bf16[8,8320]{1,0:T(8,128)(2,1)S(1)} %get-tuple-element.54), channel_id=1, source_target_pairs={{0,8},{1,9},{2,10},{3,11},{4,12},{5,13},{6,14},{7,15},{8,0},{9,1},... | collective-permute-start | bytes 399368 | tf_op jit(solution)/shard_map/ppermute | solution.py:225
  15.2 34.4 %collective-permute-start.15 = (bf16[8,8320]{1,0:T(8,128)(2,1)S(1)}, bf16[8,8320]{1,0:T(8,128)(2,1)S(1)}, u32[]{:S(2)}, u32[]{:S(2)}) collective-permute-start(bf16[8,8320]{1,0:T(8,128)(2,1)S(1)} %get-tuple-element.55), channel_id=1, source_target_pairs={{0,9},{1,8},{2,11},{3,10},{4,13},{5,12},{6,15},{7,14},{8,1},{9,0},... | collective-permute-start | bytes 399368 | tf_op jit(solution)/shard_map/ppermute | solution.py:225
  18.5 36.9 %collective-permute-start.16 = (bf16[8,8320]{1,0:T(8,128)(2,1)S(1)}, bf16[8,8320]{1,0:T(8,128)(2,1)S(1)}, u32[]{:S(2)}, u32[]{:S(2)}) collective-permute-start(bf16[8,8320]{1,0:T(8,128)(2,1)S(1)} %get-tuple-element.56), channel_id=1, source_target_pairs={{0,10},{1,11},{2,8},{3,9},{4,14},{5,15},{6,12},{7,13},{8,2},{9,3},... | collective-permute-start | bytes 399368 | tf_op jit(solution)/shard_map/ppermute | solution.py:225
  33.4 22.9 %collective-permute-start.17 = (bf16[8,8320]{1,0:T(8,128)(2,1)S(1)}, bf16[8,8320]{1,0:T(8,128)(2,1)S(1)}, u32[]{:S(2)}, u32[]{:S(2)}) collective-permute-start(bf16[8,8320]{1,0:T(8,128)(2,1)S(1)} %get-tuple-element.57), channel_id=1, source_target_pairs={{0,11},{1,10},{2,9},{3,8},{4,15},{5,14},{6,13},{7,12},{8,3},{9,2},... | collective-permute-start | bytes 399368 | tf_op jit(solution)/shard_map/ppermute | solution.py:225
  35.8 21.2 %collective-permute-start.6 = (bf16[8,8320]{1,0:T(8,128)(2,1)S(1)}, bf16[8,8320]{1,0:T(8,128)(2,1)S(1)}, u32[]{:S(2)}, u32[]{:S(2)}) collective-permute-start(bf16[8,8320]{1,0:T(8,128)(2,1)S(1)} %get-tuple-element.46), channel_id=1, source_target_pairs={{0,4},{1,5},{2,6},{3,7},{4,0},{5,1},{6,2},{7,3},{8,12},{9,13},{10,... | collective-permute-start | bytes 399368 | tf_op jit(solution)/shard_map/ppermute | solution.py:225
  48.7 13.0 %collective-permute-start.7 = (bf16[8,8320]{1,0:T(8,128)(2,1)S(1)}, bf16[8,8320]{1,0:T(8,128)(2,1)S(1)}, u32[]{:S(2)}, u32[]{:S(2)}) collective-permute-start(bf16[8,8320]{1,0:T(8,128)(2,1)S(1)} %get-tuple-element.47), channel_id=1, source_target_pairs={{0,5},{1,4},{2,7},{3,6},{4,1},{5,0},{6,3},{7,2},{8,13},{9,12},{10,... | collective-permute-start | bytes 399368 | tf_op jit(solution)/shard_map/ppermute | solution.py:225
  49.6 14.7 %collective-permute-start.8 = (bf16[8,8320]{1,0:T(8,128)(2,1)S(1)}, bf16[8,8320]{1,0:T(8,128)(2,1)S(1)}, u32[]{:S(2)}, u32[]{:S(2)}) collective-permute-start(bf16[8,8320]{1,0:T(8,128)(2,1)S(1)} %get-tuple-element.48), channel_id=1, source_target_pairs={{0,6},{1,7},{2,4},{3,5},{4,2},{5,3},{6,0},{7,1},{8,14},{9,15},{10,... | collective-permute-start | bytes 399368 | tf_op jit(solution)/shard_map/ppermute | solution.py:225
  55.3 11.9 %collective-permute-start.9 = (bf16[8,8320]{1,0:T(8,128)(2,1)S(1)}, bf16[8,8320]{1,0:T(8,128)(2,1)S(1)}, u32[]{:S(2)}, u32[]{:S(2)}) collective-permute-start(bf16[8,8320]{1,0:T(8,128)(2,1)S(1)} %get-tuple-element.49), channel_id=1, source_target_pairs={{0,7},{1,6},{2,5},{3,4},{4,3},{5,2},{6,1},{7,0},{8,15},{9,14},{10,... | collective-permute-start | bytes 399368 | tf_op jit(solution)/shard_map/ppermute | solution.py:225
  56.3 12.9 %collective-permute-start = (bf16[8,8320]{1,0:T(8,128)(2,1)S(1)}, bf16[8,8320]{1,0:T(8,128)(2,1)S(1)}, u32[]{:S(2)}, u32[]{:S(2)}) collective-permute-start(bf16[8,8320]{1,0:T(8,128)(2,1)S(1)} %get-tuple-element.39), channel_id=1, source_target_pairs={{0,1},{1,0},{2,3},{3,2},{4,5},{5,4},{6,7},{7,6},{8,9},{9,8},{10,11... | collective-permute-start | bytes 399368 | tf_op jit(solution)/shard_map/ppermute | solution.py:225
  57.1 13.4 %collective-permute-start.1 = (bf16[8,8320]{1,0:T(8,128)(2,1)S(1)}, bf16[8,8320]{1,0:T(8,128)(2,1)S(1)}, u32[]{:S(2)}, u32[]{:S(2)}) collective-permute-start(bf16[8,8320]{1,0:T(8,128)(2,1)S(1)} %get-tuple-element.40), channel_id=1, source_target_pairs={{0,2},{1,3},{2,0},{3,1},{4,6},{5,7},{6,4},{7,5},{8,10},{9,11},{10,... | collective-permute-start | bytes 399368 | tf_op jit(solution)/shard_map/ppermute | solution.py:225
  61.7 12.1 %collective-permute-start.2 = (bf16[8,8320]{1,0:T(8,128)(2,1)S(1)}, bf16[8,8320]{1,0:T(8,128)(2,1)S(1)}, u32[]{:S(2)}, u32[]{:S(2)}) collective-permute-start(bf16[8,8320]{1,0:T(8,128)(2,1)S(1)} %get-tuple-element.41), channel_id=1, source_target_pairs={{0,3},{1,2},{2,1},{3,0},{4,7},{5,6},{6,5},{7,4},{8,11},{9,10},{10,... | collective-permute-start | bytes 399368 | tf_op jit(solution)/shard_map/ppermute | solution.py:225
  61.7 1.2 %copy-start.1 = (bf16[128,4096]{1,0:T(8,128)(2,1)S(1)}, bf16[128,4096]{1,0:T(8,128)(2,1)}, u32[]{:S(2)}) copy-start(bf16[128,4096]{1,0:T(8,128)(2,1)} %refs_5_.7) | copy-start | bytes 3145732
  64.3 21.0 %copy-start.2 = (bf16[128,4096]{1,0:T(8,128)(2,1)S(1)}, bf16[128,4096]{1,0:T(8,128)(2,1)}, u32[]{:S(2)}) copy-start(bf16[128,4096]{1,0:T(8,128)(2,1)} %refs_5_.7) | copy-start | bytes 3145732
  64.3 10.2 %collective-permute-start.26 = (bf16[8,4096]{1,0:T(8,128)(2,1)S(1)}, bf16[8,4096]{1,0:T(8,128)(2,1)S(1)}, u32[]{:S(2)}, u32[]{:S(2)}) collective-permute-start(bf16[8,4096]{1,0:T(8,128)(2,1)S(1)} %get-tuple-element.66), channel_id=1, source_target_pairs={{0,12},{1,13},{2,14},{3,15},{4,8},{5,9},{6,10},{7,11},{8,4},{9,5},... | collective-permute-start | bytes 196616 | tf_op jit(solution)/shard_map/ppermute | solution.py:225
  67.2 9.8 %collective-permute-start.27 = (bf16[8,4096]{1,0:T(8,128)(2,1)S(1)}, bf16[8,4096]{1,0:T(8,128)(2,1)S(1)}, u32[]{:S(2)}, u32[]{:S(2)}) collective-permute-start(bf16[8,4096]{1,0:T(8,128)(2,1)S(1)} %get-tuple-element.67), channel_id=1, source_target_pairs={{0,13},{1,12},{2,15},{3,14},{4,9},{5,8},{6,11},{7,10},{8,5},{9,4},... | collective-permute-start | bytes 196616 | tf_op jit(solution)/shard_map/ppermute | solution.py:225
  69.2 8.5 %collective-permute-start.28 = (bf16[8,4096]{1,0:T(8,128)(2,1)S(1)}, bf16[8,4096]{1,0:T(8,128)(2,1)S(1)}, u32[]{:S(2)}, u32[]{:S(2)}) collective-permute-start(bf16[8,4096]{1,0:T(8,128)(2,1)S(1)} %get-tuple-element.68), channel_id=1, source_target_pairs={{0,14},{1,15},{2,12},{3,13},{4,10},{5,11},{6,8},{7,9},{8,6},{9,7},... | collective-permute-start | bytes 196616 | tf_op jit(solution)/shard_map/ppermute | solution.py:225
  70.5 10.3 %collective-permute-start.29 = (bf16[8,4096]{1,0:T(8,128)(2,1)S(1)}, bf16[8,4096]{1,0:T(8,128)(2,1)S(1)}, u32[]{:S(2)}, u32[]{:S(2)}) collective-permute-start(bf16[8,4096]{1,0:T(8,128)(2,1)S(1)} %get-tuple-element.69), channel_id=1, source_target_pairs={{0,15},{1,14},{2,13},{3,12},{4,11},{5,10},{6,9},{7,8},{8,7},{9,6},... | collective-permute-start | bytes 196616 | tf_op jit(solution)/shard_map/ppermute | solution.py:225
  73.8 11.5 %collective-permute-start.18 = (bf16[8,4096]{1,0:T(8,128)(2,1)S(1)}, bf16[8,4096]{1,0:T(8,128)(2,1)S(1)}, u32[]{:S(2)}, u32[]{:S(2)}) collective-permute-start(bf16[8,4096]{1,0:T(8,128)(2,1)S(1)} %get-tuple-element.58), channel_id=1, source_target_pairs={{0,8},{1,9},{2,10},{3,11},{4,12},{5,13},{6,14},{7,15},{8,0},{9,1},... | collective-permute-start | bytes 196616 | tf_op jit(solution)/shard_map/ppermute | solution.py:225
  74.5 17.6 %copy-start.8 = (s32[128]{0:T(128)S(1)}, s32[128]{0:T(128)}, u32[]{:S(2)}) copy-start(s32[128]{0:T(128)} %param.11) | copy-start | bytes 1540
  74.5 22.7 %copy-start.5 = (bf16[128,4096]{1,0:T(8,128)(2,1)S(1)}, bf16[128,4096]{1,0:T(8,128)(2,1)}, u32[]{:S(2)}) copy-start(bf16[128,4096]{1,0:T(8,128)(2,1)} %refs_17_.1) | copy-start | bytes 3145732
  74.5 12.0 %collective-permute-start.19 = (bf16[8,4096]{1,0:T(8,128)(2,1)S(1)}, bf16[8,4096]{1,0:T(8,128)(2,1)S(1)}, u32[]{:S(2)}, u32[]{:S(2)}) collective-permute-start(bf16[8,4096]{1,0:T(8,128)(2,1)S(1)} %get-tuple-element.59), channel_id=1, source_target_pairs={{0,9},{1,8},{2,11},{3,10},{4,13},{5,12},{6,15},{7,14},{8,1},{9,0},... | collective-permute-start | bytes 196616 | tf_op jit(solution)/shard_map/ppermute | solution.py:225
  77.0 11.7 %collective-permute-start.20 = (bf16[8,4096]{1,0:T(8,128)(2,1)S(1)}, bf16[8,4096]{1,0:T(8,128)(2,1)S(1)}, u32[]{:S(2)}, u32[]{:S(2)}) collective-permute-start(bf16[8,4096]{1,0:T(8,128)(2,1)S(1)} %get-tuple-element.60), channel_id=1, source_target_pairs={{0,10},{1,11},{2,8},{3,9},{4,14},{5,15},{6,12},{7,13},{8,2},{9,3},... | collective-permute-start | bytes 196616 | tf_op jit(solution)/shard_map/ppermute | solution.py:225
  77.6 12.2 %collective-permute-start.21 = (bf16[8,4096]{1,0:T(8,128)(2,1)S(1)}, bf16[8,4096]{1,0:T(8,128)(2,1)S(1)}, u32[]{:S(2)}, u32[]{:S(2)}) collective-permute-start(bf16[8,4096]{1,0:T(8,128)(2,1)S(1)} %get-tuple-element.61), channel_id=1, source_target_pairs={{0,11},{1,10},{2,9},{3,8},{4,15},{5,14},{6,13},{7,12},{8,3},{9,2},... | collective-permute-start | bytes 196616 | tf_op jit(solution)/shard_map/ppermute | solution.py:225
  80.8 9.7 %collective-permute-start.10 = (bf16[8,4096]{1,0:T(8,128)(2,1)S(1)}, bf16[8,4096]{1,0:T(8,128)(2,1)S(1)}, u32[]{:S(2)}, u32[]{:S(2)}) collective-permute-start(bf16[8,4096]{1,0:T(8,128)(2,1)S(1)} %get-tuple-element.50), channel_id=1, source_target_pairs={{0,4},{1,5},{2,6},{3,7},{4,0},{5,1},{6,2},{7,3},{8,12},{9,13},{10,... | collective-permute-start | bytes 196616 | tf_op jit(solution)/shard_map/ppermute | solution.py:225
  85.3 6.5 %collective-permute-start.11 = (bf16[8,4096]{1,0:T(8,128)(2,1)S(1)}, bf16[8,4096]{1,0:T(8,128)(2,1)S(1)}, u32[]{:S(2)}, u32[]{:S(2)}) collective-permute-start(bf16[8,4096]{1,0:T(8,128)(2,1)S(1)} %get-tuple-element.51), channel_id=1, source_target_pairs={{0,5},{1,4},{2,7},{3,6},{4,1},{5,0},{6,3},{7,2},{8,13},{9,12},{10,... | collective-permute-start | bytes 196616 | tf_op jit(solution)/shard_map/ppermute | solution.py:225
  86.6 7.0 %collective-permute-start.12 = (bf16[8,4096]{1,0:T(8,128)(2,1)S(1)}, bf16[8,4096]{1,0:T(8,128)(2,1)S(1)}, u32[]{:S(2)}, u32[]{:S(2)}) collective-permute-start(bf16[8,4096]{1,0:T(8,128)(2,1)S(1)} %get-tuple-element.52), channel_id=1, source_target_pairs={{0,6},{1,7},{2,4},{3,5},{4,2},{5,3},{6,0},{7,1},{8,14},{9,15},{10,... | collective-permute-start | bytes 196616 | tf_op jit(solution)/shard_map/ppermute | solution.py:225
  88.7 5.6 %collective-permute-start.13 = (bf16[8,4096]{1,0:T(8,128)(2,1)S(1)}, bf16[8,4096]{1,0:T(8,128)(2,1)S(1)}, u32[]{:S(2)}, u32[]{:S(2)}) collective-permute-start(bf16[8,4096]{1,0:T(8,128)(2,1)S(1)} %get-tuple-element.53), channel_id=1, source_target_pairs={{0,7},{1,6},{2,5},{3,4},{4,3},{5,2},{6,1},{7,0},{8,15},{9,14},{10,... | collective-permute-start | bytes 196616 | tf_op jit(solution)/shard_map/ppermute | solution.py:225
  89.8 4.5 %collective-permute-start.3 = (bf16[8,4096]{1,0:T(8,128)(2,1)S(1)}, bf16[8,4096]{1,0:T(8,128)(2,1)S(1)}, u32[]{:S(2)}, u32[]{:S(2)}) collective-permute-start(bf16[8,4096]{1,0:T(8,128)(2,1)S(1)} %get-tuple-element.43), channel_id=1, source_target_pairs={{0,1},{1,0},{2,3},{3,2},{4,5},{5,4},{6,7},{7,6},{8,9},{9,8},{10,11... | collective-permute-start | bytes 196616 | tf_op jit(solution)/shard_map/ppermute | solution.py:225
  90.5 5.5 %collective-permute-start.4 = (bf16[8,4096]{1,0:T(8,128)(2,1)S(1)}, bf16[8,4096]{1,0:T(8,128)(2,1)S(1)}, u32[]{:S(2)}, u32[]{:S(2)}) collective-permute-start(bf16[8,4096]{1,0:T(8,128)(2,1)S(1)} %get-tuple-element.44), channel_id=1, source_target_pairs={{0,2},{1,3},{2,0},{3,1},{4,6},{5,7},{6,4},{7,5},{8,10},{9,11},{10,... | collective-permute-start | bytes 196616 | tf_op jit(solution)/shard_map/ppermute | solution.py:225
  91.8 5.4 %collective-permute-start.5 = (bf16[8,4096]{1,0:T(8,128)(2,1)S(1)}, bf16[8,4096]{1,0:T(8,128)(2,1)S(1)}, u32[]{:S(2)}, u32[]{:S(2)}) collective-permute-start(bf16[8,4096]{1,0:T(8,128)(2,1)S(1)} %get-tuple-element.45), channel_id=1, source_target_pairs={{0,3},{1,2},{2,1},{3,0},{4,7},{5,6},{6,5},{7,4},{8,11},{9,10},{10,... | collective-permute-start | bytes 196616 | tf_op jit(solution)/shard_map/ppermute | solution.py:225
  97.2 2.2 %copy-start.3 = (bf16[128,2,16,512]{3,2,1,0:T(8,128)(2,1)S(1)}, bf16[128,2,16,512]{3,2,1,0:T(8,128)(2,1)}, u32[]{:S(2)}) copy-start(bf16[128,2,16,512]{3,2,1,0:T(8,128)(2,1)} %refs_18_.1) | copy-start | bytes 12582916

commit v3 on v1

v3 whole, which is shorter than its diff:
```python
import functools

import jax
import jax.numpy as jnp
from jax import lax
from jax.experimental import pallas as pl
from jax.experimental.pallas import tpu as pltpu
from jax.sharding import PartitionSpec as P

HEAD = 128
KVH = 4
RANK = 64
LANES = 128
SCALE = 2.0
ROWS_STEP = 8
COLUMNS_STEP = 2048


def routing(owners, slot_count, held, slots_ref, ids_ref):
    ids = ids_ref[...]
    rows = ids.shape[1]

    def look(s, slot):
        return jnp.where(ids == s, slots_ref[s], slot)

    slot = lax.fori_loop(0, slots_ref.shape[0], look, jnp.zeros_like(ids), unroll=8)
    owner = lax.div(slot, held)
    local = slot - owner * held
    hits = owner == lax.broadcasted_iota(jnp.int32, (owners, rows), 0)
    earlier = lax.broadcasted_iota(jnp.int32, (rows, rows), 0) < lax.broadcasted_iota(
        jnp.int32, (rows, rows), 1
    )
    before = jnp.dot(
        hits.astype(jnp.bfloat16), earlier.astype(jnp.bfloat16), preferred_element_type=jnp.float32
    )
    place = jnp.sum(jnp.where(hits, before, 0.0), axis=0, keepdims=True).astype(jnp.int32)
    bins = owner * slot_count + place
    routed = bins == lax.broadcasted_iota(jnp.int32, (owners * slot_count, rows), 0)
    label = jnp.sum(jnp.where(routed, local.astype(jnp.float32), 0.0), axis=1, keepdims=True)
    return routed.astype(jnp.bfloat16), label


def pack_kernel(
    owners, slot_count, held, slots_ref, ids_ref, hidden_ref, packed_ref, routed_ref, rows_ref, bins_ref, sems, out_sems
):
    width = hidden_ref.shape[1]
    spans = [pl.ds(at, min(COLUMNS_STEP, width - at)) for at in range(0, width, COLUMNS_STEP)]
    loads = [
        pltpu.make_async_copy(hidden_ref.at[:, span], rows_ref.at[:, span], sems.at[i])
        for i, span in enumerate(spans)
    ]
    spans[-1] = pl.ds(spans[-1].start, spans[-1].size + LANES)
    stores = [
        pltpu.make_async_copy(bins_ref.at[:, span], packed_ref.at[:, span], out_sems.at[i])
        for i, span in enumerate(spans)
    ]
    for load in loads:
        load.start()
    routed, label = routing(owners, slot_count, held, slots_ref, ids_ref)
    routed_ref[...] = jnp.transpose(routed.astype(jnp.float32)).astype(routed_ref.dtype)
    bins_ref[:, width:] = jnp.broadcast_to(label, (label.shape[0], LANES)).astype(bins_ref.dtype)
    for load, store, span in zip(loads, stores, spans):
        load.wait()
        at, end = span.start, min(span.start + span.size, width)
        bins_ref[:, at:end] = jnp.dot(
            routed, rows_ref[:, at:end], preferred_element_type=jnp.float32
        ).astype(bins_ref.dtype)
        store.start()
    for store in stores:
        store.wait()


def pack(hidden, adapter_id, adapter_slot, owners, slot_count, held):
    rows, width = hidden.shape
    bins = owners * slot_count
    steps = pl.cdiv(width, COLUMNS_STEP)
    return pl.pallas_call(
        functools.partial(pack_kernel, owners, slot_count, held),
        in_specs=[
            pl.BlockSpec(memory_space=pltpu.SMEM),
            pl.BlockSpec(memory_space=pltpu.VMEM),
            pl.BlockSpec(memory_space=pl.ANY),
        ],
        out_specs=[pl.BlockSpec(memory_space=pl.ANY), pl.BlockSpec(memory_space=pltpu.VMEM)],
        out_shape=[
            jax.ShapeDtypeStruct((bins, width + LANES), hidden.dtype),
            jax.ShapeDtypeStruct((rows, bins), jnp.bfloat16),
        ],
        scratch_shapes=[
            pltpu.VMEM((rows, width), hidden.dtype),
            pltpu.VMEM((bins, width + LANES), hidden.dtype),
            pltpu.SemaphoreType.DMA((steps,)),
            pltpu.SemaphoreType.DMA((steps,)),
        ],
        compiler_params=pltpu.CompilerParams(vmem_limit_bytes=56 * 2**20),
        name="pack",
    )(adapter_slot, adapter_id.reshape(1, rows), hidden)


def adapt_kernel(arrived_ref, a_ref, b_ref, change_ref):
    width = a_ref.shape[0]
    low = jnp.zeros((arrived_ref.shape[0], a_ref.shape[1]), jnp.float32)
    for at in range(0, width, COLUMNS_STEP):
        low += jnp.dot(
            arrived_ref[:, at : at + COLUMNS_STEP],
            a_ref[at : at + COLUMNS_STEP, :],
            preferred_element_type=jnp.float32,
        )
    label = arrived_ref[:, width:].astype(jnp.float32)[:, :1].astype(jnp.int32)
    column = lax.broadcasted_iota(jnp.int32, low.shape, 1) // RANK
    low = jnp.where(column == label, low, 0.0).astype(jnp.bfloat16)
    out_width = b_ref.shape[1]
    piece = min(1024, out_width)
    for at in range(0, out_width, piece):
        change_ref[:, at : at + piece] = (
            SCALE * jnp.dot(low, b_ref[:, at : at + piece], preferred_element_type=jnp.float32)
        ).astype(change_ref.dtype)


def adapt(arrived, a_maps, b_maps):
    return pl.pallas_call(
        adapt_kernel,
        in_specs=[pl.BlockSpec(memory_space=pltpu.VMEM)] * 3,
        out_specs=pl.BlockSpec(memory_space=pltpu.VMEM),
        out_shape=jax.ShapeDtypeStruct((arrived.shape[0], b_maps.shape[1]), jnp.bfloat16),
        compiler_params=pltpu.CompilerParams(vmem_limit_bytes=16 * 2**20),
        name="adapt",
    )(arrived, a_maps, b_maps)


def tall(rows, group):
    return jnp.concatenate([rows[:, g * HEAD : (g + 1) * HEAD] for g in range(group)], axis=0)


def prep_kernel(group, context, base_ref, kv_ref, len_ref, keys_ref, values_ref, scores_ref):
    step = ROWS_STEP
    cells = step * context
    lane = lax.broadcasted_iota(jnp.int32, (group * step, cells), 1)
    line = lax.broadcasted_iota(jnp.int32, (group * step, cells), 0)
    live = (lane // context == lax.rem(line, step)) & (lax.rem(lane, context) < len_ref[...][0])
    factor = 1.0 / jnp.sqrt(jnp.float32(HEAD))
    for k in range(KVH):
        head = slice(k * HEAD, (k + 1) * HEAD)
        keys = kv_ref[:, 0, :, head].astype(jnp.float32).reshape(cells, HEAD)
        keys = jnp.transpose(keys).astype(keys_ref.dtype)
        keys_ref[k] = keys
        values_ref[k] = kv_ref[:, 1, :, head].reshape(cells, HEAD)
        base = base_ref[:, k * group * HEAD : (k + 1) * group * HEAD].astype(jnp.float32)
        scores = jnp.dot(
            tall(base, group).astype(jnp.bfloat16), keys, preferred_element_type=jnp.float32
        )
        scores_ref[k, 0] = jnp.where(live, scores * factor, -jnp.inf)


def prep(base_q, kv_cache, cache_len):
    rows, width = base_q.shape
    context = kv_cache.shape[2]
    group = width // (KVH * HEAD)
    step = ROWS_STEP
    steps = rows // step
    cells = step * context
    lens = jnp.repeat(cache_len, context).reshape(steps, 1, cells)
    return pl.pallas_call(
        functools.partial(prep_kernel, group, context),
        grid=(steps,),
        in_specs=[
            pl.BlockSpec((step, width), lambda i: (i, 0)),
            pl.BlockSpec((step, *kv_cache.shape[1:]), lambda i: (i, 0, 0, 0)),
            pl.BlockSpec((1, 1, cells), lambda i: (i, 0, 0)),
        ],
        out_specs=[
            pl.BlockSpec((KVH, HEAD, cells), lambda i: (0, 0, i)),
            pl.BlockSpec((KVH, cells, HEAD), lambda i: (0, i, 0)),
            pl.BlockSpec((KVH, 1, group * step, cells), lambda i: (0, i, 0, 0)),
        ],
        out_shape=[
            jax.ShapeDtypeStruct((KVH, HEAD, rows * context), jnp.bfloat16),
            jax.ShapeDtypeStruct((KVH, rows * context, HEAD), jnp.bfloat16),
            jax.ShapeDtypeStruct((KVH, steps, group * step, cells), jnp.float32),
        ],
        compiler_params=pltpu.CompilerParams(vmem_limit_bytes=16 * 2**20),
        cost_estimate=pl.CostEstimate(
            flops=2 * rows * width * cells, bytes_accessed=16 * 2**20, transcendentals=0
        ),
        name="prep",
    )(base_q, kv_cache, lens)


def attend_kernel(group, routed_ref, returned_ref, keys_ref, values_ref, scores_ref, out_ref):
    step = ROWS_STEP
    steps, _, cells = scores_ref.shape[1:]
    span = group * HEAD
    factor = 1.0 / jnp.sqrt(jnp.float32(HEAD))
    for k in range(KVH):
        delta = jnp.dot(
            routed_ref[...],
            returned_ref[:, k * span : (k + 1) * span],
            preferred_element_type=jnp.float32,
        )
        for i in range(steps):
            lines = slice(i * step, (i + 1) * step)
            at = slice(i * cells, (i + 1) * cells)
            change = jnp.dot(
                tall(delta[lines], group).astype(jnp.bfloat16),
                keys_ref[k, :, at],
                preferred_element_type=jnp.float32,
            )
            scores = scores_ref[k, i] + change * factor
            expo = jnp.exp(scores - jnp.max(scores, axis=1, keepdims=True))
            probs = expo * (1.0 / jnp.sum(expo, axis=1, keepdims=True))
            out = jnp.dot(
                probs.astype(jnp.bfloat16), values_ref[k, at, :], preferred_element_type=jnp.float32
            )
            for g in range(group):
                out_ref[lines, (k * group + g) * HEAD : (k * group + g + 1) * HEAD] = out[
                    g * step : (g + 1) * step
                ].astype(out_ref.dtype)


def attend(routed, returned, keys, values, scores):
    rows, width = routed.shape[0], returned.shape[1]
    return pl.pallas_call(
        functools.partial(attend_kernel, width // (KVH * HEAD)),
        in_specs=[pl.BlockSpec(memory_space=pltpu.VMEM)] * 5,
        out_specs=pl.BlockSpec(memory_space=pltpu.VMEM),
        out_shape=jax.ShapeDtypeStruct((rows, width), jnp.bfloat16),
        compiler_params=pltpu.CompilerParams(vmem_limit_bytes=24 * 2**20),
        name="attend",
    )(routed, returned, keys, values, scores)


def on_device(hidden, adapter_id, adapter_slot, cache_len, base_q, kv_cache, a_maps, b_maps):
    owners = lax.axis_size("owner")
    rows = hidden.shape[0]
    held = a_maps.shape[1] // RANK
    slot_count = max(2, 2 * ((rows + 2 * owners - 1) // (2 * owners)))
    bins = owners * slot_count
    packed, routed = pack(hidden, adapter_id, adapter_slot, owners, slot_count, held)
    packed = packed.reshape(owners, slot_count, packed.shape[1])
    arrived = lax.all_to_all(packed, "owner", split_axis=0, concat_axis=0, tiled=True)
    keys, values, scores = prep(base_q, kv_cache, cache_len)
    change = adapt(arrived.reshape(bins, arrived.shape[2]), a_maps, b_maps)
    change = change.reshape(owners, slot_count, change.shape[1])
    returned = lax.all_to_all(change, "owner", split_axis=0, concat_axis=0, tiled=True)
    return attend(routed, returned.reshape(bins, returned.shape[2]), keys, values, scores)


def solution(mesh):
    return jax.shard_map(
        on_device,
        mesh=mesh,
        in_specs=(
            P(("groups", "owner"), None),
            P(("groups", "owner")),
            P("groups"),
            P(("groups", "owner")),
            P(("groups", "owner"), None),
            P(("groups", "owner"), None, None, None),
            P(None, "owner"),
            P("owner", None),
        ),
        out_specs=P(("groups", "owner"), None),
        check_vma=False,
    )
```

time: 109 us -> 101 us (0.927)
  waiting for transfers between devices: 22.6 us -> 11.6 us
  local copies, waits for them, and re-layouts: 5.36 us -> 9.5 us
  Pallas kernels: 17.7 us -> 16.1 us
    all_to_all x1, waiting for transfers between devices: 22.6 us -> 11.6 us  [on_device(): lax.all_to_all(change, 'owner', split_axis=0, concat_axis=0, tiled=True)]
    unnamed x16 -> x20, local copies, waits for them, and re-layouts: 5.11 us -> 9.24 us
    pallas_call x2 -> x3, Pallas kernels: 15.1 us -> 11.7 us  [the longest x1 4.99 us: prep(): pl.pallas_call(functools.partial(prep_kernel, group, context), grid=(step...]
    pallas_call x1, Pallas kernels: 2.65 us -> 4.38 us  [pack(): pl.pallas_call(functools.partial(pack_kernel, owners, slot_count, held),...]
  transfers between devices with their start and end apart: 1 -> 1, of which waited for: 1 -> 1; matrix products, arithmetic and copies ran while one was open for 0% -> 0% of each run, Pallas kernels for 0% -> 5%
where the time goes in v3:
time: 101 us; the launch traced here: 99.1 us
  blocking collectives  58.1 us (58%)
  Pallas kernels  16.1 us (16%)
  waiting for transfers between devices  11.6 us (11%)
  local copies, waits for them, and re-layouts  9.5 us (9%)
  starting transfers between devices  3.79 us (4%)
    all_to_all x1, blocking collectives, on_device(): lax.all_to_all(packed, 'owner', split_axis=0, concat_axis=0, tiled=True)  58.1 us
    all_to_all x1, waiting for transfers between devices, on_device(): lax.all_to_all(change, 'owner', split_axis=0, concat_axis=0, tiled=True)  11.6 us
    unnamed x20, local copies, waits for them, and re-layouts  9.24 us
    pallas_call x1, Pallas kernels, prep(): pl.pallas_call(functools.partial(prep_kernel, group, context), grid=(step...  4.99 us
    pallas_call x1, Pallas kernels, attend(): pl.pallas_call(functools.partial(attend_kernel, width // (KVH * HEAD)), i...  4.69 us
    pallas_call x1, Pallas kernels, pack(): pl.pallas_call(functools.partial(pack_kernel, owners, slot_count, held),...  4.38 us
    all_to_all x1, starting transfers between devices, on_device(): lax.all_to_all(change, 'owner', split_axis=0, concat_axis=0, tiled=True)  3.79 us
    pallas_call x1, Pallas kernels, adapt(): pl.pallas_call(adapt_kernel, in_specs=[pl.BlockSpec(memory_space=pltpu.VM...  2.05 us
  transfers between devices with their start and end apart: 1, of which 1 were waited for; matrix products, arithmetic and copies ran while one was open for 0% of the time, Pallas kernels for 5%

profile of v3, /device:TPU:0, one launch (start us, length us, event | category | flops | bytes accessed | tf_op | source)
XLA Modules:
  0.0 99.1 jit_solution(2938361469231974462)
XLA Ops:
  0.0 4.4 %pack.1 = (bf16[128,8320]{1,0:T(8,128)(2,1)}, bf16[128,128]{1,0:T(8,128)(2,1)}) custom-call(s32[32]{0:T(128)} %slots_ref.1, s32[1,128]{1,0:T(1,128)} %bitcast.8, bf16[128,8192]{1,0:T(8,128)(2,1)} %hidden_ref.1), custom_call_target="tpu_custom_call" | custom-call | tf_op jit(solution)/shard_map/pack/pallas_call | solution.py:77
  4.4 0.0 copy-start.1
  4.4 0.0 copy-start.7
  4.4 58.1 %all_to_all.10 = bf16[16,8,8320]{2,1,0:T(8,128)(2,1)S(1)} all-to-all(bf16[16,8,8320]{2,1,0:T(8,128)(2,1)} %bitcast.7), channel_id=1, replica_groups=mesh['groups'=2,'owner'=16] {'owner'}, dimensions={0} | all-to-all | bytes 4259840 | tf_op jit(solution)/shard_map/all_to_all | solution.py:240
  62.5 0.0 copy-done.1
  62.5 0.0 copy-done.7
  62.5 2.0 %adapt.1 = bf16[128,4096]{1,0:T(8,128)(2,1)} custom-call(bf16[128,8320]{1,0:T(8,128)(2,1)S(1)} %bitcast.5, bf16[8192,128]{1,0:T(8,128)(2,1)S(1)} %copy-done.1, bf16[128,4096]{1,0:T(8,128)(2,1)S(1)} %copy-done.7), custom_call_target="tpu_custom_call" | custom-call | tf_op jit(solution)/shard_map/adapt/pallas_call | solution.py:121
  64.5 0.0 copy-start.9
  64.5 3.8 %all-to-all-start.1 = ((bf16[16,8,4096]{2,1,0:T(8,128)(2,1)}), bf16[16,8,4096]{2,1,0:T(8,128)(2,1)S(1)}, u32[]{:S(2)}, u32[]{:S(2)}) async-start(bf16[16,8,4096]{2,1,0:T(8,128)(2,1)} %bitcast.3), calls=%async_computation.1 | async-start | bytes 2097152 | tf_op jit(solution)/shard_map/all_to_all | solution.py:244
  68.3 0.0 copy-done.9
  68.4 0.1 broadcast_in_dim.7
  68.4 0.1 broadcast_in_dim.8
  68.5 0.1 broadcast_in_dim.9.len_ref
  68.6 0.0 copy-start
  68.6 2.2 %copy-done = bf16[128,2,16,512]{3,2,1,0:T(8,128)(2,1)S(1)} copy-done((bf16[128,2,16,512]{3,2,1,0:T(8,128)(2,1)S(1)}, bf16[128,2,16,512]{3,2,1,0:T(8,128)(2,1)}, u32[]{:S(2)}) %copy-start) | copy-done | bytes 4194328
  70.8 0.0 copy-start.6
  70.8 1.2 %copy-done.6 = bf16[128,4096]{1,0:T(8,128)(2,1)S(1)} copy-done((bf16[128,4096]{1,0:T(8,128)(2,1)S(1)}, bf16[128,4096]{1,0:T(8,128)(2,1)}, u32[]{:S(2)}) %copy-start.6) | copy-done | bytes 1048600
  72.0 0.0 copy-start.8
  72.0 5.0 %prep.1 = (bf16[4,128,2048]{2,1,0:T(8,128)(2,1)S(1)}, bf16[4,2048,128]{2,1,0:T(8,128)(2,1)S(1)}, f32[4,16,64,128]{3,2,1,0:T(8,128)S(1)}) custom-call(bf16[128,4096]{1,0:T(8,128)(2,1)S(1)} %copy-done.6, bf16[128,2,16,512]{3,2,1,0:T(8,128)(2,1)S(1)} %copy-done, s32[16,1,128]{2,1,0:T(1,128)S(1)} %broadcast_in_dim.9.len_ref), custom_call_target="tpu_custom_call" | custom-call | flops 134217728 | bytes 16777216 | tf_op jit(solution)/shard_map/prep/pallas_call | solution.py:163
  77.0 0.0 copy-start.2
  77.0 1.3 %copy-done.2 = bf16[4,2048,128]{2,1,0:T(8,128)(2,1)} copy-done((bf16[4,2048,128]{2,1,0:T(8,128)(2,1)}, bf16[4,2048,128]{2,1,0:T(8,128)(2,1)S(1)}, u32[]{:S(2)}) %copy-start.2) | copy-done | bytes 2097176
  78.4 0.0 copy-start.4
  78.4 1.3 %copy-done.4 = f32[4,16,64,128]{3,2,1,0:T(8,128)} copy-done((f32[4,16,64,128]{3,2,1,0:T(8,128)}, f32[4,16,64,128]{3,2,1,0:T(8,128)S(1)}, u32[]{:S(2)}) %copy-start.4) | copy-done | bytes 2097176
  79.7 11.6 %all-to-all-done.1 = bf16[16,8,4096]{2,1,0:T(8,128)(2,1)S(1)} async-done(((bf16[16,8,4096]{2,1,0:T(8,128)(2,1)}), bf16[16,8,4096]{2,1,0:T(8,128)(2,1)S(1)}, u32[]{:S(2)}, u32[]{:S(2)}) %all-to-all-start.1) | async-done | bytes 1048608 | tf_op jit(solution)/shard_map/all_to_all | solution.py:244
  91.2 0.0 copy-done.8
  91.2 0.0 copy-start.3
  91.2 1.6 %copy-done.3 = bf16[4,2048,128]{2,1,0:T(8,128)(2,1)S(1)} copy-done((bf16[4,2048,128]{2,1,0:T(8,128)(2,1)S(1)}, bf16[4,2048,128]{2,1,0:T(8,128)(2,1)}, u32[]{:S(2)}) %copy-start.3) | copy-done | bytes 2097176
  92.8 0.0 copy-start.5
  92.8 1.6 %copy-done.5 = f32[4,16,64,128]{3,2,1,0:T(8,128)S(1)} copy-done((f32[4,16,64,128]{3,2,1,0:T(8,128)S(1)}, f32[4,16,64,128]{3,2,1,0:T(8,128)}, u32[]{:S(2)}) %copy-start.5) | copy-done | bytes 2097176
  94.4 4.7 %attend.1 = bf16[128,4096]{1,0:T(8,128)(2,1)} custom-call(bf16[128,128]{1,0:T(8,128)(2,1)S(1)} %copy-done.8, bf16[128,4096]{1,0:T(8,128)(2,1)S(1)} %bitcast.6, bf16[4,128,2048]{2,1,0:T(8,128)(2,1)S(1)} %get-tuple-element.12.keys_ref, bf16[4,2048,128]{2,1,0:T(8,128)(2,1)S(1)} %copy-done.3, f32[4,16,64,128]{3,2,1,0:T(8,128)S(1)} %copy-done.5), custom_call_target="tpu_custom_call" | custom-call | tf_op jit(solution)/shard_map/attend/pallas_call | solution.py:222
Async XLA Ops:
  4.4 58.1 %copy-start.1 = (bf16[8192,128]{1,0:T(8,128)(2,1)S(1)}, bf16[8192,128]{1,0:T(8,128)(2,1)}, u32[]{:S(2)}) copy-start(bf16[8192,128]{1,0:T(8,128)(2,1)} %a_ref.1) | copy-start | bytes 6291460
  4.4 58.1 %copy-start.7 = (bf16[128,4096]{1,0:T(8,128)(2,1)S(1)}, bf16[128,4096]{1,0:T(8,128)(2,1)}, u32[]{:S(2)}) copy-start(bf16[128,4096]{1,0:T(8,128)(2,1)} %b_ref.1) | copy-start | bytes 3145732
  64.5 3.8 %copy-start.9 = (s32[128]{0:T(128)S(1)}, s32[128]{0:T(128)}, u32[]{:S(2)}) copy-start(s32[128]{0:T(128)} %param.11) | copy-start | bytes 1540
  64.5 26.7 %all-to-all-start.1 = ((bf16[16,8,4096]{2,1,0:T(8,128)(2,1)}), bf16[16,8,4096]{2,1,0:T(8,128)(2,1)S(1)}, u32[]{:S(2)}, u32[]{:S(2)}) async-start(bf16[16,8,4096]{2,1,0:T(8,128)(2,1)} %bitcast.3), calls=%async_computation.1 | async-start | bytes 2097152 | tf_op jit(solution)/shard_map/all_to_all | solution.py:244
  68.6 2.2 %copy-start = (bf16[128,2,16,512]{3,2,1,0:T(8,128)(2,1)S(1)}, bf16[128,2,16,512]{3,2,1,0:T(8,128)(2,1)}, u32[]{:S(2)}) copy-start(bf16[128,2,16,512]{3,2,1,0:T(8,128)(2,1)} %kv_ref.1) | copy-start | bytes 12582916
  70.8 1.2 %copy-start.6 = (bf16[128,4096]{1,0:T(8,128)(2,1)S(1)}, bf16[128,4096]{1,0:T(8,128)(2,1)}, u32[]{:S(2)}) copy-start(bf16[128,4096]{1,0:T(8,128)(2,1)} %base_ref.1) | copy-start | bytes 3145732
  72.0 19.2 %copy-start.8 = (bf16[128,128]{1,0:T(8,128)(2,1)S(1)}, bf16[128,128]{1,0:T(8,128)(2,1)}, u32[]{:S(2)}) copy-start(bf16[128,128]{1,0:T(8,128)(2,1)} %get-tuple-element.10.routed_ref) | copy-start | bytes 98308
  77.0 1.3 %copy-start.2 = (bf16[4,2048,128]{2,1,0:T(8,128)(2,1)}, bf16[4,2048,128]{2,1,0:T(8,128)(2,1)S(1)}, u32[]{:S(2)}) copy-start(bf16[4,2048,128]{2,1,0:T(8,128)(2,1)S(1)} %get-tuple-element.13.values_ref) | copy-start | bytes 6291460
  78.4 1.3 %copy-start.4 = (f32[4,16,64,128]{3,2,1,0:T(8,128)}, f32[4,16,64,128]{3,2,1,0:T(8,128)S(1)}, u32[]{:S(2)}) copy-start(f32[4,16,64,128]{3,2,1,0:T(8,128)S(1)} %get-tuple-element.14.scores_ref) | copy-start | bytes 6291460
  91.2 1.6 %copy-start.3 = (bf16[4,2048,128]{2,1,0:T(8,128)(2,1)S(1)}, bf16[4,2048,128]{2,1,0:T(8,128)(2,1)}, u32[]{:S(2)}) copy-start(bf16[4,2048,128]{2,1,0:T(8,128)(2,1)} %copy-done.2) | copy-start | bytes 6291460
  92.8 1.6 %copy-start.5 = (f32[4,16,64,128]{3,2,1,0:T(8,128)S(1)}, f32[4,16,64,128]{3,2,1,0:T(8,128)}, u32[]{:S(2)}) copy-start(f32[4,16,64,128]{3,2,1,0:T(8,128)} %copy-done.4) | copy-start | bytes 6291460

commit v4 on v3

--- a/solution.py
+++ b/solution.py
@@ -14,11 +14,19 @@
 SCALE = 2.0
 ROWS_STEP = 8
 COLUMNS_STEP = 2048
-
-
-def routing(owners, slot_count, held, slots_ref, ids_ref):
+HALVES = 2
+
+
+def fold_of(bins, slot_count, columns):
+    line = lax.broadcasted_iota(jnp.int32, (bins, columns), 0)
+    return lax.rem(line, slot_count) // (slot_count // HALVES)
+
+
+def routing(chunk, owners, slot_count, held, slots_ref, ids_ref):
     ids = ids_ref[...]
     rows = ids.shape[1]
+    bins = owners * slot_count
+    part = slot_count // HALVES
 
     def look(s, slot):
         return jnp.where(ids == s, slots_ref[s], slot)
@@ -34,48 +42,63 @@
         hits.astype(jnp.bfloat16), earlier.astype(jnp.bfloat16), preferred_element_type=jnp.float32
     )
     place = jnp.sum(jnp.where(hits, before, 0.0), axis=0, keepdims=True).astype(jnp.int32)
-    bins = owner * slot_count + place
-    routed = bins == lax.broadcasted_iota(jnp.int32, (owners * slot_count, rows), 0)
+    line = lax.broadcasted_iota(jnp.int32, (bins, rows), 0)
+    fold = fold_of(bins, slot_count, rows)
+    routed = line + (chunk - fold) * part == owner * slot_count + place
     label = jnp.sum(jnp.where(routed, local.astype(jnp.float32), 0.0), axis=1, keepdims=True)
-    return routed.astype(jnp.bfloat16), label
+    return [(routed & (fold == f)).astype(jnp.float32) for f in range(HALVES)], label
 
 
 def pack_kernel(
-    owners, slot_count, held, slots_ref, ids_ref, hidden_ref, packed_ref, routed_ref, rows_ref, bins_ref, sems, out_sems
+    chunk, owners, slot_count, held, slots_ref, ids_ref, hidden_ref, packed_ref, routed_ref, rows_ref, bins_ref, sems, out_sems
 ):
-    width = hidden_ref.shape[1]
-    spans = [pl.ds(at, min(COLUMNS_STEP, width - at)) for at in range(0, width, COLUMNS_STEP)]
+    rows, width = hidden_ref.shape
+    half = width // HALVES
+    spans = [(at, min(COLUMNS_STEP, half - at)) for at in range(0, half, COLUMNS_STEP)]
     loads = [
-        pltpu.make_async_copy(hidden_ref.at[:, span], rows_ref.at[:, span], sems.at[i])
-        for i, span in enumerate(spans)
+        [
+            pltpu.make_async_copy(
+                hidden_ref.at[:, pl.ds(f * half + at, size)],
+                rows_ref.at[pl.ds(f * rows, rows), pl.ds(at, size)],
+                sems.at[i, f],
+            )
+            for f in range(HALVES)
+        ]
+        for i, (at, size) in enumerate(spans)
     ]
-    spans[-1] = pl.ds(spans[-1].start, spans[-1].size + LANES)
     stores = [
-        pltpu.make_async_copy(bins_ref.at[:, span], packed_ref.at[:, span], out_sems.at[i])
-        for i, span in enumerate(spans)
+        pltpu.make_async_copy(
+            bins_ref.at[:, pl.ds(at, size)], packed_ref.at[:, pl.ds(at, size)], out_sems.at[i]
+        )
+        for i, (at, size) in enumerate([(half, LANES)] + spans)
     ]
     for load in loads:
-        load.start()
-    routed, label = routing(owners, slot_count, held, slots_ref, ids_ref)
-    routed_ref[...] = jnp.transpose(routed.astype(jnp.float32)).astype(routed_ref.dtype)
-    bins_ref[:, width:] = jnp.broadcast_to(label, (label.shape[0], LANES)).astype(bins_ref.dtype)
-    for load, store, span in zip(loads, stores, spans):
-        load.wait()
-        at, end = span.start, min(span.start + span.size, width)
-        bins_ref[:, at:end] = jnp.dot(
-            routed, rows_ref[:, at:end], preferred_element_type=jnp.float32
+        for copy in load:
+            copy.start()
+    routed, label = routing(chunk, owners, slot_count, held, slots_ref, ids_ref)
+    bins_ref[:, half:] = jnp.broadcast_to(label, (label.shape[0], LANES)).astype(bins_ref.dtype)
+    stores[0].start()
+    folded = jnp.concatenate(routed, axis=1).astype(jnp.bfloat16)
+    for load, store, (at, size) in zip(loads, stores[1:], spans):
+        for copy in load:
+            copy.wait()
+        bins_ref[:, at : at + size] = jnp.dot(
+            folded, rows_ref[:, at : at + size], preferred_element_type=jnp.float32
         ).astype(bins_ref.dtype)
         store.start()
+    for f in range(HALVES):
+        routed_ref[f] = jnp.transpose(routed[f]).astype(routed_ref.dtype)
     for store in stores:
         store.wait()
 
 
-def pack(hidden, adapter_id, adapter_slot, owners, slot_count, held):
+def pack(hidden, adapter_id, adapter_slot, chunk, owners, slot_count, held):
     rows, width = hidden.shape
+    half = width // HALVES
     bins = owners * slot_count
-    steps = pl.cdiv(width, COLUMNS_STEP)
+    steps = pl.cdiv(half, COLUMNS_STEP)
     return pl.pallas_call(
-        functools.partial(pack_kernel, owners, slot_count, held),
+        functools.partial(pack_kernel, chunk, owners, slot_count, held),
         in_specs=[
             pl.BlockSpec(memory_space=pltpu.SMEM),
             pl.BlockSpec(memory_space=pltpu.VMEM),
@@ -83,47 +106,63 @@
         ],
         out_specs=[pl.BlockSpec(memory_space=pl.ANY), pl.BlockSpec(memory_space=pltpu.VMEM)],
         out_shape=[
-            jax.ShapeDtypeStruct((bins, width + LANES), hidden.dtype),
-            jax.ShapeDtypeStruct((rows, bins), jnp.bfloat16),
+            jax.ShapeDtypeStruct((bins, half + LANES), hidden.dtype),
+            jax.ShapeDtypeStruct((HALVES, rows, bins), jnp.bfloat16),
         ],
         scratch_shapes=[
-            pltpu.VMEM((rows, width), hidden.dtype),
-            pltpu.VMEM((bins, width + LANES), hidden.dtype),
-            pltpu.SemaphoreType.DMA((steps,)),
-            pltpu.SemaphoreType.DMA((steps,)),
+            pltpu.VMEM((HALVES * rows, half), hidden.dtype),
+            pltpu.VMEM((bins, half + LANES), hidden.dtype),
+            pltpu.SemaphoreType.DMA((steps, HALVES)),
+            pltpu.SemaphoreType.DMA((steps + 1,)),
         ],
         compiler_params=pltpu.CompilerParams(vmem_limit_bytes=56 * 2**20),
         name="pack",
     )(adapter_slot, adapter_id.reshape(1, rows), hidden)
 
 
-def adapt_kernel(arrived_ref, a_ref, b_ref, change_ref):
-    width = a_ref.shape[0]
-    low = jnp.zeros((arrived_ref.shape[0], a_ref.shape[1]), jnp.float32)
-    for at in range(0, width, COLUMNS_STEP):
-        low += jnp.dot(
+def adapt_kernel(slot_count, arrived_ref, a_ref, b_ref, change_ref):
+    bins = arrived_ref.shape[0]
+    half = a_ref.shape[0] // HALVES
+    columns = a_ref.shape[1]
+    part = slot_count // HALVES
+    both = jnp.zeros((bins, HALVES * columns), jnp.float32)
+    for at in range(0, half, COLUMNS_STEP):
+        both += jnp.dot(
             arrived_ref[:, at : at + COLUMNS_STEP],
-            a_ref[at : at + COLUMNS_STEP, :],
+            jnp.concatenate(
+                [a_ref[f * half + at : f * half + at + COLUMNS_STEP, :] for f in range(HALVES)], axis=1
+            ),
             preferred_element_type=jnp.float32,
         )
-    label = arrived_ref[:, width:].astype(jnp.float32)[:, :1].astype(jnp.int32)
+    upper = fold_of(bins, slot_count, columns) == 0
+    low = jnp.where(upper, both[:, :columns], both[:, columns:])
+    low += jnp.where(upper, pltpu.roll(low, bins - part, 0), pltpu.roll(low, part, 0))
+    label = arrived_ref[:, half:].astype(jnp.float32)[:, :1].astype(jnp.int32)
     column = lax.broadcasted_iota(jnp.int32, low.shape, 1) // RANK
-    low = jnp.where(column == label, low, 0.0).astype(jnp.bfloat16)
-    out_width = b_ref.shape[1]
-    piece = min(1024, out_width)
-    for at in range(0, out_width, piece):
+    low = jnp.where(column == label, low, 0.0)
+    low = jnp.concatenate([jnp.where(upper, low, 0.0), jnp.where(upper, 0.0, low)], axis=1)
+    low = low.astype(jnp.bfloat16)
+    half_out = b_ref.shape[1] // HALVES
+    piece = min(1024, half_out)
+    for at in range(0, half_out, piece):
+        b = jnp.concatenate(
+            [b_ref[:, f * half_out + at : f * half_out + at + piece] for f in range(HALVES)], axis=0
+        )
         change_ref[:, at : at + piece] = (
-            SCALE * jnp.dot(low, b_ref[:, at : at + piece], preferred_element_type=jnp.float32)
+            SCALE * jnp.dot(low, b, preferred_element_type=jnp.float32)
         ).astype(change_ref.dtype)
 
 
-def adapt(arrived, a_maps, b_maps):
+def adapt(arrived, a_maps, b_maps, slot_count):
     return pl.pallas_call(
-        adapt_kernel,
+        functools.partial(adapt_kernel, slot_count),
         in_specs=[pl.BlockSpec(memory_space=pltpu.VMEM)] * 3,
         out_specs=pl.BlockSpec(memory_space=pltpu.VMEM),
-        out_shape=jax.ShapeDtypeStruct((arrived.shape[0], b_maps.shape[1]), jnp.bfloat16),
+        out_shape=jax.ShapeDtypeStruct((arrived.shape[0], b_maps.shape[1] // HALVES), jnp.bfloat16),
         compiler_params=pltpu.CompilerParams(vmem_limit_bytes=16 * 2**20),
+        cost_estimate=pl.CostEstimate(
+            flops=4 * arrived.shape[0] * a_maps.size, bytes_accessed=4 * 2**20, transcendentals=0
+        ),
         name="adapt",
     )(arrived, a_maps, b_maps)
 
@@ -186,17 +225,36 @@
     )(base_q, kv_cache, lens)
 
 
-def attend_kernel(group, routed_ref, returned_ref, keys_ref, values_ref, scores_ref, out_ref):
+def attend_kernel(group, *refs):
+    routed_refs, returned_refs, refs = refs[:HALVES], refs[HALVES : 2 * HALVES], refs[2 * HALVES :]
+    laid_refs, (out_ref, *held_refs, sems) = refs[:3], refs[3:]
+    keys_ref, values_ref, scores_ref = held_refs
     step = ROWS_STEP
     steps, _, cells = scores_ref.shape[1:]
     span = group * HEAD
+    heads = KVH // HALVES
     factor = 1.0 / jnp.sqrt(jnp.float32(HEAD))
+    copies = [
+        [
+            pltpu.make_async_copy(laid_ref.at[k], held_ref.at[k], sems.at[k, i])
+            for i, (laid_ref, held_ref) in enumerate(zip(laid_refs, held_refs))
+        ]
+        for k in range(KVH)
+    ]
+    for copy in copies:
+        for one in copy:
+            one.start()
     for k in range(KVH):
+        fold, at = k // heads, k % heads * span
         delta = jnp.dot(
-            routed_ref[...],
-            returned_ref[:, k * span : (k + 1) * span],
+            jnp.concatenate([routed_ref[fold] for routed_ref in routed_refs], axis=1),
+            jnp.concatenate(
+                [returned_ref[:, at : at + span] for returned_ref in returned_refs], axis=0
+            ),
             preferred_element_type=jnp.float32,
         )
+        for one in copies[k]:
+            one.wait()
         for i in range(steps):
             lines = slice(i * step, (i + 1) * step)
             at = slice(i * cells, (i + 1) * cells)
@@ -217,16 +275,19 @@
                 ].astype(out_ref.dtype)
 
 
-def attend(routed, returned, keys, values, scores):
-    rows, width = routed.shape[0], returned.shape[1]
+def attend(routed, returned, laid, width):
+    rows = routed[0].shape[1]
     return pl.pallas_call(
         functools.partial(attend_kernel, width // (KVH * HEAD)),
-        in_specs=[pl.BlockSpec(memory_space=pltpu.VMEM)] * 5,
+        in_specs=[pl.BlockSpec(memory_space=pltpu.VMEM)] * (2 * HALVES)
+        + [pl.BlockSpec(memory_space=pl.ANY)] * len(laid),
         out_specs=pl.BlockSpec(memory_space=pltpu.VMEM),
         out_shape=jax.ShapeDtypeStruct((rows, width), jnp.bfloat16),
-        compiler_params=pltpu.CompilerParams(vmem_limit_bytes=24 * 2**20),
+        scratch_shapes=[pltpu.VMEM(part.shape, part.dtype) for part in laid]
+        + [pltpu.SemaphoreType.DMA((KVH, len(laid)))],
+        compiler_params=pltpu.CompilerParams(vmem_limit_bytes=56 * 2**20),
         name="attend",
-    )(routed, returned, keys, values, scores)
+    )(*routed, *returned, *laid)
 
 
 def on_device(hidden, adapter_id, adapter_slot, cache_len, base_q, kv_cache, a_maps, b_maps):
@@ -234,15 +295,23 @@
     rows = hidden.shape[0]
     held = a_maps.shape[1] // RANK
     slot_count = max(2, 2 * ((rows + 2 * owners - 1) // (2 * owners)))
-    bins = owners * slot_count
-    packed, routed = pack(hidden, adapter_id, adapter_slot, owners, slot_count, held)
-    packed = packed.reshape(owners, slot_count, packed.shape[1])
-    arrived = lax.all_to_all(packed, "owner", split_axis=0, concat_axis=0, tiled=True)
-    keys, values, scores = prep(base_q, kv_cache, cache_len)
-    change = adapt(arrived.reshape(bins, arrived.shape[2]), a_maps, b_maps)
-    change = change.reshape(owners, slot_count, change.shape[1])
-    returned = lax.all_to_all(change, "owner", split_axis=0, concat_axis=0, tiled=True)
-    return attend(routed, returned.reshape(bins, returned.shape[2]), keys, values, scores)
+
+    def swap(message):
+        blocks = message.reshape(owners, slot_count, message.shape[1])
+        blocks = lax.all_to_all(blocks, "owner", split_axis=0, concat_axis=0, tiled=True)
+        return blocks.reshape(message.shape)
+
+    routed, arrived = [], []
+    for chunk in range(HALVES):
+        packed, hits = pack(hidden, adapter_id, adapter_slot, chunk, owners, slot_count, held)
+        routed.append(hits)
+        if chunk > 0:
+            arrived[0], packed = lax.optimization_barrier((arrived[0], packed))
+        arrived.append(swap(packed))
+    laid = prep(base_q, kv_cache, cache_len)
+    arrived[0], *laid = lax.optimization_barrier((arrived[0], *laid))
+    returned = [swap(adapt(rows_in, a_maps, b_maps, slot_count)) for rows_in in arrived]
+    return attend(routed, returned, laid, base_q.shape[1])
 
 
 def solution(mesh):

time: 101 us -> 114 us (1.13)
  blocking collectives: 58.1 us -> 18.5 us
  waiting for transfers between devices: 11.6 us -> 39.4 us
  starting transfers between devices: 3.79 us -> 21.4 us
  Pallas kernels: 16.1 us -> 23.9 us
    all_to_all x1, blocking collectives: 58.1 us -> 18.5 us  [swap(): lax.all_to_all(blocks, 'owner', split_axis=0, concat_axis=0, tiled=True)]
    all_to_all x1 -> x3, waiting for transfers between devices: 11.6 us -> 39.4 us  [swap(): lax.all_to_all(blocks, 'owner', split_axis=0, concat_axis=0, tiled=True)]
    all_to_all x1 -> x3, starting transfers between devices: 3.79 us -> 21.4 us  [swap(): lax.all_to_all(blocks, 'owner', split_axis=0, concat_axis=0, tiled=True)]
    pallas_call x2 -> x4, Pallas kernels: 6.42 us -> 11.3 us  [the longest x2 8.19 us: pack(): pl.pallas_call(functools.partial(pack_kernel, chunk, owners, slot_count,...]
    pallas_call x1, Pallas kernels: 4.69 us -> 7.55 us  [attend(): pl.pallas_call(functools.partial(attend_kernel, width // (KVH * HEAD)), i...]
    unnamed x20 -> x22, local copies, waits for them, and re-layouts: 9.24 us -> 9.44 us
  transfers between devices with their start and end apart: 1 -> 3, of which waited for: 1 -> 3; matrix products, arithmetic and copies ran while one was open for 0% -> 0% of each run, Pallas kernels for 5% -> 11%
where the time goes in v4:
time: 114 us; the launch traced here: 113 us
  waiting for transfers between devices  39.4 us (35%)
  Pallas kernels  23.9 us (21%)
  starting transfers between devices  21.4 us (19%)
  blocking collectives  18.5 us (16%)
  local copies, waits for them, and re-layouts  9.7 us (9%)
    all_to_all x3, waiting for transfers between devices, swap(): lax.all_to_all(blocks, 'owner', split_axis=0, concat_axis=0, tiled=True)  39.4 us
    all_to_all x3, starting transfers between devices, swap(): lax.all_to_all(blocks, 'owner', split_axis=0, concat_axis=0, tiled=True)  21.4 us
    all_to_all x1, blocking collectives, swap(): lax.all_to_all(blocks, 'owner', split_axis=0, concat_axis=0, tiled=True)  18.5 us
    unnamed x22, local copies, waits for them, and re-layouts  9.44 us
    pallas_call x2, Pallas kernels, pack(): pl.pallas_call(functools.partial(pack_kernel, chunk, owners, slot_count,...  8.19 us
    pallas_call x1, Pallas kernels, attend(): pl.pallas_call(functools.partial(attend_kernel, width // (KVH * HEAD)), i...  7.55 us
    pallas_call x1, Pallas kernels, prep(): pl.pallas_call(functools.partial(prep_kernel, group, context), grid=(step...  4.99 us
    pallas_call x2, Pallas kernels, adapt(): pl.pallas_call(functools.partial(adapt_kernel, slot_count), in_specs=[pl....  3.13 us
  transfers between devices with their start and end apart: 3, of which 3 were waited for; matrix products, arithmetic and copies ran while one was open for 0% of the time, Pallas kernels for 11%

profile of v4, /device:TPU:0, one launch (start us, length us, event | category | flops | bytes accessed | tf_op | source)
XLA Modules:
  0.0 113.0 jit_solution(8158877516437145596)
XLA Ops:
  0.0 4.0 %pack.2 = (bf16[128,4224]{1,0:T(8,128)(2,1)}, bf16[2,128,128]{2,1,0:T(8,128)(2,1)}) custom-call(s32[32]{0:T(128)} %slots_ref.3, s32[1,128]{1,0:T(1,128)} %bitcast.16, bf16[128,8192]{1,0:T(8,128)(2,1)} %hidden_ref.3), custom_call_target="tpu_custom_call" | custom-call | tf_op jit(solution)/shard_map/pack/pallas_call | solution.py:100
  4.0 7.4 %all-to-all-start = ((bf16[16,8,4224]{2,1,0:T(8,128)(2,1)}), bf16[16,8,4224]{2,1,0:T(8,128)(2,1)S(1)}, u32[]{:S(2)}, u32[]{:S(2)}) async-start(bf16[16,8,4224]{2,1,0:T(8,128)(2,1)} %bitcast.15), calls=%async_computation | async-start | bytes 2162688 | tf_op jit(solution)/shard_map/all_to_all | solution.py:301
  11.4 0.0 copy-start.10
  11.4 4.2 %pack.3 = (bf16[128,4224]{1,0:T(8,128)(2,1)}, bf16[2,128,128]{2,1,0:T(8,128)(2,1)}) custom-call(s32[32]{0:T(128)} %slots_ref.3, s32[1,128]{1,0:T(1,128)} %bitcast.17, bf16[128,8192]{1,0:T(8,128)(2,1)} %hidden_ref.3), custom_call_target="tpu_custom_call" | custom-call | tf_op jit(solution)/shard_map/pack/pallas_call | solution.py:100
  15.6 19.3 %all-to-all-done = bf16[16,8,4224]{2,1,0:T(8,128)(2,1)S(1)} async-done(((bf16[16,8,4224]{2,1,0:T(8,128)(2,1)}), bf16[16,8,4224]{2,1,0:T(8,128)(2,1)S(1)}, u32[]{:S(2)}, u32[]{:S(2)}) %all-to-all-start) | async-done | bytes 1081376 | tf_op jit(solution)/shard_map/all_to_all | solution.py:301
  34.9 7.1 %all-to-all-start.2 = ((bf16[16,8,4224]{2,1,0:T(8,128)(2,1)}), bf16[16,8,4224]{2,1,0:T(8,128)(2,1)}, u32[]{:S(2)}, u32[]{:S(2)}) async-start(bf16[16,8,4224]{2,1,0:T(8,128)(2,1)} %bitcast.14), calls=%async_computation.2 | async-start | bytes 2162688 | tf_op jit(solution)/shard_map/all_to_all | solution.py:301
  41.9 0.0 copy-done.10
  42.0 0.1 broadcast_in_dim.7
  42.0 0.1 broadcast_in_dim.8
  42.1 0.1 broadcast_in_dim.9.len_ref
  42.2 0.0 copy-start.1
  42.2 2.2 %copy-done.1 = bf16[128,2,16,512]{3,2,1,0:T(8,128)(2,1)S(1)} copy-done((bf16[128,2,16,512]{3,2,1,0:T(8,128)(2,1)S(1)}, bf16[128,2,16,512]{3,2,1,0:T(8,128)(2,1)}, u32[]{:S(2)}) %copy-start.1) | copy-done | bytes 4194328
  44.4 0.0 copy-start.8
  44.4 1.2 %copy-done.8 = bf16[128,4096]{1,0:T(8,128)(2,1)S(1)} copy-done((bf16[128,4096]{1,0:T(8,128)(2,1)S(1)}, bf16[128,4096]{1,0:T(8,128)(2,1)}, u32[]{:S(2)}) %copy-start.8) | copy-done | bytes 1048600
  45.6 0.0 copy-start
  45.6 0.0 copy-start.2
  45.6 5.0 %prep.1 = (bf16[4,128,2048]{2,1,0:T(8,128)(2,1)S(1)}, bf16[4,2048,128]{2,1,0:T(8,128)(2,1)S(1)}, f32[4,16,64,128]{3,2,1,0:T(8,128)S(1)}) custom-call(bf16[128,4096]{1,0:T(8,128)(2,1)S(1)} %copy-done.8, bf16[128,2,16,512]{3,2,1,0:T(8,128)(2,1)S(1)} %copy-done.1, s32[16,1,128]{2,1,0:T(1,128)S(1)} %broadcast_in_dim.9.len_ref), custom_call_target="tpu_custom_call" | custom-call | flops 134217728 | bytes 16777216 | tf_op jit(solution)/shard_map/prep/pallas_call | solution.py:202
  50.6 0.0 copy-start.5
  50.6 1.3 %copy-done.5 = bf16[4,128,2048]{2,1,0:T(8,128)(2,1)} copy-done((bf16[4,128,2048]{2,1,0:T(8,128)(2,1)}, bf16[4,128,2048]{2,1,0:T(8,128)(2,1)S(1)}, u32[]{:S(2)}) %copy-start.5) | copy-done | bytes 2097176
  52.0 0.0 copy-start.6
  52.0 1.3 %copy-done.6 = bf16[4,2048,128]{2,1,0:T(8,128)(2,1)} copy-done((bf16[4,2048,128]{2,1,0:T(8,128)(2,1)}, bf16[4,2048,128]{2,1,0:T(8,128)(2,1)S(1)}, u32[]{:S(2)}) %copy-start.6) | copy-done | bytes 2097176
  53.3 0.0 copy-start.7
  53.3 1.4 %copy-done.7 = f32[4,16,64,128]{3,2,1,0:T(8,128)} copy-done((f32[4,16,64,128]{3,2,1,0:T(8,128)}, f32[4,16,64,128]{3,2,1,0:T(8,128)S(1)}, u32[]{:S(2)}) %copy-start.7) | copy-done | bytes 2097176
  54.7 0.0 copy-done
  54.7 0.0 copy-done.2
  54.7 0.9 adapt.2
  55.6 0.0 copy-start.4
  55.6 0.8 copy-done.4
  56.4 9.1 %all-to-all-done.2 = bf16[16,8,4224]{2,1,0:T(8,128)(2,1)} async-done(((bf16[16,8,4224]{2,1,0:T(8,128)(2,1)}), bf16[16,8,4224]{2,1,0:T(8,128)(2,1)}, u32[]{:S(2)}, u32[]{:S(2)}) %all-to-all-start.2) | async-done | bytes 1081376 | tf_op jit(solution)/shard_map/all_to_all | solution.py:301
  65.5 7.0 %all-to-all-start.1 = ((bf16[16,8,2048]{2,1,0:T(8,128)(2,1)}), bf16[16,8,2048]{2,1,0:T(8,128)(2,1)S(1)}, u32[]{:S(2)}, u32[]{:S(2)}) async-start(bf16[16,8,2048]{2,1,0:T(8,128)(2,1)} %bitcast.10), calls=%async_computation.1 | async-start | bytes 1048576 | tf_op jit(solution)/shard_map/all_to_all | solution.py:301
  72.5 0.0 copy-start.3
  72.5 1.2 %copy-done.3 = bf16[128,4096]{1,0:T(8,128)(2,1)S(1)} copy-done((bf16[128,4096]{1,0:T(8,128)(2,1)S(1)}, bf16[128,4096]{1,0:T(8,128)(2,1)}, u32[]{:S(2)}) %copy-start.3) | copy-done | bytes 1048600
  73.7 2.2 %adapt.3 = bf16[128,2048]{1,0:T(8,128)(2,1)S(1)} custom-call(bf16[128,4224]{1,0:T(8,128)(2,1)} %bitcast.6.arrived_ref, bf16[8192,128]{1,0:T(8,128)(2,1)S(1)} %copy-done, bf16[128,4096]{1,0:T(8,128)(2,1)S(1)} %copy-done.3), custom_call_target="tpu_custom_call" | custom-call | flops 536870912 | bytes 4194304 | tf_op jit(solution)/shard_map/adapt/pallas_call | solution.py:157
  75.9 11.1 %all-to-all-done.1 = bf16[16,8,2048]{2,1,0:T(8,128)(2,1)S(1)} async-done(((bf16[16,8,2048]{2,1,0:T(8,128)(2,1)}), bf16[16,8,2048]{2,1,0:T(8,128)(2,1)S(1)}, u32[]{:S(2)}, u32[]{:S(2)}) %all-to-all-start.1) | async-done | bytes 524320 | tf_op jit(solution)/shard_map/all_to_all | solution.py:301
  87.0 0.0 copy-start.9
  87.0 18.5 %all_to_all.20 = bf16[16,8,2048]{2,1,0:T(8,128)(2,1)} all-to-all(bf16[16,8,2048]{2,1,0:T(8,128)(2,1)S(1)} %bitcast.11), channel_id=1, replica_groups=mesh['groups'=2,'owner'=16] {'owner'}, dimensions={0} | all-to-all | bytes 1048576 | tf_op jit(solution)/shard_map/all_to_all | solution.py:301
  105.4 0.0 copy-done.9
  105.5 7.5 %attend.1 = bf16[128,4096]{1,0:T(8,128)(2,1)} custom-call(bf16[2,128,128]{2,1,0:T(8,128)(2,1)} %get-tuple-element.18.refs_0_, bf16[2,128,128]{2,1,0:T(8,128)(2,1)} %get-tuple-element.19.refs_1_, bf16[128,2048]{1,0:T(8,128)(2,1)} %bitcast.12, bf16[128,2048]{1,0:T(8,128)(2,1)} %bitcast.13, bf16[4,128,2048]{2,1,0:T(8,128)(2,1)} %copy-done.5, ...), custom_call_target="tpu_custom_call" | custom-call | tf_op jit(solution)/shard_map/attend/pallas_call | solution.py:280
Async XLA Ops:
  4.0 30.9 %all-to-all-start = ((bf16[16,8,4224]{2,1,0:T(8,128)(2,1)}), bf16[16,8,4224]{2,1,0:T(8,128)(2,1)S(1)}, u32[]{:S(2)}, u32[]{:S(2)}) async-start(bf16[16,8,4224]{2,1,0:T(8,128)(2,1)} %bitcast.15), calls=%async_computation | async-start | bytes 2162688 | tf_op jit(solution)/shard_map/all_to_all | solution.py:301
  11.4 30.6 %copy-start.10 = (s32[128]{0:T(128)S(1)}, s32[128]{0:T(128)}, u32[]{:S(2)}) copy-start(s32[128]{0:T(128)} %param.11) | copy-start | bytes 1540
  34.9 30.6 %all-to-all-start.2 = ((bf16[16,8,4224]{2,1,0:T(8,128)(2,1)}), bf16[16,8,4224]{2,1,0:T(8,128)(2,1)}, u32[]{:S(2)}, u32[]{:S(2)}) async-start(bf16[16,8,4224]{2,1,0:T(8,128)(2,1)} %bitcast.14), calls=%async_computation.2 | async-start | bytes 2162688 | tf_op jit(solution)/shard_map/all_to_all | solution.py:301
  42.2 2.2 %copy-start.1 = (bf16[128,2,16,512]{3,2,1,0:T(8,128)(2,1)S(1)}, bf16[128,2,16,512]{3,2,1,0:T(8,128)(2,1)}, u32[]{:S(2)}) copy-start(bf16[128,2,16,512]{3,2,1,0:T(8,128)(2,1)} %kv_ref.1) | copy-start | bytes 12582916
  44.4 1.2 %copy-start.8 = (bf16[128,4096]{1,0:T(8,128)(2,1)S(1)}, bf16[128,4096]{1,0:T(8,128)(2,1)}, u32[]{:S(2)}) copy-start(bf16[128,4096]{1,0:T(8,128)(2,1)} %base_ref.1) | copy-start | bytes 3145732
  45.6 9.0 %copy-start = (bf16[8192,128]{1,0:T(8,128)(2,1)S(1)}, bf16[8192,128]{1,0:T(8,128)(2,1)}, u32[]{:S(2)}) copy-start(bf16[8192,128]{1,0:T(8,128)(2,1)} %a_ref.3) | copy-start | bytes 6291460
  45.6 9.0 %copy-start.2 = (bf16[128,4096]{1,0:T(8,128)(2,1)S(1)}, bf16[128,4096]{1,0:T(8,128)(2,1)}, u32[]{:S(2)}) copy-start(bf16[128,4096]{1,0:T(8,128)(2,1)} %b_ref.3) | copy-start | bytes 3145732
  50.6 1.3 %copy-start.5 = (bf16[4,128,2048]{2,1,0:T(8,128)(2,1)}, bf16[4,128,2048]{2,1,0:T(8,128)(2,1)S(1)}, u32[]{:S(2)}) copy-start(bf16[4,128,2048]{2,1,0:T(8,128)(2,1)S(1)} %get-tuple-element.28.refs_4_) | copy-start | bytes 6291460
  52.0 1.3 %copy-start.6 = (bf16[4,2048,128]{2,1,0:T(8,128)(2,1)}, bf16[4,2048,128]{2,1,0:T(8,128)(2,1)S(1)}, u32[]{:S(2)}) copy-start(bf16[4,2048,128]{2,1,0:T(8,128)(2,1)S(1)} %get-tuple-element.29.refs_5_) | copy-start | bytes 6291460
  53.3 1.4 %copy-start.7 = (f32[4,16,64,128]{3,2,1,0:T(8,128)}, f32[4,16,64,128]{3,2,1,0:T(8,128)S(1)}, u32[]{:S(2)}) copy-start(f32[4,16,64,128]{3,2,1,0:T(8,128)S(1)} %get-tuple-element.30.refs_6_) | copy-start | bytes 6291460
  55.6 0.8 copy-start.4
  65.5 21.5 %all-to-all-start.1 = ((bf16[16,8,2048]{2,1,0:T(8,128)(2,1)}), bf16[16,8,2048]{2,1,0:T(8,128)(2,1)S(1)}, u32[]{:S(2)}, u32[]{:S(2)}) async-start(bf16[16,8,2048]{2,1,0:T(8,128)(2,1)} %bitcast.10), calls=%async_computation.1 | async-start | bytes 1048576 | tf_op jit(solution)/shard_map/all_to_all | solution.py:301
  72.5 1.2 %copy-start.3 = (bf16[128,4096]{1,0:T(8,128)(2,1)S(1)}, bf16[128,4096]{1,0:T(8,128)(2,1)}, u32[]{:S(2)}) copy-start(bf16[128,4096]{1,0:T(8,128)(2,1)} %b_ref.3) | copy-start | bytes 3145732
  87.0 18.5 %copy-start.9 = (bf16[16,8,2048]{2,1,0:T(8,128)(2,1)}, bf16[16,8,2048]{2,1,0:T(8,128)(2,1)S(1)}, u32[]{:S(2)}) copy-start(bf16[16,8,2048]{2,1,0:T(8,128)(2,1)S(1)} %all-to-all-done.1) | copy-start | bytes 1572868

commit v5 on v3

--- a/solution.py
+++ b/solution.py
@@ -16,9 +16,14 @@
 COLUMNS_STEP = 2048
 
 
-def routing(owners, slot_count, held, slots_ref, ids_ref):
+def place_of(index, quarter):
+    return lax.div(index, 2 * quarter) * quarter + lax.rem(index, quarter)
+
+
+def routing(pairs, owners, slot_count, held, slots_ref, ids_ref):
     ids = ids_ref[...]
     rows = ids.shape[1]
+    quarter = owners // 4
 
     def look(s, slot):
         return jnp.where(ids == s, slots_ref[s], slot)
@@ -34,98 +39,120 @@
         hits.astype(jnp.bfloat16), earlier.astype(jnp.bfloat16), preferred_element_type=jnp.float32
     )
     place = jnp.sum(jnp.where(hits, before, 0.0), axis=0, keepdims=True).astype(jnp.int32)
-    bins = owner * slot_count + place
-    routed = bins == lax.broadcasted_iota(jnp.int32, (owners * slot_count, rows), 0)
+    apart = owner ^ lax.axis_index("owner")
+    message = place_of(apart if pairs else owner, quarter)
+    meant = lax.rem(lax.div(apart, quarter), 2) == (1 if pairs else 0)
+    line = lax.broadcasted_iota(jnp.int32, (owners // 2 * slot_count, rows), 0)
+    routed = line == jnp.where(meant, message * slot_count + place, -1)
     label = jnp.sum(jnp.where(routed, local.astype(jnp.float32), 0.0), axis=1, keepdims=True)
     return routed.astype(jnp.bfloat16), label
 
 
 def pack_kernel(
-    owners, slot_count, held, slots_ref, ids_ref, hidden_ref, packed_ref, routed_ref, rows_ref, bins_ref, sems, out_sems
+    pairs, owners, slot_count, held, slots_ref, ids_ref, hidden_ref, after_ref, routed_ref, *refs
 ):
+    *packed_refs, rows_ref, sems = refs
     width = hidden_ref.shape[1]
-    spans = [pl.ds(at, min(COLUMNS_STEP, width - at)) for at in range(0, width, COLUMNS_STEP)]
+    spans = [(at, min(COLUMNS_STEP, width - at)) for at in range(0, width, COLUMNS_STEP)]
     loads = [
-        pltpu.make_async_copy(hidden_ref.at[:, span], rows_ref.at[:, span], sems.at[i])
-        for i, span in enumerate(spans)
-    ]
-    spans[-1] = pl.ds(spans[-1].start, spans[-1].size + LANES)
-    stores = [
-        pltpu.make_async_copy(bins_ref.at[:, span], packed_ref.at[:, span], out_sems.at[i])
-        for i, span in enumerate(spans)
+        pltpu.make_async_copy(
+            hidden_ref.at[:, pl.ds(at, size)], rows_ref.at[:, pl.ds(at, size)], sems.at[i]
+        )
+        for i, (at, size) in enumerate(spans)
     ]
     for load in loads:
         load.start()
-    routed, label = routing(owners, slot_count, held, slots_ref, ids_ref)
-    routed_ref[...] = jnp.transpose(routed.astype(jnp.float32)).astype(routed_ref.dtype)
-    bins_ref[:, width:] = jnp.broadcast_to(label, (label.shape[0], LANES)).astype(bins_ref.dtype)
-    for load, store, span in zip(loads, stores, spans):
+    routed, label = routing(pairs, owners, slot_count, held, slots_ref, ids_ref)
+    routed_ref[...] = routed
+    label = jnp.broadcast_to(label, (label.shape[0], LANES))
+    count = packed_refs[0].shape[0]
+
+    def put(at, lines):
+        for i, packed_ref in enumerate(packed_refs):
+            packed_ref[:, at : at + lines.shape[1]] = lines[i * count : (i + 1) * count].astype(
+                packed_ref.dtype
+            )
+
+    put(width, label)
+    for load, (at, size) in zip(loads, spans):
         load.wait()
-        at, end = span.start, min(span.start + span.size, width)
-        bins_ref[:, at:end] = jnp.dot(
-            routed, rows_ref[:, at:end], preferred_element_type=jnp.float32
-        ).astype(bins_ref.dtype)
-        store.start()
-    for store in stores:
-        store.wait()
-
-
-def pack(hidden, adapter_id, adapter_slot, owners, slot_count, held):
+        put(at, jnp.dot(routed, rows_ref[:, at : at + size], preferred_element_type=jnp.float32))
+
+
+def pack(hidden, adapter_id, adapter_slot, after, pairs, owners, slot_count, held):
     rows, width = hidden.shape
-    bins = owners * slot_count
+    lines = owners // 2 * slot_count
+    messages = owners // 2 if pairs else 1
     steps = pl.cdiv(width, COLUMNS_STEP)
     return pl.pallas_call(
-        functools.partial(pack_kernel, owners, slot_count, held),
+        functools.partial(pack_kernel, pairs, owners, slot_count, held),
         in_specs=[
             pl.BlockSpec(memory_space=pltpu.SMEM),
             pl.BlockSpec(memory_space=pltpu.VMEM),
             pl.BlockSpec(memory_space=pl.ANY),
-        ],
-        out_specs=[pl.BlockSpec(memory_space=pl.ANY), pl.BlockSpec(memory_space=pltpu.VMEM)],
-        out_shape=[
-            jax.ShapeDtypeStruct((bins, width + LANES), hidden.dtype),
-            jax.ShapeDtypeStruct((rows, bins), jnp.bfloat16),
-        ],
+            pl.BlockSpec(memory_space=pl.ANY),
+        ],
+        out_specs=[pl.BlockSpec(memory_space=pltpu.VMEM)] * (1 + messages),
+        out_shape=[jax.ShapeDtypeStruct((lines, rows), jnp.bfloat16)]
+        + [jax.ShapeDtypeStruct((lines // messages, width + LANES), hidden.dtype)] * messages,
         scratch_shapes=[
             pltpu.VMEM((rows, width), hidden.dtype),
-            pltpu.VMEM((bins, width + LANES), hidden.dtype),
             pltpu.SemaphoreType.DMA((steps,)),
-            pltpu.SemaphoreType.DMA((steps,)),
         ],
         compiler_params=pltpu.CompilerParams(vmem_limit_bytes=56 * 2**20),
-        name="pack",
-    )(adapter_slot, adapter_id.reshape(1, rows), hidden)
-
-
-def adapt_kernel(arrived_ref, a_ref, b_ref, change_ref):
+        name="pack_pairs" if pairs else "pack",
+    )(adapter_slot, adapter_id.reshape(1, rows), hidden, after)
+
+
+def stack(refs, at, size):
+    if len(refs) == 1:
+        return refs[0][:, at : at + size]
+    return jnp.concatenate(
+        [ref[:, at : at + size].astype(jnp.float32) for ref in refs], axis=0
+    ).astype(jnp.bfloat16)
+
+
+def adapt_kernel(count, *refs):
+    arrived_refs, (a_ref, b_ref, _), change_refs = refs[:count], refs[count : count + 3], refs[count + 3 :]
     width = a_ref.shape[0]
-    low = jnp.zeros((arrived_ref.shape[0], a_ref.shape[1]), jnp.float32)
+    lines = arrived_refs[0].shape[0]
+    low = jnp.zeros((count * lines, a_ref.shape[1]), jnp.float32)
     for at in range(0, width, COLUMNS_STEP):
         low += jnp.dot(
-            arrived_ref[:, at : at + COLUMNS_STEP],
+            stack(arrived_refs, at, COLUMNS_STEP),
             a_ref[at : at + COLUMNS_STEP, :],
             preferred_element_type=jnp.float32,
         )
-    label = arrived_ref[:, width:].astype(jnp.float32)[:, :1].astype(jnp.int32)
+    label = stack(arrived_refs, width, LANES).astype(jnp.float32)[:, :1].astype(jnp.int32)
     column = lax.broadcasted_iota(jnp.int32, low.shape, 1) // RANK
     low = jnp.where(column == label, low, 0.0).astype(jnp.bfloat16)
     out_width = b_ref.shape[1]
     piece = min(1024, out_width)
     for at in range(0, out_width, piece):
-        change_ref[:, at : at + piece] = (
-            SCALE * jnp.dot(low, b_ref[:, at : at + piece], preferred_element_type=jnp.float32)
-        ).astype(change_ref.dtype)
-
-
-def adapt(arrived, a_maps, b_maps):
+        change = SCALE * jnp.dot(low, b_ref[:, at : at + piece], preferred_element_type=jnp.float32)
+        for i, change_ref in enumerate(change_refs):
+            change_ref[:, at : at + piece] = change[i * lines : (i + 1) * lines].astype(
+                change_ref.dtype
+            )
+
+
+def adapt(arrived, a_maps, b_maps, after):
+    count = len(arrived)
+    lines = arrived[0].shape[0]
     return pl.pallas_call(
-        adapt_kernel,
-        in_specs=[pl.BlockSpec(memory_space=pltpu.VMEM)] * 3,
-        out_specs=pl.BlockSpec(memory_space=pltpu.VMEM),
-        out_shape=jax.ShapeDtypeStruct((arrived.shape[0], b_maps.shape[1]), jnp.bfloat16),
+        functools.partial(adapt_kernel, count),
+        in_specs=[pl.BlockSpec(memory_space=pltpu.VMEM)] * (count + 2)
+        + [pl.BlockSpec(memory_space=pl.ANY)],
+        out_specs=[pl.BlockSpec(memory_space=pltpu.VMEM)] * count,
+        out_shape=[jax.ShapeDtypeStruct((lines, b_maps.shape[1]), jnp.bfloat16)] * count,
         compiler_params=pltpu.CompilerParams(vmem_limit_bytes=16 * 2**20),
+        cost_estimate=pl.CostEstimate(
+            flops=2 * count * lines * (a_maps.size + b_maps.size),
+            bytes_accessed=2 * (a_maps.size + b_maps.size),
+            transcendentals=0,
+        ),
         name="adapt",
-    )(arrived, a_maps, b_maps)
+    )(*arrived, a_maps, b_maps, after)
 
 
 def tall(rows, group):
@@ -186,17 +213,32 @@
     )(base_q, kv_cache, lens)
 
 
-def attend_kernel(group, routed_ref, returned_ref, keys_ref, values_ref, scores_ref, out_ref):
+def attend_kernel(group, count, *refs):
+    routed_refs, returned_refs, refs = refs[:2], refs[2 : 2 + count], refs[2 + count :]
+    laid_refs, (out_ref, *held_refs, sems) = refs[:3], refs[3:]
+    keys_ref, values_ref, scores_ref = held_refs
     step = ROWS_STEP
     steps, _, cells = scores_ref.shape[1:]
     span = group * HEAD
     factor = 1.0 / jnp.sqrt(jnp.float32(HEAD))
+    copies = [
+        [
+            pltpu.make_async_copy(laid_ref.at[k], held_ref.at[k], sems.at[k, i])
+            for i, (laid_ref, held_ref) in enumerate(zip(laid_refs, held_refs))
+        ]
+        for k in range(KVH)
+    ]
+    for copy in copies:
+        for one in copy:
+            one.start()
+    routed = jnp.concatenate([ref[...].astype(jnp.float32) for ref in routed_refs], axis=0)
+    routed = jnp.transpose(routed).astype(jnp.bfloat16)
     for k in range(KVH):
         delta = jnp.dot(
-            routed_ref[...],
-            returned_ref[:, k * span : (k + 1) * span],
-            preferred_element_type=jnp.float32,
-        )
+            routed, stack(returned_refs, k * span, span), preferred_element_type=jnp.float32
+        )
+        for one in copies[k]:
+            one.wait()
         for i in range(steps):
             lines = slice(i * step, (i + 1) * step)
             at = slice(i * cells, (i + 1) * cells)
@@ -217,32 +259,53 @@
                 ].astype(out_ref.dtype)
 
 
-def attend(routed, returned, keys, values, scores):
-    rows, width = routed.shape[0], returned.shape[1]
+def attend(routed, returned, laid, width):
+    rows = routed[0].shape[1]
     return pl.pallas_call(
-        functools.partial(attend_kernel, width // (KVH * HEAD)),
-        in_specs=[pl.BlockSpec(memory_space=pltpu.VMEM)] * 5,
+        functools.partial(attend_kernel, width // (KVH * HEAD), len(returned)),
+        in_specs=[pl.BlockSpec(memory_space=pltpu.VMEM)] * (2 + len(returned))
+        + [pl.BlockSpec(memory_space=pl.ANY)] * len(laid),
         out_specs=pl.BlockSpec(memory_space=pltpu.VMEM),
         out_shape=jax.ShapeDtypeStruct((rows, width), jnp.bfloat16),
+        scratch_shapes=[pltpu.VMEM(part.shape, part.dtype) for part in laid]
+        + [pltpu.SemaphoreType.DMA((KVH, len(laid)))],
         compiler_params=pltpu.CompilerParams(vmem_limit_bytes=24 * 2**20),
         name="attend",
-    )(routed, returned, keys, values, scores)
+    )(*routed, *returned, *laid)
 
 
 def on_device(hidden, adapter_id, adapter_slot, cache_len, base_q, kv_cache, a_maps, b_maps):
     owners = lax.axis_size("owner")
+    quarter = owners // 4
     rows = hidden.shape[0]
     held = a_maps.shape[1] // RANK
     slot_count = max(2, 2 * ((rows + 2 * owners - 1) // (2 * owners)))
-    bins = owners * slot_count
-    packed, routed = pack(hidden, adapter_id, adapter_slot, owners, slot_count, held)
-    packed = packed.reshape(owners, slot_count, packed.shape[1])
-    arrived = lax.all_to_all(packed, "owner", split_axis=0, concat_axis=0, tiled=True)
-    keys, values, scores = prep(base_q, kv_cache, cache_len)
-    change = adapt(arrived.reshape(bins, arrived.shape[2]), a_maps, b_maps)
-    change = change.reshape(owners, slot_count, change.shape[1])
-    returned = lax.all_to_all(change, "owner", split_axis=0, concat_axis=0, tiled=True)
-    return attend(routed, returned.reshape(bins, returned.shape[2]), keys, values, scores)
+    halves = [[i for i in range(owners) if i // quarter % 2 == bit] for bit in range(2)]
+
+    def swap(lines):
+        blocks = lines.reshape(owners // 2, slot_count, lines.shape[1])
+        blocks = lax.all_to_all(
+            blocks, "owner", split_axis=0, concat_axis=0, tiled=True, axis_index_groups=halves
+        )
+        return blocks.reshape(lines.shape)
+
+    def trade(messages):
+        return [
+            lax.ppermute(message, "owner", [(i, i ^ apart) for i in range(owners)])
+            for message, apart in zip(messages, halves[1])
+        ]
+
+    whole = functools.partial(pack, hidden, adapter_id, adapter_slot)
+    routed, lines = whole(adapter_id, False, owners, slot_count, held)
+    routed_pairs, *messages = whole(routed, True, owners, slot_count, held)
+    arrived = swap(lines)
+    arrived_pairs = trade(messages)
+    laid = prep(base_q, kv_cache, cache_len)
+    (change,) = adapt([arrived], a_maps, b_maps, laid[0])
+    returned = swap(change)
+    changes = adapt(arrived_pairs, a_maps, b_maps, change)
+    returned_pairs = trade(changes)
+    return attend([routed, routed_pairs], [returned, *returned_pairs], laid, base_q.shape[1])
 
 
 def solution(mesh):

time: 101 us -> 114 us (1.13)
  blocking collectives: 58.1 us -> 0 us
  waiting for transfers between devices: 11.6 us -> 44.3 us
  starting transfers between devices: 3.79 us -> 31.8 us
  local copies, waits for them, and re-layouts: 9.5 us -> 15.3 us
  Pallas kernels: 16.1 us -> 21.3 us
    all_to_all x1 -> x0, blocking collectives: 58.1 us -> none  [on_device(): lax.all_to_all(packed, 'owner', split_axis=0, concat_axis=0, tiled=True)]
    ppermute x0 -> x16, waiting for transfers between devices: none -> 30.2 us  [trade(): lax.ppermute(message, 'owner', [(i, i ^ apart) for i in range(owners)])]
    ppermute x0 -> x16, starting transfers between devices: none -> 21.2 us  [trade(): lax.ppermute(message, 'owner', [(i, i ^ apart) for i in range(owners)])]
    all_to_all x1 -> x2, starting transfers between devices: 3.79 us -> 10.5 us  [swap(): lax.all_to_all(blocks, 'owner', split_axis=0, concat_axis=0, tiled=True,...]
    unnamed x20 -> x30, local copies, waits for them, and re-layouts: 9.24 us -> 15.1 us
    pallas_call x3 -> x5, Pallas kernels: 11.1 us -> 16.3 us  [the longest x2 7.43 us: pack(): pl.pallas_call(functools.partial(pack_kernel, pairs, owners, slot_count,...]
    all_to_all x1 -> x2, waiting for transfers between devices: 11.6 us -> 14.2 us  [swap(): lax.all_to_all(blocks, 'owner', split_axis=0, concat_axis=0, tiled=True,...]
  transfers between devices with their start and end apart: 1 -> 18, of which waited for: 1 -> 9; matrix products, arithmetic and copies ran while one was open for 0% -> 0% of each run, Pallas kernels for 5% -> 8%
where the time goes in v5:
time: 114 us; the launch traced here: 113 us
  waiting for transfers between devices  44.3 us (39%)
  starting transfers between devices  31.8 us (28%)
  Pallas kernels  21.3 us (19%)
  local copies, waits for them, and re-layouts  15.3 us (13%)
    ppermute x16, waiting for transfers between devices, trade(): lax.ppermute(message, 'owner', [(i, i ^ apart) for i in range(owners)])  30.2 us
    ppermute x16, starting transfers between devices, trade(): lax.ppermute(message, 'owner', [(i, i ^ apart) for i in range(owners)])  21.2 us
    unnamed x30, local copies, waits for them, and re-layouts  15.1 us
    all_to_all x2, waiting for transfers between devices, swap(): lax.all_to_all(blocks, 'owner', split_axis=0, concat_axis=0, tiled=True,...  14.2 us
    all_to_all x2, starting transfers between devices, swap(): lax.all_to_all(blocks, 'owner', split_axis=0, concat_axis=0, tiled=True,...  10.5 us
    pallas_call x2, Pallas kernels, pack(): pl.pallas_call(functools.partial(pack_kernel, pairs, owners, slot_count,...  7.43 us
    pallas_call x1, Pallas kernels, attend(): pl.pallas_call(functools.partial(attend_kernel, width // (KVH * HEAD), le...  6.59 us
    pallas_call x1, Pallas kernels, prep(): pl.pallas_call(functools.partial(prep_kernel, group, context), grid=(step...  4.99 us
  transfers between devices with their start and end apart: 18, of which 9 were waited for; matrix products, arithmetic and copies ran while one was open for 0% of the time, Pallas kernels for 8%

profile of v5, /device:TPU:0, one launch (start us, length us, event | category | flops | bytes accessed | tf_op | source)
XLA Modules:
  0.0 112.9 jit_solution(2980451367532382317)
XLA Ops:
  0.0 3.8 %pack.1 = (bf16[64,128]{1,0:T(8,128)(2,1)}, bf16[64,8320]{1,0:T(8,128)(2,1)}) custom-call(s32[32]{0:T(128)} %slots_ref.3, s32[1,128]{1,0:T(1,128)} %bitcast.7, bf16[128,8192]{1,0:T(8,128)(2,1)} %hidden_ref.3, s32[128]{0:T(128)} %after_ref.1), custom_call_target="tpu_custom_call" | custom-call | tf_op jit(solution)/shard_map/pack/pallas_call | solution.py:87
  3.8 6.3 %all-to-all-start = ((bf16[8,8,8320]{2,1,0:T(8,128)(2,1)}), bf16[8,8,8320]{2,1,0:T(8,128)(2,1)S(1)}, u32[]{:S(2)}, u32[]{:S(2)}) async-start(bf16[8,8,8320]{2,1,0:T(8,128)(2,1)} %bitcast.6), calls=%async_computation | async-start | bytes 2129920 | tf_op jit(solution)/shard_map/all_to_all | solution.py:287
  10.1 0.1 broadcast_in_dim.7
  10.1 0.1 broadcast_in_dim.8
  10.2 0.1 broadcast_in_dim.9.len_ref
  10.3 0.0 copy-start.4
  10.3 2.2 %copy-done.4 = bf16[128,2,16,512]{3,2,1,0:T(8,128)(2,1)S(1)} copy-done((bf16[128,2,16,512]{3,2,1,0:T(8,128)(2,1)S(1)}, bf16[128,2,16,512]{3,2,1,0:T(8,128)(2,1)}, u32[]{:S(2)}) %copy-start.4) | copy-done | bytes 4194328
  12.5 1.2 %copy-done.11 = bf16[128,4096]{1,0:T(8,128)(2,1)S(1)} copy-done((bf16[128,4096]{1,0:T(8,128)(2,1)S(1)}, bf16[128,4096]{1,0:T(8,128)(2,1)}, u32[]{:S(2)}) %copy-start.11) | copy-done | bytes 1048600
  13.7 5.0 %prep.1 = (bf16[4,128,2048]{2,1,0:T(8,128)(2,1)S(1)}, bf16[4,2048,128]{2,1,0:T(8,128)(2,1)S(1)}, f32[4,16,64,128]{3,2,1,0:T(8,128)S(1)}) custom-call(bf16[128,4096]{1,0:T(8,128)(2,1)S(1)} %copy-done.11, bf16[128,2,16,512]{3,2,1,0:T(8,128)(2,1)S(1)} %copy-done.4, s32[16,1,128]{2,1,0:T(1,128)S(1)} %broadcast_in_dim.9.len_ref), custom_call_target="tpu_custom_call" | custom-call | flops 134217728 | bytes 16777216 | tf_op jit(solution)/shard_map/prep/pallas_call | solution.py:190
  18.7 1.4 %copy-done.1 = bf16[4,128,2048]{2,1,0:T(8,128)(2,1)} copy-done((bf16[4,128,2048]{2,1,0:T(8,128)(2,1)}, bf16[4,128,2048]{2,1,0:T(8,128)(2,1)S(1)}, u32[]{:S(2)}) %copy-start.1) | copy-done | bytes 2097176
  20.1 1.3 %copy-done.7 = bf16[4,2048,128]{2,1,0:T(8,128)(2,1)} copy-done((bf16[4,2048,128]{2,1,0:T(8,128)(2,1)}, bf16[4,2048,128]{2,1,0:T(8,128)(2,1)S(1)}, u32[]{:S(2)}) %copy-start.7) | copy-done | bytes 2097176
  21.4 1.4 %copy-done.9 = f32[4,16,64,128]{3,2,1,0:T(8,128)} copy-done((f32[4,16,64,128]{3,2,1,0:T(8,128)}, f32[4,16,64,128]{3,2,1,0:T(8,128)S(1)}, u32[]{:S(2)}) %copy-start.9) | copy-done | bytes 2097176
  22.8 14.2 %all-to-all-done = bf16[8,8,8320]{2,1,0:T(8,128)(2,1)S(1)} async-done(((bf16[8,8,8320]{2,1,0:T(8,128)(2,1)}), bf16[8,8,8320]{2,1,0:T(8,128)(2,1)S(1)}, u32[]{:S(2)}, u32[]{:S(2)}) %all-to-all-start) | async-done | bytes 1064992 | tf_op jit(solution)/shard_map/all_to_all | solution.py:287
  37.0 1.6 %copy-done.2 = bf16[4,128,2048]{2,1,0:T(8,128)(2,1)S(1)} copy-done((bf16[4,128,2048]{2,1,0:T(8,128)(2,1)S(1)}, bf16[4,128,2048]{2,1,0:T(8,128)(2,1)}, u32[]{:S(2)}) %copy-start.2) | copy-done | bytes 2097176
  38.6 1.2 %copy-done.5 = bf16[128,4096]{1,0:T(8,128)(2,1)S(1)} copy-done((bf16[128,4096]{1,0:T(8,128)(2,1)S(1)}, bf16[128,4096]{1,0:T(8,128)(2,1)}, u32[]{:S(2)}) %copy-start.5) | copy-done | bytes 1048600
  39.8 1.5 %adapt.2.refs_10_ = bf16[64,4096]{1,0:T(8,128)(2,1)} custom-call(bf16[64,8320]{1,0:T(8,128)(2,1)S(1)} %bitcast.5, bf16[8192,128]{1,0:T(8,128)(2,1)S(1)} %copy-done, bf16[128,4096]{1,0:T(8,128)(2,1)S(1)} %copy-done.5, bf16[4,128,2048]{2,1,0:T(8,128)(2,1)S(1)} %copy-done.2), custom_call_target="tpu_custom_call" | custom-call | flops 201326592 | bytes 3145728 | tf_op jit(solution)/shard_map/adapt/pallas_call | solution.py:142
  41.4 4.3 %all-to-all-start.1 = ((bf16[8,8,4096]{2,1,0:T(8,128)(2,1)}), bf16[8,8,4096]{2,1,0:T(8,128)(2,1)}, u32[]{:S(2)}, u32[]{:S(2)}) async-start(bf16[8,8,4096]{2,1,0:T(8,128)(2,1)} %bitcast.3), calls=%async_computation.1 | async-start | bytes 1048576 | tf_op jit(solution)/shard_map/all_to_all | solution.py:287
  45.7 3.7 %pack_pairs.1 = (bf16[64,128]{1,0:T(8,128)(2,1)}, bf16[8,8320]{1,0:T(8,128)(2,1)}, bf16[8,8320]{1,0:T(8,128)(2,1)}, bf16[8,8320]{1,0:T(8,128)(2,1)}, bf16[8,8320...) custom-call(s32[32]{0:T(128)} %slots_ref.3, ...), custom_call_target="tpu_custom_call" | custom-call | tf_op jit(solution)/shard_map/pack_pairs/pallas_call | solution.py:87
  49.3 0.1 collective-permute-start
  49.4 1.7 %collective-permute-start.1 = (bf16[8,8320]{1,0:T(8,128)(2,1)}, bf16[8,8320]{1,0:T(8,128)(2,1)S(1)}, u32[]{:S(2)}, u32[]{:S(2)}) collective-permute-start(bf16[8,8320]{1,0:T(8,128)(2,1)} %get-tuple-element.32), channel_id=1, source_target_pairs={{0,5},{1,4},{2,7},{3,6},{4,1},{5,0},{6,3},{7,2},{8,13},{9,12},{10,... | collective-permute-start | bytes 399368 | tf_op jit(solution)/shard_map/ppermute | solution.py:294
  51.1 1.6 %collective-permute-start.2 = (bf16[8,8320]{1,0:T(8,128)(2,1)}, bf16[8,8320]{1,0:T(8,128)(2,1)S(1)}, u32[]{:S(2)}, u32[]{:S(2)}) collective-permute-start(bf16[8,8320]{1,0:T(8,128)(2,1)} %get-tuple-element.33), channel_id=1, source_target_pairs={{0,6},{1,7},{2,4},{3,5},{4,2},{5,3},{6,0},{7,1},{8,14},{9,15},{10,... | collective-permute-start | bytes 399368 | tf_op jit(solution)/shard_map/ppermute | solution.py:294
  52.7 1.1 collective-permute-start.3
  53.8 2.5 %collective-permute-start.4 = (bf16[8,8320]{1,0:T(8,128)(2,1)}, bf16[8,8320]{1,0:T(8,128)(2,1)S(1)}, u32[]{:S(2)}, u32[]{:S(2)}) collective-permute-start(bf16[8,8320]{1,0:T(8,128)(2,1)} %get-tuple-element.35), channel_id=1, source_target_pairs={{0,12},{1,13},{2,14},{3,15},{4,8},{5,9},{6,10},{7,11},{8,4},{9,5},... | collective-permute-start | bytes 399368 | tf_op jit(solution)/shard_map/ppermute | solution.py:294
  56.3 5.1 %collective-permute-done.refs_0_ = bf16[8,8320]{1,0:T(8,128)(2,1)S(1)} collective-permute-done((bf16[8,8320]{1,0:T(8,128)(2,1)}, bf16[8,8320]{1,0:T(8,128)(2,1)S(1)}, u32[]{:S(2)}, u32[]{:S(2)}) %collective-permute-start) | collective-permute-done | bytes 133152 | tf_op jit(solution)/shard_map/ppermute | solution.py:294
  61.5 1.7 %collective-permute-done.1.refs_1_ = bf16[8,8320]{1,0:T(8,128)(2,1)S(1)} collective-permute-done((bf16[8,8320]{1,0:T(8,128)(2,1)}, bf16[8,8320]{1,0:T(8,128)(2,1)S(1)}, u32[]{:S(2)}, u32[]{:S(2)}) %collective-permute-start.1) | collective-permute-done | bytes 133152 | tf_op jit(solution)/shard_map/ppermute | solution.py:294
  63.2 1.8 %collective-permute-start.6 = (bf16[8,8320]{1,0:T(8,128)(2,1)}, bf16[8,8320]{1,0:T(8,128)(2,1)S(1)}, u32[]{:S(2)}, u32[]{:S(2)}) collective-permute-start(bf16[8,8320]{1,0:T(8,128)(2,1)} %get-tuple-element.37), channel_id=1, source_target_pairs={{0,14},{1,15},{2,12},{3,13},{4,10},{5,11},{6,8},{7,9},{8,6},{9,7},... | collective-permute-start | bytes 399368 | tf_op jit(solution)/shard_map/ppermute | solution.py:294
  65.1 12.0 %collective-permute-done.2.refs_2_ = bf16[8,8320]{1,0:T(8,128)(2,1)S(1)} collective-permute-done((bf16[8,8320]{1,0:T(8,128)(2,1)}, bf16[8,8320]{1,0:T(8,128)(2,1)S(1)}, u32[]{:S(2)}, u32[]{:S(2)}) %collective-permute-start.2) | collective-permute-done | bytes 133152 | tf_op jit(solution)/shard_map/ppermute | solution.py:294
  77.1 1.3 %collective-permute-done.3.refs_3_ = bf16[8,8320]{1,0:T(8,128)(2,1)S(1)} collective-permute-done((bf16[8,8320]{1,0:T(8,128)(2,1)}, bf16[8,8320]{1,0:T(8,128)(2,1)S(1)}, u32[]{:S(2)}, u32[]{:S(2)}) %collective-permute-start.3) | collective-permute-done | bytes 133152 | tf_op jit(solution)/shard_map/ppermute | solution.py:294
  78.4 0.0 collective-permute-done.4.refs_4_
  78.4 0.0 collective-permute-done.5.refs_5_
  78.4 0.0 collective-permute-done.6.refs_6_
  78.4 6.0 %collective-permute-done.7.refs_7_ = bf16[8,8320]{1,0:T(8,128)(2,1)S(1)} collective-permute-done((bf16[8,8320]{1,0:T(8,128)(2,1)}, bf16[8,8320]{1,0:T(8,128)(2,1)S(1)}, u32[]{:S(2)}, u32[]{:S(2)}) %collective-permute-start.7) | collective-permute-done | bytes 133152 | tf_op jit(solution)/shard_map/ppermute | solution.py:294
  84.4 0.8 adapt.3
  85.2 0.1 collective-permute-start.8
  85.3 0.1 collective-permute-start.9
  85.3 2.9 %collective-permute-start.10 = (bf16[8,4096]{1,0:T(8,128)(2,1)S(1)}, bf16[8,4096]{1,0:T(8,128)(2,1)S(1)}, u32[]{:S(2)}, u32[]{:S(2)}) collective-permute-start(bf16[8,4096]{1,0:T(8,128)(2,1)S(1)} %get-tuple-element.41), channel_id=1, source_target_pairs={{0,6},{1,7},{2,4},{3,5},{4,2},{5,3},{6,0},{7,1},{8,14},{9,15},{10,... | collective-permute-start | bytes 196616 | tf_op jit(solution)/shard_map/ppermute | solution.py:294
  88.2 1.4 %collective-permute-start.11 = (bf16[8,4096]{1,0:T(8,128)(2,1)S(1)}, bf16[8,4096]{1,0:T(8,128)(2,1)S(1)}, u32[]{:S(2)}, u32[]{:S(2)}) collective-permute-start(bf16[8,4096]{1,0:T(8,128)(2,1)S(1)} %get-tuple-element.42), channel_id=1, source_target_pairs={{0,7},{1,6},{2,5},{3,4},{4,3},{5,2},{6,1},{7,0},{8,15},{9,14},{10,... | collective-permute-start | bytes 196616 | tf_op jit(solution)/shard_map/ppermute | solution.py:294
  89.6 0.0 collective-permute-start.12
  89.6 0.1 collective-permute-done.8.refs_3_
  89.7 1.9 %collective-permute-start.13 = (bf16[8,4096]{1,0:T(8,128)(2,1)S(1)}, bf16[8,4096]{1,0:T(8,128)(2,1)S(1)}, u32[]{:S(2)}, u32[]{:S(2)}) collective-permute-start(bf16[8,4096]{1,0:T(8,128)(2,1)S(1)} %get-tuple-element.44), channel_id=1, source_target_pairs={{0,13},{1,12},{2,15},{3,14},{4,9},{5,8},{6,11},{7,10},{8,5},{9,4},... | collective-permute-start | bytes 196616 | tf_op jit(solution)/shard_map/ppermute | solution.py:294
  91.6 3.3 %collective-permute-start.14 = (bf16[8,4096]{1,0:T(8,128)(2,1)S(1)}, bf16[8,4096]{1,0:T(8,128)(2,1)S(1)}, u32[]{:S(2)}, u32[]{:S(2)}) collective-permute-start(bf16[8,4096]{1,0:T(8,128)(2,1)S(1)} %get-tuple-element.45), channel_id=1, source_target_pairs={{0,14},{1,15},{2,12},{3,13},{4,10},{5,11},{6,8},{7,9},{8,6},{9,7},... | collective-permute-start | bytes 196616 | tf_op jit(solution)/shard_map/ppermute | solution.py:294
  94.9 2.7 %collective-permute-start.15 = (bf16[8,4096]{1,0:T(8,128)(2,1)S(1)}, bf16[8,4096]{1,0:T(8,128)(2,1)S(1)}, u32[]{:S(2)}, u32[]{:S(2)}) collective-permute-start(bf16[8,4096]{1,0:T(8,128)(2,1)S(1)} %get-tuple-element.46), channel_id=1, source_target_pairs={{0,15},{1,14},{2,13},{3,12},{4,11},{5,10},{6,9},{7,8},{8,7},{9,6},... | collective-permute-start | bytes 196616 | tf_op jit(solution)/shard_map/ppermute | solution.py:294
  97.6 1.2 %collective-permute-done.14.refs_9_ = bf16[8,4096]{1,0:T(8,128)(2,1)S(1)} collective-permute-done((bf16[8,4096]{1,0:T(8,128)(2,1)S(1)}, bf16[8,4096]{1,0:T(8,128)(2,1)S(1)}, u32[]{:S(2)}, u32[]{:S(2)}) %collective-permute-start.14) | collective-permute-done | bytes 65568 | tf_op jit(solution)/shard_map/ppermute | solution.py:294
  98.9 2.6 %collective-permute-done.15.refs_10_ = bf16[8,4096]{1,0:T(8,128)(2,1)S(1)} collective-permute-done((bf16[8,4096]{1,0:T(8,128)(2,1)S(1)}, bf16[8,4096]{1,0:T(8,128)(2,1)S(1)}, u32[]{:S(2)}, u32[]{:S(2)}) %collective-permute-start.15) | collective-permute-done | bytes 65568 | tf_op jit(solution)/shard_map/ppermute | solution.py:294
  101.5 1.6 %copy-done.3 = bf16[4,128,2048]{2,1,0:T(8,128)(2,1)S(1)} copy-done((bf16[4,128,2048]{2,1,0:T(8,128)(2,1)S(1)}, bf16[4,128,2048]{2,1,0:T(8,128)(2,1)}, u32[]{:S(2)}) %copy-start.3) | copy-done | bytes 2097176
  103.1 1.6 %copy-done.8 = bf16[4,2048,128]{2,1,0:T(8,128)(2,1)S(1)} copy-done((bf16[4,2048,128]{2,1,0:T(8,128)(2,1)S(1)}, bf16[4,2048,128]{2,1,0:T(8,128)(2,1)}, u32[]{:S(2)}) %copy-start.8) | copy-done | bytes 2097176
  104.7 1.6 %copy-done.10 = f32[4,16,64,128]{3,2,1,0:T(8,128)S(1)} copy-done((f32[4,16,64,128]{3,2,1,0:T(8,128)S(1)}, f32[4,16,64,128]{3,2,1,0:T(8,128)}, u32[]{:S(2)}) %copy-start.10) | copy-done | bytes 2097176
  106.3 6.6 %attend.1 = bf16[128,4096]{1,0:T(8,128)(2,1)} custom-call(bf16[64,128]{1,0:T(8,128)(2,1)S(1)} %copy-done.12, bf16[64,128]{1,0:T(8,128)(2,1)S(1)} %copy-done.13, bf16[64,4096]{1,0:T(8,128)(2,1)} %bitcast.4.refs_2_, bf16[8,4096]{1,0:T(8,128)(2,1)S(1)} %collective-permute-done.8.refs_3_, bf16[8,4096]{1,0:T(8,128)(2,1)S(1)} %collective-permute-done.9.refs_4_, ...), custom_call_target="tpu_custom_call" | custom-call | tf_op jit(solution)/shard_map/attend/pallas_call | solution.py:264
  (27 shorter events, 0.1 us)
Async XLA Ops:
  0.0 10.0 %copy-start.14 = (s32[128]{0:T(128)S(1)}, s32[128]{0:T(128)}, u32[]{:S(2)}) copy-start(s32[128]{0:T(128)} %param.11) | copy-start | bytes 1540
  3.8 33.2 %all-to-all-start = ((bf16[8,8,8320]{2,1,0:T(8,128)(2,1)}), bf16[8,8,8320]{2,1,0:T(8,128)(2,1)S(1)}, u32[]{:S(2)}, u32[]{:S(2)}) async-start(bf16[8,8,8320]{2,1,0:T(8,128)(2,1)} %bitcast.6), calls=%async_computation | async-start | bytes 2129920 | tf_op jit(solution)/shard_map/all_to_all | solution.py:287
  10.3 2.2 %copy-start.4 = (bf16[128,2,16,512]{3,2,1,0:T(8,128)(2,1)S(1)}, bf16[128,2,16,512]{3,2,1,0:T(8,128)(2,1)}, u32[]{:S(2)}) copy-start(bf16[128,2,16,512]{3,2,1,0:T(8,128)(2,1)} %kv_ref.1) | copy-start | bytes 12582916
  12.5 1.2 %copy-start.11 = (bf16[128,4096]{1,0:T(8,128)(2,1)S(1)}, bf16[128,4096]{1,0:T(8,128)(2,1)}, u32[]{:S(2)}) copy-start(bf16[128,4096]{1,0:T(8,128)(2,1)} %base_ref.1) | copy-start | bytes 3145732
  13.7 23.3 %copy-start = (bf16[8192,128]{1,0:T(8,128)(2,1)S(1)}, bf16[8192,128]{1,0:T(8,128)(2,1)}, u32[]{:S(2)}) copy-start(bf16[8192,128]{1,0:T(8,128)(2,1)} %refs_8_.1) | copy-start | bytes 6291460
  18.7 1.4 %copy-start.1 = (bf16[4,128,2048]{2,1,0:T(8,128)(2,1)}, bf16[4,128,2048]{2,1,0:T(8,128)(2,1)S(1)}, u32[]{:S(2)}) copy-start(bf16[4,128,2048]{2,1,0:T(8,128)(2,1)S(1)} %get-tuple-element.30.refs_3_.refs_11_) | copy-start | bytes 6291460
  20.1 1.3 %copy-start.7 = (bf16[4,2048,128]{2,1,0:T(8,128)(2,1)}, bf16[4,2048,128]{2,1,0:T(8,128)(2,1)S(1)}, u32[]{:S(2)}) copy-start(bf16[4,2048,128]{2,1,0:T(8,128)(2,1)S(1)} %get-tuple-element.47.refs_12_) | copy-start | bytes 6291460
  21.4 1.4 %copy-start.9 = (f32[4,16,64,128]{3,2,1,0:T(8,128)}, f32[4,16,64,128]{3,2,1,0:T(8,128)S(1)}, u32[]{:S(2)}) copy-start(f32[4,16,64,128]{3,2,1,0:T(8,128)S(1)} %get-tuple-element.48.refs_13_) | copy-start | bytes 6291460
  37.0 1.6 %copy-start.2 = (bf16[4,128,2048]{2,1,0:T(8,128)(2,1)S(1)}, bf16[4,128,2048]{2,1,0:T(8,128)(2,1)}, u32[]{:S(2)}) copy-start(bf16[4,128,2048]{2,1,0:T(8,128)(2,1)} %copy-done.1) | copy-start | bytes 6291460
  38.6 1.2 %copy-start.5 = (bf16[128,4096]{1,0:T(8,128)(2,1)S(1)}, bf16[128,4096]{1,0:T(8,128)(2,1)}, u32[]{:S(2)}) copy-start(bf16[128,4096]{1,0:T(8,128)(2,1)} %refs_9_.1) | copy-start | bytes 3145732
  41.4 43.1 %copy-start.6 = (bf16[128,4096]{1,0:T(8,128)(2,1)S(1)}, bf16[128,4096]{1,0:T(8,128)(2,1)}, u32[]{:S(2)}) copy-start(bf16[128,4096]{1,0:T(8,128)(2,1)} %refs_9_.1) | copy-start | bytes 3145732
  41.4 60.1 %all-to-all-start.1 = ((bf16[8,8,4096]{2,1,0:T(8,128)(2,1)}), bf16[8,8,4096]{2,1,0:T(8,128)(2,1)}, u32[]{:S(2)}, u32[]{:S(2)}) async-start(bf16[8,8,4096]{2,1,0:T(8,128)(2,1)} %bitcast.3), calls=%async_computation.1 | async-start | bytes 1048576 | tf_op jit(solution)/shard_map/all_to_all | solution.py:287
  49.3 12.2 %collective-permute-start = (bf16[8,8320]{1,0:T(8,128)(2,1)}, bf16[8,8320]{1,0:T(8,128)(2,1)S(1)}, u32[]{:S(2)}, u32[]{:S(2)}) collective-permute-start(bf16[8,8320]{1,0:T(8,128)(2,1)} %get-tuple-element.31), channel_id=1, source_target_pairs={{0,4},{1,5},{2,6},{3,7},{4,0},{5,1},{6,2},{7,3},{8,12},{9,13},{10,... | collective-permute-start | bytes 399368 | tf_op jit(solution)/shard_map/ppermute | solution.py:294
  49.4 13.8 %collective-permute-start.1 = (bf16[8,8320]{1,0:T(8,128)(2,1)}, bf16[8,8320]{1,0:T(8,128)(2,1)S(1)}, u32[]{:S(2)}, u32[]{:S(2)}) collective-permute-start(bf16[8,8320]{1,0:T(8,128)(2,1)} %get-tuple-element.32), channel_id=1, source_target_pairs={{0,5},{1,4},{2,7},{3,6},{4,1},{5,0},{6,3},{7,2},{8,13},{9,12},{10,... | collective-permute-start | bytes 399368 | tf_op jit(solution)/shard_map/ppermute | solution.py:294
  51.1 26.0 %collective-permute-start.2 = (bf16[8,8320]{1,0:T(8,128)(2,1)}, bf16[8,8320]{1,0:T(8,128)(2,1)S(1)}, u32[]{:S(2)}, u32[]{:S(2)}) collective-permute-start(bf16[8,8320]{1,0:T(8,128)(2,1)} %get-tuple-element.33), channel_id=1, source_target_pairs={{0,6},{1,7},{2,4},{3,5},{4,2},{5,3},{6,0},{7,1},{8,14},{9,15},{10,... | collective-permute-start | bytes 399368 | tf_op jit(solution)/shard_map/ppermute | solution.py:294
  52.7 25.6 %collective-permute-start.3 = (bf16[8,8320]{1,0:T(8,128)(2,1)}, bf16[8,8320]{1,0:T(8,128)(2,1)S(1)}, u32[]{:S(2)}, u32[]{:S(2)}) collective-permute-start(bf16[8,8320]{1,0:T(8,128)(2,1)} %get-tuple-element.34), channel_id=1, source_target_pairs={{0,7},{1,6},{2,5},{3,4},{4,3},{5,2},{6,1},{7,0},{8,15},{9,14},{10,... | collective-permute-start | bytes 399368 | tf_op jit(solution)/shard_map/ppermute | solution.py:294
  53.8 24.6 %collective-permute-start.4 = (bf16[8,8320]{1,0:T(8,128)(2,1)}, bf16[8,8320]{1,0:T(8,128)(2,1)S(1)}, u32[]{:S(2)}, u32[]{:S(2)}) collective-permute-start(bf16[8,8320]{1,0:T(8,128)(2,1)} %get-tuple-element.35), channel_id=1, source_target_pairs={{0,12},{1,13},{2,14},{3,15},{4,8},{5,9},{6,10},{7,11},{8,4},{9,5},... | collective-permute-start | bytes 399368 | tf_op jit(solution)/shard_map/ppermute | solution.py:294
  61.5 16.9 %collective-permute-start.5 = (bf16[8,8320]{1,0:T(8,128)(2,1)}, bf16[8,8320]{1,0:T(8,128)(2,1)S(1)}, u32[]{:S(2)}, u32[]{:S(2)}) collective-permute-start(bf16[8,8320]{1,0:T(8,128)(2,1)} %get-tuple-element.36), channel_id=1, source_target_pairs={{0,13},{1,12},{2,15},{3,14},{4,9},{5,8},{6,11},{7,10},{8,5},{9,4},... | collective-permute-start | bytes 399368 | tf_op jit(solution)/shard_map/ppermute | solution.py:294
  63.2 15.1 %collective-permute-start.6 = (bf16[8,8320]{1,0:T(8,128)(2,1)}, bf16[8,8320]{1,0:T(8,128)(2,1)S(1)}, u32[]{:S(2)}, u32[]{:S(2)}) collective-permute-start(bf16[8,8320]{1,0:T(8,128)(2,1)} %get-tuple-element.37), channel_id=1, source_target_pairs={{0,14},{1,15},{2,12},{3,13},{4,10},{5,11},{6,8},{7,9},{8,6},{9,7},... | collective-permute-start | bytes 399368 | tf_op jit(solution)/shard_map/ppermute | solution.py:294
  77.1 24.4 %copy-start.12 = (bf16[64,128]{1,0:T(8,128)(2,1)S(1)}, bf16[64,128]{1,0:T(8,128)(2,1)}, u32[]{:S(2)}) copy-start(bf16[64,128]{1,0:T(8,128)(2,1)} %get-tuple-element.27.after_ref.refs_0_) | copy-start | bytes 49156
  77.1 24.4 %copy-start.13 = (bf16[64,128]{1,0:T(8,128)(2,1)S(1)}, bf16[64,128]{1,0:T(8,128)(2,1)}, u32[]{:S(2)}) copy-start(bf16[64,128]{1,0:T(8,128)(2,1)} %get-tuple-element.28.refs_1_) | copy-start | bytes 49156
  77.1 7.3 %collective-permute-start.7 = (bf16[8,8320]{1,0:T(8,128)(2,1)}, bf16[8,8320]{1,0:T(8,128)(2,1)S(1)}, u32[]{:S(2)}, u32[]{:S(2)}) collective-permute-start(bf16[8,8320]{1,0:T(8,128)(2,1)} %get-tuple-element.38), channel_id=1, source_target_pairs={{0,15},{1,14},{2,13},{3,12},{4,11},{5,10},{6,9},{7,8},{8,7},{9,6},... | collective-permute-start | bytes 399368 | tf_op jit(solution)/shard_map/ppermute | solution.py:294
  85.2 4.5 %collective-permute-start.8 = (bf16[8,4096]{1,0:T(8,128)(2,1)S(1)}, bf16[8,4096]{1,0:T(8,128)(2,1)S(1)}, u32[]{:S(2)}, u32[]{:S(2)}) collective-permute-start(bf16[8,4096]{1,0:T(8,128)(2,1)S(1)} %get-tuple-element.39), channel_id=1, source_target_pairs={{0,4},{1,5},{2,6},{3,7},{4,0},{5,1},{6,2},{7,3},{8,12},{9,13},{10,... | collective-permute-start | bytes 196616 | tf_op jit(solution)/shard_map/ppermute | solution.py:294
  85.3 6.3 %collective-permute-start.9 = (bf16[8,4096]{1,0:T(8,128)(2,1)S(1)}, bf16[8,4096]{1,0:T(8,128)(2,1)S(1)}, u32[]{:S(2)}, u32[]{:S(2)}) collective-permute-start(bf16[8,4096]{1,0:T(8,128)(2,1)S(1)} %get-tuple-element.40), channel_id=1, source_target_pairs={{0,5},{1,4},{2,7},{3,6},{4,1},{5,0},{6,3},{7,2},{8,13},{9,12},{10,... | collective-permute-start | bytes 196616 | tf_op jit(solution)/shard_map/ppermute | solution.py:294
  85.3 9.6 %collective-permute-start.10 = (bf16[8,4096]{1,0:T(8,128)(2,1)S(1)}, bf16[8,4096]{1,0:T(8,128)(2,1)S(1)}, u32[]{:S(2)}, u32[]{:S(2)}) collective-permute-start(bf16[8,4096]{1,0:T(8,128)(2,1)S(1)} %get-tuple-element.41), channel_id=1, source_target_pairs={{0,6},{1,7},{2,4},{3,5},{4,2},{5,3},{6,0},{7,1},{8,14},{9,15},{10,... | collective-permute-start | bytes 196616 | tf_op jit(solution)/shard_map/ppermute | solution.py:294
  88.2 9.4 %collective-permute-start.11 = (bf16[8,4096]{1,0:T(8,128)(2,1)S(1)}, bf16[8,4096]{1,0:T(8,128)(2,1)S(1)}, u32[]{:S(2)}, u32[]{:S(2)}) collective-permute-start(bf16[8,4096]{1,0:T(8,128)(2,1)S(1)} %get-tuple-element.42), channel_id=1, source_target_pairs={{0,7},{1,6},{2,5},{3,4},{4,3},{5,2},{6,1},{7,0},{8,15},{9,14},{10,... | collective-permute-start | bytes 196616 | tf_op jit(solution)/shard_map/ppermute | solution.py:294
  89.6 8.0 %collective-permute-start.12 = (bf16[8,4096]{1,0:T(8,128)(2,1)S(1)}, bf16[8,4096]{1,0:T(8,128)(2,1)S(1)}, u32[]{:S(2)}, u32[]{:S(2)}) collective-permute-start(bf16[8,4096]{1,0:T(8,128)(2,1)S(1)} %get-tuple-element.43), channel_id=1, source_target_pairs={{0,12},{1,13},{2,14},{3,15},{4,8},{5,9},{6,10},{7,11},{8,4},{9,5},... | collective-permute-start | bytes 196616 | tf_op jit(solution)/shard_map/ppermute | solution.py:294
  89.7 7.9 %collective-permute-start.13 = (bf16[8,4096]{1,0:T(8,128)(2,1)S(1)}, bf16[8,4096]{1,0:T(8,128)(2,1)S(1)}, u32[]{:S(2)}, u32[]{:S(2)}) collective-permute-start(bf16[8,4096]{1,0:T(8,128)(2,1)S(1)} %get-tuple-element.44), channel_id=1, source_target_pairs={{0,13},{1,12},{2,15},{3,14},{4,9},{5,8},{6,11},{7,10},{8,5},{9,4},... | collective-permute-start | bytes 196616 | tf_op jit(solution)/shard_map/ppermute | solution.py:294
  91.6 7.3 %collective-permute-start.14 = (bf16[8,4096]{1,0:T(8,128)(2,1)S(1)}, bf16[8,4096]{1,0:T(8,128)(2,1)S(1)}, u32[]{:S(2)}, u32[]{:S(2)}) collective-permute-start(bf16[8,4096]{1,0:T(8,128)(2,1)S(1)} %get-tuple-element.45), channel_id=1, source_target_pairs={{0,14},{1,15},{2,12},{3,13},{4,10},{5,11},{6,8},{7,9},{8,6},{9,7},... | collective-permute-start | bytes 196616 | tf_op jit(solution)/shard_map/ppermute | solution.py:294
  94.9 6.6 %collective-permute-start.15 = (bf16[8,4096]{1,0:T(8,128)(2,1)S(1)}, bf16[8,4096]{1,0:T(8,128)(2,1)S(1)}, u32[]{:S(2)}, u32[]{:S(2)}) collective-permute-start(bf16[8,4096]{1,0:T(8,128)(2,1)S(1)} %get-tuple-element.46), channel_id=1, source_target_pairs={{0,15},{1,14},{2,13},{3,12},{4,11},{5,10},{6,9},{7,8},{8,7},{9,6},... | collective-permute-start | bytes 196616 | tf_op jit(solution)/shard_map/ppermute | solution.py:294
  101.5 1.6 %copy-start.3 = (bf16[4,128,2048]{2,1,0:T(8,128)(2,1)S(1)}, bf16[4,128,2048]{2,1,0:T(8,128)(2,1)}, u32[]{:S(2)}) copy-start(bf16[4,128,2048]{2,1,0:T(8,128)(2,1)} %copy-done.1) | copy-start | bytes 6291460
  103.1 1.6 %copy-start.8 = (bf16[4,2048,128]{2,1,0:T(8,128)(2,1)S(1)}, bf16[4,2048,128]{2,1,0:T(8,128)(2,1)}, u32[]{:S(2)}) copy-start(bf16[4,2048,128]{2,1,0:T(8,128)(2,1)} %copy-done.7) | copy-start | bytes 6291460
  104.7 1.6 %copy-start.10 = (f32[4,16,64,128]{3,2,1,0:T(8,128)S(1)}, f32[4,16,64,128]{3,2,1,0:T(8,128)}, u32[]{:S(2)}) copy-start(f32[4,16,64,128]{3,2,1,0:T(8,128)} %copy-done.9) | copy-start | bytes 6291460

commit v6 on v5

--- a/solution.py
+++ b/solution.py
@@ -159,7 +159,7 @@
     return jnp.concatenate([rows[:, g * HEAD : (g + 1) * HEAD] for g in range(group)], axis=0)
 
 
-def prep_kernel(group, context, base_ref, kv_ref, len_ref, keys_ref, values_ref, scores_ref):
+def prep_kernel(group, context, base_ref, kv_ref, len_ref, _, keys_ref, values_ref, scores_ref):
     step = ROWS_STEP
     cells = step * context
     lane = lax.broadcasted_iota(jnp.int32, (group * step, cells), 1)
@@ -179,7 +179,7 @@
         scores_ref[k, 0] = jnp.where(live, scores * factor, -jnp.inf)
 
 
-def prep(base_q, kv_cache, cache_len):
+def prep(base_q, kv_cache, cache_len, after):
     rows, width = base_q.shape
     context = kv_cache.shape[2]
     group = width // (KVH * HEAD)
@@ -194,6 +194,7 @@
             pl.BlockSpec((step, width), lambda i: (i, 0)),
             pl.BlockSpec((step, *kv_cache.shape[1:]), lambda i: (i, 0, 0, 0)),
             pl.BlockSpec((1, 1, cells), lambda i: (i, 0, 0)),
+            pl.BlockSpec(memory_space=pl.ANY),
         ],
         out_specs=[
             pl.BlockSpec((KVH, HEAD, cells), lambda i: (0, 0, i)),
@@ -210,7 +211,7 @@
             flops=2 * rows * width * cells, bytes_accessed=16 * 2**20, transcendentals=0
         ),
         name="prep",
-    )(base_q, kv_cache, lens)
+    )(base_q, kv_cache, lens, after)
 
 
 def attend_kernel(group, count, *refs):
@@ -264,7 +265,7 @@
     return pl.pallas_call(
         functools.partial(attend_kernel, width // (KVH * HEAD), len(returned)),
         in_specs=[pl.BlockSpec(memory_space=pltpu.VMEM)] * (2 + len(returned))
-        + [pl.BlockSpec(memory_space=pl.ANY)] * len(laid),
+        + [pl.BlockSpec(memory_space=pltpu.HBM)] * len(laid),
         out_specs=pl.BlockSpec(memory_space=pltpu.VMEM),
         out_shape=jax.ShapeDtypeStruct((rows, width), jnp.bfloat16),
         scratch_shapes=[pltpu.VMEM(part.shape, part.dtype) for part in laid]
@@ -289,23 +290,28 @@
         )
         return blocks.reshape(lines.shape)
 
-    def trade(messages):
+    def trade(messages, offsets):
         return [
             lax.ppermute(message, "owner", [(i, i ^ apart) for i in range(owners)])
-            for message, apart in zip(messages, halves[1])
+            for message, apart in zip(messages, offsets)
         ]
 
+    near, far = halves[1][:quarter], halves[1][quarter:]
     whole = functools.partial(pack, hidden, adapter_id, adapter_slot)
     routed, lines = whole(adapter_id, False, owners, slot_count, held)
+    arrived = swap(lines)
     routed_pairs, *messages = whole(routed, True, owners, slot_count, held)
-    arrived = swap(lines)
-    arrived_pairs = trade(messages)
-    laid = prep(base_q, kv_cache, cache_len)
-    (change,) = adapt([arrived], a_maps, b_maps, laid[0])
+    arrived_near = trade(messages[:quarter], near)
+    arrived_far = trade(messages[quarter:], far)
+    laid = prep(base_q, kv_cache, cache_len, routed_pairs)
+    change_near = adapt(arrived_near, a_maps, b_maps, laid[0])
+    (change,) = adapt([arrived], a_maps, b_maps, change_near[0])
     returned = swap(change)
-    changes = adapt(arrived_pairs, a_maps, b_maps, change)
-    returned_pairs = trade(changes)
-    return attend([routed, routed_pairs], [returned, *returned_pairs], laid, base_q.shape[1])
+    change_far = adapt(arrived_far, a_maps, b_maps, change)
+    returned_far = trade(change_far, far)
+    returned_near = trade(change_near, near)
+    returned = [returned, *returned_near, *returned_far]
+    return attend([routed, routed_pairs], returned, laid, base_q.shape[1])
 
 
 def solution(mesh):

time: 114 us -> 118 us (1.035)
  the two profiles are of different devices: /device:TPU:0 before, /device:TPU:9 now
where the time goes in v6:
time: 118 us; the launch traced here: 117 us
  waiting for transfers between devices  44.3 us (38%)
  starting transfers between devices  31.2 us (26%)
  Pallas kernels  23.7 us (20%)
  local copies, waits for them, and re-layouts  17.8 us (15%)
    ppermute x16, waiting for transfers between devices, trade(): lax.ppermute(message, 'owner', [(i, i ^ apart) for i in range(owners)])  44.3 us
    ppermute x16, starting transfers between devices, trade(): lax.ppermute(message, 'owner', [(i, i ^ apart) for i in range(owners)])  17.8 us
    unnamed x42, local copies, waits for them, and re-layouts  17 us
    all_to_all x2, starting transfers between devices, swap(): lax.all_to_all(blocks, 'owner', split_axis=0, concat_axis=0, tiled=True,...  13.5 us
    pallas_call x2, Pallas kernels, pack(): pl.pallas_call(functools.partial(pack_kernel, pairs, owners, slot_count,...  7.19 us
    pallas_call x1, Pallas kernels, attend(): pl.pallas_call(functools.partial(attend_kernel, width // (KVH * HEAD), le...  6.6 us
    pallas_call x1, Pallas kernels, prep(): pl.pallas_call(functools.partial(prep_kernel, group, context), grid=(step...  4.99 us
    pallas_call x3, Pallas kernels, adapt(): pl.pallas_call(functools.partial(adapt_kernel, count), in_specs=[pl.Block...  4.96 us
  transfers between devices with their start and end apart: 18, of which 10 were waited for; matrix products, arithmetic and copies ran while one was open for 1% of the time, Pallas kernels for 10%

profile of v6, /device:TPU:9, one launch (start us, length us, event | category | flops | bytes accessed | tf_op | source)
XLA Modules:
  0.0 117.2 jit_solution(17755422944714281719)
XLA Ops:
  0.0 3.6 %pack.1 = (bf16[64,128]{1,0:T(8,128)(2,1)}, bf16[64,8320]{1,0:T(8,128)(2,1)}) custom-call(s32[32]{0:T(128)} %slots_ref.3, s32[1,128]{1,0:T(1,128)} %bitcast.7, bf16[128,8192]{1,0:T(8,128)(2,1)} %hidden_ref.3, s32[128]{0:T(128)} %after_ref.1), custom_call_target="tpu_custom_call" | custom-call | tf_op jit(solution)/shard_map/pack/pallas_call | solution.py:87
  3.6 5.5 %all-to-all-start = ((bf16[8,8,8320]{2,1,0:T(8,128)(2,1)}), bf16[8,8,8320]{2,1,0:T(8,128)(2,1)}, u32[]{:S(2)}, u32[]{:S(2)}) async-start(bf16[8,8,8320]{2,1,0:T(8,128)(2,1)} %bitcast.6), calls=%async_computation | async-start | bytes 2129920 | tf_op jit(solution)/shard_map/all_to_all | solution.py:288
  9.1 3.6 %pack_pairs.1 = (bf16[64,128]{1,0:T(8,128)(2,1)}, bf16[8,8320]{1,0:T(8,128)(2,1)}, bf16[8,8320]{1,0:T(8,128)(2,1)}, bf16[8,8320]{1,0:T(8,128)(2,1)}, bf16[8,8320...) custom-call(s32[32]{0:T(128)} %slots_ref.3, ...), custom_call_target="tpu_custom_call" | custom-call | tf_op jit(solution)/shard_map/pack_pairs/pallas_call | solution.py:87
  12.7 0.2 collective-permute-start
  12.9 1.5 %collective-permute-start.1 = (bf16[8,8320]{1,0:T(8,128)(2,1)}, bf16[8,8320]{1,0:T(8,128)(2,1)S(1)}, u32[]{:S(2)}, u32[]{:S(2)}) collective-permute-start(bf16[8,8320]{1,0:T(8,128)(2,1)} %get-tuple-element.31), channel_id=1, source_target_pairs={{0,5},{1,4},{2,7},{3,6},{4,1},{5,0},{6,3},{7,2},{8,13},{9,12},{10,... | collective-permute-start | bytes 399368 | tf_op jit(solution)/shard_map/ppermute | solution.py:295
  14.4 1.6 %collective-permute-start.2 = (bf16[8,8320]{1,0:T(8,128)(2,1)}, bf16[8,8320]{1,0:T(8,128)(2,1)S(1)}, u32[]{:S(2)}, u32[]{:S(2)}) collective-permute-start(bf16[8,8320]{1,0:T(8,128)(2,1)} %get-tuple-element.32), channel_id=1, source_target_pairs={{0,6},{1,7},{2,4},{3,5},{4,2},{5,3},{6,0},{7,1},{8,14},{9,15},{10,... | collective-permute-start | bytes 399368 | tf_op jit(solution)/shard_map/ppermute | solution.py:295
  16.0 1.1 collective-permute-start.3
  17.3 0.7 broadcast_in_dim.9.len_ref
  18.0 2.2 %copy-done.6 = bf16[128,2,16,512]{3,2,1,0:T(8,128)(2,1)S(1)} copy-done((bf16[128,2,16,512]{3,2,1,0:T(8,128)(2,1)S(1)}, bf16[128,2,16,512]{3,2,1,0:T(8,128)(2,1)}, u32[]{:S(2)}) %copy-start.6) | copy-done | bytes 4194328
  20.2 1.2 %copy-done.11 = bf16[128,4096]{1,0:T(8,128)(2,1)S(1)} copy-done((bf16[128,4096]{1,0:T(8,128)(2,1)S(1)}, bf16[128,4096]{1,0:T(8,128)(2,1)}, u32[]{:S(2)}) %copy-start.11) | copy-done | bytes 1048600
  21.4 0.7 copy-done.16
  22.2 0.7 copy-done.18
  22.9 5.0 %prep.1 = (bf16[4,128,2048]{2,1,0:T(8,128)(2,1)S(1)}, bf16[4,2048,128]{2,1,0:T(8,128)(2,1)S(1)}, f32[4,16,64,128]{3,2,1,0:T(8,128)S(1)}) custom-call(bf16[128,4096]{1,0:T(8,128)(2,1)S(1)} %copy-done.11, bf16[128,2,16,512]{3,2,1,0:T(8,128)(2,1)S(1)} %copy-done.6, s32[16,1,128]{2,1,0:T(1,128)S(1)} %copy-done.18, bf16[64,128]{1,0:T(8,128)(2,1)S(1)} %copy-done.16), custom_call_target="tpu_custom_call" | custom-call | flops 134217728 | bytes 16777216 | tf_op jit(solution)/shard_map/prep/pallas_call | solution.py:190
  27.9 1.3 %copy-done.7 = bf16[4,2048,128]{2,1,0:T(8,128)(2,1)} copy-done((bf16[4,2048,128]{2,1,0:T(8,128)(2,1)}, bf16[4,2048,128]{2,1,0:T(8,128)(2,1)S(1)}, u32[]{:S(2)}) %copy-start.7) | copy-done | bytes 2097176
  29.2 1.3 %copy-done.9 = f32[4,16,64,128]{3,2,1,0:T(8,128)} copy-done((f32[4,16,64,128]{3,2,1,0:T(8,128)}, f32[4,16,64,128]{3,2,1,0:T(8,128)S(1)}, u32[]{:S(2)}) %copy-start.9) | copy-done | bytes 2097176
  30.5 0.8 collective-permute-done.2.refs_2_
  31.4 3.7 %collective-permute-done.3.refs_3_ = bf16[8,8320]{1,0:T(8,128)(2,1)} collective-permute-done((bf16[8,8320]{1,0:T(8,128)(2,1)}, bf16[8,8320]{1,0:T(8,128)(2,1)}, u32[]{:S(2)}, u32[]{:S(2)}) %collective-permute-start.3) | collective-permute-done | bytes 133152 | tf_op jit(solution)/shard_map/ppermute | solution.py:295
  35.1 2.3 %adapt.3 = (bf16[8,4096]{1,0:T(8,128)(2,1)S(1)}, bf16[8,4096]{1,0:T(8,128)(2,1)}, bf16[8,4096]{1,0:T(8,128)(2,1)}, bf16[8,4096]{1,0:T(8,128)(2,1)}) custom-call(bf16[8,8320]{1,0:T(8,128)(2,1)S(1)} %collective-permute-done.refs_0_, bf16[8,8320]{1,0:T(8,128)(2,1)S(1)} %collective-permute-done.1.refs_1_, bf16[8,8320]{1,0:T(8,128)(2,1)S(1)} %collective-permute-done.2.refs_2_, ...), custom_call_target="tpu_custom_call" | custom-call | flops 100663296 | bytes 3145728 | tf_op jit(solution)/shard_map/adapt/pallas_call | solution.py:142
  37.3 1.4 %copy-done.2 = bf16[4,128,2048]{2,1,0:T(8,128)(2,1)} copy-done((bf16[4,128,2048]{2,1,0:T(8,128)(2,1)}, bf16[4,128,2048]{2,1,0:T(8,128)(2,1)S(1)}, u32[]{:S(2)}) %copy-start.2) | copy-done | bytes 2097176
  38.7 0.6 copy-done.12
  39.3 0.8 copy-done.13
  40.2 2.0 %adapt.4.refs_6_ = bf16[64,4096]{1,0:T(8,128)(2,1)S(1)} custom-call(bf16[64,8320]{1,0:T(8,128)(2,1)} %bitcast.2.refs_0_, bf16[8192,128]{1,0:T(8,128)(2,1)S(1)} %copy-done, bf16[128,4096]{1,0:T(8,128)(2,1)S(1)} %copy-done.1, bf16[8,4096]{1,0:T(8,128)(2,1)S(1)} %copy-done.13), custom_call_target="tpu_custom_call" | custom-call | flops 201326592 | bytes 3145728 | tf_op jit(solution)/shard_map/adapt/pallas_call | solution.py:142
  42.2 0.8 copy-done.4
  43.0 8.0 %all-to-all-start.1 = ((bf16[8,8,4096]{2,1,0:T(8,128)(2,1)}), bf16[8,8,4096]{2,1,0:T(8,128)(2,1)}, u32[]{:S(2)}, u32[]{:S(2)}) async-start(bf16[8,8,4096]{2,1,0:T(8,128)(2,1)} %bitcast.5), calls=%async_computation.1 | async-start | bytes 1048576 | tf_op jit(solution)/shard_map/all_to_all | solution.py:288
  51.0 0.9 collective-permute-start.8
  51.9 0.7 collective-permute-start.9
  52.6 2.2 %collective-permute-start.10 = (bf16[8,8320]{1,0:T(8,128)(2,1)S(1)}, bf16[8,8320]{1,0:T(8,128)(2,1)S(1)}, u32[]{:S(2)}, u32[]{:S(2)}) collective-permute-start(bf16[8,8320]{1,0:T(8,128)(2,1)S(1)} %copy-done.20), channel_id=1, source_target_pairs={{0,14},{1,15},{2,12},{3,13},{4,10},{5,11},{6,8},{7,9},{8,6},{9,7},... | collective-permute-start | bytes 399368 | tf_op jit(solution)/shard_map/ppermute | solution.py:295
  54.8 0.6 collective-permute-start.11
  55.4 4.1 %collective-permute-start.5 = (bf16[8,4096]{1,0:T(8,128)(2,1)}, bf16[8,4096]{1,0:T(8,128)(2,1)S(1)}, u32[]{:S(2)}, u32[]{:S(2)}) collective-permute-start(bf16[8,4096]{1,0:T(8,128)(2,1)} %get-tuple-element.36), channel_id=1, source_target_pairs={{0,5},{1,4},{2,7},{3,6},{4,1},{5,0},{6,3},{7,2},{8,13},{9,12},{10,... | collective-permute-start | bytes 196616 | tf_op jit(solution)/shard_map/ppermute | solution.py:295
  59.5 19.0 %collective-permute-done.8.refs_0_ = bf16[8,8320]{1,0:T(8,128)(2,1)S(1)} collective-permute-done((bf16[8,8320]{1,0:T(8,128)(2,1)}, bf16[8,8320]{1,0:T(8,128)(2,1)S(1)}, u32[]{:S(2)}, u32[]{:S(2)}) %collective-permute-start.8) | collective-permute-done | bytes 133152 | tf_op jit(solution)/shard_map/ppermute | solution.py:295
  78.5 3.5 %collective-permute-done.9.refs_1_ = bf16[8,8320]{1,0:T(8,128)(2,1)S(1)} collective-permute-done((bf16[8,8320]{1,0:T(8,128)(2,1)}, bf16[8,8320]{1,0:T(8,128)(2,1)S(1)}, u32[]{:S(2)}, u32[]{:S(2)}) %collective-permute-start.9) | collective-permute-done | bytes 133152 | tf_op jit(solution)/shard_map/ppermute | solution.py:295
  82.0 0.4 collective-permute-start.7
  82.3 3.5 %collective-permute-done.10.refs_2_ = bf16[8,8320]{1,0:T(8,128)(2,1)S(1)} collective-permute-done((bf16[8,8320]{1,0:T(8,128)(2,1)S(1)}, bf16[8,8320]{1,0:T(8,128)(2,1)S(1)}, u32[]{:S(2)}, u32[]{:S(2)}) %collective-permute-start.10) | collective-permute-done | bytes 133152 | tf_op jit(solution)/shard_map/ppermute | solution.py:295
  85.8 4.6 %collective-permute-done.11.refs_3_ = bf16[8,8320]{1,0:T(8,128)(2,1)S(1)} collective-permute-done((bf16[8,8320]{1,0:T(8,128)(2,1)}, bf16[8,8320]{1,0:T(8,128)(2,1)S(1)}, u32[]{:S(2)}, u32[]{:S(2)}) %collective-permute-start.11) | collective-permute-done | bytes 133152 | tf_op jit(solution)/shard_map/ppermute | solution.py:295
  90.5 1.0 copy-done.5
  91.5 0.7 adapt.5
  92.2 0.8 collective-permute-start.12
  93.0 1.1 collective-permute-start.13
  94.1 1.0 collective-permute-start.14
  95.1 1.6 %collective-permute-start.15 = (bf16[8,4096]{1,0:T(8,128)(2,1)S(1)}, bf16[8,4096]{1,0:T(8,128)(2,1)S(1)}, u32[]{:S(2)}, u32[]{:S(2)}) collective-permute-start(bf16[8,4096]{1,0:T(8,128)(2,1)S(1)} %get-tuple-element.46), channel_id=1, source_target_pairs={{0,15},{1,14},{2,13},{3,12},{4,11},{5,10},{6,9},{7,8},{8,7},{9,6},... | collective-permute-start | bytes 196616 | tf_op jit(solution)/shard_map/ppermute | solution.py:295
  96.7 2.2 %collective-permute-done.12.refs_7_ = bf16[8,4096]{1,0:T(8,128)(2,1)S(1)} collective-permute-done((bf16[8,4096]{1,0:T(8,128)(2,1)S(1)}, bf16[8,4096]{1,0:T(8,128)(2,1)S(1)}, u32[]{:S(2)}, u32[]{:S(2)}) %collective-permute-start.12) | collective-permute-done | bytes 65568 | tf_op jit(solution)/shard_map/ppermute | solution.py:295
  98.8 4.1 %collective-permute-done.13.refs_8_ = bf16[8,4096]{1,0:T(8,128)(2,1)S(1)} collective-permute-done((bf16[8,4096]{1,0:T(8,128)(2,1)S(1)}, bf16[8,4096]{1,0:T(8,128)(2,1)S(1)}, u32[]{:S(2)}, u32[]{:S(2)}) %collective-permute-start.13) | collective-permute-done | bytes 65568 | tf_op jit(solution)/shard_map/ppermute | solution.py:295
  102.9 1.4 %collective-permute-done.14.refs_9_ = bf16[8,4096]{1,0:T(8,128)(2,1)S(1)} collective-permute-done((bf16[8,4096]{1,0:T(8,128)(2,1)S(1)}, bf16[8,4096]{1,0:T(8,128)(2,1)S(1)}, u32[]{:S(2)}, u32[]{:S(2)}) %collective-permute-start.14) | collective-permute-done | bytes 65568 | tf_op jit(solution)/shard_map/ppermute | solution.py:295
  104.4 1.4 %collective-permute-done.15.refs_10_ = bf16[8,4096]{1,0:T(8,128)(2,1)S(1)} collective-permute-done((bf16[8,4096]{1,0:T(8,128)(2,1)S(1)}, bf16[8,4096]{1,0:T(8,128)(2,1)S(1)}, u32[]{:S(2)}, u32[]{:S(2)}) %collective-permute-start.15) | collective-permute-done | bytes 65568 | tf_op jit(solution)/shard_map/ppermute | solution.py:295
  105.8 1.6 %copy-done.3 = bf16[4,128,2048]{2,1,0:T(8,128)(2,1)S(1)} copy-done((bf16[4,128,2048]{2,1,0:T(8,128)(2,1)S(1)}, bf16[4,128,2048]{2,1,0:T(8,128)(2,1)}, u32[]{:S(2)}) %copy-start.3) | copy-done | bytes 2097176
  107.4 1.6 %copy-done.8 = bf16[4,2048,128]{2,1,0:T(8,128)(2,1)S(1)} copy-done((bf16[4,2048,128]{2,1,0:T(8,128)(2,1)S(1)}, bf16[4,2048,128]{2,1,0:T(8,128)(2,1)}, u32[]{:S(2)}) %copy-start.8) | copy-done | bytes 2097176
  109.0 1.6 %copy-done.10 = f32[4,16,64,128]{3,2,1,0:T(8,128)S(1)} copy-done((f32[4,16,64,128]{3,2,1,0:T(8,128)S(1)}, f32[4,16,64,128]{3,2,1,0:T(8,128)}, u32[]{:S(2)}) %copy-start.10) | copy-done | bytes 2097176
  110.6 6.6 %attend.1 = bf16[128,4096]{1,0:T(8,128)(2,1)} custom-call(bf16[64,128]{1,0:T(8,128)(2,1)S(1)} %copy-done.15, bf16[64,128]{1,0:T(8,128)(2,1)S(1)} %copy-done.17, bf16[64,4096]{1,0:T(8,128)(2,1)} %bitcast.4.refs_2_, bf16[8,4096]{1,0:T(8,128)(2,1)S(1)} %collective-permute-done.4.refs_3_, bf16[8,4096]{1,0:T(8,128)(2,1)S(1)} %collective-permute-done.5.refs_4_, ...), custom_call_target="tpu_custom_call" | custom-call | tf_op jit(solution)/shard_map/attend/pallas_call | solution.py:265
  (40 shorter events, 0.2 us)
Async XLA Ops:
  3.6 13.5 %copy-start.19 = (s32[128]{0:T(128)S(1)}, s32[128]{0:T(128)}, u32[]{:S(2)}) copy-start(s32[128]{0:T(128)} %param.11) | copy-start | bytes 1540
  3.6 35.7 %all-to-all-start = ((bf16[8,8,8320]{2,1,0:T(8,128)(2,1)}), bf16[8,8,8320]{2,1,0:T(8,128)(2,1)}, u32[]{:S(2)}, u32[]{:S(2)}) async-start(bf16[8,8,8320]{2,1,0:T(8,128)(2,1)} %bitcast.6), calls=%async_computation | async-start | bytes 2129920 | tf_op jit(solution)/shard_map/all_to_all | solution.py:288
  12.7 17.9 %collective-permute-start = (bf16[8,8320]{1,0:T(8,128)(2,1)}, bf16[8,8320]{1,0:T(8,128)(2,1)S(1)}, u32[]{:S(2)}, u32[]{:S(2)}) collective-permute-start(bf16[8,8320]{1,0:T(8,128)(2,1)} %get-tuple-element.30), channel_id=1, source_target_pairs={{0,4},{1,5},{2,6},{3,7},{4,0},{5,1},{6,2},{7,3},{8,12},{9,13},{10,... | collective-permute-start | bytes 399368 | tf_op jit(solution)/shard_map/ppermute | solution.py:295
  12.9 17.6 %collective-permute-start.1 = (bf16[8,8320]{1,0:T(8,128)(2,1)}, bf16[8,8320]{1,0:T(8,128)(2,1)S(1)}, u32[]{:S(2)}, u32[]{:S(2)}) collective-permute-start(bf16[8,8320]{1,0:T(8,128)(2,1)} %get-tuple-element.31), channel_id=1, source_target_pairs={{0,5},{1,4},{2,7},{3,6},{4,1},{5,0},{6,3},{7,2},{8,13},{9,12},{10,... | collective-permute-start | bytes 399368 | tf_op jit(solution)/shard_map/ppermute | solution.py:295
  14.4 17.0 %collective-permute-start.2 = (bf16[8,8320]{1,0:T(8,128)(2,1)}, bf16[8,8320]{1,0:T(8,128)(2,1)S(1)}, u32[]{:S(2)}, u32[]{:S(2)}) collective-permute-start(bf16[8,8320]{1,0:T(8,128)(2,1)} %get-tuple-element.32), channel_id=1, source_target_pairs={{0,6},{1,7},{2,4},{3,5},{4,2},{5,3},{6,0},{7,1},{8,14},{9,15},{10,... | collective-permute-start | bytes 399368 | tf_op jit(solution)/shard_map/ppermute | solution.py:295
  16.0 19.0 %collective-permute-start.3 = (bf16[8,8320]{1,0:T(8,128)(2,1)}, bf16[8,8320]{1,0:T(8,128)(2,1)}, u32[]{:S(2)}, u32[]{:S(2)}) collective-permute-start(bf16[8,8320]{1,0:T(8,128)(2,1)} %get-tuple-element.33), channel_id=1, source_target_pairs={{0,7},{1,6},{2,5},{3,4},{4,3},{5,2},{6,1},{7,0},{8,15},{9,14},{10,... | collective-permute-start | bytes 399368 | tf_op jit(solution)/shard_map/ppermute | solution.py:295
  18.0 2.2 %copy-start.6 = (bf16[128,2,16,512]{3,2,1,0:T(8,128)(2,1)S(1)}, bf16[128,2,16,512]{3,2,1,0:T(8,128)(2,1)}, u32[]{:S(2)}) copy-start(bf16[128,2,16,512]{3,2,1,0:T(8,128)(2,1)} %kv_ref.1) | copy-start | bytes 12582916
  20.2 1.2 %copy-start.11 = (bf16[128,4096]{1,0:T(8,128)(2,1)S(1)}, bf16[128,4096]{1,0:T(8,128)(2,1)}, u32[]{:S(2)}) copy-start(bf16[128,4096]{1,0:T(8,128)(2,1)} %base_ref.1) | copy-start | bytes 3145732
  21.4 0.7 copy-start.16
  22.2 0.7 copy-start.18
  22.9 12.2 %copy-start = (bf16[8192,128]{1,0:T(8,128)(2,1)S(1)}, bf16[8192,128]{1,0:T(8,128)(2,1)}, u32[]{:S(2)}) copy-start(bf16[8192,128]{1,0:T(8,128)(2,1)} %refs_4_.3) | copy-start | bytes 6291460
  22.9 12.2 %copy-start.1 = (bf16[128,4096]{1,0:T(8,128)(2,1)S(1)}, bf16[128,4096]{1,0:T(8,128)(2,1)}, u32[]{:S(2)}) copy-start(bf16[128,4096]{1,0:T(8,128)(2,1)} %refs_5_.3) | copy-start | bytes 3145732
  27.9 1.4 %copy-start.7 = (bf16[4,2048,128]{2,1,0:T(8,128)(2,1)}, bf16[4,2048,128]{2,1,0:T(8,128)(2,1)S(1)}, u32[]{:S(2)}) copy-start(bf16[4,2048,128]{2,1,0:T(8,128)(2,1)S(1)} %get-tuple-element.47.refs_12_) | copy-start | bytes 6291460
  29.2 1.3 %copy-start.9 = (f32[4,16,64,128]{3,2,1,0:T(8,128)}, f32[4,16,64,128]{3,2,1,0:T(8,128)S(1)}, u32[]{:S(2)}) copy-start(f32[4,16,64,128]{3,2,1,0:T(8,128)S(1)} %get-tuple-element.48.refs_13_) | copy-start | bytes 6291460
  37.3 1.4 %copy-start.2 = (bf16[4,128,2048]{2,1,0:T(8,128)(2,1)}, bf16[4,128,2048]{2,1,0:T(8,128)(2,1)S(1)}, u32[]{:S(2)}) copy-start(bf16[4,128,2048]{2,1,0:T(8,128)(2,1)S(1)} %get-tuple-element.34.refs_6_.refs_11_) | copy-start | bytes 6291460
  38.7 0.6 copy-start.12
  39.3 0.8 copy-start.13
  40.2 12.5 %copy-start.20 = (bf16[8,8320]{1,0:T(8,128)(2,1)S(1)}, bf16[8,8320]{1,0:T(8,128)(2,1)}, u32[]{:S(2)}) copy-start(bf16[8,8320]{1,0:T(8,128)(2,1)} %get-tuple-element.41) | copy-start | bytes 399364
  40.2 45.6 %copy-start.14 = (bf16[8,4096]{1,0:T(8,128)(2,1)S(1)}, bf16[8,4096]{1,0:T(8,128)(2,1)}, u32[]{:S(2)}) copy-start(bf16[8,4096]{1,0:T(8,128)(2,1)} %copy-done.12) | copy-start | bytes 196612
  42.2 0.8 copy-start.4
  43.0 62.8 %all-to-all-start.1 = ((bf16[8,8,4096]{2,1,0:T(8,128)(2,1)}), bf16[8,8,4096]{2,1,0:T(8,128)(2,1)}, u32[]{:S(2)}, u32[]{:S(2)}) async-start(bf16[8,8,4096]{2,1,0:T(8,128)(2,1)} %bitcast.5), calls=%async_computation.1 | async-start | bytes 1048576 | tf_op jit(solution)/shard_map/all_to_all | solution.py:288
  51.0 27.5 %collective-permute-start.8 = (bf16[8,8320]{1,0:T(8,128)(2,1)}, bf16[8,8320]{1,0:T(8,128)(2,1)S(1)}, u32[]{:S(2)}, u32[]{:S(2)}) collective-permute-start(bf16[8,8320]{1,0:T(8,128)(2,1)} %get-tuple-element.39), channel_id=1, source_target_pairs={{0,12},{1,13},{2,14},{3,15},{4,8},{5,9},{6,10},{7,11},{8,4},{9,5},... | collective-permute-start | bytes 399368 | tf_op jit(solution)/shard_map/ppermute | solution.py:295
  51.9 30.0 %collective-permute-start.9 = (bf16[8,8320]{1,0:T(8,128)(2,1)}, bf16[8,8320]{1,0:T(8,128)(2,1)S(1)}, u32[]{:S(2)}, u32[]{:S(2)}) collective-permute-start(bf16[8,8320]{1,0:T(8,128)(2,1)} %get-tuple-element.40), channel_id=1, source_target_pairs={{0,13},{1,12},{2,15},{3,14},{4,9},{5,8},{6,11},{7,10},{8,5},{9,4},... | collective-permute-start | bytes 399368 | tf_op jit(solution)/shard_map/ppermute | solution.py:295
  52.6 33.2 %collective-permute-start.10 = (bf16[8,8320]{1,0:T(8,128)(2,1)S(1)}, bf16[8,8320]{1,0:T(8,128)(2,1)S(1)}, u32[]{:S(2)}, u32[]{:S(2)}) collective-permute-start(bf16[8,8320]{1,0:T(8,128)(2,1)S(1)} %copy-done.20), channel_id=1, source_target_pairs={{0,14},{1,15},{2,12},{3,13},{4,10},{5,11},{6,8},{7,9},{8,6},{9,7},... | collective-permute-start | bytes 399368 | tf_op jit(solution)/shard_map/ppermute | solution.py:295
  54.8 35.6 %collective-permute-start.11 = (bf16[8,8320]{1,0:T(8,128)(2,1)}, bf16[8,8320]{1,0:T(8,128)(2,1)S(1)}, u32[]{:S(2)}, u32[]{:S(2)}) collective-permute-start(bf16[8,8320]{1,0:T(8,128)(2,1)} %get-tuple-element.42), channel_id=1, source_target_pairs={{0,15},{1,14},{2,13},{3,12},{4,11},{5,10},{6,9},{7,8},{8,7},{9,6},... | collective-permute-start | bytes 399368 | tf_op jit(solution)/shard_map/ppermute | solution.py:295
  55.4 37.6 %collective-permute-start.5 = (bf16[8,4096]{1,0:T(8,128)(2,1)}, bf16[8,4096]{1,0:T(8,128)(2,1)S(1)}, u32[]{:S(2)}, u32[]{:S(2)}) collective-permute-start(bf16[8,4096]{1,0:T(8,128)(2,1)} %get-tuple-element.36), channel_id=1, source_target_pairs={{0,5},{1,4},{2,7},{3,6},{4,1},{5,0},{6,3},{7,2},{8,13},{9,12},{10,... | collective-permute-start | bytes 196616 | tf_op jit(solution)/shard_map/ppermute | solution.py:295
  78.5 15.6 %collective-permute-start.6 = (bf16[8,4096]{1,0:T(8,128)(2,1)}, bf16[8,4096]{1,0:T(8,128)(2,1)S(1)}, u32[]{:S(2)}, u32[]{:S(2)}) collective-permute-start(bf16[8,4096]{1,0:T(8,128)(2,1)} %get-tuple-element.37), channel_id=1, source_target_pairs={{0,6},{1,7},{2,4},{3,5},{4,2},{5,3},{6,0},{7,1},{8,14},{9,15},{10,... | collective-permute-start | bytes 196616 | tf_op jit(solution)/shard_map/ppermute | solution.py:295
  82.0 13.1 %collective-permute-start.7 = (bf16[8,4096]{1,0:T(8,128)(2,1)}, bf16[8,4096]{1,0:T(8,128)(2,1)S(1)}, u32[]{:S(2)}, u32[]{:S(2)}) collective-permute-start(bf16[8,4096]{1,0:T(8,128)(2,1)} %get-tuple-element.38), channel_id=1, source_target_pairs={{0,7},{1,6},{2,5},{3,4},{4,3},{5,2},{6,1},{7,0},{8,15},{9,14},{10,... | collective-permute-start | bytes 196616 | tf_op jit(solution)/shard_map/ppermute | solution.py:295
  85.8 10.8 %collective-permute-start.4 = (bf16[8,4096]{1,0:T(8,128)(2,1)S(1)}, bf16[8,4096]{1,0:T(8,128)(2,1)S(1)}, u32[]{:S(2)}, u32[]{:S(2)}) collective-permute-start(bf16[8,4096]{1,0:T(8,128)(2,1)S(1)} %copy-done.14), channel_id=1, source_target_pairs={{0,4},{1,5},{2,6},{3,7},{4,0},{5,1},{6,2},{7,3},{8,12},{9,13},{10,... | collective-permute-start | bytes 196616 | tf_op jit(solution)/shard_map/ppermute | solution.py:295
  90.5 1.0 copy-start.5
  91.5 14.3 %copy-start.15 = (bf16[64,128]{1,0:T(8,128)(2,1)S(1)}, bf16[64,128]{1,0:T(8,128)(2,1)}, u32[]{:S(2)}) copy-start(bf16[64,128]{1,0:T(8,128)(2,1)} %get-tuple-element.27.after_ref.refs_0_) | copy-start | bytes 49156
  91.5 14.3 %copy-start.17 = (bf16[64,128]{1,0:T(8,128)(2,1)S(1)}, bf16[64,128]{1,0:T(8,128)(2,1)}, u32[]{:S(2)}) copy-start(bf16[64,128]{1,0:T(8,128)(2,1)} %get-tuple-element.28._.refs_1_) | copy-start | bytes 49156
  92.2 6.6 %collective-permute-start.12 = (bf16[8,4096]{1,0:T(8,128)(2,1)S(1)}, bf16[8,4096]{1,0:T(8,128)(2,1)S(1)}, u32[]{:S(2)}, u32[]{:S(2)}) collective-permute-start(bf16[8,4096]{1,0:T(8,128)(2,1)S(1)} %get-tuple-element.43), channel_id=1, source_target_pairs={{0,12},{1,13},{2,14},{3,15},{4,8},{5,9},{6,10},{7,11},{8,4},{9,5},... | collective-permute-start | bytes 196616 | tf_op jit(solution)/shard_map/ppermute | solution.py:295
  93.0 9.9 %collective-permute-start.13 = (bf16[8,4096]{1,0:T(8,128)(2,1)S(1)}, bf16[8,4096]{1,0:T(8,128)(2,1)S(1)}, u32[]{:S(2)}, u32[]{:S(2)}) collective-permute-start(bf16[8,4096]{1,0:T(8,128)(2,1)S(1)} %get-tuple-element.44), channel_id=1, source_target_pairs={{0,13},{1,12},{2,15},{3,14},{4,9},{5,8},{6,11},{7,10},{8,5},{9,4},... | collective-permute-start | bytes 196616 | tf_op jit(solution)/shard_map/ppermute | solution.py:295
  94.1 10.3 %collective-permute-start.14 = (bf16[8,4096]{1,0:T(8,128)(2,1)S(1)}, bf16[8,4096]{1,0:T(8,128)(2,1)S(1)}, u32[]{:S(2)}, u32[]{:S(2)}) collective-permute-start(bf16[8,4096]{1,0:T(8,128)(2,1)S(1)} %get-tuple-element.45), channel_id=1, source_target_pairs={{0,14},{1,15},{2,12},{3,13},{4,10},{5,11},{6,8},{7,9},{8,6},{9,7},... | collective-permute-start | bytes 196616 | tf_op jit(solution)/shard_map/ppermute | solution.py:295
  95.1 10.7 %collective-permute-start.15 = (bf16[8,4096]{1,0:T(8,128)(2,1)S(1)}, bf16[8,4096]{1,0:T(8,128)(2,1)S(1)}, u32[]{:S(2)}, u32[]{:S(2)}) collective-permute-start(bf16[8,4096]{1,0:T(8,128)(2,1)S(1)} %get-tuple-element.46), channel_id=1, source_target_pairs={{0,15},{1,14},{2,13},{3,12},{4,11},{5,10},{6,9},{7,8},{8,7},{9,6},... | collective-permute-start | bytes 196616 | tf_op jit(solution)/shard_map/ppermute | solution.py:295
  105.8 1.6 %copy-start.3 = (bf16[4,128,2048]{2,1,0:T(8,128)(2,1)S(1)}, bf16[4,128,2048]{2,1,0:T(8,128)(2,1)}, u32[]{:S(2)}) copy-start(bf16[4,128,2048]{2,1,0:T(8,128)(2,1)} %copy-done.2) | copy-start | bytes 6291460
  107.4 1.6 %copy-start.8 = (bf16[4,2048,128]{2,1,0:T(8,128)(2,1)S(1)}, bf16[4,2048,128]{2,1,0:T(8,128)(2,1)}, u32[]{:S(2)}) copy-start(bf16[4,2048,128]{2,1,0:T(8,128)(2,1)} %copy-done.7) | copy-start | bytes 6291460
  109.0 1.6 %copy-start.10 = (f32[4,16,64,128]{3,2,1,0:T(8,128)S(1)}, f32[4,16,64,128]{3,2,1,0:T(8,128)}, u32[]{:S(2)}) copy-start(f32[4,16,64,128]{3,2,1,0:T(8,128)} %copy-done.9) | copy-start | bytes 6291460

commit v7 on v6

--- a/solution.py
+++ b/solution.py
@@ -14,16 +14,13 @@
 SCALE = 2.0
 ROWS_STEP = 8
 COLUMNS_STEP = 2048
-
-
-def place_of(index, quarter):
-    return lax.div(index, 2 * quarter) * quarter + lax.rem(index, quarter)
+FAR_GROUPS = 4
 
 
 def routing(pairs, owners, slot_count, held, slots_ref, ids_ref):
     ids = ids_ref[...]
     rows = ids.shape[1]
-    quarter = owners // 4
+    half = owners // 2
 
     def look(s, slot):
         return jnp.where(ids == s, slots_ref[s], slot)
@@ -40,9 +37,9 @@
     )
     place = jnp.sum(jnp.where(hits, before, 0.0), axis=0, keepdims=True).astype(jnp.int32)
     apart = owner ^ lax.axis_index("owner")
-    message = place_of(apart if pairs else owner, quarter)
-    meant = lax.rem(lax.div(apart, quarter), 2) == (1 if pairs else 0)
-    line = lax.broadcasted_iota(jnp.int32, (owners // 2 * slot_count, rows), 0)
+    message = lax.rem(apart if pairs else owner, half)
+    meant = (apart >= half) == pairs
+    line = lax.broadcasted_iota(jnp.int32, (half * slot_count, rows), 0)
     routed = line == jnp.where(meant, message * slot_count + place, -1)
     label = jnp.sum(jnp.where(routed, local.astype(jnp.float32), 0.0), axis=1, keepdims=True)
     return routed.astype(jnp.bfloat16), label
@@ -215,31 +212,36 @@
 
 
 def attend_kernel(group, count, *refs):
-    routed_refs, returned_refs, refs = refs[:2], refs[2 : 2 + count], refs[2 + count :]
-    laid_refs, (out_ref, *held_refs, sems) = refs[:3], refs[3:]
-    keys_ref, values_ref, scores_ref = held_refs
+    routed_refs, given_refs, out_ref = refs[:2], refs[2 : 5 + count], refs[5 + count]
+    *held_refs, sems, laid_sems = refs[6 + count :]
+    returned_refs, (keys_ref, values_ref, scores_ref) = held_refs[:count], held_refs[count:]
     step = ROWS_STEP
     steps, _, cells = scores_ref.shape[1:]
     span = group * HEAD
     factor = 1.0 / jnp.sqrt(jnp.float32(HEAD))
     copies = [
+        pltpu.make_async_copy(given_ref, held_ref, sems.at[i])
+        for i, (given_ref, held_ref) in enumerate(zip(given_refs[:count], returned_refs))
+    ]
+    laid_copies = [
         [
-            pltpu.make_async_copy(laid_ref.at[k], held_ref.at[k], sems.at[k, i])
-            for i, (laid_ref, held_ref) in enumerate(zip(laid_refs, held_refs))
+            pltpu.make_async_copy(given_ref.at[k], held_ref.at[k], laid_sems.at[k, i])
+            for i, (given_ref, held_ref) in enumerate(zip(given_refs[count:], held_refs[count:]))
         ]
         for k in range(KVH)
     ]
-    for copy in copies:
-        for one in copy:
-            one.start()
+    for copy in sum(laid_copies, copies):
+        copy.start()
     routed = jnp.concatenate([ref[...].astype(jnp.float32) for ref in routed_refs], axis=0)
     routed = jnp.transpose(routed).astype(jnp.bfloat16)
+    for copy in copies:
+        copy.wait()
     for k in range(KVH):
         delta = jnp.dot(
             routed, stack(returned_refs, k * span, span), preferred_element_type=jnp.float32
         )
-        for one in copies[k]:
-            one.wait()
+        for copy in laid_copies[k]:
+            copy.wait()
         for i in range(steps):
             lines = slice(i * step, (i + 1) * step)
             at = slice(i * cells, (i + 1) * cells)
@@ -262,56 +264,59 @@
 
 def attend(routed, returned, laid, width):
     rows = routed[0].shape[1]
+    given = [*returned, *laid]
     return pl.pallas_call(
         functools.partial(attend_kernel, width // (KVH * HEAD), len(returned)),
-        in_specs=[pl.BlockSpec(memory_space=pltpu.VMEM)] * (2 + len(returned))
-        + [pl.BlockSpec(memory_space=pltpu.HBM)] * len(laid),
+        in_specs=[pl.BlockSpec(memory_space=pltpu.VMEM)] * 2
+        + [pl.BlockSpec(memory_space=pl.ANY)] * len(given),
         out_specs=pl.BlockSpec(memory_space=pltpu.VMEM),
         out_shape=jax.ShapeDtypeStruct((rows, width), jnp.bfloat16),
-        scratch_shapes=[pltpu.VMEM(part.shape, part.dtype) for part in laid]
-        + [pltpu.SemaphoreType.DMA((KVH, len(laid)))],
-        compiler_params=pltpu.CompilerParams(vmem_limit_bytes=24 * 2**20),
+        scratch_shapes=[pltpu.VMEM(part.shape, part.dtype) for part in given]
+        + [pltpu.SemaphoreType.DMA((len(returned),)), pltpu.SemaphoreType.DMA((KVH, len(laid)))],
+        compiler_params=pltpu.CompilerParams(vmem_limit_bytes=56 * 2**20),
         name="attend",
-    )(*routed, *returned, *laid)
+    )(*routed, *given)
 
 
 def on_device(hidden, adapter_id, adapter_slot, cache_len, base_q, kv_cache, a_maps, b_maps):
     owners = lax.axis_size("owner")
-    quarter = owners // 4
+    half = owners // 2
     rows = hidden.shape[0]
     held = a_maps.shape[1] // RANK
     slot_count = max(2, 2 * ((rows + 2 * owners - 1) // (2 * owners)))
-    halves = [[i for i in range(owners) if i // quarter % 2 == bit] for bit in range(2)]
+    halves = [list(range(half)), list(range(half, owners))]
 
     def swap(lines):
-        blocks = lines.reshape(owners // 2, slot_count, lines.shape[1])
+        blocks = lines.reshape(half, slot_count, lines.shape[1])
         blocks = lax.all_to_all(
             blocks, "owner", split_axis=0, concat_axis=0, tiled=True, axis_index_groups=halves
         )
         return blocks.reshape(lines.shape)
 
-    def trade(messages, offsets):
+    def trade(messages, first):
         return [
-            lax.ppermute(message, "owner", [(i, i ^ apart) for i in range(owners)])
-            for message, apart in zip(messages, offsets)
+            lax.ppermute(message, "owner", [(i, i ^ (first + j)) for i in range(owners)])
+            for j, message in enumerate(messages)
         ]
 
-    near, far = halves[1][:quarter], halves[1][quarter:]
     whole = functools.partial(pack, hidden, adapter_id, adapter_slot)
-    routed, lines = whole(adapter_id, False, owners, slot_count, held)
+    routed_far, *messages = whole(adapter_id, True, owners, slot_count, held)
+    size = max(1, half // FAR_GROUPS)
+    starts = range(0, half, size)
+    arrived_far = [trade(messages[at : at + size], half + at) for at in starts]
+    routed, lines = whole(routed_far, False, owners, slot_count, held)
     arrived = swap(lines)
-    routed_pairs, *messages = whole(routed, True, owners, slot_count, held)
-    arrived_near = trade(messages[:quarter], near)
-    arrived_far = trade(messages[quarter:], far)
-    laid = prep(base_q, kv_cache, cache_len, routed_pairs)
-    change_near = adapt(arrived_near, a_maps, b_maps, laid[0])
-    (change,) = adapt([arrived], a_maps, b_maps, change_near[0])
-    returned = swap(change)
-    change_far = adapt(arrived_far, a_maps, b_maps, change)
-    returned_far = trade(change_far, far)
-    returned_near = trade(change_near, near)
-    returned = [returned, *returned_near, *returned_far]
-    return attend([routed, routed_pairs], returned, laid, base_q.shape[1])
+    laid = prep(base_q, kv_cache, cache_len, routed)
+    returned, after = [], laid[0]
+    for i, at in enumerate(starts):
+        change_far = adapt(arrived_far[i], a_maps, b_maps, after)
+        after = change_far[0]
+        returned += trade(change_far, half + at)
+        if i == 0:
+            (after,) = adapt([arrived], a_maps, b_maps, after)
+            returned.append(swap(after))
+    returned = returned[:size] + returned[size + 1 :] + returned[size : size + 1]
+    return attend([routed_far, routed], returned, laid, base_q.shape[1])
 
 
 def solution(mesh):

time: 118 us -> 116 us (0.983)
  the two profiles are of different devices: /device:TPU:9 before, /device:TPU:0 now
where the time goes in v7:
time: 116 us; the launch traced here: 115 us
  starting transfers between devices  40.3 us (35%)
  waiting for transfers between devices  39 us (34%)
  Pallas kernels  25.6 us (22%)
  local copies, waits for them, and re-layouts  10.2 us (9%)
    ppermute x16, waiting for transfers between devices, trade(): lax.ppermute(message, 'owner', [(i, i ^ first + j) for i in range(owners)])  39 us
    ppermute x16, starting transfers between devices, trade(): lax.ppermute(message, 'owner', [(i, i ^ first + j) for i in range(owners)])  28.4 us
    all_to_all x2, starting transfers between devices, swap(): lax.all_to_all(blocks, 'owner', split_axis=0, concat_axis=0, tiled=True,...  11.8 us
    unnamed x40, local copies, waits for them, and re-layouts  9.89 us
    pallas_call x1, Pallas kernels, attend(): pl.pallas_call(functools.partial(attend_kernel, width // (KVH * HEAD), le...  8.81 us
    pallas_call x2, Pallas kernels, pack(): pl.pallas_call(functools.partial(pack_kernel, pairs, owners, slot_count,...  7.3 us
    pallas_call x1, Pallas kernels, prep(): pl.pallas_call(functools.partial(prep_kernel, group, context), grid=(step...  4.99 us
    pallas_call x5, Pallas kernels, adapt(): pl.pallas_call(functools.partial(adapt_kernel, count), in_specs=[pl.Block...  4.52 us
  transfers between devices with their start and end apart: 18, of which 7 were waited for; matrix products, arithmetic and copies ran while one was open for 0% of the time, Pallas kernels for 6%

profile of v7, /device:TPU:0, one launch (start us, length us, event | category | flops | bytes accessed | tf_op | source)
XLA Modules:
  0.0 115.3 jit_solution(18014701315175978221)
XLA Ops:
  0.0 3.6 %pack_pairs.1 = (bf16[64,128]{1,0:T(8,128)(2,1)}, bf16[8,8320]{1,0:T(8,128)(2,1)}, bf16[8,8320]{1,0:T(8,128)(2,1)}, bf16[8,8320]{1,0:T(8,128)(2,1)}, bf16[8,8320...) custom-call(s32[32]{0:T(128)} %slots_ref.3, ...), custom_call_target="tpu_custom_call" | custom-call | tf_op jit(solution)/shard_map/pack_pairs/pallas_call | solution.py:84
  3.6 0.0 copy-start.18
  3.6 3.7 %pack.1 = (bf16[64,128]{1,0:T(8,128)(2,1)}, bf16[64,8320]{1,0:T(8,128)(2,1)}) custom-call(s32[32]{0:T(128)} %slots_ref.3, s32[1,128]{1,0:T(1,128)} %bitcast.8, bf16[128,8192]{1,0:T(8,128)(2,1)} %hidden_ref.3, bf16[64,128]{1,0:T(8,128)(2,1)} %get-tuple-element.27.after_ref.refs_0_), custom_call_target="tpu_custom_call" | custom-call | tf_op jit(solution)/shard_map/pack/pallas_call | solution.py:84
  7.3 5.2 %all-to-all-start = ((bf16[8,8,8320]{2,1,0:T(8,128)(2,1)}), bf16[8,8,8320]{2,1,0:T(8,128)(2,1)}, u32[]{:S(2)}, u32[]{:S(2)}) async-start(bf16[8,8,8320]{2,1,0:T(8,128)(2,1)} %bitcast.6), calls=%async_computation | async-start | bytes 2129920 | tf_op jit(solution)/shard_map/all_to_all | solution.py:291
  12.6 3.1 %collective-permute-start = (bf16[8,8320]{1,0:T(8,128)(2,1)}, bf16[8,8320]{1,0:T(8,128)(2,1)S(1)}, u32[]{:S(2)}, u32[]{:S(2)}) collective-permute-start(bf16[8,8320]{1,0:T(8,128)(2,1)} %get-tuple-element.29), channel_id=1, source_target_pairs={{0,8},{1,9},{2,10},{3,11},{4,12},{5,13},{6,14},{7,15},{8,0},{9,1},... | collective-permute-start | bytes 399368 | tf_op jit(solution)/shard_map/ppermute | solution.py:298
  15.7 0.1 broadcast_in_dim.7
  15.8 0.1 broadcast_in_dim.8
  15.9 0.1 broadcast_in_dim.9.len_ref
  16.0 0.0 copy-start.5
  16.0 2.2 %copy-done.5 = bf16[128,2,16,512]{3,2,1,0:T(8,128)(2,1)S(1)} copy-done((bf16[128,2,16,512]{3,2,1,0:T(8,128)(2,1)S(1)}, bf16[128,2,16,512]{3,2,1,0:T(8,128)(2,1)}, u32[]{:S(2)}) %copy-start.5) | copy-done | bytes 4194328
  18.2 1.2 %copy-done.8 = bf16[128,4096]{1,0:T(8,128)(2,1)S(1)} copy-done((bf16[128,4096]{1,0:T(8,128)(2,1)S(1)}, bf16[128,4096]{1,0:T(8,128)(2,1)}, u32[]{:S(2)}) %copy-start.8) | copy-done | bytes 1048600
  19.4 5.0 %prep.1 = (bf16[4,128,2048]{2,1,0:T(8,128)(2,1)S(1)}, bf16[4,2048,128]{2,1,0:T(8,128)(2,1)S(1)}, f32[4,16,64,128]{3,2,1,0:T(8,128)S(1)}) custom-call(bf16[128,4096]{1,0:T(8,128)(2,1)S(1)} %copy-done.8, bf16[128,2,16,512]{3,2,1,0:T(8,128)(2,1)S(1)} %copy-done.5, s32[16,1,128]{2,1,0:T(1,128)S(1)} %broadcast_in_dim.9.len_ref, bf16[64,128]{1,0:T(8,128)(2,1)S(1)} %copy-done.9), custom_call_target="tpu_custom_call" | custom-call | flops 134217728 | bytes 16777216 | tf_op jit(solution)/shard_map/prep/pallas_call | solution.py:187
  24.4 1.3 %copy-done.6 = bf16[4,2048,128]{2,1,0:T(8,128)(2,1)} copy-done((bf16[4,2048,128]{2,1,0:T(8,128)(2,1)}, bf16[4,2048,128]{2,1,0:T(8,128)(2,1)S(1)}, u32[]{:S(2)}) %copy-start.6) | copy-done | bytes 2097176
  25.7 1.3 %copy-done.7 = f32[4,16,64,128]{3,2,1,0:T(8,128)} copy-done((f32[4,16,64,128]{3,2,1,0:T(8,128)}, f32[4,16,64,128]{3,2,1,0:T(8,128)S(1)}, u32[]{:S(2)}) %copy-start.7) | copy-done | bytes 2097176
  27.1 1.2 %collective-permute-done.refs_0_ = bf16[8,8320]{1,0:T(8,128)(2,1)S(1)} collective-permute-done((bf16[8,8320]{1,0:T(8,128)(2,1)}, bf16[8,8320]{1,0:T(8,128)(2,1)S(1)}, u32[]{:S(2)}, u32[]{:S(2)}) %collective-permute-start) | collective-permute-done | bytes 133152 | tf_op jit(solution)/shard_map/ppermute | solution.py:298
  28.3 2.7 %collective-permute-done.1.refs_1_ = bf16[8,8320]{1,0:T(8,128)(2,1)S(1)} collective-permute-done((bf16[8,8320]{1,0:T(8,128)(2,1)}, bf16[8,8320]{1,0:T(8,128)(2,1)S(1)}, u32[]{:S(2)}, u32[]{:S(2)}) %collective-permute-start.1) | collective-permute-done | bytes 133152 | tf_op jit(solution)/shard_map/ppermute | solution.py:298
  31.0 0.6 adapt.5
  31.6 1.4 %copy-done.2 = bf16[4,128,2048]{2,1,0:T(8,128)(2,1)} copy-done((bf16[4,128,2048]{2,1,0:T(8,128)(2,1)}, bf16[4,128,2048]{2,1,0:T(8,128)(2,1)S(1)}, u32[]{:S(2)}) %copy-start.2) | copy-done | bytes 2097176
  33.0 0.1 all-to-all-done
  33.0 2.0 %adapt.6.refs_4_ = bf16[64,4096]{1,0:T(8,128)(2,1)S(1)} custom-call(bf16[64,8320]{1,0:T(8,128)(2,1)} %bitcast.2.refs_0_, bf16[8192,128]{1,0:T(8,128)(2,1)S(1)} %copy-done, bf16[128,4096]{1,0:T(8,128)(2,1)S(1)} %copy-done.1, bf16[8,4096]{1,0:T(8,128)(2,1)S(1)} %get-tuple-element.32.refs_3_), custom_call_target="tpu_custom_call" | custom-call | flops 201326592 | bytes 3145728 | tf_op jit(solution)/shard_map/adapt/pallas_call | solution.py:139
  35.1 0.0 copy-start.3
  35.1 0.8 copy-done.3
  35.8 6.6 %all-to-all-start.1 = ((bf16[8,8,4096]{2,1,0:T(8,128)(2,1)}), bf16[8,8,4096]{2,1,0:T(8,128)(2,1)}, u32[]{:S(2)}, u32[]{:S(2)}) async-start(bf16[8,8,4096]{2,1,0:T(8,128)(2,1)} %bitcast.5), calls=%async_computation.1 | async-start | bytes 1048576 | tf_op jit(solution)/shard_map/all_to_all | solution.py:291
  42.4 1.9 %collective-permute-start.4 = (bf16[8,8320]{1,0:T(8,128)(2,1)}, bf16[8,8320]{1,0:T(8,128)(2,1)S(1)}, u32[]{:S(2)}, u32[]{:S(2)}) collective-permute-start(bf16[8,8320]{1,0:T(8,128)(2,1)} %get-tuple-element.34), channel_id=1, source_target_pairs={{0,10},{1,11},{2,8},{3,9},{4,14},{5,15},{6,12},{7,13},{8,2},{9,3},... | collective-permute-start | bytes 399368 | tf_op jit(solution)/shard_map/ppermute | solution.py:298
  44.4 1.7 %collective-permute-start.5 = (bf16[8,8320]{1,0:T(8,128)(2,1)}, bf16[8,8320]{1,0:T(8,128)(2,1)S(1)}, u32[]{:S(2)}, u32[]{:S(2)}) collective-permute-start(bf16[8,8320]{1,0:T(8,128)(2,1)} %get-tuple-element.35), channel_id=1, source_target_pairs={{0,11},{1,10},{2,9},{3,8},{4,15},{5,14},{6,13},{7,12},{8,3},{9,2},... | collective-permute-start | bytes 399368 | tf_op jit(solution)/shard_map/ppermute | solution.py:298
  46.1 1.6 %collective-permute-start.8 = (bf16[8,8320]{1,0:T(8,128)(2,1)}, bf16[8,8320]{1,0:T(8,128)(2,1)S(1)}, u32[]{:S(2)}, u32[]{:S(2)}) collective-permute-start(bf16[8,8320]{1,0:T(8,128)(2,1)} %get-tuple-element.39), channel_id=1, source_target_pairs={{0,12},{1,13},{2,14},{3,15},{4,8},{5,9},{6,10},{7,11},{8,4},{9,5},... | collective-permute-start | bytes 399368 | tf_op jit(solution)/shard_map/ppermute | solution.py:298
  47.7 1.8 %collective-permute-start.9 = (bf16[8,8320]{1,0:T(8,128)(2,1)}, bf16[8,8320]{1,0:T(8,128)(2,1)S(1)}, u32[]{:S(2)}, u32[]{:S(2)}) collective-permute-start(bf16[8,8320]{1,0:T(8,128)(2,1)} %get-tuple-element.40), channel_id=1, source_target_pairs={{0,13},{1,12},{2,15},{3,14},{4,9},{5,8},{6,11},{7,10},{8,5},{9,4},... | collective-permute-start | bytes 399368 | tf_op jit(solution)/shard_map/ppermute | solution.py:298
  49.5 2.9 %collective-permute-start.12 = (bf16[8,8320]{1,0:T(8,128)(2,1)}, bf16[8,8320]{1,0:T(8,128)(2,1)S(1)}, u32[]{:S(2)}, u32[]{:S(2)}) collective-permute-start(bf16[8,8320]{1,0:T(8,128)(2,1)} %get-tuple-element.43), channel_id=1, source_target_pairs={{0,14},{1,15},{2,12},{3,13},{4,10},{5,11},{6,8},{7,9},{8,6},{9,7},... | collective-permute-start | bytes 399368 | tf_op jit(solution)/shard_map/ppermute | solution.py:298
  52.4 0.0 collective-permute-done.4.refs_0_
  52.4 1.7 %collective-permute-start.13 = (bf16[8,8320]{1,0:T(8,128)(2,1)S(1)}, bf16[8,8320]{1,0:T(8,128)(2,1)S(1)}, u32[]{:S(2)}, u32[]{:S(2)}) collective-permute-start(bf16[8,8320]{1,0:T(8,128)(2,1)S(1)} %copy-done.19), channel_id=1, source_target_pairs={{0,15},{1,14},{2,13},{3,12},{4,11},{5,10},{6,9},{7,8},{8,7},{9,6},... | collective-permute-start | bytes 399368 | tf_op jit(solution)/shard_map/ppermute | solution.py:298
  54.1 15.9 %collective-permute-done.5.refs_1_ = bf16[8,8320]{1,0:T(8,128)(2,1)S(1)} collective-permute-done((bf16[8,8320]{1,0:T(8,128)(2,1)}, bf16[8,8320]{1,0:T(8,128)(2,1)S(1)}, u32[]{:S(2)}, u32[]{:S(2)}) %collective-permute-start.5) | collective-permute-done | bytes 133152 | tf_op jit(solution)/shard_map/ppermute | solution.py:298
  70.0 1.0 copy-done.4
  71.1 0.6 adapt.7
  71.7 2.9 %collective-permute-start.3 = (bf16[8,4096]{1,0:T(8,128)(2,1)S(1)}, bf16[8,4096]{1,0:T(8,128)(2,1)S(1)}, u32[]{:S(2)}, u32[]{:S(2)}) collective-permute-start(bf16[8,4096]{1,0:T(8,128)(2,1)S(1)} %get-tuple-element.33), channel_id=1, source_target_pairs={{0,9},{1,8},{2,11},{3,10},{4,13},{5,12},{6,15},{7,14},{8,1},{9,0},... | collective-permute-start | bytes 196616 | tf_op jit(solution)/shard_map/ppermute | solution.py:298
  74.6 0.6 adapt.8
  75.2 0.0 collective-permute-done.13.refs_1_
  75.2 0.6 adapt.9
  75.9 2.3 %collective-permute-start.14 = (bf16[8,4096]{1,0:T(8,128)(2,1)S(1)}, bf16[8,4096]{1,0:T(8,128)(2,1)S(1)}, u32[]{:S(2)}, u32[]{:S(2)}) collective-permute-start(bf16[8,4096]{1,0:T(8,128)(2,1)S(1)} %get-tuple-element.45), channel_id=1, source_target_pairs={{0,14},{1,15},{2,12},{3,13},{4,10},{5,11},{6,8},{7,9},{8,6},{9,7},... | collective-permute-start | bytes 196616 | tf_op jit(solution)/shard_map/ppermute | solution.py:298
  78.2 2.2 %collective-permute-start.10 = (bf16[8,4096]{1,0:T(8,128)(2,1)S(1)}, bf16[8,4096]{1,0:T(8,128)(2,1)S(1)}, u32[]{:S(2)}, u32[]{:S(2)}) collective-permute-start(bf16[8,4096]{1,0:T(8,128)(2,1)S(1)} %get-tuple-element.41.refs_4_), channel_id=1, source_target_pairs={{0,12},{1,13},{2,14},{3,15},{4,8},{5,9},{6,10},{7,11},{8,4},{9,5},... | collective-permute-start | bytes 196616 | tf_op jit(solution)/shard_map/ppermute | solution.py:298
  80.4 0.6 collective-permute-start.15
  81.0 10.0 %collective-permute-done.3.refs_3_ = bf16[8,4096]{1,0:T(8,128)(2,1)S(1)} collective-permute-done((bf16[8,4096]{1,0:T(8,128)(2,1)S(1)}, bf16[8,4096]{1,0:T(8,128)(2,1)S(1)}, u32[]{:S(2)}, u32[]{:S(2)}) %collective-permute-start.3) | collective-permute-done | bytes 65568 | tf_op jit(solution)/shard_map/ppermute | solution.py:298
  91.1 1.8 %collective-permute-start.11 = (bf16[8,4096]{1,0:T(8,128)(2,1)S(1)}, bf16[8,4096]{1,0:T(8,128)(2,1)S(1)}, u32[]{:S(2)}, u32[]{:S(2)}) collective-permute-start(bf16[8,4096]{1,0:T(8,128)(2,1)S(1)} %get-tuple-element.42), channel_id=1, source_target_pairs={{0,13},{1,12},{2,15},{3,14},{4,9},{5,8},{6,11},{7,10},{8,5},{9,4},... | collective-permute-start | bytes 196616 | tf_op jit(solution)/shard_map/ppermute | solution.py:298
  92.8 2.4 %collective-permute-start.7 = (bf16[8,4096]{1,0:T(8,128)(2,1)S(1)}, bf16[8,4096]{1,0:T(8,128)(2,1)S(1)}, u32[]{:S(2)}, u32[]{:S(2)}) collective-permute-start(bf16[8,4096]{1,0:T(8,128)(2,1)S(1)} %get-tuple-element.38), channel_id=1, source_target_pairs={{0,11},{1,10},{2,9},{3,8},{4,15},{5,14},{6,13},{7,12},{8,3},{9,2},... | collective-permute-start | bytes 196616 | tf_op jit(solution)/shard_map/ppermute | solution.py:298
  95.2 1.4 %collective-permute-start.6 = (bf16[8,4096]{1,0:T(8,128)(2,1)S(1)}, bf16[8,4096]{1,0:T(8,128)(2,1)S(1)}, u32[]{:S(2)}, u32[]{:S(2)}) collective-permute-start(bf16[8,4096]{1,0:T(8,128)(2,1)S(1)} %get-tuple-element.37.refs_4_), channel_id=1, source_target_pairs={{0,10},{1,11},{2,8},{3,9},{4,14},{5,15},{6,12},{7,13},{8,2},{9,3},... | collective-permute-start | bytes 196616 | tf_op jit(solution)/shard_map/ppermute | solution.py:298
  96.7 7.4 %collective-permute-done.7.refs_5_ = bf16[8,4096]{1,0:T(8,128)(2,1)S(1)} collective-permute-done((bf16[8,4096]{1,0:T(8,128)(2,1)S(1)}, bf16[8,4096]{1,0:T(8,128)(2,1)S(1)}, u32[]{:S(2)}, u32[]{:S(2)}) %collective-permute-start.7) | collective-permute-done | bytes 65568 | tf_op jit(solution)/shard_map/ppermute | solution.py:298
  104.1 1.8 %collective-permute-done.6.refs_4_ = bf16[8,4096]{1,0:T(8,128)(2,1)S(1)} collective-permute-done((bf16[8,4096]{1,0:T(8,128)(2,1)S(1)}, bf16[8,4096]{1,0:T(8,128)(2,1)S(1)}, u32[]{:S(2)}, u32[]{:S(2)}) %collective-permute-start.6) | collective-permute-done | bytes 65568 | tf_op jit(solution)/shard_map/ppermute | solution.py:298
  105.9 0.6 copy-done.17
  106.5 8.8 %attend.1 = bf16[128,4096]{1,0:T(8,128)(2,1)} custom-call(bf16[64,128]{1,0:T(8,128)(2,1)} %get-tuple-element.27.after_ref.refs_0_, bf16[64,128]{1,0:T(8,128)(2,1)} %get-tuple-element.28._.refs_1_, bf16[8,4096]{1,0:T(8,128)(2,1)} %copy-done.10, bf16[8,4096]{1,0:T(8,128)(2,1)} %copy-done.11, bf16[8,4096]{1,0:T(8,128)(2,1)} %copy-done.17, ...), custom_call_target="tpu_custom_call" | custom-call | tf_op jit(solution)/shard_map/attend/pallas_call | solution.py:268
  (40 shorter events, 0.1 us)
Async XLA Ops:
  3.6 12.1 %copy-start.18 = (s32[128]{0:T(128)S(1)}, s32[128]{0:T(128)}, u32[]{:S(2)}) copy-start(s32[128]{0:T(128)} %param.11) | copy-start | bytes 1540
  7.3 8.6 %copy-start.9 = (bf16[64,128]{1,0:T(8,128)(2,1)S(1)}, bf16[64,128]{1,0:T(8,128)(2,1)}, u32[]{:S(2)}) copy-start(bf16[64,128]{1,0:T(8,128)(2,1)} %get-tuple-element.28._.refs_1_) | copy-start | bytes 49156
  7.3 25.7 %all-to-all-start = ((bf16[8,8,8320]{2,1,0:T(8,128)(2,1)}), bf16[8,8,8320]{2,1,0:T(8,128)(2,1)}, u32[]{:S(2)}, u32[]{:S(2)}) async-start(bf16[8,8,8320]{2,1,0:T(8,128)(2,1)} %bitcast.6), calls=%async_computation | async-start | bytes 2129920 | tf_op jit(solution)/shard_map/all_to_all | solution.py:291
  12.6 15.7 %collective-permute-start = (bf16[8,8320]{1,0:T(8,128)(2,1)}, bf16[8,8320]{1,0:T(8,128)(2,1)S(1)}, u32[]{:S(2)}, u32[]{:S(2)}) collective-permute-start(bf16[8,8320]{1,0:T(8,128)(2,1)} %get-tuple-element.29), channel_id=1, source_target_pairs={{0,8},{1,9},{2,10},{3,11},{4,12},{5,13},{6,14},{7,15},{8,0},{9,1},... | collective-permute-start | bytes 399368 | tf_op jit(solution)/shard_map/ppermute | solution.py:298
  15.7 15.3 %collective-permute-start.1 = (bf16[8,8320]{1,0:T(8,128)(2,1)}, bf16[8,8320]{1,0:T(8,128)(2,1)S(1)}, u32[]{:S(2)}, u32[]{:S(2)}) collective-permute-start(bf16[8,8320]{1,0:T(8,128)(2,1)} %get-tuple-element.30), channel_id=1, source_target_pairs={{0,9},{1,8},{2,11},{3,10},{4,13},{5,12},{6,15},{7,14},{8,1},{9,0},... | collective-permute-start | bytes 399368 | tf_op jit(solution)/shard_map/ppermute | solution.py:298
  16.0 2.2 %copy-start.5 = (bf16[128,2,16,512]{3,2,1,0:T(8,128)(2,1)S(1)}, bf16[128,2,16,512]{3,2,1,0:T(8,128)(2,1)}, u32[]{:S(2)}) copy-start(bf16[128,2,16,512]{3,2,1,0:T(8,128)(2,1)} %kv_ref.1) | copy-start | bytes 12582916
  18.2 1.2 %copy-start.8 = (bf16[128,4096]{1,0:T(8,128)(2,1)S(1)}, bf16[128,4096]{1,0:T(8,128)(2,1)}, u32[]{:S(2)}) copy-start(bf16[128,4096]{1,0:T(8,128)(2,1)} %base_ref.1) | copy-start | bytes 3145732
  19.4 11.6 %copy-start = (bf16[8192,128]{1,0:T(8,128)(2,1)S(1)}, bf16[8192,128]{1,0:T(8,128)(2,1)}, u32[]{:S(2)}) copy-start(bf16[8192,128]{1,0:T(8,128)(2,1)} %refs_2_.9) | copy-start | bytes 6291460
  19.4 11.6 %copy-start.1 = (bf16[128,4096]{1,0:T(8,128)(2,1)S(1)}, bf16[128,4096]{1,0:T(8,128)(2,1)}, u32[]{:S(2)}) copy-start(bf16[128,4096]{1,0:T(8,128)(2,1)} %refs_3_.7) | copy-start | bytes 3145732
  24.4 1.3 %copy-start.6 = (bf16[4,2048,128]{2,1,0:T(8,128)(2,1)}, bf16[4,2048,128]{2,1,0:T(8,128)(2,1)S(1)}, u32[]{:S(2)}) copy-start(bf16[4,2048,128]{2,1,0:T(8,128)(2,1)S(1)} %get-tuple-element.47.refs_12_) | copy-start | bytes 6291460
  25.7 1.3 %copy-start.7 = (f32[4,16,64,128]{3,2,1,0:T(8,128)}, f32[4,16,64,128]{3,2,1,0:T(8,128)S(1)}, u32[]{:S(2)}) copy-start(f32[4,16,64,128]{3,2,1,0:T(8,128)S(1)} %get-tuple-element.48.refs_13_) | copy-start | bytes 6291460
  31.6 1.4 %copy-start.2 = (bf16[4,128,2048]{2,1,0:T(8,128)(2,1)}, bf16[4,128,2048]{2,1,0:T(8,128)(2,1)S(1)}, u32[]{:S(2)}) copy-start(bf16[4,128,2048]{2,1,0:T(8,128)(2,1)S(1)} %get-tuple-element.31.refs_4_.refs_11_) | copy-start | bytes 6291460
  33.0 19.4 %copy-start.19 = (bf16[8,8320]{1,0:T(8,128)(2,1)S(1)}, bf16[8,8320]{1,0:T(8,128)(2,1)}, u32[]{:S(2)}) copy-start(bf16[8,8320]{1,0:T(8,128)(2,1)} %get-tuple-element.44) | copy-start | bytes 399364
  35.1 0.8 copy-start.3
  35.8 70.0 %all-to-all-start.1 = ((bf16[8,8,4096]{2,1,0:T(8,128)(2,1)}), bf16[8,8,4096]{2,1,0:T(8,128)(2,1)}, u32[]{:S(2)}, u32[]{:S(2)}) async-start(bf16[8,8,4096]{2,1,0:T(8,128)(2,1)} %bitcast.5), calls=%async_computation.1 | async-start | bytes 1048576 | tf_op jit(solution)/shard_map/all_to_all | solution.py:291
  42.4 10.0 %collective-permute-start.4 = (bf16[8,8320]{1,0:T(8,128)(2,1)}, bf16[8,8320]{1,0:T(8,128)(2,1)S(1)}, u32[]{:S(2)}, u32[]{:S(2)}) collective-permute-start(bf16[8,8320]{1,0:T(8,128)(2,1)} %get-tuple-element.34), channel_id=1, source_target_pairs={{0,10},{1,11},{2,8},{3,9},{4,14},{5,15},{6,12},{7,13},{8,2},{9,3},... | collective-permute-start | bytes 399368 | tf_op jit(solution)/shard_map/ppermute | solution.py:298
  44.4 25.6 %collective-permute-start.5 = (bf16[8,8320]{1,0:T(8,128)(2,1)}, bf16[8,8320]{1,0:T(8,128)(2,1)S(1)}, u32[]{:S(2)}, u32[]{:S(2)}) collective-permute-start(bf16[8,8320]{1,0:T(8,128)(2,1)} %get-tuple-element.35), channel_id=1, source_target_pairs={{0,11},{1,10},{2,9},{3,8},{4,15},{5,14},{6,13},{7,12},{8,3},{9,2},... | collective-permute-start | bytes 399368 | tf_op jit(solution)/shard_map/ppermute | solution.py:298
  46.1 25.6 %collective-permute-start.8 = (bf16[8,8320]{1,0:T(8,128)(2,1)}, bf16[8,8320]{1,0:T(8,128)(2,1)S(1)}, u32[]{:S(2)}, u32[]{:S(2)}) collective-permute-start(bf16[8,8320]{1,0:T(8,128)(2,1)} %get-tuple-element.39), channel_id=1, source_target_pairs={{0,12},{1,13},{2,14},{3,15},{4,8},{5,9},{6,10},{7,11},{8,4},{9,5},... | collective-permute-start | bytes 399368 | tf_op jit(solution)/shard_map/ppermute | solution.py:298
  47.7 26.9 %collective-permute-start.9 = (bf16[8,8320]{1,0:T(8,128)(2,1)}, bf16[8,8320]{1,0:T(8,128)(2,1)S(1)}, u32[]{:S(2)}, u32[]{:S(2)}) collective-permute-start(bf16[8,8320]{1,0:T(8,128)(2,1)} %get-tuple-element.40), channel_id=1, source_target_pairs={{0,13},{1,12},{2,15},{3,14},{4,9},{5,8},{6,11},{7,10},{8,5},{9,4},... | collective-permute-start | bytes 399368 | tf_op jit(solution)/shard_map/ppermute | solution.py:298
  49.5 25.7 %collective-permute-start.12 = (bf16[8,8320]{1,0:T(8,128)(2,1)}, bf16[8,8320]{1,0:T(8,128)(2,1)S(1)}, u32[]{:S(2)}, u32[]{:S(2)}) collective-permute-start(bf16[8,8320]{1,0:T(8,128)(2,1)} %get-tuple-element.43), channel_id=1, source_target_pairs={{0,14},{1,15},{2,12},{3,13},{4,10},{5,11},{6,8},{7,9},{8,6},{9,7},... | collective-permute-start | bytes 399368 | tf_op jit(solution)/shard_map/ppermute | solution.py:298
  52.4 22.8 %collective-permute-start.13 = (bf16[8,8320]{1,0:T(8,128)(2,1)S(1)}, bf16[8,8320]{1,0:T(8,128)(2,1)S(1)}, u32[]{:S(2)}, u32[]{:S(2)}) collective-permute-start(bf16[8,8320]{1,0:T(8,128)(2,1)S(1)} %copy-done.19), channel_id=1, source_target_pairs={{0,15},{1,14},{2,13},{3,12},{4,11},{5,10},{6,9},{7,8},{8,7},{9,6},... | collective-permute-start | bytes 399368 | tf_op jit(solution)/shard_map/ppermute | solution.py:298
  70.0 22.8 %collective-permute-start.2 = (bf16[8,4096]{1,0:T(8,128)(2,1)S(1)}, bf16[8,4096]{1,0:T(8,128)(2,1)S(1)}, u32[]{:S(2)}, u32[]{:S(2)}) collective-permute-start(bf16[8,4096]{1,0:T(8,128)(2,1)S(1)} %get-tuple-element.32.refs_3_), channel_id=1, source_target_pairs={{0,8},{1,9},{2,10},{3,11},{4,12},{5,13},{6,14},{7,15},{8,0},{9,1},... | collective-permute-start | bytes 196616 | tf_op jit(solution)/shard_map/ppermute | solution.py:298
  70.0 1.0 copy-start.4
  71.7 19.4 %collective-permute-start.3 = (bf16[8,4096]{1,0:T(8,128)(2,1)S(1)}, bf16[8,4096]{1,0:T(8,128)(2,1)S(1)}, u32[]{:S(2)}, u32[]{:S(2)}) collective-permute-start(bf16[8,4096]{1,0:T(8,128)(2,1)S(1)} %get-tuple-element.33), channel_id=1, source_target_pairs={{0,9},{1,8},{2,11},{3,10},{4,13},{5,12},{6,15},{7,14},{8,1},{9,0},... | collective-permute-start | bytes 196616 | tf_op jit(solution)/shard_map/ppermute | solution.py:298
  75.9 19.4 %collective-permute-start.14 = (bf16[8,4096]{1,0:T(8,128)(2,1)S(1)}, bf16[8,4096]{1,0:T(8,128)(2,1)S(1)}, u32[]{:S(2)}, u32[]{:S(2)}) collective-permute-start(bf16[8,4096]{1,0:T(8,128)(2,1)S(1)} %get-tuple-element.45), channel_id=1, source_target_pairs={{0,14},{1,15},{2,12},{3,13},{4,10},{5,11},{6,8},{7,9},{8,6},{9,7},... | collective-permute-start | bytes 196616 | tf_op jit(solution)/shard_map/ppermute | solution.py:298
  78.2 18.5 %collective-permute-start.10 = (bf16[8,4096]{1,0:T(8,128)(2,1)S(1)}, bf16[8,4096]{1,0:T(8,128)(2,1)S(1)}, u32[]{:S(2)}, u32[]{:S(2)}) collective-permute-start(bf16[8,4096]{1,0:T(8,128)(2,1)S(1)} %get-tuple-element.41.refs_4_), channel_id=1, source_target_pairs={{0,12},{1,13},{2,14},{3,15},{4,8},{5,9},{6,10},{7,11},{8,4},{9,5},... | collective-permute-start | bytes 196616 | tf_op jit(solution)/shard_map/ppermute | solution.py:298
  80.4 16.2 %collective-permute-start.15 = (bf16[8,4096]{1,0:T(8,128)(2,1)S(1)}, bf16[8,4096]{1,0:T(8,128)(2,1)S(1)}, u32[]{:S(2)}, u32[]{:S(2)}) collective-permute-start(bf16[8,4096]{1,0:T(8,128)(2,1)S(1)} %get-tuple-element.46), channel_id=1, source_target_pairs={{0,15},{1,14},{2,13},{3,12},{4,11},{5,10},{6,9},{7,8},{8,7},{9,6},... | collective-permute-start | bytes 196616 | tf_op jit(solution)/shard_map/ppermute | solution.py:298
  91.1 14.8 %copy-start.11 = (bf16[8,4096]{1,0:T(8,128)(2,1)}, bf16[8,4096]{1,0:T(8,128)(2,1)S(1)}, u32[]{:S(2)}) copy-start(bf16[8,4096]{1,0:T(8,128)(2,1)S(1)} %collective-permute-done.3.refs_3_) | copy-start | bytes 196612
  91.1 5.6 %collective-permute-start.11 = (bf16[8,4096]{1,0:T(8,128)(2,1)S(1)}, bf16[8,4096]{1,0:T(8,128)(2,1)S(1)}, u32[]{:S(2)}, u32[]{:S(2)}) collective-permute-start(bf16[8,4096]{1,0:T(8,128)(2,1)S(1)} %get-tuple-element.42), channel_id=1, source_target_pairs={{0,13},{1,12},{2,15},{3,14},{4,9},{5,8},{6,11},{7,10},{8,5},{9,4},... | collective-permute-start | bytes 196616 | tf_op jit(solution)/shard_map/ppermute | solution.py:298
  92.8 13.0 %copy-start.10 = (bf16[8,4096]{1,0:T(8,128)(2,1)}, bf16[8,4096]{1,0:T(8,128)(2,1)S(1)}, u32[]{:S(2)}) copy-start(bf16[8,4096]{1,0:T(8,128)(2,1)S(1)} %collective-permute-done.2.refs_2_) | copy-start | bytes 196612
  92.8 11.3 %collective-permute-start.7 = (bf16[8,4096]{1,0:T(8,128)(2,1)S(1)}, bf16[8,4096]{1,0:T(8,128)(2,1)S(1)}, u32[]{:S(2)}, u32[]{:S(2)}) collective-permute-start(bf16[8,4096]{1,0:T(8,128)(2,1)S(1)} %get-tuple-element.38), channel_id=1, source_target_pairs={{0,11},{1,10},{2,9},{3,8},{4,15},{5,14},{6,13},{7,12},{8,3},{9,2},... | collective-permute-start | bytes 196616 | tf_op jit(solution)/shard_map/ppermute | solution.py:298
  95.2 10.6 %copy-start.12 = (bf16[8,4096]{1,0:T(8,128)(2,1)}, bf16[8,4096]{1,0:T(8,128)(2,1)S(1)}, u32[]{:S(2)}) copy-start(bf16[8,4096]{1,0:T(8,128)(2,1)S(1)} %collective-permute-done.14.refs_8_) | copy-start | bytes 196612
  95.2 10.6 %collective-permute-start.6 = (bf16[8,4096]{1,0:T(8,128)(2,1)S(1)}, bf16[8,4096]{1,0:T(8,128)(2,1)S(1)}, u32[]{:S(2)}, u32[]{:S(2)}) collective-permute-start(bf16[8,4096]{1,0:T(8,128)(2,1)S(1)} %get-tuple-element.37.refs_4_), channel_id=1, source_target_pairs={{0,10},{1,11},{2,8},{3,9},{4,14},{5,15},{6,12},{7,13},{8,2},{9,3},... | collective-permute-start | bytes 196616 | tf_op jit(solution)/shard_map/ppermute | solution.py:298
  96.7 9.2 %copy-start.14 = (bf16[8,4096]{1,0:T(8,128)(2,1)}, bf16[8,4096]{1,0:T(8,128)(2,1)S(1)}, u32[]{:S(2)}) copy-start(bf16[8,4096]{1,0:T(8,128)(2,1)S(1)} %collective-permute-done.15.refs_9_) | copy-start | bytes 196612
  96.7 9.2 %copy-start.15 = (bf16[8,4096]{1,0:T(8,128)(2,1)}, bf16[8,4096]{1,0:T(8,128)(2,1)S(1)}, u32[]{:S(2)}) copy-start(bf16[8,4096]{1,0:T(8,128)(2,1)S(1)} %collective-permute-done.11.refs_7_) | copy-start | bytes 196612
  96.7 9.2 %copy-start.13 = (bf16[8,4096]{1,0:T(8,128)(2,1)}, bf16[8,4096]{1,0:T(8,128)(2,1)S(1)}, u32[]{:S(2)}) copy-start(bf16[8,4096]{1,0:T(8,128)(2,1)S(1)} %collective-permute-done.10.refs_6_) | copy-start | bytes 196612
  104.1 1.8 %copy-start.16 = (bf16[8,4096]{1,0:T(8,128)(2,1)}, bf16[8,4096]{1,0:T(8,128)(2,1)S(1)}, u32[]{:S(2)}) copy-start(bf16[8,4096]{1,0:T(8,128)(2,1)S(1)} %collective-permute-done.7.refs_5_) | copy-start | bytes 196612
  105.8 0.6 copy-start.17

commit v8 on v6

--- a/solution.py
+++ b/solution.py
@@ -14,6 +14,8 @@
 SCALE = 2.0
 ROWS_STEP = 8
 COLUMNS_STEP = 2048
+LIGHT = pl.CostEstimate(flops=1, bytes_accessed=1, transcendentals=0)
+HEAVY = pl.CostEstimate(flops=1, bytes_accessed=100_000_000, transcendentals=0)
 
 
 def place_of(index, quarter):
@@ -100,6 +102,7 @@
             pltpu.SemaphoreType.DMA((steps,)),
         ],
         compiler_params=pltpu.CompilerParams(vmem_limit_bytes=56 * 2**20),
+        cost_estimate=LIGHT,
         name="pack_pairs" if pairs else "pack",
     )(adapter_slot, adapter_id.reshape(1, rows), hidden, after)
 
@@ -136,7 +139,7 @@
             )
 
 
-def adapt(arrived, a_maps, b_maps, after):
+def adapt(arrived, a_maps, b_maps, after, weight=LIGHT):
     count = len(arrived)
     lines = arrived[0].shape[0]
     return pl.pallas_call(
@@ -146,11 +149,7 @@
         out_specs=[pl.BlockSpec(memory_space=pltpu.VMEM)] * count,
         out_shape=[jax.ShapeDtypeStruct((lines, b_maps.shape[1]), jnp.bfloat16)] * count,
         compiler_params=pltpu.CompilerParams(vmem_limit_bytes=16 * 2**20),
-        cost_estimate=pl.CostEstimate(
-            flops=2 * count * lines * (a_maps.size + b_maps.size),
-            bytes_accessed=2 * (a_maps.size + b_maps.size),
-            transcendentals=0,
-        ),
+        cost_estimate=weight,
         name="adapt",
     )(*arrived, a_maps, b_maps, after)
 
@@ -207,39 +206,42 @@
             jax.ShapeDtypeStruct((KVH, steps, group * step, cells), jnp.float32),
         ],
         compiler_params=pltpu.CompilerParams(vmem_limit_bytes=16 * 2**20),
-        cost_estimate=pl.CostEstimate(
-            flops=2 * rows * width * cells, bytes_accessed=16 * 2**20, transcendentals=0
-        ),
+        cost_estimate=LIGHT,
         name="prep",
     )(base_q, kv_cache, lens, after)
 
 
 def attend_kernel(group, count, *refs):
-    routed_refs, returned_refs, refs = refs[:2], refs[2 : 2 + count], refs[2 + count :]
-    laid_refs, (out_ref, *held_refs, sems) = refs[:3], refs[3:]
-    keys_ref, values_ref, scores_ref = held_refs
+    routed_refs, given_refs, out_ref = refs[:2], refs[2 : 5 + count], refs[5 + count]
+    *held_refs, sems, laid_sems = refs[6 + count :]
+    returned_refs, (keys_ref, values_ref, scores_ref) = held_refs[:count], held_refs[count:]
     step = ROWS_STEP
     steps, _, cells = scores_ref.shape[1:]
     span = group * HEAD
     factor = 1.0 / jnp.sqrt(jnp.float32(HEAD))
     copies = [
+        pltpu.make_async_copy(given_ref, held_ref, sems.at[i])
+        for i, (given_ref, held_ref) in enumerate(zip(given_refs[:count], returned_refs))
+    ]
+    laid_copies = [
         [
-            pltpu.make_async_copy(laid_ref.at[k], held_ref.at[k], sems.at[k, i])
-            for i, (laid_ref, held_ref) in enumerate(zip(laid_refs, held_refs))
+            pltpu.make_async_copy(given_ref.at[k], held_ref.at[k], laid_sems.at[k, i])
+            for i, (given_ref, held_ref) in enumerate(zip(given_refs[count:], held_refs[count:]))
         ]
         for k in range(KVH)
     ]
-    for copy in copies:
-        for one in copy:
-            one.start()
+    for copy in sum(laid_copies, copies):
+        copy.start()
     routed = jnp.concatenate([ref[...].astype(jnp.float32) for ref in routed_refs], axis=0)
     routed = jnp.transpose(routed).astype(jnp.bfloat16)
+    for copy in copies:
+        copy.wait()
     for k in range(KVH):
         delta = jnp.dot(
             routed, stack(returned_refs, k * span, span), preferred_element_type=jnp.float32
         )
-        for one in copies[k]:
-            one.wait()
+        for copy in laid_copies[k]:
+            copy.wait()
         for i in range(steps):
             lines = slice(i * step, (i + 1) * step)
             at = slice(i * cells, (i + 1) * cells)
@@ -262,17 +264,18 @@
 
 def attend(routed, returned, laid, width):
     rows = routed[0].shape[1]
+    given = [*returned, *laid]
     return pl.pallas_call(
         functools.partial(attend_kernel, width // (KVH * HEAD), len(returned)),
-        in_specs=[pl.BlockSpec(memory_space=pltpu.VMEM)] * (2 + len(returned))
-        + [pl.BlockSpec(memory_space=pltpu.HBM)] * len(laid),
+        in_specs=[pl.BlockSpec(memory_space=pltpu.VMEM)] * 2
+        + [pl.BlockSpec(memory_space=pl.ANY)] * len(given),
         out_specs=pl.BlockSpec(memory_space=pltpu.VMEM),
         out_shape=jax.ShapeDtypeStruct((rows, width), jnp.bfloat16),
-        scratch_shapes=[pltpu.VMEM(part.shape, part.dtype) for part in laid]
-        + [pltpu.SemaphoreType.DMA((KVH, len(laid)))],
-        compiler_params=pltpu.CompilerParams(vmem_limit_bytes=24 * 2**20),
+        scratch_shapes=[pltpu.VMEM(part.shape, part.dtype) for part in given]
+        + [pltpu.SemaphoreType.DMA((len(returned),)), pltpu.SemaphoreType.DMA((KVH, len(laid)))],
+        compiler_params=pltpu.CompilerParams(vmem_limit_bytes=56 * 2**20),
         name="attend",
-    )(*routed, *returned, *laid)
+    )(*routed, *given)
 
 
 def on_device(hidden, adapter_id, adapter_slot, cache_len, base_q, kv_cache, a_maps, b_maps):
@@ -307,7 +310,7 @@
     change_near = adapt(arrived_near, a_maps, b_maps, laid[0])
     (change,) = adapt([arrived], a_maps, b_maps, change_near[0])
     returned = swap(change)
-    change_far = adapt(arrived_far, a_maps, b_maps, change)
+    change_far = adapt(arrived_far, a_maps, b_maps, change, HEAVY)
     returned_far = trade(change_far, far)
     returned_near = trade(change_near, near)
     returned = [returned, *returned_near, *returned_far]

time: 118 us -> 117 us (level)
  local copies, waits for them, and re-layouts: 17.8 us -> 15.5 us
  Pallas kernels: 23.7 us -> 25.2 us
    unnamed x42 -> x58, local copies, waits for them, and re-layouts: 17 us -> 14.6 us
    pallas_call x1, Pallas kernels: 6.6 us -> 8.73 us  [attend(): pl.pallas_call(functools.partial(attend_kernel, width // (KVH * HEAD), le...]
  transfers between devices with their start and end apart: 18 -> 18, of which waited for: 10 -> 10; matrix products, arithmetic and copies ran while one was open for 1% -> 1% of each run, Pallas kernels for 10% -> 9%
where the time goes in v8:
time: 117 us; the launch traced here: 116 us
  waiting for transfers between devices  44 us (38%)
  starting transfers between devices  31.2 us (27%)
  Pallas kernels  25.2 us (22%)
  local copies, waits for them, and re-layouts  15.5 us (13%)
    ppermute x16, waiting for transfers between devices, trade(): lax.ppermute(message, 'owner', [(i, i ^ apart) for i in range(owners)])  44 us
    ppermute x16, starting transfers between devices, trade(): lax.ppermute(message, 'owner', [(i, i ^ apart) for i in range(owners)])  17.8 us
    unnamed x58, local copies, waits for them, and re-layouts  14.6 us
    all_to_all x2, starting transfers between devices, swap(): lax.all_to_all(blocks, 'owner', split_axis=0, concat_axis=0, tiled=True,...  13.5 us
    pallas_call x1, Pallas kernels, attend(): pl.pallas_call(functools.partial(attend_kernel, width // (KVH * HEAD), le...  8.73 us
    pallas_call x2, Pallas kernels, pack(): pl.pallas_call(functools.partial(pack_kernel, pairs, owners, slot_count,...  7.18 us
    pallas_call x1, Pallas kernels, prep(): pl.pallas_call(functools.partial(prep_kernel, group, context), grid=(step...  4.99 us
    pallas_call x3, Pallas kernels, adapt(): pl.pallas_call(functools.partial(adapt_kernel, count), in_specs=[pl.Block...  4.28 us
  transfers between devices with their start and end apart: 18, of which 10 were waited for; matrix products, arithmetic and copies ran while one was open for 1% of the time, Pallas kernels for 9%

profile of v8, /device:TPU:9, one launch (start us, length us, event | category | flops | bytes accessed | tf_op | source)
XLA Modules:
  0.0 116.1 jit_solution(1989629268600435099)
XLA Ops:
  0.0 3.6 %pack.1 = (bf16[64,128]{1,0:T(8,128)(2,1)}, bf16[64,8320]{1,0:T(8,128)(2,1)}) custom-call(s32[32]{0:T(128)} %slots_ref.3, s32[1,128]{1,0:T(1,128)} %bitcast.7, bf16[128,8192]{1,0:T(8,128)(2,1)} %hidden_ref.3, s32[128]{0:T(128)} %after_ref.1), custom_call_target="tpu_custom_call" | custom-call | flops 1 | bytes 1 | tf_op jit(solution)/shard_map/pack/pallas_call | solution.py:89
  3.6 5.5 %all-to-all-start = ((bf16[8,8,8320]{2,1,0:T(8,128)(2,1)}), bf16[8,8,8320]{2,1,0:T(8,128)(2,1)}, u32[]{:S(2)}, u32[]{:S(2)}) async-start(bf16[8,8,8320]{2,1,0:T(8,128)(2,1)} %bitcast.6), calls=%async_computation | async-start | bytes 2129920 | tf_op jit(solution)/shard_map/all_to_all | solution.py:291
  9.1 3.6 %pack_pairs.1 = (bf16[64,128]{1,0:T(8,128)(2,1)}, bf16[8,8320]{1,0:T(8,128)(2,1)}, bf16[8,8320]{1,0:T(8,128)(2,1)}, bf16[8,8320]{1,0:T(8,128)(2,1)}, bf16[8,8320...) custom-call(s32[32]{0:T(128)} %slots_ref.3, ...), custom_call_target="tpu_custom_call" | custom-call | flops 1 | bytes 1 | tf_op jit(solution)/shard_map/pack_pairs/pallas_call | solution.py:89
  12.9 1.5 %collective-permute-start.1 = (bf16[8,8320]{1,0:T(8,128)(2,1)}, bf16[8,8320]{1,0:T(8,128)(2,1)S(1)}, u32[]{:S(2)}, u32[]{:S(2)}) collective-permute-start(bf16[8,8320]{1,0:T(8,128)(2,1)} %get-tuple-element.31), channel_id=1, source_target_pairs={{0,5},{1,4},{2,7},{3,6},{4,1},{5,0},{6,3},{7,2},{8,13},{9,12},{10,... | collective-permute-start | bytes 399368 | tf_op jit(solution)/shard_map/ppermute | solution.py:298
  14.4 1.6 %collective-permute-start.2 = (bf16[8,8320]{1,0:T(8,128)(2,1)}, bf16[8,8320]{1,0:T(8,128)(2,1)S(1)}, u32[]{:S(2)}, u32[]{:S(2)}) collective-permute-start(bf16[8,8320]{1,0:T(8,128)(2,1)} %get-tuple-element.32), channel_id=1, source_target_pairs={{0,6},{1,7},{2,4},{3,5},{4,2},{5,3},{6,0},{7,1},{8,14},{9,15},{10,... | collective-permute-start | bytes 399368 | tf_op jit(solution)/shard_map/ppermute | solution.py:298
  16.0 1.1 collective-permute-start.3
  17.3 0.7 broadcast_in_dim.9.len_ref
  18.0 2.2 %copy-done.5 = bf16[128,2,16,512]{3,2,1,0:T(8,128)(2,1)S(1)} copy-done((bf16[128,2,16,512]{3,2,1,0:T(8,128)(2,1)S(1)}, bf16[128,2,16,512]{3,2,1,0:T(8,128)(2,1)}, u32[]{:S(2)}) %copy-start.5) | copy-done | bytes 4194328
  20.2 1.2 %copy-done.8 = bf16[128,4096]{1,0:T(8,128)(2,1)S(1)} copy-done((bf16[128,4096]{1,0:T(8,128)(2,1)S(1)}, bf16[128,4096]{1,0:T(8,128)(2,1)}, u32[]{:S(2)}) %copy-start.8) | copy-done | bytes 1048600
  21.4 0.7 copy-done.12
  22.1 0.7 copy-done.13
  22.8 5.0 %prep.1 = (bf16[4,128,2048]{2,1,0:T(8,128)(2,1)S(1)}, bf16[4,2048,128]{2,1,0:T(8,128)(2,1)S(1)}, f32[4,16,64,128]{3,2,1,0:T(8,128)S(1)}) custom-call(bf16[128,4096]{1,0:T(8,128)(2,1)S(1)} %copy-done.8, bf16[128,2,16,512]{3,2,1,0:T(8,128)(2,1)S(1)} %copy-done.5, s32[16,1,128]{2,1,0:T(1,128)S(1)} %copy-done.13, bf16[64,128]{1,0:T(8,128)(2,1)S(1)} %copy-done.12), custom_call_target="tpu_custom_call" | custom-call | flops 1 | bytes 1 | tf_op jit(solution)/shard_map/prep/pallas_call | solution.py:189
  27.9 1.3 %copy-done.6 = bf16[4,2048,128]{2,1,0:T(8,128)(2,1)} copy-done((bf16[4,2048,128]{2,1,0:T(8,128)(2,1)}, bf16[4,2048,128]{2,1,0:T(8,128)(2,1)S(1)}, u32[]{:S(2)}) %copy-start.6) | copy-done | bytes 2097176
  29.2 1.3 %copy-done.7 = f32[4,16,64,128]{3,2,1,0:T(8,128)} copy-done((f32[4,16,64,128]{3,2,1,0:T(8,128)}, f32[4,16,64,128]{3,2,1,0:T(8,128)S(1)}, u32[]{:S(2)}) %copy-start.7) | copy-done | bytes 2097176
  30.5 0.8 collective-permute-done.2.refs_2_
  31.4 3.7 %collective-permute-done.3.refs_3_ = bf16[8,8320]{1,0:T(8,128)(2,1)} collective-permute-done((bf16[8,8320]{1,0:T(8,128)(2,1)}, bf16[8,8320]{1,0:T(8,128)(2,1)}, u32[]{:S(2)}, u32[]{:S(2)}) %collective-permute-start.3) | collective-permute-done | bytes 133152 | tf_op jit(solution)/shard_map/ppermute | solution.py:298
  35.1 1.6 %adapt.3 = (bf16[8,4096]{1,0:T(8,128)(2,1)S(1)}, bf16[8,4096]{1,0:T(8,128)(2,1)S(1)}, bf16[8,4096]{1,0:T(8,128)(2,1)S(1)}, bf16[8,4096]{1,0:T(8,128)(2,1)S(1)}) custom-call(bf16[8,8320]{1,0:T(8,128)(2,1)S(1)} %collective-permute-done.refs_0_, bf16[8,8320]{1,0:T(8,128)(2,1)S(1)} %collective-permute-done.1.refs_1_, ...), custom_call_target="tpu_custom_call" | custom-call | flops 1 | bytes 1 | tf_op jit(solution)/shard_map/adapt/pallas_call | solution.py:145
  36.7 1.4 %copy-done.2 = bf16[4,128,2048]{2,1,0:T(8,128)(2,1)} copy-done((bf16[4,128,2048]{2,1,0:T(8,128)(2,1)}, bf16[4,128,2048]{2,1,0:T(8,128)(2,1)S(1)}, u32[]{:S(2)}) %copy-start.2) | copy-done | bytes 2097176
  38.0 0.6 copy-done.9
  38.6 0.6 copy-done.14
  39.2 0.6 copy-done.16
  39.9 0.6 copy-done.18
  40.5 0.8 copy-done.10
  41.3 2.0 %adapt.4.refs_6_ = bf16[64,4096]{1,0:T(8,128)(2,1)S(1)} custom-call(bf16[64,8320]{1,0:T(8,128)(2,1)} %bitcast.2.refs_0_, bf16[8192,128]{1,0:T(8,128)(2,1)S(1)} %copy-done, bf16[128,4096]{1,0:T(8,128)(2,1)S(1)} %copy-done.1, bf16[8,4096]{1,0:T(8,128)(2,1)S(1)} %copy-done.10), custom_call_target="tpu_custom_call" | custom-call | flops 1 | bytes 1 | tf_op jit(solution)/shard_map/adapt/pallas_call | solution.py:145
  43.4 0.8 copy-done.3
  44.2 8.0 %all-to-all-start.1 = ((bf16[8,8,4096]{2,1,0:T(8,128)(2,1)}), bf16[8,8,4096]{2,1,0:T(8,128)(2,1)}, u32[]{:S(2)}, u32[]{:S(2)}) async-start(bf16[8,8,4096]{2,1,0:T(8,128)(2,1)} %bitcast.5), calls=%async_computation.1 | async-start | bytes 1048576 | tf_op jit(solution)/shard_map/all_to_all | solution.py:291
  52.2 0.9 collective-permute-start.8
  53.1 0.7 collective-permute-start.9
  53.8 2.2 %collective-permute-start.10 = (bf16[8,8320]{1,0:T(8,128)(2,1)}, bf16[8,8320]{1,0:T(8,128)(2,1)S(1)}, u32[]{:S(2)}, u32[]{:S(2)}) collective-permute-start(bf16[8,8320]{1,0:T(8,128)(2,1)} %get-tuple-element.41), channel_id=1, source_target_pairs={{0,14},{1,15},{2,12},{3,13},{4,10},{5,11},{6,8},{7,9},{8,6},{9,7},... | collective-permute-start | bytes 399368 | tf_op jit(solution)/shard_map/ppermute | solution.py:298
  56.0 0.6 collective-permute-start.11
  56.6 4.1 %collective-permute-start.5 = (bf16[8,4096]{1,0:T(8,128)(2,1)S(1)}, bf16[8,4096]{1,0:T(8,128)(2,1)S(1)}, u32[]{:S(2)}, u32[]{:S(2)}) collective-permute-start(bf16[8,4096]{1,0:T(8,128)(2,1)S(1)} %copy-done.19), channel_id=1, source_target_pairs={{0,5},{1,4},{2,7},{3,6},{4,1},{5,0},{6,3},{7,2},{8,13},{9,12},{10,... | collective-permute-start | bytes 196616 | tf_op jit(solution)/shard_map/ppermute | solution.py:298
  60.6 19.0 %collective-permute-done.8.refs_0_ = bf16[8,8320]{1,0:T(8,128)(2,1)S(1)} collective-permute-done((bf16[8,8320]{1,0:T(8,128)(2,1)}, bf16[8,8320]{1,0:T(8,128)(2,1)S(1)}, u32[]{:S(2)}, u32[]{:S(2)}) %collective-permute-start.8) | collective-permute-done | bytes 133152 | tf_op jit(solution)/shard_map/ppermute | solution.py:298
  79.6 3.5 %collective-permute-done.9.refs_1_ = bf16[8,8320]{1,0:T(8,128)(2,1)S(1)} collective-permute-done((bf16[8,8320]{1,0:T(8,128)(2,1)}, bf16[8,8320]{1,0:T(8,128)(2,1)S(1)}, u32[]{:S(2)}, u32[]{:S(2)}) %collective-permute-start.9) | collective-permute-done | bytes 133152 | tf_op jit(solution)/shard_map/ppermute | solution.py:298
  83.1 0.4 collective-permute-start.7
  83.5 3.4 %collective-permute-done.10.refs_2_ = bf16[8,8320]{1,0:T(8,128)(2,1)S(1)} collective-permute-done((bf16[8,8320]{1,0:T(8,128)(2,1)}, bf16[8,8320]{1,0:T(8,128)(2,1)S(1)}, u32[]{:S(2)}, u32[]{:S(2)}) %collective-permute-start.10) | collective-permute-done | bytes 133152 | tf_op jit(solution)/shard_map/ppermute | solution.py:298
  86.9 4.6 %collective-permute-done.11.refs_3_ = bf16[8,8320]{1,0:T(8,128)(2,1)S(1)} collective-permute-done((bf16[8,8320]{1,0:T(8,128)(2,1)}, bf16[8,8320]{1,0:T(8,128)(2,1)S(1)}, u32[]{:S(2)}, u32[]{:S(2)}) %collective-permute-start.11) | collective-permute-done | bytes 133152 | tf_op jit(solution)/shard_map/ppermute | solution.py:298
  91.5 1.0 copy-done.4
  92.5 0.7 adapt.5
  93.2 0.8 collective-permute-start.12
  94.0 1.1 collective-permute-start.13
  95.1 1.2 %collective-permute-start.14 = (bf16[8,4096]{1,0:T(8,128)(2,1)S(1)}, bf16[8,4096]{1,0:T(8,128)(2,1)S(1)}, u32[]{:S(2)}, u32[]{:S(2)}) collective-permute-start(bf16[8,4096]{1,0:T(8,128)(2,1)S(1)} %get-tuple-element.45), channel_id=1, source_target_pairs={{0,14},{1,15},{2,12},{3,13},{4,10},{5,11},{6,8},{7,9},{8,6},{9,7},... | collective-permute-start | bytes 196616 | tf_op jit(solution)/shard_map/ppermute | solution.py:298
  96.3 1.4 %collective-permute-start.15 = (bf16[8,4096]{1,0:T(8,128)(2,1)S(1)}, bf16[8,4096]{1,0:T(8,128)(2,1)S(1)}, u32[]{:S(2)}, u32[]{:S(2)}) collective-permute-start(bf16[8,4096]{1,0:T(8,128)(2,1)S(1)} %get-tuple-element.46), channel_id=1, source_target_pairs={{0,15},{1,14},{2,13},{3,12},{4,11},{5,10},{6,9},{7,8},{8,7},{9,6},... | collective-permute-start | bytes 196616 | tf_op jit(solution)/shard_map/ppermute | solution.py:298
  97.7 2.1 %collective-permute-done.12.refs_7_ = bf16[8,4096]{1,0:T(8,128)(2,1)S(1)} collective-permute-done((bf16[8,4096]{1,0:T(8,128)(2,1)S(1)}, bf16[8,4096]{1,0:T(8,128)(2,1)S(1)}, u32[]{:S(2)}, u32[]{:S(2)}) %collective-permute-start.12) | collective-permute-done | bytes 65568 | tf_op jit(solution)/shard_map/ppermute | solution.py:298
  99.8 4.1 %collective-permute-done.13.refs_8_ = bf16[8,4096]{1,0:T(8,128)(2,1)S(1)} collective-permute-done((bf16[8,4096]{1,0:T(8,128)(2,1)S(1)}, bf16[8,4096]{1,0:T(8,128)(2,1)S(1)}, u32[]{:S(2)}, u32[]{:S(2)}) %collective-permute-start.13) | collective-permute-done | bytes 65568 | tf_op jit(solution)/shard_map/ppermute | solution.py:298
  103.9 1.5 %collective-permute-done.14.refs_9_ = bf16[8,4096]{1,0:T(8,128)(2,1)S(1)} collective-permute-done((bf16[8,4096]{1,0:T(8,128)(2,1)S(1)}, bf16[8,4096]{1,0:T(8,128)(2,1)S(1)}, u32[]{:S(2)}, u32[]{:S(2)}) %collective-permute-start.14) | collective-permute-done | bytes 65568 | tf_op jit(solution)/shard_map/ppermute | solution.py:298
  105.3 1.4 %collective-permute-done.15.refs_10_ = bf16[8,4096]{1,0:T(8,128)(2,1)S(1)} collective-permute-done((bf16[8,4096]{1,0:T(8,128)(2,1)S(1)}, bf16[8,4096]{1,0:T(8,128)(2,1)S(1)}, u32[]{:S(2)}, u32[]{:S(2)}) %collective-permute-start.15) | collective-permute-done | bytes 65568 | tf_op jit(solution)/shard_map/ppermute | solution.py:298
  106.8 0.6 copy-done.27
  107.3 8.7 %attend.1 = bf16[128,4096]{1,0:T(8,128)(2,1)} custom-call(bf16[64,128]{1,0:T(8,128)(2,1)} %get-tuple-element.27.after_ref.refs_0_, bf16[64,128]{1,0:T(8,128)(2,1)} %get-tuple-element.28._.refs_1_, bf16[64,4096]{1,0:T(8,128)(2,1)} %bitcast.4.refs_2_, bf16[8,4096]{1,0:T(8,128)(2,1)} %copy-done.23, bf16[8,4096]{1,0:T(8,128)(2,1)} %copy-done.20, ...), custom_call_target="tpu_custom_call" | custom-call | tf_op jit(solution)/shard_map/attend/pallas_call | solution.py:268
  (56 shorter events, 0.5 us)
Async XLA Ops:
  3.6 13.5 %copy-start.28 = (s32[128]{0:T(128)S(1)}, s32[128]{0:T(128)}, u32[]{:S(2)}) copy-start(s32[128]{0:T(128)} %param.11) | copy-start | bytes 1540
  3.6 36.9 %all-to-all-start = ((bf16[8,8,8320]{2,1,0:T(8,128)(2,1)}), bf16[8,8,8320]{2,1,0:T(8,128)(2,1)}, u32[]{:S(2)}, u32[]{:S(2)}) async-start(bf16[8,8,8320]{2,1,0:T(8,128)(2,1)} %bitcast.6), calls=%async_computation | async-start | bytes 2129920 | tf_op jit(solution)/shard_map/all_to_all | solution.py:291
  12.7 17.8 %collective-permute-start = (bf16[8,8320]{1,0:T(8,128)(2,1)}, bf16[8,8320]{1,0:T(8,128)(2,1)S(1)}, u32[]{:S(2)}, u32[]{:S(2)}) collective-permute-start(bf16[8,8320]{1,0:T(8,128)(2,1)} %get-tuple-element.30), channel_id=1, source_target_pairs={{0,4},{1,5},{2,6},{3,7},{4,0},{5,1},{6,2},{7,3},{8,12},{9,13},{10,... | collective-permute-start | bytes 399368 | tf_op jit(solution)/shard_map/ppermute | solution.py:298
  12.9 17.6 %collective-permute-start.1 = (bf16[8,8320]{1,0:T(8,128)(2,1)}, bf16[8,8320]{1,0:T(8,128)(2,1)S(1)}, u32[]{:S(2)}, u32[]{:S(2)}) collective-permute-start(bf16[8,8320]{1,0:T(8,128)(2,1)} %get-tuple-element.31), channel_id=1, source_target_pairs={{0,5},{1,4},{2,7},{3,6},{4,1},{5,0},{6,3},{7,2},{8,13},{9,12},{10,... | collective-permute-start | bytes 399368 | tf_op jit(solution)/shard_map/ppermute | solution.py:298
  14.4 17.0 %collective-permute-start.2 = (bf16[8,8320]{1,0:T(8,128)(2,1)}, bf16[8,8320]{1,0:T(8,128)(2,1)S(1)}, u32[]{:S(2)}, u32[]{:S(2)}) collective-permute-start(bf16[8,8320]{1,0:T(8,128)(2,1)} %get-tuple-element.32), channel_id=1, source_target_pairs={{0,6},{1,7},{2,4},{3,5},{4,2},{5,3},{6,0},{7,1},{8,14},{9,15},{10,... | collective-permute-start | bytes 399368 | tf_op jit(solution)/shard_map/ppermute | solution.py:298
  16.0 19.0 %collective-permute-start.3 = (bf16[8,8320]{1,0:T(8,128)(2,1)}, bf16[8,8320]{1,0:T(8,128)(2,1)}, u32[]{:S(2)}, u32[]{:S(2)}) collective-permute-start(bf16[8,8320]{1,0:T(8,128)(2,1)} %get-tuple-element.33), channel_id=1, source_target_pairs={{0,7},{1,6},{2,5},{3,4},{4,3},{5,2},{6,1},{7,0},{8,15},{9,14},{10,... | collective-permute-start | bytes 399368 | tf_op jit(solution)/shard_map/ppermute | solution.py:298
  18.0 2.2 %copy-start.5 = (bf16[128,2,16,512]{3,2,1,0:T(8,128)(2,1)S(1)}, bf16[128,2,16,512]{3,2,1,0:T(8,128)(2,1)}, u32[]{:S(2)}) copy-start(bf16[128,2,16,512]{3,2,1,0:T(8,128)(2,1)} %kv_ref.1) | copy-start | bytes 12582916
  20.2 1.2 %copy-start.8 = (bf16[128,4096]{1,0:T(8,128)(2,1)S(1)}, bf16[128,4096]{1,0:T(8,128)(2,1)}, u32[]{:S(2)}) copy-start(bf16[128,4096]{1,0:T(8,128)(2,1)} %base_ref.1) | copy-start | bytes 3145732
  21.4 0.7 copy-start.12
  22.1 0.7 copy-start.13
  22.8 12.2 %copy-start = (bf16[8192,128]{1,0:T(8,128)(2,1)S(1)}, bf16[8192,128]{1,0:T(8,128)(2,1)}, u32[]{:S(2)}) copy-start(bf16[8192,128]{1,0:T(8,128)(2,1)} %refs_4_.3) | copy-start | bytes 6291460
  22.8 12.2 %copy-start.1 = (bf16[128,4096]{1,0:T(8,128)(2,1)S(1)}, bf16[128,4096]{1,0:T(8,128)(2,1)}, u32[]{:S(2)}) copy-start(bf16[128,4096]{1,0:T(8,128)(2,1)} %refs_5_.3) | copy-start | bytes 3145732
  27.8 1.3 %copy-start.6 = (bf16[4,2048,128]{2,1,0:T(8,128)(2,1)}, bf16[4,2048,128]{2,1,0:T(8,128)(2,1)S(1)}, u32[]{:S(2)}) copy-start(bf16[4,2048,128]{2,1,0:T(8,128)(2,1)S(1)} %get-tuple-element.47.refs_12_) | copy-start | bytes 6291460
  29.2 1.3 %copy-start.7 = (f32[4,16,64,128]{3,2,1,0:T(8,128)}, f32[4,16,64,128]{3,2,1,0:T(8,128)S(1)}, u32[]{:S(2)}) copy-start(f32[4,16,64,128]{3,2,1,0:T(8,128)S(1)} %get-tuple-element.48.refs_13_) | copy-start | bytes 6291460
  36.6 1.4 %copy-start.2 = (bf16[4,128,2048]{2,1,0:T(8,128)(2,1)}, bf16[4,128,2048]{2,1,0:T(8,128)(2,1)S(1)}, u32[]{:S(2)}) copy-start(bf16[4,128,2048]{2,1,0:T(8,128)(2,1)S(1)} %get-tuple-element.34.refs_6_.refs_11_) | copy-start | bytes 6291460
  38.0 0.6 copy-start.9
  38.6 0.6 copy-start.14
  39.2 0.6 copy-start.16
  39.9 0.6 copy-start.18
  40.5 0.8 copy-start.10
  41.3 15.2 %copy-start.19 = (bf16[8,4096]{1,0:T(8,128)(2,1)S(1)}, bf16[8,4096]{1,0:T(8,128)(2,1)}, u32[]{:S(2)}) copy-start(bf16[8,4096]{1,0:T(8,128)(2,1)} %copy-done.18) | copy-start | bytes 196612
  41.3 38.3 %copy-start.17 = (bf16[8,4096]{1,0:T(8,128)(2,1)S(1)}, bf16[8,4096]{1,0:T(8,128)(2,1)}, u32[]{:S(2)}) copy-start(bf16[8,4096]{1,0:T(8,128)(2,1)} %copy-done.16) | copy-start | bytes 196612
  41.3 41.8 %copy-start.15 = (bf16[8,4096]{1,0:T(8,128)(2,1)S(1)}, bf16[8,4096]{1,0:T(8,128)(2,1)}, u32[]{:S(2)}) copy-start(bf16[8,4096]{1,0:T(8,128)(2,1)} %copy-done.14) | copy-start | bytes 196612
  41.3 45.5 %copy-start.11 = (bf16[8,4096]{1,0:T(8,128)(2,1)S(1)}, bf16[8,4096]{1,0:T(8,128)(2,1)}, u32[]{:S(2)}) copy-start(bf16[8,4096]{1,0:T(8,128)(2,1)} %copy-done.9) | copy-start | bytes 196612
  43.4 0.8 copy-start.3
  44.2 62.6 %all-to-all-start.1 = ((bf16[8,8,4096]{2,1,0:T(8,128)(2,1)}), bf16[8,8,4096]{2,1,0:T(8,128)(2,1)}, u32[]{:S(2)}, u32[]{:S(2)}) async-start(bf16[8,8,4096]{2,1,0:T(8,128)(2,1)} %bitcast.5), calls=%async_computation.1 | async-start | bytes 1048576 | tf_op jit(solution)/shard_map/all_to_all | solution.py:291
  52.2 27.5 %collective-permute-start.8 = (bf16[8,8320]{1,0:T(8,128)(2,1)}, bf16[8,8320]{1,0:T(8,128)(2,1)S(1)}, u32[]{:S(2)}, u32[]{:S(2)}) collective-permute-start(bf16[8,8320]{1,0:T(8,128)(2,1)} %get-tuple-element.39), channel_id=1, source_target_pairs={{0,12},{1,13},{2,14},{3,15},{4,8},{5,9},{6,10},{7,11},{8,4},{9,5},... | collective-permute-start | bytes 399368 | tf_op jit(solution)/shard_map/ppermute | solution.py:298
  53.1 30.0 %collective-permute-start.9 = (bf16[8,8320]{1,0:T(8,128)(2,1)}, bf16[8,8320]{1,0:T(8,128)(2,1)S(1)}, u32[]{:S(2)}, u32[]{:S(2)}) collective-permute-start(bf16[8,8320]{1,0:T(8,128)(2,1)} %get-tuple-element.40), channel_id=1, source_target_pairs={{0,13},{1,12},{2,15},{3,14},{4,9},{5,8},{6,11},{7,10},{8,5},{9,4},... | collective-permute-start | bytes 399368 | tf_op jit(solution)/shard_map/ppermute | solution.py:298
  53.8 33.1 %collective-permute-start.10 = (bf16[8,8320]{1,0:T(8,128)(2,1)}, bf16[8,8320]{1,0:T(8,128)(2,1)S(1)}, u32[]{:S(2)}, u32[]{:S(2)}) collective-permute-start(bf16[8,8320]{1,0:T(8,128)(2,1)} %get-tuple-element.41), channel_id=1, source_target_pairs={{0,14},{1,15},{2,12},{3,13},{4,10},{5,11},{6,8},{7,9},{8,6},{9,7},... | collective-permute-start | bytes 399368 | tf_op jit(solution)/shard_map/ppermute | solution.py:298
  56.0 35.5 %collective-permute-start.11 = (bf16[8,8320]{1,0:T(8,128)(2,1)}, bf16[8,8320]{1,0:T(8,128)(2,1)S(1)}, u32[]{:S(2)}, u32[]{:S(2)}) collective-permute-start(bf16[8,8320]{1,0:T(8,128)(2,1)} %get-tuple-element.42), channel_id=1, source_target_pairs={{0,15},{1,14},{2,13},{3,12},{4,11},{5,10},{6,9},{7,8},{8,7},{9,6},... | collective-permute-start | bytes 399368 | tf_op jit(solution)/shard_map/ppermute | solution.py:298
  56.6 37.4 %collective-permute-start.5 = (bf16[8,4096]{1,0:T(8,128)(2,1)S(1)}, bf16[8,4096]{1,0:T(8,128)(2,1)S(1)}, u32[]{:S(2)}, u32[]{:S(2)}) collective-permute-start(bf16[8,4096]{1,0:T(8,128)(2,1)S(1)} %copy-done.19), channel_id=1, source_target_pairs={{0,5},{1,4},{2,7},{3,6},{4,1},{5,0},{6,3},{7,2},{8,13},{9,12},{10,... | collective-permute-start | bytes 196616 | tf_op jit(solution)/shard_map/ppermute | solution.py:298
  79.6 15.5 %collective-permute-start.6 = (bf16[8,4096]{1,0:T(8,128)(2,1)S(1)}, bf16[8,4096]{1,0:T(8,128)(2,1)S(1)}, u32[]{:S(2)}, u32[]{:S(2)}) collective-permute-start(bf16[8,4096]{1,0:T(8,128)(2,1)S(1)} %copy-done.17), channel_id=1, source_target_pairs={{0,6},{1,7},{2,4},{3,5},{4,2},{5,3},{6,0},{7,1},{8,14},{9,15},{10,... | collective-permute-start | bytes 196616 | tf_op jit(solution)/shard_map/ppermute | solution.py:298
  83.1 13.1 %collective-permute-start.7 = (bf16[8,4096]{1,0:T(8,128)(2,1)S(1)}, bf16[8,4096]{1,0:T(8,128)(2,1)S(1)}, u32[]{:S(2)}, u32[]{:S(2)}) collective-permute-start(bf16[8,4096]{1,0:T(8,128)(2,1)S(1)} %copy-done.15), channel_id=1, source_target_pairs={{0,7},{1,6},{2,5},{3,4},{4,3},{5,2},{6,1},{7,0},{8,15},{9,14},{10,... | collective-permute-start | bytes 196616 | tf_op jit(solution)/shard_map/ppermute | solution.py:298
  86.9 10.8 %collective-permute-start.4 = (bf16[8,4096]{1,0:T(8,128)(2,1)S(1)}, bf16[8,4096]{1,0:T(8,128)(2,1)S(1)}, u32[]{:S(2)}, u32[]{:S(2)}) collective-permute-start(bf16[8,4096]{1,0:T(8,128)(2,1)S(1)} %copy-done.11), channel_id=1, source_target_pairs={{0,4},{1,5},{2,6},{3,7},{4,0},{5,1},{6,2},{7,3},{8,12},{9,13},{10,... | collective-permute-start | bytes 196616 | tf_op jit(solution)/shard_map/ppermute | solution.py:298
  91.5 1.0 copy-start.4
  93.2 6.6 %collective-permute-start.12 = (bf16[8,4096]{1,0:T(8,128)(2,1)S(1)}, bf16[8,4096]{1,0:T(8,128)(2,1)S(1)}, u32[]{:S(2)}, u32[]{:S(2)}) collective-permute-start(bf16[8,4096]{1,0:T(8,128)(2,1)S(1)} %get-tuple-element.43), channel_id=1, source_target_pairs={{0,12},{1,13},{2,14},{3,15},{4,8},{5,9},{6,10},{7,11},{8,4},{9,5},... | collective-permute-start | bytes 196616 | tf_op jit(solution)/shard_map/ppermute | solution.py:298
  94.0 12.8 %copy-start.20 = (bf16[8,4096]{1,0:T(8,128)(2,1)}, bf16[8,4096]{1,0:T(8,128)(2,1)S(1)}, u32[]{:S(2)}) copy-start(bf16[8,4096]{1,0:T(8,128)(2,1)S(1)} %collective-permute-done.5.refs_4_) | copy-start | bytes 196612
  94.0 9.9 %collective-permute-start.13 = (bf16[8,4096]{1,0:T(8,128)(2,1)S(1)}, bf16[8,4096]{1,0:T(8,128)(2,1)S(1)}, u32[]{:S(2)}, u32[]{:S(2)}) collective-permute-start(bf16[8,4096]{1,0:T(8,128)(2,1)S(1)} %get-tuple-element.44), channel_id=1, source_target_pairs={{0,13},{1,12},{2,15},{3,14},{4,9},{5,8},{6,11},{7,10},{8,5},{9,4},... | collective-permute-start | bytes 196616 | tf_op jit(solution)/shard_map/ppermute | solution.py:298
  95.1 11.7 %copy-start.21 = (bf16[8,4096]{1,0:T(8,128)(2,1)}, bf16[8,4096]{1,0:T(8,128)(2,1)S(1)}, u32[]{:S(2)}) copy-start(bf16[8,4096]{1,0:T(8,128)(2,1)S(1)} %collective-permute-done.6.refs_5_) | copy-start | bytes 196612
  95.1 10.2 %collective-permute-start.14 = (bf16[8,4096]{1,0:T(8,128)(2,1)S(1)}, bf16[8,4096]{1,0:T(8,128)(2,1)S(1)}, u32[]{:S(2)}, u32[]{:S(2)}) collective-permute-start(bf16[8,4096]{1,0:T(8,128)(2,1)S(1)} %get-tuple-element.45), channel_id=1, source_target_pairs={{0,14},{1,15},{2,12},{3,13},{4,10},{5,11},{6,8},{7,9},{8,6},{9,7},... | collective-permute-start | bytes 196616 | tf_op jit(solution)/shard_map/ppermute | solution.py:298
  96.3 9.1 %copy-start.22 = (bf16[8,4096]{1,0:T(8,128)(2,1)}, bf16[8,4096]{1,0:T(8,128)(2,1)S(1)}, u32[]{:S(2)}) copy-start(bf16[8,4096]{1,0:T(8,128)(2,1)S(1)} %collective-permute-done.7.refs_6_) | copy-start | bytes 196612
  96.3 10.5 %collective-permute-start.15 = (bf16[8,4096]{1,0:T(8,128)(2,1)S(1)}, bf16[8,4096]{1,0:T(8,128)(2,1)S(1)}, u32[]{:S(2)}, u32[]{:S(2)}) collective-permute-start(bf16[8,4096]{1,0:T(8,128)(2,1)S(1)} %get-tuple-element.46), channel_id=1, source_target_pairs={{0,15},{1,14},{2,13},{3,12},{4,11},{5,10},{6,9},{7,8},{8,7},{9,6},... | collective-permute-start | bytes 196616 | tf_op jit(solution)/shard_map/ppermute | solution.py:298
  97.7 7.7 %copy-start.23 = (bf16[8,4096]{1,0:T(8,128)(2,1)}, bf16[8,4096]{1,0:T(8,128)(2,1)S(1)}, u32[]{:S(2)}) copy-start(bf16[8,4096]{1,0:T(8,128)(2,1)S(1)} %collective-permute-done.4.refs_3_) | copy-start | bytes 196612
  99.8 7.0 %copy-start.24 = (bf16[8,4096]{1,0:T(8,128)(2,1)}, bf16[8,4096]{1,0:T(8,128)(2,1)S(1)}, u32[]{:S(2)}) copy-start(bf16[8,4096]{1,0:T(8,128)(2,1)S(1)} %collective-permute-done.12.refs_7_) | copy-start | bytes 196612
  103.9 2.9 %copy-start.25 = (bf16[8,4096]{1,0:T(8,128)(2,1)}, bf16[8,4096]{1,0:T(8,128)(2,1)S(1)}, u32[]{:S(2)}) copy-start(bf16[8,4096]{1,0:T(8,128)(2,1)S(1)} %collective-permute-done.13.refs_8_) | copy-start | bytes 196612
  105.3 1.4 %copy-start.26 = (bf16[8,4096]{1,0:T(8,128)(2,1)}, bf16[8,4096]{1,0:T(8,128)(2,1)S(1)}, u32[]{:S(2)}) copy-start(bf16[8,4096]{1,0:T(8,128)(2,1)S(1)} %collective-permute-done.14.refs_9_) | copy-start | bytes 196612
  106.7 0.6 copy-start.27

commit v9 on v3

--- a/solution.py
+++ b/solution.py
@@ -97,7 +97,7 @@
     )(adapter_slot, adapter_id.reshape(1, rows), hidden)
 
 
-def adapt_kernel(arrived_ref, a_ref, b_ref, change_ref):
+def adapt_kernel(arrived_ref, a_ref, b_ref, _, change_ref):
     width = a_ref.shape[0]
     low = jnp.zeros((arrived_ref.shape[0], a_ref.shape[1]), jnp.float32)
     for at in range(0, width, COLUMNS_STEP):
@@ -117,116 +117,160 @@
         ).astype(change_ref.dtype)
 
 
-def adapt(arrived, a_maps, b_maps):
+def adapt(arrived, a_maps, b_maps, after):
     return pl.pallas_call(
         adapt_kernel,
-        in_specs=[pl.BlockSpec(memory_space=pltpu.VMEM)] * 3,
+        in_specs=[pl.BlockSpec(memory_space=pltpu.VMEM)] * 3 + [pl.BlockSpec(memory_space=pl.ANY)],
         out_specs=pl.BlockSpec(memory_space=pltpu.VMEM),
         out_shape=jax.ShapeDtypeStruct((arrived.shape[0], b_maps.shape[1]), jnp.bfloat16),
         compiler_params=pltpu.CompilerParams(vmem_limit_bytes=16 * 2**20),
         name="adapt",
-    )(arrived, a_maps, b_maps)
+    )(arrived, a_maps, b_maps, after)
 
 
 def tall(rows, group):
     return jnp.concatenate([rows[:, g * HEAD : (g + 1) * HEAD] for g in range(group)], axis=0)
 
 
-def prep_kernel(group, context, base_ref, kv_ref, len_ref, keys_ref, values_ref, scores_ref):
-    step = ROWS_STEP
+def prep_kernel(group, base_ref, kv_ref, keys_ref, values_ref, query_ref):
+    step, context = kv_ref.shape[0], kv_ref.shape[2]
     cells = step * context
-    lane = lax.broadcasted_iota(jnp.int32, (group * step, cells), 1)
-    line = lax.broadcasted_iota(jnp.int32, (group * step, cells), 0)
-    live = (lane // context == lax.rem(line, step)) & (lax.rem(lane, context) < len_ref[...][0])
-    factor = 1.0 / jnp.sqrt(jnp.float32(HEAD))
     for k in range(KVH):
         head = slice(k * HEAD, (k + 1) * HEAD)
         keys = kv_ref[:, 0, :, head].astype(jnp.float32).reshape(cells, HEAD)
-        keys = jnp.transpose(keys).astype(keys_ref.dtype)
-        keys_ref[k] = keys
+        keys_ref[k] = jnp.transpose(keys).astype(keys_ref.dtype)
         values_ref[k] = kv_ref[:, 1, :, head].reshape(cells, HEAD)
         base = base_ref[:, k * group * HEAD : (k + 1) * group * HEAD].astype(jnp.float32)
-        scores = jnp.dot(
-            tall(base, group).astype(jnp.bfloat16), keys, preferred_element_type=jnp.float32
-        )
-        scores_ref[k, 0] = jnp.where(live, scores * factor, -jnp.inf)
-
-
-def prep(base_q, kv_cache, cache_len):
+        query_ref[k, 0] = tall(base, group).astype(query_ref.dtype)
+
+
+def prep(base_q, kv_cache):
     rows, width = base_q.shape
     context = kv_cache.shape[2]
     group = width // (KVH * HEAD)
     step = ROWS_STEP
     steps = rows // step
     cells = step * context
-    lens = jnp.repeat(cache_len, context).reshape(steps, 1, cells)
     return pl.pallas_call(
-        functools.partial(prep_kernel, group, context),
+        functools.partial(prep_kernel, group),
         grid=(steps,),
         in_specs=[
             pl.BlockSpec((step, width), lambda i: (i, 0)),
             pl.BlockSpec((step, *kv_cache.shape[1:]), lambda i: (i, 0, 0, 0)),
-            pl.BlockSpec((1, 1, cells), lambda i: (i, 0, 0)),
         ],
         out_specs=[
             pl.BlockSpec((KVH, HEAD, cells), lambda i: (0, 0, i)),
             pl.BlockSpec((KVH, cells, HEAD), lambda i: (0, i, 0)),
-            pl.BlockSpec((KVH, 1, group * step, cells), lambda i: (0, i, 0, 0)),
+            pl.BlockSpec((KVH, 1, group * step, HEAD), lambda i: (0, i, 0, 0)),
         ],
         out_shape=[
             jax.ShapeDtypeStruct((KVH, HEAD, rows * context), jnp.bfloat16),
             jax.ShapeDtypeStruct((KVH, rows * context, HEAD), jnp.bfloat16),
-            jax.ShapeDtypeStruct((KVH, steps, group * step, cells), jnp.float32),
+            jax.ShapeDtypeStruct((KVH, steps, group * step, HEAD), jnp.bfloat16),
         ],
         compiler_params=pltpu.CompilerParams(vmem_limit_bytes=16 * 2**20),
-        cost_estimate=pl.CostEstimate(
-            flops=2 * rows * width * cells, bytes_accessed=16 * 2**20, transcendentals=0
-        ),
         name="prep",
-    )(base_q, kv_cache, lens)
-
-
-def attend_kernel(group, routed_ref, returned_ref, keys_ref, values_ref, scores_ref, out_ref):
+    )(base_q, kv_cache)
+
+
+def attend_kernel(
+    group,
+    context,
+    routed_ref,
+    returned_ref,
+    keys_ref,
+    lens_ref,
+    values_hbm,
+    query_hbm,
+    out_hbm,
+    values_ref,
+    query_ref,
+    bias_ref,
+    out_ref,
+    sems,
+):
     step = ROWS_STEP
-    steps, _, cells = scores_ref.shape[1:]
+    steps, lines = query_ref.shape[1:3]
+    cells = step * context
     span = group * HEAD
     factor = 1.0 / jnp.sqrt(jnp.float32(HEAD))
+    loads = [
+        [
+            pltpu.make_async_copy(query_hbm.at[k], query_ref.at[k], sems.at[k, 0]),
+            pltpu.make_async_copy(values_hbm.at[k], values_ref.at[k], sems.at[k, 1]),
+        ]
+        for k in range(KVH)
+    ]
+    stores = [
+        pltpu.make_async_copy(
+            out_ref.at[:, pl.ds(k * span, span)], out_hbm.at[:, pl.ds(k * span, span)], sems.at[k, 2]
+        )
+        for k in range(KVH)
+    ]
+    for load in loads:
+        for copy in load:
+            copy.start()
+    lane = lax.broadcasted_iota(jnp.int32, (lines, cells), 1)
+    line = lax.broadcasted_iota(jnp.int32, (lines, cells), 0)
+    own = lax.div(lane, context) == lax.rem(line, step)
+    position = lax.rem(lane, context)
+    for i in range(steps):
+        bias_ref[i] = jnp.where(own & (position < lens_ref[i]), 0.0, -jnp.inf)
     for k in range(KVH):
         delta = jnp.dot(
             routed_ref[...],
             returned_ref[:, k * span : (k + 1) * span],
             preferred_element_type=jnp.float32,
         )
+        for copy in loads[k]:
+            copy.wait()
         for i in range(steps):
-            lines = slice(i * step, (i + 1) * step)
+            rows = slice(i * step, (i + 1) * step)
             at = slice(i * cells, (i + 1) * cells)
-            change = jnp.dot(
-                tall(delta[lines], group).astype(jnp.bfloat16),
-                keys_ref[k, :, at],
+            keys = keys_ref[k, :, at]
+            change = tall(delta[rows], group).astype(jnp.bfloat16)
+            scores = jnp.dot(
+                jnp.concatenate([query_ref[k, i], change], axis=1),
+                jnp.concatenate([keys, keys], axis=0),
                 preferred_element_type=jnp.float32,
             )
-            scores = scores_ref[k, i] + change * factor
+            scores = scores * factor + bias_ref[i]
             expo = jnp.exp(scores - jnp.max(scores, axis=1, keepdims=True))
             probs = expo * (1.0 / jnp.sum(expo, axis=1, keepdims=True))
             out = jnp.dot(
                 probs.astype(jnp.bfloat16), values_ref[k, at, :], preferred_element_type=jnp.float32
             )
             for g in range(group):
-                out_ref[lines, (k * group + g) * HEAD : (k * group + g + 1) * HEAD] = out[
+                out_ref[rows, (k * group + g) * HEAD : (k * group + g + 1) * HEAD] = out[
                     g * step : (g + 1) * step
                 ].astype(out_ref.dtype)
-
-
-def attend(routed, returned, keys, values, scores):
+        stores[k].start()
+    for store in stores:
+        store.wait()
+
+
+def attend(routed, returned, cache_len, laid, context):
+    keys, values, query = laid
     rows, width = routed.shape[0], returned.shape[1]
+    steps = query.shape[1]
+    cells = ROWS_STEP * context
+    lens = jnp.repeat(cache_len, context).reshape(steps, 1, cells)
     return pl.pallas_call(
-        functools.partial(attend_kernel, width // (KVH * HEAD)),
-        in_specs=[pl.BlockSpec(memory_space=pltpu.VMEM)] * 5,
-        out_specs=pl.BlockSpec(memory_space=pltpu.VMEM),
+        functools.partial(attend_kernel, width // (KVH * HEAD), context),
+        in_specs=[pl.BlockSpec(memory_space=pltpu.VMEM)] * 4
+        + [pl.BlockSpec(memory_space=pl.ANY)] * 2,
+        out_specs=pl.BlockSpec(memory_space=pl.ANY),
         out_shape=jax.ShapeDtypeStruct((rows, width), jnp.bfloat16),
-        compiler_params=pltpu.CompilerParams(vmem_limit_bytes=24 * 2**20),
+        scratch_shapes=[
+            pltpu.VMEM(values.shape, values.dtype),
+            pltpu.VMEM(query.shape, query.dtype),
+            pltpu.VMEM((steps, query.shape[2], cells), jnp.float32),
+            pltpu.VMEM((rows, width), jnp.bfloat16),
+            pltpu.SemaphoreType.DMA((KVH, 3)),
+        ],
+        compiler_params=pltpu.CompilerParams(vmem_limit_bytes=60 * 2**20),
         name="attend",
-    )(routed, returned, keys, values, scores)
+    )(routed, returned, keys, lens, values, query)
 
 
 def on_device(hidden, adapter_id, adapter_slot, cache_len, base_q, kv_cache, a_maps, b_maps):
@@ -238,11 +282,12 @@
     packed, routed = pack(hidden, adapter_id, adapter_slot, owners, slot_count, held)
     packed = packed.reshape(owners, slot_count, packed.shape[1])
     arrived = lax.all_to_all(packed, "owner", split_axis=0, concat_axis=0, tiled=True)
-    keys, values, scores = prep(base_q, kv_cache, cache_len)
-    change = adapt(arrived.reshape(bins, arrived.shape[2]), a_maps, b_maps)
+    laid = prep(base_q, kv_cache)
+    change = adapt(arrived.reshape(bins, arrived.shape[2]), a_maps, b_maps, laid[0])
     change = change.reshape(owners, slot_count, change.shape[1])
     returned = lax.all_to_all(change, "owner", split_axis=0, concat_axis=0, tiled=True)
-    return attend(routed, returned.reshape(bins, returned.shape[2]), keys, values, scores)
+    returned = returned.reshape(bins, returned.shape[2])
+    return attend(routed, returned, cache_len, laid, kv_cache.shape[2])
 
 
 def solution(mesh):

time: 101 us -> 105 us (1.040)
  blocking collectives: 58.1 us -> 0 us
  waiting for transfers between devices: 11.6 us -> 55.3 us
  starting transfers between devices: 3.79 us -> 19 us
  local copies, waits for them, and re-layouts: 9.5 us -> 12.1 us
    all_to_all x1 -> x0, blocking collectives: 58.1 us -> none  [on_device(): lax.all_to_all(packed, 'owner', split_axis=0, concat_axis=0, tiled=True)]
    all_to_all x0 -> x1, waiting for transfers between devices: none -> 33.2 us  [on_device(): lax.all_to_all(packed, 'owner', split_axis=0, concat_axis=0, tiled=True)]
    all_to_all x1, waiting for transfers between devices: 11.6 us -> 22.1 us  [on_device(): lax.all_to_all(change, 'owner', split_axis=0, concat_axis=0, tiled=True)]
    all_to_all x1, starting transfers between devices: 3.79 us -> 11.5 us  [on_device(): lax.all_to_all(change, 'owner', split_axis=0, concat_axis=0, tiled=True)]
    all_to_all x0 -> x1, starting transfers between devices: none -> 7.5 us  [on_device(): lax.all_to_all(packed, 'owner', split_axis=0, concat_axis=0, tiled=True)]
    unnamed x20, local copies, waits for them, and re-layouts: 9.24 us -> 11.2 us
  transfers between devices with their start and end apart: 1 -> 2, of which waited for: 1 -> 2; matrix products, arithmetic and copies ran while one was open for 0% -> 1% of each run, Pallas kernels for 5% -> 2%
where the time goes in v9:
time: 105 us; the launch traced here: 103 us
  waiting for transfers between devices  55.3 us (53%)
  starting transfers between devices  19 us (18%)
  Pallas kernels  16.6 us (16%)
  local copies, waits for them, and re-layouts  12.1 us (12%)
    all_to_all x1, waiting for transfers between devices, on_device(): lax.all_to_all(packed, 'owner', split_axis=0, concat_axis=0, tiled=True)  33.2 us
    all_to_all x1, waiting for transfers between devices, on_device(): lax.all_to_all(change, 'owner', split_axis=0, concat_axis=0, tiled=True)  22.1 us
    all_to_all x1, starting transfers between devices, on_device(): lax.all_to_all(change, 'owner', split_axis=0, concat_axis=0, tiled=True)  11.5 us
    unnamed x20, local copies, waits for them, and re-layouts  11.2 us
    pallas_call x1, Pallas kernels, attend(): pl.pallas_call(functools.partial(attend_kernel, width // (KVH * HEAD), co...  7.62 us
    all_to_all x1, starting transfers between devices, on_device(): lax.all_to_all(packed, 'owner', split_axis=0, concat_axis=0, tiled=True)  7.5 us
    pallas_call x1, Pallas kernels, pack(): pl.pallas_call(functools.partial(pack_kernel, owners, slot_count, held),...  4.36 us
    pallas_call x1, Pallas kernels, prep(): pl.pallas_call(functools.partial(prep_kernel, group), grid=(steps,), in_s...  2.56 us
  transfers between devices with their start and end apart: 2, of which 2 were waited for; matrix products, arithmetic and copies ran while one was open for 1% of the time, Pallas kernels for 2%

profile of v9, /device:TPU:0, one launch (start us, length us, event | category | flops | bytes accessed | tf_op | source)
XLA Modules:
  0.0 103.0 jit_solution(10378979273660562154)
XLA Ops:
  0.0 4.4 %pack.1 = (bf16[128,8320]{1,0:T(8,128)(2,1)}, bf16[128,128]{1,0:T(8,128)(2,1)}) custom-call(s32[32]{0:T(128)} %slots_ref.1, s32[1,128]{1,0:T(1,128)} %bitcast.8, bf16[128,8192]{1,0:T(8,128)(2,1)} %hidden_ref.1), custom_call_target="tpu_custom_call" | custom-call | tf_op jit(solution)/shard_map/pack/pallas_call | solution.py:77
  4.4 0.0 copy-start.5
  4.4 7.5 %all-to-all-start = ((bf16[16,8,8320]{2,1,0:T(8,128)(2,1)}), bf16[16,8,8320]{2,1,0:T(8,128)(2,1)S(1)}, u32[]{:S(2)}, u32[]{:S(2)}) async-start(bf16[16,8,8320]{2,1,0:T(8,128)(2,1)} %bitcast.7), calls=%async_computation | async-start | bytes 4259840 | tf_op jit(solution)/shard_map/all_to_all | solution.py:284
  11.9 0.0 copy-done.5
  11.9 0.0 copy-start.2
  11.9 2.2 %copy-done.2 = bf16[128,2,16,512]{3,2,1,0:T(8,128)(2,1)S(1)} copy-done((bf16[128,2,16,512]{3,2,1,0:T(8,128)(2,1)S(1)}, bf16[128,2,16,512]{3,2,1,0:T(8,128)(2,1)}, u32[]{:S(2)}) %copy-start.2) | copy-done | bytes 4194328
  14.1 2.6 %prep.1 = (bf16[4,128,2048]{2,1,0:T(8,128)(2,1)S(1)}, bf16[4,2048,128]{2,1,0:T(8,128)(2,1)S(1)}, bf16[4,16,64,128]{3,2,1,0:T(8,128)(2,1)S(1)}) custom-call(bf16[128,4096]{1,0:T(8,128)(2,1)S(1)} %copy-done.5, bf16[128,2,16,512]{3,2,1,0:T(8,128)(2,1)S(1)} %copy-done.2), custom_call_target="tpu_custom_call" | custom-call | tf_op jit(solution)/shard_map/prep/pallas_call | solution.py:154
  16.7 0.0 copy-start
  16.7 1.3 %copy-done = bf16[4,128,2048]{2,1,0:T(8,128)(2,1)} copy-done((bf16[4,128,2048]{2,1,0:T(8,128)(2,1)}, bf16[4,128,2048]{2,1,0:T(8,128)(2,1)S(1)}, u32[]{:S(2)}) %copy-start) | copy-done | bytes 2097176
  18.0 0.0 copy-start.4
  18.0 1.3 %copy-done.4 = bf16[4,2048,128]{2,1,0:T(8,128)(2,1)} copy-done((bf16[4,2048,128]{2,1,0:T(8,128)(2,1)}, bf16[4,2048,128]{2,1,0:T(8,128)(2,1)S(1)}, u32[]{:S(2)}) %copy-start.4) | copy-done | bytes 2097176
  19.3 0.0 copy-start.6
  19.3 1.0 copy-done.6
  20.3 33.2 %all-to-all-done = bf16[16,8,8320]{2,1,0:T(8,128)(2,1)S(1)} async-done(((bf16[16,8,8320]{2,1,0:T(8,128)(2,1)}), bf16[16,8,8320]{2,1,0:T(8,128)(2,1)S(1)}, u32[]{:S(2)}, u32[]{:S(2)}) %all-to-all-start) | async-done | bytes 2129952 | tf_op jit(solution)/shard_map/all_to_all | solution.py:284
  53.6 0.0 copy-start.1
  53.6 1.6 %copy-done.1 = bf16[4,128,2048]{2,1,0:T(8,128)(2,1)S(1)} copy-done((bf16[4,128,2048]{2,1,0:T(8,128)(2,1)S(1)}, bf16[4,128,2048]{2,1,0:T(8,128)(2,1)}, u32[]{:S(2)}) %copy-start.1) | copy-done | bytes 2097176
  55.2 0.0 copy-start.3
  55.2 1.6 %copy-done.3 = bf16[8192,128]{1,0:T(8,128)(2,1)S(1)} copy-done((bf16[8192,128]{1,0:T(8,128)(2,1)S(1)}, bf16[8192,128]{1,0:T(8,128)(2,1)}, u32[]{:S(2)}) %copy-start.3) | copy-done | bytes 2097176
  56.8 0.0 copy-start.7
  56.8 1.2 %copy-done.7 = bf16[128,4096]{1,0:T(8,128)(2,1)S(1)} copy-done((bf16[128,4096]{1,0:T(8,128)(2,1)S(1)}, bf16[128,4096]{1,0:T(8,128)(2,1)}, u32[]{:S(2)}) %copy-start.7) | copy-done | bytes 1048600
  58.0 2.0 %adapt.1 = bf16[128,4096]{1,0:T(8,128)(2,1)} custom-call(bf16[128,8320]{1,0:T(8,128)(2,1)S(1)} %bitcast.5, bf16[8192,128]{1,0:T(8,128)(2,1)S(1)} %copy-done.3, bf16[128,4096]{1,0:T(8,128)(2,1)S(1)} %copy-done.7, bf16[4,128,2048]{2,1,0:T(8,128)(2,1)S(1)} %copy-done.1), custom_call_target="tpu_custom_call" | custom-call | tf_op jit(solution)/shard_map/adapt/pallas_call | solution.py:121
  60.0 0.0 copy-start.9
  60.0 11.5 %all-to-all-start.1 = ((bf16[16,8,4096]{2,1,0:T(8,128)(2,1)}), bf16[16,8,4096]{2,1,0:T(8,128)(2,1)S(1)}, u32[]{:S(2)}, u32[]{:S(2)}) async-start(bf16[16,8,4096]{2,1,0:T(8,128)(2,1)} %bitcast.3), calls=%async_computation.1 | async-start | bytes 2097152 | tf_op jit(solution)/shard_map/all_to_all | solution.py:288
  71.5 0.0 copy-done.9
  71.5 0.1 broadcast_in_dim.7
  71.6 0.1 broadcast_in_dim.8
  71.7 0.7 broadcast_in_dim.9.lens_ref
  72.4 22.1 %all-to-all-done.1 = bf16[16,8,4096]{2,1,0:T(8,128)(2,1)S(1)} async-done(((bf16[16,8,4096]{2,1,0:T(8,128)(2,1)}), bf16[16,8,4096]{2,1,0:T(8,128)(2,1)S(1)}, u32[]{:S(2)}, u32[]{:S(2)}) %all-to-all-start.1) | async-done | bytes 1048608 | tf_op jit(solution)/shard_map/all_to_all | solution.py:288
  94.4 0.0 copy-start.8
  94.5 1.0 copy-done.8
  95.4 7.6 %attend.1 = bf16[128,4096]{1,0:T(8,128)(2,1)} custom-call(bf16[128,128]{1,0:T(8,128)(2,1)} %get-tuple-element.10.routed_ref, bf16[128,4096]{1,0:T(8,128)(2,1)} %bitcast.6, bf16[4,128,2048]{2,1,0:T(8,128)(2,1)} %copy-done, s32[16,1,128]{2,1,0:T(1,128)} %broadcast_in_dim.9.lens_ref, bf16[4,2048,128]{2,1,0:T(8,128)(2,1)} %copy-done.4, ...), custom_call_target="tpu_custom_call" | custom-call | tf_op jit(solution)/shard_map/attend/pallas_call | solution.py:258
Async XLA Ops:
  4.4 7.5 %copy-start.5 = (bf16[128,4096]{1,0:T(8,128)(2,1)S(1)}, bf16[128,4096]{1,0:T(8,128)(2,1)}, u32[]{:S(2)}) copy-start(bf16[128,4096]{1,0:T(8,128)(2,1)} %base_ref.1) | copy-start | bytes 3145732
  4.4 49.2 %all-to-all-start = ((bf16[16,8,8320]{2,1,0:T(8,128)(2,1)}), bf16[16,8,8320]{2,1,0:T(8,128)(2,1)S(1)}, u32[]{:S(2)}, u32[]{:S(2)}) async-start(bf16[16,8,8320]{2,1,0:T(8,128)(2,1)} %bitcast.7), calls=%async_computation | async-start | bytes 4259840 | tf_op jit(solution)/shard_map/all_to_all | solution.py:284
  11.9 2.2 %copy-start.2 = (bf16[128,2,16,512]{3,2,1,0:T(8,128)(2,1)S(1)}, bf16[128,2,16,512]{3,2,1,0:T(8,128)(2,1)}, u32[]{:S(2)}) copy-start(bf16[128,2,16,512]{3,2,1,0:T(8,128)(2,1)} %kv_ref.1) | copy-start | bytes 12582916
  16.7 1.3 %copy-start = (bf16[4,128,2048]{2,1,0:T(8,128)(2,1)}, bf16[4,128,2048]{2,1,0:T(8,128)(2,1)S(1)}, u32[]{:S(2)}) copy-start(bf16[4,128,2048]{2,1,0:T(8,128)(2,1)S(1)} %get-tuple-element.12._.keys_ref) | copy-start | bytes 6291460
  18.0 1.4 %copy-start.4 = (bf16[4,2048,128]{2,1,0:T(8,128)(2,1)}, bf16[4,2048,128]{2,1,0:T(8,128)(2,1)S(1)}, u32[]{:S(2)}) copy-start(bf16[4,2048,128]{2,1,0:T(8,128)(2,1)S(1)} %get-tuple-element.13.values_hbm) | copy-start | bytes 6291460
  19.3 1.0 copy-start.6
  53.6 1.6 %copy-start.1 = (bf16[4,128,2048]{2,1,0:T(8,128)(2,1)S(1)}, bf16[4,128,2048]{2,1,0:T(8,128)(2,1)}, u32[]{:S(2)}) copy-start(bf16[4,128,2048]{2,1,0:T(8,128)(2,1)} %copy-done) | copy-start | bytes 6291460
  55.2 1.6 %copy-start.3 = (bf16[8192,128]{1,0:T(8,128)(2,1)S(1)}, bf16[8192,128]{1,0:T(8,128)(2,1)}, u32[]{:S(2)}) copy-start(bf16[8192,128]{1,0:T(8,128)(2,1)} %a_ref.1) | copy-start | bytes 6291460
  56.8 1.2 %copy-start.7 = (bf16[128,4096]{1,0:T(8,128)(2,1)S(1)}, bf16[128,4096]{1,0:T(8,128)(2,1)}, u32[]{:S(2)}) copy-start(bf16[128,4096]{1,0:T(8,128)(2,1)} %b_ref.1) | copy-start | bytes 3145732
  60.0 11.5 %copy-start.9 = (s32[128]{0:T(128)S(1)}, s32[128]{0:T(128)}, u32[]{:S(2)}) copy-start(s32[128]{0:T(128)} %param.11) | copy-start | bytes 1540
  60.0 34.4 %all-to-all-start.1 = ((bf16[16,8,4096]{2,1,0:T(8,128)(2,1)}), bf16[16,8,4096]{2,1,0:T(8,128)(2,1)S(1)}, u32[]{:S(2)}, u32[]{:S(2)}) async-start(bf16[16,8,4096]{2,1,0:T(8,128)(2,1)} %bitcast.3), calls=%async_computation.1 | async-start | bytes 2097152 | tf_op jit(solution)/shard_map/all_to_all | solution.py:288
  94.4 1.0 copy-start.8

commit v10 on v9

v10 whole, which is shorter than its diff:
```python
import functools

import jax
import jax.numpy as jnp
from jax import lax
from jax.experimental import pallas as pl
from jax.experimental.pallas import tpu as pltpu
from jax.sharding import PartitionSpec as P

HEAD = 128
KVH = 4
RANK = 64
LANES = 128
SCALE = 2.0
ROWS_STEP = 8
COLUMNS_STEP = 1024
GRANT = 48 * 2**20
TALL_BYTES = 17 * 2**20


def routing(owners, slot_count, held, slots, ids):
    rows = ids.shape[1]
    named = lax.broadcasted_iota(jnp.int32, (slots.shape[1], rows), 0) == ids
    slot = jnp.dot(
        slots.astype(jnp.float32).astype(jnp.bfloat16),
        named.astype(jnp.bfloat16),
        preferred_element_type=jnp.float32,
    ).astype(jnp.int32)
    owner = lax.div(slot, held)
    local = slot - owner * held
    hits = owner == lax.broadcasted_iota(jnp.int32, (owners, rows), 0)
    earlier = lax.broadcasted_iota(jnp.int32, (rows, rows), 0) < lax.broadcasted_iota(
        jnp.int32, (rows, rows), 1
    )
    before = jnp.dot(
        hits.astype(jnp.bfloat16), earlier.astype(jnp.bfloat16), preferred_element_type=jnp.float32
    )
    place = jnp.sum(jnp.where(hits, before, 0.0), axis=0, keepdims=True).astype(jnp.int32)
    bins = owner * slot_count + place
    routed = bins == lax.broadcasted_iota(jnp.int32, (owners * slot_count, rows), 0)
    label = jnp.sum(jnp.where(routed, local.astype(jnp.float32), 0.0), axis=1, keepdims=True)
    return routed.astype(jnp.bfloat16), label


def pack_kernel(owners, slot_count, held, slots_hbm, ids_hbm, hidden_hbm, packed_hbm, routed_hbm, *scratch):
    slots_ref, ids_ref, rows_ref, bins_ref, routed_ref, small_sems, sems, out_sems = scratch
    width = rows_ref.shape[1]
    spans = [(at, min(COLUMNS_STEP, width - at)) for at in range(0, width, COLUMNS_STEP)]
    small = [
        pltpu.make_async_copy(slots_hbm, slots_ref, small_sems.at[0]),
        pltpu.make_async_copy(ids_hbm, ids_ref, small_sems.at[1]),
    ]
    loads = [
        pltpu.make_async_copy(
            hidden_hbm.at[:, pl.ds(at, size)], rows_ref.at[:, pl.ds(at, size)], sems.at[i]
        )
        for i, (at, size) in enumerate(spans)
    ]
    stores = [
        pltpu.make_async_copy(
            bins_ref.at[:, pl.ds(at, size)], packed_hbm.at[:, pl.ds(at, size)], out_sems.at[i]
        )
        for i, (at, size) in enumerate([*spans, (width, LANES)])
    ]
    routed_store = pltpu.make_async_copy(routed_ref, routed_hbm, small_sems.at[2])
    for copy in [*small, *loads]:
        copy.start()
    for copy in small:
        copy.wait()
    routed, label = routing(owners, slot_count, held, slots_ref[...], ids_ref[...])
    for load, store, (at, size) in zip(loads, stores, spans):
        load.wait()
        bins_ref[:, at : at + size] = jnp.dot(
            routed, rows_ref[:, at : at + size], preferred_element_type=jnp.float32
        ).astype(bins_ref.dtype)
        store.start()
        if at == 0:
            bins_ref[:, width:] = jnp.broadcast_to(label, (label.shape[0], LANES)).astype(
                bins_ref.dtype
            )
            stores[-1].start()
            routed_ref[...] = jnp.transpose(routed.astype(jnp.float32)).astype(routed_ref.dtype)
            routed_store.start()
    for store in stores:
        store.wait()
    routed_store.wait()


def pack(hidden, adapter_id, adapter_slot, owners, slot_count, held):
    rows, width = hidden.shape
    bins = owners * slot_count
    steps = pl.cdiv(width, COLUMNS_STEP)
    slots = adapter_slot.reshape(1, -1)
    return pl.pallas_call(
        functools.partial(pack_kernel, owners, slot_count, held),
        in_specs=[pl.BlockSpec(memory_space=pl.ANY)] * 3,
        out_specs=[pl.BlockSpec(memory_space=pl.ANY)] * 2,
        out_shape=[
            jax.ShapeDtypeStruct((bins, width + LANES), hidden.dtype),
            jax.ShapeDtypeStruct((rows, bins), jnp.bfloat16),
        ],
        scratch_shapes=[
            pltpu.VMEM(slots.shape, jnp.int32),
            pltpu.VMEM((1, rows), jnp.int32),
            pltpu.VMEM((rows, width), hidden.dtype),
            pltpu.VMEM((bins, width + LANES), hidden.dtype),
            pltpu.VMEM((rows, bins), jnp.bfloat16),
            pltpu.SemaphoreType.DMA((3,)),
            pltpu.SemaphoreType.DMA((steps,)),
            pltpu.SemaphoreType.DMA((steps + 1,)),
        ],
        compiler_params=pltpu.CompilerParams(vmem_limit_bytes=56 * 2**20),
        name="pack",
    )(slots, adapter_id.reshape(1, rows), hidden)


def adapt_kernel(arrived_ref, a_ref, b_ref, _, change_ref):
    width = a_ref.shape[0]
    low = jnp.zeros((arrived_ref.shape[0], a_ref.shape[1]), jnp.float32)
    for at in range(0, width, COLUMNS_STEP):
        low += jnp.dot(
            arrived_ref[:, at : at + COLUMNS_STEP],
            a_ref[at : at + COLUMNS_STEP, :],
            preferred_element_type=jnp.float32,
        )
    label = arrived_ref[:, width:].astype(jnp.float32)[:, :1].astype(jnp.int32)
    column = lax.broadcasted_iota(jnp.int32, low.shape, 1) // RANK
    low = jnp.where(column == label, low, 0.0).astype(jnp.bfloat16)
    out_width = b_ref.shape[1]
    piece = min(1024, out_width)
    for at in range(0, out_width, piece):
        change_ref[:, at : at + piece] = (
            SCALE * jnp.dot(low, b_ref[:, at : at + piece], preferred_element_type=jnp.float32)
        ).astype(change_ref.dtype)


def adapt(arrived, a_maps, b_maps, after):
    return pl.pallas_call(
        adapt_kernel,
        in_specs=[pl.BlockSpec(memory_space=pltpu.VMEM)] * 3 + [pl.BlockSpec(memory_space=pl.ANY)],
        out_specs=pl.BlockSpec(memory_space=pltpu.VMEM),
        out_shape=jax.ShapeDtypeStruct((arrived.shape[0], b_maps.shape[1]), jnp.bfloat16),
        compiler_params=pltpu.CompilerParams(vmem_limit_bytes=GRANT),
        name="adapt",
    )(arrived, a_maps, b_maps, after)


def tall(rows, group):
    return jnp.concatenate([rows[:, g * HEAD : (g + 1) * HEAD] for g in range(group)], axis=0)


def prep_kernel(group, base_ref, kv_ref, keys_ref, rest_ref):
    step, context = kv_ref.shape[0], kv_ref.shape[2]
    cells = step * context
    for k in range(KVH):
        head = slice(k * HEAD, (k + 1) * HEAD)
        keys = kv_ref[:, 0, :, head].astype(jnp.float32).reshape(cells, HEAD)
        keys_ref[k] = jnp.transpose(keys).astype(keys_ref.dtype)
        rest_ref[k, :cells] = kv_ref[:, 1, :, head].reshape(cells, HEAD)
        base = base_ref[:, k * group * HEAD : (k + 1) * group * HEAD].astype(jnp.float32)
        rest_ref[k, cells:] = tall(base, group).astype(rest_ref.dtype)


def prep(base_q, kv_cache):
    rows, width = base_q.shape
    context = kv_cache.shape[2]
    group = width // (KVH * HEAD)
    step = ROWS_STEP
    steps = rows // step
    cells = step * context
    lines = cells + group * step
    length = pl.cdiv(max(TALL_BYTES // (2 * KVH * HEAD), steps * lines), lines) * lines
    return pl.pallas_call(
        functools.partial(prep_kernel, group),
        grid=(steps,),
        in_specs=[
            pl.BlockSpec((step, width), lambda i: (i, 0)),
            pl.BlockSpec((step, *kv_cache.shape[1:]), lambda i: (i, 0, 0, 0)),
        ],
        out_specs=[
            pl.BlockSpec((KVH, HEAD, cells), lambda i: (0, 0, i)),
            pl.BlockSpec((KVH, lines, HEAD), lambda i: (0, i, 0)),
        ],
        out_shape=[
            jax.ShapeDtypeStruct((KVH, HEAD, rows * context), jnp.bfloat16),
            jax.ShapeDtypeStruct((KVH, length, HEAD), jnp.bfloat16),
        ],
        compiler_params=pltpu.CompilerParams(vmem_limit_bytes=GRANT),
        name="prep",
    )(base_q, kv_cache)


def attend_kernel(
    group, context, routed_ref, returned_ref, keys_ref, lens_ref, rest_hbm, out_hbm, rest_ref, bias_ref, out_ref, sems
):
    step = ROWS_STEP
    steps, lines, cells = bias_ref.shape
    block = cells + lines
    span = group * HEAD
    factor = 1.0 / jnp.sqrt(jnp.float32(HEAD))
    loads = [
        pltpu.make_async_copy(
            rest_hbm.at[k, pl.ds(0, steps * block)], rest_ref.at[k], sems.at[k, 0]
        )
        for k in range(KVH)
    ]
    stores = [
        pltpu.make_async_copy(
            out_ref.at[:, pl.ds(k * span, span)], out_hbm.at[:, pl.ds(k * span, span)], sems.at[k, 1]
        )
        for k in range(KVH)
    ]
    for load in loads:
        load.start()
    lane = lax.broadcasted_iota(jnp.int32, (lines, cells), 1)
    line = lax.broadcasted_iota(jnp.int32, (lines, cells), 0)
    own = lax.div(lane, context) == lax.rem(line, step)
    position = lax.rem(lane, context)
    for i in range(steps):
        bias_ref[i] = jnp.where(own & (position < lens_ref[i]), 0.0, -jnp.inf)
    for k in range(KVH):
        delta = jnp.dot(
            routed_ref[...],
            returned_ref[:, k * span : (k + 1) * span],
            preferred_element_type=jnp.float32,
        )
        loads[k].wait()
        for i in range(steps):
            rows = slice(i * step, (i + 1) * step)
            keys = keys_ref[k, :, i * cells : (i + 1) * cells]
            values = rest_ref[k, i * block : i * block + cells, :]
            query = rest_ref[k, i * block + cells : (i + 1) * block, :]
            change = tall(delta[rows], group).astype(jnp.bfloat16)
            scores = jnp.dot(
                jnp.concatenate([query, change], axis=1),
                jnp.concatenate([keys, keys], axis=0),
                preferred_element_type=jnp.float32,
            )
            scores = scores * factor + bias_ref[i]
            expo = jnp.exp(scores - jnp.max(scores, axis=1, keepdims=True))
            probs = expo * (1.0 / jnp.sum(expo, axis=1, keepdims=True))
            out = jnp.dot(probs.astype(jnp.bfloat16), values, preferred_element_type=jnp.float32)
            for g in range(group):
                out_ref[rows, (k * group + g) * HEAD : (k * group + g + 1) * HEAD] = out[
                    g * step : (g + 1) * step
                ].astype(out_ref.dtype)
        stores[k].start()
    for store in stores:
        store.wait()


def attend(routed, returned, cache_len, keys, rest, context):
    rows, width = routed.shape[0], returned.shape[1]
    group = width // (KVH * HEAD)
    step = ROWS_STEP
    steps = rows // step
    cells = step * context
    lens = jnp.repeat(cache_len, context).reshape(steps, 1, cells)
    return pl.pallas_call(
        functools.partial(attend_kernel, group, context),
        in_specs=[pl.BlockSpec(memory_space=pltpu.VMEM)] * 4 + [pl.BlockSpec(memory_space=pl.ANY)],
        out_specs=pl.BlockSpec(memory_space=pl.ANY),
        out_shape=jax.ShapeDtypeStruct((rows, width), jnp.bfloat16),
        scratch_shapes=[
            pltpu.VMEM((KVH, steps * (cells + group * step), HEAD), rest.dtype),
            pltpu.VMEM((steps, group * step, cells), jnp.float32),
            pltpu.VMEM((rows, width), jnp.bfloat16),
            pltpu.SemaphoreType.DMA((KVH, 2)),
        ],
        compiler_params=pltpu.CompilerParams(vmem_limit_bytes=GRANT),
        name="attend",
    )(routed, returned, keys, lens, rest)


def on_device(hidden, adapter_id, adapter_slot, cache_len, base_q, kv_cache, a_maps, b_maps):
    owners = lax.axis_size("owner")
    rows = hidden.shape[0]
    held = a_maps.shape[1] // RANK
    slot_count = max(2, 2 * ((rows + 2 * owners - 1) // (2 * owners)))
    bins = owners * slot_count
    packed, routed = pack(hidden, adapter_id, adapter_slot, owners, slot_count, held)
    packed = packed.reshape(owners, slot_count, packed.shape[1])
    arrived = lax.all_to_all(packed, "owner", split_axis=0, concat_axis=0, tiled=True)
    keys, rest = prep(base_q, kv_cache)
    change = adapt(arrived.reshape(bins, arrived.shape[2]), a_maps, b_maps, rest)
    change = change.reshape(owners, slot_count, change.shape[1])
    returned = lax.all_to_all(change, "owner", split_axis=0, concat_axis=0, tiled=True)
    returned = returned.reshape(bins, returned.shape[2])
    return attend(routed, returned, cache_len, keys, rest, kv_cache.shape[2])


def solution(mesh):
    return jax.shard_map(
        on_device,
        mesh=mesh,
        in_specs=(
            P(("groups", "owner"), None),
            P(("groups", "owner")),
            P("groups"),
            P(("groups", "owner")),
            P(("groups", "owner"), None),
            P(("groups", "owner"), None, None, None),
            P(None, "owner"),
            P("owner", None),
        ),
        out_specs=P(("groups", "owner"), None),
        check_vma=False,
    )
```

time: 105 us -> 100 us (0.952)
  local copies, waits for them, and re-layouts: 12.1 us -> 2.86 us
  Pallas kernels: 16.6 us -> 24.6 us
  waiting for transfers between devices: 55.3 us -> 52 us
    unnamed x20 -> x14, local copies, waits for them, and re-layouts: 11.2 us -> 2.6 us
    pallas_call x1, Pallas kernels: 2.56 us -> 11 us  [prep(): pl.pallas_call(functools.partial(prep_kernel, group), grid=(steps,), in_s...]
    all_to_all x1, waiting for transfers between devices: 33.2 us -> 29.3 us  [on_device(): lax.all_to_all(packed, 'owner', split_axis=0, concat_axis=0, tiled=True)]
    pallas_call x1, Pallas kernels: 7.62 us -> 5.67 us  [attend(): pl.pallas_call(functools.partial(attend_kernel, group, context), in_specs...]
    pallas_call x1, Pallas kernels: 2.04 us -> 3.67 us  [adapt(): pl.pallas_call(adapt_kernel, in_specs=[pl.BlockSpec(memory_space=pltpu.VM...]
  transfers between devices with their start and end apart: 2 -> 2, of which waited for: 2 -> 2; matrix products, arithmetic and copies ran while one was open for 1% -> 0% of each run, Pallas kernels for 2% -> 11%
where the time goes in v10:
time: 100 us; the launch traced here: 98.6 us
  waiting for transfers between devices  52 us (52%)
  Pallas kernels  24.6 us (25%)
  starting transfers between devices  19 us (19%)
  local copies, waits for them, and re-layouts  2.86 us (3%)
    all_to_all x1, waiting for transfers between devices, on_device(): lax.all_to_all(packed, 'owner', split_axis=0, concat_axis=0, tiled=True)  29.3 us
    all_to_all x1, waiting for transfers between devices, on_device(): lax.all_to_all(change, 'owner', split_axis=0, concat_axis=0, tiled=True)  22.7 us
    all_to_all x1, starting transfers between devices, on_device(): lax.all_to_all(change, 'owner', split_axis=0, concat_axis=0, tiled=True)  11.5 us
    pallas_call x1, Pallas kernels, prep(): pl.pallas_call(functools.partial(prep_kernel, group), grid=(steps,), in_s...  11 us
    all_to_all x1, starting transfers between devices, on_device(): lax.all_to_all(packed, 'owner', split_axis=0, concat_axis=0, tiled=True)  7.56 us
    pallas_call x1, Pallas kernels, attend(): pl.pallas_call(functools.partial(attend_kernel, group, context), in_specs...  5.67 us
    pallas_call x1, Pallas kernels, pack(): pl.pallas_call(functools.partial(pack_kernel, owners, slot_count, held),...  4.23 us
    pallas_call x1, Pallas kernels, adapt(): pl.pallas_call(adapt_kernel, in_specs=[pl.BlockSpec(memory_space=pltpu.VM...  3.67 us
  transfers between devices with their start and end apart: 2, of which 2 were waited for; matrix products, arithmetic and copies ran while one was open for 0% of the time, Pallas kernels for 11%

profile of v10, /device:TPU:0, one launch (start us, length us, event | category | flops | bytes accessed | tf_op | source)
XLA Modules:
  0.0 98.6 jit_solution(1382450961816996267)
XLA Ops:
  0.0 4.2 %pack.1 = (bf16[128,8320]{1,0:T(8,128)(2,1)}, bf16[128,128]{1,0:T(8,128)(2,1)}) custom-call(s32[1,32]{1,0:T(1,128)} %bitcast.8, s32[1,128]{1,0:T(1,128)} %bitcast.9, bf16[128,8192]{1,0:T(8,128)(2,1)} %hidden_hbm.1), custom_call_target="tpu_custom_call" | custom-call | tf_op jit(solution)/shard_map/pack/pallas_call | solution.py:94
  4.2 0.0 copy-start.3
  4.3 7.6 %all-to-all-start = ((bf16[16,8,8320]{2,1,0:T(8,128)(2,1)}), bf16[16,8,8320]{2,1,0:T(8,128)(2,1)}, u32[]{:S(2)}, u32[]{:S(2)}) async-start(bf16[16,8,8320]{2,1,0:T(8,128)(2,1)} %bitcast.7), calls=%async_computation | async-start | bytes 4259840 | tf_op jit(solution)/shard_map/all_to_all | solution.py:283
  11.8 0.0 copy-done.3
  11.8 0.0 copy-start
  11.8 11.0 %prep.1 = (bf16[4,128,2048]{2,1,0:T(8,128)(2,1)S(1)}, bf16[4,17472,128]{2,1,0:T(8,128)(2,1)}) custom-call(bf16[128,4096]{1,0:T(8,128)(2,1)S(1)} %copy-done.3, bf16[128,2,16,512]{3,2,1,0:T(8,128)(2,1)} %kv_ref.1), custom_call_target="tpu_custom_call" | custom-call | tf_op jit(solution)/shard_map/prep/pallas_call | solution.py:173
  22.9 0.0 copy-start.1
  22.9 1.3 %copy-done.1 = bf16[4,128,2048]{2,1,0:T(8,128)(2,1)} copy-done((bf16[4,128,2048]{2,1,0:T(8,128)(2,1)}, bf16[4,128,2048]{2,1,0:T(8,128)(2,1)S(1)}, u32[]{:S(2)}) %copy-start.1) | copy-done | bytes 2097176
  24.2 29.3 %all-to-all-done = bf16[16,8,8320]{2,1,0:T(8,128)(2,1)} async-done(((bf16[16,8,8320]{2,1,0:T(8,128)(2,1)}), bf16[16,8,8320]{2,1,0:T(8,128)(2,1)}, u32[]{:S(2)}, u32[]{:S(2)}) %all-to-all-start) | async-done | bytes 2129952 | tf_op jit(solution)/shard_map/all_to_all | solution.py:283
  53.6 0.0 copy-done
  53.6 0.0 copy-start.4
  53.6 1.2 %copy-done.4 = bf16[128,4096]{1,0:T(8,128)(2,1)S(1)} copy-done((bf16[128,4096]{1,0:T(8,128)(2,1)S(1)}, bf16[128,4096]{1,0:T(8,128)(2,1)}, u32[]{:S(2)}) %copy-start.4) | copy-done | bytes 1048600
  54.8 0.0 copy-start.6
  54.8 3.7 %adapt.1 = bf16[128,4096]{1,0:T(8,128)(2,1)} custom-call(bf16[128,8320]{1,0:T(8,128)(2,1)} %bitcast.3.arrived_ref, bf16[8192,128]{1,0:T(8,128)(2,1)S(1)} %copy-done, bf16[128,4096]{1,0:T(8,128)(2,1)S(1)} %copy-done.4, bf16[4,17472,128]{2,1,0:T(8,128)(2,1)} %get-tuple-element.11._.rest_hbm), custom_call_target="tpu_custom_call" | custom-call | tf_op jit(solution)/shard_map/adapt/pallas_call | solution.py:138
  58.5 0.0 copy-start.2
  58.5 0.0 copy-start.5
  58.5 11.5 %all-to-all-start.1 = ((bf16[16,8,4096]{2,1,0:T(8,128)(2,1)}), bf16[16,8,4096]{2,1,0:T(8,128)(2,1)S(1)}, u32[]{:S(2)}, u32[]{:S(2)}) async-start(bf16[16,8,4096]{2,1,0:T(8,128)(2,1)} %bitcast.4), calls=%async_computation.1 | async-start | bytes 2097152 | tf_op jit(solution)/shard_map/all_to_all | solution.py:287
  69.9 0.0 copy-done.6
  69.9 0.1 broadcast_in_dim.7
  70.0 0.1 broadcast_in_dim.8
  70.1 0.1 broadcast_in_dim.9.lens_ref
  70.2 22.7 %all-to-all-done.1 = bf16[16,8,4096]{2,1,0:T(8,128)(2,1)S(1)} async-done(((bf16[16,8,4096]{2,1,0:T(8,128)(2,1)}), bf16[16,8,4096]{2,1,0:T(8,128)(2,1)S(1)}, u32[]{:S(2)}, u32[]{:S(2)}) %all-to-all-start.1) | async-done | bytes 1048608 | tf_op jit(solution)/shard_map/all_to_all | solution.py:287
  92.9 0.0 copy-done.2
  92.9 0.0 copy-done.5
  92.9 5.7 %attend.1 = bf16[128,4096]{1,0:T(8,128)(2,1)} custom-call(bf16[128,128]{1,0:T(8,128)(2,1)S(1)} %copy-done.5, bf16[128,4096]{1,0:T(8,128)(2,1)S(1)} %bitcast.6, bf16[4,128,2048]{2,1,0:T(8,128)(2,1)S(1)} %copy-done.2, s32[16,1,128]{2,1,0:T(1,128)S(1)} %broadcast_in_dim.9.lens_ref, bf16[4,17472,128]{2,1,0:T(8,128)(2,1)} %get-tuple-element.11._.rest_hbm), custom_call_target="tpu_custom_call" | custom-call | tf_op jit(solution)/shard_map/attend/pallas_call | solution.py:259
Async XLA Ops:
  4.2 7.6 %copy-start.3 = (bf16[128,4096]{1,0:T(8,128)(2,1)S(1)}, bf16[128,4096]{1,0:T(8,128)(2,1)}, u32[]{:S(2)}) copy-start(bf16[128,4096]{1,0:T(8,128)(2,1)} %base_ref.1) | copy-start | bytes 3145732
  4.3 49.3 %all-to-all-start = ((bf16[16,8,8320]{2,1,0:T(8,128)(2,1)}), bf16[16,8,8320]{2,1,0:T(8,128)(2,1)}, u32[]{:S(2)}, u32[]{:S(2)}) async-start(bf16[16,8,8320]{2,1,0:T(8,128)(2,1)} %bitcast.7), calls=%async_computation | async-start | bytes 4259840 | tf_op jit(solution)/shard_map/all_to_all | solution.py:283
  11.8 41.7 %copy-start = (bf16[8192,128]{1,0:T(8,128)(2,1)S(1)}, bf16[8192,128]{1,0:T(8,128)(2,1)}, u32[]{:S(2)}) copy-start(bf16[8192,128]{1,0:T(8,128)(2,1)} %a_ref.1) | copy-start | bytes 6291460
  22.9 1.3 %copy-start.1 = (bf16[4,128,2048]{2,1,0:T(8,128)(2,1)}, bf16[4,128,2048]{2,1,0:T(8,128)(2,1)S(1)}, u32[]{:S(2)}) copy-start(bf16[4,128,2048]{2,1,0:T(8,128)(2,1)S(1)} %get-tuple-element.12.keys_ref) | copy-start | bytes 6291460
  53.6 1.2 %copy-start.4 = (bf16[128,4096]{1,0:T(8,128)(2,1)S(1)}, bf16[128,4096]{1,0:T(8,128)(2,1)}, u32[]{:S(2)}) copy-start(bf16[128,4096]{1,0:T(8,128)(2,1)} %b_ref.1) | copy-start | bytes 3145732
  54.8 15.1 %copy-start.6 = (s32[128]{0:T(128)S(1)}, s32[128]{0:T(128)}, u32[]{:S(2)}) copy-start(s32[128]{0:T(128)} %param.11) | copy-start | bytes 1540
  58.5 34.4 %copy-start.2 = (bf16[4,128,2048]{2,1,0:T(8,128)(2,1)S(1)}, bf16[4,128,2048]{2,1,0:T(8,128)(2,1)}, u32[]{:S(2)}) copy-start(bf16[4,128,2048]{2,1,0:T(8,128)(2,1)} %copy-done.1) | copy-start | bytes 6291460
  58.5 34.4 %copy-start.5 = (bf16[128,128]{1,0:T(8,128)(2,1)S(1)}, bf16[128,128]{1,0:T(8,128)(2,1)}, u32[]{:S(2)}) copy-start(bf16[128,128]{1,0:T(8,128)(2,1)} %get-tuple-element.9.routed_ref) | copy-start | bytes 98308
  58.5 34.4 %all-to-all-start.1 = ((bf16[16,8,4096]{2,1,0:T(8,128)(2,1)}), bf16[16,8,4096]{2,1,0:T(8,128)(2,1)S(1)}, u32[]{:S(2)}, u32[]{:S(2)}) async-start(bf16[16,8,4096]{2,1,0:T(8,128)(2,1)} %bitcast.4), calls=%async_computation.1 | async-start | bytes 2097152 | tf_op jit(solution)/shard_map/all_to_all | solution.py:287

commit v11 on v7

--- a/solution.py
+++ b/solution.py
@@ -14,18 +14,21 @@
 SCALE = 2.0
 ROWS_STEP = 8
 COLUMNS_STEP = 2048
-FAR_GROUPS = 4
+FAR_GROUPS = 2
+GRANT = 48 * 2**20
+TALL_BYTES = 17 * 2**20
 
 
 def routing(pairs, owners, slot_count, held, slots_ref, ids_ref):
     ids = ids_ref[...]
     rows = ids.shape[1]
     half = owners // 2
-
-    def look(s, slot):
-        return jnp.where(ids == s, slots_ref[s], slot)
-
-    slot = lax.fori_loop(0, slots_ref.shape[0], look, jnp.zeros_like(ids), unroll=8)
+    named = lax.broadcasted_iota(jnp.int32, (slots_ref.shape[1], rows), 0) == ids
+    slot = jnp.dot(
+        slots_ref[...].astype(jnp.float32).astype(jnp.bfloat16),
+        named.astype(jnp.bfloat16),
+        preferred_element_type=jnp.float32,
+    ).astype(jnp.int32)
     owner = lax.div(slot, held)
     local = slot - owner * held
     hits = owner == lax.broadcasted_iota(jnp.int32, (owners, rows), 0)
@@ -84,7 +87,7 @@
     return pl.pallas_call(
         functools.partial(pack_kernel, pairs, owners, slot_count, held),
         in_specs=[
-            pl.BlockSpec(memory_space=pltpu.SMEM),
+            pl.BlockSpec(memory_space=pltpu.VMEM),
             pl.BlockSpec(memory_space=pltpu.VMEM),
             pl.BlockSpec(memory_space=pl.ANY),
             pl.BlockSpec(memory_space=pl.ANY),
@@ -98,7 +101,7 @@
         ],
         compiler_params=pltpu.CompilerParams(vmem_limit_bytes=56 * 2**20),
         name="pack_pairs" if pairs else "pack",
-    )(adapter_slot, adapter_id.reshape(1, rows), hidden, after)
+    )(adapter_slot.reshape(1, -1), adapter_id.reshape(1, rows), hidden, after)
 
 
 def stack(refs, at, size):
@@ -142,12 +145,7 @@
         + [pl.BlockSpec(memory_space=pl.ANY)],
         out_specs=[pl.BlockSpec(memory_space=pltpu.VMEM)] * count,
         out_shape=[jax.ShapeDtypeStruct((lines, b_maps.shape[1]), jnp.bfloat16)] * count,
-        compiler_params=pltpu.CompilerParams(vmem_limit_bytes=16 * 2**20),
-        cost_estimate=pl.CostEstimate(
-            flops=2 * count * lines * (a_maps.size + b_maps.size),
-            bytes_accessed=2 * (a_maps.size + b_maps.size),
-            transcendentals=0,
-        ),
+        compiler_params=pltpu.CompilerParams(vmem_limit_bytes=GRANT),
         name="adapt",
     )(*arrived, a_maps, b_maps, after)
 
@@ -156,126 +154,128 @@
     return jnp.concatenate([rows[:, g * HEAD : (g + 1) * HEAD] for g in range(group)], axis=0)
 
 
-def prep_kernel(group, context, base_ref, kv_ref, len_ref, _, keys_ref, values_ref, scores_ref):
-    step = ROWS_STEP
+def prep_kernel(group, base_ref, kv_ref, _, keys_ref, rest_ref):
+    step, context = kv_ref.shape[0], kv_ref.shape[2]
     cells = step * context
-    lane = lax.broadcasted_iota(jnp.int32, (group * step, cells), 1)
-    line = lax.broadcasted_iota(jnp.int32, (group * step, cells), 0)
-    live = (lane // context == lax.rem(line, step)) & (lax.rem(lane, context) < len_ref[...][0])
-    factor = 1.0 / jnp.sqrt(jnp.float32(HEAD))
     for k in range(KVH):
         head = slice(k * HEAD, (k + 1) * HEAD)
         keys = kv_ref[:, 0, :, head].astype(jnp.float32).reshape(cells, HEAD)
-        keys = jnp.transpose(keys).astype(keys_ref.dtype)
-        keys_ref[k] = keys
-        values_ref[k] = kv_ref[:, 1, :, head].reshape(cells, HEAD)
+        keys_ref[k] = jnp.transpose(keys).astype(keys_ref.dtype)
+        rest_ref[k, :cells] = kv_ref[:, 1, :, head].reshape(cells, HEAD)
         base = base_ref[:, k * group * HEAD : (k + 1) * group * HEAD].astype(jnp.float32)
-        scores = jnp.dot(
-            tall(base, group).astype(jnp.bfloat16), keys, preferred_element_type=jnp.float32
-        )
-        scores_ref[k, 0] = jnp.where(live, scores * factor, -jnp.inf)
-
-
-def prep(base_q, kv_cache, cache_len, after):
+        rest_ref[k, cells:] = tall(base, group).astype(rest_ref.dtype)
+
+
+def prep(base_q, kv_cache, after):
     rows, width = base_q.shape
     context = kv_cache.shape[2]
     group = width // (KVH * HEAD)
     step = ROWS_STEP
     steps = rows // step
     cells = step * context
-    lens = jnp.repeat(cache_len, context).reshape(steps, 1, cells)
+    lines = cells + group * step
+    length = pl.cdiv(max(TALL_BYTES // (2 * KVH * HEAD), steps * lines), lines) * lines
     return pl.pallas_call(
-        functools.partial(prep_kernel, group, context),
+        functools.partial(prep_kernel, group),
         grid=(steps,),
         in_specs=[
             pl.BlockSpec((step, width), lambda i: (i, 0)),
             pl.BlockSpec((step, *kv_cache.shape[1:]), lambda i: (i, 0, 0, 0)),
-            pl.BlockSpec((1, 1, cells), lambda i: (i, 0, 0)),
             pl.BlockSpec(memory_space=pl.ANY),
         ],
         out_specs=[
             pl.BlockSpec((KVH, HEAD, cells), lambda i: (0, 0, i)),
-            pl.BlockSpec((KVH, cells, HEAD), lambda i: (0, i, 0)),
-            pl.BlockSpec((KVH, 1, group * step, cells), lambda i: (0, i, 0, 0)),
+            pl.BlockSpec((KVH, lines, HEAD), lambda i: (0, i, 0)),
         ],
         out_shape=[
             jax.ShapeDtypeStruct((KVH, HEAD, rows * context), jnp.bfloat16),
-            jax.ShapeDtypeStruct((KVH, rows * context, HEAD), jnp.bfloat16),
-            jax.ShapeDtypeStruct((KVH, steps, group * step, cells), jnp.float32),
-        ],
-        compiler_params=pltpu.CompilerParams(vmem_limit_bytes=16 * 2**20),
-        cost_estimate=pl.CostEstimate(
-            flops=2 * rows * width * cells, bytes_accessed=16 * 2**20, transcendentals=0
-        ),
+            jax.ShapeDtypeStruct((KVH, length, HEAD), jnp.bfloat16),
+        ],
+        compiler_params=pltpu.CompilerParams(vmem_limit_bytes=GRANT),
         name="prep",
-    )(base_q, kv_cache, lens, after)
-
-
-def attend_kernel(group, count, *refs):
-    routed_refs, given_refs, out_ref = refs[:2], refs[2 : 5 + count], refs[5 + count]
-    *held_refs, sems, laid_sems = refs[6 + count :]
-    returned_refs, (keys_ref, values_ref, scores_ref) = held_refs[:count], held_refs[count:]
+    )(base_q, kv_cache, after)
+
+
+def attend_kernel(group, context, count, *refs):
+    routed_refs, returned_refs, refs = refs[:2], refs[2 : 2 + count], refs[2 + count :]
+    keys_ref, lens_ref, rest_hbm, out_hbm, rest_ref, bias_ref, out_ref, sems = refs
     step = ROWS_STEP
-    steps, _, cells = scores_ref.shape[1:]
+    steps, lines, cells = bias_ref.shape
+    block = cells + lines
     span = group * HEAD
     factor = 1.0 / jnp.sqrt(jnp.float32(HEAD))
-    copies = [
-        pltpu.make_async_copy(given_ref, held_ref, sems.at[i])
-        for i, (given_ref, held_ref) in enumerate(zip(given_refs[:count], returned_refs))
-    ]
-    laid_copies = [
-        [
-            pltpu.make_async_copy(given_ref.at[k], held_ref.at[k], laid_sems.at[k, i])
-            for i, (given_ref, held_ref) in enumerate(zip(given_refs[count:], held_refs[count:]))
-        ]
+    loads = [
+        pltpu.make_async_copy(
+            rest_hbm.at[k, pl.ds(0, steps * block)], rest_ref.at[k], sems.at[k, 0]
+        )
         for k in range(KVH)
     ]
-    for copy in sum(laid_copies, copies):
-        copy.start()
+    stores = [
+        pltpu.make_async_copy(
+            out_ref.at[:, pl.ds(k * span, span)], out_hbm.at[:, pl.ds(k * span, span)], sems.at[k, 1]
+        )
+        for k in range(KVH)
+    ]
+    for load in loads:
+        load.start()
+    lane = lax.broadcasted_iota(jnp.int32, (lines, cells), 1)
+    line = lax.broadcasted_iota(jnp.int32, (lines, cells), 0)
+    own = lax.div(lane, context) == lax.rem(line, step)
+    position = lax.rem(lane, context)
+    for i in range(steps):
+        bias_ref[i] = jnp.where(own & (position < lens_ref[i]), 0.0, -jnp.inf)
     routed = jnp.concatenate([ref[...].astype(jnp.float32) for ref in routed_refs], axis=0)
     routed = jnp.transpose(routed).astype(jnp.bfloat16)
-    for copy in copies:
-        copy.wait()
     for k in range(KVH):
         delta = jnp.dot(
             routed, stack(returned_refs, k * span, span), preferred_element_type=jnp.float32
         )
-        for copy in laid_copies[k]:
-            copy.wait()
+        loads[k].wait()
         for i in range(steps):
-            lines = slice(i * step, (i + 1) * step)
-            at = slice(i * cells, (i + 1) * cells)
-            change = jnp.dot(
-                tall(delta[lines], group).astype(jnp.bfloat16),
-                keys_ref[k, :, at],
+            rows = slice(i * step, (i + 1) * step)
+            keys = keys_ref[k, :, i * cells : (i + 1) * cells]
+            values = rest_ref[k, i * block : i * block + cells, :]
+            query = rest_ref[k, i * block + cells : (i + 1) * block, :]
+            change = tall(delta[rows], group).astype(jnp.bfloat16)
+            scores = jnp.dot(
+                jnp.concatenate([query, change], axis=1),
+                jnp.concatenate([keys, keys], axis=0),
                 preferred_element_type=jnp.float32,
             )
-            scores = scores_ref[k, i] + change * factor
+            scores = scores * factor + bias_ref[i]
             expo = jnp.exp(scores - jnp.max(scores, axis=1, keepdims=True))
             probs = expo * (1.0 / jnp.sum(expo, axis=1, keepdims=True))
-            out = jnp.dot(
-                probs.astype(jnp.bfloat16), values_ref[k, at, :], preferred_element_type=jnp.float32
-            )
+            out = jnp.dot(probs.astype(jnp.bfloat16), values, preferred_element_type=jnp.float32)
             for g in range(group):
-                out_ref[lines, (k * group + g) * HEAD : (k * group + g + 1) * HEAD] = out[
+                out_ref[rows, (k * group + g) * HEAD : (k * group + g + 1) * HEAD] = out[
                     g * step : (g + 1) * step
                 ].astype(out_ref.dtype)
-
-
-def attend(routed, returned, laid, width):
-    rows = routed[0].shape[1]
-    given = [*returned, *laid]
+        stores[k].start()
+    for store in stores:
+        store.wait()
+
+
+def attend(routed, returned, cache_len, keys, rest, context):
+    rows, width = routed[0].shape[1], returned[0].shape[1]
+    group = width // (KVH * HEAD)
+    step = ROWS_STEP
+    steps = rows // step
+    cells = step * context
+    lens = jnp.repeat(cache_len, context).reshape(steps, 1, cells)
     return pl.pallas_call(
-        functools.partial(attend_kernel, width // (KVH * HEAD), len(returned)),
-        in_specs=[pl.BlockSpec(memory_space=pltpu.VMEM)] * 2
-        + [pl.BlockSpec(memory_space=pl.ANY)] * len(given),
-        out_specs=pl.BlockSpec(memory_space=pltpu.VMEM),
+        functools.partial(attend_kernel, group, context, len(returned)),
+        in_specs=[pl.BlockSpec(memory_space=pltpu.VMEM)] * (4 + len(returned)) + [pl.BlockSpec(memory_space=pl.ANY)],
+        out_specs=pl.BlockSpec(memory_space=pl.ANY),
         out_shape=jax.ShapeDtypeStruct((rows, width), jnp.bfloat16),
-        scratch_shapes=[pltpu.VMEM(part.shape, part.dtype) for part in given]
-        + [pltpu.SemaphoreType.DMA((len(returned),)), pltpu.SemaphoreType.DMA((KVH, len(laid)))],
-        compiler_params=pltpu.CompilerParams(vmem_limit_bytes=56 * 2**20),
+        scratch_shapes=[
+            pltpu.VMEM((KVH, steps * (cells + group * step), HEAD), rest.dtype),
+            pltpu.VMEM((steps, group * step, cells), jnp.float32),
+            pltpu.VMEM((rows, width), jnp.bfloat16),
+            pltpu.SemaphoreType.DMA((KVH, 2)),
+        ],
+        compiler_params=pltpu.CompilerParams(vmem_limit_bytes=GRANT),
         name="attend",
-    )(*routed, *given)
+    )(*routed, *returned, keys, lens, rest)
 
 
 def on_device(hidden, adapter_id, adapter_slot, cache_len, base_q, kv_cache, a_maps, b_maps):
@@ -304,19 +304,17 @@
     size = max(1, half // FAR_GROUPS)
     starts = range(0, half, size)
     arrived_far = [trade(messages[at : at + size], half + at) for at in starts]
-    routed, lines = whole(routed_far, False, owners, slot_count, held)
+    routed, lines = whole(arrived_far[0][0], False, owners, slot_count, held)
     arrived = swap(lines)
-    laid = prep(base_q, kv_cache, cache_len, routed)
-    returned, after = [], laid[0]
-    for i, at in enumerate(starts):
-        change_far = adapt(arrived_far[i], a_maps, b_maps, after)
-        after = change_far[0]
-        returned += trade(change_far, half + at)
-        if i == 0:
-            (after,) = adapt([arrived], a_maps, b_maps, after)
-            returned.append(swap(after))
-    returned = returned[:size] + returned[size + 1 :] + returned[size : size + 1]
-    return attend([routed_far, routed], returned, laid, base_q.shape[1])
+    keys, rest = prep(base_q, kv_cache, routed)
+    returned, after = [], rest
+    for group, at in zip(arrived_far, starts):
+        change = adapt(group, a_maps, b_maps, after)
+        after = change[0]
+        returned += trade(change, half + at)
+    (change,) = adapt([arrived], a_maps, b_maps, returned[0])
+    returned.append(swap(change))
+    return attend([routed_far, routed], returned, cache_len, keys, rest, kv_cache.shape[2])
 
 
 def solution(mesh):

time: 116 us -> 115 us (level)
  starting transfers between devices: 40.3 us -> 50.2 us
  waiting for transfers between devices: 39 us -> 29.8 us
  local copies, waits for them, and re-layouts: 10.2 us -> 4.56 us
  Pallas kernels: 25.6 us -> 29.8 us
    ppermute x16, starting transfers between devices: 28.4 us -> 41.3 us  [trade(): lax.ppermute(message, 'owner', [(i, i ^ first + j) for i in range(owners)])]
    ppermute x16, waiting for transfers between devices: 39 us -> 29.8 us  [trade(): lax.ppermute(message, 'owner', [(i, i ^ first + j) for i in range(owners)])]
    unnamed x40 -> x28, local copies, waits for them, and re-layouts: 9.89 us -> 4.3 us
    pallas_call x2, Pallas kernels: 13.8 us -> 17.8 us  [the longest x1 11.1 us: prep(): pl.pallas_call(functools.partial(prep_kernel, group), grid=(steps,), in_s...]
    all_to_all x2, starting transfers between devices: 11.8 us -> 8.89 us  [swap(): lax.all_to_all(blocks, 'owner', split_axis=0, concat_axis=0, tiled=True,...]
    pallas_call x5 -> x3, Pallas kernels: 4.52 us -> 4.7 us  [adapt(): pl.pallas_call(functools.partial(adapt_kernel, count), in_specs=[pl.Block...]
  transfers between devices with their start and end apart: 18 -> 18, of which waited for: 7 -> 9; matrix products, arithmetic and copies ran while one was open for 0% -> 0% of each run, Pallas kernels for 6% -> 12%
where the time goes in v11:
time: 115 us; the launch traced here: 114 us
  starting transfers between devices  50.2 us (44%)
  Pallas kernels  29.8 us (26%)
  waiting for transfers between devices  29.8 us (26%)
  local copies, waits for them, and re-layouts  4.56 us (4%)
    ppermute x16, starting transfers between devices, trade(): lax.ppermute(message, 'owner', [(i, i ^ first + j) for i in range(owners)])  41.3 us
    ppermute x16, waiting for transfers between devices, trade(): lax.ppermute(message, 'owner', [(i, i ^ first + j) for i in range(owners)])  29.8 us
    pallas_call x1, Pallas kernels, prep(): pl.pallas_call(functools.partial(prep_kernel, group), grid=(steps,), in_s...  11.1 us
    all_to_all x2, starting transfers between devices, swap(): lax.all_to_all(blocks, 'owner', split_axis=0, concat_axis=0, tiled=True,...  8.89 us
    pallas_call x2, Pallas kernels, pack(): pl.pallas_call(functools.partial(pack_kernel, pairs, owners, slot_count,...  7.23 us
    pallas_call x1, Pallas kernels, attend(): pl.pallas_call(functools.partial(attend_kernel, group, context, len(retur...  6.73 us
    pallas_call x3, Pallas kernels, adapt(): pl.pallas_call(functools.partial(adapt_kernel, count), in_specs=[pl.Block...  4.7 us
    unnamed x28, local copies, waits for them, and re-layouts  4.3 us
  transfers between devices with their start and end apart: 18, of which 9 were waited for; matrix products, arithmetic and copies ran while one was open for 0% of the time, Pallas kernels for 12%

profile of v11, /device:TPU:0, one launch (start us, length us, event | category | flops | bytes accessed | tf_op | source)
XLA Modules:
  0.0 114.4 jit_solution(112400613063281719)
XLA Ops:
  0.0 3.6 %pack_pairs.1 = (bf16[64,128]{1,0:T(8,128)(2,1)}, bf16[8,8320]{1,0:T(8,128)(2,1)}, bf16[8,8320]{1,0:T(8,128)(2,1)}, bf16[8,8320]{1,0:T(8,128)(2,1)}, bf16[8,8320...) custom-call(s32[1,32]{1,0:T(1,128)} %bitcast.10, ...), custom_call_target="tpu_custom_call" | custom-call | tf_op jit(solution)/shard_map/pack_pairs/pallas_call | solution.py:87
  3.6 4.1 %collective-permute-start = (bf16[8,8320]{1,0:T(8,128)(2,1)}, bf16[8,8320]{1,0:T(8,128)(2,1)S(1)}, u32[]{:S(2)}, u32[]{:S(2)}) collective-permute-start(bf16[8,8320]{1,0:T(8,128)(2,1)} %get-tuple-element.27), channel_id=1, source_target_pairs={{0,8},{1,9},{2,10},{3,11},{4,12},{5,13},{6,14},{7,15},{8,0},{9,1},... | collective-permute-start | bytes 399368 | tf_op jit(solution)/shard_map/ppermute | solution.py:298
  7.7 6.6 %collective-permute-done.after_ref.refs_0_ = bf16[8,8320]{1,0:T(8,128)(2,1)S(1)} collective-permute-done((bf16[8,8320]{1,0:T(8,128)(2,1)}, bf16[8,8320]{1,0:T(8,128)(2,1)S(1)}, u32[]{:S(2)}, u32[]{:S(2)}) %collective-permute-start) | collective-permute-done | bytes 133152 | tf_op jit(solution)/shard_map/ppermute | solution.py:298
  14.3 0.7 copy-done.6
  15.0 3.6 %pack.1 = (bf16[64,128]{1,0:T(8,128)(2,1)}, bf16[64,8320]{1,0:T(8,128)(2,1)}) custom-call(s32[1,32]{1,0:T(1,128)} %bitcast.11, s32[1,128]{1,0:T(1,128)} %bitcast.9, bf16[128,8192]{1,0:T(8,128)(2,1)} %hidden_ref.3, bf16[8,8320]{1,0:T(8,128)(2,1)} %copy-done.6), custom_call_target="tpu_custom_call" | custom-call | tf_op jit(solution)/shard_map/pack/pallas_call | solution.py:87
  18.6 4.3 %all-to-all-start = ((bf16[8,8,8320]{2,1,0:T(8,128)(2,1)}), bf16[8,8,8320]{2,1,0:T(8,128)(2,1)}, u32[]{:S(2)}, u32[]{:S(2)}) async-start(bf16[8,8,8320]{2,1,0:T(8,128)(2,1)} %bitcast.7), calls=%async_computation | async-start | bytes 2129920 | tf_op jit(solution)/shard_map/all_to_all | solution.py:291
  22.9 2.2 %collective-permute-start.1 = (bf16[8,8320]{1,0:T(8,128)(2,1)}, bf16[8,8320]{1,0:T(8,128)(2,1)S(1)}, u32[]{:S(2)}, u32[]{:S(2)}) collective-permute-start(bf16[8,8320]{1,0:T(8,128)(2,1)} %get-tuple-element.29), channel_id=1, source_target_pairs={{0,9},{1,8},{2,11},{3,10},{4,13},{5,12},{6,15},{7,14},{8,1},{9,0},... | collective-permute-start | bytes 399368 | tf_op jit(solution)/shard_map/ppermute | solution.py:298
  25.1 1.9 %collective-permute-start.2 = (bf16[8,8320]{1,0:T(8,128)(2,1)S(1)}, bf16[8,8320]{1,0:T(8,128)(2,1)S(1)}, u32[]{:S(2)}, u32[]{:S(2)}) collective-permute-start(bf16[8,8320]{1,0:T(8,128)(2,1)S(1)} %copy-done.13), channel_id=1, source_target_pairs={{0,10},{1,11},{2,8},{3,9},{4,14},{5,15},{6,12},{7,13},{8,2},{9,3},... | collective-permute-start | bytes 399368 | tf_op jit(solution)/shard_map/ppermute | solution.py:298
  26.9 1.3 %collective-permute-start.3 = (bf16[8,8320]{1,0:T(8,128)(2,1)S(1)}, bf16[8,8320]{1,0:T(8,128)(2,1)S(1)}, u32[]{:S(2)}, u32[]{:S(2)}) collective-permute-start(bf16[8,8320]{1,0:T(8,128)(2,1)S(1)} %copy-done.12), channel_id=1, source_target_pairs={{0,11},{1,10},{2,9},{3,8},{4,15},{5,14},{6,13},{7,12},{8,3},{9,2},... | collective-permute-start | bytes 399368 | tf_op jit(solution)/shard_map/ppermute | solution.py:298
  28.2 1.2 %copy-done.5 = bf16[128,4096]{1,0:T(8,128)(2,1)S(1)} copy-done((bf16[128,4096]{1,0:T(8,128)(2,1)S(1)}, bf16[128,4096]{1,0:T(8,128)(2,1)}, u32[]{:S(2)}) %copy-start.5) | copy-done | bytes 1048600
  29.5 11.1 %prep.1 = (bf16[4,128,2048]{2,1,0:T(8,128)(2,1)S(1)}, bf16[4,17472,128]{2,1,0:T(8,128)(2,1)}) custom-call(bf16[128,4096]{1,0:T(8,128)(2,1)S(1)} %copy-done.5, bf16[128,2,16,512]{3,2,1,0:T(8,128)(2,1)} %kv_ref.1, bf16[64,128]{1,0:T(8,128)(2,1)S(1)} %copy-done.8), custom_call_target="tpu_custom_call" | custom-call | tf_op jit(solution)/shard_map/prep/pallas_call | solution.py:178
  40.6 0.0 collective-permute-done.1.refs_1_
  40.6 0.7 collective-permute-done.2.refs_2_
  41.3 2.6 %collective-permute-done.3.refs_3_ = bf16[8,8320]{1,0:T(8,128)(2,1)S(1)} collective-permute-done((bf16[8,8320]{1,0:T(8,128)(2,1)S(1)}, bf16[8,8320]{1,0:T(8,128)(2,1)S(1)}, u32[]{:S(2)}, u32[]{:S(2)}) %collective-permute-start.3) | collective-permute-done | bytes 133152 | tf_op jit(solution)/shard_map/ppermute | solution.py:298
  43.9 1.3 %adapt.3 = (bf16[8,4096]{1,0:T(8,128)(2,1)S(1)}, bf16[8,4096]{1,0:T(8,128)(2,1)}, bf16[8,4096]{1,0:T(8,128)(2,1)}, bf16[8,4096]{1,0:T(8,128)(2,1)S(1)}) custom-call(bf16[8,8320]{1,0:T(8,128)(2,1)S(1)} %copy-done.7, bf16[8,8320]{1,0:T(8,128)(2,1)S(1)} %collective-permute-done.1.refs_1_, bf16[8,8320]{1,0:T(8,128)(2,1)S(1)} %collective-permute-done.2.refs_2_, ...), custom_call_target="tpu_custom_call" | custom-call | tf_op jit(solution)/shard_map/adapt/pallas_call | solution.py:142
  45.2 4.0 %collective-permute-start.4 = (bf16[8,4096]{1,0:T(8,128)(2,1)S(1)}, bf16[8,4096]{1,0:T(8,128)(2,1)S(1)}, u32[]{:S(2)}, u32[]{:S(2)}) collective-permute-start(bf16[8,4096]{1,0:T(8,128)(2,1)S(1)} %get-tuple-element.33.refs_6_), channel_id=1, source_target_pairs={{0,8},{1,9},{2,10},{3,11},{4,12},{5,13},{6,14},{7,15},{8,0},{9,1},... | collective-permute-start | bytes 196616 | tf_op jit(solution)/shard_map/ppermute | solution.py:298
  49.2 2.6 %collective-permute-done.4.refs_3_.refs_2_ = bf16[8,4096]{1,0:T(8,128)(2,1)S(1)} collective-permute-done((bf16[8,4096]{1,0:T(8,128)(2,1)S(1)}, bf16[8,4096]{1,0:T(8,128)(2,1)S(1)}, u32[]{:S(2)}, u32[]{:S(2)}) %collective-permute-start.4) | collective-permute-done | bytes 65568 | tf_op jit(solution)/shard_map/ppermute | solution.py:298
  51.8 0.0 all-to-all-done
  51.8 2.0 %adapt.5 = bf16[64,4096]{1,0:T(8,128)(2,1)S(1)} custom-call(bf16[64,8320]{1,0:T(8,128)(2,1)} %bitcast.3.refs_0_, bf16[8192,128]{1,0:T(8,128)(2,1)S(1)} %copy-done, bf16[128,4096]{1,0:T(8,128)(2,1)S(1)} %copy-done.1, bf16[8,4096]{1,0:T(8,128)(2,1)S(1)} %collective-permute-done.4.refs_3_.refs_2_), custom_call_target="tpu_custom_call" | custom-call | tf_op jit(solution)/shard_map/adapt/pallas_call | solution.py:142
  53.8 0.0 copy-start.4
  53.8 0.8 copy-done.4
  54.6 4.6 %all-to-all-start.1 = ((bf16[8,8,4096]{2,1,0:T(8,128)(2,1)}), bf16[8,8,4096]{2,1,0:T(8,128)(2,1)}, u32[]{:S(2)}, u32[]{:S(2)}) async-start(bf16[8,8,4096]{2,1,0:T(8,128)(2,1)} %bitcast.6), calls=%async_computation.1 | async-start | bytes 1048576 | tf_op jit(solution)/shard_map/all_to_all | solution.py:291
  59.2 4.0 %collective-permute-start.8 = (bf16[8,8320]{1,0:T(8,128)(2,1)}, bf16[8,8320]{1,0:T(8,128)(2,1)S(1)}, u32[]{:S(2)}, u32[]{:S(2)}) collective-permute-start(bf16[8,8320]{1,0:T(8,128)(2,1)} %get-tuple-element.37), channel_id=1, source_target_pairs={{0,12},{1,13},{2,14},{3,15},{4,8},{5,9},{6,10},{7,11},{8,4},{9,5},... | collective-permute-start | bytes 399368 | tf_op jit(solution)/shard_map/ppermute | solution.py:298
  63.2 0.0 collective-permute-start.9
  63.2 3.8 %collective-permute-start.10 = (bf16[8,8320]{1,0:T(8,128)(2,1)}, bf16[8,8320]{1,0:T(8,128)(2,1)S(1)}, u32[]{:S(2)}, u32[]{:S(2)}) collective-permute-start(bf16[8,8320]{1,0:T(8,128)(2,1)} %get-tuple-element.39), channel_id=1, source_target_pairs={{0,14},{1,15},{2,12},{3,13},{4,10},{5,11},{6,8},{7,9},{8,6},{9,7},... | collective-permute-start | bytes 399368 | tf_op jit(solution)/shard_map/ppermute | solution.py:298
  67.0 0.5 collective-permute-start.11
  67.5 0.0 collective-permute-start.5
  67.5 5.9 %collective-permute-done.8.refs_0_ = bf16[8,8320]{1,0:T(8,128)(2,1)S(1)} collective-permute-done((bf16[8,8320]{1,0:T(8,128)(2,1)}, bf16[8,8320]{1,0:T(8,128)(2,1)S(1)}, u32[]{:S(2)}, u32[]{:S(2)}) %collective-permute-start.8) | collective-permute-done | bytes 133152 | tf_op jit(solution)/shard_map/ppermute | solution.py:298
  73.4 0.0 collective-permute-start.6
  73.4 1.3 %collective-permute-done.9.refs_1_ = bf16[8,8320]{1,0:T(8,128)(2,1)S(1)} collective-permute-done((bf16[8,8320]{1,0:T(8,128)(2,1)}, bf16[8,8320]{1,0:T(8,128)(2,1)S(1)}, u32[]{:S(2)}, u32[]{:S(2)}) %collective-permute-start.9) | collective-permute-done | bytes 133152 | tf_op jit(solution)/shard_map/ppermute | solution.py:298
  74.7 11.5 %collective-permute-start.7 = (bf16[8,4096]{1,0:T(8,128)(2,1)}, bf16[8,4096]{1,0:T(8,128)(2,1)S(1)}, u32[]{:S(2)}, u32[]{:S(2)}) collective-permute-start(bf16[8,4096]{1,0:T(8,128)(2,1)} %copy-done.10), channel_id=1, source_target_pairs={{0,11},{1,10},{2,9},{3,8},{4,15},{5,14},{6,13},{7,12},{8,3},{9,2},... | collective-permute-start | bytes 196616 | tf_op jit(solution)/shard_map/ppermute | solution.py:298
  86.2 1.4 %adapt.4 = (bf16[8,4096]{1,0:T(8,128)(2,1)}, bf16[8,4096]{1,0:T(8,128)(2,1)}, bf16[8,4096]{1,0:T(8,128)(2,1)}, bf16[8,4096]{1,0:T(8,128)(2,1)}) custom-call(bf16[8,8320]{1,0:T(8,128)(2,1)S(1)} %collective-permute-done.8.refs_0_, bf16[8,8320]{1,0:T(8,128)(2,1)S(1)} %collective-permute-done.9.refs_1_, bf16[8,8320]{1,0:T(8,128)(2,1)S(1)} %collective-permute-done.10.refs_2_, ...), custom_call_target="tpu_custom_call" | custom-call | tf_op jit(solution)/shard_map/adapt/pallas_call | solution.py:142
  87.6 1.4 %collective-permute-start.12 = (bf16[8,4096]{1,0:T(8,128)(2,1)}, bf16[8,4096]{1,0:T(8,128)(2,1)S(1)}, u32[]{:S(2)}, u32[]{:S(2)}) collective-permute-start(bf16[8,4096]{1,0:T(8,128)(2,1)} %get-tuple-element.41), channel_id=1, source_target_pairs={{0,12},{1,13},{2,14},{3,15},{4,8},{5,9},{6,10},{7,11},{8,4},{9,5},... | collective-permute-start | bytes 196616 | tf_op jit(solution)/shard_map/ppermute | solution.py:298
  89.0 0.5 collective-permute-start.13
  89.5 1.2 %collective-permute-done.5.refs_3_ = bf16[8,4096]{1,0:T(8,128)(2,1)S(1)} collective-permute-done((bf16[8,4096]{1,0:T(8,128)(2,1)}, bf16[8,4096]{1,0:T(8,128)(2,1)S(1)}, u32[]{:S(2)}, u32[]{:S(2)}) %collective-permute-start.5) | collective-permute-done | bytes 65568 | tf_op jit(solution)/shard_map/ppermute | solution.py:298
  90.8 4.2 %collective-permute-start.14 = (bf16[8,4096]{1,0:T(8,128)(2,1)}, bf16[8,4096]{1,0:T(8,128)(2,1)S(1)}, u32[]{:S(2)}, u32[]{:S(2)}) collective-permute-start(bf16[8,4096]{1,0:T(8,128)(2,1)} %get-tuple-element.43), channel_id=1, source_target_pairs={{0,14},{1,15},{2,12},{3,13},{4,10},{5,11},{6,8},{7,9},{8,6},{9,7},... | collective-permute-start | bytes 196616 | tf_op jit(solution)/shard_map/ppermute | solution.py:298
  95.0 3.7 %collective-permute-done.6.refs_4_ = bf16[8,4096]{1,0:T(8,128)(2,1)S(1)} collective-permute-done((bf16[8,4096]{1,0:T(8,128)(2,1)}, bf16[8,4096]{1,0:T(8,128)(2,1)S(1)}, u32[]{:S(2)}, u32[]{:S(2)}) %collective-permute-start.6) | collective-permute-done | bytes 65568 | tf_op jit(solution)/shard_map/ppermute | solution.py:298
  98.7 2.0 %collective-permute-start.15 = (bf16[8,4096]{1,0:T(8,128)(2,1)}, bf16[8,4096]{1,0:T(8,128)(2,1)S(1)}, u32[]{:S(2)}, u32[]{:S(2)}) collective-permute-start(bf16[8,4096]{1,0:T(8,128)(2,1)} %get-tuple-element.44), channel_id=1, source_target_pairs={{0,15},{1,14},{2,13},{3,12},{4,11},{5,10},{6,9},{7,8},{8,7},{9,6},... | collective-permute-start | bytes 196616 | tf_op jit(solution)/shard_map/ppermute | solution.py:298
  100.7 0.1 broadcast_in_dim.7
  100.8 0.1 broadcast_in_dim.8
  100.8 0.1 broadcast_in_dim.9.refs_12_
  101.0 0.0 collective-permute-done.7.refs_5_
  101.0 0.0 collective-permute-done.12.refs_6_
  101.0 0.0 collective-permute-done.14.refs_8_
  101.0 5.1 %collective-permute-done.15.refs_9_ = bf16[8,4096]{1,0:T(8,128)(2,1)S(1)} collective-permute-done((bf16[8,4096]{1,0:T(8,128)(2,1)}, bf16[8,4096]{1,0:T(8,128)(2,1)S(1)}, u32[]{:S(2)}, u32[]{:S(2)}) %collective-permute-start.15) | collective-permute-done | bytes 65568 | tf_op jit(solution)/shard_map/ppermute | solution.py:298
  106.1 0.0 all-to-all-done.1
  106.1 1.6 %copy-done.3 = bf16[4,128,2048]{2,1,0:T(8,128)(2,1)S(1)} copy-done((bf16[4,128,2048]{2,1,0:T(8,128)(2,1)S(1)}, bf16[4,128,2048]{2,1,0:T(8,128)(2,1)}, u32[]{:S(2)}) %copy-start.3) | copy-done | bytes 2097176
  107.7 6.7 %attend.1 = bf16[128,4096]{1,0:T(8,128)(2,1)} custom-call(bf16[64,128]{1,0:T(8,128)(2,1)S(1)} %copy-done.9, bf16[64,128]{1,0:T(8,128)(2,1)S(1)} %copy-done.8, bf16[8,4096]{1,0:T(8,128)(2,1)S(1)} %collective-permute-done.4.refs_3_.refs_2_, bf16[8,4096]{1,0:T(8,128)(2,1)S(1)} %collective-permute-done.5.refs_3_, ...), custom_call_target="tpu_custom_call" | custom-call | tf_op jit(solution)/shard_map/attend/pallas_call | solution.py:265
  (26 shorter events, 0.1 us)
Async XLA Ops:
  3.6 21.5 %copy-start.13 = (bf16[8,8320]{1,0:T(8,128)(2,1)S(1)}, bf16[8,8320]{1,0:T(8,128)(2,1)}, u32[]{:S(2)}) copy-start(bf16[8,8320]{1,0:T(8,128)(2,1)} %get-tuple-element.30) | copy-start | bytes 399364
  3.6 23.3 %copy-start.12 = (bf16[8,8320]{1,0:T(8,128)(2,1)S(1)}, bf16[8,8320]{1,0:T(8,128)(2,1)}, u32[]{:S(2)}) copy-start(bf16[8,8320]{1,0:T(8,128)(2,1)} %get-tuple-element.31) | copy-start | bytes 399364
  3.6 10.7 %collective-permute-start = (bf16[8,8320]{1,0:T(8,128)(2,1)}, bf16[8,8320]{1,0:T(8,128)(2,1)S(1)}, u32[]{:S(2)}, u32[]{:S(2)}) collective-permute-start(bf16[8,8320]{1,0:T(8,128)(2,1)} %get-tuple-element.27), channel_id=1, source_target_pairs={{0,8},{1,9},{2,10},{3,11},{4,12},{5,13},{6,14},{7,15},{8,0},{9,1},... | collective-permute-start | bytes 399368 | tf_op jit(solution)/shard_map/ppermute | solution.py:298
  14.3 0.7 copy-start.6
  18.6 9.6 %copy-start.8 = (bf16[64,128]{1,0:T(8,128)(2,1)S(1)}, bf16[64,128]{1,0:T(8,128)(2,1)}, u32[]{:S(2)}) copy-start(bf16[64,128]{1,0:T(8,128)(2,1)} %get-tuple-element.28._.refs_1_) | copy-start | bytes 49156
  18.6 33.1 %all-to-all-start = ((bf16[8,8,8320]{2,1,0:T(8,128)(2,1)}), bf16[8,8,8320]{2,1,0:T(8,128)(2,1)}, u32[]{:S(2)}, u32[]{:S(2)}) async-start(bf16[8,8,8320]{2,1,0:T(8,128)(2,1)} %bitcast.7), calls=%async_computation | async-start | bytes 2129920 | tf_op jit(solution)/shard_map/all_to_all | solution.py:291
  22.9 17.7 %collective-permute-start.1 = (bf16[8,8320]{1,0:T(8,128)(2,1)}, bf16[8,8320]{1,0:T(8,128)(2,1)S(1)}, u32[]{:S(2)}, u32[]{:S(2)}) collective-permute-start(bf16[8,8320]{1,0:T(8,128)(2,1)} %get-tuple-element.29), channel_id=1, source_target_pairs={{0,9},{1,8},{2,11},{3,10},{4,13},{5,12},{6,15},{7,14},{8,1},{9,0},... | collective-permute-start | bytes 399368 | tf_op jit(solution)/shard_map/ppermute | solution.py:298
  25.1 16.2 %collective-permute-start.2 = (bf16[8,8320]{1,0:T(8,128)(2,1)S(1)}, bf16[8,8320]{1,0:T(8,128)(2,1)S(1)}, u32[]{:S(2)}, u32[]{:S(2)}) collective-permute-start(bf16[8,8320]{1,0:T(8,128)(2,1)S(1)} %copy-done.13), channel_id=1, source_target_pairs={{0,10},{1,11},{2,8},{3,9},{4,14},{5,15},{6,12},{7,13},{8,2},{9,3},... | collective-permute-start | bytes 399368 | tf_op jit(solution)/shard_map/ppermute | solution.py:298
  26.9 17.0 %collective-permute-start.3 = (bf16[8,8320]{1,0:T(8,128)(2,1)S(1)}, bf16[8,8320]{1,0:T(8,128)(2,1)S(1)}, u32[]{:S(2)}, u32[]{:S(2)}) collective-permute-start(bf16[8,8320]{1,0:T(8,128)(2,1)S(1)} %copy-done.12), channel_id=1, source_target_pairs={{0,11},{1,10},{2,9},{3,8},{4,15},{5,14},{6,13},{7,12},{8,3},{9,2},... | collective-permute-start | bytes 399368 | tf_op jit(solution)/shard_map/ppermute | solution.py:298
  28.2 1.2 %copy-start.5 = (bf16[128,4096]{1,0:T(8,128)(2,1)S(1)}, bf16[128,4096]{1,0:T(8,128)(2,1)}, u32[]{:S(2)}) copy-start(bf16[128,4096]{1,0:T(8,128)(2,1)} %base_ref.1) | copy-start | bytes 3145732
  29.5 14.4 %copy-start = (bf16[8192,128]{1,0:T(8,128)(2,1)S(1)}, bf16[8192,128]{1,0:T(8,128)(2,1)}, u32[]{:S(2)}) copy-start(bf16[8192,128]{1,0:T(8,128)(2,1)} %refs_1_.1) | copy-start | bytes 6291460
  29.5 14.4 %copy-start.1 = (bf16[128,4096]{1,0:T(8,128)(2,1)S(1)}, bf16[128,4096]{1,0:T(8,128)(2,1)}, u32[]{:S(2)}) copy-start(bf16[128,4096]{1,0:T(8,128)(2,1)} %refs_2_.1) | copy-start | bytes 3145732
  29.5 14.4 %copy-start.7 = (bf16[8,8320]{1,0:T(8,128)(2,1)S(1)}, bf16[8,8320]{1,0:T(8,128)(2,1)}, u32[]{:S(2)}) copy-start(bf16[8,8320]{1,0:T(8,128)(2,1)} %copy-done.6) | copy-start | bytes 399364
  40.6 4.7 %copy-start.2 = (bf16[4,128,2048]{2,1,0:T(8,128)(2,1)}, bf16[4,128,2048]{2,1,0:T(8,128)(2,1)S(1)}, u32[]{:S(2)}) copy-start(bf16[4,128,2048]{2,1,0:T(8,128)(2,1)S(1)} %get-tuple-element.46.refs_11_) | copy-start | bytes 6291460
  45.2 8.5 %copy-start.10 = (bf16[8,4096]{1,0:T(8,128)(2,1)}, bf16[8,4096]{1,0:T(8,128)(2,1)S(1)}, u32[]{:S(2)}) copy-start(bf16[8,4096]{1,0:T(8,128)(2,1)S(1)} %get-tuple-element.36) | copy-start | bytes 196612
  45.2 6.5 %collective-permute-start.4 = (bf16[8,4096]{1,0:T(8,128)(2,1)S(1)}, bf16[8,4096]{1,0:T(8,128)(2,1)S(1)}, u32[]{:S(2)}, u32[]{:S(2)}) collective-permute-start(bf16[8,4096]{1,0:T(8,128)(2,1)S(1)} %get-tuple-element.33.refs_6_), channel_id=1, source_target_pairs={{0,8},{1,9},{2,10},{3,11},{4,12},{5,13},{6,14},{7,15},{8,0},{9,1},... | collective-permute-start | bytes 196616 | tf_op jit(solution)/shard_map/ppermute | solution.py:298
  53.8 0.8 copy-start.4
  54.6 51.5 %all-to-all-start.1 = ((bf16[8,8,4096]{2,1,0:T(8,128)(2,1)}), bf16[8,8,4096]{2,1,0:T(8,128)(2,1)}, u32[]{:S(2)}, u32[]{:S(2)}) async-start(bf16[8,8,4096]{2,1,0:T(8,128)(2,1)} %bitcast.6), calls=%async_computation.1 | async-start | bytes 1048576 | tf_op jit(solution)/shard_map/all_to_all | solution.py:291
  59.2 41.5 %copy-start.11 = (s32[128]{0:T(128)S(1)}, s32[128]{0:T(128)}, u32[]{:S(2)}) copy-start(s32[128]{0:T(128)} %param.11) | copy-start | bytes 1540
  59.2 46.9 %copy-start.9 = (bf16[64,128]{1,0:T(8,128)(2,1)S(1)}, bf16[64,128]{1,0:T(8,128)(2,1)}, u32[]{:S(2)}) copy-start(bf16[64,128]{1,0:T(8,128)(2,1)} %get-tuple-element.26.refs_0_) | copy-start | bytes 49156
  59.2 14.2 %collective-permute-start.8 = (bf16[8,8320]{1,0:T(8,128)(2,1)}, bf16[8,8320]{1,0:T(8,128)(2,1)S(1)}, u32[]{:S(2)}, u32[]{:S(2)}) collective-permute-start(bf16[8,8320]{1,0:T(8,128)(2,1)} %get-tuple-element.37), channel_id=1, source_target_pairs={{0,12},{1,13},{2,14},{3,15},{4,8},{5,9},{6,10},{7,11},{8,4},{9,5},... | collective-permute-start | bytes 399368 | tf_op jit(solution)/shard_map/ppermute | solution.py:298
  63.2 11.5 %collective-permute-start.9 = (bf16[8,8320]{1,0:T(8,128)(2,1)}, bf16[8,8320]{1,0:T(8,128)(2,1)S(1)}, u32[]{:S(2)}, u32[]{:S(2)}) collective-permute-start(bf16[8,8320]{1,0:T(8,128)(2,1)} %get-tuple-element.38), channel_id=1, source_target_pairs={{0,13},{1,12},{2,15},{3,14},{4,9},{5,8},{6,11},{7,10},{8,5},{9,4},... | collective-permute-start | bytes 399368 | tf_op jit(solution)/shard_map/ppermute | solution.py:298
  63.2 23.0 %collective-permute-start.10 = (bf16[8,8320]{1,0:T(8,128)(2,1)}, bf16[8,8320]{1,0:T(8,128)(2,1)S(1)}, u32[]{:S(2)}, u32[]{:S(2)}) collective-permute-start(bf16[8,8320]{1,0:T(8,128)(2,1)} %get-tuple-element.39), channel_id=1, source_target_pairs={{0,14},{1,15},{2,12},{3,13},{4,10},{5,11},{6,8},{7,9},{8,6},{9,7},... | collective-permute-start | bytes 399368 | tf_op jit(solution)/shard_map/ppermute | solution.py:298
  67.0 19.2 %collective-permute-start.11 = (bf16[8,8320]{1,0:T(8,128)(2,1)}, bf16[8,8320]{1,0:T(8,128)(2,1)S(1)}, u32[]{:S(2)}, u32[]{:S(2)}) collective-permute-start(bf16[8,8320]{1,0:T(8,128)(2,1)} %get-tuple-element.40), channel_id=1, source_target_pairs={{0,15},{1,14},{2,13},{3,12},{4,11},{5,10},{6,9},{7,8},{8,7},{9,6},... | collective-permute-start | bytes 399368 | tf_op jit(solution)/shard_map/ppermute | solution.py:298
  67.5 23.3 %collective-permute-start.5 = (bf16[8,4096]{1,0:T(8,128)(2,1)}, bf16[8,4096]{1,0:T(8,128)(2,1)S(1)}, u32[]{:S(2)}, u32[]{:S(2)}) collective-permute-start(bf16[8,4096]{1,0:T(8,128)(2,1)} %get-tuple-element.34), channel_id=1, source_target_pairs={{0,9},{1,8},{2,11},{3,10},{4,13},{5,12},{6,15},{7,14},{8,1},{9,0},... | collective-permute-start | bytes 196616 | tf_op jit(solution)/shard_map/ppermute | solution.py:298
  73.4 25.3 %collective-permute-start.6 = (bf16[8,4096]{1,0:T(8,128)(2,1)}, bf16[8,4096]{1,0:T(8,128)(2,1)S(1)}, u32[]{:S(2)}, u32[]{:S(2)}) collective-permute-start(bf16[8,4096]{1,0:T(8,128)(2,1)} %get-tuple-element.35), channel_id=1, source_target_pairs={{0,10},{1,11},{2,8},{3,9},{4,14},{5,15},{6,12},{7,13},{8,2},{9,3},... | collective-permute-start | bytes 196616 | tf_op jit(solution)/shard_map/ppermute | solution.py:298
  74.7 26.2 %collective-permute-start.7 = (bf16[8,4096]{1,0:T(8,128)(2,1)}, bf16[8,4096]{1,0:T(8,128)(2,1)S(1)}, u32[]{:S(2)}, u32[]{:S(2)}) collective-permute-start(bf16[8,4096]{1,0:T(8,128)(2,1)} %copy-done.10), channel_id=1, source_target_pairs={{0,11},{1,10},{2,9},{3,8},{4,15},{5,14},{6,13},{7,12},{8,3},{9,2},... | collective-permute-start | bytes 196616 | tf_op jit(solution)/shard_map/ppermute | solution.py:298
  87.6 13.4 %collective-permute-start.12 = (bf16[8,4096]{1,0:T(8,128)(2,1)}, bf16[8,4096]{1,0:T(8,128)(2,1)S(1)}, u32[]{:S(2)}, u32[]{:S(2)}) collective-permute-start(bf16[8,4096]{1,0:T(8,128)(2,1)} %get-tuple-element.41), channel_id=1, source_target_pairs={{0,12},{1,13},{2,14},{3,15},{4,8},{5,9},{6,10},{7,11},{8,4},{9,5},... | collective-permute-start | bytes 196616 | tf_op jit(solution)/shard_map/ppermute | solution.py:298
  89.0 12.0 %collective-permute-start.13 = (bf16[8,4096]{1,0:T(8,128)(2,1)}, bf16[8,4096]{1,0:T(8,128)(2,1)S(1)}, u32[]{:S(2)}, u32[]{:S(2)}) collective-permute-start(bf16[8,4096]{1,0:T(8,128)(2,1)} %get-tuple-element.42), channel_id=1, source_target_pairs={{0,13},{1,12},{2,15},{3,14},{4,9},{5,8},{6,11},{7,10},{8,5},{9,4},... | collective-permute-start | bytes 196616 | tf_op jit(solution)/shard_map/ppermute | solution.py:298
  90.8 10.2 %collective-permute-start.14 = (bf16[8,4096]{1,0:T(8,128)(2,1)}, bf16[8,4096]{1,0:T(8,128)(2,1)S(1)}, u32[]{:S(2)}, u32[]{:S(2)}) collective-permute-start(bf16[8,4096]{1,0:T(8,128)(2,1)} %get-tuple-element.43), channel_id=1, source_target_pairs={{0,14},{1,15},{2,12},{3,13},{4,10},{5,11},{6,8},{7,9},{8,6},{9,7},... | collective-permute-start | bytes 196616 | tf_op jit(solution)/shard_map/ppermute | solution.py:298
  98.7 7.4 %collective-permute-start.15 = (bf16[8,4096]{1,0:T(8,128)(2,1)}, bf16[8,4096]{1,0:T(8,128)(2,1)S(1)}, u32[]{:S(2)}, u32[]{:S(2)}) collective-permute-start(bf16[8,4096]{1,0:T(8,128)(2,1)} %get-tuple-element.44), channel_id=1, source_target_pairs={{0,15},{1,14},{2,13},{3,12},{4,11},{5,10},{6,9},{7,8},{8,7},{9,6},... | collective-permute-start | bytes 196616 | tf_op jit(solution)/shard_map/ppermute | solution.py:298
  106.1 1.6 %copy-start.3 = (bf16[4,128,2048]{2,1,0:T(8,128)(2,1)S(1)}, bf16[4,128,2048]{2,1,0:T(8,128)(2,1)}, u32[]{:S(2)}) copy-start(bf16[4,128,2048]{2,1,0:T(8,128)(2,1)} %copy-done.2) | copy-start | bytes 6291460

commit v12 on v10

--- a/solution.py
+++ b/solution.py
@@ -140,7 +140,7 @@
         in_specs=[pl.BlockSpec(memory_space=pltpu.VMEM)] * 3 + [pl.BlockSpec(memory_space=pl.ANY)],
         out_specs=pl.BlockSpec(memory_space=pltpu.VMEM),
         out_shape=jax.ShapeDtypeStruct((arrived.shape[0], b_maps.shape[1]), jnp.bfloat16),
-        compiler_params=pltpu.CompilerParams(vmem_limit_bytes=GRANT),
+        compiler_params=pltpu.CompilerParams(vmem_limit_bytes=16 * 2**20),
         name="adapt",
     )(arrived, a_maps, b_maps, after)
 
@@ -149,7 +149,8 @@
     return jnp.concatenate([rows[:, g * HEAD : (g + 1) * HEAD] for g in range(group)], axis=0)
 
 
-def prep_kernel(group, base_ref, kv_ref, keys_ref, rest_ref):
+def prep_kernel(group, base_ref, kv_ref, keys_ref, rest_ref, token_ref):
+    token_ref[...] = jnp.zeros_like(token_ref)
     step, context = kv_ref.shape[0], kv_ref.shape[2]
     cells = step * context
     for k in range(KVH):
@@ -180,12 +181,14 @@
         out_specs=[
             pl.BlockSpec((KVH, HEAD, cells), lambda i: (0, 0, i)),
             pl.BlockSpec((KVH, lines, HEAD), lambda i: (0, i, 0)),
+            pl.BlockSpec((8, LANES), lambda i: (0, 0)),
         ],
         out_shape=[
             jax.ShapeDtypeStruct((KVH, HEAD, rows * context), jnp.bfloat16),
             jax.ShapeDtypeStruct((KVH, length, HEAD), jnp.bfloat16),
-        ],
-        compiler_params=pltpu.CompilerParams(vmem_limit_bytes=GRANT),
+            jax.ShapeDtypeStruct((8, LANES), jnp.float32),
+        ],
+        compiler_params=pltpu.CompilerParams(vmem_limit_bytes=60 * 2**20),
         name="prep",
     )(base_q, kv_cache)
 
@@ -281,8 +284,8 @@
     packed, routed = pack(hidden, adapter_id, adapter_slot, owners, slot_count, held)
     packed = packed.reshape(owners, slot_count, packed.shape[1])
     arrived = lax.all_to_all(packed, "owner", split_axis=0, concat_axis=0, tiled=True)
-    keys, rest = prep(base_q, kv_cache)
-    change = adapt(arrived.reshape(bins, arrived.shape[2]), a_maps, b_maps, rest)
+    keys, rest, token = prep(base_q, kv_cache)
+    change = adapt(arrived.reshape(bins, arrived.shape[2]), a_maps, b_maps, token)
     change = change.reshape(owners, slot_count, change.shape[1])
     returned = lax.all_to_all(change, "owner", split_axis=0, concat_axis=0, tiled=True)
     returned = returned.reshape(bins, returned.shape[2])

time: 100 us -> 99.5 us (level)
  Pallas kernels: 24.6 us -> 23.6 us
    pallas_call x1, Pallas kernels: 3.67 us -> 2.04 us  [adapt(): pl.pallas_call(adapt_kernel, in_specs=[pl.BlockSpec(memory_space=pltpu.VM...]
    unnamed x14 -> x12, local copies, waits for them, and re-layouts: 2.6 us -> 2.3 us
  transfers between devices with their start and end apart: 2 -> 2, of which waited for: 2 -> 2; matrix products, arithmetic and copies ran while one was open for 0% -> 0% of each run, Pallas kernels for 11% -> 12%
where the time goes in v12:
time: 99.5 us; the launch traced here: 97.7 us
  waiting for transfers between devices  52.7 us (53%)
  Pallas kernels  23.6 us (24%)
  starting transfers between devices  18.9 us (19%)
  local copies, waits for them, and re-layouts  2.56 us (3%)
    all_to_all x1, waiting for transfers between devices, on_device(): lax.all_to_all(packed, 'owner', split_axis=0, concat_axis=0, tiled=True)  30 us
    all_to_all x1, waiting for transfers between devices, on_device(): lax.all_to_all(change, 'owner', split_axis=0, concat_axis=0, tiled=True)  22.7 us
    pallas_call x1, Pallas kernels, prep(): pl.pallas_call(functools.partial(prep_kernel, group), grid=(steps,), in_s...  11.6 us
    all_to_all x1, starting transfers between devices, on_device(): lax.all_to_all(change, 'owner', split_axis=0, concat_axis=0, tiled=True)  11.5 us
    all_to_all x1, starting transfers between devices, on_device(): lax.all_to_all(packed, 'owner', split_axis=0, concat_axis=0, tiled=True)  7.38 us
    pallas_call x1, Pallas kernels, attend(): pl.pallas_call(functools.partial(attend_kernel, group, context), in_specs...  5.67 us
    pallas_call x1, Pallas kernels, pack(): pl.pallas_call(functools.partial(pack_kernel, owners, slot_count, held),...  4.23 us
    unnamed x12, local copies, waits for them, and re-layouts  2.3 us
  transfers between devices with their start and end apart: 2, of which 2 were waited for; matrix products, arithmetic and copies ran while one was open for 0% of the time, Pallas kernels for 12%

profile of v12, /device:TPU:0, one launch (start us, length us, event | category | flops | bytes accessed | tf_op | source)
XLA Modules:
  0.0 97.7 jit_solution(6316645855318613293)
XLA Ops:
  0.0 4.2 %pack.1 = (bf16[128,8320]{1,0:T(8,128)(2,1)}, bf16[128,128]{1,0:T(8,128)(2,1)}) custom-call(s32[1,32]{1,0:T(1,128)} %bitcast.9, s32[1,128]{1,0:T(1,128)} %bitcast.10, bf16[128,8192]{1,0:T(8,128)(2,1)} %hidden_hbm.1), custom_call_target="tpu_custom_call" | custom-call | tf_op jit(solution)/shard_map/pack/pallas_call | solution.py:94
  4.2 7.4 %all-to-all-start = ((bf16[16,8,8320]{2,1,0:T(8,128)(2,1)}), bf16[16,8,8320]{2,1,0:T(8,128)(2,1)S(1)}, u32[]{:S(2)}, u32[]{:S(2)}) async-start(bf16[16,8,8320]{2,1,0:T(8,128)(2,1)} %bitcast.8), calls=%async_computation | async-start | bytes 4259840 | tf_op jit(solution)/shard_map/all_to_all | solution.py:286
  11.6 0.0 copy-start.2
  11.6 11.6 %prep.1 = (bf16[4,128,2048]{2,1,0:T(8,128)(2,1)}, bf16[4,17472,128]{2,1,0:T(8,128)(2,1)}, f32[8,128]{1,0:T(8,128)}) custom-call(bf16[128,4096]{1,0:T(8,128)(2,1)} %base_ref.1, bf16[128,2,16,512]{3,2,1,0:T(8,128)(2,1)} %kv_ref.1), custom_call_target="tpu_custom_call" | custom-call | tf_op jit(solution)/shard_map/prep/pallas_call | solution.py:174
  23.3 30.0 %all-to-all-done = bf16[16,8,8320]{2,1,0:T(8,128)(2,1)S(1)} async-done(((bf16[16,8,8320]{2,1,0:T(8,128)(2,1)}), bf16[16,8,8320]{2,1,0:T(8,128)(2,1)S(1)}, u32[]{:S(2)}, u32[]{:S(2)}) %all-to-all-start) | async-done | bytes 2129952 | tf_op jit(solution)/shard_map/all_to_all | solution.py:286
  53.3 0.0 copy-done.2
  53.3 0.0 copy-start.1
  53.3 1.6 %copy-done.1 = bf16[8192,128]{1,0:T(8,128)(2,1)S(1)} copy-done((bf16[8192,128]{1,0:T(8,128)(2,1)S(1)}, bf16[8192,128]{1,0:T(8,128)(2,1)}, u32[]{:S(2)}) %copy-start.1) | copy-done | bytes 2097176
  54.9 0.0 copy-start.4
  54.9 0.7 copy-done.4
  55.6 0.0 copy-start.5
  55.6 2.0 %adapt.1 = bf16[128,4096]{1,0:T(8,128)(2,1)} custom-call(bf16[128,8320]{1,0:T(8,128)(2,1)S(1)} %bitcast.6, bf16[8192,128]{1,0:T(8,128)(2,1)S(1)} %copy-done.1, bf16[128,4096]{1,0:T(8,128)(2,1)S(1)} %copy-done.2, f32[8,128]{1,0:T(8,128)S(1)} %copy-done.4), custom_call_target="tpu_custom_call" | custom-call | tf_op jit(solution)/shard_map/adapt/pallas_call | solution.py:138
  57.6 0.0 copy-start
  57.6 0.0 copy-start.3
  57.6 11.5 %all-to-all-start.1 = ((bf16[16,8,4096]{2,1,0:T(8,128)(2,1)}), bf16[16,8,4096]{2,1,0:T(8,128)(2,1)S(1)}, u32[]{:S(2)}, u32[]{:S(2)}) async-start(bf16[16,8,4096]{2,1,0:T(8,128)(2,1)} %bitcast.4), calls=%async_computation.1 | async-start | bytes 2097152 | tf_op jit(solution)/shard_map/all_to_all | solution.py:290
  69.1 0.0 copy-done.5
  69.1 0.1 broadcast_in_dim.7
  69.2 0.1 broadcast_in_dim.8
  69.3 0.1 broadcast_in_dim.9.lens_ref
  69.4 22.7 %all-to-all-done.1 = bf16[16,8,4096]{2,1,0:T(8,128)(2,1)S(1)} async-done(((bf16[16,8,4096]{2,1,0:T(8,128)(2,1)}), bf16[16,8,4096]{2,1,0:T(8,128)(2,1)S(1)}, u32[]{:S(2)}, u32[]{:S(2)}) %all-to-all-start.1) | async-done | bytes 1048608 | tf_op jit(solution)/shard_map/all_to_all | solution.py:290
  92.1 0.0 copy-done
  92.1 0.0 copy-done.3
  92.1 5.7 %attend.1 = bf16[128,4096]{1,0:T(8,128)(2,1)} custom-call(bf16[128,128]{1,0:T(8,128)(2,1)S(1)} %copy-done.3, bf16[128,4096]{1,0:T(8,128)(2,1)S(1)} %bitcast.7, bf16[4,128,2048]{2,1,0:T(8,128)(2,1)S(1)} %copy-done, s32[16,1,128]{2,1,0:T(1,128)S(1)} %broadcast_in_dim.9.lens_ref, bf16[4,17472,128]{2,1,0:T(8,128)(2,1)} %get-tuple-element.14.rest_hbm), custom_call_target="tpu_custom_call" | custom-call | tf_op jit(solution)/shard_map/attend/pallas_call | solution.py:262
Async XLA Ops:
  4.2 49.1 %all-to-all-start = ((bf16[16,8,8320]{2,1,0:T(8,128)(2,1)}), bf16[16,8,8320]{2,1,0:T(8,128)(2,1)S(1)}, u32[]{:S(2)}, u32[]{:S(2)}) async-start(bf16[16,8,8320]{2,1,0:T(8,128)(2,1)} %bitcast.8), calls=%async_computation | async-start | bytes 4259840 | tf_op jit(solution)/shard_map/all_to_all | solution.py:286
  11.6 41.7 %copy-start.2 = (bf16[128,4096]{1,0:T(8,128)(2,1)S(1)}, bf16[128,4096]{1,0:T(8,128)(2,1)}, u32[]{:S(2)}) copy-start(bf16[128,4096]{1,0:T(8,128)(2,1)} %b_ref.1) | copy-start | bytes 3145732
  53.3 1.6 %copy-start.1 = (bf16[8192,128]{1,0:T(8,128)(2,1)S(1)}, bf16[8192,128]{1,0:T(8,128)(2,1)}, u32[]{:S(2)}) copy-start(bf16[8192,128]{1,0:T(8,128)(2,1)} %a_ref.1) | copy-start | bytes 6291460
  54.9 0.7 copy-start.4
  55.6 13.5 %copy-start.5 = (s32[128]{0:T(128)S(1)}, s32[128]{0:T(128)}, u32[]{:S(2)}) copy-start(s32[128]{0:T(128)} %param.11) | copy-start | bytes 1540
  57.6 34.4 %copy-start = (bf16[4,128,2048]{2,1,0:T(8,128)(2,1)S(1)}, bf16[4,128,2048]{2,1,0:T(8,128)(2,1)}, u32[]{:S(2)}) copy-start(bf16[4,128,2048]{2,1,0:T(8,128)(2,1)} %get-tuple-element.13.keys_ref) | copy-start | bytes 6291460
  57.6 34.4 %copy-start.3 = (bf16[128,128]{1,0:T(8,128)(2,1)S(1)}, bf16[128,128]{1,0:T(8,128)(2,1)}, u32[]{:S(2)}) copy-start(bf16[128,128]{1,0:T(8,128)(2,1)} %get-tuple-element.10.routed_ref) | copy-start | bytes 98308
  57.6 34.4 %all-to-all-start.1 = ((bf16[16,8,4096]{2,1,0:T(8,128)(2,1)}), bf16[16,8,4096]{2,1,0:T(8,128)(2,1)S(1)}, u32[]{:S(2)}, u32[]{:S(2)}) async-start(bf16[16,8,4096]{2,1,0:T(8,128)(2,1)} %bitcast.4), calls=%async_computation.1 | async-start | bytes 2097152 | tf_op jit(solution)/shard_map/all_to_all | solution.py:290

commit v13 on v10

--- a/solution.py
+++ b/solution.py
@@ -10,7 +10,6 @@
 HEAD = 128
 KVH = 4
 RANK = 64
-LANES = 128
 SCALE = 2.0
 ROWS_STEP = 8
 COLUMNS_STEP = 1024
@@ -38,12 +37,13 @@
     place = jnp.sum(jnp.where(hits, before, 0.0), axis=0, keepdims=True).astype(jnp.int32)
     bins = owner * slot_count + place
     routed = bins == lax.broadcasted_iota(jnp.int32, (owners * slot_count, rows), 0)
-    label = jnp.sum(jnp.where(routed, local.astype(jnp.float32), 0.0), axis=1, keepdims=True)
-    return routed.astype(jnp.bfloat16), label
-
-
-def pack_kernel(owners, slot_count, held, slots_hbm, ids_hbm, hidden_hbm, packed_hbm, routed_hbm, *scratch):
-    slots_ref, ids_ref, rows_ref, bins_ref, routed_ref, small_sems, sems, out_sems = scratch
+    return routed.astype(jnp.bfloat16), local.astype(jnp.float32).astype(jnp.bfloat16)
+
+
+def pack_kernel(
+    owners, slot_count, held, slots_hbm, ids_hbm, hidden_hbm, packed_hbm, routed_hbm, labels_hbm, *scratch
+):
+    slots_ref, ids_ref, rows_ref, bins_ref, routed_ref, labels_ref, small_sems, sems, out_sems = scratch
     width = rows_ref.shape[1]
     spans = [(at, min(COLUMNS_STEP, width - at)) for at in range(0, width, COLUMNS_STEP)]
     small = [
@@ -60,14 +60,17 @@
         pltpu.make_async_copy(
             bins_ref.at[:, pl.ds(at, size)], packed_hbm.at[:, pl.ds(at, size)], out_sems.at[i]
         )
-        for i, (at, size) in enumerate([*spans, (width, LANES)])
-    ]
-    routed_store = pltpu.make_async_copy(routed_ref, routed_hbm, small_sems.at[2])
+        for i, (at, size) in enumerate(spans)
+    ]
+    small_stores = [
+        pltpu.make_async_copy(routed_ref, routed_hbm, small_sems.at[2]),
+        pltpu.make_async_copy(labels_ref, labels_hbm, small_sems.at[3]),
+    ]
     for copy in [*small, *loads]:
         copy.start()
     for copy in small:
         copy.wait()
-    routed, label = routing(owners, slot_count, held, slots_ref[...], ids_ref[...])
+    routed, local = routing(owners, slot_count, held, slots_ref[...], ids_ref[...])
     for load, store, (at, size) in zip(loads, stores, spans):
         load.wait()
         bins_ref[:, at : at + size] = jnp.dot(
@@ -75,15 +78,13 @@
         ).astype(bins_ref.dtype)
         store.start()
         if at == 0:
-            bins_ref[:, width:] = jnp.broadcast_to(label, (label.shape[0], LANES)).astype(
-                bins_ref.dtype
-            )
-            stores[-1].start()
-            routed_ref[...] = jnp.transpose(routed.astype(jnp.float32)).astype(routed_ref.dtype)
-            routed_store.start()
-    for store in stores:
-        store.wait()
-    routed_store.wait()
+            turned = jnp.transpose(routed.astype(jnp.float32)).astype(routed_ref.dtype)
+            routed_ref[...] = turned
+            labels_ref[...] = jnp.dot(local, turned, preferred_element_type=jnp.float32)
+            for copy in small_stores:
+                copy.start()
+    for copy in [*stores, *small_stores]:
+        copy.wait()
 
 
 def pack(hidden, adapter_id, adapter_slot, owners, slot_count, held):
@@ -94,36 +95,50 @@
     return pl.pallas_call(
         functools.partial(pack_kernel, owners, slot_count, held),
         in_specs=[pl.BlockSpec(memory_space=pl.ANY)] * 3,
-        out_specs=[pl.BlockSpec(memory_space=pl.ANY)] * 2,
+        out_specs=[pl.BlockSpec(memory_space=pl.ANY)] * 3,
         out_shape=[
-            jax.ShapeDtypeStruct((bins, width + LANES), hidden.dtype),
+            jax.ShapeDtypeStruct((bins, width), hidden.dtype),
             jax.ShapeDtypeStruct((rows, bins), jnp.bfloat16),
+            jax.ShapeDtypeStruct((1, bins), jnp.float32),
         ],
         scratch_shapes=[
             pltpu.VMEM(slots.shape, jnp.int32),
             pltpu.VMEM((1, rows), jnp.int32),
             pltpu.VMEM((rows, width), hidden.dtype),
-            pltpu.VMEM((bins, width + LANES), hidden.dtype),
+            pltpu.VMEM((bins, width), hidden.dtype),
             pltpu.VMEM((rows, bins), jnp.bfloat16),
-            pltpu.SemaphoreType.DMA((3,)),
+            pltpu.VMEM((1, bins), jnp.float32),
+            pltpu.SemaphoreType.DMA((4,)),
             pltpu.SemaphoreType.DMA((steps,)),
-            pltpu.SemaphoreType.DMA((steps + 1,)),
+            pltpu.SemaphoreType.DMA((steps,)),
         ],
         compiler_params=pltpu.CompilerParams(vmem_limit_bytes=56 * 2**20),
         name="pack",
     )(slots, adapter_id.reshape(1, rows), hidden)
 
 
-def adapt_kernel(arrived_ref, a_ref, b_ref, _, change_ref):
+def adapt_kernel(slot_count, arrived_ref, labels_ref, a_ref, b_ref, change_ref):
     width = a_ref.shape[0]
-    low = jnp.zeros((arrived_ref.shape[0], a_ref.shape[1]), jnp.float32)
+    bins = arrived_ref.shape[0]
+    owners = labels_ref.shape[0]
+    source = lax.broadcasted_iota(jnp.int32, (bins, owners), 0) // slot_count
+    named = source == lax.broadcasted_iota(jnp.int32, (bins, owners), 1)
+    labels = jnp.dot(
+        named.astype(jnp.bfloat16),
+        labels_ref[...].astype(jnp.bfloat16),
+        preferred_element_type=jnp.float32,
+    )
+    line = lax.broadcasted_iota(jnp.int32, (bins, bins), 0)
+    mine = lax.rem(line, slot_count) + lax.axis_index("owner") * slot_count
+    mine = mine == lax.broadcasted_iota(jnp.int32, (bins, bins), 1)
+    label = jnp.sum(jnp.where(mine, labels, 0.0), axis=1, keepdims=True).astype(jnp.int32)
+    low = jnp.zeros((bins, a_ref.shape[1]), jnp.float32)
     for at in range(0, width, COLUMNS_STEP):
         low += jnp.dot(
             arrived_ref[:, at : at + COLUMNS_STEP],
             a_ref[at : at + COLUMNS_STEP, :],
             preferred_element_type=jnp.float32,
         )
-    label = arrived_ref[:, width:].astype(jnp.float32)[:, :1].astype(jnp.int32)
     column = lax.broadcasted_iota(jnp.int32, low.shape, 1) // RANK
     low = jnp.where(column == label, low, 0.0).astype(jnp.bfloat16)
     out_width = b_ref.shape[1]
@@ -134,15 +149,15 @@
         ).astype(change_ref.dtype)
 
 
-def adapt(arrived, a_maps, b_maps, after):
+def adapt(arrived, labels, a_maps, b_maps, slot_count):
     return pl.pallas_call(
-        adapt_kernel,
-        in_specs=[pl.BlockSpec(memory_space=pltpu.VMEM)] * 3 + [pl.BlockSpec(memory_space=pl.ANY)],
+        functools.partial(adapt_kernel, slot_count),
+        in_specs=[pl.BlockSpec(memory_space=pltpu.VMEM)] * 4,
         out_specs=pl.BlockSpec(memory_space=pltpu.VMEM),
         out_shape=jax.ShapeDtypeStruct((arrived.shape[0], b_maps.shape[1]), jnp.bfloat16),
-        compiler_params=pltpu.CompilerParams(vmem_limit_bytes=GRANT),
+        compiler_params=pltpu.CompilerParams(vmem_limit_bytes=16 * 2**20),
         name="adapt",
-    )(arrived, a_maps, b_maps, after)
+    )(arrived, labels, a_maps, b_maps)
 
 
 def tall(rows, group):
@@ -185,7 +200,7 @@
             jax.ShapeDtypeStruct((KVH, HEAD, rows * context), jnp.bfloat16),
             jax.ShapeDtypeStruct((KVH, length, HEAD), jnp.bfloat16),
         ],
-        compiler_params=pltpu.CompilerParams(vmem_limit_bytes=GRANT),
+        compiler_params=pltpu.CompilerParams(vmem_limit_bytes=60 * 2**20),
         name="prep",
     )(base_q, kv_cache)
 
@@ -278,11 +293,12 @@
     held = a_maps.shape[1] // RANK
     slot_count = max(2, 2 * ((rows + 2 * owners - 1) // (2 * owners)))
     bins = owners * slot_count
-    packed, routed = pack(hidden, adapter_id, adapter_slot, owners, slot_count, held)
+    packed, routed, labels = pack(hidden, adapter_id, adapter_slot, owners, slot_count, held)
     packed = packed.reshape(owners, slot_count, packed.shape[1])
     arrived = lax.all_to_all(packed, "owner", split_axis=0, concat_axis=0, tiled=True)
+    labels = lax.all_gather(labels, "owner", axis=0, tiled=True)
     keys, rest = prep(base_q, kv_cache)
-    change = adapt(arrived.reshape(bins, arrived.shape[2]), a_maps, b_maps, rest)
+    change = adapt(arrived.reshape(bins, arrived.shape[2]), labels, a_maps, b_maps, slot_count)
     change = change.reshape(owners, slot_count, change.shape[1])
     returned = lax.all_to_all(change, "owner", split_axis=0, concat_axis=0, tiled=True)
     returned = returned.reshape(bins, returned.shape[2])

time: 100 us -> 109 us (1.090)
  blocking collectives: 0 us -> 50.2 us
  waiting for transfers between devices: 52 us -> 11.1 us
  Pallas kernels: 24.6 us -> 23.4 us
    all_gather x0 -> x1, blocking collectives: none -> 50.2 us  [on_device(): labels = lax.all_gather(labels, 'owner', axis=0, tiled=True)]
    all_to_all x1, waiting for transfers between devices: 29.3 us -> 0.01 us  [on_device(): lax.all_to_all(packed, 'owner', split_axis=0, concat_axis=0, tiled=True)]
    all_to_all x1, waiting for transfers between devices: 22.7 us -> 11.1 us  [on_device(): lax.all_to_all(change, 'owner', split_axis=0, concat_axis=0, tiled=True)]
    pallas_call x1, Pallas kernels: 3.67 us -> 2.05 us  [adapt(): pl.pallas_call(functools.partial(adapt_kernel, slot_count), in_specs=[pl....]
    unnamed x14 -> x12, local copies, waits for them, and re-layouts: 2.6 us -> 3.2 us
  transfers between devices with their start and end apart: 2 -> 2, of which waited for: 2 -> 1; matrix products, arithmetic and copies ran while one was open for 0% -> 0% of each run, Pallas kernels for 11% -> 11%
where the time goes in v13:
time: 109 us; the launch traced here: 107 us
  blocking collectives  50.2 us (46%)
  Pallas kernels  23.4 us (21%)
  starting transfers between devices  19.1 us (18%)
  waiting for transfers between devices  11.1 us (10%)
  local copies, waits for them, and re-layouts  3.47 us (3%)
    all_gather x1, blocking collectives, on_device(): labels = lax.all_gather(labels, 'owner', axis=0, tiled=True)  50.2 us
    all_to_all x1, starting transfers between devices, on_device(): lax.all_to_all(change, 'owner', split_axis=0, concat_axis=0, tiled=True)  11.6 us
    pallas_call x1, Pallas kernels, prep(): pl.pallas_call(functools.partial(prep_kernel, group), grid=(steps,), in_s...  11.5 us
    all_to_all x1, waiting for transfers between devices, on_device(): lax.all_to_all(change, 'owner', split_axis=0, concat_axis=0, tiled=True)  11.1 us
    all_to_all x1, starting transfers between devices, on_device(): lax.all_to_all(packed, 'owner', split_axis=0, concat_axis=0, tiled=True)  7.49 us
    pallas_call x1, Pallas kernels, attend(): pl.pallas_call(functools.partial(attend_kernel, group, context), in_specs...  5.67 us
    pallas_call x1, Pallas kernels, pack(): pl.pallas_call(functools.partial(pack_kernel, owners, slot_count, held),...  4.18 us
    unnamed x12, local copies, waits for them, and re-layouts  3.2 us
  transfers between devices with their start and end apart: 2, of which 1 were waited for; matrix products, arithmetic and copies ran while one was open for 0% of the time, Pallas kernels for 11%

profile of v13, /device:TPU:0, one launch (start us, length us, event | category | flops | bytes accessed | tf_op | source)
XLA Modules:
  0.0 107.4 jit_solution(7227762901589514229)
XLA Ops:
  0.0 4.2 %pack.1 = (bf16[128,8192]{1,0:T(8,128)(2,1)}, bf16[128,128]{1,0:T(8,128)(2,1)}, f32[1,128]{1,0:T(1,128)}) custom-call(s32[1,32]{1,0:T(1,128)} %bitcast.13, s32[1,128]{1,0:T(1,128)} %bitcast.14, bf16[128,8192]{1,0:T(8,128)(2,1)} %hidden_hbm.1), custom_call_target="tpu_custom_call" | custom-call | tf_op jit(solution)/shard_map/pack/pallas_call | solution.py:95
  4.2 0.0 copy-start.5
  4.2 0.0 copy-start.2
  4.2 7.5 %all-to-all-start = ((bf16[16,8,8192]{2,1,0:T(8,128)(2,1)}), bf16[16,8,8192]{2,1,0:T(8,128)(2,1)S(1)}, u32[]{:S(2)}, u32[]{:S(2)}) async-start(bf16[16,8,8192]{2,1,0:T(8,128)(2,1)} %bitcast.11), calls=%async_computation | async-start | bytes 4194304 | tf_op jit(solution)/shard_map/all_to_all | solution.py:298
  11.7 0.0 copy-done.5
  11.7 50.2 %all-gather = f32[16,1,128]{2,1,0:T(1,128)S(1)} all-gather(f32[1,1,128]{2,1,0:T(1,128)S(1)} %bitcast.12), channel_id=1, replica_groups=mesh['groups'=2,'owner'=16] {'owner'}, dimensions={0}, use_global_device_ids=true | all-gather | bytes 8704 | tf_op jit(solution)/shard_map/all_gather | solution.py:299
  61.9 0.0 all-to-all-done
  61.9 0.0 copy-done.2
  61.9 0.0 copy-start.1
  61.9 1.6 %copy-done.1 = bf16[8192,128]{1,0:T(8,128)(2,1)S(1)} copy-done((bf16[8192,128]{1,0:T(8,128)(2,1)S(1)}, bf16[8192,128]{1,0:T(8,128)(2,1)}, u32[]{:S(2)}) %copy-start.1) | copy-done | bytes 2097176
  63.5 2.0 %adapt.1 = bf16[128,4096]{1,0:T(8,128)(2,1)} custom-call(bf16[128,8192]{1,0:T(8,128)(2,1)S(1)} %bitcast.8, f32[16,128]{1,0:T(8,128)S(1)} %bitcast.10, bf16[8192,128]{1,0:T(8,128)(2,1)S(1)} %copy-done.1, bf16[128,4096]{1,0:T(8,128)(2,1)S(1)} %copy-done.2), custom_call_target="tpu_custom_call" | custom-call | tf_op jit(solution)/shard_map/adapt/pallas_call | solution.py:153
  65.6 0.0 copy-start.4
  65.6 11.6 %all-to-all-start.1 = ((bf16[16,8,4096]{2,1,0:T(8,128)(2,1)}), bf16[16,8,4096]{2,1,0:T(8,128)(2,1)S(1)}, u32[]{:S(2)}, u32[]{:S(2)}) async-start(bf16[16,8,4096]{2,1,0:T(8,128)(2,1)} %bitcast.6), calls=%async_computation.1 | async-start | bytes 2097152 | tf_op jit(solution)/shard_map/all_to_all | solution.py:303
  77.2 0.0 copy-done.4
  77.2 0.1 broadcast_in_dim.7
  77.3 0.1 broadcast_in_dim.8
  77.4 0.1 broadcast_in_dim.9.lens_ref
  77.5 0.0 copy-start.3
  77.5 11.5 %prep.1 = (bf16[4,128,2048]{2,1,0:T(8,128)(2,1)}, bf16[4,17472,128]{2,1,0:T(8,128)(2,1)}) custom-call(bf16[128,4096]{1,0:T(8,128)(2,1)} %base_ref.1, bf16[128,2,16,512]{3,2,1,0:T(8,128)(2,1)} %kv_ref.1), custom_call_target="tpu_custom_call" | custom-call | tf_op jit(solution)/shard_map/prep/pallas_call | solution.py:188
  89.0 11.1 %all-to-all-done.1 = bf16[16,8,4096]{2,1,0:T(8,128)(2,1)S(1)} async-done(((bf16[16,8,4096]{2,1,0:T(8,128)(2,1)}), bf16[16,8,4096]{2,1,0:T(8,128)(2,1)S(1)}, u32[]{:S(2)}, u32[]{:S(2)}) %all-to-all-start.1) | async-done | bytes 1048608 | tf_op jit(solution)/shard_map/all_to_all | solution.py:303
  100.1 0.0 copy-done.3
  100.1 0.0 copy-start
  100.1 1.6 %copy-done = bf16[4,128,2048]{2,1,0:T(8,128)(2,1)S(1)} copy-done((bf16[4,128,2048]{2,1,0:T(8,128)(2,1)S(1)}, bf16[4,128,2048]{2,1,0:T(8,128)(2,1)}, u32[]{:S(2)}) %copy-start) | copy-done | bytes 2097176
  101.7 5.7 %attend.1 = bf16[128,4096]{1,0:T(8,128)(2,1)} custom-call(bf16[128,128]{1,0:T(8,128)(2,1)S(1)} %copy-done.3, bf16[128,4096]{1,0:T(8,128)(2,1)S(1)} %bitcast.9, bf16[4,128,2048]{2,1,0:T(8,128)(2,1)S(1)} %copy-done, s32[16,1,128]{2,1,0:T(1,128)S(1)} %broadcast_in_dim.9.lens_ref, bf16[4,17472,128]{2,1,0:T(8,128)(2,1)} %get-tuple-element.14.rest_hbm), custom_call_target="tpu_custom_call" | custom-call | tf_op jit(solution)/shard_map/attend/pallas_call | solution.py:274
Async XLA Ops:
  4.2 7.5 %copy-start.5 = (f32[1,128]{1,0:T(1,128)S(1)}, f32[1,128]{1,0:T(1,128)}, u32[]{:S(2)}) copy-start(f32[1,128]{1,0:T(1,128)} %get-tuple-element.12) | copy-start | bytes 1540
  4.2 57.7 %copy-start.2 = (bf16[128,4096]{1,0:T(8,128)(2,1)S(1)}, bf16[128,4096]{1,0:T(8,128)(2,1)}, u32[]{:S(2)}) copy-start(bf16[128,4096]{1,0:T(8,128)(2,1)} %b_ref.1) | copy-start | bytes 3145732
  4.2 57.7 %all-to-all-start = ((bf16[16,8,8192]{2,1,0:T(8,128)(2,1)}), bf16[16,8,8192]{2,1,0:T(8,128)(2,1)S(1)}, u32[]{:S(2)}, u32[]{:S(2)}) async-start(bf16[16,8,8192]{2,1,0:T(8,128)(2,1)} %bitcast.11), calls=%async_computation | async-start | bytes 4194304 | tf_op jit(solution)/shard_map/all_to_all | solution.py:298
  61.9 1.6 %copy-start.1 = (bf16[8192,128]{1,0:T(8,128)(2,1)S(1)}, bf16[8192,128]{1,0:T(8,128)(2,1)}, u32[]{:S(2)}) copy-start(bf16[8192,128]{1,0:T(8,128)(2,1)} %a_ref.1) | copy-start | bytes 6291460
  65.6 11.6 %copy-start.4 = (s32[128]{0:T(128)S(1)}, s32[128]{0:T(128)}, u32[]{:S(2)}) copy-start(s32[128]{0:T(128)} %param.11) | copy-start | bytes 1540
  65.6 34.6 %all-to-all-start.1 = ((bf16[16,8,4096]{2,1,0:T(8,128)(2,1)}), bf16[16,8,4096]{2,1,0:T(8,128)(2,1)S(1)}, u32[]{:S(2)}, u32[]{:S(2)}) async-start(bf16[16,8,4096]{2,1,0:T(8,128)(2,1)} %bitcast.6), calls=%async_computation.1 | async-start | bytes 2097152 | tf_op jit(solution)/shard_map/all_to_all | solution.py:303
  77.5 22.7 %copy-start.3 = (bf16[128,128]{1,0:T(8,128)(2,1)S(1)}, bf16[128,128]{1,0:T(8,128)(2,1)}, u32[]{:S(2)}) copy-start(bf16[128,128]{1,0:T(8,128)(2,1)} %get-tuple-element.10.routed_ref) | copy-start | bytes 98308
  100.1 1.6 %copy-start = (bf16[4,128,2048]{2,1,0:T(8,128)(2,1)S(1)}, bf16[4,128,2048]{2,1,0:T(8,128)(2,1)}, u32[]{:S(2)}) copy-start(bf16[4,128,2048]{2,1,0:T(8,128)(2,1)} %get-tuple-element.13.keys_ref) | copy-start | bytes 6291460

commit v14 on v10

--- a/solution.py
+++ b/solution.py
@@ -14,6 +14,8 @@
 SCALE = 2.0
 ROWS_STEP = 8
 COLUMNS_STEP = 1024
+ADAPT_STEP = 1024
+OUT_STEP = 1024
 GRANT = 48 * 2**20
 TALL_BYTES = 17 * 2**20
 
@@ -114,32 +116,60 @@
     )(slots, adapter_id.reshape(1, rows), hidden)
 
 
-def adapt_kernel(arrived_ref, a_ref, b_ref, _, change_ref):
+def adapt_kernel(arrived_hbm, a_ref, b_ref, _, change_hbm, arrived_ref, change_ref, sems, out_sems):
     width = a_ref.shape[0]
+    spans = [(at, min(ADAPT_STEP, width - at)) for at in range(0, width, ADAPT_STEP)]
+    spans[-1] = (spans[-1][0], spans[-1][1] + LANES)
+    loads = [
+        pltpu.make_async_copy(
+            arrived_hbm.at[:, pl.ds(at, size)], arrived_ref.at[:, pl.ds(at, size)], sems.at[i]
+        )
+        for i, (at, size) in enumerate(spans)
+    ]
+    for load in loads:
+        load.start()
     low = jnp.zeros((arrived_ref.shape[0], a_ref.shape[1]), jnp.float32)
-    for at in range(0, width, COLUMNS_STEP):
+    for load, (at, size) in zip(loads, spans):
+        load.wait()
+        end = min(at + size, width)
         low += jnp.dot(
-            arrived_ref[:, at : at + COLUMNS_STEP],
-            a_ref[at : at + COLUMNS_STEP, :],
-            preferred_element_type=jnp.float32,
+            arrived_ref[:, at:end], a_ref[at:end, :], preferred_element_type=jnp.float32
         )
     label = arrived_ref[:, width:].astype(jnp.float32)[:, :1].astype(jnp.int32)
     column = lax.broadcasted_iota(jnp.int32, low.shape, 1) // RANK
     low = jnp.where(column == label, low, 0.0).astype(jnp.bfloat16)
-    out_width = b_ref.shape[1]
-    piece = min(1024, out_width)
-    for at in range(0, out_width, piece):
-        change_ref[:, at : at + piece] = (
-            SCALE * jnp.dot(low, b_ref[:, at : at + piece], preferred_element_type=jnp.float32)
+    stores = []
+    for i, at in enumerate(range(0, b_ref.shape[1], OUT_STEP)):
+        span = pl.ds(at, OUT_STEP)
+        change_ref[:, at : at + OUT_STEP] = (
+            SCALE * jnp.dot(low, b_ref[:, at : at + OUT_STEP], preferred_element_type=jnp.float32)
         ).astype(change_ref.dtype)
+        stores.append(
+            pltpu.make_async_copy(change_ref.at[:, span], change_hbm.at[:, span], out_sems.at[i])
+        )
+        stores[-1].start()
+    for store in stores:
+        store.wait()
 
 
 def adapt(arrived, a_maps, b_maps, after):
+    change = jax.ShapeDtypeStruct((arrived.shape[0], b_maps.shape[1]), jnp.bfloat16)
     return pl.pallas_call(
         adapt_kernel,
-        in_specs=[pl.BlockSpec(memory_space=pltpu.VMEM)] * 3 + [pl.BlockSpec(memory_space=pl.ANY)],
-        out_specs=pl.BlockSpec(memory_space=pltpu.VMEM),
-        out_shape=jax.ShapeDtypeStruct((arrived.shape[0], b_maps.shape[1]), jnp.bfloat16),
+        in_specs=[
+            pl.BlockSpec(memory_space=pl.ANY),
+            pl.BlockSpec(memory_space=pltpu.VMEM),
+            pl.BlockSpec(memory_space=pltpu.VMEM),
+            pl.BlockSpec(memory_space=pl.ANY),
+        ],
+        out_specs=pl.BlockSpec(memory_space=pl.ANY),
+        out_shape=change,
+        scratch_shapes=[
+            pltpu.VMEM(arrived.shape, arrived.dtype),
+            pltpu.VMEM(change.shape, change.dtype),
+            pltpu.SemaphoreType.DMA((pl.cdiv(a_maps.shape[0], ADAPT_STEP),)),
+            pltpu.SemaphoreType.DMA((pl.cdiv(b_maps.shape[1], OUT_STEP),)),
+        ],
         compiler_params=pltpu.CompilerParams(vmem_limit_bytes=GRANT),
         name="adapt",
     )(arrived, a_maps, b_maps, after)
@@ -156,9 +186,9 @@
         head = slice(k * HEAD, (k + 1) * HEAD)
         keys = kv_ref[:, 0, :, head].astype(jnp.float32).reshape(cells, HEAD)
         keys_ref[k] = jnp.transpose(keys).astype(keys_ref.dtype)
-        rest_ref[k, :cells] = kv_ref[:, 1, :, head].reshape(cells, HEAD)
+        rest_ref[k, 0, :cells] = kv_ref[:, 1, :, head].reshape(cells, HEAD)
         base = base_ref[:, k * group * HEAD : (k + 1) * group * HEAD].astype(jnp.float32)
-        rest_ref[k, cells:] = tall(base, group).astype(rest_ref.dtype)
+        rest_ref[k, 0, cells:] = tall(base, group).astype(rest_ref.dtype)
 
 
 def prep(base_q, kv_cache):
@@ -169,7 +199,7 @@
     steps = rows // step
     cells = step * context
     lines = cells + group * step
-    length = pl.cdiv(max(TALL_BYTES // (2 * KVH * HEAD), steps * lines), lines) * lines
+    length = max(pl.cdiv(TALL_BYTES, 2 * KVH * lines * HEAD), steps)
     return pl.pallas_call(
         functools.partial(prep_kernel, group),
         grid=(steps,),
@@ -179,39 +209,45 @@
         ],
         out_specs=[
             pl.BlockSpec((KVH, HEAD, cells), lambda i: (0, 0, i)),
-            pl.BlockSpec((KVH, lines, HEAD), lambda i: (0, i, 0)),
+            pl.BlockSpec((KVH, 1, lines, HEAD), lambda i: (0, i, 0, 0)),
         ],
         out_shape=[
             jax.ShapeDtypeStruct((KVH, HEAD, rows * context), jnp.bfloat16),
-            jax.ShapeDtypeStruct((KVH, length, HEAD), jnp.bfloat16),
-        ],
-        compiler_params=pltpu.CompilerParams(vmem_limit_bytes=GRANT),
+            jax.ShapeDtypeStruct((KVH, length, lines, HEAD), jnp.bfloat16),
+        ],
+        compiler_params=pltpu.CompilerParams(vmem_limit_bytes=60 * 2**20),
         name="prep",
     )(base_q, kv_cache)
 
 
 def attend_kernel(
-    group, context, routed_ref, returned_ref, keys_ref, lens_ref, rest_hbm, out_hbm, rest_ref, bias_ref, out_ref, sems
+    group, context, routed_ref, returned_ref, keys_ref, lens_ref, rest_hbm, out_hbm, *scratch
 ):
+    query_ref, values_ref, bias_ref, out_ref, sems = scratch
     step = ROWS_STEP
     steps, lines, cells = bias_ref.shape
-    block = cells + lines
     span = group * HEAD
     factor = 1.0 / jnp.sqrt(jnp.float32(HEAD))
     loads = [
-        pltpu.make_async_copy(
-            rest_hbm.at[k, pl.ds(0, steps * block)], rest_ref.at[k], sems.at[k, 0]
-        )
+        [
+            pltpu.make_async_copy(
+                rest_hbm.at[k, pl.ds(0, steps), pl.ds(cells, lines)], query_ref.at[k], sems.at[k, 1]
+            ),
+            pltpu.make_async_copy(
+                rest_hbm.at[k, pl.ds(0, steps), pl.ds(0, cells)], values_ref.at[k], sems.at[k, 2]
+            ),
+        ]
         for k in range(KVH)
     ]
     stores = [
         pltpu.make_async_copy(
-            out_ref.at[:, pl.ds(k * span, span)], out_hbm.at[:, pl.ds(k * span, span)], sems.at[k, 1]
+            out_ref.at[:, pl.ds(k * span, span)], out_hbm.at[:, pl.ds(k * span, span)], sems.at[k, 0]
         )
         for k in range(KVH)
     ]
     for load in loads:
-        load.start()
+        for copy in load:
+            copy.start()
     lane = lax.broadcasted_iota(jnp.int32, (lines, cells), 1)
     line = lax.broadcasted_iota(jnp.int32, (lines, cells), 0)
     own = lax.div(lane, context) == lax.rem(line, step)
@@ -224,22 +260,23 @@
             returned_ref[:, k * span : (k + 1) * span],
             preferred_element_type=jnp.float32,
         )
-        loads[k].wait()
+        for copy in loads[k]:
+            copy.wait()
         for i in range(steps):
             rows = slice(i * step, (i + 1) * step)
             keys = keys_ref[k, :, i * cells : (i + 1) * cells]
-            values = rest_ref[k, i * block : i * block + cells, :]
-            query = rest_ref[k, i * block + cells : (i + 1) * block, :]
             change = tall(delta[rows], group).astype(jnp.bfloat16)
             scores = jnp.dot(
-                jnp.concatenate([query, change], axis=1),
+                jnp.concatenate([query_ref[k, i], change], axis=1),
                 jnp.concatenate([keys, keys], axis=0),
                 preferred_element_type=jnp.float32,
             )
             scores = scores * factor + bias_ref[i]
             expo = jnp.exp(scores - jnp.max(scores, axis=1, keepdims=True))
             probs = expo * (1.0 / jnp.sum(expo, axis=1, keepdims=True))
-            out = jnp.dot(probs.astype(jnp.bfloat16), values, preferred_element_type=jnp.float32)
+            out = jnp.dot(
+                probs.astype(jnp.bfloat16), values_ref[k, i], preferred_element_type=jnp.float32
+            )
             for g in range(group):
                 out_ref[rows, (k * group + g) * HEAD : (k * group + g + 1) * HEAD] = out[
                     g * step : (g + 1) * step
@@ -262,10 +299,11 @@
         out_specs=pl.BlockSpec(memory_space=pl.ANY),
         out_shape=jax.ShapeDtypeStruct((rows, width), jnp.bfloat16),
         scratch_shapes=[
-            pltpu.VMEM((KVH, steps * (cells + group * step), HEAD), rest.dtype),
+            pltpu.VMEM((KVH, steps, group * step, HEAD), rest.dtype),
+            pltpu.VMEM((KVH, steps, cells, HEAD), rest.dtype),
             pltpu.VMEM((steps, group * step, cells), jnp.float32),
             pltpu.VMEM((rows, width), jnp.bfloat16),
-            pltpu.SemaphoreType.DMA((KVH, 2)),
+            pltpu.SemaphoreType.DMA((KVH, 3)),
         ],
         compiler_params=pltpu.CompilerParams(vmem_limit_bytes=GRANT),
         name="attend",

time: 100 us -> 99.1 us (level)
  local copies, waits for them, and re-layouts: 2.86 us -> 0.29 us
    unnamed x14 -> x10, local copies, waits for them, and re-layouts: 2.6 us -> 0.02 us
  transfers between devices with their start and end apart: 2 -> 2, of which waited for: 2 -> 2; matrix products, arithmetic and copies ran while one was open for 0% -> 0% of each run, Pallas kernels for 11% -> 12%
where the time goes in v14:
time: 99.1 us; the launch traced here: 97.5 us
  waiting for transfers between devices  52.7 us (53%)
  Pallas kernels  25.5 us (26%)
  starting transfers between devices  18.9 us (19%)
    all_to_all x1, waiting for transfers between devices, on_device(): lax.all_to_all(packed, 'owner', split_axis=0, concat_axis=0, tiled=True)  30 us
    all_to_all x1, waiting for transfers between devices, on_device(): lax.all_to_all(change, 'owner', split_axis=0, concat_axis=0, tiled=True)  22.7 us
    pallas_call x1, Pallas kernels, prep(): pl.pallas_call(functools.partial(prep_kernel, group), grid=(steps,), in_s...  11.7 us
    all_to_all x1, starting transfers between devices, on_device(): lax.all_to_all(change, 'owner', split_axis=0, concat_axis=0, tiled=True)  11.5 us
    all_to_all x1, starting transfers between devices, on_device(): lax.all_to_all(packed, 'owner', split_axis=0, concat_axis=0, tiled=True)  7.43 us
    pallas_call x1, Pallas kernels, attend(): pl.pallas_call(functools.partial(attend_kernel, group, context), in_specs...  5.72 us
    pallas_call x1, Pallas kernels, pack(): pl.pallas_call(functools.partial(pack_kernel, owners, slot_count, held),...  4.22 us
    pallas_call x1, Pallas kernels, adapt(): pl.pallas_call(adapt_kernel, in_specs=[pl.BlockSpec(memory_space=pl.ANY),...  3.89 us
  transfers between devices with their start and end apart: 2, of which 2 were waited for; matrix products, arithmetic and copies ran while one was open for 0% of the time, Pallas kernels for 12%

profile of v14, /device:TPU:0, one launch (start us, length us, event | category | flops | bytes accessed | tf_op | source)
XLA Modules:
  0.0 97.5 jit_solution(15938848058476129861)
XLA Ops:
  0.0 4.2 %pack.1 = (bf16[128,8320]{1,0:T(8,128)(2,1)}, bf16[128,128]{1,0:T(8,128)(2,1)}) custom-call(s32[1,32]{1,0:T(1,128)} %bitcast.8, s32[1,128]{1,0:T(1,128)} %bitcast.9, bf16[128,8192]{1,0:T(8,128)(2,1)} %hidden_hbm.1), custom_call_target="tpu_custom_call" | custom-call | tf_op jit(solution)/shard_map/pack/pallas_call | solution.py:96
  4.2 7.4 %all-to-all-start = ((bf16[16,8,8320]{2,1,0:T(8,128)(2,1)}), bf16[16,8,8320]{2,1,0:T(8,128)(2,1)}, u32[]{:S(2)}, u32[]{:S(2)}) async-start(bf16[16,8,8320]{2,1,0:T(8,128)(2,1)} %bitcast.7), calls=%async_computation | async-start | bytes 4259840 | tf_op jit(solution)/shard_map/all_to_all | solution.py:321
  11.7 0.0 copy-start
  11.7 0.0 copy-start.2
  11.7 11.7 %prep.1 = (bf16[4,128,2048]{2,1,0:T(8,128)(2,1)}, bf16[4,91,192,128]{3,2,1,0:T(8,128)(2,1)}) custom-call(bf16[128,4096]{1,0:T(8,128)(2,1)} %base_ref.1, bf16[128,2,16,512]{3,2,1,0:T(8,128)(2,1)} %kv_ref.1), custom_call_target="tpu_custom_call" | custom-call | tf_op jit(solution)/shard_map/prep/pallas_call | solution.py:203
  23.4 30.0 %all-to-all-done = bf16[16,8,8320]{2,1,0:T(8,128)(2,1)} async-done(((bf16[16,8,8320]{2,1,0:T(8,128)(2,1)}), bf16[16,8,8320]{2,1,0:T(8,128)(2,1)}, u32[]{:S(2)}, u32[]{:S(2)}) %all-to-all-start) | async-done | bytes 2129952 | tf_op jit(solution)/shard_map/all_to_all | solution.py:321
  53.4 0.0 copy-done
  53.4 0.0 copy-done.2
  53.4 0.0 copy-start.4
  53.4 3.9 %adapt.1 = bf16[128,4096]{1,0:T(8,128)(2,1)} custom-call(bf16[128,8320]{1,0:T(8,128)(2,1)} %bitcast.3.arrived_hbm, bf16[8192,128]{1,0:T(8,128)(2,1)S(1)} %copy-done, bf16[128,4096]{1,0:T(8,128)(2,1)S(1)} %copy-done.2, bf16[4,91,192,128]{3,2,1,0:T(8,128)(2,1)} %get-tuple-element.11._.rest_hbm), custom_call_target="tpu_custom_call" | custom-call | tf_op jit(solution)/shard_map/adapt/pallas_call | solution.py:157
  57.3 0.0 copy-start.1
  57.3 0.0 copy-start.3
  57.3 11.5 %all-to-all-start.1 = ((bf16[16,8,4096]{2,1,0:T(8,128)(2,1)}), bf16[16,8,4096]{2,1,0:T(8,128)(2,1)S(1)}, u32[]{:S(2)}, u32[]{:S(2)}) async-start(bf16[16,8,4096]{2,1,0:T(8,128)(2,1)} %bitcast.4), calls=%async_computation.1 | async-start | bytes 2097152 | tf_op jit(solution)/shard_map/all_to_all | solution.py:325
  68.8 0.0 copy-done.4
  68.8 0.1 broadcast_in_dim.7
  68.9 0.1 broadcast_in_dim.8
  69.0 0.1 broadcast_in_dim.9.lens_ref
  69.1 22.7 %all-to-all-done.1 = bf16[16,8,4096]{2,1,0:T(8,128)(2,1)S(1)} async-done(((bf16[16,8,4096]{2,1,0:T(8,128)(2,1)}), bf16[16,8,4096]{2,1,0:T(8,128)(2,1)S(1)}, u32[]{:S(2)}, u32[]{:S(2)}) %all-to-all-start.1) | async-done | bytes 1048608 | tf_op jit(solution)/shard_map/all_to_all | solution.py:325
  91.8 0.0 copy-done.1
  91.8 0.0 copy-done.3
  91.8 5.7 %attend.1 = bf16[128,4096]{1,0:T(8,128)(2,1)} custom-call(bf16[128,128]{1,0:T(8,128)(2,1)S(1)} %copy-done.3, bf16[128,4096]{1,0:T(8,128)(2,1)S(1)} %bitcast.6, bf16[4,128,2048]{2,1,0:T(8,128)(2,1)S(1)} %copy-done.1, s32[16,1,128]{2,1,0:T(1,128)S(1)} %broadcast_in_dim.9.lens_ref, bf16[4,91,192,128]{3,2,1,0:T(8,128)(2,1)} %get-tuple-element.11._.rest_hbm), custom_call_target="tpu_custom_call" | custom-call | tf_op jit(solution)/shard_map/attend/pallas_call | solution.py:296
Async XLA Ops:
  4.2 49.2 %all-to-all-start = ((bf16[16,8,8320]{2,1,0:T(8,128)(2,1)}), bf16[16,8,8320]{2,1,0:T(8,128)(2,1)}, u32[]{:S(2)}, u32[]{:S(2)}) async-start(bf16[16,8,8320]{2,1,0:T(8,128)(2,1)} %bitcast.7), calls=%async_computation | async-start | bytes 4259840 | tf_op jit(solution)/shard_map/all_to_all | solution.py:321
  11.7 41.7 %copy-start = (bf16[8192,128]{1,0:T(8,128)(2,1)S(1)}, bf16[8192,128]{1,0:T(8,128)(2,1)}, u32[]{:S(2)}) copy-start(bf16[8192,128]{1,0:T(8,128)(2,1)} %a_ref.1) | copy-start | bytes 6291460
  11.7 41.7 %copy-start.2 = (bf16[128,4096]{1,0:T(8,128)(2,1)S(1)}, bf16[128,4096]{1,0:T(8,128)(2,1)}, u32[]{:S(2)}) copy-start(bf16[128,4096]{1,0:T(8,128)(2,1)} %b_ref.1) | copy-start | bytes 3145732
  53.4 15.4 %copy-start.4 = (s32[128]{0:T(128)S(1)}, s32[128]{0:T(128)}, u32[]{:S(2)}) copy-start(s32[128]{0:T(128)} %param.11) | copy-start | bytes 1540
  57.3 34.5 %copy-start.1 = (bf16[4,128,2048]{2,1,0:T(8,128)(2,1)S(1)}, bf16[4,128,2048]{2,1,0:T(8,128)(2,1)}, u32[]{:S(2)}) copy-start(bf16[4,128,2048]{2,1,0:T(8,128)(2,1)} %get-tuple-element.12.keys_ref) | copy-start | bytes 6291460
  57.3 34.4 %copy-start.3 = (bf16[128,128]{1,0:T(8,128)(2,1)S(1)}, bf16[128,128]{1,0:T(8,128)(2,1)}, u32[]{:S(2)}) copy-start(bf16[128,128]{1,0:T(8,128)(2,1)} %get-tuple-element.9.routed_ref) | copy-start | bytes 98308
  57.3 34.4 %all-to-all-start.1 = ((bf16[16,8,4096]{2,1,0:T(8,128)(2,1)}), bf16[16,8,4096]{2,1,0:T(8,128)(2,1)S(1)}, u32[]{:S(2)}, u32[]{:S(2)}) async-start(bf16[16,8,4096]{2,1,0:T(8,128)(2,1)} %bitcast.4), calls=%async_computation.1 | async-start | bytes 2097152 | tf_op jit(solution)/shard_map/all_to_all | solution.py:325

commit v15 on v10

--- a/solution.py
+++ b/solution.py
@@ -14,6 +14,7 @@
 SCALE = 2.0
 ROWS_STEP = 8
 COLUMNS_STEP = 1024
+ADAPT_STEP = 2048
 GRANT = 48 * 2**20
 TALL_BYTES = 17 * 2**20
 
@@ -114,13 +115,13 @@
     )(slots, adapter_id.reshape(1, rows), hidden)
 
 
-def adapt_kernel(arrived_ref, a_ref, b_ref, _, change_ref):
+def adapt_kernel(arrived_ref, a_ref, b_ref, change_ref):
     width = a_ref.shape[0]
     low = jnp.zeros((arrived_ref.shape[0], a_ref.shape[1]), jnp.float32)
-    for at in range(0, width, COLUMNS_STEP):
+    for at in range(0, width, ADAPT_STEP):
         low += jnp.dot(
-            arrived_ref[:, at : at + COLUMNS_STEP],
-            a_ref[at : at + COLUMNS_STEP, :],
+            arrived_ref[:, at : at + ADAPT_STEP],
+            a_ref[at : at + ADAPT_STEP, :],
             preferred_element_type=jnp.float32,
         )
     label = arrived_ref[:, width:].astype(jnp.float32)[:, :1].astype(jnp.int32)
@@ -134,15 +135,15 @@
         ).astype(change_ref.dtype)
 
 
-def adapt(arrived, a_maps, b_maps, after):
+def adapt(arrived, a_maps, b_maps):
     return pl.pallas_call(
         adapt_kernel,
-        in_specs=[pl.BlockSpec(memory_space=pltpu.VMEM)] * 3 + [pl.BlockSpec(memory_space=pl.ANY)],
+        in_specs=[pl.BlockSpec(memory_space=pltpu.VMEM)] * 3,
         out_specs=pl.BlockSpec(memory_space=pltpu.VMEM),
         out_shape=jax.ShapeDtypeStruct((arrived.shape[0], b_maps.shape[1]), jnp.bfloat16),
-        compiler_params=pltpu.CompilerParams(vmem_limit_bytes=GRANT),
+        compiler_params=pltpu.CompilerParams(vmem_limit_bytes=16 * 2**20),
         name="adapt",
-    )(arrived, a_maps, b_maps, after)
+    )(arrived, a_maps, b_maps)
 
 
 def tall(rows, group):
@@ -156,9 +157,9 @@
         head = slice(k * HEAD, (k + 1) * HEAD)
         keys = kv_ref[:, 0, :, head].astype(jnp.float32).reshape(cells, HEAD)
         keys_ref[k] = jnp.transpose(keys).astype(keys_ref.dtype)
-        rest_ref[k, :cells] = kv_ref[:, 1, :, head].reshape(cells, HEAD)
+        rest_ref[k, 0, :cells] = kv_ref[:, 1, :, head].reshape(cells, HEAD)
         base = base_ref[:, k * group * HEAD : (k + 1) * group * HEAD].astype(jnp.float32)
-        rest_ref[k, cells:] = tall(base, group).astype(rest_ref.dtype)
+        rest_ref[k, 0, cells:] = tall(base, group).astype(rest_ref.dtype)
 
 
 def prep(base_q, kv_cache):
@@ -169,7 +170,7 @@
     steps = rows // step
     cells = step * context
     lines = cells + group * step
-    length = pl.cdiv(max(TALL_BYTES // (2 * KVH * HEAD), steps * lines), lines) * lines
+    length = max(pl.cdiv(TALL_BYTES, 2 * KVH * lines * HEAD), steps)
     return pl.pallas_call(
         functools.partial(prep_kernel, group),
         grid=(steps,),
@@ -179,11 +180,11 @@
         ],
         out_specs=[
             pl.BlockSpec((KVH, HEAD, cells), lambda i: (0, 0, i)),
-            pl.BlockSpec((KVH, lines, HEAD), lambda i: (0, i, 0)),
+            pl.BlockSpec((KVH, 1, lines, HEAD), lambda i: (0, i, 0, 0)),
         ],
         out_shape=[
             jax.ShapeDtypeStruct((KVH, HEAD, rows * context), jnp.bfloat16),
-            jax.ShapeDtypeStruct((KVH, length, HEAD), jnp.bfloat16),
+            jax.ShapeDtypeStruct((KVH, length, lines, HEAD), jnp.bfloat16),
         ],
         compiler_params=pltpu.CompilerParams(vmem_limit_bytes=GRANT),
         name="prep",
@@ -191,27 +192,33 @@
 
 
 def attend_kernel(
-    group, context, routed_ref, returned_ref, keys_ref, lens_ref, rest_hbm, out_hbm, rest_ref, bias_ref, out_ref, sems
+    group, context, routed_ref, returned_ref, keys_ref, lens_ref, rest_hbm, out_hbm, *scratch
 ):
+    query_ref, values_ref, bias_ref, scores_ref, probs_ref, out_ref, sems = scratch
     step = ROWS_STEP
     steps, lines, cells = bias_ref.shape
-    block = cells + lines
     span = group * HEAD
     factor = 1.0 / jnp.sqrt(jnp.float32(HEAD))
     loads = [
-        pltpu.make_async_copy(
-            rest_hbm.at[k, pl.ds(0, steps * block)], rest_ref.at[k], sems.at[k, 0]
-        )
+        [
+            pltpu.make_async_copy(
+                rest_hbm.at[k, pl.ds(0, steps), pl.ds(cells, lines)], query_ref.at[k], sems.at[k, 1]
+            ),
+            pltpu.make_async_copy(
+                rest_hbm.at[k, pl.ds(0, steps), pl.ds(0, cells)], values_ref.at[k], sems.at[k, 2]
+            ),
+        ]
         for k in range(KVH)
     ]
     stores = [
         pltpu.make_async_copy(
-            out_ref.at[:, pl.ds(k * span, span)], out_hbm.at[:, pl.ds(k * span, span)], sems.at[k, 1]
+            out_ref.at[:, pl.ds(k * span, span)], out_hbm.at[:, pl.ds(k * span, span)], sems.at[k, 0]
         )
         for k in range(KVH)
     ]
     for load in loads:
-        load.start()
+        for copy in load:
+            copy.start()
     lane = lax.broadcasted_iota(jnp.int32, (lines, cells), 1)
     line = lax.broadcasted_iota(jnp.int32, (lines, cells), 0)
     own = lax.div(lane, context) == lax.rem(line, step)
@@ -224,22 +231,25 @@
             returned_ref[:, k * span : (k + 1) * span],
             preferred_element_type=jnp.float32,
         )
-        loads[k].wait()
+        for copy in loads[k]:
+            copy.wait()
         for i in range(steps):
-            rows = slice(i * step, (i + 1) * step)
             keys = keys_ref[k, :, i * cells : (i + 1) * cells]
-            values = rest_ref[k, i * block : i * block + cells, :]
-            query = rest_ref[k, i * block + cells : (i + 1) * block, :]
-            change = tall(delta[rows], group).astype(jnp.bfloat16)
+            change = tall(delta[i * step : (i + 1) * step], group).astype(jnp.bfloat16)
             scores = jnp.dot(
-                jnp.concatenate([query, change], axis=1),
+                jnp.concatenate([query_ref[k, i], change], axis=1),
                 jnp.concatenate([keys, keys], axis=0),
                 preferred_element_type=jnp.float32,
             )
-            scores = scores * factor + bias_ref[i]
+            scores_ref[k, i] = scores * factor + bias_ref[i]
+        for i in range(steps):
+            scores = scores_ref[k, i]
             expo = jnp.exp(scores - jnp.max(scores, axis=1, keepdims=True))
             probs = expo * (1.0 / jnp.sum(expo, axis=1, keepdims=True))
-            out = jnp.dot(probs.astype(jnp.bfloat16), values, preferred_element_type=jnp.float32)
+            probs_ref[k, i] = probs.astype(probs_ref.dtype)
+        for i in range(steps):
+            rows = slice(i * step, (i + 1) * step)
+            out = jnp.dot(probs_ref[k, i], values_ref[k, i], preferred_element_type=jnp.float32)
             for g in range(group):
                 out_ref[rows, (k * group + g) * HEAD : (k * group + g + 1) * HEAD] = out[
                     g * step : (g + 1) * step
@@ -262,10 +272,13 @@
         out_specs=pl.BlockSpec(memory_space=pl.ANY),
         out_shape=jax.ShapeDtypeStruct((rows, width), jnp.bfloat16),
         scratch_shapes=[
-            pltpu.VMEM((KVH, steps * (cells + group * step), HEAD), rest.dtype),
+            pltpu.VMEM((KVH, steps, group * step, HEAD), rest.dtype),
+            pltpu.VMEM((KVH, steps, cells, HEAD), rest.dtype),
             pltpu.VMEM((steps, group * step, cells), jnp.float32),
+            pltpu.VMEM((KVH, steps, group * step, cells), jnp.float32),
+            pltpu.VMEM((KVH, steps, group * step, cells), jnp.bfloat16),
             pltpu.VMEM((rows, width), jnp.bfloat16),
-            pltpu.SemaphoreType.DMA((KVH, 2)),
+            pltpu.SemaphoreType.DMA((KVH, 3)),
         ],
         compiler_params=pltpu.CompilerParams(vmem_limit_bytes=GRANT),
         name="attend",
@@ -282,7 +295,7 @@
     packed = packed.reshape(owners, slot_count, packed.shape[1])
     arrived = lax.all_to_all(packed, "owner", split_axis=0, concat_axis=0, tiled=True)
     keys, rest = prep(base_q, kv_cache)
-    change = adapt(arrived.reshape(bins, arrived.shape[2]), a_maps, b_maps, rest)
+    change = adapt(arrived.reshape(bins, arrived.shape[2]), a_maps, b_maps)
     change = change.reshape(owners, slot_count, change.shape[1])
     returned = lax.all_to_all(change, "owner", split_axis=0, concat_axis=0, tiled=True)
     returned = returned.reshape(bins, returned.shape[2])

time: 100 us -> 97.6 us (0.976)
  blocking collectives: 0 us -> 58.1 us
  waiting for transfers between devices: 52 us -> 10.5 us
  starting transfers between devices: 19 us -> 3.66 us
  Pallas kernels: 24.6 us -> 22.2 us
  local copies, waits for them, and re-layouts: 2.86 us -> 1.5 us
    all_to_all x0 -> x1, blocking collectives: none -> 58.1 us  [on_device(): lax.all_to_all(packed, 'owner', split_axis=0, concat_axis=0, tiled=True)]
    all_to_all x1 -> x0, waiting for transfers between devices: 29.3 us -> none  [on_device(): lax.all_to_all(packed, 'owner', split_axis=0, concat_axis=0, tiled=True)]
    all_to_all x1, waiting for transfers between devices: 22.7 us -> 10.5 us  [on_device(): lax.all_to_all(change, 'owner', split_axis=0, concat_axis=0, tiled=True)]
    all_to_all x1, starting transfers between devices: 11.5 us -> 3.66 us  [on_device(): lax.all_to_all(change, 'owner', split_axis=0, concat_axis=0, tiled=True)]
    all_to_all x1 -> x0, starting transfers between devices: 7.56 us -> none  [on_device(): lax.all_to_all(packed, 'owner', split_axis=0, concat_axis=0, tiled=True)]
    pallas_call x1, Pallas kernels: 3.67 us -> 2.05 us  [adapt(): pl.pallas_call(adapt_kernel, in_specs=[pl.BlockSpec(memory_space=pltpu.VM...]
    unnamed x14 -> x10, local copies, waits for them, and re-layouts: 2.6 us -> 1.24 us
  transfers between devices with their start and end apart: 2 -> 1, of which waited for: 2 -> 1; matrix products, arithmetic and copies ran while one was open for 0% -> 0% of each run, Pallas kernels for 11% -> 11%
where the time goes in v15:
time: 97.6 us; the launch traced here: 95.9 us
  blocking collectives  58.1 us (60%)
  Pallas kernels  22.2 us (23%)
  waiting for transfers between devices  10.5 us (11%)
  starting transfers between devices  3.66 us (4%)
  local copies, waits for them, and re-layouts  1.5 us (2%)
    all_to_all x1, blocking collectives, on_device(): lax.all_to_all(packed, 'owner', split_axis=0, concat_axis=0, tiled=True)  58.1 us
    pallas_call x1, Pallas kernels, prep(): pl.pallas_call(functools.partial(prep_kernel, group), grid=(steps,), in_s...  10.9 us
    all_to_all x1, waiting for transfers between devices, on_device(): lax.all_to_all(change, 'owner', split_axis=0, concat_axis=0, tiled=True)  10.5 us
    pallas_call x1, Pallas kernels, attend(): pl.pallas_call(functools.partial(attend_kernel, group, context), in_specs...  4.98 us
    pallas_call x1, Pallas kernels, pack(): pl.pallas_call(functools.partial(pack_kernel, owners, slot_count, held),...  4.21 us
    all_to_all x1, starting transfers between devices, on_device(): lax.all_to_all(change, 'owner', split_axis=0, concat_axis=0, tiled=True)  3.66 us
    pallas_call x1, Pallas kernels, adapt(): pl.pallas_call(adapt_kernel, in_specs=[pl.BlockSpec(memory_space=pltpu.VM...  2.05 us
  transfers between devices with their start and end apart: 1, of which 1 were waited for; matrix products, arithmetic and copies ran while one was open for 0% of the time, Pallas kernels for 11%

profile of v15, /device:TPU:0, one launch (start us, length us, event | category | flops | bytes accessed | tf_op | source)
XLA Modules:
  0.0 95.9 jit_solution(14764752852895895045)
XLA Ops:
  0.0 4.2 %pack.1 = (bf16[128,8320]{1,0:T(8,128)(2,1)}, bf16[128,128]{1,0:T(8,128)(2,1)}) custom-call(s32[1,32]{1,0:T(1,128)} %bitcast.9, s32[1,128]{1,0:T(1,128)} %bitcast.10, bf16[128,8192]{1,0:T(8,128)(2,1)} %hidden_hbm.1), custom_call_target="tpu_custom_call" | custom-call | tf_op jit(solution)/shard_map/pack/pallas_call | solution.py:95
  4.2 0.0 copy-start
  4.2 0.0 copy-start.2
  4.2 58.1 %all_to_all.10 = bf16[16,8,8320]{2,1,0:T(8,128)(2,1)S(1)} all-to-all(bf16[16,8,8320]{2,1,0:T(8,128)(2,1)} %bitcast.8), channel_id=1, replica_groups=mesh['groups'=2,'owner'=16] {'owner'}, dimensions={0} | all-to-all | bytes 4259840 | tf_op jit(solution)/shard_map/all_to_all | solution.py:296
  62.3 0.0 copy-done
  62.3 0.0 copy-done.2
  62.3 0.0 copy-start.4
  62.3 2.0 %adapt.1 = bf16[128,4096]{1,0:T(8,128)(2,1)} custom-call(bf16[128,8320]{1,0:T(8,128)(2,1)S(1)} %bitcast.6, bf16[8192,128]{1,0:T(8,128)(2,1)S(1)} %copy-done, bf16[128,4096]{1,0:T(8,128)(2,1)S(1)} %copy-done.2), custom_call_target="tpu_custom_call" | custom-call | tf_op jit(solution)/shard_map/adapt/pallas_call | solution.py:139
  64.4 3.7 %all-to-all-start.1 = ((bf16[16,8,4096]{2,1,0:T(8,128)(2,1)}), bf16[16,8,4096]{2,1,0:T(8,128)(2,1)S(1)}, u32[]{:S(2)}, u32[]{:S(2)}) async-start(bf16[16,8,4096]{2,1,0:T(8,128)(2,1)} %bitcast.4), calls=%async_computation.1 | async-start | bytes 2097152 | tf_op jit(solution)/shard_map/all_to_all | solution.py:300
  68.1 0.0 copy-done.4
  68.1 0.1 broadcast_in_dim.7
  68.1 0.1 broadcast_in_dim.8
  68.2 0.1 broadcast_in_dim.9.lens_ref
  68.3 0.0 copy-start.1
  68.3 1.2 %copy-done.1 = bf16[128,4096]{1,0:T(8,128)(2,1)S(1)} copy-done((bf16[128,4096]{1,0:T(8,128)(2,1)S(1)}, bf16[128,4096]{1,0:T(8,128)(2,1)}, u32[]{:S(2)}) %copy-start.1) | copy-done | bytes 1048600
  69.6 0.0 copy-start.3
  69.6 10.9 %prep.1 = (bf16[4,128,2048]{2,1,0:T(8,128)(2,1)S(1)}, bf16[4,91,192,128]{3,2,1,0:T(8,128)(2,1)}) custom-call(bf16[128,4096]{1,0:T(8,128)(2,1)S(1)} %copy-done.1, bf16[128,2,16,512]{3,2,1,0:T(8,128)(2,1)} %kv_ref.1), custom_call_target="tpu_custom_call" | custom-call | tf_op jit(solution)/shard_map/prep/pallas_call | solution.py:174
  80.5 10.5 %all-to-all-done.1 = bf16[16,8,4096]{2,1,0:T(8,128)(2,1)S(1)} async-done(((bf16[16,8,4096]{2,1,0:T(8,128)(2,1)}), bf16[16,8,4096]{2,1,0:T(8,128)(2,1)S(1)}, u32[]{:S(2)}, u32[]{:S(2)}) %all-to-all-start.1) | async-done | bytes 1048608 | tf_op jit(solution)/shard_map/all_to_all | solution.py:300
  91.0 0.0 copy-done.3
  91.0 5.0 %attend.1 = bf16[128,4096]{1,0:T(8,128)(2,1)} custom-call(bf16[128,128]{1,0:T(8,128)(2,1)S(1)} %copy-done.3, bf16[128,4096]{1,0:T(8,128)(2,1)S(1)} %bitcast.7, bf16[4,128,2048]{2,1,0:T(8,128)(2,1)S(1)} %get-tuple-element.11.keys_ref, s32[16,1,128]{2,1,0:T(1,128)S(1)} %broadcast_in_dim.9.lens_ref, bf16[4,91,192,128]{3,2,1,0:T(8,128)(2,1)} %get-tuple-element.12.rest_hbm), custom_call_target="tpu_custom_call" | custom-call | tf_op jit(solution)/shard_map/attend/pallas_call | solution.py:269
Async XLA Ops:
  4.2 58.1 %copy-start = (bf16[8192,128]{1,0:T(8,128)(2,1)S(1)}, bf16[8192,128]{1,0:T(8,128)(2,1)}, u32[]{:S(2)}) copy-start(bf16[8192,128]{1,0:T(8,128)(2,1)} %a_ref.1) | copy-start | bytes 6291460
  4.2 58.1 %copy-start.2 = (bf16[128,4096]{1,0:T(8,128)(2,1)S(1)}, bf16[128,4096]{1,0:T(8,128)(2,1)}, u32[]{:S(2)}) copy-start(bf16[128,4096]{1,0:T(8,128)(2,1)} %b_ref.1) | copy-start | bytes 3145732
  62.3 5.7 %copy-start.4 = (s32[128]{0:T(128)S(1)}, s32[128]{0:T(128)}, u32[]{:S(2)}) copy-start(s32[128]{0:T(128)} %param.11) | copy-start | bytes 1540
  64.4 26.6 %all-to-all-start.1 = ((bf16[16,8,4096]{2,1,0:T(8,128)(2,1)}), bf16[16,8,4096]{2,1,0:T(8,128)(2,1)S(1)}, u32[]{:S(2)}, u32[]{:S(2)}) async-start(bf16[16,8,4096]{2,1,0:T(8,128)(2,1)} %bitcast.4), calls=%async_computation.1 | async-start | bytes 2097152 | tf_op jit(solution)/shard_map/all_to_all | solution.py:300
  68.3 1.2 %copy-start.1 = (bf16[128,4096]{1,0:T(8,128)(2,1)S(1)}, bf16[128,4096]{1,0:T(8,128)(2,1)}, u32[]{:S(2)}) copy-start(bf16[128,4096]{1,0:T(8,128)(2,1)} %base_ref.1) | copy-start | bytes 3145732
  69.6 21.4 %copy-start.3 = (bf16[128,128]{1,0:T(8,128)(2,1)S(1)}, bf16[128,128]{1,0:T(8,128)(2,1)}, u32[]{:S(2)}) copy-start(bf16[128,128]{1,0:T(8,128)(2,1)} %get-tuple-element.9.routed_ref) | copy-start | bytes 98308

commit v16 on v15

--- a/solution.py
+++ b/solution.py
@@ -150,16 +150,21 @@
     return jnp.concatenate([rows[:, g * HEAD : (g + 1) * HEAD] for g in range(group)], axis=0)
 
 
-def prep_kernel(group, base_ref, kv_ref, keys_ref, rest_ref):
+def prep_kernel(group, base_ref, kv_ref, keys_ref, query_ref, rest_ref):
     step, context = kv_ref.shape[0], kv_ref.shape[2]
     cells = step * context
     for k in range(KVH):
         head = slice(k * HEAD, (k + 1) * HEAD)
         keys = kv_ref[:, 0, :, head].astype(jnp.float32).reshape(cells, HEAD)
-        keys_ref[k] = jnp.transpose(keys).astype(keys_ref.dtype)
+        keys = jnp.transpose(keys).astype(keys_ref.dtype)
+        base = base_ref[:, k * group * HEAD : (k + 1) * group * HEAD].astype(jnp.float32)
+        query = tall(base, group).astype(query_ref.dtype)
+        if k == 0:
+            keys_ref[0] = keys
+            query_ref[0] = query
         rest_ref[k, 0, :cells] = kv_ref[:, 1, :, head].reshape(cells, HEAD)
-        base = base_ref[:, k * group * HEAD : (k + 1) * group * HEAD].astype(jnp.float32)
-        rest_ref[k, 0, cells:] = tall(base, group).astype(rest_ref.dtype)
+        rest_ref[k, 0, cells : cells + HEAD] = keys
+        rest_ref[k, 0, cells + HEAD :] = query
 
 
 def prep(base_q, kv_cache):
@@ -169,8 +174,9 @@
     step = ROWS_STEP
     steps = rows // step
     cells = step * context
-    lines = cells + group * step
-    length = max(pl.cdiv(TALL_BYTES, 2 * KVH * lines * HEAD), steps)
+    lines = group * step
+    block = cells + HEAD + lines
+    length = max(pl.cdiv(TALL_BYTES, 2 * KVH * block * HEAD), steps)
     return pl.pallas_call(
         functools.partial(prep_kernel, group),
         grid=(steps,),
@@ -179,12 +185,14 @@
             pl.BlockSpec((step, *kv_cache.shape[1:]), lambda i: (i, 0, 0, 0)),
         ],
         out_specs=[
-            pl.BlockSpec((KVH, HEAD, cells), lambda i: (0, 0, i)),
-            pl.BlockSpec((KVH, 1, lines, HEAD), lambda i: (0, i, 0, 0)),
+            pl.BlockSpec((1, HEAD, cells), lambda i: (i, 0, 0)),
+            pl.BlockSpec((1, lines, HEAD), lambda i: (i, 0, 0)),
+            pl.BlockSpec((KVH, 1, block, HEAD), lambda i: (0, i, 0, 0)),
         ],
         out_shape=[
-            jax.ShapeDtypeStruct((KVH, HEAD, rows * context), jnp.bfloat16),
-            jax.ShapeDtypeStruct((KVH, length, lines, HEAD), jnp.bfloat16),
+            jax.ShapeDtypeStruct((steps, HEAD, cells), jnp.bfloat16),
+            jax.ShapeDtypeStruct((steps, lines, HEAD), jnp.bfloat16),
+            jax.ShapeDtypeStruct((KVH, length, block, HEAD), jnp.bfloat16),
         ],
         compiler_params=pltpu.CompilerParams(vmem_limit_bytes=GRANT),
         name="prep",
@@ -192,33 +200,37 @@
 
 
 def attend_kernel(
-    group, context, routed_ref, returned_ref, keys_ref, lens_ref, rest_hbm, out_hbm, *scratch
+    group, context, routed_ref, returned_ref, keys_ref, query_ref, lens_ref, rest_hbm, out_hbm, *scratch
 ):
-    query_ref, values_ref, bias_ref, scores_ref, probs_ref, out_ref, sems = scratch
+    values_ref, later_ref, bias_ref, scores_ref, probs_ref, out_ref, sems = scratch
     step = ROWS_STEP
     steps, lines, cells = bias_ref.shape
     span = group * HEAD
     factor = 1.0 / jnp.sqrt(jnp.float32(HEAD))
-    loads = [
-        [
-            pltpu.make_async_copy(
-                rest_hbm.at[k, pl.ds(0, steps), pl.ds(cells, lines)], query_ref.at[k], sems.at[k, 1]
-            ),
-            pltpu.make_async_copy(
-                rest_hbm.at[k, pl.ds(0, steps), pl.ds(0, cells)], values_ref.at[k], sems.at[k, 2]
-            ),
-        ]
+    values_loads = [
+        pltpu.make_async_copy(
+            rest_hbm.at[k, pl.ds(0, steps), pl.ds(0, cells)], values_ref.at[k], sems.at[k, 1]
+        )
         for k in range(KVH)
     ]
+    later_loads = [
+        pltpu.make_async_copy(
+            rest_hbm.at[k, pl.ds(0, steps), pl.ds(cells, HEAD + lines)],
+            later_ref.at[k - 1],
+            sems.at[k, 2],
+        )
+        for k in range(1, KVH)
+    ]
     stores = [
         pltpu.make_async_copy(
             out_ref.at[:, pl.ds(k * span, span)], out_hbm.at[:, pl.ds(k * span, span)], sems.at[k, 0]
         )
         for k in range(KVH)
     ]
-    for load in loads:
-        for copy in load:
-            copy.start()
+    for k in range(KVH):
+        values_loads[k].start()
+        if k < KVH - 1:
+            later_loads[k].start()
     lane = lax.broadcasted_iota(jnp.int32, (lines, cells), 1)
     line = lax.broadcasted_iota(jnp.int32, (lines, cells), 0)
     own = lax.div(lane, context) == lax.rem(line, step)
@@ -231,13 +243,14 @@
             returned_ref[:, k * span : (k + 1) * span],
             preferred_element_type=jnp.float32,
         )
-        for copy in loads[k]:
-            copy.wait()
+        if k > 0:
+            later_loads[k - 1].wait()
         for i in range(steps):
-            keys = keys_ref[k, :, i * cells : (i + 1) * cells]
+            keys = keys_ref[i] if k == 0 else later_ref[k - 1, i, :HEAD]
+            query = query_ref[i] if k == 0 else later_ref[k - 1, i, HEAD:]
             change = tall(delta[i * step : (i + 1) * step], group).astype(jnp.bfloat16)
             scores = jnp.dot(
-                jnp.concatenate([query_ref[k, i], change], axis=1),
+                jnp.concatenate([query, change], axis=1),
                 jnp.concatenate([keys, keys], axis=0),
                 preferred_element_type=jnp.float32,
             )
@@ -247,6 +260,7 @@
             expo = jnp.exp(scores - jnp.max(scores, axis=1, keepdims=True))
             probs = expo * (1.0 / jnp.sum(expo, axis=1, keepdims=True))
             probs_ref[k, i] = probs.astype(probs_ref.dtype)
+        values_loads[k].wait()
         for i in range(steps):
             rows = slice(i * step, (i + 1) * step)
             out = jnp.dot(probs_ref[k, i], values_ref[k, i], preferred_element_type=jnp.float32)
@@ -259,7 +273,7 @@
         store.wait()
 
 
-def attend(routed, returned, cache_len, keys, rest, context):
+def attend(routed, returned, cache_len, keys, query, rest, context):
     rows, width = routed.shape[0], returned.shape[1]
     group = width // (KVH * HEAD)
     step = ROWS_STEP
@@ -268,12 +282,12 @@
     lens = jnp.repeat(cache_len, context).reshape(steps, 1, cells)
     return pl.pallas_call(
         functools.partial(attend_kernel, group, context),
-        in_specs=[pl.BlockSpec(memory_space=pltpu.VMEM)] * 4 + [pl.BlockSpec(memory_space=pl.ANY)],
+        in_specs=[pl.BlockSpec(memory_space=pltpu.VMEM)] * 5 + [pl.BlockSpec(memory_space=pl.ANY)],
         out_specs=pl.BlockSpec(memory_space=pl.ANY),
         out_shape=jax.ShapeDtypeStruct((rows, width), jnp.bfloat16),
         scratch_shapes=[
-            pltpu.VMEM((KVH, steps, group * step, HEAD), rest.dtype),
             pltpu.VMEM((KVH, steps, cells, HEAD), rest.dtype),
+            pltpu.VMEM((KVH - 1, steps, HEAD + group * step, HEAD), rest.dtype),
             pltpu.VMEM((steps, group * step, cells), jnp.float32),
             pltpu.VMEM((KVH, steps, group * step, cells), jnp.float32),
             pltpu.VMEM((KVH, steps, group * step, cells), jnp.bfloat16),
@@ -282,7 +296,7 @@
         ],
         compiler_params=pltpu.CompilerParams(vmem_limit_bytes=GRANT),
         name="attend",
-    )(routed, returned, keys, lens, rest)
+    )(routed, returned, keys, query, lens, rest)
 
 
 def on_device(hidden, adapter_id, adapter_slot, cache_len, base_q, kv_cache, a_maps, b_maps):
@@ -294,12 +308,12 @@
     packed, routed = pack(hidden, adapter_id, adapter_slot, owners, slot_count, held)
     packed = packed.reshape(owners, slot_count, packed.shape[1])
     arrived = lax.all_to_all(packed, "owner", split_axis=0, concat_axis=0, tiled=True)
-    keys, rest = prep(base_q, kv_cache)
+    keys, query, rest = prep(base_q, kv_cache)
     change = adapt(arrived.reshape(bins, arrived.shape[2]), a_maps, b_maps)
     change = change.reshape(owners, slot_count, change.shape[1])
     returned = lax.all_to_all(change, "owner", split_axis=0, concat_axis=0, tiled=True)
     returned = returned.reshape(bins, returned.shape[2])
-    return attend(routed, returned, cache_len, keys, rest, kv_cache.shape[2])
+    return attend(routed, returned, cache_len, keys, query, rest, kv_cache.shape[2])
 
 
 def solution(mesh):

time: 97.6 us -> 97.7 us (level)
  Pallas kernels: 22.2 us -> 18.4 us
  waiting for transfers between devices: 10.5 us -> 13.5 us
    pallas_call x1, Pallas kernels: 10.9 us -> 6.91 us  [prep(): pl.pallas_call(functools.partial(prep_kernel, group), grid=(steps,), in_s...]
    all_to_all x1, waiting for transfers between devices: 10.5 us -> 13.5 us  [on_device(): lax.all_to_all(change, 'owner', split_axis=0, concat_axis=0, tiled=True)]
    unnamed x10 -> x12, local copies, waits for them, and re-layouts: 1.24 us -> 2.21 us
  transfers between devices with their start and end apart: 1 -> 1, of which waited for: 1 -> 1; matrix products, arithmetic and copies ran while one was open for 0% -> 0% of each run, Pallas kernels for 11% -> 7%
where the time goes in v16:
time: 97.7 us; the launch traced here: 96.3 us
  blocking collectives  58.1 us (59%)
  Pallas kernels  18.4 us (19%)
  waiting for transfers between devices  13.5 us (14%)
  starting transfers between devices  3.79 us (4%)
  local copies, waits for them, and re-layouts  2.47 us (3%)
    all_to_all x1, blocking collectives, on_device(): lax.all_to_all(packed, 'owner', split_axis=0, concat_axis=0, tiled=True)  58.1 us
    all_to_all x1, waiting for transfers between devices, on_device(): lax.all_to_all(change, 'owner', split_axis=0, concat_axis=0, tiled=True)  13.5 us
    pallas_call x1, Pallas kernels, prep(): pl.pallas_call(functools.partial(prep_kernel, group), grid=(steps,), in_s...  6.91 us
    pallas_call x1, Pallas kernels, attend(): pl.pallas_call(functools.partial(attend_kernel, group, context), in_specs...  5.22 us
    pallas_call x1, Pallas kernels, pack(): pl.pallas_call(functools.partial(pack_kernel, owners, slot_count, held),...  4.23 us
    all_to_all x1, starting transfers between devices, on_device(): lax.all_to_all(change, 'owner', split_axis=0, concat_axis=0, tiled=True)  3.79 us
    unnamed x12, local copies, waits for them, and re-layouts  2.21 us
    pallas_call x1, Pallas kernels, adapt(): pl.pallas_call(adapt_kernel, in_specs=[pl.BlockSpec(memory_space=pltpu.VM...  2.05 us
  transfers between devices with their start and end apart: 1, of which 1 were waited for; matrix products, arithmetic and copies ran while one was open for 0% of the time, Pallas kernels for 7%

profile of v16, /device:TPU:0, one launch (start us, length us, event | category | flops | bytes accessed | tf_op | source)
XLA Modules:
  0.0 96.3 jit_solution(4218038562887730943)
XLA Ops:
  0.0 4.2 %pack.1 = (bf16[128,8320]{1,0:T(8,128)(2,1)}, bf16[128,128]{1,0:T(8,128)(2,1)}) custom-call(s32[1,32]{1,0:T(1,128)} %bitcast.9, s32[1,128]{1,0:T(1,128)} %bitcast.10, bf16[128,8192]{1,0:T(8,128)(2,1)} %hidden_hbm.1), custom_call_target="tpu_custom_call" | custom-call | tf_op jit(solution)/shard_map/pack/pallas_call | solution.py:95
  4.2 0.0 copy-start.1
  4.2 0.0 copy-start.3
  4.3 58.1 %all_to_all.10 = bf16[16,8,8320]{2,1,0:T(8,128)(2,1)S(1)} all-to-all(bf16[16,8,8320]{2,1,0:T(8,128)(2,1)} %bitcast.8), channel_id=1, replica_groups=mesh['groups'=2,'owner'=16] {'owner'}, dimensions={0} | all-to-all | bytes 4259840 | tf_op jit(solution)/shard_map/all_to_all | solution.py:310
  62.4 0.0 copy-done.1
  62.4 0.0 copy-done.3
  62.4 0.0 copy-start.5
  62.4 2.0 %adapt.1 = bf16[128,4096]{1,0:T(8,128)(2,1)} custom-call(bf16[128,8320]{1,0:T(8,128)(2,1)S(1)} %bitcast.6, bf16[8192,128]{1,0:T(8,128)(2,1)S(1)} %copy-done.1, bf16[128,4096]{1,0:T(8,128)(2,1)S(1)} %copy-done.3), custom_call_target="tpu_custom_call" | custom-call | tf_op jit(solution)/shard_map/adapt/pallas_call | solution.py:139
  64.4 0.0 copy-start.2
  64.4 3.8 %all-to-all-start.1 = ((bf16[16,8,4096]{2,1,0:T(8,128)(2,1)}), bf16[16,8,4096]{2,1,0:T(8,128)(2,1)S(1)}, u32[]{:S(2)}, u32[]{:S(2)}) async-start(bf16[16,8,4096]{2,1,0:T(8,128)(2,1)} %bitcast.4), calls=%async_computation.1 | async-start | bytes 2097152 | tf_op jit(solution)/shard_map/all_to_all | solution.py:314
  68.2 0.0 copy-done.5
  68.2 0.1 broadcast_in_dim.7
  68.3 0.1 broadcast_in_dim.8
  68.4 0.1 broadcast_in_dim.9.lens_ref
  68.5 0.0 copy-done.2
  68.5 0.0 copy-start
  68.5 2.2 %copy-done = bf16[128,2,16,512]{3,2,1,0:T(8,128)(2,1)S(1)} copy-done((bf16[128,2,16,512]{3,2,1,0:T(8,128)(2,1)S(1)}, bf16[128,2,16,512]{3,2,1,0:T(8,128)(2,1)}, u32[]{:S(2)}) %copy-start) | copy-done | bytes 4194328
  70.7 0.0 copy-start.4
  70.7 6.9 %prep.1 = (bf16[16,128,128]{2,1,0:T(8,128)(2,1)S(1)}, bf16[16,64,128]{2,1,0:T(8,128)(2,1)S(1)}, bf16[4,55,320,128]{3,2,1,0:T(8,128)(2,1)}) custom-call(bf16[128,4096]{1,0:T(8,128)(2,1)S(1)} %copy-done.2, bf16[128,2,16,512]{3,2,1,0:T(8,128)(2,1)S(1)} %copy-done), custom_call_target="tpu_custom_call" | custom-call | tf_op jit(solution)/shard_map/prep/pallas_call | solution.py:180
  77.6 13.5 %all-to-all-done.1 = bf16[16,8,4096]{2,1,0:T(8,128)(2,1)S(1)} async-done(((bf16[16,8,4096]{2,1,0:T(8,128)(2,1)}), bf16[16,8,4096]{2,1,0:T(8,128)(2,1)S(1)}, u32[]{:S(2)}, u32[]{:S(2)}) %all-to-all-start.1) | async-done | bytes 1048608 | tf_op jit(solution)/shard_map/all_to_all | solution.py:314
  91.1 0.0 copy-done.4
  91.1 5.2 %attend.1 = bf16[128,4096]{1,0:T(8,128)(2,1)} custom-call(bf16[128,128]{1,0:T(8,128)(2,1)S(1)} %copy-done.4, bf16[128,4096]{1,0:T(8,128)(2,1)S(1)} %bitcast.7, bf16[16,128,128]{2,1,0:T(8,128)(2,1)S(1)} %get-tuple-element.12.keys_ref, bf16[16,64,128]{2,1,0:T(8,128)(2,1)S(1)} %get-tuple-element.13.query_ref, s32[16,1,128]{2,1,0:T(1,128)S(1)} %broadcast_in_dim.9.lens_ref, ...), custom_call_target="tpu_custom_call" | custom-call | tf_op jit(solution)/shard_map/attend/pallas_call | solution.py:283
Async XLA Ops:
  4.2 58.1 %copy-start.1 = (bf16[8192,128]{1,0:T(8,128)(2,1)S(1)}, bf16[8192,128]{1,0:T(8,128)(2,1)}, u32[]{:S(2)}) copy-start(bf16[8192,128]{1,0:T(8,128)(2,1)} %a_ref.1) | copy-start | bytes 6291460
  4.2 58.1 %copy-start.3 = (bf16[128,4096]{1,0:T(8,128)(2,1)S(1)}, bf16[128,4096]{1,0:T(8,128)(2,1)}, u32[]{:S(2)}) copy-start(bf16[128,4096]{1,0:T(8,128)(2,1)} %b_ref.1) | copy-start | bytes 3145732
  62.4 5.8 %copy-start.5 = (s32[128]{0:T(128)S(1)}, s32[128]{0:T(128)}, u32[]{:S(2)}) copy-start(s32[128]{0:T(128)} %param.11) | copy-start | bytes 1540
  64.4 4.1 %copy-start.2 = (bf16[128,4096]{1,0:T(8,128)(2,1)S(1)}, bf16[128,4096]{1,0:T(8,128)(2,1)}, u32[]{:S(2)}) copy-start(bf16[128,4096]{1,0:T(8,128)(2,1)} %base_ref.1) | copy-start | bytes 3145732
  64.4 26.7 %all-to-all-start.1 = ((bf16[16,8,4096]{2,1,0:T(8,128)(2,1)}), bf16[16,8,4096]{2,1,0:T(8,128)(2,1)S(1)}, u32[]{:S(2)}, u32[]{:S(2)}) async-start(bf16[16,8,4096]{2,1,0:T(8,128)(2,1)} %bitcast.4), calls=%async_computation.1 | async-start | bytes 2097152 | tf_op jit(solution)/shard_map/all_to_all | solution.py:314
  68.5 2.2 %copy-start = (bf16[128,2,16,512]{3,2,1,0:T(8,128)(2,1)S(1)}, bf16[128,2,16,512]{3,2,1,0:T(8,128)(2,1)}, u32[]{:S(2)}) copy-start(bf16[128,2,16,512]{3,2,1,0:T(8,128)(2,1)} %kv_ref.1) | copy-start | bytes 12582916
  70.7 20.4 %copy-start.4 = (bf16[128,128]{1,0:T(8,128)(2,1)S(1)}, bf16[128,128]{1,0:T(8,128)(2,1)}, u32[]{:S(2)}) copy-start(bf16[128,128]{1,0:T(8,128)(2,1)} %get-tuple-element.10.routed_ref) | copy-start | bytes 98308

commit v17 on v15

--- a/solution.py
+++ b/solution.py
@@ -15,7 +15,9 @@
 ROWS_STEP = 8
 COLUMNS_STEP = 1024
 ADAPT_STEP = 2048
+OUT_STEP = 1024
 GRANT = 48 * 2**20
+LOG2E = 1.4426950408889634
 TALL_BYTES = 17 * 2**20
 
 
@@ -115,7 +117,7 @@
     )(slots, adapter_id.reshape(1, rows), hidden)
 
 
-def adapt_kernel(arrived_ref, a_ref, b_ref, change_ref):
+def adapt_kernel(arrived_ref, a_ref, b_ref, change_hbm, change_ref, sems):
     width = a_ref.shape[0]
     low = jnp.zeros((arrived_ref.shape[0], a_ref.shape[1]), jnp.float32)
     for at in range(0, width, ADAPT_STEP):
@@ -127,20 +129,31 @@
     label = arrived_ref[:, width:].astype(jnp.float32)[:, :1].astype(jnp.int32)
     column = lax.broadcasted_iota(jnp.int32, low.shape, 1) // RANK
     low = jnp.where(column == label, low, 0.0).astype(jnp.bfloat16)
-    out_width = b_ref.shape[1]
-    piece = min(1024, out_width)
-    for at in range(0, out_width, piece):
-        change_ref[:, at : at + piece] = (
-            SCALE * jnp.dot(low, b_ref[:, at : at + piece], preferred_element_type=jnp.float32)
+    stores = []
+    for i, at in enumerate(range(0, b_ref.shape[1], OUT_STEP)):
+        span = pl.ds(at, OUT_STEP)
+        change_ref[:, at : at + OUT_STEP] = (
+            SCALE * jnp.dot(low, b_ref[:, at : at + OUT_STEP], preferred_element_type=jnp.float32)
         ).astype(change_ref.dtype)
+        stores.append(
+            pltpu.make_async_copy(change_ref.at[:, span], change_hbm.at[:, span], sems.at[i])
+        )
+        stores[-1].start()
+    for store in stores:
+        store.wait()
 
 
 def adapt(arrived, a_maps, b_maps):
+    change = jax.ShapeDtypeStruct((arrived.shape[0], b_maps.shape[1]), jnp.bfloat16)
     return pl.pallas_call(
         adapt_kernel,
         in_specs=[pl.BlockSpec(memory_space=pltpu.VMEM)] * 3,
-        out_specs=pl.BlockSpec(memory_space=pltpu.VMEM),
-        out_shape=jax.ShapeDtypeStruct((arrived.shape[0], b_maps.shape[1]), jnp.bfloat16),
+        out_specs=pl.BlockSpec(memory_space=pl.ANY),
+        out_shape=change,
+        scratch_shapes=[
+            pltpu.VMEM(change.shape, change.dtype),
+            pltpu.SemaphoreType.DMA((pl.cdiv(b_maps.shape[1], OUT_STEP),)),
+        ],
         compiler_params=pltpu.CompilerParams(vmem_limit_bytes=16 * 2**20),
         name="adapt",
     )(arrived, a_maps, b_maps)
@@ -194,11 +207,11 @@
 def attend_kernel(
     group, context, routed_ref, returned_ref, keys_ref, lens_ref, rest_hbm, out_hbm, *scratch
 ):
-    query_ref, values_ref, bias_ref, scores_ref, probs_ref, out_ref, sems = scratch
+    query_ref, values_ref, bias_ref, scores_ref, expo_ref, out_ref, sems = scratch
     step = ROWS_STEP
     steps, lines, cells = bias_ref.shape
     span = group * HEAD
-    factor = 1.0 / jnp.sqrt(jnp.float32(HEAD))
+    factor = LOG2E / jnp.sqrt(jnp.float32(HEAD))
     loads = [
         [
             pltpu.make_async_copy(
@@ -223,6 +236,7 @@
     line = lax.broadcasted_iota(jnp.int32, (lines, cells), 0)
     own = lax.div(lane, context) == lax.rem(line, step)
     position = lax.rem(lane, context)
+    ones = jnp.ones((cells, HEAD), expo_ref.dtype)
     for i in range(steps):
         bias_ref[i] = jnp.where(own & (position < lens_ref[i]), 0.0, -jnp.inf)
     for k in range(KVH):
@@ -244,12 +258,16 @@
             scores_ref[k, i] = scores * factor + bias_ref[i]
         for i in range(steps):
             scores = scores_ref[k, i]
-            expo = jnp.exp(scores - jnp.max(scores, axis=1, keepdims=True))
-            probs = expo * (1.0 / jnp.sum(expo, axis=1, keepdims=True))
-            probs_ref[k, i] = probs.astype(probs_ref.dtype)
+            expo = jnp.exp2(scores - jnp.max(scores, axis=1, keepdims=True))
+            expo_ref[k, i] = expo.astype(expo_ref.dtype)
         for i in range(steps):
             rows = slice(i * step, (i + 1) * step)
-            out = jnp.dot(probs_ref[k, i], values_ref[k, i], preferred_element_type=jnp.float32)
+            out = jnp.dot(
+                expo_ref[k, i],
+                jnp.concatenate([values_ref[k, i], ones], axis=1),
+                preferred_element_type=jnp.float32,
+            )
+            out = out[:, :HEAD] * (1.0 / out[:, HEAD:])
             for g in range(group):
                 out_ref[rows, (k * group + g) * HEAD : (k * group + g + 1) * HEAD] = out[
                     g * step : (g + 1) * step

time: 97.6 us -> 96.9 us (level)
  no operation moved by 1% of the time
where the time goes in v17:
time: 96.9 us; the launch traced here: 95.2 us
  blocking collectives  58.1 us (60%)
  Pallas kernels  21.4 us (22%)
  waiting for transfers between devices  10.5 us (11%)
  starting transfers between devices  3.67 us (4%)
  local copies, waits for them, and re-layouts  1.5 us (2%)
    all_to_all x1, blocking collectives, on_device(): lax.all_to_all(packed, 'owner', split_axis=0, concat_axis=0, tiled=True)  58.1 us
    pallas_call x1, Pallas kernels, prep(): pl.pallas_call(functools.partial(prep_kernel, group), grid=(steps,), in_s...  10.9 us
    all_to_all x1, waiting for transfers between devices, on_device(): lax.all_to_all(change, 'owner', split_axis=0, concat_axis=0, tiled=True)  10.5 us
    pallas_call x1, Pallas kernels, attend(): pl.pallas_call(functools.partial(attend_kernel, group, context), in_specs...  4.42 us
    pallas_call x1, Pallas kernels, pack(): pl.pallas_call(functools.partial(pack_kernel, owners, slot_count, held),...  4.21 us
    all_to_all x1, starting transfers between devices, on_device(): lax.all_to_all(change, 'owner', split_axis=0, concat_axis=0, tiled=True)  3.67 us
  transfers between devices with their start and end apart: 1, of which 1 were waited for; matrix products, arithmetic and copies ran while one was open for 0% of the time, Pallas kernels for 11%

profile of v17, /device:TPU:0, one launch (start us, length us, event | category | flops | bytes accessed | tf_op | source)
XLA Modules:
  0.0 95.2 jit_solution(18066424441427631292)
XLA Ops:
  0.0 4.2 %pack.1 = (bf16[128,8320]{1,0:T(8,128)(2,1)}, bf16[128,128]{1,0:T(8,128)(2,1)}) custom-call(s32[1,32]{1,0:T(1,128)} %bitcast.9, s32[1,128]{1,0:T(1,128)} %bitcast.10, bf16[128,8192]{1,0:T(8,128)(2,1)} %hidden_hbm.1), custom_call_target="tpu_custom_call" | custom-call | tf_op jit(solution)/shard_map/pack/pallas_call | solution.py:97
  4.2 0.0 copy-start
  4.2 0.0 copy-start.2
  4.2 58.1 %all_to_all.10 = bf16[16,8,8320]{2,1,0:T(8,128)(2,1)S(1)} all-to-all(bf16[16,8,8320]{2,1,0:T(8,128)(2,1)} %bitcast.8), channel_id=1, replica_groups=mesh['groups'=2,'owner'=16] {'owner'}, dimensions={0} | all-to-all | bytes 4259840 | tf_op jit(solution)/shard_map/all_to_all | solution.py:314
  62.3 0.0 copy-done
  62.3 0.0 copy-done.2
  62.3 0.0 copy-start.4
  62.3 1.9 %adapt.1 = bf16[128,4096]{1,0:T(8,128)(2,1)} custom-call(bf16[128,8320]{1,0:T(8,128)(2,1)S(1)} %bitcast.6, bf16[8192,128]{1,0:T(8,128)(2,1)S(1)} %copy-done, bf16[128,4096]{1,0:T(8,128)(2,1)S(1)} %copy-done.2), custom_call_target="tpu_custom_call" | custom-call | tf_op jit(solution)/shard_map/adapt/pallas_call | solution.py:148
  64.2 3.7 %all-to-all-start.1 = ((bf16[16,8,4096]{2,1,0:T(8,128)(2,1)}), bf16[16,8,4096]{2,1,0:T(8,128)(2,1)S(1)}, u32[]{:S(2)}, u32[]{:S(2)}) async-start(bf16[16,8,4096]{2,1,0:T(8,128)(2,1)} %bitcast.4), calls=%async_computation.1 | async-start | bytes 2097152 | tf_op jit(solution)/shard_map/all_to_all | solution.py:318
  67.9 0.0 copy-done.4
  67.9 0.1 broadcast_in_dim.7
  68.0 0.1 broadcast_in_dim.8
  68.1 0.1 broadcast_in_dim.9.lens_ref
  68.2 0.0 copy-start.1
  68.2 1.2 %copy-done.1 = bf16[128,4096]{1,0:T(8,128)(2,1)S(1)} copy-done((bf16[128,4096]{1,0:T(8,128)(2,1)S(1)}, bf16[128,4096]{1,0:T(8,128)(2,1)}, u32[]{:S(2)}) %copy-start.1) | copy-done | bytes 1048600
  69.4 0.0 copy-start.3
  69.4 10.9 %prep.1 = (bf16[4,128,2048]{2,1,0:T(8,128)(2,1)S(1)}, bf16[4,91,192,128]{3,2,1,0:T(8,128)(2,1)}) custom-call(bf16[128,4096]{1,0:T(8,128)(2,1)S(1)} %copy-done.1, bf16[128,2,16,512]{3,2,1,0:T(8,128)(2,1)} %kv_ref.1), custom_call_target="tpu_custom_call" | custom-call | tf_op jit(solution)/shard_map/prep/pallas_call | solution.py:187
  80.3 10.5 %all-to-all-done.1 = bf16[16,8,4096]{2,1,0:T(8,128)(2,1)S(1)} async-done(((bf16[16,8,4096]{2,1,0:T(8,128)(2,1)}), bf16[16,8,4096]{2,1,0:T(8,128)(2,1)S(1)}, u32[]{:S(2)}, u32[]{:S(2)}) %all-to-all-start.1) | async-done | bytes 1048608 | tf_op jit(solution)/shard_map/all_to_all | solution.py:318
  90.8 0.0 copy-done.3
  90.8 4.4 %attend.1 = bf16[128,4096]{1,0:T(8,128)(2,1)} custom-call(bf16[128,128]{1,0:T(8,128)(2,1)S(1)} %copy-done.3, bf16[128,4096]{1,0:T(8,128)(2,1)S(1)} %bitcast.7, bf16[4,128,2048]{2,1,0:T(8,128)(2,1)S(1)} %get-tuple-element.11.keys_ref, s32[16,1,128]{2,1,0:T(1,128)S(1)} %broadcast_in_dim.9.lens_ref, bf16[4,91,192,128]{3,2,1,0:T(8,128)(2,1)} %get-tuple-element.12.rest_hbm), custom_call_target="tpu_custom_call" | custom-call | tf_op jit(solution)/shard_map/attend/pallas_call | solution.py:287
Async XLA Ops:
  4.2 58.1 %copy-start = (bf16[8192,128]{1,0:T(8,128)(2,1)S(1)}, bf16[8192,128]{1,0:T(8,128)(2,1)}, u32[]{:S(2)}) copy-start(bf16[8192,128]{1,0:T(8,128)(2,1)} %a_ref.1) | copy-start | bytes 6291460
  4.2 58.1 %copy-start.2 = (bf16[128,4096]{1,0:T(8,128)(2,1)S(1)}, bf16[128,4096]{1,0:T(8,128)(2,1)}, u32[]{:S(2)}) copy-start(bf16[128,4096]{1,0:T(8,128)(2,1)} %b_ref.1) | copy-start | bytes 3145732
  62.3 5.6 %copy-start.4 = (s32[128]{0:T(128)S(1)}, s32[128]{0:T(128)}, u32[]{:S(2)}) copy-start(s32[128]{0:T(128)} %param.11) | copy-start | bytes 1540
  64.2 26.6 %all-to-all-start.1 = ((bf16[16,8,4096]{2,1,0:T(8,128)(2,1)}), bf16[16,8,4096]{2,1,0:T(8,128)(2,1)S(1)}, u32[]{:S(2)}, u32[]{:S(2)}) async-start(bf16[16,8,4096]{2,1,0:T(8,128)(2,1)} %bitcast.4), calls=%async_computation.1 | async-start | bytes 2097152 | tf_op jit(solution)/shard_map/all_to_all | solution.py:318
  68.2 1.2 %copy-start.1 = (bf16[128,4096]{1,0:T(8,128)(2,1)S(1)}, bf16[128,4096]{1,0:T(8,128)(2,1)}, u32[]{:S(2)}) copy-start(bf16[128,4096]{1,0:T(8,128)(2,1)} %base_ref.1) | copy-start | bytes 3145732
  69.4 21.4 %copy-start.3 = (bf16[128,128]{1,0:T(8,128)(2,1)S(1)}, bf16[128,128]{1,0:T(8,128)(2,1)}, u32[]{:S(2)}) copy-start(bf16[128,128]{1,0:T(8,128)(2,1)} %get-tuple-element.9.routed_ref) | copy-start | bytes 98308

commit v18 on v17

--- a/solution.py
+++ b/solution.py
@@ -39,14 +39,15 @@
         hits.astype(jnp.bfloat16), earlier.astype(jnp.bfloat16), preferred_element_type=jnp.float32
     )
     place = jnp.sum(jnp.where(hits, before, 0.0), axis=0, keepdims=True).astype(jnp.int32)
-    bins = owner * slot_count + place
-    routed = bins == lax.broadcasted_iota(jnp.int32, (owners * slot_count, rows), 0)
-    label = jnp.sum(jnp.where(routed, local.astype(jnp.float32), 0.0), axis=1, keepdims=True)
-    return routed.astype(jnp.bfloat16), label
-
-
-def pack_kernel(owners, slot_count, held, slots_hbm, ids_hbm, hidden_hbm, packed_hbm, routed_hbm, *scratch):
-    slots_ref, ids_ref, rows_ref, bins_ref, routed_ref, small_sems, sems, out_sems = scratch
+    line = lax.broadcasted_iota(jnp.int32, (owners * slot_count, rows), 0)
+    apart = owner ^ lax.axis_index("owner")
+    sent = line == apart * slot_count + place
+    label = jnp.sum(jnp.where(sent, local.astype(jnp.float32), 0.0), axis=1, keepdims=True)
+    return sent, line == owner * slot_count + place, label
+
+
+def pack_kernel(owners, slot_count, held, slots_hbm, ids_hbm, hidden_hbm, routed_ref, *refs):
+    message_refs, (slots_ref, ids_ref, rows_ref, small_sems, sems) = refs[:owners], refs[owners:]
     width = rows_ref.shape[1]
     spans = [(at, min(COLUMNS_STEP, width - at)) for at in range(0, width, COLUMNS_STEP)]
     small = [
@@ -59,34 +60,24 @@
         )
         for i, (at, size) in enumerate(spans)
     ]
-    stores = [
-        pltpu.make_async_copy(
-            bins_ref.at[:, pl.ds(at, size)], packed_hbm.at[:, pl.ds(at, size)], out_sems.at[i]
-        )
-        for i, (at, size) in enumerate([*spans, (width, LANES)])
-    ]
-    routed_store = pltpu.make_async_copy(routed_ref, routed_hbm, small_sems.at[2])
     for copy in [*small, *loads]:
         copy.start()
     for copy in small:
         copy.wait()
-    routed, label = routing(owners, slot_count, held, slots_ref[...], ids_ref[...])
-    for load, store, (at, size) in zip(loads, stores, spans):
+    sent, routed, label = routing(owners, slot_count, held, slots_ref[...], ids_ref[...])
+    sent = sent.astype(jnp.bfloat16)
+    routed_ref[...] = jnp.transpose(routed.astype(jnp.float32)).astype(routed_ref.dtype)
+
+    def put(at, lines):
+        for i, message_ref in enumerate(message_refs):
+            message_ref[:, at : at + lines.shape[1]] = lines[
+                i * slot_count : (i + 1) * slot_count
+            ].astype(message_ref.dtype)
+
+    put(width, jnp.broadcast_to(label, (label.shape[0], LANES)))
+    for load, (at, size) in zip(loads, spans):
         load.wait()
-        bins_ref[:, at : at + size] = jnp.dot(
-            routed, rows_ref[:, at : at + size], preferred_element_type=jnp.float32
-        ).astype(bins_ref.dtype)
-        store.start()
-        if at == 0:
-            bins_ref[:, width:] = jnp.broadcast_to(label, (label.shape[0], LANES)).astype(
-                bins_ref.dtype
-            )
-            stores[-1].start()
-            routed_ref[...] = jnp.transpose(routed.astype(jnp.float32)).astype(routed_ref.dtype)
-            routed_store.start()
-    for store in stores:
-        store.wait()
-    routed_store.wait()
+        put(at, jnp.dot(sent, rows_ref[:, at : at + size], preferred_element_type=jnp.float32))
 
 
 def pack(hidden, adapter_id, adapter_slot, owners, slot_count, held):
@@ -97,57 +88,65 @@
     return pl.pallas_call(
         functools.partial(pack_kernel, owners, slot_count, held),
         in_specs=[pl.BlockSpec(memory_space=pl.ANY)] * 3,
-        out_specs=[pl.BlockSpec(memory_space=pl.ANY)] * 2,
-        out_shape=[
-            jax.ShapeDtypeStruct((bins, width + LANES), hidden.dtype),
-            jax.ShapeDtypeStruct((rows, bins), jnp.bfloat16),
-        ],
+        out_specs=[pl.BlockSpec(memory_space=pltpu.VMEM)] * (1 + owners),
+        out_shape=[jax.ShapeDtypeStruct((rows, bins), jnp.bfloat16)]
+        + [jax.ShapeDtypeStruct((slot_count, width + LANES), hidden.dtype)] * owners,
         scratch_shapes=[
             pltpu.VMEM(slots.shape, jnp.int32),
             pltpu.VMEM((1, rows), jnp.int32),
             pltpu.VMEM((rows, width), hidden.dtype),
-            pltpu.VMEM((bins, width + LANES), hidden.dtype),
-            pltpu.VMEM((rows, bins), jnp.bfloat16),
-            pltpu.SemaphoreType.DMA((3,)),
+            pltpu.SemaphoreType.DMA((2,)),
             pltpu.SemaphoreType.DMA((steps,)),
-            pltpu.SemaphoreType.DMA((steps + 1,)),
         ],
         compiler_params=pltpu.CompilerParams(vmem_limit_bytes=56 * 2**20),
         name="pack",
     )(slots, adapter_id.reshape(1, rows), hidden)
 
 
-def adapt_kernel(arrived_ref, a_ref, b_ref, change_hbm, change_ref, sems):
+def stack(refs, at, size):
+    return jnp.concatenate(
+        [ref[:, at : at + size].astype(jnp.float32) for ref in refs], axis=0
+    ).astype(jnp.bfloat16)
+
+
+def adapt_kernel(order, *refs):
+    owners = len(order)
+    arrived_refs, (a_ref, b_ref, change_hbm, change_ref, sems) = refs[:owners], refs[owners:]
     width = a_ref.shape[0]
-    low = jnp.zeros((arrived_ref.shape[0], a_ref.shape[1]), jnp.float32)
+    slot_count = arrived_refs[0].shape[0]
+    me = lax.axis_index("owner")
+    low = jnp.zeros((owners * slot_count, a_ref.shape[1]), jnp.float32)
     for at in range(0, width, ADAPT_STEP):
         low += jnp.dot(
-            arrived_ref[:, at : at + ADAPT_STEP],
+            stack(arrived_refs, at, ADAPT_STEP),
             a_ref[at : at + ADAPT_STEP, :],
             preferred_element_type=jnp.float32,
         )
-    label = arrived_ref[:, width:].astype(jnp.float32)[:, :1].astype(jnp.int32)
+    label = stack(arrived_refs, width, LANES).astype(jnp.float32)[:, :1].astype(jnp.int32)
     column = lax.broadcasted_iota(jnp.int32, low.shape, 1) // RANK
     low = jnp.where(column == label, low, 0.0).astype(jnp.bfloat16)
     stores = []
     for i, at in enumerate(range(0, b_ref.shape[1], OUT_STEP)):
         span = pl.ds(at, OUT_STEP)
-        change_ref[:, at : at + OUT_STEP] = (
-            SCALE * jnp.dot(low, b_ref[:, at : at + OUT_STEP], preferred_element_type=jnp.float32)
-        ).astype(change_ref.dtype)
+        change = SCALE * jnp.dot(low, b_ref[:, at : at + OUT_STEP], preferred_element_type=jnp.float32)
+        for j, s in enumerate(order):
+            change_ref[me ^ s, :, at : at + OUT_STEP] = change[
+                j * slot_count : (j + 1) * slot_count
+            ].astype(change_ref.dtype)
         stores.append(
-            pltpu.make_async_copy(change_ref.at[:, span], change_hbm.at[:, span], sems.at[i])
+            pltpu.make_async_copy(change_ref.at[:, :, span], change_hbm.at[:, :, span], sems.at[i])
         )
         stores[-1].start()
     for store in stores:
         store.wait()
 
 
-def adapt(arrived, a_maps, b_maps):
-    change = jax.ShapeDtypeStruct((arrived.shape[0], b_maps.shape[1]), jnp.bfloat16)
+def adapt(arrived, order, a_maps, b_maps):
+    owners = len(order)
+    change = jax.ShapeDtypeStruct((owners, arrived[0].shape[0], b_maps.shape[1]), jnp.bfloat16)
     return pl.pallas_call(
-        adapt_kernel,
-        in_specs=[pl.BlockSpec(memory_space=pltpu.VMEM)] * 3,
+        functools.partial(adapt_kernel, order),
+        in_specs=[pl.BlockSpec(memory_space=pltpu.VMEM)] * (owners + 2),
         out_specs=pl.BlockSpec(memory_space=pl.ANY),
         out_shape=change,
         scratch_shapes=[
@@ -156,7 +155,7 @@
         ],
         compiler_params=pltpu.CompilerParams(vmem_limit_bytes=16 * 2**20),
         name="adapt",
-    )(arrived, a_maps, b_maps)
+    )(*arrived, a_maps, b_maps)
 
 
 def tall(rows, group):
@@ -309,12 +308,16 @@
     held = a_maps.shape[1] // RANK
     slot_count = max(2, 2 * ((rows + 2 * owners - 1) // (2 * owners)))
     bins = owners * slot_count
-    packed, routed = pack(hidden, adapter_id, adapter_slot, owners, slot_count, held)
-    packed = packed.reshape(owners, slot_count, packed.shape[1])
-    arrived = lax.all_to_all(packed, "owner", split_axis=0, concat_axis=0, tiled=True)
+    routed, *messages = pack(hidden, adapter_id, adapter_slot, owners, slot_count, held)
+    half = owners // 2
+    near = [*range(half // 2, half), *range(1, half // 2)]
+    order = [s for pair in zip(range(half, owners), [*near, 0]) for s in pair]
+    arrived = [
+        lax.ppermute(messages[s], "owner", [(i, i ^ s) for i in range(owners)]) if s else messages[s]
+        for s in order
+    ]
     keys, rest = prep(base_q, kv_cache)
-    change = adapt(arrived.reshape(bins, arrived.shape[2]), a_maps, b_maps)
-    change = change.reshape(owners, slot_count, change.shape[1])
+    change = adapt(arrived, order, a_maps, b_maps)
     returned = lax.all_to_all(change, "owner", split_axis=0, concat_axis=0, tiled=True)
     returned = returned.reshape(bins, returned.shape[2])
     return attend(routed, returned, cache_len, keys, rest, kv_cache.shape[2])

time: 96.9 us -> 93.6 us (0.966)
  blocking collectives: 58.1 us -> 0 us
  starting transfers between devices: 3.67 us -> 40.7 us
  waiting for transfers between devices: 10.5 us -> 25.4 us
  local copies, waits for them, and re-layouts: 1.5 us -> 3.63 us
    all_to_all x1 -> x0, blocking collectives: 58.1 us -> none  [on_device(): lax.all_to_all(packed, 'owner', split_axis=0, concat_axis=0, tiled=True)]
    ppermute x0 -> x15, starting transfers between devices: none -> 32.1 us  [on_device(): lax.ppermute(messages[s], 'owner', [(i, i ^ s) for i in range(owners)])]
    ppermute x0 -> x15, waiting for transfers between devices: none -> 14.8 us  [on_device(): lax.ppermute(messages[s], 'owner', [(i, i ^ s) for i in range(owners)])]
    all_to_all x1, starting transfers between devices: 3.67 us -> 8.56 us  [on_device(): lax.all_to_all(change, 'owner', split_axis=0, concat_axis=0, tiled=True)]
    unnamed x10 -> x12, local copies, waits for them, and re-layouts: 1.24 us -> 3.36 us
  transfers between devices with their start and end apart: 1 -> 16, of which waited for: 1 -> 6; matrix products, arithmetic and copies ran while one was open for 0% -> 0% of each run, Pallas kernels for 11% -> 12%
where the time goes in v18:
time: 93.6 us; the launch traced here: 91.9 us
  starting transfers between devices  40.7 us (43%)
  waiting for transfers between devices  25.4 us (27%)
  Pallas kernels  22.2 us (24%)
  local copies, waits for them, and re-layouts  3.63 us (4%)
    ppermute x15, starting transfers between devices, on_device(): lax.ppermute(messages[s], 'owner', [(i, i ^ s) for i in range(owners)])  32.1 us
    ppermute x15, waiting for transfers between devices, on_device(): lax.ppermute(messages[s], 'owner', [(i, i ^ s) for i in range(owners)])  14.8 us
    pallas_call x1, Pallas kernels, prep(): pl.pallas_call(functools.partial(prep_kernel, group), grid=(steps,), in_s...  10.9 us
    all_to_all x1, waiting for transfers between devices, on_device(): lax.all_to_all(change, 'owner', split_axis=0, concat_axis=0, tiled=True)  10.5 us
    all_to_all x1, starting transfers between devices, on_device(): lax.all_to_all(change, 'owner', split_axis=0, concat_axis=0, tiled=True)  8.56 us
    pallas_call x1, Pallas kernels, pack(): pl.pallas_call(functools.partial(pack_kernel, owners, slot_count, held),...  4.96 us
    pallas_call x1, Pallas kernels, attend(): pl.pallas_call(functools.partial(attend_kernel, group, context), in_specs...  4.41 us
    unnamed x12, local copies, waits for them, and re-layouts  3.36 us
  transfers between devices with their start and end apart: 16, of which 6 were waited for; matrix products, arithmetic and copies ran while one was open for 0% of the time, Pallas kernels for 12%

profile of v18, /device:TPU:0, one launch (start us, length us, event | category | flops | bytes accessed | tf_op | source)
XLA Modules:
  0.0 91.9 jit_solution(11469010448784106854)
XLA Ops:
  0.0 0.0 copy-start
  0.0 5.0 %pack.1 = (bf16[128,128]{1,0:T(8,128)(2,1)}, bf16[8,8320]{1,0:T(8,128)(2,1)}, bf16[8,8320]{1,0:T(8,128)(2,1)}, bf16[8,8320]{1,0:T(8,128)(2,1)}, bf16[8,8320]{1,0...) custom-call(s32[1,32]{1,0:T(1,128)} %bitcast.4, ...), custom_call_target="tpu_custom_call" | custom-call | tf_op jit(solution)/shard_map/pack/pallas_call | solution.py:88
  5.0 4.1 %collective-permute-start = (bf16[8,8320]{1,0:T(8,128)(2,1)}, bf16[8,8320]{1,0:T(8,128)(2,1)S(1)}, u32[]{:S(2)}, u32[]{:S(2)}) collective-permute-start(bf16[8,8320]{1,0:T(8,128)(2,1)} %get-tuple-element.25), channel_id=1, source_target_pairs={{0,8},{1,9},{2,10},{3,11},{4,12},{5,13},{6,14},{7,15},{8,0},{9,1},... | collective-permute-start | bytes 399368 | tf_op jit(solution)/shard_map/ppermute | solution.py:316
  9.1 1.6 %collective-permute-start.1 = (bf16[8,8320]{1,0:T(8,128)(2,1)}, bf16[8,8320]{1,0:T(8,128)(2,1)S(1)}, u32[]{:S(2)}, u32[]{:S(2)}) collective-permute-start(bf16[8,8320]{1,0:T(8,128)(2,1)} %get-tuple-element.26), channel_id=1, source_target_pairs={{0,4},{1,5},{2,6},{3,7},{4,0},{5,1},{6,2},{7,3},{8,12},{9,13},{10,... | collective-permute-start | bytes 399368 | tf_op jit(solution)/shard_map/ppermute | solution.py:316
  10.7 0.0 collective-permute-start.2
  10.7 0.2 collective-permute-start.3
  10.9 3.8 %collective-permute-start.4 = (bf16[8,8320]{1,0:T(8,128)(2,1)}, bf16[8,8320]{1,0:T(8,128)(2,1)S(1)}, u32[]{:S(2)}, u32[]{:S(2)}) collective-permute-start(bf16[8,8320]{1,0:T(8,128)(2,1)} %get-tuple-element.29), channel_id=1, source_target_pairs={{0,10},{1,11},{2,8},{3,9},{4,14},{5,15},{6,12},{7,13},{8,2},{9,3},... | collective-permute-start | bytes 399368 | tf_op jit(solution)/shard_map/ppermute | solution.py:316
  14.7 2.4 %collective-permute-done.refs_0_ = bf16[8,8320]{1,0:T(8,128)(2,1)S(1)} collective-permute-done((bf16[8,8320]{1,0:T(8,128)(2,1)}, bf16[8,8320]{1,0:T(8,128)(2,1)S(1)}, u32[]{:S(2)}, u32[]{:S(2)}) %collective-permute-start) | collective-permute-done | bytes 133152 | tf_op jit(solution)/shard_map/ppermute | solution.py:316
  17.1 1.3 %collective-permute-start.5 = (bf16[8,8320]{1,0:T(8,128)(2,1)}, bf16[8,8320]{1,0:T(8,128)(2,1)S(1)}, u32[]{:S(2)}, u32[]{:S(2)}) collective-permute-start(bf16[8,8320]{1,0:T(8,128)(2,1)} %get-tuple-element.30), channel_id=1, source_target_pairs={{0,6},{1,7},{2,4},{3,5},{4,2},{5,3},{6,0},{7,1},{8,14},{9,15},{10,... | collective-permute-start | bytes 399368 | tf_op jit(solution)/shard_map/ppermute | solution.py:316
  18.4 0.0 collective-permute-done.1.refs_1_
  18.4 2.6 %collective-permute-start.6 = (bf16[8,8320]{1,0:T(8,128)(2,1)}, bf16[8,8320]{1,0:T(8,128)(2,1)S(1)}, u32[]{:S(2)}, u32[]{:S(2)}) collective-permute-start(bf16[8,8320]{1,0:T(8,128)(2,1)} %get-tuple-element.31), channel_id=1, source_target_pairs={{0,11},{1,10},{2,9},{3,8},{4,15},{5,14},{6,13},{7,12},{8,3},{9,2},... | collective-permute-start | bytes 399368 | tf_op jit(solution)/shard_map/ppermute | solution.py:316
  21.1 0.0 collective-permute-done.2.refs_2_
  21.1 2.2 %collective-permute-start.7 = (bf16[8,8320]{1,0:T(8,128)(2,1)}, bf16[8,8320]{1,0:T(8,128)(2,1)S(1)}, u32[]{:S(2)}, u32[]{:S(2)}) collective-permute-start(bf16[8,8320]{1,0:T(8,128)(2,1)} %get-tuple-element.32), channel_id=1, source_target_pairs={{0,7},{1,6},{2,5},{3,4},{4,3},{5,2},{6,1},{7,0},{8,15},{9,14},{10,... | collective-permute-start | bytes 399368 | tf_op jit(solution)/shard_map/ppermute | solution.py:316
  23.3 0.0 collective-permute-done.3.refs_3_
  23.3 2.6 %collective-permute-start.8 = (bf16[8,8320]{1,0:T(8,128)(2,1)}, bf16[8,8320]{1,0:T(8,128)(2,1)S(1)}, u32[]{:S(2)}, u32[]{:S(2)}) collective-permute-start(bf16[8,8320]{1,0:T(8,128)(2,1)} %get-tuple-element.33), channel_id=1, source_target_pairs={{0,12},{1,13},{2,14},{3,15},{4,8},{5,9},{6,10},{7,11},{8,4},{9,5},... | collective-permute-start | bytes 399368 | tf_op jit(solution)/shard_map/ppermute | solution.py:316
  25.9 3.8 %collective-permute-done.4.refs_4_ = bf16[8,8320]{1,0:T(8,128)(2,1)S(1)} collective-permute-done((bf16[8,8320]{1,0:T(8,128)(2,1)}, bf16[8,8320]{1,0:T(8,128)(2,1)S(1)}, u32[]{:S(2)}, u32[]{:S(2)}) %collective-permute-start.4) | collective-permute-done | bytes 133152 | tf_op jit(solution)/shard_map/ppermute | solution.py:316
  29.7 0.0 collective-permute-start.9
  29.7 0.8 collective-permute-done.5.refs_5_
  30.4 2.5 %collective-permute-start.10 = (bf16[8,8320]{1,0:T(8,128)(2,1)}, bf16[8,8320]{1,0:T(8,128)(2,1)S(1)}, u32[]{:S(2)}, u32[]{:S(2)}) collective-permute-start(bf16[8,8320]{1,0:T(8,128)(2,1)} %get-tuple-element.35), channel_id=1, source_target_pairs={{0,13},{1,12},{2,15},{3,14},{4,9},{5,8},{6,11},{7,10},{8,5},{9,4},... | collective-permute-start | bytes 399368 | tf_op jit(solution)/shard_map/ppermute | solution.py:316
  32.9 0.0 collective-permute-done.6.refs_6_
  32.9 0.5 collective-permute-start.11
  33.5 0.0 collective-permute-done.7.refs_7_
  33.5 6.2 %collective-permute-start.12 = (bf16[8,8320]{1,0:T(8,128)(2,1)}, bf16[8,8320]{1,0:T(8,128)(2,1)S(1)}, u32[]{:S(2)}, u32[]{:S(2)}) collective-permute-start(bf16[8,8320]{1,0:T(8,128)(2,1)} %get-tuple-element.37), channel_id=1, source_target_pairs={{0,14},{1,15},{2,12},{3,13},{4,10},{5,11},{6,8},{7,9},{8,6},{9,7},... | collective-permute-start | bytes 399368 | tf_op jit(solution)/shard_map/ppermute | solution.py:316
  39.7 0.0 collective-permute-done.8.refs_8_
  39.7 4.4 %collective-permute-start.13 = (bf16[8,8320]{1,0:T(8,128)(2,1)}, bf16[8,8320]{1,0:T(8,128)(2,1)S(1)}, u32[]{:S(2)}, u32[]{:S(2)}) collective-permute-start(bf16[8,8320]{1,0:T(8,128)(2,1)} %get-tuple-element.38), channel_id=1, source_target_pairs={{0,3},{1,2},{2,1},{3,0},{4,7},{5,6},{6,5},{7,4},{8,11},{9,10},{10,... | collective-permute-start | bytes 399368 | tf_op jit(solution)/shard_map/ppermute | solution.py:316
  44.1 0.0 collective-permute-done.9.refs_9_
  44.1 0.0 collective-permute-start.14
  44.1 0.0 collective-permute-done.10.refs_10_
  44.1 0.0 collective-permute-done.11.refs_11_
  44.1 0.0 collective-permute-done.12.refs_12_
  44.1 4.0 %collective-permute-done.13.refs_13_ = bf16[8,8320]{1,0:T(8,128)(2,1)S(1)} collective-permute-done((bf16[8,8320]{1,0:T(8,128)(2,1)}, bf16[8,8320]{1,0:T(8,128)(2,1)S(1)}, u32[]{:S(2)}, u32[]{:S(2)}) %collective-permute-start.13) | collective-permute-done | bytes 133152 | tf_op jit(solution)/shard_map/ppermute | solution.py:316
  48.1 3.9 %collective-permute-done.14.refs_14_ = bf16[8,8320]{1,0:T(8,128)(2,1)S(1)} collective-permute-done((bf16[8,8320]{1,0:T(8,128)(2,1)}, bf16[8,8320]{1,0:T(8,128)(2,1)S(1)}, u32[]{:S(2)}, u32[]{:S(2)}) %collective-permute-start.14) | collective-permute-done | bytes 133152 | tf_op jit(solution)/shard_map/ppermute | solution.py:316
  51.9 0.0 copy-done
  51.9 1.2 %copy-done.2 = bf16[128,4096]{1,0:T(8,128)(2,1)S(1)} copy-done((bf16[128,4096]{1,0:T(8,128)(2,1)S(1)}, bf16[128,4096]{1,0:T(8,128)(2,1)}, u32[]{:S(2)}) %copy-start.2) | copy-done | bytes 1048600
  53.2 0.9 copy-done.3
  54.1 1.9 %adapt.1 = bf16[16,8,4096]{2,1,0:T(8,128)(2,1)} custom-call(bf16[8,8320]{1,0:T(8,128)(2,1)S(1)} %collective-permute-done.refs_0_, bf16[8,8320]{1,0:T(8,128)(2,1)S(1)} %collective-permute-done.1.refs_1_, bf16[8,8320]{1,0:T(8,128)(2,1)S(1)} %collective-permute-done.2.refs_2_, bf16[8,8320]{1,0:T(8,128)(2,1)S(1)} %collective-permute-done.3.refs_3_, ...), custom_call_target="tpu_custom_call" | custom-call | tf_op jit(solution)/shard_map/adapt/pallas_call | solution.py:147
  56.0 0.0 copy-start.5
  56.0 8.6 %all-to-all-start = ((bf16[16,8,4096]{2,1,0:T(8,128)(2,1)}), bf16[16,8,4096]{2,1,0:T(8,128)(2,1)S(1)}, u32[]{:S(2)}, u32[]{:S(2)}) async-start(bf16[16,8,4096]{2,1,0:T(8,128)(2,1)} %adapt.1), calls=%async_computation | async-start | bytes 2097152 | tf_op jit(solution)/shard_map/all_to_all | solution.py:321
  64.6 0.0 copy-done.5
  64.6 0.1 broadcast_in_dim.7
  64.6 0.1 broadcast_in_dim.8
  64.7 0.1 broadcast_in_dim.9.lens_ref
  64.8 0.0 copy-start.1
  64.8 1.2 %copy-done.1 = bf16[128,4096]{1,0:T(8,128)(2,1)S(1)} copy-done((bf16[128,4096]{1,0:T(8,128)(2,1)S(1)}, bf16[128,4096]{1,0:T(8,128)(2,1)}, u32[]{:S(2)}) %copy-start.1) | copy-done | bytes 1048600
  66.1 10.9 %prep.1 = (bf16[4,128,2048]{2,1,0:T(8,128)(2,1)S(1)}, bf16[4,91,192,128]{3,2,1,0:T(8,128)(2,1)}) custom-call(bf16[128,4096]{1,0:T(8,128)(2,1)S(1)} %copy-done.1, bf16[128,2,16,512]{3,2,1,0:T(8,128)(2,1)} %kv_ref.1), custom_call_target="tpu_custom_call" | custom-call | tf_op jit(solution)/shard_map/prep/pallas_call | solution.py:186
  77.0 10.5 %all-to-all-done = bf16[16,8,4096]{2,1,0:T(8,128)(2,1)S(1)} async-done(((bf16[16,8,4096]{2,1,0:T(8,128)(2,1)}), bf16[16,8,4096]{2,1,0:T(8,128)(2,1)S(1)}, u32[]{:S(2)}, u32[]{:S(2)}) %all-to-all-start) | async-done | bytes 1048608 | tf_op jit(solution)/shard_map/all_to_all | solution.py:321
  87.5 0.0 copy-done.4
  87.5 4.4 %attend.1 = bf16[128,4096]{1,0:T(8,128)(2,1)} custom-call(bf16[128,128]{1,0:T(8,128)(2,1)S(1)} %copy-done.4, bf16[128,4096]{1,0:T(8,128)(2,1)S(1)} %bitcast.3, bf16[4,128,2048]{2,1,0:T(8,128)(2,1)S(1)} %get-tuple-element.41.keys_ref, s32[16,1,128]{2,1,0:T(1,128)S(1)} %broadcast_in_dim.9.lens_ref, bf16[4,91,192,128]{3,2,1,0:T(8,128)(2,1)} %get-tuple-element.42.rest_hbm), custom_call_target="tpu_custom_call" | custom-call | tf_op jit(solution)/shard_map/attend/pallas_call | solution.py:286
  (3 shorter events, 0.0 us)
Async XLA Ops:
  0.0 51.9 %copy-start = (bf16[8192,128]{1,0:T(8,128)(2,1)S(1)}, bf16[8192,128]{1,0:T(8,128)(2,1)}, u32[]{:S(2)}) copy-start(bf16[8192,128]{1,0:T(8,128)(2,1)} %refs_16_.1) | copy-start | bytes 6291460
  5.0 12.1 %collective-permute-start = (bf16[8,8320]{1,0:T(8,128)(2,1)}, bf16[8,8320]{1,0:T(8,128)(2,1)S(1)}, u32[]{:S(2)}, u32[]{:S(2)}) collective-permute-start(bf16[8,8320]{1,0:T(8,128)(2,1)} %get-tuple-element.25), channel_id=1, source_target_pairs={{0,8},{1,9},{2,10},{3,11},{4,12},{5,13},{6,14},{7,15},{8,0},{9,1},... | collective-permute-start | bytes 399368 | tf_op jit(solution)/shard_map/ppermute | solution.py:316
  9.1 9.4 %collective-permute-start.1 = (bf16[8,8320]{1,0:T(8,128)(2,1)}, bf16[8,8320]{1,0:T(8,128)(2,1)S(1)}, u32[]{:S(2)}, u32[]{:S(2)}) collective-permute-start(bf16[8,8320]{1,0:T(8,128)(2,1)} %get-tuple-element.26), channel_id=1, source_target_pairs={{0,4},{1,5},{2,6},{3,7},{4,0},{5,1},{6,2},{7,3},{8,12},{9,13},{10,... | collective-permute-start | bytes 399368 | tf_op jit(solution)/shard_map/ppermute | solution.py:316
  10.7 10.4 %collective-permute-start.2 = (bf16[8,8320]{1,0:T(8,128)(2,1)}, bf16[8,8320]{1,0:T(8,128)(2,1)S(1)}, u32[]{:S(2)}, u32[]{:S(2)}) collective-permute-start(bf16[8,8320]{1,0:T(8,128)(2,1)} %get-tuple-element.27), channel_id=1, source_target_pairs={{0,9},{1,8},{2,11},{3,10},{4,13},{5,12},{6,15},{7,14},{8,1},{9,0},... | collective-permute-start | bytes 399368 | tf_op jit(solution)/shard_map/ppermute | solution.py:316
  10.7 12.6 %collective-permute-start.3 = (bf16[8,8320]{1,0:T(8,128)(2,1)}, bf16[8,8320]{1,0:T(8,128)(2,1)S(1)}, u32[]{:S(2)}, u32[]{:S(2)}) collective-permute-start(bf16[8,8320]{1,0:T(8,128)(2,1)} %get-tuple-element.28), channel_id=1, source_target_pairs={{0,5},{1,4},{2,7},{3,6},{4,1},{5,0},{6,3},{7,2},{8,13},{9,12},{10,... | collective-permute-start | bytes 399368 | tf_op jit(solution)/shard_map/ppermute | solution.py:316
  10.9 18.7 %collective-permute-start.4 = (bf16[8,8320]{1,0:T(8,128)(2,1)}, bf16[8,8320]{1,0:T(8,128)(2,1)S(1)}, u32[]{:S(2)}, u32[]{:S(2)}) collective-permute-start(bf16[8,8320]{1,0:T(8,128)(2,1)} %get-tuple-element.29), channel_id=1, source_target_pairs={{0,10},{1,11},{2,8},{3,9},{4,14},{5,15},{6,12},{7,13},{8,2},{9,3},... | collective-permute-start | bytes 399368 | tf_op jit(solution)/shard_map/ppermute | solution.py:316
  17.1 13.3 %collective-permute-start.5 = (bf16[8,8320]{1,0:T(8,128)(2,1)}, bf16[8,8320]{1,0:T(8,128)(2,1)S(1)}, u32[]{:S(2)}, u32[]{:S(2)}) collective-permute-start(bf16[8,8320]{1,0:T(8,128)(2,1)} %get-tuple-element.30), channel_id=1, source_target_pairs={{0,6},{1,7},{2,4},{3,5},{4,2},{5,3},{6,0},{7,1},{8,14},{9,15},{10,... | collective-permute-start | bytes 399368 | tf_op jit(solution)/shard_map/ppermute | solution.py:316
  18.4 14.5 %collective-permute-start.6 = (bf16[8,8320]{1,0:T(8,128)(2,1)}, bf16[8,8320]{1,0:T(8,128)(2,1)S(1)}, u32[]{:S(2)}, u32[]{:S(2)}) collective-permute-start(bf16[8,8320]{1,0:T(8,128)(2,1)} %get-tuple-element.31), channel_id=1, source_target_pairs={{0,11},{1,10},{2,9},{3,8},{4,15},{5,14},{6,13},{7,12},{8,3},{9,2},... | collective-permute-start | bytes 399368 | tf_op jit(solution)/shard_map/ppermute | solution.py:316
  21.1 12.4 %collective-permute-start.7 = (bf16[8,8320]{1,0:T(8,128)(2,1)}, bf16[8,8320]{1,0:T(8,128)(2,1)S(1)}, u32[]{:S(2)}, u32[]{:S(2)}) collective-permute-start(bf16[8,8320]{1,0:T(8,128)(2,1)} %get-tuple-element.32), channel_id=1, source_target_pairs={{0,7},{1,6},{2,5},{3,4},{4,3},{5,2},{6,1},{7,0},{8,15},{9,14},{10,... | collective-permute-start | bytes 399368 | tf_op jit(solution)/shard_map/ppermute | solution.py:316
  23.3 16.4 %collective-permute-start.8 = (bf16[8,8320]{1,0:T(8,128)(2,1)}, bf16[8,8320]{1,0:T(8,128)(2,1)S(1)}, u32[]{:S(2)}, u32[]{:S(2)}) collective-permute-start(bf16[8,8320]{1,0:T(8,128)(2,1)} %get-tuple-element.33), channel_id=1, source_target_pairs={{0,12},{1,13},{2,14},{3,15},{4,8},{5,9},{6,10},{7,11},{8,4},{9,5},... | collective-permute-start | bytes 399368 | tf_op jit(solution)/shard_map/ppermute | solution.py:316
  29.7 14.4 %collective-permute-start.9 = (bf16[8,8320]{1,0:T(8,128)(2,1)}, bf16[8,8320]{1,0:T(8,128)(2,1)S(1)}, u32[]{:S(2)}, u32[]{:S(2)}) collective-permute-start(bf16[8,8320]{1,0:T(8,128)(2,1)} %get-tuple-element.34), channel_id=1, source_target_pairs={{0,1},{1,0},{2,3},{3,2},{4,5},{5,4},{6,7},{7,6},{8,9},{9,8},{10,11... | collective-permute-start | bytes 399368 | tf_op jit(solution)/shard_map/ppermute | solution.py:316
  30.4 13.7 %collective-permute-start.10 = (bf16[8,8320]{1,0:T(8,128)(2,1)}, bf16[8,8320]{1,0:T(8,128)(2,1)S(1)}, u32[]{:S(2)}, u32[]{:S(2)}) collective-permute-start(bf16[8,8320]{1,0:T(8,128)(2,1)} %get-tuple-element.35), channel_id=1, source_target_pairs={{0,13},{1,12},{2,15},{3,14},{4,9},{5,8},{6,11},{7,10},{8,5},{9,4},... | collective-permute-start | bytes 399368 | tf_op jit(solution)/shard_map/ppermute | solution.py:316
  32.9 11.2 %collective-permute-start.11 = (bf16[8,8320]{1,0:T(8,128)(2,1)}, bf16[8,8320]{1,0:T(8,128)(2,1)S(1)}, u32[]{:S(2)}, u32[]{:S(2)}) collective-permute-start(bf16[8,8320]{1,0:T(8,128)(2,1)} %get-tuple-element.36), channel_id=1, source_target_pairs={{0,2},{1,3},{2,0},{3,1},{4,6},{5,7},{6,4},{7,5},{8,10},{9,11},{10,... | collective-permute-start | bytes 399368 | tf_op jit(solution)/shard_map/ppermute | solution.py:316
  33.5 10.6 %collective-permute-start.12 = (bf16[8,8320]{1,0:T(8,128)(2,1)}, bf16[8,8320]{1,0:T(8,128)(2,1)S(1)}, u32[]{:S(2)}, u32[]{:S(2)}) collective-permute-start(bf16[8,8320]{1,0:T(8,128)(2,1)} %get-tuple-element.37), channel_id=1, source_target_pairs={{0,14},{1,15},{2,12},{3,13},{4,10},{5,11},{6,8},{7,9},{8,6},{9,7},... | collective-permute-start | bytes 399368 | tf_op jit(solution)/shard_map/ppermute | solution.py:316
  39.7 8.4 %collective-permute-start.13 = (bf16[8,8320]{1,0:T(8,128)(2,1)}, bf16[8,8320]{1,0:T(8,128)(2,1)S(1)}, u32[]{:S(2)}, u32[]{:S(2)}) collective-permute-start(bf16[8,8320]{1,0:T(8,128)(2,1)} %get-tuple-element.38), channel_id=1, source_target_pairs={{0,3},{1,2},{2,1},{3,0},{4,7},{5,6},{6,5},{7,4},{8,11},{9,10},{10,... | collective-permute-start | bytes 399368 | tf_op jit(solution)/shard_map/ppermute | solution.py:316
  44.1 7.9 %collective-permute-start.14 = (bf16[8,8320]{1,0:T(8,128)(2,1)}, bf16[8,8320]{1,0:T(8,128)(2,1)S(1)}, u32[]{:S(2)}, u32[]{:S(2)}) collective-permute-start(bf16[8,8320]{1,0:T(8,128)(2,1)} %get-tuple-element.39), channel_id=1, source_target_pairs={{0,15},{1,14},{2,13},{3,12},{4,11},{5,10},{6,9},{7,8},{8,7},{9,6},... | collective-permute-start | bytes 399368 | tf_op jit(solution)/shard_map/ppermute | solution.py:316
  51.9 1.2 %copy-start.2 = (bf16[128,4096]{1,0:T(8,128)(2,1)S(1)}, bf16[128,4096]{1,0:T(8,128)(2,1)}, u32[]{:S(2)}) copy-start(bf16[128,4096]{1,0:T(8,128)(2,1)} %refs_17_.1) | copy-start | bytes 3145732
  53.2 0.9 copy-start.3
  56.0 8.6 %copy-start.5 = (s32[128]{0:T(128)S(1)}, s32[128]{0:T(128)}, u32[]{:S(2)}) copy-start(s32[128]{0:T(128)} %param.11) | copy-start | bytes 1540
  56.0 31.5 %all-to-all-start = ((bf16[16,8,4096]{2,1,0:T(8,128)(2,1)}), bf16[16,8,4096]{2,1,0:T(8,128)(2,1)S(1)}, u32[]{:S(2)}, u32[]{:S(2)}) async-start(bf16[16,8,4096]{2,1,0:T(8,128)(2,1)} %adapt.1), calls=%async_computation | async-start | bytes 2097152 | tf_op jit(solution)/shard_map/all_to_all | solution.py:321
  64.8 1.2 %copy-start.1 = (bf16[128,4096]{1,0:T(8,128)(2,1)S(1)}, bf16[128,4096]{1,0:T(8,128)(2,1)}, u32[]{:S(2)}) copy-start(bf16[128,4096]{1,0:T(8,128)(2,1)} %base_ref.1) | copy-start | bytes 3145732
  66.1 21.4 %copy-start.4 = (bf16[128,128]{1,0:T(8,128)(2,1)S(1)}, bf16[128,128]{1,0:T(8,128)(2,1)}, u32[]{:S(2)}) copy-start(bf16[128,128]{1,0:T(8,128)(2,1)} %get-tuple-element.24.routed_ref) | copy-start | bytes 98308

commit v19 on v18

--- a/solution.py
+++ b/solution.py
@@ -13,6 +13,9 @@
 LANES = 128
 SCALE = 2.0
 ROWS_STEP = 8
+PREP_STEPS = 2
+GROUPS = 4
+MOST_PERMUTES = 32
 COLUMNS_STEP = 1024
 ADAPT_STEP = 2048
 OUT_STEP = 1024
@@ -41,9 +44,9 @@
     place = jnp.sum(jnp.where(hits, before, 0.0), axis=0, keepdims=True).astype(jnp.int32)
     line = lax.broadcasted_iota(jnp.int32, (owners * slot_count, rows), 0)
     apart = owner ^ lax.axis_index("owner")
-    sent = line == apart * slot_count + place
-    label = jnp.sum(jnp.where(sent, local.astype(jnp.float32), 0.0), axis=1, keepdims=True)
-    return sent, line == owner * slot_count + place, label
+    routed = line == apart * slot_count + place
+    label = jnp.sum(jnp.where(routed, local.astype(jnp.float32), 0.0), axis=1, keepdims=True)
+    return routed, label
 
 
 def pack_kernel(owners, slot_count, held, slots_hbm, ids_hbm, hidden_hbm, routed_ref, *refs):
@@ -64,9 +67,9 @@
         copy.start()
     for copy in small:
         copy.wait()
-    sent, routed, label = routing(owners, slot_count, held, slots_ref[...], ids_ref[...])
-    sent = sent.astype(jnp.bfloat16)
+    routed, label = routing(owners, slot_count, held, slots_ref[...], ids_ref[...])
     routed_ref[...] = jnp.transpose(routed.astype(jnp.float32)).astype(routed_ref.dtype)
+    routed = routed.astype(jnp.bfloat16)
 
     def put(at, lines):
         for i, message_ref in enumerate(message_refs):
@@ -77,7 +80,7 @@
     put(width, jnp.broadcast_to(label, (label.shape[0], LANES)))
     for load, (at, size) in zip(loads, spans):
         load.wait()
-        put(at, jnp.dot(sent, rows_ref[:, at : at + size], preferred_element_type=jnp.float32))
+        put(at, jnp.dot(routed, rows_ref[:, at : at + size], preferred_element_type=jnp.float32))
 
 
 def pack(hidden, adapter_id, adapter_slot, owners, slot_count, held):
@@ -109,13 +112,11 @@
     ).astype(jnp.bfloat16)
 
 
-def adapt_kernel(order, *refs):
-    owners = len(order)
-    arrived_refs, (a_ref, b_ref, change_hbm, change_ref, sems) = refs[:owners], refs[owners:]
+def adapt_kernel(count, *refs):
+    arrived_refs, (a_ref, b_ref), change_refs = refs[:count], refs[count : count + 2], refs[-count:]
     width = a_ref.shape[0]
     slot_count = arrived_refs[0].shape[0]
-    me = lax.axis_index("owner")
-    low = jnp.zeros((owners * slot_count, a_ref.shape[1]), jnp.float32)
+    low = jnp.zeros((count * slot_count, a_ref.shape[1]), jnp.float32)
     for at in range(0, width, ADAPT_STEP):
         low += jnp.dot(
             stack(arrived_refs, at, ADAPT_STEP),
@@ -125,37 +126,26 @@
     label = stack(arrived_refs, width, LANES).astype(jnp.float32)[:, :1].astype(jnp.int32)
     column = lax.broadcasted_iota(jnp.int32, low.shape, 1) // RANK
     low = jnp.where(column == label, low, 0.0).astype(jnp.bfloat16)
-    stores = []
-    for i, at in enumerate(range(0, b_ref.shape[1], OUT_STEP)):
-        span = pl.ds(at, OUT_STEP)
+    for at in range(0, b_ref.shape[1], OUT_STEP):
         change = SCALE * jnp.dot(low, b_ref[:, at : at + OUT_STEP], preferred_element_type=jnp.float32)
-        for j, s in enumerate(order):
-            change_ref[me ^ s, :, at : at + OUT_STEP] = change[
-                j * slot_count : (j + 1) * slot_count
+        for i, change_ref in enumerate(change_refs):
+            change_ref[:, at : at + OUT_STEP] = change[
+                i * slot_count : (i + 1) * slot_count
             ].astype(change_ref.dtype)
-        stores.append(
-            pltpu.make_async_copy(change_ref.at[:, :, span], change_hbm.at[:, :, span], sems.at[i])
-        )
-        stores[-1].start()
-    for store in stores:
-        store.wait()
-
-
-def adapt(arrived, order, a_maps, b_maps):
-    owners = len(order)
-    change = jax.ShapeDtypeStruct((owners, arrived[0].shape[0], b_maps.shape[1]), jnp.bfloat16)
+
+
+def adapt(arrived, a_maps, b_maps, after):
+    count = len(arrived)
+    change = jax.ShapeDtypeStruct((arrived[0].shape[0], b_maps.shape[1]), jnp.bfloat16)
     return pl.pallas_call(
-        functools.partial(adapt_kernel, order),
-        in_specs=[pl.BlockSpec(memory_space=pltpu.VMEM)] * (owners + 2),
-        out_specs=pl.BlockSpec(memory_space=pl.ANY),
-        out_shape=change,
-        scratch_shapes=[
-            pltpu.VMEM(change.shape, change.dtype),
-            pltpu.SemaphoreType.DMA((pl.cdiv(b_maps.shape[1], OUT_STEP),)),
-        ],
-        compiler_params=pltpu.CompilerParams(vmem_limit_bytes=16 * 2**20),
+        functools.partial(adapt_kernel, count),
+        in_specs=[pl.BlockSpec(memory_space=pltpu.VMEM)] * (count + 2)
+        + [pl.BlockSpec(memory_space=pl.ANY)],
+        out_specs=[pl.BlockSpec(memory_space=pltpu.VMEM)] * count,
+        out_shape=[change] * count,
+        compiler_params=pltpu.CompilerParams(vmem_limit_bytes=GRANT),
         name="adapt",
-    )(*arrived, a_maps, b_maps)
+    )(*arrived, a_maps, b_maps, after)
 
 
 def tall(rows, group):
@@ -163,26 +153,28 @@
 
 
 def prep_kernel(group, base_ref, kv_ref, keys_ref, rest_ref):
-    step, context = kv_ref.shape[0], kv_ref.shape[2]
+    step, context = ROWS_STEP, kv_ref.shape[2]
     cells = step * context
-    for k in range(KVH):
-        head = slice(k * HEAD, (k + 1) * HEAD)
-        keys = kv_ref[:, 0, :, head].astype(jnp.float32).reshape(cells, HEAD)
-        keys_ref[k] = jnp.transpose(keys).astype(keys_ref.dtype)
-        rest_ref[k, 0, :cells] = kv_ref[:, 1, :, head].reshape(cells, HEAD)
-        base = base_ref[:, k * group * HEAD : (k + 1) * group * HEAD].astype(jnp.float32)
-        rest_ref[k, 0, cells:] = tall(base, group).astype(rest_ref.dtype)
+    for j in range(PREP_STEPS):
+        rows = slice(j * step, (j + 1) * step)
+        for k in range(KVH):
+            head = slice(k * HEAD, (k + 1) * HEAD)
+            keys = kv_ref[rows, 0, :, head].astype(jnp.float32).reshape(cells, HEAD)
+            keys_ref[k, :, j * cells : (j + 1) * cells] = jnp.transpose(keys).astype(keys_ref.dtype)
+            rest_ref[k, j, :cells] = kv_ref[rows, 1, :, head].reshape(cells, HEAD)
+            base = base_ref[:, k * group * HEAD : (k + 1) * group * HEAD].astype(jnp.float32)
+            rest_ref[k, j, cells:] = tall(base[rows], group).astype(rest_ref.dtype)
 
 
 def prep(base_q, kv_cache):
     rows, width = base_q.shape
     context = kv_cache.shape[2]
     group = width // (KVH * HEAD)
-    step = ROWS_STEP
+    step = ROWS_STEP * PREP_STEPS
     steps = rows // step
-    cells = step * context
-    lines = cells + group * step
-    length = max(pl.cdiv(TALL_BYTES, 2 * KVH * lines * HEAD), steps)
+    cells = ROWS_STEP * context
+    lines = cells + group * ROWS_STEP
+    length = max(pl.cdiv(TALL_BYTES, 2 * KVH * lines * HEAD * PREP_STEPS), steps) * PREP_STEPS
     return pl.pallas_call(
         functools.partial(prep_kernel, group),
         grid=(steps,),
@@ -191,8 +183,8 @@
             pl.BlockSpec((step, *kv_cache.shape[1:]), lambda i: (i, 0, 0, 0)),
         ],
         out_specs=[
-            pl.BlockSpec((KVH, HEAD, cells), lambda i: (0, 0, i)),
-            pl.BlockSpec((KVH, 1, lines, HEAD), lambda i: (0, i, 0, 0)),
+            pl.BlockSpec((KVH, HEAD, PREP_STEPS * cells), lambda i: (0, 0, i)),
+            pl.BlockSpec((KVH, PREP_STEPS, lines, HEAD), lambda i: (0, i, 0, 0)),
         ],
         out_shape=[
             jax.ShapeDtypeStruct((KVH, HEAD, rows * context), jnp.bfloat16),
@@ -203,9 +195,10 @@
     )(base_q, kv_cache)
 
 
-def attend_kernel(
-    group, context, routed_ref, returned_ref, keys_ref, lens_ref, rest_hbm, out_hbm, *scratch
-):
+def attend_kernel(group, context, order, *refs):
+    returned_refs, refs = refs[: len(order)], refs[len(order) :]
+    returned_refs = [returned_refs[order.index(s)] for s in range(len(order))]
+    routed_ref, keys_ref, lens_ref, rest_hbm, out_hbm, *scratch = refs
     query_ref, values_ref, bias_ref, scores_ref, expo_ref, out_ref, sems = scratch
     step = ROWS_STEP
     steps, lines, cells = bias_ref.shape
@@ -241,7 +234,7 @@
     for k in range(KVH):
         delta = jnp.dot(
             routed_ref[...],
-            returned_ref[:, k * span : (k + 1) * span],
+            stack(returned_refs, k * span, span),
             preferred_element_type=jnp.float32,
         )
         for copy in loads[k]:
@@ -276,16 +269,16 @@
         store.wait()
 
 
-def attend(routed, returned, cache_len, keys, rest, context):
-    rows, width = routed.shape[0], returned.shape[1]
+def attend(routed, returned, order, cache_len, keys, rest, context):
+    rows, width = routed.shape[0], returned[0].shape[1]
     group = width // (KVH * HEAD)
     step = ROWS_STEP
     steps = rows // step
     cells = step * context
     lens = jnp.repeat(cache_len, context).reshape(steps, 1, cells)
     return pl.pallas_call(
-        functools.partial(attend_kernel, group, context),
-        in_specs=[pl.BlockSpec(memory_space=pltpu.VMEM)] * 4 + [pl.BlockSpec(memory_space=pl.ANY)],
+        functools.partial(attend_kernel, group, context, order),
+        in_specs=[pl.BlockSpec(memory_space=pltpu.VMEM)] * (3 + len(order)) + [pl.BlockSpec(memory_space=pl.ANY)],
         out_specs=pl.BlockSpec(memory_space=pl.ANY),
         out_shape=jax.ShapeDtypeStruct((rows, width), jnp.bfloat16),
         scratch_shapes=[
@@ -299,7 +292,7 @@
         ],
         compiler_params=pltpu.CompilerParams(vmem_limit_bytes=GRANT),
         name="attend",
-    )(routed, returned, keys, lens, rest)
+    )(*returned, routed, keys, lens, rest)
 
 
 def on_device(hidden, adapter_id, adapter_slot, cache_len, base_q, kv_cache, a_maps, b_maps):
@@ -307,20 +300,36 @@
     rows = hidden.shape[0]
     held = a_maps.shape[1] // RANK
     slot_count = max(2, 2 * ((rows + 2 * owners - 1) // (2 * owners)))
-    bins = owners * slot_count
     routed, *messages = pack(hidden, adapter_id, adapter_slot, owners, slot_count, held)
     half = owners // 2
     near = [*range(half // 2, half), *range(1, half // 2)]
     order = [s for pair in zip(range(half, owners), [*near, 0]) for s in pair]
-    arrived = [
-        lax.ppermute(messages[s], "owner", [(i, i ^ s) for i in range(owners)]) if s else messages[s]
-        for s in order
-    ]
+
     keys, rest = prep(base_q, kv_cache)
-    change = adapt(arrived, order, a_maps, b_maps)
-    returned = lax.all_to_all(change, "owner", split_axis=0, concat_axis=0, tiled=True)
-    returned = returned.reshape(bins, returned.shape[2])
-    return attend(routed, returned, cache_len, keys, rest, kv_cache.shape[2])
+    size = owners // GROUPS
+    arrived = exchange(order, owners)(messages[s] for s in order)
+    changes = []
+    for at in range(0, owners, size):
+        changes += adapt(arrived[at : at + size], a_maps, b_maps, rest)
+    returned = exchange(order, owners)(changes)
+    return attend(routed, returned, order, cache_len, keys, rest, kv_cache.shape[2])
+
+
+def exchange(order, owners):
+    def permutes(messages):
+        return [
+            lax.ppermute(message, "owner", [(i, i ^ s) for i in range(owners)]) if s else message
+            for message, s in zip(messages, order)
+        ]
+
+    def whole(messages):
+        messages = dict(zip(order, messages))
+        place = lax.axis_index("owner") ^ jnp.arange(owners, dtype=jnp.int32)
+        blocks = jnp.stack([messages[s] for s in range(owners)])[place]
+        blocks = lax.all_to_all(blocks, "owner", split_axis=0, concat_axis=0, tiled=True)[place]
+        return [blocks[s] for s in order]
+
+    return permutes if owners <= MOST_PERMUTES else whole
 
 
 def solution(mesh):

time: 93.6 us -> 90.7 us (0.969); the launches traced: 91.9 us -> 90.4 us
  starting transfers between devices: 40.7 us -> 55.3 us
  waiting for transfers between devices: 25.4 us -> 14 us
  Pallas kernels: 22.2 us -> 19.3 us
  local copies, waits for them, and re-layouts: 3.63 us -> 1.75 us
    ppermute x15 -> x30, starting transfers between devices: 32.1 us -> 55.3 us  [permutes(): lax.ppermute(message, 'owner', [(i, i ^ s) for i in range(owners)])]
    all_to_all x1 -> x0, waiting for transfers between devices: 10.5 us -> none  [on_device(): lax.all_to_all(change, 'owner', split_axis=0, concat_axis=0, tiled=True)]
    all_to_all x1 -> x0, starting transfers between devices: 8.56 us -> none  [on_device(): lax.all_to_all(change, 'owner', split_axis=0, concat_axis=0, tiled=True)]
    pallas_call x1, Pallas kernels: 10.9 us -> 7.25 us  [prep(): pl.pallas_call(functools.partial(prep_kernel, group), grid=(steps,), in_s...]
    unnamed x12, local copies, waits for them, and re-layouts: 3.36 us -> 0.02 us
    broadcast_in_dim x3, local copies, waits for them, and re-layouts: 0.26 us -> 1.73 us  [attend(): lens = jnp.repeat(cache_len, context).reshape(steps, 1, cells)]
    ppermute x15 -> x30, waiting for transfers between devices: 14.8 us -> 14 us  [permutes(): lax.ppermute(message, 'owner', [(i, i ^ s) for i in range(owners)])]
    pallas_call x2 -> x5, Pallas kernels: 6.31 us -> 7.14 us  [the longest x1 4.41 us: attend(): pl.pallas_call(functools.partial(attend_kernel, group, context, order), i...]
  transfers between devices with their start and end apart: 16 -> 30, of which waited for: 6 -> 7; matrix products, arithmetic and copies ran while one was open for 0% -> 2% of each run, Pallas kernels for 12% -> 11%
where the time goes in v19:
time: 90.7 us; the launch traced here: 90.4 us
  starting transfers between devices  55.3 us (61%)
  Pallas kernels  19.3 us (21%)
  waiting for transfers between devices  14 us (15%)
  local copies, waits for them, and re-layouts  1.75 us (2%)
    ppermute x30, starting transfers between devices, permutes(): lax.ppermute(message, 'owner', [(i, i ^ s) for i in range(owners)])  55.3 us
    ppermute x30, waiting for transfers between devices, permutes(): lax.ppermute(message, 'owner', [(i, i ^ s) for i in range(owners)])  14 us
    pallas_call x1, Pallas kernels, prep(): pl.pallas_call(functools.partial(prep_kernel, group), grid=(steps,), in_s...  7.25 us
    pallas_call x1, Pallas kernels, pack(): pl.pallas_call(functools.partial(pack_kernel, owners, slot_count, held),...  4.91 us
    pallas_call x1, Pallas kernels, attend(): pl.pallas_call(functools.partial(attend_kernel, group, context, order), i...  4.41 us
    pallas_call x4, Pallas kernels, adapt(): pl.pallas_call(functools.partial(adapt_kernel, count), in_specs=[pl.Block...  2.73 us
  transfers between devices with their start and end apart: 30, of which 7 were waited for; matrix products, arithmetic and copies ran while one was open for 2% of the time, Pallas kernels for 11%

profile of v19, /device:TPU:0, one launch (start us, length us, event | category | flops | bytes accessed | tf_op | source)
XLA Modules:
  0.0 90.4 jit_solution(16449027714150743846)
XLA Ops:
  0.0 4.9 %pack.1 = (bf16[128,128]{1,0:T(8,128)(2,1)}, bf16[8,8320]{1,0:T(8,128)(2,1)}, bf16[8,8320]{1,0:T(8,128)(2,1)}, bf16[8,8320]{1,0:T(8,128)(2,1)}, bf16[8,8320]{1,0...) custom-call(s32[1,32]{1,0:T(1,128)} %bitcast.2, ...), custom_call_target="tpu_custom_call" | custom-call | tf_op jit(solution)/shard_map/pack/pallas_call | solution.py:91
  4.9 6.0 %collective-permute-start.24 = (bf16[8,8320]{1,0:T(8,128)(2,1)}, bf16[8,8320]{1,0:T(8,128)(2,1)S(1)}, u32[]{:S(2)}, u32[]{:S(2)}) collective-permute-start(bf16[8,8320]{1,0:T(8,128)(2,1)} %get-tuple-element.65), channel_id=1, source_target_pairs={{0,14},{1,15},{2,12},{3,13},{4,10},{5,11},{6,8},{7,9},{8,6},{9,7},... | collective-permute-start | bytes 399368 | tf_op jit(solution)/shard_map/ppermute | solution.py:321
  11.0 0.0 collective-permute-start.25
  11.0 1.4 %collective-permute-start.26 = (bf16[8,8320]{1,0:T(8,128)(2,1)}, bf16[8,8320]{1,0:T(8,128)(2,1)S(1)}, u32[]{:S(2)}, u32[]{:S(2)}) collective-permute-start(bf16[8,8320]{1,0:T(8,128)(2,1)} %get-tuple-element.67), channel_id=1, source_target_pairs={{0,15},{1,14},{2,13},{3,12},{4,11},{5,10},{6,9},{7,8},{8,7},{9,6},... | collective-permute-start | bytes 399368 | tf_op jit(solution)/shard_map/ppermute | solution.py:321
  12.4 3.6 %collective-permute-start.16 = (bf16[8,8320]{1,0:T(8,128)(2,1)}, bf16[8,8320]{1,0:T(8,128)(2,1)S(1)}, u32[]{:S(2)}, u32[]{:S(2)}) collective-permute-start(bf16[8,8320]{1,0:T(8,128)(2,1)} %get-tuple-element.57), channel_id=1, source_target_pairs={{0,12},{1,13},{2,14},{3,15},{4,8},{5,9},{6,10},{7,11},{8,4},{9,5},... | collective-permute-start | bytes 399368 | tf_op jit(solution)/shard_map/ppermute | solution.py:321
  16.0 0.9 collective-permute-start.18
  16.9 3.5 %collective-permute-done.25.refs_1_ = bf16[8,8320]{1,0:T(8,128)(2,1)S(1)} collective-permute-done((bf16[8,8320]{1,0:T(8,128)(2,1)}, bf16[8,8320]{1,0:T(8,128)(2,1)S(1)}, u32[]{:S(2)}, u32[]{:S(2)}) %collective-permute-start.25) | collective-permute-done | bytes 133152 | tf_op jit(solution)/shard_map/ppermute | solution.py:321
  20.4 1.3 %collective-permute-start.19 = (bf16[8,8320]{1,0:T(8,128)(2,1)}, bf16[8,8320]{1,0:T(8,128)(2,1)S(1)}, u32[]{:S(2)}, u32[]{:S(2)}) collective-permute-start(bf16[8,8320]{1,0:T(8,128)(2,1)} %get-tuple-element.60), channel_id=1, source_target_pairs={{0,2},{1,3},{2,0},{3,1},{4,6},{5,7},{6,4},{7,5},{8,10},{9,11},{10,... | collective-permute-start | bytes 399368 | tf_op jit(solution)/shard_map/ppermute | solution.py:321
  21.7 0.0 collective-permute-done.26.refs_2_
  21.7 9.5 %collective-permute-start.10 = (bf16[8,8320]{1,0:T(8,128)(2,1)}, bf16[8,8320]{1,0:T(8,128)(2,1)S(1)}, u32[]{:S(2)}, u32[]{:S(2)}) collective-permute-start(bf16[8,8320]{1,0:T(8,128)(2,1)} %get-tuple-element.51), channel_id=1, source_target_pairs={{0,11},{1,10},{2,9},{3,8},{4,15},{5,14},{6,13},{7,12},{8,3},{9,2},... | collective-permute-start | bytes 399368 | tf_op jit(solution)/shard_map/ppermute | solution.py:321
  31.2 0.0 collective-permute-done.16.refs_0_
  31.2 0.0 collective-permute-start.11
  31.2 0.0 collective-permute-done.17.refs_1_
  31.2 1.6 %collective-permute-start.8 = (bf16[8,8320]{1,0:T(8,128)(2,1)}, bf16[8,8320]{1,0:T(8,128)(2,1)S(1)}, u32[]{:S(2)}, u32[]{:S(2)}) collective-permute-start(bf16[8,8320]{1,0:T(8,128)(2,1)} %get-tuple-element.49), channel_id=1, source_target_pairs={{0,10},{1,11},{2,8},{3,9},{4,14},{5,15},{6,12},{7,13},{8,2},{9,3},... | collective-permute-start | bytes 399368 | tf_op jit(solution)/shard_map/ppermute | solution.py:321
  32.9 0.0 collective-permute-done.18.refs_2_
  32.9 3.9 %collective-permute-start.9 = (bf16[8,8320]{1,0:T(8,128)(2,1)}, bf16[8,8320]{1,0:T(8,128)(2,1)S(1)}, u32[]{:S(2)}, u32[]{:S(2)}) collective-permute-start(bf16[8,8320]{1,0:T(8,128)(2,1)} %get-tuple-element.50), channel_id=1, source_target_pairs={{0,6},{1,7},{2,4},{3,5},{4,2},{5,3},{6,0},{7,1},{8,14},{9,15},{10,... | collective-permute-start | bytes 399368 | tf_op jit(solution)/shard_map/ppermute | solution.py:321
  36.7 0.5 collective-permute-start
  37.3 2.8 %collective-permute-done.10.refs_2_ = bf16[8,8320]{1,0:T(8,128)(2,1)S(1)} collective-permute-done((bf16[8,8320]{1,0:T(8,128)(2,1)}, bf16[8,8320]{1,0:T(8,128)(2,1)S(1)}, u32[]{:S(2)}, u32[]{:S(2)}) %collective-permute-start.10) | collective-permute-done | bytes 133152 | tf_op jit(solution)/shard_map/ppermute | solution.py:321
  40.1 3.3 %collective-permute-start.1 = (bf16[8,8320]{1,0:T(8,128)(2,1)}, bf16[8,8320]{1,0:T(8,128)(2,1)S(1)}, u32[]{:S(2)}, u32[]{:S(2)}) collective-permute-start(bf16[8,8320]{1,0:T(8,128)(2,1)} %get-tuple-element.41), channel_id=1, source_target_pairs={{0,4},{1,5},{2,6},{3,7},{4,0},{5,1},{6,2},{7,3},{8,12},{9,13},{10,... | collective-permute-start | bytes 399368 | tf_op jit(solution)/shard_map/ppermute | solution.py:321
  43.4 0.0 collective-permute-done.11.refs_3_
  43.4 0.4 collective-permute-start.2
  43.8 2.9 %collective-permute-done.8.refs_0_ = bf16[8,8320]{1,0:T(8,128)(2,1)S(1)} collective-permute-done((bf16[8,8320]{1,0:T(8,128)(2,1)}, bf16[8,8320]{1,0:T(8,128)(2,1)S(1)}, u32[]{:S(2)}, u32[]{:S(2)}) %collective-permute-start.8) | collective-permute-done | bytes 133152 | tf_op jit(solution)/shard_map/ppermute | solution.py:321
  46.7 0.0 collective-permute-start.3
  46.8 7.3 %prep.1 = (bf16[4,128,2048]{2,1,0:T(8,128)(2,1)S(1)}, bf16[4,92,192,128]{3,2,1,0:T(8,128)(2,1)}) custom-call(bf16[128,4096]{1,0:T(8,128)(2,1)S(1)} %copy-done.2, bf16[128,2,16,512]{3,2,1,0:T(8,128)(2,1)} %kv_ref.1), custom_call_target="tpu_custom_call" | custom-call | tf_op jit(solution)/shard_map/prep/pallas_call | solution.py:178
  54.0 0.7 adapt.7
  54.7 0.7 adapt.6
  55.4 6.1 %collective-permute-start.27 = (bf16[8,4096]{1,0:T(8,128)(2,1)S(1)}, bf16[8,4096]{1,0:T(8,128)(2,1)S(1)}, u32[]{:S(2)}, u32[]{:S(2)}) collective-permute-start(bf16[8,4096]{1,0:T(8,128)(2,1)S(1)} %get-tuple-element.69), channel_id=1, source_target_pairs={{0,14},{1,15},{2,12},{3,13},{4,10},{5,11},{6,8},{7,9},{8,6},{9,7},... | collective-permute-start | bytes 196616 | tf_op jit(solution)/shard_map/ppermute | solution.py:321
  61.5 2.3 %collective-permute-start.29 = (bf16[8,4096]{1,0:T(8,128)(2,1)S(1)}, bf16[8,4096]{1,0:T(8,128)(2,1)S(1)}, u32[]{:S(2)}, u32[]{:S(2)}) collective-permute-start(bf16[8,4096]{1,0:T(8,128)(2,1)S(1)} %get-tuple-element.71), channel_id=1, source_target_pairs={{0,15},{1,14},{2,13},{3,12},{4,11},{5,10},{6,9},{7,8},{8,7},{9,6},... | collective-permute-start | bytes 196616 | tf_op jit(solution)/shard_map/ppermute | solution.py:321
  63.8 2.7 %collective-permute-start.20 = (bf16[8,4096]{1,0:T(8,128)(2,1)S(1)}, bf16[8,4096]{1,0:T(8,128)(2,1)S(1)}, u32[]{:S(2)}, u32[]{:S(2)}) collective-permute-start(bf16[8,4096]{1,0:T(8,128)(2,1)S(1)} %get-tuple-element.61), channel_id=1, source_target_pairs={{0,12},{1,13},{2,14},{3,15},{4,8},{5,9},{6,10},{7,11},{8,4},{9,5},... | collective-permute-start | bytes 196616 | tf_op jit(solution)/shard_map/ppermute | solution.py:321
  66.5 0.7 adapt.5
  67.2 1.3 %collective-permute-start.22 = (bf16[8,4096]{1,0:T(8,128)(2,1)S(1)}, bf16[8,4096]{1,0:T(8,128)(2,1)S(1)}, u32[]{:S(2)}, u32[]{:S(2)}) collective-permute-start(bf16[8,4096]{1,0:T(8,128)(2,1)S(1)} %get-tuple-element.63), channel_id=1, source_target_pairs={{0,13},{1,12},{2,15},{3,14},{4,9},{5,8},{6,11},{7,10},{8,5},{9,4},... | collective-permute-start | bytes 196616 | tf_op jit(solution)/shard_map/ppermute | solution.py:321
  68.5 2.2 %collective-permute-start.12 = (bf16[8,4096]{1,0:T(8,128)(2,1)S(1)}, bf16[8,4096]{1,0:T(8,128)(2,1)S(1)}, u32[]{:S(2)}, u32[]{:S(2)}) collective-permute-start(bf16[8,4096]{1,0:T(8,128)(2,1)S(1)} %get-tuple-element.53), channel_id=1, source_target_pairs={{0,10},{1,11},{2,8},{3,9},{4,14},{5,15},{6,12},{7,13},{8,2},{9,3},... | collective-permute-start | bytes 196616 | tf_op jit(solution)/shard_map/ppermute | solution.py:321
  70.8 2.0 %collective-permute-start.13 = (bf16[8,4096]{1,0:T(8,128)(2,1)S(1)}, bf16[8,4096]{1,0:T(8,128)(2,1)S(1)}, u32[]{:S(2)}, u32[]{:S(2)}) collective-permute-start(bf16[8,4096]{1,0:T(8,128)(2,1)S(1)} %get-tuple-element.54), channel_id=1, source_target_pairs={{0,6},{1,7},{2,4},{3,5},{4,2},{5,3},{6,0},{7,1},{8,14},{9,15},{10,... | collective-permute-start | bytes 196616 | tf_op jit(solution)/shard_map/ppermute | solution.py:321
  72.8 0.1 collective-permute-start.14
  72.8 0.7 adapt.4
  73.5 2.3 %collective-permute-start.15 = (bf16[8,4096]{1,0:T(8,128)(2,1)S(1)}, bf16[8,4096]{1,0:T(8,128)(2,1)S(1)}, u32[]{:S(2)}, u32[]{:S(2)}) collective-permute-start(bf16[8,4096]{1,0:T(8,128)(2,1)S(1)} %get-tuple-element.56), channel_id=1, source_target_pairs={{0,7},{1,6},{2,5},{3,4},{4,3},{5,2},{6,1},{7,0},{8,15},{9,14},{10,... | collective-permute-start | bytes 196616 | tf_op jit(solution)/shard_map/ppermute | solution.py:321
  75.8 1.8 %collective-permute-start.4 = (bf16[8,4096]{1,0:T(8,128)(2,1)S(1)}, bf16[8,4096]{1,0:T(8,128)(2,1)S(1)}, u32[]{:S(2)}, u32[]{:S(2)}) collective-permute-start(bf16[8,4096]{1,0:T(8,128)(2,1)S(1)} %get-tuple-element.45), channel_id=1, source_target_pairs={{0,8},{1,9},{2,10},{3,11},{4,12},{5,13},{6,14},{7,15},{8,0},{9,1},... | collective-permute-start | bytes 196616 | tf_op jit(solution)/shard_map/ppermute | solution.py:321
  77.7 1.4 %collective-permute-start.5 = (bf16[8,4096]{1,0:T(8,128)(2,1)S(1)}, bf16[8,4096]{1,0:T(8,128)(2,1)S(1)}, u32[]{:S(2)}, u32[]{:S(2)}) collective-permute-start(bf16[8,4096]{1,0:T(8,128)(2,1)S(1)} %get-tuple-element.46), channel_id=1, source_target_pairs={{0,4},{1,5},{2,6},{3,7},{4,0},{5,1},{6,2},{7,3},{8,12},{9,13},{10,... | collective-permute-start | bytes 196616 | tf_op jit(solution)/shard_map/ppermute | solution.py:321
  79.1 1.0 %collective-permute-done.14.refs_6_ = bf16[8,4096]{1,0:T(8,128)(2,1)S(1)} collective-permute-done((bf16[8,4096]{1,0:T(8,128)(2,1)S(1)}, bf16[8,4096]{1,0:T(8,128)(2,1)S(1)}, u32[]{:S(2)}, u32[]{:S(2)}) %collective-permute-start.14) | collective-permute-done | bytes 65568 | tf_op jit(solution)/shard_map/ppermute | solution.py:321
  80.1 0.4 collective-permute-start.7
  80.5 0.1 broadcast_in_dim.7
  80.6 0.7 broadcast_in_dim.8
  81.3 0.9 %broadcast_in_dim.9.refs_18_ = s32[16,1,128]{2,1,0:T(1,128)S(1)} reshape(s32[16,8,16]{2,1,0:T(8,128)} %broadcast_in_dim.8) | data formatting | bytes 16384 | tf_op jit(solution)/shard_map/broadcast_in_dim | solution.py:278
  82.3 0.0 collective-permute-done.4.refs_0_
  82.3 2.6 %collective-permute-done.5.refs_1_ = bf16[8,4096]{1,0:T(8,128)(2,1)S(1)} collective-permute-done((bf16[8,4096]{1,0:T(8,128)(2,1)S(1)}, bf16[8,4096]{1,0:T(8,128)(2,1)S(1)}, u32[]{:S(2)}, u32[]{:S(2)}) %collective-permute-start.5) | collective-permute-done | bytes 65568 | tf_op jit(solution)/shard_map/ppermute | solution.py:321
  84.9 0.6 collective-permute-done.6.refs_2_
  85.5 0.5 collective-permute-done.7.refs_3_
  86.0 4.4 %attend.1 = bf16[128,4096]{1,0:T(8,128)(2,1)} custom-call(bf16[8,4096]{1,0:T(8,128)(2,1)S(1)} %collective-permute-done.4.refs_0_, bf16[8,4096]{1,0:T(8,128)(2,1)S(1)} %collective-permute-done.5.refs_1_, bf16[8,4096]{1,0:T(8,128)(2,1)S(1)} %collective-permute-done.6.refs_2_, bf16[8,4096]{1,0:T(8,128)(2,1)S(1)} %collective-permute-done.7.refs_3_, ...), custom_call_target="tpu_custom_call" | custom-call | tf_op jit(solution)/shard_map/attend/pallas_call | solution.py:279
  (34 shorter events, 0.1 us)
Async XLA Ops:
  0.0 46.7 %copy-start.2 = (bf16[128,4096]{1,0:T(8,128)(2,1)S(1)}, bf16[128,4096]{1,0:T(8,128)(2,1)}, u32[]{:S(2)}) copy-start(bf16[128,4096]{1,0:T(8,128)(2,1)} %base_ref.1) | copy-start | bytes 3145732
  4.9 11.1 %collective-permute-start.24 = (bf16[8,8320]{1,0:T(8,128)(2,1)}, bf16[8,8320]{1,0:T(8,128)(2,1)S(1)}, u32[]{:S(2)}, u32[]{:S(2)}) collective-permute-start(bf16[8,8320]{1,0:T(8,128)(2,1)} %get-tuple-element.65), channel_id=1, source_target_pairs={{0,14},{1,15},{2,12},{3,13},{4,10},{5,11},{6,8},{7,9},{8,6},{9,7},... | collective-permute-start | bytes 399368 | tf_op jit(solution)/shard_map/ppermute | solution.py:321
  11.0 9.4 %collective-permute-start.25 = (bf16[8,8320]{1,0:T(8,128)(2,1)}, bf16[8,8320]{1,0:T(8,128)(2,1)S(1)}, u32[]{:S(2)}, u32[]{:S(2)}) collective-permute-start(bf16[8,8320]{1,0:T(8,128)(2,1)} %get-tuple-element.66), channel_id=1, source_target_pairs={{0,3},{1,2},{2,1},{3,0},{4,7},{5,6},{6,5},{7,4},{8,11},{9,10},{10,... | collective-permute-start | bytes 399368 | tf_op jit(solution)/shard_map/ppermute | solution.py:321
  11.0 10.8 %collective-permute-start.26 = (bf16[8,8320]{1,0:T(8,128)(2,1)}, bf16[8,8320]{1,0:T(8,128)(2,1)S(1)}, u32[]{:S(2)}, u32[]{:S(2)}) collective-permute-start(bf16[8,8320]{1,0:T(8,128)(2,1)} %get-tuple-element.67), channel_id=1, source_target_pairs={{0,15},{1,14},{2,13},{3,12},{4,11},{5,10},{6,9},{7,8},{8,7},{9,6},... | collective-permute-start | bytes 399368 | tf_op jit(solution)/shard_map/ppermute | solution.py:321
  12.4 18.8 %collective-permute-start.16 = (bf16[8,8320]{1,0:T(8,128)(2,1)}, bf16[8,8320]{1,0:T(8,128)(2,1)S(1)}, u32[]{:S(2)}, u32[]{:S(2)}) collective-permute-start(bf16[8,8320]{1,0:T(8,128)(2,1)} %get-tuple-element.57), channel_id=1, source_target_pairs={{0,12},{1,13},{2,14},{3,15},{4,8},{5,9},{6,10},{7,11},{8,4},{9,5},... | collective-permute-start | bytes 399368 | tf_op jit(solution)/shard_map/ppermute | solution.py:321
  16.0 15.2 %collective-permute-start.17 = (bf16[8,8320]{1,0:T(8,128)(2,1)}, bf16[8,8320]{1,0:T(8,128)(2,1)S(1)}, u32[]{:S(2)}, u32[]{:S(2)}) collective-permute-start(bf16[8,8320]{1,0:T(8,128)(2,1)} %get-tuple-element.58), channel_id=1, source_target_pairs={{0,1},{1,0},{2,3},{3,2},{4,5},{5,4},{6,7},{7,6},{8,9},{9,8},{10,11... | collective-permute-start | bytes 399368 | tf_op jit(solution)/shard_map/ppermute | solution.py:321
  16.0 16.9 %collective-permute-start.18 = (bf16[8,8320]{1,0:T(8,128)(2,1)}, bf16[8,8320]{1,0:T(8,128)(2,1)S(1)}, u32[]{:S(2)}, u32[]{:S(2)}) collective-permute-start(bf16[8,8320]{1,0:T(8,128)(2,1)} %get-tuple-element.59), channel_id=1, source_target_pairs={{0,13},{1,12},{2,15},{3,14},{4,9},{5,8},{6,11},{7,10},{8,5},{9,4},... | collective-permute-start | bytes 399368 | tf_op jit(solution)/shard_map/ppermute | solution.py:321
  20.4 16.3 %collective-permute-start.19 = (bf16[8,8320]{1,0:T(8,128)(2,1)}, bf16[8,8320]{1,0:T(8,128)(2,1)S(1)}, u32[]{:S(2)}, u32[]{:S(2)}) collective-permute-start(bf16[8,8320]{1,0:T(8,128)(2,1)} %get-tuple-element.60), channel_id=1, source_target_pairs={{0,2},{1,3},{2,0},{3,1},{4,6},{5,7},{6,4},{7,5},{8,10},{9,11},{10,... | collective-permute-start | bytes 399368 | tf_op jit(solution)/shard_map/ppermute | solution.py:321
  21.7 18.4 %collective-permute-start.10 = (bf16[8,8320]{1,0:T(8,128)(2,1)}, bf16[8,8320]{1,0:T(8,128)(2,1)S(1)}, u32[]{:S(2)}, u32[]{:S(2)}) collective-permute-start(bf16[8,8320]{1,0:T(8,128)(2,1)} %get-tuple-element.51), channel_id=1, source_target_pairs={{0,11},{1,10},{2,9},{3,8},{4,15},{5,14},{6,13},{7,12},{8,3},{9,2},... | collective-permute-start | bytes 399368 | tf_op jit(solution)/shard_map/ppermute | solution.py:321
  31.2 12.2 %collective-permute-start.11 = (bf16[8,8320]{1,0:T(8,128)(2,1)}, bf16[8,8320]{1,0:T(8,128)(2,1)S(1)}, u32[]{:S(2)}, u32[]{:S(2)}) collective-permute-start(bf16[8,8320]{1,0:T(8,128)(2,1)} %get-tuple-element.52), channel_id=1, source_target_pairs={{0,7},{1,6},{2,5},{3,4},{4,3},{5,2},{6,1},{7,0},{8,15},{9,14},{10,... | collective-permute-start | bytes 399368 | tf_op jit(solution)/shard_map/ppermute | solution.py:321
  31.2 15.5 %collective-permute-start.8 = (bf16[8,8320]{1,0:T(8,128)(2,1)}, bf16[8,8320]{1,0:T(8,128)(2,1)S(1)}, u32[]{:S(2)}, u32[]{:S(2)}) collective-permute-start(bf16[8,8320]{1,0:T(8,128)(2,1)} %get-tuple-element.49), channel_id=1, source_target_pairs={{0,10},{1,11},{2,8},{3,9},{4,14},{5,15},{6,12},{7,13},{8,2},{9,3},... | collective-permute-start | bytes 399368 | tf_op jit(solution)/shard_map/ppermute | solution.py:321
  32.9 22.5 %collective-permute-start.9 = (bf16[8,8320]{1,0:T(8,128)(2,1)}, bf16[8,8320]{1,0:T(8,128)(2,1)S(1)}, u32[]{:S(2)}, u32[]{:S(2)}) collective-permute-start(bf16[8,8320]{1,0:T(8,128)(2,1)} %get-tuple-element.50), channel_id=1, source_target_pairs={{0,6},{1,7},{2,4},{3,5},{4,2},{5,3},{6,0},{7,1},{8,14},{9,15},{10,... | collective-permute-start | bytes 399368 | tf_op jit(solution)/shard_map/ppermute | solution.py:321
  36.7 24.8 %collective-permute-start = (bf16[8,8320]{1,0:T(8,128)(2,1)}, bf16[8,8320]{1,0:T(8,128)(2,1)S(1)}, u32[]{:S(2)}, u32[]{:S(2)}) collective-permute-start(bf16[8,8320]{1,0:T(8,128)(2,1)} %get-tuple-element.40), channel_id=1, source_target_pairs={{0,8},{1,9},{2,10},{3,11},{4,12},{5,13},{6,14},{7,15},{8,0},{9,1},... | collective-permute-start | bytes 399368 | tf_op jit(solution)/shard_map/ppermute | solution.py:321
  40.1 21.4 %collective-permute-start.1 = (bf16[8,8320]{1,0:T(8,128)(2,1)}, bf16[8,8320]{1,0:T(8,128)(2,1)S(1)}, u32[]{:S(2)}, u32[]{:S(2)}) collective-permute-start(bf16[8,8320]{1,0:T(8,128)(2,1)} %get-tuple-element.41), channel_id=1, source_target_pairs={{0,4},{1,5},{2,6},{3,7},{4,0},{5,1},{6,2},{7,3},{8,12},{9,13},{10,... | collective-permute-start | bytes 399368 | tf_op jit(solution)/shard_map/ppermute | solution.py:321
  43.4 20.4 %collective-permute-start.2 = (bf16[8,8320]{1,0:T(8,128)(2,1)}, bf16[8,8320]{1,0:T(8,128)(2,1)S(1)}, u32[]{:S(2)}, u32[]{:S(2)}) collective-permute-start(bf16[8,8320]{1,0:T(8,128)(2,1)} %get-tuple-element.42), channel_id=1, source_target_pairs={{0,9},{1,8},{2,11},{3,10},{4,13},{5,12},{6,15},{7,14},{8,1},{9,0},... | collective-permute-start | bytes 399368 | tf_op jit(solution)/shard_map/ppermute | solution.py:321
  46.7 7.3 %copy-start = (bf16[8192,128]{1,0:T(8,128)(2,1)S(1)}, bf16[8192,128]{1,0:T(8,128)(2,1)}, u32[]{:S(2)}) copy-start(bf16[8192,128]{1,0:T(8,128)(2,1)} %refs_4_.7) | copy-start | bytes 6291460
  46.7 7.3 %copy-start.1 = (bf16[128,4096]{1,0:T(8,128)(2,1)S(1)}, bf16[128,4096]{1,0:T(8,128)(2,1)}, u32[]{:S(2)}) copy-start(bf16[128,4096]{1,0:T(8,128)(2,1)} %refs_5_.7) | copy-start | bytes 3145732
  46.7 7.3 %copy-start.3 = (bf16[8,8320]{1,0:T(8,128)(2,1)S(1)}, bf16[8,8320]{1,0:T(8,128)(2,1)}, u32[]{:S(2)}) copy-start(bf16[8,8320]{1,0:T(8,128)(2,1)} %get-tuple-element.68.refs_3_) | copy-start | bytes 399364
  46.7 19.8 %collective-permute-start.3 = (bf16[8,8320]{1,0:T(8,128)(2,1)}, bf16[8,8320]{1,0:T(8,128)(2,1)S(1)}, u32[]{:S(2)}, u32[]{:S(2)}) collective-permute-start(bf16[8,8320]{1,0:T(8,128)(2,1)} %get-tuple-element.43), channel_id=1, source_target_pairs={{0,5},{1,4},{2,7},{3,6},{4,1},{5,0},{6,3},{7,2},{8,13},{9,12},{10,... | collective-permute-start | bytes 399368 | tf_op jit(solution)/shard_map/ppermute | solution.py:321
  55.4 11.8 %collective-permute-start.27 = (bf16[8,4096]{1,0:T(8,128)(2,1)S(1)}, bf16[8,4096]{1,0:T(8,128)(2,1)S(1)}, u32[]{:S(2)}, u32[]{:S(2)}) collective-permute-start(bf16[8,4096]{1,0:T(8,128)(2,1)S(1)} %get-tuple-element.69), channel_id=1, source_target_pairs={{0,14},{1,15},{2,12},{3,13},{4,10},{5,11},{6,8},{7,9},{8,6},{9,7},... | collective-permute-start | bytes 196616 | tf_op jit(solution)/shard_map/ppermute | solution.py:321
  61.5 7.0 %collective-permute-start.28 = (bf16[8,4096]{1,0:T(8,128)(2,1)S(1)}, bf16[8,4096]{1,0:T(8,128)(2,1)S(1)}, u32[]{:S(2)}, u32[]{:S(2)}) collective-permute-start(bf16[8,4096]{1,0:T(8,128)(2,1)S(1)} %get-tuple-element.70), channel_id=1, source_target_pairs={{0,3},{1,2},{2,1},{3,0},{4,7},{5,6},{6,5},{7,4},{8,11},{9,10},{10,... | collective-permute-start | bytes 196616 | tf_op jit(solution)/shard_map/ppermute | solution.py:321
  61.5 7.0 %collective-permute-start.29 = (bf16[8,4096]{1,0:T(8,128)(2,1)S(1)}, bf16[8,4096]{1,0:T(8,128)(2,1)S(1)}, u32[]{:S(2)}, u32[]{:S(2)}) collective-permute-start(bf16[8,4096]{1,0:T(8,128)(2,1)S(1)} %get-tuple-element.71), channel_id=1, source_target_pairs={{0,15},{1,14},{2,13},{3,12},{4,11},{5,10},{6,9},{7,8},{8,7},{9,6},... | collective-permute-start | bytes 196616 | tf_op jit(solution)/shard_map/ppermute | solution.py:321
  63.8 6.9 %collective-permute-start.20 = (bf16[8,4096]{1,0:T(8,128)(2,1)S(1)}, bf16[8,4096]{1,0:T(8,128)(2,1)S(1)}, u32[]{:S(2)}, u32[]{:S(2)}) collective-permute-start(bf16[8,4096]{1,0:T(8,128)(2,1)S(1)} %get-tuple-element.61), channel_id=1, source_target_pairs={{0,12},{1,13},{2,14},{3,15},{4,8},{5,9},{6,10},{7,11},{8,4},{9,5},... | collective-permute-start | bytes 196616 | tf_op jit(solution)/shard_map/ppermute | solution.py:321
  66.5 6.2 %collective-permute-start.21 = (bf16[8,4096]{1,0:T(8,128)(2,1)S(1)}, bf16[8,4096]{1,0:T(8,128)(2,1)S(1)}, u32[]{:S(2)}, u32[]{:S(2)}) collective-permute-start(bf16[8,4096]{1,0:T(8,128)(2,1)S(1)} %get-tuple-element.62), channel_id=1, source_target_pairs={{0,1},{1,0},{2,3},{3,2},{4,5},{5,4},{6,7},{7,6},{8,9},{9,8},{10,11... | collective-permute-start | bytes 196616 | tf_op jit(solution)/shard_map/ppermute | solution.py:321
  67.2 6.3 %collective-permute-start.22 = (bf16[8,4096]{1,0:T(8,128)(2,1)S(1)}, bf16[8,4096]{1,0:T(8,128)(2,1)S(1)}, u32[]{:S(2)}, u32[]{:S(2)}) collective-permute-start(bf16[8,4096]{1,0:T(8,128)(2,1)S(1)} %get-tuple-element.63), channel_id=1, source_target_pairs={{0,13},{1,12},{2,15},{3,14},{4,9},{5,8},{6,11},{7,10},{8,5},{9,4},... | collective-permute-start | bytes 196616 | tf_op jit(solution)/shard_map/ppermute | solution.py:321
  68.5 7.3 %collective-permute-start.23 = (bf16[8,4096]{1,0:T(8,128)(2,1)S(1)}, bf16[8,4096]{1,0:T(8,128)(2,1)S(1)}, u32[]{:S(2)}, u32[]{:S(2)}) collective-permute-start(bf16[8,4096]{1,0:T(8,128)(2,1)S(1)} %get-tuple-element.64), channel_id=1, source_target_pairs={{0,2},{1,3},{2,0},{3,1},{4,6},{5,7},{6,4},{7,5},{8,10},{9,11},{10,... | collective-permute-start | bytes 196616 | tf_op jit(solution)/shard_map/ppermute | solution.py:321
  68.5 9.2 %collective-permute-start.12 = (bf16[8,4096]{1,0:T(8,128)(2,1)S(1)}, bf16[8,4096]{1,0:T(8,128)(2,1)S(1)}, u32[]{:S(2)}, u32[]{:S(2)}) collective-permute-start(bf16[8,4096]{1,0:T(8,128)(2,1)S(1)} %get-tuple-element.53), channel_id=1, source_target_pairs={{0,10},{1,11},{2,8},{3,9},{4,14},{5,15},{6,12},{7,13},{8,2},{9,3},... | collective-permute-start | bytes 196616 | tf_op jit(solution)/shard_map/ppermute | solution.py:321
  70.8 8.3 %collective-permute-start.13 = (bf16[8,4096]{1,0:T(8,128)(2,1)S(1)}, bf16[8,4096]{1,0:T(8,128)(2,1)S(1)}, u32[]{:S(2)}, u32[]{:S(2)}) collective-permute-start(bf16[8,4096]{1,0:T(8,128)(2,1)S(1)} %get-tuple-element.54), channel_id=1, source_target_pairs={{0,6},{1,7},{2,4},{3,5},{4,2},{5,3},{6,0},{7,1},{8,14},{9,15},{10,... | collective-permute-start | bytes 196616 | tf_op jit(solution)/shard_map/ppermute | solution.py:321
  72.8 7.8 %copy-start.5 = (s32[128]{0:T(128)S(1)}, s32[128]{0:T(128)}, u32[]{:S(2)}) copy-start(s32[128]{0:T(128)} %param.11) | copy-start | bytes 1540
  72.8 13.2 %copy-start.4 = (bf16[128,128]{1,0:T(8,128)(2,1)S(1)}, bf16[128,128]{1,0:T(8,128)(2,1)}, u32[]{:S(2)}) copy-start(bf16[128,128]{1,0:T(8,128)(2,1)} %get-tuple-element.73.refs_16_) | copy-start | bytes 98308
  72.8 7.3 %collective-permute-start.14 = (bf16[8,4096]{1,0:T(8,128)(2,1)S(1)}, bf16[8,4096]{1,0:T(8,128)(2,1)S(1)}, u32[]{:S(2)}, u32[]{:S(2)}) collective-permute-start(bf16[8,4096]{1,0:T(8,128)(2,1)S(1)} %get-tuple-element.55), channel_id=1, source_target_pairs={{0,11},{1,10},{2,9},{3,8},{4,15},{5,14},{6,13},{7,12},{8,3},{9,2},... | collective-permute-start | bytes 196616 | tf_op jit(solution)/shard_map/ppermute | solution.py:321
  73.5 8.7 %collective-permute-start.15 = (bf16[8,4096]{1,0:T(8,128)(2,1)S(1)}, bf16[8,4096]{1,0:T(8,128)(2,1)S(1)}, u32[]{:S(2)}, u32[]{:S(2)}) collective-permute-start(bf16[8,4096]{1,0:T(8,128)(2,1)S(1)} %get-tuple-element.56), channel_id=1, source_target_pairs={{0,7},{1,6},{2,5},{3,4},{4,3},{5,2},{6,1},{7,0},{8,15},{9,14},{10,... | collective-permute-start | bytes 196616 | tf_op jit(solution)/shard_map/ppermute | solution.py:321
  75.8 6.5 %collective-permute-start.4 = (bf16[8,4096]{1,0:T(8,128)(2,1)S(1)}, bf16[8,4096]{1,0:T(8,128)(2,1)S(1)}, u32[]{:S(2)}, u32[]{:S(2)}) collective-permute-start(bf16[8,4096]{1,0:T(8,128)(2,1)S(1)} %get-tuple-element.45), channel_id=1, source_target_pairs={{0,8},{1,9},{2,10},{3,11},{4,12},{5,13},{6,14},{7,15},{8,0},{9,1},... | collective-permute-start | bytes 196616 | tf_op jit(solution)/shard_map/ppermute | solution.py:321
  77.7 7.2 %collective-permute-start.5 = (bf16[8,4096]{1,0:T(8,128)(2,1)S(1)}, bf16[8,4096]{1,0:T(8,128)(2,1)S(1)}, u32[]{:S(2)}, u32[]{:S(2)}) collective-permute-start(bf16[8,4096]{1,0:T(8,128)(2,1)S(1)} %get-tuple-element.46), channel_id=1, source_target_pairs={{0,4},{1,5},{2,6},{3,7},{4,0},{5,1},{6,2},{7,3},{8,12},{9,13},{10,... | collective-permute-start | bytes 196616 | tf_op jit(solution)/shard_map/ppermute | solution.py:321
  79.1 6.4 %collective-permute-start.6 = (bf16[8,4096]{1,0:T(8,128)(2,1)S(1)}, bf16[8,4096]{1,0:T(8,128)(2,1)S(1)}, u32[]{:S(2)}, u32[]{:S(2)}) collective-permute-start(bf16[8,4096]{1,0:T(8,128)(2,1)S(1)} %get-tuple-element.47), channel_id=1, source_target_pairs={{0,9},{1,8},{2,11},{3,10},{4,13},{5,12},{6,15},{7,14},{8,1},{9,0},... | collective-permute-start | bytes 196616 | tf_op jit(solution)/shard_map/ppermute | solution.py:321
  80.1 5.9 %collective-permute-start.7 = (bf16[8,4096]{1,0:T(8,128)(2,1)S(1)}, bf16[8,4096]{1,0:T(8,128)(2,1)S(1)}, u32[]{:S(2)}, u32[]{:S(2)}) collective-permute-start(bf16[8,4096]{1,0:T(8,128)(2,1)S(1)} %get-tuple-element.48), channel_id=1, source_target_pairs={{0,5},{1,4},{2,7},{3,6},{4,1},{5,0},{6,3},{7,2},{8,13},{9,12},{10,... | collective-permute-start | bytes 196616 | tf_op jit(solution)/shard_map/ppermute | solution.py:321

commit v20 on v19

--- a/solution.py
+++ b/solution.py
@@ -15,6 +15,7 @@
 ROWS_STEP = 8
 PREP_STEPS = 2
 GROUPS = 4
+HELD = 4
 MOST_PERMUTES = 32
 COLUMNS_STEP = 1024
 ADAPT_STEP = 2048
@@ -134,25 +135,25 @@
             ].astype(change_ref.dtype)
 
 
-def adapt(arrived, a_maps, b_maps, after):
+def adapt(arrived, a_maps, b_maps):
     count = len(arrived)
     change = jax.ShapeDtypeStruct((arrived[0].shape[0], b_maps.shape[1]), jnp.bfloat16)
     return pl.pallas_call(
         functools.partial(adapt_kernel, count),
-        in_specs=[pl.BlockSpec(memory_space=pltpu.VMEM)] * (count + 2)
-        + [pl.BlockSpec(memory_space=pl.ANY)],
+        in_specs=[pl.BlockSpec(memory_space=pltpu.VMEM)] * (count + 2),
         out_specs=[pl.BlockSpec(memory_space=pltpu.VMEM)] * count,
         out_shape=[change] * count,
         compiler_params=pltpu.CompilerParams(vmem_limit_bytes=GRANT),
         name="adapt",
-    )(*arrived, a_maps, b_maps, after)
+    )(*arrived, a_maps, b_maps)
 
 
 def tall(rows, group):
     return jnp.concatenate([rows[:, g * HEAD : (g + 1) * HEAD] for g in range(group)], axis=0)
 
 
-def prep_kernel(group, base_ref, kv_ref, keys_ref, rest_ref):
+def prep_kernel(group, base_ref, kv_ref, given_ref, keys_ref, rest_ref, lens_ref):
+    lens_ref[...] = given_ref[...]
     step, context = ROWS_STEP, kv_ref.shape[2]
     cells = step * context
     for j in range(PREP_STEPS):
@@ -166,7 +167,7 @@
             rest_ref[k, j, cells:] = tall(base[rows], group).astype(rest_ref.dtype)
 
 
-def prep(base_q, kv_cache):
+def prep(base_q, kv_cache, cache_len):
     rows, width = base_q.shape
     context = kv_cache.shape[2]
     group = width // (KVH * HEAD)
@@ -174,6 +175,7 @@
     steps = rows // step
     cells = ROWS_STEP * context
     lines = cells + group * ROWS_STEP
+    lens = jnp.repeat(cache_len, context).reshape(rows // ROWS_STEP, 1, cells)
     length = max(pl.cdiv(TALL_BYTES, 2 * KVH * lines * HEAD * PREP_STEPS), steps) * PREP_STEPS
     return pl.pallas_call(
         functools.partial(prep_kernel, group),
@@ -181,18 +183,37 @@
         in_specs=[
             pl.BlockSpec((step, width), lambda i: (i, 0)),
             pl.BlockSpec((step, *kv_cache.shape[1:]), lambda i: (i, 0, 0, 0)),
+            pl.BlockSpec((PREP_STEPS, 1, cells), lambda i: (i, 0, 0)),
         ],
         out_specs=[
             pl.BlockSpec((KVH, HEAD, PREP_STEPS * cells), lambda i: (0, 0, i)),
             pl.BlockSpec((KVH, PREP_STEPS, lines, HEAD), lambda i: (0, i, 0, 0)),
+            pl.BlockSpec((PREP_STEPS, 1, cells), lambda i: (i, 0, 0)),
         ],
         out_shape=[
             jax.ShapeDtypeStruct((KVH, HEAD, rows * context), jnp.bfloat16),
             jax.ShapeDtypeStruct((KVH, length, lines, HEAD), jnp.bfloat16),
+            jax.ShapeDtypeStruct(lens.shape, lens.dtype),
         ],
         compiler_params=pltpu.CompilerParams(vmem_limit_bytes=GRANT),
         name="prep",
-    )(base_q, kv_cache)
+    )(base_q, kv_cache, lens)
+
+
+def hold_kernel(*refs):
+    del refs
+
+
+def hold(message, after):
+    return pl.pallas_call(
+        hold_kernel,
+        in_specs=[pl.BlockSpec(memory_space=pl.ANY)] * 2,
+        out_specs=pl.BlockSpec(memory_space=pl.ANY),
+        out_shape=jax.ShapeDtypeStruct(message.shape, message.dtype),
+        input_output_aliases={0: 0},
+        compiler_params=pltpu.CompilerParams(vmem_limit_bytes=GRANT),
+        name="hold",
+    )(message, after)
 
 
 def attend_kernel(group, context, order, *refs):
@@ -269,13 +290,12 @@
         store.wait()
 
 
-def attend(routed, returned, order, cache_len, keys, rest, context):
+def attend(routed, returned, order, keys, rest, lens, context):
     rows, width = routed.shape[0], returned[0].shape[1]
     group = width // (KVH * HEAD)
     step = ROWS_STEP
     steps = rows // step
     cells = step * context
-    lens = jnp.repeat(cache_len, context).reshape(steps, 1, cells)
     return pl.pallas_call(
         functools.partial(attend_kernel, group, context, order),
         in_specs=[pl.BlockSpec(memory_space=pltpu.VMEM)] * (3 + len(order)) + [pl.BlockSpec(memory_space=pl.ANY)],
@@ -305,14 +325,15 @@
     near = [*range(half // 2, half), *range(1, half // 2)]
     order = [s for pair in zip(range(half, owners), [*near, 0]) for s in pair]
 
-    keys, rest = prep(base_q, kv_cache)
+    keys, rest, lens = prep(base_q, kv_cache, cache_len)
+    messages[order[HELD]] = hold(messages[order[HELD]], rest)
     size = owners // GROUPS
     arrived = exchange(order, owners)(messages[s] for s in order)
     changes = []
     for at in range(0, owners, size):
-        changes += adapt(arrived[at : at + size], a_maps, b_maps, rest)
+        changes += adapt(arrived[at : at + size], a_maps, b_maps)
     returned = exchange(order, owners)(changes)
-    return attend(routed, returned, order, cache_len, keys, rest, kv_cache.shape[2])
+    return attend(routed, returned, order, keys, rest, lens, kv_cache.shape[2])
 
 
 def exchange(order, owners):

time: 90.7 us -> 88.9 us (0.980)
  starting transfers between devices: 55.3 us -> 53.3 us
    ppermute x30, starting transfers between devices: 55.3 us -> 53.3 us  [permutes(): lax.ppermute(message, 'owner', [(i, i ^ s) for i in range(owners)])]
    broadcast_in_dim x3, local copies, waits for them, and re-layouts: 1.73 us -> 0.26 us  [prep(): lens = jnp.repeat(cache_len, context).reshape(rows // ROWS_STEP, 1, cells)]
  transfers between devices with their start and end apart: 30 -> 30, of which waited for: 7 -> 8; matrix products, arithmetic and copies ran while one was open for 2% -> 0% of each run, Pallas kernels for 11% -> 11%
where the time goes in v20:
time: 88.9 us; the launch traced here: 88.6 us
  starting transfers between devices  53.3 us (60%)
  Pallas kernels  19.3 us (22%)
  waiting for transfers between devices  14.7 us (17%)
  local copies, waits for them, and re-layouts  1.09 us (1%)
    ppermute x30, starting transfers between devices, permutes(): lax.ppermute(message, 'owner', [(i, i ^ s) for i in range(owners)])  53.3 us
    ppermute x30, waiting for transfers between devices, permutes(): lax.ppermute(message, 'owner', [(i, i ^ s) for i in range(owners)])  14.7 us
    pallas_call x1, Pallas kernels, prep(): pl.pallas_call(functools.partial(prep_kernel, group), grid=(steps,), in_s...  7.21 us
    pallas_call x1, Pallas kernels, pack(): pl.pallas_call(functools.partial(pack_kernel, owners, slot_count, held),...  4.92 us
    pallas_call x1, Pallas kernels, attend(): pl.pallas_call(functools.partial(attend_kernel, group, context, order), i...  4.42 us
    pallas_call x4, Pallas kernels, adapt(): pl.pallas_call(functools.partial(adapt_kernel, count), in_specs=[pl.Block...  2.7 us
  transfers between devices with their start and end apart: 30, of which 8 were waited for; matrix products, arithmetic and copies ran while one was open for 0% of the time, Pallas kernels for 11%

profile of v20, /device:TPU:0, one launch (start us, length us, event | category | flops | bytes accessed | tf_op | source)
XLA Modules:
  0.0 88.6 jit_solution(7364052491540480362)
XLA Ops:
  0.0 4.9 %pack.1 = (bf16[128,128]{1,0:T(8,128)(2,1)}, bf16[8,8320]{1,0:T(8,128)(2,1)}, bf16[8,8320]{1,0:T(8,128)(2,1)}, bf16[8,8320]{1,0:T(8,128)(2,1)}, bf16[8,8320]{1,0...) custom-call(s32[1,32]{1,0:T(1,128)} %bitcast.2, ...), custom_call_target="tpu_custom_call" | custom-call | tf_op jit(solution)/shard_map/pack/pallas_call | solution.py:92
  4.9 4.1 %collective-permute-start = (bf16[8,8320]{1,0:T(8,128)(2,1)}, bf16[8,8320]{1,0:T(8,128)(2,1)S(1)}, u32[]{:S(2)}, u32[]{:S(2)}) collective-permute-start(bf16[8,8320]{1,0:T(8,128)(2,1)} %get-tuple-element.41), channel_id=1, source_target_pairs={{0,8},{1,9},{2,10},{3,11},{4,12},{5,13},{6,14},{7,15},{8,0},{9,1},... | collective-permute-start | bytes 399368 | tf_op jit(solution)/shard_map/ppermute | solution.py:342
  9.0 1.6 %collective-permute-start.1 = (bf16[8,8320]{1,0:T(8,128)(2,1)}, bf16[8,8320]{1,0:T(8,128)(2,1)S(1)}, u32[]{:S(2)}, u32[]{:S(2)}) collective-permute-start(bf16[8,8320]{1,0:T(8,128)(2,1)} %get-tuple-element.42), channel_id=1, source_target_pairs={{0,4},{1,5},{2,6},{3,7},{4,0},{5,1},{6,2},{7,3},{8,12},{9,13},{10,... | collective-permute-start | bytes 399368 | tf_op jit(solution)/shard_map/ppermute | solution.py:342
  10.6 0.2 collective-permute-start.3
  10.9 2.8 %collective-permute-start.9 = (bf16[8,8320]{1,0:T(8,128)(2,1)}, bf16[8,8320]{1,0:T(8,128)(2,1)S(1)}, u32[]{:S(2)}, u32[]{:S(2)}) collective-permute-start(bf16[8,8320]{1,0:T(8,128)(2,1)} %get-tuple-element.51), channel_id=1, source_target_pairs={{0,6},{1,7},{2,4},{3,5},{4,2},{5,3},{6,0},{7,1},{8,14},{9,15},{10,... | collective-permute-start | bytes 399368 | tf_op jit(solution)/shard_map/ppermute | solution.py:342
  13.6 3.5 %collective-permute-done.refs_0_ = bf16[8,8320]{1,0:T(8,128)(2,1)S(1)} collective-permute-done((bf16[8,8320]{1,0:T(8,128)(2,1)}, bf16[8,8320]{1,0:T(8,128)(2,1)S(1)}, u32[]{:S(2)}, u32[]{:S(2)}) %collective-permute-start) | collective-permute-done | bytes 133152 | tf_op jit(solution)/shard_map/ppermute | solution.py:342
  17.1 0.0 collective-permute-start.10
  17.1 1.0 %collective-permute-done.1.refs_1_ = bf16[8,8320]{1,0:T(8,128)(2,1)S(1)} collective-permute-done((bf16[8,8320]{1,0:T(8,128)(2,1)}, bf16[8,8320]{1,0:T(8,128)(2,1)S(1)}, u32[]{:S(2)}, u32[]{:S(2)}) %collective-permute-start.1) | collective-permute-done | bytes 133152 | tf_op jit(solution)/shard_map/ppermute | solution.py:342
  18.0 2.4 %collective-permute-start.16 = (bf16[8,8320]{1,0:T(8,128)(2,1)}, bf16[8,8320]{1,0:T(8,128)(2,1)S(1)}, u32[]{:S(2)}, u32[]{:S(2)}) collective-permute-start(bf16[8,8320]{1,0:T(8,128)(2,1)} %get-tuple-element.58), channel_id=1, source_target_pairs={{0,12},{1,13},{2,14},{3,15},{4,8},{5,9},{6,10},{7,11},{8,4},{9,5},... | collective-permute-start | bytes 399368 | tf_op jit(solution)/shard_map/ppermute | solution.py:342
  20.4 0.1 collective-permute-done.2.refs_2_
  20.5 0.7 collective-permute-start.17
  21.3 0.6 collective-permute-done.3.refs_3_
  21.9 3.1 %collective-permute-start.18 = (bf16[8,8320]{1,0:T(8,128)(2,1)}, bf16[8,8320]{1,0:T(8,128)(2,1)S(1)}, u32[]{:S(2)}, u32[]{:S(2)}) collective-permute-start(bf16[8,8320]{1,0:T(8,128)(2,1)} %get-tuple-element.60), channel_id=1, source_target_pairs={{0,13},{1,12},{2,15},{3,14},{4,9},{5,8},{6,11},{7,10},{8,5},{9,4},... | collective-permute-start | bytes 399368 | tf_op jit(solution)/shard_map/ppermute | solution.py:342
  25.0 3.6 %collective-permute-done.9.refs_1_ = bf16[8,8320]{1,0:T(8,128)(2,1)S(1)} collective-permute-done((bf16[8,8320]{1,0:T(8,128)(2,1)}, bf16[8,8320]{1,0:T(8,128)(2,1)S(1)}, u32[]{:S(2)}, u32[]{:S(2)}) %collective-permute-start.9) | collective-permute-done | bytes 133152 | tf_op jit(solution)/shard_map/ppermute | solution.py:342
  28.6 0.4 collective-permute-start.19
  29.0 0.1 broadcast_in_dim.7
  29.1 0.1 broadcast_in_dim.8
  29.2 0.1 broadcast_in_dim.9.given_ref
  29.3 7.2 %prep.1 = (bf16[4,128,2048]{2,1,0:T(8,128)(2,1)S(1)}, bf16[4,92,192,128]{3,2,1,0:T(8,128)(2,1)}, s32[16,1,128]{2,1,0:T(1,128)S(1)}) custom-call(bf16[128,4096]{1,0:T(8,128)(2,1)S(1)} %copy-done.2, bf16[128,2,16,512]{3,2,1,0:T(8,128)(2,1)} %kv_ref.1, s32[16,1,128]{2,1,0:T(1,128)S(1)} %broadcast_in_dim.9.given_ref), custom_call_target="tpu_custom_call" | custom-call | tf_op jit(solution)/shard_map/prep/pallas_call | solution.py:180
  36.5 0.0 collective-permute-start.11
  36.6 3.7 %collective-permute-start.24 = (bf16[8,8320]{1,0:T(8,128)(2,1)S(1)}, bf16[8,8320]{1,0:T(8,128)(2,1)S(1)}, u32[]{:S(2)}, u32[]{:S(2)}) collective-permute-start(bf16[8,8320]{1,0:T(8,128)(2,1)S(1)} %copy-done.9), channel_id=1, source_target_pairs={{0,14},{1,15},{2,12},{3,13},{4,10},{5,11},{6,8},{7,9},{8,6},{9,7},... | collective-permute-start | bytes 399368 | tf_op jit(solution)/shard_map/ppermute | solution.py:342
  40.3 2.3 %collective-permute-start.26 = (bf16[8,8320]{1,0:T(8,128)(2,1)S(1)}, bf16[8,8320]{1,0:T(8,128)(2,1)S(1)}, u32[]{:S(2)}, u32[]{:S(2)}) collective-permute-start(bf16[8,8320]{1,0:T(8,128)(2,1)S(1)} %copy-done.7), channel_id=1, source_target_pairs={{0,15},{1,14},{2,13},{3,12},{4,11},{5,10},{6,9},{7,8},{8,7},{9,6},... | collective-permute-start | bytes 399368 | tf_op jit(solution)/shard_map/ppermute | solution.py:342
  42.7 1.1 %collective-permute-start.8 = (bf16[8,8320]{1,0:T(8,128)(2,1)S(1)}, bf16[8,8320]{1,0:T(8,128)(2,1)S(1)}, u32[]{:S(2)}, u32[]{:S(2)}) collective-permute-start(bf16[8,8320]{1,0:T(8,128)(2,1)S(1)} %hold.1), channel_id=1, source_target_pairs={{0,10},{1,11},{2,8},{3,9},{4,14},{5,15},{6,12},{7,13},{8,2},{9,3},... | collective-permute-start | bytes 399368 | tf_op jit(solution)/shard_map/ppermute | solution.py:342
  43.8 0.5 copy-done
  44.3 0.3 copy-done.1
  44.6 0.7 adapt.4
  45.2 0.0 copy-start.3
  45.2 0.7 adapt.6
  45.9 1.1 %collective-permute-start.4 = (bf16[8,4096]{1,0:T(8,128)(2,1)S(1)}, bf16[8,4096]{1,0:T(8,128)(2,1)S(1)}, u32[]{:S(2)}, u32[]{:S(2)}) collective-permute-start(bf16[8,4096]{1,0:T(8,128)(2,1)S(1)} %get-tuple-element.45), channel_id=1, source_target_pairs={{0,8},{1,9},{2,10},{3,11},{4,12},{5,13},{6,14},{7,15},{8,0},{9,1},... | collective-permute-start | bytes 196616 | tf_op jit(solution)/shard_map/ppermute | solution.py:342
  47.0 6.8 %collective-permute-start.5 = (bf16[8,4096]{1,0:T(8,128)(2,1)S(1)}, bf16[8,4096]{1,0:T(8,128)(2,1)S(1)}, u32[]{:S(2)}, u32[]{:S(2)}) collective-permute-start(bf16[8,4096]{1,0:T(8,128)(2,1)S(1)} %get-tuple-element.46), channel_id=1, source_target_pairs={{0,4},{1,5},{2,6},{3,7},{4,0},{5,1},{6,2},{7,3},{8,12},{9,13},{10,... | collective-permute-start | bytes 196616 | tf_op jit(solution)/shard_map/ppermute | solution.py:342
  53.8 2.1 %collective-permute-start.6 = (bf16[8,4096]{1,0:T(8,128)(2,1)S(1)}, bf16[8,4096]{1,0:T(8,128)(2,1)S(1)}, u32[]{:S(2)}, u32[]{:S(2)}) collective-permute-start(bf16[8,4096]{1,0:T(8,128)(2,1)S(1)} %get-tuple-element.47), channel_id=1, source_target_pairs={{0,9},{1,8},{2,11},{3,10},{4,13},{5,12},{6,15},{7,14},{8,1},{9,0},... | collective-permute-start | bytes 196616 | tf_op jit(solution)/shard_map/ppermute | solution.py:342
  55.9 1.9 %collective-permute-start.7 = (bf16[8,4096]{1,0:T(8,128)(2,1)S(1)}, bf16[8,4096]{1,0:T(8,128)(2,1)S(1)}, u32[]{:S(2)}, u32[]{:S(2)}) collective-permute-start(bf16[8,4096]{1,0:T(8,128)(2,1)S(1)} %get-tuple-element.48), channel_id=1, source_target_pairs={{0,5},{1,4},{2,7},{3,6},{4,1},{5,0},{6,3},{7,2},{8,13},{9,12},{10,... | collective-permute-start | bytes 196616 | tf_op jit(solution)/shard_map/ppermute | solution.py:342
  57.8 2.0 %collective-permute-done.8.refs_0_ = bf16[8,8320]{1,0:T(8,128)(2,1)S(1)} collective-permute-done((bf16[8,8320]{1,0:T(8,128)(2,1)S(1)}, bf16[8,8320]{1,0:T(8,128)(2,1)S(1)}, u32[]{:S(2)}, u32[]{:S(2)}) %collective-permute-start.8) | collective-permute-done | bytes 133152 | tf_op jit(solution)/shard_map/ppermute | solution.py:342
  59.9 4.4 %collective-permute-start.20 = (bf16[8,4096]{1,0:T(8,128)(2,1)S(1)}, bf16[8,4096]{1,0:T(8,128)(2,1)S(1)}, u32[]{:S(2)}, u32[]{:S(2)}) collective-permute-start(bf16[8,4096]{1,0:T(8,128)(2,1)S(1)} %get-tuple-element.62), channel_id=1, source_target_pairs={{0,12},{1,13},{2,14},{3,15},{4,8},{5,9},{6,10},{7,11},{8,4},{9,5},... | collective-permute-start | bytes 196616 | tf_op jit(solution)/shard_map/ppermute | solution.py:342
  64.2 0.7 adapt.7
  64.9 0.1 collective-permute-start.21
  65.0 1.5 %collective-permute-start.22 = (bf16[8,4096]{1,0:T(8,128)(2,1)S(1)}, bf16[8,4096]{1,0:T(8,128)(2,1)S(1)}, u32[]{:S(2)}, u32[]{:S(2)}) collective-permute-start(bf16[8,4096]{1,0:T(8,128)(2,1)S(1)} %get-tuple-element.64), channel_id=1, source_target_pairs={{0,13},{1,12},{2,15},{3,14},{4,9},{5,8},{6,11},{7,10},{8,5},{9,4},... | collective-permute-start | bytes 196616 | tf_op jit(solution)/shard_map/ppermute | solution.py:342
  66.5 0.5 collective-permute-start.23
  67.0 3.4 %collective-permute-start.27 = (bf16[8,4096]{1,0:T(8,128)(2,1)S(1)}, bf16[8,4096]{1,0:T(8,128)(2,1)S(1)}, u32[]{:S(2)}, u32[]{:S(2)}) collective-permute-start(bf16[8,4096]{1,0:T(8,128)(2,1)S(1)} %get-tuple-element.70), channel_id=1, source_target_pairs={{0,14},{1,15},{2,12},{3,13},{4,10},{5,11},{6,8},{7,9},{8,6},{9,7},... | collective-permute-start | bytes 196616 | tf_op jit(solution)/shard_map/ppermute | solution.py:342
  70.4 0.2 collective-permute-start.28
  70.7 0.7 adapt.5
  71.3 2.4 %collective-permute-start.29 = (bf16[8,4096]{1,0:T(8,128)(2,1)S(1)}, bf16[8,4096]{1,0:T(8,128)(2,1)S(1)}, u32[]{:S(2)}, u32[]{:S(2)}) collective-permute-start(bf16[8,4096]{1,0:T(8,128)(2,1)S(1)} %get-tuple-element.72), channel_id=1, source_target_pairs={{0,15},{1,14},{2,13},{3,12},{4,11},{5,10},{6,9},{7,8},{8,7},{9,6},... | collective-permute-start | bytes 196616 | tf_op jit(solution)/shard_map/ppermute | solution.py:342
  73.7 3.9 %collective-permute-start.13 = (bf16[8,4096]{1,0:T(8,128)(2,1)S(1)}, bf16[8,4096]{1,0:T(8,128)(2,1)S(1)}, u32[]{:S(2)}, u32[]{:S(2)}) collective-permute-start(bf16[8,4096]{1,0:T(8,128)(2,1)S(1)} %get-tuple-element.55), channel_id=1, source_target_pairs={{0,6},{1,7},{2,4},{3,5},{4,2},{5,3},{6,0},{7,1},{8,14},{9,15},{10,... | collective-permute-start | bytes 196616 | tf_op jit(solution)/shard_map/ppermute | solution.py:342
  77.7 2.5 %collective-permute-start.15 = (bf16[8,4096]{1,0:T(8,128)(2,1)S(1)}, bf16[8,4096]{1,0:T(8,128)(2,1)S(1)}, u32[]{:S(2)}, u32[]{:S(2)}) collective-permute-start(bf16[8,4096]{1,0:T(8,128)(2,1)S(1)} %get-tuple-element.57), channel_id=1, source_target_pairs={{0,7},{1,6},{2,5},{3,4},{4,3},{5,2},{6,1},{7,0},{8,15},{9,14},{10,... | collective-permute-start | bytes 196616 | tf_op jit(solution)/shard_map/ppermute | solution.py:342
  80.2 1.1 %collective-permute-done.12.refs_4_ = bf16[8,4096]{1,0:T(8,128)(2,1)S(1)} collective-permute-done((bf16[8,4096]{1,0:T(8,128)(2,1)S(1)}, bf16[8,4096]{1,0:T(8,128)(2,1)S(1)}, u32[]{:S(2)}, u32[]{:S(2)}) %collective-permute-start.12) | collective-permute-done | bytes 65568 | tf_op jit(solution)/shard_map/ppermute | solution.py:342
  81.3 2.8 %collective-permute-done.14.refs_6_ = bf16[8,4096]{1,0:T(8,128)(2,1)S(1)} collective-permute-done((bf16[8,4096]{1,0:T(8,128)(2,1)S(1)}, bf16[8,4096]{1,0:T(8,128)(2,1)S(1)}, u32[]{:S(2)}, u32[]{:S(2)}) %collective-permute-start.14) | collective-permute-done | bytes 65568 | tf_op jit(solution)/shard_map/ppermute | solution.py:342
  84.1 0.0 collective-permute-done.15.refs_7_
  84.2 4.4 %attend.1 = bf16[128,4096]{1,0:T(8,128)(2,1)} custom-call(bf16[8,4096]{1,0:T(8,128)(2,1)S(1)} %collective-permute-done.4.refs_0_, bf16[8,4096]{1,0:T(8,128)(2,1)S(1)} %collective-permute-done.5.refs_1_, bf16[8,4096]{1,0:T(8,128)(2,1)S(1)} %collective-permute-done.6.refs_2_, bf16[8,4096]{1,0:T(8,128)(2,1)S(1)} %collective-permute-done.7.refs_3_, ...), custom_call_target="tpu_custom_call" | custom-call | tf_op jit(solution)/shard_map/attend/pallas_call | solution.py:299
  (45 shorter events, 0.1 us)
Async XLA Ops:
  0.0 29.0 %copy-start.6 = (s32[128]{0:T(128)S(1)}, s32[128]{0:T(128)}, u32[]{:S(2)}) copy-start(s32[128]{0:T(128)} %param.11) | copy-start | bytes 1540
  0.0 29.3 %copy-start.2 = (bf16[128,4096]{1,0:T(8,128)(2,1)S(1)}, bf16[128,4096]{1,0:T(8,128)(2,1)}, u32[]{:S(2)}) copy-start(bf16[128,4096]{1,0:T(8,128)(2,1)} %base_ref.1) | copy-start | bytes 3145732
  4.9 12.1 %collective-permute-start = (bf16[8,8320]{1,0:T(8,128)(2,1)}, bf16[8,8320]{1,0:T(8,128)(2,1)S(1)}, u32[]{:S(2)}, u32[]{:S(2)}) collective-permute-start(bf16[8,8320]{1,0:T(8,128)(2,1)} %get-tuple-element.41), channel_id=1, source_target_pairs={{0,8},{1,9},{2,10},{3,11},{4,12},{5,13},{6,14},{7,15},{8,0},{9,1},... | collective-permute-start | bytes 399368 | tf_op jit(solution)/shard_map/ppermute | solution.py:342
  9.0 9.0 %collective-permute-start.1 = (bf16[8,8320]{1,0:T(8,128)(2,1)}, bf16[8,8320]{1,0:T(8,128)(2,1)S(1)}, u32[]{:S(2)}, u32[]{:S(2)}) collective-permute-start(bf16[8,8320]{1,0:T(8,128)(2,1)} %get-tuple-element.42), channel_id=1, source_target_pairs={{0,4},{1,5},{2,6},{3,7},{4,0},{5,1},{6,2},{7,3},{8,12},{9,13},{10,... | collective-permute-start | bytes 399368 | tf_op jit(solution)/shard_map/ppermute | solution.py:342
  10.6 9.9 %collective-permute-start.2 = (bf16[8,8320]{1,0:T(8,128)(2,1)}, bf16[8,8320]{1,0:T(8,128)(2,1)S(1)}, u32[]{:S(2)}, u32[]{:S(2)}) collective-permute-start(bf16[8,8320]{1,0:T(8,128)(2,1)} %get-tuple-element.43), channel_id=1, source_target_pairs={{0,9},{1,8},{2,11},{3,10},{4,13},{5,12},{6,15},{7,14},{8,1},{9,0},... | collective-permute-start | bytes 399368 | tf_op jit(solution)/shard_map/ppermute | solution.py:342
  10.6 11.3 %collective-permute-start.3 = (bf16[8,8320]{1,0:T(8,128)(2,1)}, bf16[8,8320]{1,0:T(8,128)(2,1)S(1)}, u32[]{:S(2)}, u32[]{:S(2)}) collective-permute-start(bf16[8,8320]{1,0:T(8,128)(2,1)} %get-tuple-element.44), channel_id=1, source_target_pairs={{0,5},{1,4},{2,7},{3,6},{4,1},{5,0},{6,3},{7,2},{8,13},{9,12},{10,... | collective-permute-start | bytes 399368 | tf_op jit(solution)/shard_map/ppermute | solution.py:342
  10.9 17.7 %collective-permute-start.9 = (bf16[8,8320]{1,0:T(8,128)(2,1)}, bf16[8,8320]{1,0:T(8,128)(2,1)S(1)}, u32[]{:S(2)}, u32[]{:S(2)}) collective-permute-start(bf16[8,8320]{1,0:T(8,128)(2,1)} %get-tuple-element.51), channel_id=1, source_target_pairs={{0,6},{1,7},{2,4},{3,5},{4,2},{5,3},{6,0},{7,1},{8,14},{9,15},{10,... | collective-permute-start | bytes 399368 | tf_op jit(solution)/shard_map/ppermute | solution.py:342
  17.1 19.5 %collective-permute-start.10 = (bf16[8,8320]{1,0:T(8,128)(2,1)}, bf16[8,8320]{1,0:T(8,128)(2,1)S(1)}, u32[]{:S(2)}, u32[]{:S(2)}) collective-permute-start(bf16[8,8320]{1,0:T(8,128)(2,1)} %get-tuple-element.52), channel_id=1, source_target_pairs={{0,11},{1,10},{2,9},{3,8},{4,15},{5,14},{6,13},{7,12},{8,3},{9,2},... | collective-permute-start | bytes 399368 | tf_op jit(solution)/shard_map/ppermute | solution.py:342
  18.0 18.5 %collective-permute-start.16 = (bf16[8,8320]{1,0:T(8,128)(2,1)}, bf16[8,8320]{1,0:T(8,128)(2,1)S(1)}, u32[]{:S(2)}, u32[]{:S(2)}) collective-permute-start(bf16[8,8320]{1,0:T(8,128)(2,1)} %get-tuple-element.58), channel_id=1, source_target_pairs={{0,12},{1,13},{2,14},{3,15},{4,8},{5,9},{6,10},{7,11},{8,4},{9,5},... | collective-permute-start | bytes 399368 | tf_op jit(solution)/shard_map/ppermute | solution.py:342
  20.5 19.8 %collective-permute-start.17 = (bf16[8,8320]{1,0:T(8,128)(2,1)}, bf16[8,8320]{1,0:T(8,128)(2,1)S(1)}, u32[]{:S(2)}, u32[]{:S(2)}) collective-permute-start(bf16[8,8320]{1,0:T(8,128)(2,1)} %get-tuple-element.59), channel_id=1, source_target_pairs={{0,1},{1,0},{2,3},{3,2},{4,5},{5,4},{6,7},{7,6},{8,9},{9,8},{10,11... | collective-permute-start | bytes 399368 | tf_op jit(solution)/shard_map/ppermute | solution.py:342
  21.9 18.5 %collective-permute-start.18 = (bf16[8,8320]{1,0:T(8,128)(2,1)}, bf16[8,8320]{1,0:T(8,128)(2,1)S(1)}, u32[]{:S(2)}, u32[]{:S(2)}) collective-permute-start(bf16[8,8320]{1,0:T(8,128)(2,1)} %get-tuple-element.60), channel_id=1, source_target_pairs={{0,13},{1,12},{2,15},{3,14},{4,9},{5,8},{6,11},{7,10},{8,5},{9,4},... | collective-permute-start | bytes 399368 | tf_op jit(solution)/shard_map/ppermute | solution.py:342
  28.6 14.1 %collective-permute-start.19 = (bf16[8,8320]{1,0:T(8,128)(2,1)}, bf16[8,8320]{1,0:T(8,128)(2,1)S(1)}, u32[]{:S(2)}, u32[]{:S(2)}) collective-permute-start(bf16[8,8320]{1,0:T(8,128)(2,1)} %get-tuple-element.61), channel_id=1, source_target_pairs={{0,2},{1,3},{2,0},{3,1},{4,6},{5,7},{6,4},{7,5},{8,10},{9,11},{10,... | collective-permute-start | bytes 399368 | tf_op jit(solution)/shard_map/ppermute | solution.py:342
  29.3 7.3 %copy-start.10 = (bf16[8,8320]{1,0:T(8,128)(2,1)S(1)}, bf16[8,8320]{1,0:T(8,128)(2,1)}, u32[]{:S(2)}) copy-start(bf16[8,8320]{1,0:T(8,128)(2,1)} %get-tuple-element.53) | copy-start | bytes 399364
  29.3 7.3 %copy-start.9 = (bf16[8,8320]{1,0:T(8,128)(2,1)S(1)}, bf16[8,8320]{1,0:T(8,128)(2,1)}, u32[]{:S(2)}) copy-start(bf16[8,8320]{1,0:T(8,128)(2,1)} %get-tuple-element.66) | copy-start | bytes 399364
  29.3 11.0 %copy-start.8 = (bf16[8,8320]{1,0:T(8,128)(2,1)S(1)}, bf16[8,8320]{1,0:T(8,128)(2,1)}, u32[]{:S(2)}) copy-start(bf16[8,8320]{1,0:T(8,128)(2,1)} %get-tuple-element.67) | copy-start | bytes 399364
  29.3 11.0 %copy-start.7 = (bf16[8,8320]{1,0:T(8,128)(2,1)S(1)}, bf16[8,8320]{1,0:T(8,128)(2,1)}, u32[]{:S(2)}) copy-start(bf16[8,8320]{1,0:T(8,128)(2,1)} %get-tuple-element.68) | copy-start | bytes 399364
  29.3 13.4 %copy-start.4 = (bf16[8,8320]{1,0:T(8,128)(2,1)S(1)}, bf16[8,8320]{1,0:T(8,128)(2,1)}, u32[]{:S(2)}) copy-start(bf16[8,8320]{1,0:T(8,128)(2,1)} %get-tuple-element.49.refs_0_) | copy-start | bytes 399364
  36.5 9.4 %collective-permute-start.11 = (bf16[8,8320]{1,0:T(8,128)(2,1)S(1)}, bf16[8,8320]{1,0:T(8,128)(2,1)S(1)}, u32[]{:S(2)}, u32[]{:S(2)}) collective-permute-start(bf16[8,8320]{1,0:T(8,128)(2,1)S(1)} %copy-done.10), channel_id=1, source_target_pairs={{0,7},{1,6},{2,5},{3,4},{4,3},{5,2},{6,1},{7,0},{8,15},{9,14},{10,... | collective-permute-start | bytes 399368 | tf_op jit(solution)/shard_map/ppermute | solution.py:342
  36.6 10.4 %collective-permute-start.24 = (bf16[8,8320]{1,0:T(8,128)(2,1)S(1)}, bf16[8,8320]{1,0:T(8,128)(2,1)S(1)}, u32[]{:S(2)}, u32[]{:S(2)}) collective-permute-start(bf16[8,8320]{1,0:T(8,128)(2,1)S(1)} %copy-done.9), channel_id=1, source_target_pairs={{0,14},{1,15},{2,12},{3,13},{4,10},{5,11},{6,8},{7,9},{8,6},{9,7},... | collective-permute-start | bytes 399368 | tf_op jit(solution)/shard_map/ppermute | solution.py:342
  40.3 13.5 %collective-permute-start.25 = (bf16[8,8320]{1,0:T(8,128)(2,1)S(1)}, bf16[8,8320]{1,0:T(8,128)(2,1)S(1)}, u32[]{:S(2)}, u32[]{:S(2)}) collective-permute-start(bf16[8,8320]{1,0:T(8,128)(2,1)S(1)} %copy-done.8), channel_id=1, source_target_pairs={{0,3},{1,2},{2,1},{3,0},{4,7},{5,6},{6,5},{7,4},{8,11},{9,10},{10,... | collective-permute-start | bytes 399368 | tf_op jit(solution)/shard_map/ppermute | solution.py:342
  40.3 15.5 %collective-permute-start.26 = (bf16[8,8320]{1,0:T(8,128)(2,1)S(1)}, bf16[8,8320]{1,0:T(8,128)(2,1)S(1)}, u32[]{:S(2)}, u32[]{:S(2)}) collective-permute-start(bf16[8,8320]{1,0:T(8,128)(2,1)S(1)} %copy-done.7), channel_id=1, source_target_pairs={{0,15},{1,14},{2,13},{3,12},{4,11},{5,10},{6,9},{7,8},{8,7},{9,6},... | collective-permute-start | bytes 399368 | tf_op jit(solution)/shard_map/ppermute | solution.py:342
  42.7 1.6 %copy-start = (bf16[8192,128]{1,0:T(8,128)(2,1)S(1)}, bf16[8192,128]{1,0:T(8,128)(2,1)}, u32[]{:S(2)}) copy-start(bf16[8192,128]{1,0:T(8,128)(2,1)} %refs_4_.7) | copy-start | bytes 6291460
  42.7 1.9 %copy-start.1 = (bf16[128,4096]{1,0:T(8,128)(2,1)S(1)}, bf16[128,4096]{1,0:T(8,128)(2,1)}, u32[]{:S(2)}) copy-start(bf16[128,4096]{1,0:T(8,128)(2,1)} %refs_5_.7) | copy-start | bytes 3145732
  42.7 17.2 %collective-permute-start.8 = (bf16[8,8320]{1,0:T(8,128)(2,1)S(1)}, bf16[8,8320]{1,0:T(8,128)(2,1)S(1)}, u32[]{:S(2)}, u32[]{:S(2)}) collective-permute-start(bf16[8,8320]{1,0:T(8,128)(2,1)S(1)} %hold.1), channel_id=1, source_target_pairs={{0,10},{1,11},{2,8},{3,9},{4,14},{5,15},{6,12},{7,13},{8,2},{9,3},... | collective-permute-start | bytes 399368 | tf_op jit(solution)/shard_map/ppermute | solution.py:342
  45.2 19.0 %copy-start.3 = (bf16[8,8320]{1,0:T(8,128)(2,1)S(1)}, bf16[8,8320]{1,0:T(8,128)(2,1)}, u32[]{:S(2)}) copy-start(bf16[8,8320]{1,0:T(8,128)(2,1)} %get-tuple-element.69.refs_3_) | copy-start | bytes 399364
  45.9 19.0 %collective-permute-start.4 = (bf16[8,4096]{1,0:T(8,128)(2,1)S(1)}, bf16[8,4096]{1,0:T(8,128)(2,1)S(1)}, u32[]{:S(2)}, u32[]{:S(2)}) collective-permute-start(bf16[8,4096]{1,0:T(8,128)(2,1)S(1)} %get-tuple-element.45), channel_id=1, source_target_pairs={{0,8},{1,9},{2,10},{3,11},{4,12},{5,13},{6,14},{7,15},{8,0},{9,1},... | collective-permute-start | bytes 196616 | tf_op jit(solution)/shard_map/ppermute | solution.py:342
  47.0 18.0 %collective-permute-start.5 = (bf16[8,4096]{1,0:T(8,128)(2,1)S(1)}, bf16[8,4096]{1,0:T(8,128)(2,1)S(1)}, u32[]{:S(2)}, u32[]{:S(2)}) collective-permute-start(bf16[8,4096]{1,0:T(8,128)(2,1)S(1)} %get-tuple-element.46), channel_id=1, source_target_pairs={{0,4},{1,5},{2,6},{3,7},{4,0},{5,1},{6,2},{7,3},{8,12},{9,13},{10,... | collective-permute-start | bytes 196616 | tf_op jit(solution)/shard_map/ppermute | solution.py:342
  53.8 12.7 %collective-permute-start.6 = (bf16[8,4096]{1,0:T(8,128)(2,1)S(1)}, bf16[8,4096]{1,0:T(8,128)(2,1)S(1)}, u32[]{:S(2)}, u32[]{:S(2)}) collective-permute-start(bf16[8,4096]{1,0:T(8,128)(2,1)S(1)} %get-tuple-element.47), channel_id=1, source_target_pairs={{0,9},{1,8},{2,11},{3,10},{4,13},{5,12},{6,15},{7,14},{8,1},{9,0},... | collective-permute-start | bytes 196616 | tf_op jit(solution)/shard_map/ppermute | solution.py:342
  55.9 11.1 %collective-permute-start.7 = (bf16[8,4096]{1,0:T(8,128)(2,1)S(1)}, bf16[8,4096]{1,0:T(8,128)(2,1)S(1)}, u32[]{:S(2)}, u32[]{:S(2)}) collective-permute-start(bf16[8,4096]{1,0:T(8,128)(2,1)S(1)} %get-tuple-element.48), channel_id=1, source_target_pairs={{0,5},{1,4},{2,7},{3,6},{4,1},{5,0},{6,3},{7,2},{8,13},{9,12},{10,... | collective-permute-start | bytes 196616 | tf_op jit(solution)/shard_map/ppermute | solution.py:342
  59.9 10.5 %collective-permute-start.20 = (bf16[8,4096]{1,0:T(8,128)(2,1)S(1)}, bf16[8,4096]{1,0:T(8,128)(2,1)S(1)}, u32[]{:S(2)}, u32[]{:S(2)}) collective-permute-start(bf16[8,4096]{1,0:T(8,128)(2,1)S(1)} %get-tuple-element.62), channel_id=1, source_target_pairs={{0,12},{1,13},{2,14},{3,15},{4,8},{5,9},{6,10},{7,11},{8,4},{9,5},... | collective-permute-start | bytes 196616 | tf_op jit(solution)/shard_map/ppermute | solution.py:342
  64.9 19.3 %copy-start.5 = (bf16[128,128]{1,0:T(8,128)(2,1)S(1)}, bf16[128,128]{1,0:T(8,128)(2,1)}, u32[]{:S(2)}) copy-start(bf16[128,128]{1,0:T(8,128)(2,1)} %get-tuple-element.74.refs_16_) | copy-start | bytes 98308
  64.9 6.4 %collective-permute-start.21 = (bf16[8,4096]{1,0:T(8,128)(2,1)S(1)}, bf16[8,4096]{1,0:T(8,128)(2,1)S(1)}, u32[]{:S(2)}, u32[]{:S(2)}) collective-permute-start(bf16[8,4096]{1,0:T(8,128)(2,1)S(1)} %get-tuple-element.63), channel_id=1, source_target_pairs={{0,1},{1,0},{2,3},{3,2},{4,5},{5,4},{6,7},{7,6},{8,9},{9,8},{10,11... | collective-permute-start | bytes 196616 | tf_op jit(solution)/shard_map/ppermute | solution.py:342
  65.0 8.7 %collective-permute-start.22 = (bf16[8,4096]{1,0:T(8,128)(2,1)S(1)}, bf16[8,4096]{1,0:T(8,128)(2,1)S(1)}, u32[]{:S(2)}, u32[]{:S(2)}) collective-permute-start(bf16[8,4096]{1,0:T(8,128)(2,1)S(1)} %get-tuple-element.64), channel_id=1, source_target_pairs={{0,13},{1,12},{2,15},{3,14},{4,9},{5,8},{6,11},{7,10},{8,5},{9,4},... | collective-permute-start | bytes 196616 | tf_op jit(solution)/shard_map/ppermute | solution.py:342
  66.5 7.2 %collective-permute-start.23 = (bf16[8,4096]{1,0:T(8,128)(2,1)S(1)}, bf16[8,4096]{1,0:T(8,128)(2,1)S(1)}, u32[]{:S(2)}, u32[]{:S(2)}) collective-permute-start(bf16[8,4096]{1,0:T(8,128)(2,1)S(1)} %get-tuple-element.65), channel_id=1, source_target_pairs={{0,2},{1,3},{2,0},{3,1},{4,6},{5,7},{6,4},{7,5},{8,10},{9,11},{10,... | collective-permute-start | bytes 196616 | tf_op jit(solution)/shard_map/ppermute | solution.py:342
  67.0 10.6 %collective-permute-start.27 = (bf16[8,4096]{1,0:T(8,128)(2,1)S(1)}, bf16[8,4096]{1,0:T(8,128)(2,1)S(1)}, u32[]{:S(2)}, u32[]{:S(2)}) collective-permute-start(bf16[8,4096]{1,0:T(8,128)(2,1)S(1)} %get-tuple-element.70), channel_id=1, source_target_pairs={{0,14},{1,15},{2,12},{3,13},{4,10},{5,11},{6,8},{7,9},{8,6},{9,7},... | collective-permute-start | bytes 196616 | tf_op jit(solution)/shard_map/ppermute | solution.py:342
  70.4 7.2 %collective-permute-start.28 = (bf16[8,4096]{1,0:T(8,128)(2,1)S(1)}, bf16[8,4096]{1,0:T(8,128)(2,1)S(1)}, u32[]{:S(2)}, u32[]{:S(2)}) collective-permute-start(bf16[8,4096]{1,0:T(8,128)(2,1)S(1)} %get-tuple-element.71), channel_id=1, source_target_pairs={{0,3},{1,2},{2,1},{3,0},{4,7},{5,6},{6,5},{7,4},{8,11},{9,10},{10,... | collective-permute-start | bytes 196616 | tf_op jit(solution)/shard_map/ppermute | solution.py:342
  71.3 8.9 %collective-permute-start.29 = (bf16[8,4096]{1,0:T(8,128)(2,1)S(1)}, bf16[8,4096]{1,0:T(8,128)(2,1)S(1)}, u32[]{:S(2)}, u32[]{:S(2)}) collective-permute-start(bf16[8,4096]{1,0:T(8,128)(2,1)S(1)} %get-tuple-element.72), channel_id=1, source_target_pairs={{0,15},{1,14},{2,13},{3,12},{4,11},{5,10},{6,9},{7,8},{8,7},{9,6},... | collective-permute-start | bytes 196616 | tf_op jit(solution)/shard_map/ppermute | solution.py:342
  73.7 7.6 %collective-permute-start.12 = (bf16[8,4096]{1,0:T(8,128)(2,1)S(1)}, bf16[8,4096]{1,0:T(8,128)(2,1)S(1)}, u32[]{:S(2)}, u32[]{:S(2)}) collective-permute-start(bf16[8,4096]{1,0:T(8,128)(2,1)S(1)} %get-tuple-element.54), channel_id=1, source_target_pairs={{0,10},{1,11},{2,8},{3,9},{4,14},{5,15},{6,12},{7,13},{8,2},{9,3},... | collective-permute-start | bytes 196616 | tf_op jit(solution)/shard_map/ppermute | solution.py:342
  73.7 7.6 %collective-permute-start.13 = (bf16[8,4096]{1,0:T(8,128)(2,1)S(1)}, bf16[8,4096]{1,0:T(8,128)(2,1)S(1)}, u32[]{:S(2)}, u32[]{:S(2)}) collective-permute-start(bf16[8,4096]{1,0:T(8,128)(2,1)S(1)} %get-tuple-element.55), channel_id=1, source_target_pairs={{0,6},{1,7},{2,4},{3,5},{4,2},{5,3},{6,0},{7,1},{8,14},{9,15},{10,... | collective-permute-start | bytes 196616 | tf_op jit(solution)/shard_map/ppermute | solution.py:342
  77.7 6.5 %collective-permute-start.14 = (bf16[8,4096]{1,0:T(8,128)(2,1)S(1)}, bf16[8,4096]{1,0:T(8,128)(2,1)S(1)}, u32[]{:S(2)}, u32[]{:S(2)}) collective-permute-start(bf16[8,4096]{1,0:T(8,128)(2,1)S(1)} %get-tuple-element.56), channel_id=1, source_target_pairs={{0,11},{1,10},{2,9},{3,8},{4,15},{5,14},{6,13},{7,12},{8,3},{9,2},... | collective-permute-start | bytes 196616 | tf_op jit(solution)/shard_map/ppermute | solution.py:342
  77.7 6.5 %collective-permute-start.15 = (bf16[8,4096]{1,0:T(8,128)(2,1)S(1)}, bf16[8,4096]{1,0:T(8,128)(2,1)S(1)}, u32[]{:S(2)}, u32[]{:S(2)}) collective-permute-start(bf16[8,4096]{1,0:T(8,128)(2,1)S(1)} %get-tuple-element.57), channel_id=1, source_target_pairs={{0,7},{1,6},{2,5},{3,4},{4,3},{5,2},{6,1},{7,0},{8,15},{9,14},{10,... | collective-permute-start | bytes 196616 | tf_op jit(solution)/shard_map/ppermute | solution.py:342

commit v21 on v20

--- a/solution.py
+++ b/solution.py
@@ -13,9 +13,9 @@
 LANES = 128
 SCALE = 2.0
 ROWS_STEP = 8
-PREP_STEPS = 2
+PREP_STEPS = 4
 GROUPS = 4
-HELD = 4
+HELD = 13
 MOST_PERMUTES = 32
 COLUMNS_STEP = 1024
 ADAPT_STEP = 2048

time: 88.9 us -> 88 us (0.990)
  starting transfers between devices: 53.3 us -> 59 us
  waiting for transfers between devices: 14.7 us -> 11 us
  Pallas kernels: 19.3 us -> 17.2 us
    ppermute x30, starting transfers between devices: 53.3 us -> 59 us  [permutes(): lax.ppermute(message, 'owner', [(i, i ^ s) for i in range(owners)])]
    ppermute x30, waiting for transfers between devices: 14.7 us -> 11 us  [permutes(): lax.ppermute(message, 'owner', [(i, i ^ s) for i in range(owners)])]
    pallas_call x1, Pallas kernels: 7.21 us -> 5.14 us  [prep(): pl.pallas_call(functools.partial(prep_kernel, group), grid=(steps,), in_s...]
  transfers between devices with their start and end apart: 30 -> 30, of which waited for: 8 -> 6; matrix products, arithmetic and copies ran while one was open for 0% -> 0% of each run, Pallas kernels for 11% -> 9%
where the time goes in v21:
time: 88 us; the launch traced here: 87.8 us
  starting transfers between devices  59 us (67%)
  Pallas kernels  17.2 us (20%)
  waiting for transfers between devices  11 us (12%)
    ppermute x30, starting transfers between devices, permutes(): lax.ppermute(message, 'owner', [(i, i ^ s) for i in range(owners)])  59 us
    ppermute x30, waiting for transfers between devices, permutes(): lax.ppermute(message, 'owner', [(i, i ^ s) for i in range(owners)])  11 us
    pallas_call x1, Pallas kernels, prep(): pl.pallas_call(functools.partial(prep_kernel, group), grid=(steps,), in_s...  5.14 us
    pallas_call x1, Pallas kernels, pack(): pl.pallas_call(functools.partial(pack_kernel, owners, slot_count, held),...  4.92 us
    pallas_call x1, Pallas kernels, attend(): pl.pallas_call(functools.partial(attend_kernel, group, context, order), i...  4.42 us
    pallas_call x4, Pallas kernels, adapt(): pl.pallas_call(functools.partial(adapt_kernel, count), in_specs=[pl.Block...  2.73 us
  transfers between devices with their start and end apart: 30, of which 6 were waited for; matrix products, arithmetic and copies ran while one was open for 0% of the time, Pallas kernels for 9%

profile of v21, /device:TPU:0, one launch (start us, length us, event | category | flops | bytes accessed | tf_op | source)
XLA Modules:
  0.0 87.8 jit_solution(2937748540945601377)
XLA Ops:
  0.0 4.9 %pack.1 = (bf16[128,128]{1,0:T(8,128)(2,1)}, bf16[8,8320]{1,0:T(8,128)(2,1)}, bf16[8,8320]{1,0:T(8,128)(2,1)}, bf16[8,8320]{1,0:T(8,128)(2,1)}, bf16[8,8320]{1,0...) custom-call(s32[1,32]{1,0:T(1,128)} %bitcast.2, ...), custom_call_target="tpu_custom_call" | custom-call | tf_op jit(solution)/shard_map/pack/pallas_call | solution.py:92
  4.9 4.1 %collective-permute-start = (bf16[8,8320]{1,0:T(8,128)(2,1)}, bf16[8,8320]{1,0:T(8,128)(2,1)S(1)}, u32[]{:S(2)}, u32[]{:S(2)}) collective-permute-start(bf16[8,8320]{1,0:T(8,128)(2,1)} %get-tuple-element.41), channel_id=1, source_target_pairs={{0,8},{1,9},{2,10},{3,11},{4,12},{5,13},{6,14},{7,15},{8,0},{9,1},... | collective-permute-start | bytes 399368 | tf_op jit(solution)/shard_map/ppermute | solution.py:342
  9.0 1.6 %collective-permute-start.1 = (bf16[8,8320]{1,0:T(8,128)(2,1)}, bf16[8,8320]{1,0:T(8,128)(2,1)S(1)}, u32[]{:S(2)}, u32[]{:S(2)}) collective-permute-start(bf16[8,8320]{1,0:T(8,128)(2,1)} %get-tuple-element.42), channel_id=1, source_target_pairs={{0,4},{1,5},{2,6},{3,7},{4,0},{5,1},{6,2},{7,3},{8,12},{9,13},{10,... | collective-permute-start | bytes 399368 | tf_op jit(solution)/shard_map/ppermute | solution.py:342
  10.6 0.0 collective-permute-start.2
  10.6 0.2 collective-permute-start.3
  10.9 3.8 %collective-permute-start.8 = (bf16[8,8320]{1,0:T(8,128)(2,1)}, bf16[8,8320]{1,0:T(8,128)(2,1)S(1)}, u32[]{:S(2)}, u32[]{:S(2)}) collective-permute-start(bf16[8,8320]{1,0:T(8,128)(2,1)} %get-tuple-element.49), channel_id=1, source_target_pairs={{0,10},{1,11},{2,8},{3,9},{4,14},{5,15},{6,12},{7,13},{8,2},{9,3},... | collective-permute-start | bytes 399368 | tf_op jit(solution)/shard_map/ppermute | solution.py:342
  14.6 2.4 %collective-permute-done.refs_0_ = bf16[8,8320]{1,0:T(8,128)(2,1)S(1)} collective-permute-done((bf16[8,8320]{1,0:T(8,128)(2,1)}, bf16[8,8320]{1,0:T(8,128)(2,1)S(1)}, u32[]{:S(2)}, u32[]{:S(2)}) %collective-permute-start) | collective-permute-done | bytes 133152 | tf_op jit(solution)/shard_map/ppermute | solution.py:342
  17.1 1.3 %collective-permute-start.9 = (bf16[8,8320]{1,0:T(8,128)(2,1)}, bf16[8,8320]{1,0:T(8,128)(2,1)S(1)}, u32[]{:S(2)}, u32[]{:S(2)}) collective-permute-start(bf16[8,8320]{1,0:T(8,128)(2,1)} %get-tuple-element.50), channel_id=1, source_target_pairs={{0,6},{1,7},{2,4},{3,5},{4,2},{5,3},{6,0},{7,1},{8,14},{9,15},{10,... | collective-permute-start | bytes 399368 | tf_op jit(solution)/shard_map/ppermute | solution.py:342
  18.4 0.0 collective-permute-done.1.refs_1_
  18.4 2.6 %collective-permute-start.10 = (bf16[8,8320]{1,0:T(8,128)(2,1)}, bf16[8,8320]{1,0:T(8,128)(2,1)S(1)}, u32[]{:S(2)}, u32[]{:S(2)}) collective-permute-start(bf16[8,8320]{1,0:T(8,128)(2,1)} %get-tuple-element.51), channel_id=1, source_target_pairs={{0,11},{1,10},{2,9},{3,8},{4,15},{5,14},{6,13},{7,12},{8,3},{9,2},... | collective-permute-start | bytes 399368 | tf_op jit(solution)/shard_map/ppermute | solution.py:342
  21.0 0.0 collective-permute-done.2.refs_2_
  21.0 2.2 %collective-permute-start.11 = (bf16[8,8320]{1,0:T(8,128)(2,1)}, bf16[8,8320]{1,0:T(8,128)(2,1)S(1)}, u32[]{:S(2)}, u32[]{:S(2)}) collective-permute-start(bf16[8,8320]{1,0:T(8,128)(2,1)} %get-tuple-element.52), channel_id=1, source_target_pairs={{0,7},{1,6},{2,5},{3,4},{4,3},{5,2},{6,1},{7,0},{8,15},{9,14},{10,... | collective-permute-start | bytes 399368 | tf_op jit(solution)/shard_map/ppermute | solution.py:342
  23.3 0.0 collective-permute-done.3.refs_3_
  23.3 2.6 %collective-permute-start.16 = (bf16[8,8320]{1,0:T(8,128)(2,1)}, bf16[8,8320]{1,0:T(8,128)(2,1)S(1)}, u32[]{:S(2)}, u32[]{:S(2)}) collective-permute-start(bf16[8,8320]{1,0:T(8,128)(2,1)} %get-tuple-element.57), channel_id=1, source_target_pairs={{0,12},{1,13},{2,14},{3,15},{4,8},{5,9},{6,10},{7,11},{8,4},{9,5},... | collective-permute-start | bytes 399368 | tf_op jit(solution)/shard_map/ppermute | solution.py:342
  25.8 3.8 %collective-permute-done.8.refs_0_ = bf16[8,8320]{1,0:T(8,128)(2,1)S(1)} collective-permute-done((bf16[8,8320]{1,0:T(8,128)(2,1)}, bf16[8,8320]{1,0:T(8,128)(2,1)S(1)}, u32[]{:S(2)}, u32[]{:S(2)}) %collective-permute-start.8) | collective-permute-done | bytes 133152 | tf_op jit(solution)/shard_map/ppermute | solution.py:342
  29.6 0.0 collective-permute-start.17
  29.6 0.1 broadcast_in_dim.7
  29.7 0.1 broadcast_in_dim.8
  29.8 0.1 broadcast_in_dim.9.given_ref
  29.9 5.1 %prep.1 = (bf16[4,128,2048]{2,1,0:T(8,128)(2,1)S(1)}, bf16[4,92,192,128]{3,2,1,0:T(8,128)(2,1)}, s32[16,1,128]{2,1,0:T(1,128)S(1)}) custom-call(bf16[128,4096]{1,0:T(8,128)(2,1)S(1)} %copy-done.2, bf16[128,2,16,512]{3,2,1,0:T(8,128)(2,1)} %kv_ref.1, s32[16,1,128]{2,1,0:T(1,128)S(1)} %broadcast_in_dim.9.given_ref), custom_call_target="tpu_custom_call" | custom-call | tf_op jit(solution)/shard_map/prep/pallas_call | solution.py:180
  35.1 3.3 %collective-permute-start.18 = (bf16[8,8320]{1,0:T(8,128)(2,1)S(1)}, bf16[8,8320]{1,0:T(8,128)(2,1)S(1)}, u32[]{:S(2)}, u32[]{:S(2)}) collective-permute-start(bf16[8,8320]{1,0:T(8,128)(2,1)S(1)} %copy-done.10), channel_id=1, source_target_pairs={{0,13},{1,12},{2,15},{3,14},{4,9},{5,8},{6,11},{7,10},{8,5},{9,4},... | collective-permute-start | bytes 399368 | tf_op jit(solution)/shard_map/ppermute | solution.py:342
  38.4 0.0 collective-permute-done.10.refs_2_
  38.4 0.5 collective-permute-start.19
  38.9 0.0 collective-permute-done.11.refs_3_
  38.9 1.6 %collective-permute-start.24 = (bf16[8,8320]{1,0:T(8,128)(2,1)S(1)}, bf16[8,8320]{1,0:T(8,128)(2,1)S(1)}, u32[]{:S(2)}, u32[]{:S(2)}) collective-permute-start(bf16[8,8320]{1,0:T(8,128)(2,1)S(1)} %copy-done.8), channel_id=1, source_target_pairs={{0,14},{1,15},{2,12},{3,13},{4,10},{5,11},{6,8},{7,9},{8,6},{9,7},... | collective-permute-start | bytes 399368 | tf_op jit(solution)/shard_map/ppermute | solution.py:342
  40.5 2.2 %collective-permute-start.26 = (bf16[8,8320]{1,0:T(8,128)(2,1)S(1)}, bf16[8,8320]{1,0:T(8,128)(2,1)S(1)}, u32[]{:S(2)}, u32[]{:S(2)}) collective-permute-start(bf16[8,8320]{1,0:T(8,128)(2,1)S(1)} %copy-done.7), channel_id=1, source_target_pairs={{0,15},{1,14},{2,13},{3,12},{4,11},{5,10},{6,9},{7,8},{8,7},{9,6},... | collective-permute-start | bytes 399368 | tf_op jit(solution)/shard_map/ppermute | solution.py:342
  42.7 2.2 %collective-permute-start.25 = (bf16[8,8320]{1,0:T(8,128)(2,1)S(1)}, bf16[8,8320]{1,0:T(8,128)(2,1)S(1)}, u32[]{:S(2)}, u32[]{:S(2)}) collective-permute-start(bf16[8,8320]{1,0:T(8,128)(2,1)S(1)} %hold.1), channel_id=1, source_target_pairs={{0,3},{1,2},{2,1},{3,0},{4,7},{5,6},{6,5},{7,4},{8,11},{9,10},{10,... | collective-permute-start | bytes 399368 | tf_op jit(solution)/shard_map/ppermute | solution.py:342
  44.9 0.7 adapt.4
  45.6 0.7 adapt.5
  46.3 0.0 copy-start.3
  46.3 6.1 %collective-permute-start.4 = (bf16[8,4096]{1,0:T(8,128)(2,1)S(1)}, bf16[8,4096]{1,0:T(8,128)(2,1)S(1)}, u32[]{:S(2)}, u32[]{:S(2)}) collective-permute-start(bf16[8,4096]{1,0:T(8,128)(2,1)S(1)} %get-tuple-element.45), channel_id=1, source_target_pairs={{0,8},{1,9},{2,10},{3,11},{4,12},{5,13},{6,14},{7,15},{8,0},{9,1},... | collective-permute-start | bytes 196616 | tf_op jit(solution)/shard_map/ppermute | solution.py:342
  52.5 3.4 %collective-permute-start.6 = (bf16[8,4096]{1,0:T(8,128)(2,1)S(1)}, bf16[8,4096]{1,0:T(8,128)(2,1)S(1)}, u32[]{:S(2)}, u32[]{:S(2)}) collective-permute-start(bf16[8,4096]{1,0:T(8,128)(2,1)S(1)} %get-tuple-element.47), channel_id=1, source_target_pairs={{0,9},{1,8},{2,11},{3,10},{4,13},{5,12},{6,15},{7,14},{8,1},{9,0},... | collective-permute-start | bytes 196616 | tf_op jit(solution)/shard_map/ppermute | solution.py:342
  55.9 4.2 %collective-permute-start.7 = (bf16[8,4096]{1,0:T(8,128)(2,1)S(1)}, bf16[8,4096]{1,0:T(8,128)(2,1)S(1)}, u32[]{:S(2)}, u32[]{:S(2)}) collective-permute-start(bf16[8,4096]{1,0:T(8,128)(2,1)S(1)} %get-tuple-element.48), channel_id=1, source_target_pairs={{0,5},{1,4},{2,7},{3,6},{4,1},{5,0},{6,3},{7,2},{8,13},{9,12},{10,... | collective-permute-start | bytes 196616 | tf_op jit(solution)/shard_map/ppermute | solution.py:342
  60.1 0.4 collective-permute-start.12
  60.5 0.7 adapt.6
  61.2 4.1 %collective-permute-start.13 = (bf16[8,4096]{1,0:T(8,128)(2,1)S(1)}, bf16[8,4096]{1,0:T(8,128)(2,1)S(1)}, u32[]{:S(2)}, u32[]{:S(2)}) collective-permute-start(bf16[8,4096]{1,0:T(8,128)(2,1)S(1)} %get-tuple-element.54), channel_id=1, source_target_pairs={{0,6},{1,7},{2,4},{3,5},{4,2},{5,3},{6,0},{7,1},{8,14},{9,15},{10,... | collective-permute-start | bytes 196616 | tf_op jit(solution)/shard_map/ppermute | solution.py:342
  65.3 2.1 %collective-permute-start.15 = (bf16[8,4096]{1,0:T(8,128)(2,1)S(1)}, bf16[8,4096]{1,0:T(8,128)(2,1)S(1)}, u32[]{:S(2)}, u32[]{:S(2)}) collective-permute-start(bf16[8,4096]{1,0:T(8,128)(2,1)S(1)} %get-tuple-element.56), channel_id=1, source_target_pairs={{0,7},{1,6},{2,5},{3,4},{4,3},{5,2},{6,1},{7,0},{8,15},{9,14},{10,... | collective-permute-start | bytes 196616 | tf_op jit(solution)/shard_map/ppermute | solution.py:342
  67.4 2.9 %collective-permute-start.20 = (bf16[8,4096]{1,0:T(8,128)(2,1)S(1)}, bf16[8,4096]{1,0:T(8,128)(2,1)S(1)}, u32[]{:S(2)}, u32[]{:S(2)}) collective-permute-start(bf16[8,4096]{1,0:T(8,128)(2,1)S(1)} %get-tuple-element.61), channel_id=1, source_target_pairs={{0,12},{1,13},{2,14},{3,15},{4,8},{5,9},{6,10},{7,11},{8,4},{9,5},... | collective-permute-start | bytes 196616 | tf_op jit(solution)/shard_map/ppermute | solution.py:342
  70.3 0.7 adapt.7
  71.0 1.1 %collective-permute-start.22 = (bf16[8,4096]{1,0:T(8,128)(2,1)S(1)}, bf16[8,4096]{1,0:T(8,128)(2,1)S(1)}, u32[]{:S(2)}, u32[]{:S(2)}) collective-permute-start(bf16[8,4096]{1,0:T(8,128)(2,1)S(1)} %get-tuple-element.63), channel_id=1, source_target_pairs={{0,13},{1,12},{2,15},{3,14},{4,9},{5,8},{6,11},{7,10},{8,5},{9,4},... | collective-permute-start | bytes 196616 | tf_op jit(solution)/shard_map/ppermute | solution.py:342
  72.1 0.3 collective-permute-done.14.refs_6_
  72.3 0.4 collective-permute-start.23
  72.7 3.8 %collective-permute-start.27 = (bf16[8,4096]{1,0:T(8,128)(2,1)S(1)}, bf16[8,4096]{1,0:T(8,128)(2,1)S(1)}, u32[]{:S(2)}, u32[]{:S(2)}) collective-permute-start(bf16[8,4096]{1,0:T(8,128)(2,1)S(1)} %get-tuple-element.70), channel_id=1, source_target_pairs={{0,14},{1,15},{2,12},{3,13},{4,10},{5,11},{6,8},{7,9},{8,6},{9,7},... | collective-permute-start | bytes 196616 | tf_op jit(solution)/shard_map/ppermute | solution.py:342
  76.5 2.3 %collective-permute-start.29 = (bf16[8,4096]{1,0:T(8,128)(2,1)S(1)}, bf16[8,4096]{1,0:T(8,128)(2,1)S(1)}, u32[]{:S(2)}, u32[]{:S(2)}) collective-permute-start(bf16[8,4096]{1,0:T(8,128)(2,1)S(1)} %get-tuple-element.72), channel_id=1, source_target_pairs={{0,15},{1,14},{2,13},{3,12},{4,11},{5,10},{6,9},{7,8},{8,7},{9,6},... | collective-permute-start | bytes 196616 | tf_op jit(solution)/shard_map/ppermute | solution.py:342
  78.8 0.9 %collective-permute-done.27.refs_12_ = bf16[8,4096]{1,0:T(8,128)(2,1)S(1)} collective-permute-done((bf16[8,4096]{1,0:T(8,128)(2,1)S(1)}, bf16[8,4096]{1,0:T(8,128)(2,1)S(1)}, u32[]{:S(2)}, u32[]{:S(2)}) %collective-permute-start.27) | collective-permute-done | bytes 65568 | tf_op jit(solution)/shard_map/ppermute | solution.py:342
  79.7 1.3 %collective-permute-done.28.refs_13_ = bf16[8,4096]{1,0:T(8,128)(2,1)S(1)} collective-permute-done((bf16[8,4096]{1,0:T(8,128)(2,1)S(1)}, bf16[8,4096]{1,0:T(8,128)(2,1)S(1)}, u32[]{:S(2)}, u32[]{:S(2)}) %collective-permute-start.28) | collective-permute-done | bytes 65568 | tf_op jit(solution)/shard_map/ppermute | solution.py:342
  81.1 2.3 %collective-permute-done.29.refs_14_ = bf16[8,4096]{1,0:T(8,128)(2,1)S(1)} collective-permute-done((bf16[8,4096]{1,0:T(8,128)(2,1)S(1)}, bf16[8,4096]{1,0:T(8,128)(2,1)S(1)}, u32[]{:S(2)}, u32[]{:S(2)}) %collective-permute-start.29) | collective-permute-done | bytes 65568 | tf_op jit(solution)/shard_map/ppermute | solution.py:342
  83.3 4.4 %attend.1 = bf16[128,4096]{1,0:T(8,128)(2,1)} custom-call(bf16[8,4096]{1,0:T(8,128)(2,1)S(1)} %collective-permute-done.4.refs_0_, bf16[8,4096]{1,0:T(8,128)(2,1)S(1)} %collective-permute-done.5.refs_1_, bf16[8,4096]{1,0:T(8,128)(2,1)S(1)} %collective-permute-done.6.refs_2_, bf16[8,4096]{1,0:T(8,128)(2,1)S(1)} %collective-permute-done.7.refs_3_, ...), custom_call_target="tpu_custom_call" | custom-call | tf_op jit(solution)/shard_map/attend/pallas_call | solution.py:299
  (45 shorter events, 0.1 us)
Async XLA Ops:
  0.0 29.6 %copy-start.6 = (s32[128]{0:T(128)S(1)}, s32[128]{0:T(128)}, u32[]{:S(2)}) copy-start(s32[128]{0:T(128)} %param.11) | copy-start | bytes 1540
  0.0 29.9 %copy-start.2 = (bf16[128,4096]{1,0:T(8,128)(2,1)S(1)}, bf16[128,4096]{1,0:T(8,128)(2,1)}, u32[]{:S(2)}) copy-start(bf16[128,4096]{1,0:T(8,128)(2,1)} %base_ref.1) | copy-start | bytes 3145732
  4.9 12.1 %collective-permute-start = (bf16[8,8320]{1,0:T(8,128)(2,1)}, bf16[8,8320]{1,0:T(8,128)(2,1)S(1)}, u32[]{:S(2)}, u32[]{:S(2)}) collective-permute-start(bf16[8,8320]{1,0:T(8,128)(2,1)} %get-tuple-element.41), channel_id=1, source_target_pairs={{0,8},{1,9},{2,10},{3,11},{4,12},{5,13},{6,14},{7,15},{8,0},{9,1},... | collective-permute-start | bytes 399368 | tf_op jit(solution)/shard_map/ppermute | solution.py:342
  9.0 9.4 %collective-permute-start.1 = (bf16[8,8320]{1,0:T(8,128)(2,1)}, bf16[8,8320]{1,0:T(8,128)(2,1)S(1)}, u32[]{:S(2)}, u32[]{:S(2)}) collective-permute-start(bf16[8,8320]{1,0:T(8,128)(2,1)} %get-tuple-element.42), channel_id=1, source_target_pairs={{0,4},{1,5},{2,6},{3,7},{4,0},{5,1},{6,2},{7,3},{8,12},{9,13},{10,... | collective-permute-start | bytes 399368 | tf_op jit(solution)/shard_map/ppermute | solution.py:342
  10.6 10.4 %collective-permute-start.2 = (bf16[8,8320]{1,0:T(8,128)(2,1)}, bf16[8,8320]{1,0:T(8,128)(2,1)S(1)}, u32[]{:S(2)}, u32[]{:S(2)}) collective-permute-start(bf16[8,8320]{1,0:T(8,128)(2,1)} %get-tuple-element.43), channel_id=1, source_target_pairs={{0,9},{1,8},{2,11},{3,10},{4,13},{5,12},{6,15},{7,14},{8,1},{9,0},... | collective-permute-start | bytes 399368 | tf_op jit(solution)/shard_map/ppermute | solution.py:342
  10.6 12.7 %collective-permute-start.3 = (bf16[8,8320]{1,0:T(8,128)(2,1)}, bf16[8,8320]{1,0:T(8,128)(2,1)S(1)}, u32[]{:S(2)}, u32[]{:S(2)}) collective-permute-start(bf16[8,8320]{1,0:T(8,128)(2,1)} %get-tuple-element.44), channel_id=1, source_target_pairs={{0,5},{1,4},{2,7},{3,6},{4,1},{5,0},{6,3},{7,2},{8,13},{9,12},{10,... | collective-permute-start | bytes 399368 | tf_op jit(solution)/shard_map/ppermute | solution.py:342
  10.9 18.7 %collective-permute-start.8 = (bf16[8,8320]{1,0:T(8,128)(2,1)}, bf16[8,8320]{1,0:T(8,128)(2,1)S(1)}, u32[]{:S(2)}, u32[]{:S(2)}) collective-permute-start(bf16[8,8320]{1,0:T(8,128)(2,1)} %get-tuple-element.49), channel_id=1, source_target_pairs={{0,10},{1,11},{2,8},{3,9},{4,14},{5,15},{6,12},{7,13},{8,2},{9,3},... | collective-permute-start | bytes 399368 | tf_op jit(solution)/shard_map/ppermute | solution.py:342
  17.1 18.0 %collective-permute-start.9 = (bf16[8,8320]{1,0:T(8,128)(2,1)}, bf16[8,8320]{1,0:T(8,128)(2,1)S(1)}, u32[]{:S(2)}, u32[]{:S(2)}) collective-permute-start(bf16[8,8320]{1,0:T(8,128)(2,1)} %get-tuple-element.50), channel_id=1, source_target_pairs={{0,6},{1,7},{2,4},{3,5},{4,2},{5,3},{6,0},{7,1},{8,14},{9,15},{10,... | collective-permute-start | bytes 399368 | tf_op jit(solution)/shard_map/ppermute | solution.py:342
  18.4 20.0 %collective-permute-start.10 = (bf16[8,8320]{1,0:T(8,128)(2,1)}, bf16[8,8320]{1,0:T(8,128)(2,1)S(1)}, u32[]{:S(2)}, u32[]{:S(2)}) collective-permute-start(bf16[8,8320]{1,0:T(8,128)(2,1)} %get-tuple-element.51), channel_id=1, source_target_pairs={{0,11},{1,10},{2,9},{3,8},{4,15},{5,14},{6,13},{7,12},{8,3},{9,2},... | collective-permute-start | bytes 399368 | tf_op jit(solution)/shard_map/ppermute | solution.py:342
  21.0 17.9 %collective-permute-start.11 = (bf16[8,8320]{1,0:T(8,128)(2,1)}, bf16[8,8320]{1,0:T(8,128)(2,1)S(1)}, u32[]{:S(2)}, u32[]{:S(2)}) collective-permute-start(bf16[8,8320]{1,0:T(8,128)(2,1)} %get-tuple-element.52), channel_id=1, source_target_pairs={{0,7},{1,6},{2,5},{3,4},{4,3},{5,2},{6,1},{7,0},{8,15},{9,14},{10,... | collective-permute-start | bytes 399368 | tf_op jit(solution)/shard_map/ppermute | solution.py:342
  23.3 17.2 %collective-permute-start.16 = (bf16[8,8320]{1,0:T(8,128)(2,1)}, bf16[8,8320]{1,0:T(8,128)(2,1)S(1)}, u32[]{:S(2)}, u32[]{:S(2)}) collective-permute-start(bf16[8,8320]{1,0:T(8,128)(2,1)} %get-tuple-element.57), channel_id=1, source_target_pairs={{0,12},{1,13},{2,14},{3,15},{4,8},{5,9},{6,10},{7,11},{8,4},{9,5},... | collective-permute-start | bytes 399368 | tf_op jit(solution)/shard_map/ppermute | solution.py:342
  29.6 13.1 %collective-permute-start.17 = (bf16[8,8320]{1,0:T(8,128)(2,1)}, bf16[8,8320]{1,0:T(8,128)(2,1)S(1)}, u32[]{:S(2)}, u32[]{:S(2)}) collective-permute-start(bf16[8,8320]{1,0:T(8,128)(2,1)} %get-tuple-element.58), channel_id=1, source_target_pairs={{0,1},{1,0},{2,3},{3,2},{4,5},{5,4},{6,7},{7,6},{8,9},{9,8},{10,11... | collective-permute-start | bytes 399368 | tf_op jit(solution)/shard_map/ppermute | solution.py:342
  29.9 5.2 %copy-start.10 = (bf16[8,8320]{1,0:T(8,128)(2,1)S(1)}, bf16[8,8320]{1,0:T(8,128)(2,1)}, u32[]{:S(2)}) copy-start(bf16[8,8320]{1,0:T(8,128)(2,1)} %get-tuple-element.59) | copy-start | bytes 399364
  29.9 8.5 %copy-start.9 = (bf16[8,8320]{1,0:T(8,128)(2,1)S(1)}, bf16[8,8320]{1,0:T(8,128)(2,1)}, u32[]{:S(2)}) copy-start(bf16[8,8320]{1,0:T(8,128)(2,1)} %get-tuple-element.60) | copy-start | bytes 399364
  29.9 9.0 %copy-start.8 = (bf16[8,8320]{1,0:T(8,128)(2,1)S(1)}, bf16[8,8320]{1,0:T(8,128)(2,1)}, u32[]{:S(2)}) copy-start(bf16[8,8320]{1,0:T(8,128)(2,1)} %get-tuple-element.65) | copy-start | bytes 399364
  29.9 10.6 %copy-start.7 = (bf16[8,8320]{1,0:T(8,128)(2,1)S(1)}, bf16[8,8320]{1,0:T(8,128)(2,1)}, u32[]{:S(2)}) copy-start(bf16[8,8320]{1,0:T(8,128)(2,1)} %get-tuple-element.68) | copy-start | bytes 399364
  29.9 12.8 %copy-start.4 = (bf16[8,8320]{1,0:T(8,128)(2,1)S(1)}, bf16[8,8320]{1,0:T(8,128)(2,1)}, u32[]{:S(2)}) copy-start(bf16[8,8320]{1,0:T(8,128)(2,1)} %get-tuple-element.66.refs_0_) | copy-start | bytes 399364
  35.1 11.2 %collective-permute-start.18 = (bf16[8,8320]{1,0:T(8,128)(2,1)S(1)}, bf16[8,8320]{1,0:T(8,128)(2,1)S(1)}, u32[]{:S(2)}, u32[]{:S(2)}) collective-permute-start(bf16[8,8320]{1,0:T(8,128)(2,1)S(1)} %copy-done.10), channel_id=1, source_target_pairs={{0,13},{1,12},{2,15},{3,14},{4,9},{5,8},{6,11},{7,10},{8,5},{9,4},... | collective-permute-start | bytes 399368 | tf_op jit(solution)/shard_map/ppermute | solution.py:342
  38.4 14.1 %collective-permute-start.19 = (bf16[8,8320]{1,0:T(8,128)(2,1)S(1)}, bf16[8,8320]{1,0:T(8,128)(2,1)S(1)}, u32[]{:S(2)}, u32[]{:S(2)}) collective-permute-start(bf16[8,8320]{1,0:T(8,128)(2,1)S(1)} %copy-done.9), channel_id=1, source_target_pairs={{0,2},{1,3},{2,0},{3,1},{4,6},{5,7},{6,4},{7,5},{8,10},{9,11},{10,... | collective-permute-start | bytes 399368 | tf_op jit(solution)/shard_map/ppermute | solution.py:342
  38.9 13.6 %collective-permute-start.24 = (bf16[8,8320]{1,0:T(8,128)(2,1)S(1)}, bf16[8,8320]{1,0:T(8,128)(2,1)S(1)}, u32[]{:S(2)}, u32[]{:S(2)}) collective-permute-start(bf16[8,8320]{1,0:T(8,128)(2,1)S(1)} %copy-done.8), channel_id=1, source_target_pairs={{0,14},{1,15},{2,12},{3,13},{4,10},{5,11},{6,8},{7,9},{8,6},{9,7},... | collective-permute-start | bytes 399368 | tf_op jit(solution)/shard_map/ppermute | solution.py:342
  40.5 15.4 %collective-permute-start.26 = (bf16[8,8320]{1,0:T(8,128)(2,1)S(1)}, bf16[8,8320]{1,0:T(8,128)(2,1)S(1)}, u32[]{:S(2)}, u32[]{:S(2)}) collective-permute-start(bf16[8,8320]{1,0:T(8,128)(2,1)S(1)} %copy-done.7), channel_id=1, source_target_pairs={{0,15},{1,14},{2,13},{3,12},{4,11},{5,10},{6,9},{7,8},{8,7},{9,6},... | collective-permute-start | bytes 399368 | tf_op jit(solution)/shard_map/ppermute | solution.py:342
  42.7 2.2 %copy-start = (bf16[8192,128]{1,0:T(8,128)(2,1)S(1)}, bf16[8192,128]{1,0:T(8,128)(2,1)}, u32[]{:S(2)}) copy-start(bf16[8192,128]{1,0:T(8,128)(2,1)} %refs_4_.7) | copy-start | bytes 6291460
  42.7 2.2 %copy-start.1 = (bf16[128,4096]{1,0:T(8,128)(2,1)S(1)}, bf16[128,4096]{1,0:T(8,128)(2,1)}, u32[]{:S(2)}) copy-start(bf16[128,4096]{1,0:T(8,128)(2,1)} %refs_5_.7) | copy-start | bytes 3145732
  42.7 17.4 %collective-permute-start.25 = (bf16[8,8320]{1,0:T(8,128)(2,1)S(1)}, bf16[8,8320]{1,0:T(8,128)(2,1)S(1)}, u32[]{:S(2)}, u32[]{:S(2)}) collective-permute-start(bf16[8,8320]{1,0:T(8,128)(2,1)S(1)} %hold.1), channel_id=1, source_target_pairs={{0,3},{1,2},{2,1},{3,0},{4,7},{5,6},{6,5},{7,4},{8,11},{9,10},{10,... | collective-permute-start | bytes 399368 | tf_op jit(solution)/shard_map/ppermute | solution.py:342
  46.3 24.0 %copy-start.3 = (bf16[8,8320]{1,0:T(8,128)(2,1)S(1)}, bf16[8,8320]{1,0:T(8,128)(2,1)}, u32[]{:S(2)}) copy-start(bf16[8,8320]{1,0:T(8,128)(2,1)} %get-tuple-element.69.refs_3_) | copy-start | bytes 399364
  46.3 14.9 %collective-permute-start.4 = (bf16[8,4096]{1,0:T(8,128)(2,1)S(1)}, bf16[8,4096]{1,0:T(8,128)(2,1)S(1)}, u32[]{:S(2)}, u32[]{:S(2)}) collective-permute-start(bf16[8,4096]{1,0:T(8,128)(2,1)S(1)} %get-tuple-element.45), channel_id=1, source_target_pairs={{0,8},{1,9},{2,10},{3,11},{4,12},{5,13},{6,14},{7,15},{8,0},{9,1},... | collective-permute-start | bytes 196616 | tf_op jit(solution)/shard_map/ppermute | solution.py:342
  52.5 12.8 %collective-permute-start.5 = (bf16[8,4096]{1,0:T(8,128)(2,1)S(1)}, bf16[8,4096]{1,0:T(8,128)(2,1)S(1)}, u32[]{:S(2)}, u32[]{:S(2)}) collective-permute-start(bf16[8,4096]{1,0:T(8,128)(2,1)S(1)} %get-tuple-element.46), channel_id=1, source_target_pairs={{0,4},{1,5},{2,6},{3,7},{4,0},{5,1},{6,2},{7,3},{8,12},{9,13},{10,... | collective-permute-start | bytes 196616 | tf_op jit(solution)/shard_map/ppermute | solution.py:342
  52.5 12.8 %collective-permute-start.6 = (bf16[8,4096]{1,0:T(8,128)(2,1)S(1)}, bf16[8,4096]{1,0:T(8,128)(2,1)S(1)}, u32[]{:S(2)}, u32[]{:S(2)}) collective-permute-start(bf16[8,4096]{1,0:T(8,128)(2,1)S(1)} %get-tuple-element.47), channel_id=1, source_target_pairs={{0,9},{1,8},{2,11},{3,10},{4,13},{5,12},{6,15},{7,14},{8,1},{9,0},... | collective-permute-start | bytes 196616 | tf_op jit(solution)/shard_map/ppermute | solution.py:342
  55.9 11.5 %collective-permute-start.7 = (bf16[8,4096]{1,0:T(8,128)(2,1)S(1)}, bf16[8,4096]{1,0:T(8,128)(2,1)S(1)}, u32[]{:S(2)}, u32[]{:S(2)}) collective-permute-start(bf16[8,4096]{1,0:T(8,128)(2,1)S(1)} %get-tuple-element.48), channel_id=1, source_target_pairs={{0,5},{1,4},{2,7},{3,6},{4,1},{5,0},{6,3},{7,2},{8,13},{9,12},{10,... | collective-permute-start | bytes 196616 | tf_op jit(solution)/shard_map/ppermute | solution.py:342
  60.1 10.2 %collective-permute-start.12 = (bf16[8,4096]{1,0:T(8,128)(2,1)S(1)}, bf16[8,4096]{1,0:T(8,128)(2,1)S(1)}, u32[]{:S(2)}, u32[]{:S(2)}) collective-permute-start(bf16[8,4096]{1,0:T(8,128)(2,1)S(1)} %get-tuple-element.53), channel_id=1, source_target_pairs={{0,10},{1,11},{2,8},{3,9},{4,14},{5,15},{6,12},{7,13},{8,2},{9,3},... | collective-permute-start | bytes 196616 | tf_op jit(solution)/shard_map/ppermute | solution.py:342
  61.2 22.2 %copy-start.5 = (bf16[128,128]{1,0:T(8,128)(2,1)S(1)}, bf16[128,128]{1,0:T(8,128)(2,1)}, u32[]{:S(2)}) copy-start(bf16[128,128]{1,0:T(8,128)(2,1)} %get-tuple-element.74.refs_16_) | copy-start | bytes 98308
  61.2 9.8 %collective-permute-start.13 = (bf16[8,4096]{1,0:T(8,128)(2,1)S(1)}, bf16[8,4096]{1,0:T(8,128)(2,1)S(1)}, u32[]{:S(2)}, u32[]{:S(2)}) collective-permute-start(bf16[8,4096]{1,0:T(8,128)(2,1)S(1)} %get-tuple-element.54), channel_id=1, source_target_pairs={{0,6},{1,7},{2,4},{3,5},{4,2},{5,3},{6,0},{7,1},{8,14},{9,15},{10,... | collective-permute-start | bytes 196616 | tf_op jit(solution)/shard_map/ppermute | solution.py:342
  65.3 7.0 %collective-permute-start.14 = (bf16[8,4096]{1,0:T(8,128)(2,1)S(1)}, bf16[8,4096]{1,0:T(8,128)(2,1)S(1)}, u32[]{:S(2)}, u32[]{:S(2)}) collective-permute-start(bf16[8,4096]{1,0:T(8,128)(2,1)S(1)} %get-tuple-element.55), channel_id=1, source_target_pairs={{0,11},{1,10},{2,9},{3,8},{4,15},{5,14},{6,13},{7,12},{8,3},{9,2},... | collective-permute-start | bytes 196616 | tf_op jit(solution)/shard_map/ppermute | solution.py:342
  65.3 7.4 %collective-permute-start.15 = (bf16[8,4096]{1,0:T(8,128)(2,1)S(1)}, bf16[8,4096]{1,0:T(8,128)(2,1)S(1)}, u32[]{:S(2)}, u32[]{:S(2)}) collective-permute-start(bf16[8,4096]{1,0:T(8,128)(2,1)S(1)} %get-tuple-element.56), channel_id=1, source_target_pairs={{0,7},{1,6},{2,5},{3,4},{4,3},{5,2},{6,1},{7,0},{8,15},{9,14},{10,... | collective-permute-start | bytes 196616 | tf_op jit(solution)/shard_map/ppermute | solution.py:342
  67.4 9.1 %collective-permute-start.20 = (bf16[8,4096]{1,0:T(8,128)(2,1)S(1)}, bf16[8,4096]{1,0:T(8,128)(2,1)S(1)}, u32[]{:S(2)}, u32[]{:S(2)}) collective-permute-start(bf16[8,4096]{1,0:T(8,128)(2,1)S(1)} %get-tuple-element.61), channel_id=1, source_target_pairs={{0,12},{1,13},{2,14},{3,15},{4,8},{5,9},{6,10},{7,11},{8,4},{9,5},... | collective-permute-start | bytes 196616 | tf_op jit(solution)/shard_map/ppermute | solution.py:342
  70.3 6.2 %collective-permute-start.21 = (bf16[8,4096]{1,0:T(8,128)(2,1)S(1)}, bf16[8,4096]{1,0:T(8,128)(2,1)S(1)}, u32[]{:S(2)}, u32[]{:S(2)}) collective-permute-start(bf16[8,4096]{1,0:T(8,128)(2,1)S(1)} %get-tuple-element.62), channel_id=1, source_target_pairs={{0,1},{1,0},{2,3},{3,2},{4,5},{5,4},{6,7},{7,6},{8,9},{9,8},{10,11... | collective-permute-start | bytes 196616 | tf_op jit(solution)/shard_map/ppermute | solution.py:342
  71.0 7.8 %collective-permute-start.22 = (bf16[8,4096]{1,0:T(8,128)(2,1)S(1)}, bf16[8,4096]{1,0:T(8,128)(2,1)S(1)}, u32[]{:S(2)}, u32[]{:S(2)}) collective-permute-start(bf16[8,4096]{1,0:T(8,128)(2,1)S(1)} %get-tuple-element.63), channel_id=1, source_target_pairs={{0,13},{1,12},{2,15},{3,14},{4,9},{5,8},{6,11},{7,10},{8,5},{9,4},... | collective-permute-start | bytes 196616 | tf_op jit(solution)/shard_map/ppermute | solution.py:342
  72.3 6.5 %collective-permute-start.23 = (bf16[8,4096]{1,0:T(8,128)(2,1)S(1)}, bf16[8,4096]{1,0:T(8,128)(2,1)S(1)}, u32[]{:S(2)}, u32[]{:S(2)}) collective-permute-start(bf16[8,4096]{1,0:T(8,128)(2,1)S(1)} %get-tuple-element.64), channel_id=1, source_target_pairs={{0,2},{1,3},{2,0},{3,1},{4,6},{5,7},{6,4},{7,5},{8,10},{9,11},{10,... | collective-permute-start | bytes 196616 | tf_op jit(solution)/shard_map/ppermute | solution.py:342
  72.7 7.0 %collective-permute-start.27 = (bf16[8,4096]{1,0:T(8,128)(2,1)S(1)}, bf16[8,4096]{1,0:T(8,128)(2,1)S(1)}, u32[]{:S(2)}, u32[]{:S(2)}) collective-permute-start(bf16[8,4096]{1,0:T(8,128)(2,1)S(1)} %get-tuple-element.70), channel_id=1, source_target_pairs={{0,14},{1,15},{2,12},{3,13},{4,10},{5,11},{6,8},{7,9},{8,6},{9,7},... | collective-permute-start | bytes 196616 | tf_op jit(solution)/shard_map/ppermute | solution.py:342
  76.5 4.6 %collective-permute-start.28 = (bf16[8,4096]{1,0:T(8,128)(2,1)S(1)}, bf16[8,4096]{1,0:T(8,128)(2,1)S(1)}, u32[]{:S(2)}, u32[]{:S(2)}) collective-permute-start(bf16[8,4096]{1,0:T(8,128)(2,1)S(1)} %get-tuple-element.71), channel_id=1, source_target_pairs={{0,3},{1,2},{2,1},{3,0},{4,7},{5,6},{6,5},{7,4},{8,11},{9,10},{10,... | collective-permute-start | bytes 196616 | tf_op jit(solution)/shard_map/ppermute | solution.py:342
  76.5 6.9 %collective-permute-start.29 = (bf16[8,4096]{1,0:T(8,128)(2,1)S(1)}, bf16[8,4096]{1,0:T(8,128)(2,1)S(1)}, u32[]{:S(2)}, u32[]{:S(2)}) collective-permute-start(bf16[8,4096]{1,0:T(8,128)(2,1)S(1)} %get-tuple-element.72), channel_id=1, source_target_pairs={{0,15},{1,14},{2,13},{3,12},{4,11},{5,10},{6,9},{7,8},{8,7},{9,6},... | collective-permute-start | bytes 196616 | tf_op jit(solution)/shard_map/ppermute | solution.py:342

commit v22 on v21

--- a/solution.py
+++ b/solution.py
@@ -16,6 +16,7 @@
 PREP_STEPS = 4
 GROUPS = 4
 HELD = 13
+FIRST = 4
 MOST_PERMUTES = 32
 COLUMNS_STEP = 1024
 ADAPT_STEP = 2048
@@ -25,7 +26,7 @@
 TALL_BYTES = 17 * 2**20
 
 
-def routing(owners, slot_count, held, slots, ids):
+def routing(which, owners, slot_count, held, slots, ids):
     rows = ids.shape[1]
     named = lax.broadcasted_iota(jnp.int32, (slots.shape[1], rows), 0) == ids
     slot = jnp.dot(
@@ -43,15 +44,18 @@
         hits.astype(jnp.bfloat16), earlier.astype(jnp.bfloat16), preferred_element_type=jnp.float32
     )
     place = jnp.sum(jnp.where(hits, before, 0.0), axis=0, keepdims=True).astype(jnp.int32)
-    line = lax.broadcasted_iota(jnp.int32, (owners * slot_count, rows), 0)
     apart = owner ^ lax.axis_index("owner")
-    routed = line == apart * slot_count + place
+    target = jnp.full_like(apart, -1)
+    for j, s in enumerate(which):
+        target = jnp.where(apart == s, j * slot_count + place, target)
+    routed = target == lax.broadcasted_iota(jnp.int32, (len(which) * slot_count, rows), 0)
     label = jnp.sum(jnp.where(routed, local.astype(jnp.float32), 0.0), axis=1, keepdims=True)
     return routed, label
 
 
-def pack_kernel(owners, slot_count, held, slots_hbm, ids_hbm, hidden_hbm, routed_ref, *refs):
-    message_refs, (slots_ref, ids_ref, rows_ref, small_sems, sems) = refs[:owners], refs[owners:]
+def pack_kernel(which, owners, slot_count, held, slots_hbm, ids_hbm, hidden_hbm, routed_ref, *refs):
+    message_refs, refs = refs[: len(which)], refs[len(which) :]
+    slots_ref, ids_ref, rows_ref, small_sems, sems = refs
     width = rows_ref.shape[1]
     spans = [(at, min(COLUMNS_STEP, width - at)) for at in range(0, width, COLUMNS_STEP)]
     small = [
@@ -68,9 +72,9 @@
         copy.start()
     for copy in small:
         copy.wait()
-    routed, label = routing(owners, slot_count, held, slots_ref[...], ids_ref[...])
-    routed_ref[...] = jnp.transpose(routed.astype(jnp.float32)).astype(routed_ref.dtype)
+    routed, label = routing(which, owners, slot_count, held, slots_ref[...], ids_ref[...])
     routed = routed.astype(jnp.bfloat16)
+    routed_ref[...] = routed
 
     def put(at, lines):
         for i, message_ref in enumerate(message_refs):
@@ -84,17 +88,17 @@
         put(at, jnp.dot(routed, rows_ref[:, at : at + size], preferred_element_type=jnp.float32))
 
 
-def pack(hidden, adapter_id, adapter_slot, owners, slot_count, held):
+def pack(which, hidden, adapter_id, adapter_slot, owners, slot_count, held):
     rows, width = hidden.shape
-    bins = owners * slot_count
+    lines = len(which) * slot_count
     steps = pl.cdiv(width, COLUMNS_STEP)
     slots = adapter_slot.reshape(1, -1)
     return pl.pallas_call(
-        functools.partial(pack_kernel, owners, slot_count, held),
+        functools.partial(pack_kernel, which, owners, slot_count, held),
         in_specs=[pl.BlockSpec(memory_space=pl.ANY)] * 3,
-        out_specs=[pl.BlockSpec(memory_space=pltpu.VMEM)] * (1 + owners),
-        out_shape=[jax.ShapeDtypeStruct((rows, bins), jnp.bfloat16)]
-        + [jax.ShapeDtypeStruct((slot_count, width + LANES), hidden.dtype)] * owners,
+        out_specs=[pl.BlockSpec(memory_space=pltpu.VMEM)] * (1 + len(which)),
+        out_shape=[jax.ShapeDtypeStruct((lines, rows), jnp.bfloat16)]
+        + [jax.ShapeDtypeStruct((slot_count, width + LANES), hidden.dtype)] * len(which),
         scratch_shapes=[
             pltpu.VMEM(slots.shape, jnp.int32),
             pltpu.VMEM((1, rows), jnp.int32),
@@ -216,10 +220,9 @@
     )(message, after)
 
 
-def attend_kernel(group, context, order, *refs):
-    returned_refs, refs = refs[: len(order)], refs[len(order) :]
-    returned_refs = [returned_refs[order.index(s)] for s in range(len(order))]
-    routed_ref, keys_ref, lens_ref, rest_hbm, out_hbm, *scratch = refs
+def attend_kernel(group, context, count, *refs):
+    returned_refs, routed_refs, refs = refs[:count], refs[count : count + 2], refs[count + 2 :]
+    keys_ref, lens_ref, rest_hbm, out_hbm, *scratch = refs
     query_ref, values_ref, bias_ref, scores_ref, expo_ref, out_ref, sems = scratch
     step = ROWS_STEP
     steps, lines, cells = bias_ref.shape
@@ -252,9 +255,11 @@
     ones = jnp.ones((cells, HEAD), expo_ref.dtype)
     for i in range(steps):
         bias_ref[i] = jnp.where(own & (position < lens_ref[i]), 0.0, -jnp.inf)
+    routed = jnp.concatenate([ref[...].astype(jnp.float32) for ref in routed_refs], axis=0)
+    routed = jnp.transpose(routed).astype(jnp.bfloat16)
     for k in range(KVH):
         delta = jnp.dot(
-            routed_ref[...],
+            routed,
             stack(returned_refs, k * span, span),
             preferred_element_type=jnp.float32,
         )
@@ -290,15 +295,15 @@
         store.wait()
 
 
-def attend(routed, returned, order, keys, rest, lens, context):
-    rows, width = routed.shape[0], returned[0].shape[1]
+def attend(routed, returned, keys, rest, lens, context):
+    rows, width = routed[0].shape[1], returned[0].shape[1]
     group = width // (KVH * HEAD)
     step = ROWS_STEP
     steps = rows // step
     cells = step * context
     return pl.pallas_call(
-        functools.partial(attend_kernel, group, context, order),
-        in_specs=[pl.BlockSpec(memory_space=pltpu.VMEM)] * (3 + len(order)) + [pl.BlockSpec(memory_space=pl.ANY)],
+        functools.partial(attend_kernel, group, context, len(returned)),
+        in_specs=[pl.BlockSpec(memory_space=pltpu.VMEM)] * (4 + len(returned)) + [pl.BlockSpec(memory_space=pl.ANY)],
         out_specs=pl.BlockSpec(memory_space=pl.ANY),
         out_shape=jax.ShapeDtypeStruct((rows, width), jnp.bfloat16),
         scratch_shapes=[
@@ -312,7 +317,7 @@
         ],
         compiler_params=pltpu.CompilerParams(vmem_limit_bytes=GRANT),
         name="attend",
-    )(*returned, routed, keys, lens, rest)
+    )(*returned, *routed, keys, lens, rest)
 
 
 def on_device(hidden, adapter_id, adapter_slot, cache_len, base_q, kv_cache, a_maps, b_maps):
@@ -320,20 +325,24 @@
     rows = hidden.shape[0]
     held = a_maps.shape[1] // RANK
     slot_count = max(2, 2 * ((rows + 2 * owners - 1) // (2 * owners)))
-    routed, *messages = pack(hidden, adapter_id, adapter_slot, owners, slot_count, held)
     half = owners // 2
     near = [*range(half // 2, half), *range(1, half // 2)]
     order = [s for pair in zip(range(half, owners), [*near, 0]) for s in pair]
 
+    routed, messages = [], []
+    for which in (order[:FIRST], order[FIRST:]):
+        hits, *packed = pack(which, hidden, adapter_id, adapter_slot, owners, slot_count, held)
+        routed.append(hits)
+        messages += packed
     keys, rest, lens = prep(base_q, kv_cache, cache_len)
-    messages[order[HELD]] = hold(messages[order[HELD]], rest)
+    messages[HELD] = hold(messages[HELD], rest)
     size = owners // GROUPS
-    arrived = exchange(order, owners)(messages[s] for s in order)
+    arrived = exchange(order, owners)(messages)
     changes = []
     for at in range(0, owners, size):
         changes += adapt(arrived[at : at + size], a_maps, b_maps)
     returned = exchange(order, owners)(changes)
-    return attend(routed, returned, order, keys, rest, lens, kv_cache.shape[2])
+    return attend(routed, returned, keys, rest, lens, kv_cache.shape[2])
 
 
 def exchange(order, owners):

time: 88 us -> 86.9 us (0.988)
  Pallas kernels: 17.2 us -> 20.6 us
  waiting for transfers between devices: 11 us -> 8.61 us
  starting transfers between devices: 59 us -> 57 us
    pallas_call x2 -> x3, Pallas kernels: 9.34 us -> 12.7 us  [the longest x2 8.31 us: pack(): pl.pallas_call(functools.partial(pack_kernel, which, owners, slot_count,...]
    ppermute x30, waiting for transfers between devices: 11 us -> 8.61 us  [permutes(): lax.ppermute(message, 'owner', [(i, i ^ s) for i in range(owners)])]
    ppermute x30, starting transfers between devices: 59 us -> 57 us  [permutes(): lax.ppermute(message, 'owner', [(i, i ^ s) for i in range(owners)])]
  transfers between devices with their start and end apart: 30 -> 30, of which waited for: 6 -> 5; matrix products, arithmetic and copies ran while one was open for 0% -> 0% of each run, Pallas kernels for 9% -> 14%
where the time goes in v22:
time: 86.9 us; the launch traced here: 86.7 us
  starting transfers between devices  57 us (66%)
  Pallas kernels  20.6 us (24%)
  waiting for transfers between devices  8.61 us (10%)
    ppermute x30, starting transfers between devices, permutes(): lax.ppermute(message, 'owner', [(i, i ^ s) for i in range(owners)])  57 us
    ppermute x30, waiting for transfers between devices, permutes(): lax.ppermute(message, 'owner', [(i, i ^ s) for i in range(owners)])  8.61 us
    pallas_call x2, Pallas kernels, pack(): pl.pallas_call(functools.partial(pack_kernel, which, owners, slot_count,...  8.31 us
    pallas_call x1, Pallas kernels, prep(): pl.pallas_call(functools.partial(prep_kernel, group), grid=(steps,), in_s...  5.14 us
    pallas_call x1, Pallas kernels, attend(): pl.pallas_call(functools.partial(attend_kernel, group, context, len(retur...  4.44 us
    pallas_call x4, Pallas kernels, adapt(): pl.pallas_call(functools.partial(adapt_kernel, count), in_specs=[pl.Block...  2.74 us
  transfers between devices with their start and end apart: 30, of which 5 were waited for; matrix products, arithmetic and copies ran while one was open for 0% of the time, Pallas kernels for 14%

profile of v22, /device:TPU:0, one launch (start us, length us, event | category | flops | bytes accessed | tf_op | source)
XLA Modules:
  0.0 86.7 jit_solution(4938849581345875359)
XLA Ops:
  0.0 3.9 %pack.2 = (bf16[32,128]{1,0:T(8,128)(2,1)}, bf16[8,8320]{1,0:T(8,128)(2,1)}, bf16[8,8320]{1,0:T(8,128)(2,1)}, bf16[8,8320]{1,0:T(8,128)(2,1)}, bf16[8,8320]{1,0:T(8,128)(2,1)}) custom-call(s32[1,32]{1,0:T(1,128)} %bitcast.2, s32[1,128]{1,0:T(1,128)} %bitcast.4, bf16[128,8192]{1,0:T(8,128)(2,1)} %hidden_hbm.3), custom_call_target="tpu_custom_call" | custom-call | tf_op jit(solution)/shard_map/pack/pallas_call | solution.py:96
  3.9 4.1 %collective-permute-start = (bf16[8,8320]{1,0:T(8,128)(2,1)}, bf16[8,8320]{1,0:T(8,128)(2,1)S(1)}, u32[]{:S(2)}, u32[]{:S(2)}) collective-permute-start(bf16[8,8320]{1,0:T(8,128)(2,1)} %get-tuple-element.42), channel_id=1, source_target_pairs={{0,8},{1,9},{2,10},{3,11},{4,12},{5,13},{6,14},{7,15},{8,0},{9,1},... | collective-permute-start | bytes 399368 | tf_op jit(solution)/shard_map/ppermute | solution.py:351
  8.0 1.6 %collective-permute-start.1 = (bf16[8,8320]{1,0:T(8,128)(2,1)}, bf16[8,8320]{1,0:T(8,128)(2,1)S(1)}, u32[]{:S(2)}, u32[]{:S(2)}) collective-permute-start(bf16[8,8320]{1,0:T(8,128)(2,1)} %get-tuple-element.43), channel_id=1, source_target_pairs={{0,4},{1,5},{2,6},{3,7},{4,0},{5,1},{6,2},{7,3},{8,12},{9,13},{10,... | collective-permute-start | bytes 399368 | tf_op jit(solution)/shard_map/ppermute | solution.py:351
  9.5 0.2 collective-permute-start.3
  9.8 4.5 %pack.3 = (bf16[96,128]{1,0:T(8,128)(2,1)}, bf16[8,8320]{1,0:T(8,128)(2,1)}, bf16[8,8320]{1,0:T(8,128)(2,1)}, bf16[8,8320]{1,0:T(8,128)(2,1)}, bf16[8,8320]{1,0:...) custom-call(s32[1,32]{1,0:T(1,128)} %bitcast.3, ...), custom_call_target="tpu_custom_call" | custom-call | tf_op jit(solution)/shard_map/pack/pallas_call | solution.py:96
  14.3 3.8 %collective-permute-start.8 = (bf16[8,8320]{1,0:T(8,128)(2,1)}, bf16[8,8320]{1,0:T(8,128)(2,1)S(1)}, u32[]{:S(2)}, u32[]{:S(2)}) collective-permute-start(bf16[8,8320]{1,0:T(8,128)(2,1)} %get-tuple-element.50), channel_id=1, source_target_pairs={{0,10},{1,11},{2,8},{3,9},{4,14},{5,15},{6,12},{7,13},{8,2},{9,3},... | collective-permute-start | bytes 399368 | tf_op jit(solution)/shard_map/ppermute | solution.py:351
  18.1 0.0 collective-permute-done.refs_0_
  18.1 1.6 %collective-permute-start.9 = (bf16[8,8320]{1,0:T(8,128)(2,1)}, bf16[8,8320]{1,0:T(8,128)(2,1)S(1)}, u32[]{:S(2)}, u32[]{:S(2)}) collective-permute-start(bf16[8,8320]{1,0:T(8,128)(2,1)} %get-tuple-element.51), channel_id=1, source_target_pairs={{0,6},{1,7},{2,4},{3,5},{4,2},{5,3},{6,0},{7,1},{8,14},{9,15},{10,... | collective-permute-start | bytes 399368 | tf_op jit(solution)/shard_map/ppermute | solution.py:351
  19.7 0.4 collective-permute-start.10
  20.0 0.0 collective-permute-done.2.refs_2_
  20.0 2.2 %collective-permute-start.11 = (bf16[8,8320]{1,0:T(8,128)(2,1)}, bf16[8,8320]{1,0:T(8,128)(2,1)S(1)}, u32[]{:S(2)}, u32[]{:S(2)}) collective-permute-start(bf16[8,8320]{1,0:T(8,128)(2,1)} %get-tuple-element.53), channel_id=1, source_target_pairs={{0,7},{1,6},{2,5},{3,4},{4,3},{5,2},{6,1},{7,0},{8,15},{9,14},{10,... | collective-permute-start | bytes 399368 | tf_op jit(solution)/shard_map/ppermute | solution.py:351
  22.2 0.0 collective-permute-done.3.refs_3_
  22.2 2.6 %collective-permute-start.16 = (bf16[8,8320]{1,0:T(8,128)(2,1)}, bf16[8,8320]{1,0:T(8,128)(2,1)S(1)}, u32[]{:S(2)}, u32[]{:S(2)}) collective-permute-start(bf16[8,8320]{1,0:T(8,128)(2,1)} %get-tuple-element.58), channel_id=1, source_target_pairs={{0,12},{1,13},{2,14},{3,15},{4,8},{5,9},{6,10},{7,11},{8,4},{9,5},... | collective-permute-start | bytes 399368 | tf_op jit(solution)/shard_map/ppermute | solution.py:351
  24.8 3.8 %collective-permute-done.8.refs_0_ = bf16[8,8320]{1,0:T(8,128)(2,1)S(1)} collective-permute-done((bf16[8,8320]{1,0:T(8,128)(2,1)}, bf16[8,8320]{1,0:T(8,128)(2,1)S(1)}, u32[]{:S(2)}, u32[]{:S(2)}) %collective-permute-start.8) | collective-permute-done | bytes 133152 | tf_op jit(solution)/shard_map/ppermute | solution.py:351
  28.5 0.1 broadcast_in_dim.7
  28.6 0.1 broadcast_in_dim.8
  28.7 0.1 broadcast_in_dim.9.given_ref
  28.9 5.1 %prep.1 = (bf16[4,128,2048]{2,1,0:T(8,128)(2,1)S(1)}, bf16[4,92,192,128]{3,2,1,0:T(8,128)(2,1)}, s32[16,1,128]{2,1,0:T(1,128)S(1)}) custom-call(bf16[128,4096]{1,0:T(8,128)(2,1)S(1)} %copy-done.2, bf16[128,2,16,512]{3,2,1,0:T(8,128)(2,1)} %kv_ref.1, s32[16,1,128]{2,1,0:T(1,128)S(1)} %broadcast_in_dim.9.given_ref), custom_call_target="tpu_custom_call" | custom-call | tf_op jit(solution)/shard_map/prep/pallas_call | solution.py:184
  34.0 3.3 %collective-permute-start.18 = (bf16[8,8320]{1,0:T(8,128)(2,1)S(1)}, bf16[8,8320]{1,0:T(8,128)(2,1)S(1)}, u32[]{:S(2)}, u32[]{:S(2)}) collective-permute-start(bf16[8,8320]{1,0:T(8,128)(2,1)S(1)} %copy-done.11), channel_id=1, source_target_pairs={{0,13},{1,12},{2,15},{3,14},{4,9},{5,8},{6,11},{7,10},{8,5},{9,4},... | collective-permute-start | bytes 399368 | tf_op jit(solution)/shard_map/ppermute | solution.py:351
  37.3 0.0 collective-permute-done.10.refs_2_
  37.3 0.5 collective-permute-start.19
  37.8 0.0 collective-permute-done.11.refs_3_
  37.8 1.6 %collective-permute-start.24 = (bf16[8,8320]{1,0:T(8,128)(2,1)S(1)}, bf16[8,8320]{1,0:T(8,128)(2,1)S(1)}, u32[]{:S(2)}, u32[]{:S(2)}) collective-permute-start(bf16[8,8320]{1,0:T(8,128)(2,1)S(1)} %copy-done.9), channel_id=1, source_target_pairs={{0,14},{1,15},{2,12},{3,13},{4,10},{5,11},{6,8},{7,9},{8,6},{9,7},... | collective-permute-start | bytes 399368 | tf_op jit(solution)/shard_map/ppermute | solution.py:351
  39.4 0.0 collective-permute-done.16.refs_0_
  39.4 2.2 %collective-permute-start.26 = (bf16[8,8320]{1,0:T(8,128)(2,1)S(1)}, bf16[8,8320]{1,0:T(8,128)(2,1)S(1)}, u32[]{:S(2)}, u32[]{:S(2)}) collective-permute-start(bf16[8,8320]{1,0:T(8,128)(2,1)S(1)} %copy-done.8), channel_id=1, source_target_pairs={{0,15},{1,14},{2,13},{3,12},{4,11},{5,10},{6,9},{7,8},{8,7},{9,6},... | collective-permute-start | bytes 399368 | tf_op jit(solution)/shard_map/ppermute | solution.py:351
  41.6 2.2 %collective-permute-start.25 = (bf16[8,8320]{1,0:T(8,128)(2,1)S(1)}, bf16[8,8320]{1,0:T(8,128)(2,1)S(1)}, u32[]{:S(2)}, u32[]{:S(2)}) collective-permute-start(bf16[8,8320]{1,0:T(8,128)(2,1)S(1)} %hold.1), channel_id=1, source_target_pairs={{0,3},{1,2},{2,1},{3,0},{4,7},{5,6},{6,5},{7,4},{8,11},{9,10},{10,... | collective-permute-start | bytes 399368 | tf_op jit(solution)/shard_map/ppermute | solution.py:351
  43.9 0.7 adapt.4
  44.6 0.7 adapt.5
  45.2 0.0 collective-permute-done.18.refs_2_
  45.3 6.1 %collective-permute-start.4 = (bf16[8,4096]{1,0:T(8,128)(2,1)S(1)}, bf16[8,4096]{1,0:T(8,128)(2,1)S(1)}, u32[]{:S(2)}, u32[]{:S(2)}) collective-permute-start(bf16[8,4096]{1,0:T(8,128)(2,1)S(1)} %get-tuple-element.46), channel_id=1, source_target_pairs={{0,8},{1,9},{2,10},{3,11},{4,12},{5,13},{6,14},{7,15},{8,0},{9,1},... | collective-permute-start | bytes 196616 | tf_op jit(solution)/shard_map/ppermute | solution.py:351
  51.4 0.0 collective-permute-done.19.refs_3_
  51.4 3.4 %collective-permute-start.6 = (bf16[8,4096]{1,0:T(8,128)(2,1)S(1)}, bf16[8,4096]{1,0:T(8,128)(2,1)S(1)}, u32[]{:S(2)}, u32[]{:S(2)}) collective-permute-start(bf16[8,4096]{1,0:T(8,128)(2,1)S(1)} %get-tuple-element.48), channel_id=1, source_target_pairs={{0,9},{1,8},{2,11},{3,10},{4,13},{5,12},{6,15},{7,14},{8,1},{9,0},... | collective-permute-start | bytes 196616 | tf_op jit(solution)/shard_map/ppermute | solution.py:351
  54.8 4.2 %collective-permute-start.7 = (bf16[8,4096]{1,0:T(8,128)(2,1)S(1)}, bf16[8,4096]{1,0:T(8,128)(2,1)S(1)}, u32[]{:S(2)}, u32[]{:S(2)}) collective-permute-start(bf16[8,4096]{1,0:T(8,128)(2,1)S(1)} %get-tuple-element.49), channel_id=1, source_target_pairs={{0,5},{1,4},{2,7},{3,6},{4,1},{5,0},{6,3},{7,2},{8,13},{9,12},{10,... | collective-permute-start | bytes 196616 | tf_op jit(solution)/shard_map/ppermute | solution.py:351
  59.1 0.4 collective-permute-start.12
  59.4 0.7 adapt.6
  60.1 4.1 %collective-permute-start.13 = (bf16[8,4096]{1,0:T(8,128)(2,1)S(1)}, bf16[8,4096]{1,0:T(8,128)(2,1)S(1)}, u32[]{:S(2)}, u32[]{:S(2)}) collective-permute-start(bf16[8,4096]{1,0:T(8,128)(2,1)S(1)} %get-tuple-element.55), channel_id=1, source_target_pairs={{0,6},{1,7},{2,4},{3,5},{4,2},{5,3},{6,0},{7,1},{8,14},{9,15},{10,... | collective-permute-start | bytes 196616 | tf_op jit(solution)/shard_map/ppermute | solution.py:351
  64.2 2.1 %collective-permute-start.15 = (bf16[8,4096]{1,0:T(8,128)(2,1)S(1)}, bf16[8,4096]{1,0:T(8,128)(2,1)S(1)}, u32[]{:S(2)}, u32[]{:S(2)}) collective-permute-start(bf16[8,4096]{1,0:T(8,128)(2,1)S(1)} %get-tuple-element.57), channel_id=1, source_target_pairs={{0,7},{1,6},{2,5},{3,4},{4,3},{5,2},{6,1},{7,0},{8,15},{9,14},{10,... | collective-permute-start | bytes 196616 | tf_op jit(solution)/shard_map/ppermute | solution.py:351
  66.3 2.9 %collective-permute-start.20 = (bf16[8,4096]{1,0:T(8,128)(2,1)S(1)}, bf16[8,4096]{1,0:T(8,128)(2,1)S(1)}, u32[]{:S(2)}, u32[]{:S(2)}) collective-permute-start(bf16[8,4096]{1,0:T(8,128)(2,1)S(1)} %get-tuple-element.62), channel_id=1, source_target_pairs={{0,12},{1,13},{2,14},{3,15},{4,8},{5,9},{6,10},{7,11},{8,4},{9,5},... | collective-permute-start | bytes 196616 | tf_op jit(solution)/shard_map/ppermute | solution.py:351
  69.2 0.7 adapt.7
  69.9 1.1 %collective-permute-start.22 = (bf16[8,4096]{1,0:T(8,128)(2,1)S(1)}, bf16[8,4096]{1,0:T(8,128)(2,1)S(1)}, u32[]{:S(2)}, u32[]{:S(2)}) collective-permute-start(bf16[8,4096]{1,0:T(8,128)(2,1)S(1)} %get-tuple-element.64), channel_id=1, source_target_pairs={{0,13},{1,12},{2,15},{3,14},{4,9},{5,8},{6,11},{7,10},{8,5},{9,4},... | collective-permute-start | bytes 196616 | tf_op jit(solution)/shard_map/ppermute | solution.py:351
  71.0 0.3 collective-permute-done.14.refs_6_
  71.3 0.4 collective-permute-start.23
  71.6 3.8 %collective-permute-start.27 = (bf16[8,4096]{1,0:T(8,128)(2,1)S(1)}, bf16[8,4096]{1,0:T(8,128)(2,1)S(1)}, u32[]{:S(2)}, u32[]{:S(2)}) collective-permute-start(bf16[8,4096]{1,0:T(8,128)(2,1)S(1)} %get-tuple-element.71), channel_id=1, source_target_pairs={{0,14},{1,15},{2,12},{3,13},{4,10},{5,11},{6,8},{7,9},{8,6},{9,7},... | collective-permute-start | bytes 196616 | tf_op jit(solution)/shard_map/ppermute | solution.py:351
  75.4 2.3 %collective-permute-start.29 = (bf16[8,4096]{1,0:T(8,128)(2,1)S(1)}, bf16[8,4096]{1,0:T(8,128)(2,1)S(1)}, u32[]{:S(2)}, u32[]{:S(2)}) collective-permute-start(bf16[8,4096]{1,0:T(8,128)(2,1)S(1)} %get-tuple-element.73), channel_id=1, source_target_pairs={{0,15},{1,14},{2,13},{3,12},{4,11},{5,10},{6,9},{7,8},{8,7},{9,6},... | collective-permute-start | bytes 196616 | tf_op jit(solution)/shard_map/ppermute | solution.py:351
  77.8 0.9 %collective-permute-done.27.refs_12_ = bf16[8,4096]{1,0:T(8,128)(2,1)S(1)} collective-permute-done((bf16[8,4096]{1,0:T(8,128)(2,1)S(1)}, bf16[8,4096]{1,0:T(8,128)(2,1)S(1)}, u32[]{:S(2)}, u32[]{:S(2)}) %collective-permute-start.27) | collective-permute-done | bytes 65568 | tf_op jit(solution)/shard_map/ppermute | solution.py:351
  78.7 1.3 %collective-permute-done.28.refs_13_ = bf16[8,4096]{1,0:T(8,128)(2,1)S(1)} collective-permute-done((bf16[8,4096]{1,0:T(8,128)(2,1)S(1)}, bf16[8,4096]{1,0:T(8,128)(2,1)S(1)}, u32[]{:S(2)}, u32[]{:S(2)}) %collective-permute-start.28) | collective-permute-done | bytes 65568 | tf_op jit(solution)/shard_map/ppermute | solution.py:351
  80.0 2.3 %collective-permute-done.29.refs_14_ = bf16[8,4096]{1,0:T(8,128)(2,1)S(1)} collective-permute-done((bf16[8,4096]{1,0:T(8,128)(2,1)S(1)}, bf16[8,4096]{1,0:T(8,128)(2,1)S(1)}, u32[]{:S(2)}, u32[]{:S(2)}) %collective-permute-start.29) | collective-permute-done | bytes 65568 | tf_op jit(solution)/shard_map/ppermute | solution.py:351
  82.3 4.4 %attend.1 = bf16[128,4096]{1,0:T(8,128)(2,1)} custom-call(bf16[8,4096]{1,0:T(8,128)(2,1)S(1)} %collective-permute-done.4.refs_0_, bf16[8,4096]{1,0:T(8,128)(2,1)S(1)} %collective-permute-done.5.refs_1_, bf16[8,4096]{1,0:T(8,128)(2,1)S(1)} %collective-permute-done.6.refs_2_, bf16[8,4096]{1,0:T(8,128)(2,1)S(1)} %collective-permute-done.7.refs_3_, ...), custom_call_target="tpu_custom_call" | custom-call | tf_op jit(solution)/shard_map/attend/pallas_call | solution.py:304
  (48 shorter events, 0.1 us)
Async XLA Ops:
  0.0 28.5 %copy-start.7 = (s32[128]{0:T(128)S(1)}, s32[128]{0:T(128)}, u32[]{:S(2)}) copy-start(s32[128]{0:T(128)} %param.11) | copy-start | bytes 1540
  0.0 28.8 %copy-start.2 = (bf16[128,4096]{1,0:T(8,128)(2,1)S(1)}, bf16[128,4096]{1,0:T(8,128)(2,1)}, u32[]{:S(2)}) copy-start(bf16[128,4096]{1,0:T(8,128)(2,1)} %base_ref.1) | copy-start | bytes 3145732
  3.9 14.2 %collective-permute-start = (bf16[8,8320]{1,0:T(8,128)(2,1)}, bf16[8,8320]{1,0:T(8,128)(2,1)S(1)}, u32[]{:S(2)}, u32[]{:S(2)}) collective-permute-start(bf16[8,8320]{1,0:T(8,128)(2,1)} %get-tuple-element.42), channel_id=1, source_target_pairs={{0,8},{1,9},{2,10},{3,11},{4,12},{5,13},{6,14},{7,15},{8,0},{9,1},... | collective-permute-start | bytes 399368 | tf_op jit(solution)/shard_map/ppermute | solution.py:351
  8.0 11.7 %collective-permute-start.1 = (bf16[8,8320]{1,0:T(8,128)(2,1)}, bf16[8,8320]{1,0:T(8,128)(2,1)S(1)}, u32[]{:S(2)}, u32[]{:S(2)}) collective-permute-start(bf16[8,8320]{1,0:T(8,128)(2,1)} %get-tuple-element.43), channel_id=1, source_target_pairs={{0,4},{1,5},{2,6},{3,7},{4,0},{5,1},{6,2},{7,3},{8,12},{9,13},{10,... | collective-permute-start | bytes 399368 | tf_op jit(solution)/shard_map/ppermute | solution.py:351
  9.5 10.5 %collective-permute-start.2 = (bf16[8,8320]{1,0:T(8,128)(2,1)}, bf16[8,8320]{1,0:T(8,128)(2,1)S(1)}, u32[]{:S(2)}, u32[]{:S(2)}) collective-permute-start(bf16[8,8320]{1,0:T(8,128)(2,1)} %get-tuple-element.44), channel_id=1, source_target_pairs={{0,9},{1,8},{2,11},{3,10},{4,13},{5,12},{6,15},{7,14},{8,1},{9,0},... | collective-permute-start | bytes 399368 | tf_op jit(solution)/shard_map/ppermute | solution.py:351
  9.5 12.7 %collective-permute-start.3 = (bf16[8,8320]{1,0:T(8,128)(2,1)}, bf16[8,8320]{1,0:T(8,128)(2,1)S(1)}, u32[]{:S(2)}, u32[]{:S(2)}) collective-permute-start(bf16[8,8320]{1,0:T(8,128)(2,1)} %get-tuple-element.45), channel_id=1, source_target_pairs={{0,5},{1,4},{2,7},{3,6},{4,1},{5,0},{6,3},{7,2},{8,13},{9,12},{10,... | collective-permute-start | bytes 399368 | tf_op jit(solution)/shard_map/ppermute | solution.py:351
  14.3 14.3 %collective-permute-start.8 = (bf16[8,8320]{1,0:T(8,128)(2,1)}, bf16[8,8320]{1,0:T(8,128)(2,1)S(1)}, u32[]{:S(2)}, u32[]{:S(2)}) collective-permute-start(bf16[8,8320]{1,0:T(8,128)(2,1)} %get-tuple-element.50), channel_id=1, source_target_pairs={{0,10},{1,11},{2,8},{3,9},{4,14},{5,15},{6,12},{7,13},{8,2},{9,3},... | collective-permute-start | bytes 399368 | tf_op jit(solution)/shard_map/ppermute | solution.py:351
  18.1 15.9 %collective-permute-start.9 = (bf16[8,8320]{1,0:T(8,128)(2,1)}, bf16[8,8320]{1,0:T(8,128)(2,1)S(1)}, u32[]{:S(2)}, u32[]{:S(2)}) collective-permute-start(bf16[8,8320]{1,0:T(8,128)(2,1)} %get-tuple-element.51), channel_id=1, source_target_pairs={{0,6},{1,7},{2,4},{3,5},{4,2},{5,3},{6,0},{7,1},{8,14},{9,15},{10,... | collective-permute-start | bytes 399368 | tf_op jit(solution)/shard_map/ppermute | solution.py:351
  19.7 17.6 %collective-permute-start.10 = (bf16[8,8320]{1,0:T(8,128)(2,1)}, bf16[8,8320]{1,0:T(8,128)(2,1)S(1)}, u32[]{:S(2)}, u32[]{:S(2)}) collective-permute-start(bf16[8,8320]{1,0:T(8,128)(2,1)} %get-tuple-element.52), channel_id=1, source_target_pairs={{0,11},{1,10},{2,9},{3,8},{4,15},{5,14},{6,13},{7,12},{8,3},{9,2},... | collective-permute-start | bytes 399368 | tf_op jit(solution)/shard_map/ppermute | solution.py:351
  20.0 17.8 %collective-permute-start.11 = (bf16[8,8320]{1,0:T(8,128)(2,1)}, bf16[8,8320]{1,0:T(8,128)(2,1)S(1)}, u32[]{:S(2)}, u32[]{:S(2)}) collective-permute-start(bf16[8,8320]{1,0:T(8,128)(2,1)} %get-tuple-element.53), channel_id=1, source_target_pairs={{0,7},{1,6},{2,5},{3,4},{4,3},{5,2},{6,1},{7,0},{8,15},{9,14},{10,... | collective-permute-start | bytes 399368 | tf_op jit(solution)/shard_map/ppermute | solution.py:351
  22.2 17.2 %collective-permute-start.16 = (bf16[8,8320]{1,0:T(8,128)(2,1)}, bf16[8,8320]{1,0:T(8,128)(2,1)S(1)}, u32[]{:S(2)}, u32[]{:S(2)}) collective-permute-start(bf16[8,8320]{1,0:T(8,128)(2,1)} %get-tuple-element.58), channel_id=1, source_target_pairs={{0,12},{1,13},{2,14},{3,15},{4,8},{5,9},{6,10},{7,11},{8,4},{9,5},... | collective-permute-start | bytes 399368 | tf_op jit(solution)/shard_map/ppermute | solution.py:351
  28.5 13.1 %collective-permute-start.17 = (bf16[8,8320]{1,0:T(8,128)(2,1)}, bf16[8,8320]{1,0:T(8,128)(2,1)S(1)}, u32[]{:S(2)}, u32[]{:S(2)}) collective-permute-start(bf16[8,8320]{1,0:T(8,128)(2,1)} %get-tuple-element.59), channel_id=1, source_target_pairs={{0,1},{1,0},{2,3},{3,2},{4,5},{5,4},{6,7},{7,6},{8,9},{9,8},{10,11... | collective-permute-start | bytes 399368 | tf_op jit(solution)/shard_map/ppermute | solution.py:351
  28.8 5.2 %copy-start.11 = (bf16[8,8320]{1,0:T(8,128)(2,1)S(1)}, bf16[8,8320]{1,0:T(8,128)(2,1)}, u32[]{:S(2)}) copy-start(bf16[8,8320]{1,0:T(8,128)(2,1)} %get-tuple-element.60) | copy-start | bytes 399364
  28.8 8.5 %copy-start.10 = (bf16[8,8320]{1,0:T(8,128)(2,1)S(1)}, bf16[8,8320]{1,0:T(8,128)(2,1)}, u32[]{:S(2)}) copy-start(bf16[8,8320]{1,0:T(8,128)(2,1)} %get-tuple-element.61) | copy-start | bytes 399364
  28.8 9.0 %copy-start.9 = (bf16[8,8320]{1,0:T(8,128)(2,1)S(1)}, bf16[8,8320]{1,0:T(8,128)(2,1)}, u32[]{:S(2)}) copy-start(bf16[8,8320]{1,0:T(8,128)(2,1)} %get-tuple-element.66) | copy-start | bytes 399364
  28.9 10.6 %copy-start.8 = (bf16[8,8320]{1,0:T(8,128)(2,1)S(1)}, bf16[8,8320]{1,0:T(8,128)(2,1)}, u32[]{:S(2)}) copy-start(bf16[8,8320]{1,0:T(8,128)(2,1)} %get-tuple-element.69) | copy-start | bytes 399364
  28.9 12.8 %copy-start.4 = (bf16[8,8320]{1,0:T(8,128)(2,1)S(1)}, bf16[8,8320]{1,0:T(8,128)(2,1)}, u32[]{:S(2)}) copy-start(bf16[8,8320]{1,0:T(8,128)(2,1)} %get-tuple-element.67.refs_0_) | copy-start | bytes 399364
  34.0 11.2 %collective-permute-start.18 = (bf16[8,8320]{1,0:T(8,128)(2,1)S(1)}, bf16[8,8320]{1,0:T(8,128)(2,1)S(1)}, u32[]{:S(2)}, u32[]{:S(2)}) collective-permute-start(bf16[8,8320]{1,0:T(8,128)(2,1)S(1)} %copy-done.11), channel_id=1, source_target_pairs={{0,13},{1,12},{2,15},{3,14},{4,9},{5,8},{6,11},{7,10},{8,5},{9,4},... | collective-permute-start | bytes 399368 | tf_op jit(solution)/shard_map/ppermute | solution.py:351
  37.3 14.1 %collective-permute-start.19 = (bf16[8,8320]{1,0:T(8,128)(2,1)S(1)}, bf16[8,8320]{1,0:T(8,128)(2,1)S(1)}, u32[]{:S(2)}, u32[]{:S(2)}) collective-permute-start(bf16[8,8320]{1,0:T(8,128)(2,1)S(1)} %copy-done.10), channel_id=1, source_target_pairs={{0,2},{1,3},{2,0},{3,1},{4,6},{5,7},{6,4},{7,5},{8,10},{9,11},{10,... | collective-permute-start | bytes 399368 | tf_op jit(solution)/shard_map/ppermute | solution.py:351
  37.8 13.6 %collective-permute-start.24 = (bf16[8,8320]{1,0:T(8,128)(2,1)S(1)}, bf16[8,8320]{1,0:T(8,128)(2,1)S(1)}, u32[]{:S(2)}, u32[]{:S(2)}) collective-permute-start(bf16[8,8320]{1,0:T(8,128)(2,1)S(1)} %copy-done.9), channel_id=1, source_target_pairs={{0,14},{1,15},{2,12},{3,13},{4,10},{5,11},{6,8},{7,9},{8,6},{9,7},... | collective-permute-start | bytes 399368 | tf_op jit(solution)/shard_map/ppermute | solution.py:351
  39.4 15.4 %collective-permute-start.26 = (bf16[8,8320]{1,0:T(8,128)(2,1)S(1)}, bf16[8,8320]{1,0:T(8,128)(2,1)S(1)}, u32[]{:S(2)}, u32[]{:S(2)}) collective-permute-start(bf16[8,8320]{1,0:T(8,128)(2,1)S(1)} %copy-done.8), channel_id=1, source_target_pairs={{0,15},{1,14},{2,13},{3,12},{4,11},{5,10},{6,9},{7,8},{8,7},{9,6},... | collective-permute-start | bytes 399368 | tf_op jit(solution)/shard_map/ppermute | solution.py:351
  41.6 2.2 %copy-start = (bf16[8192,128]{1,0:T(8,128)(2,1)S(1)}, bf16[8192,128]{1,0:T(8,128)(2,1)}, u32[]{:S(2)}) copy-start(bf16[8192,128]{1,0:T(8,128)(2,1)} %refs_4_.7) | copy-start | bytes 6291460
  41.6 2.2 %copy-start.1 = (bf16[128,4096]{1,0:T(8,128)(2,1)S(1)}, bf16[128,4096]{1,0:T(8,128)(2,1)}, u32[]{:S(2)}) copy-start(bf16[128,4096]{1,0:T(8,128)(2,1)} %refs_5_.7) | copy-start | bytes 3145732
  41.6 17.4 %collective-permute-start.25 = (bf16[8,8320]{1,0:T(8,128)(2,1)S(1)}, bf16[8,8320]{1,0:T(8,128)(2,1)S(1)}, u32[]{:S(2)}, u32[]{:S(2)}) collective-permute-start(bf16[8,8320]{1,0:T(8,128)(2,1)S(1)} %hold.1), channel_id=1, source_target_pairs={{0,3},{1,2},{2,1},{3,0},{4,7},{5,6},{6,5},{7,4},{8,11},{9,10},{10,... | collective-permute-start | bytes 399368 | tf_op jit(solution)/shard_map/ppermute | solution.py:351
  45.2 24.0 %copy-start.3 = (bf16[8,8320]{1,0:T(8,128)(2,1)S(1)}, bf16[8,8320]{1,0:T(8,128)(2,1)}, u32[]{:S(2)}) copy-start(bf16[8,8320]{1,0:T(8,128)(2,1)} %get-tuple-element.70.refs_3_) | copy-start | bytes 399364
  45.3 14.9 %collective-permute-start.4 = (bf16[8,4096]{1,0:T(8,128)(2,1)S(1)}, bf16[8,4096]{1,0:T(8,128)(2,1)S(1)}, u32[]{:S(2)}, u32[]{:S(2)}) collective-permute-start(bf16[8,4096]{1,0:T(8,128)(2,1)S(1)} %get-tuple-element.46), channel_id=1, source_target_pairs={{0,8},{1,9},{2,10},{3,11},{4,12},{5,13},{6,14},{7,15},{8,0},{9,1},... | collective-permute-start | bytes 196616 | tf_op jit(solution)/shard_map/ppermute | solution.py:351
  51.4 12.8 %collective-permute-start.5 = (bf16[8,4096]{1,0:T(8,128)(2,1)S(1)}, bf16[8,4096]{1,0:T(8,128)(2,1)S(1)}, u32[]{:S(2)}, u32[]{:S(2)}) collective-permute-start(bf16[8,4096]{1,0:T(8,128)(2,1)S(1)} %get-tuple-element.47), channel_id=1, source_target_pairs={{0,4},{1,5},{2,6},{3,7},{4,0},{5,1},{6,2},{7,3},{8,12},{9,13},{10,... | collective-permute-start | bytes 196616 | tf_op jit(solution)/shard_map/ppermute | solution.py:351
  51.4 12.8 %collective-permute-start.6 = (bf16[8,4096]{1,0:T(8,128)(2,1)S(1)}, bf16[8,4096]{1,0:T(8,128)(2,1)S(1)}, u32[]{:S(2)}, u32[]{:S(2)}) collective-permute-start(bf16[8,4096]{1,0:T(8,128)(2,1)S(1)} %get-tuple-element.48), channel_id=1, source_target_pairs={{0,9},{1,8},{2,11},{3,10},{4,13},{5,12},{6,15},{7,14},{8,1},{9,0},... | collective-permute-start | bytes 196616 | tf_op jit(solution)/shard_map/ppermute | solution.py:351
  54.8 11.5 %collective-permute-start.7 = (bf16[8,4096]{1,0:T(8,128)(2,1)S(1)}, bf16[8,4096]{1,0:T(8,128)(2,1)S(1)}, u32[]{:S(2)}, u32[]{:S(2)}) collective-permute-start(bf16[8,4096]{1,0:T(8,128)(2,1)S(1)} %get-tuple-element.49), channel_id=1, source_target_pairs={{0,5},{1,4},{2,7},{3,6},{4,1},{5,0},{6,3},{7,2},{8,13},{9,12},{10,... | collective-permute-start | bytes 196616 | tf_op jit(solution)/shard_map/ppermute | solution.py:351
  59.1 10.2 %collective-permute-start.12 = (bf16[8,4096]{1,0:T(8,128)(2,1)S(1)}, bf16[8,4096]{1,0:T(8,128)(2,1)S(1)}, u32[]{:S(2)}, u32[]{:S(2)}) collective-permute-start(bf16[8,4096]{1,0:T(8,128)(2,1)S(1)} %get-tuple-element.54), channel_id=1, source_target_pairs={{0,10},{1,11},{2,8},{3,9},{4,14},{5,15},{6,12},{7,13},{8,2},{9,3},... | collective-permute-start | bytes 196616 | tf_op jit(solution)/shard_map/ppermute | solution.py:351
  60.1 22.2 %copy-start.5 = (bf16[96,128]{1,0:T(8,128)(2,1)S(1)}, bf16[96,128]{1,0:T(8,128)(2,1)}, u32[]{:S(2)}) copy-start(bf16[96,128]{1,0:T(8,128)(2,1)} %get-tuple-element.76.refs_17_) | copy-start | bytes 73732
  60.1 22.2 %copy-start.6 = (bf16[32,128]{1,0:T(8,128)(2,1)S(1)}, bf16[32,128]{1,0:T(8,128)(2,1)}, u32[]{:S(2)}) copy-start(bf16[32,128]{1,0:T(8,128)(2,1)} %get-tuple-element.75.refs_16_) | copy-start | bytes 24580
  60.1 9.8 %collective-permute-start.13 = (bf16[8,4096]{1,0:T(8,128)(2,1)S(1)}, bf16[8,4096]{1,0:T(8,128)(2,1)S(1)}, u32[]{:S(2)}, u32[]{:S(2)}) collective-permute-start(bf16[8,4096]{1,0:T(8,128)(2,1)S(1)} %get-tuple-element.55), channel_id=1, source_target_pairs={{0,6},{1,7},{2,4},{3,5},{4,2},{5,3},{6,0},{7,1},{8,14},{9,15},{10,... | collective-permute-start | bytes 196616 | tf_op jit(solution)/shard_map/ppermute | solution.py:351
  64.2 7.1 %collective-permute-start.14 = (bf16[8,4096]{1,0:T(8,128)(2,1)S(1)}, bf16[8,4096]{1,0:T(8,128)(2,1)S(1)}, u32[]{:S(2)}, u32[]{:S(2)}) collective-permute-start(bf16[8,4096]{1,0:T(8,128)(2,1)S(1)} %get-tuple-element.56), channel_id=1, source_target_pairs={{0,11},{1,10},{2,9},{3,8},{4,15},{5,14},{6,13},{7,12},{8,3},{9,2},... | collective-permute-start | bytes 196616 | tf_op jit(solution)/shard_map/ppermute | solution.py:351
  64.2 7.4 %collective-permute-start.15 = (bf16[8,4096]{1,0:T(8,128)(2,1)S(1)}, bf16[8,4096]{1,0:T(8,128)(2,1)S(1)}, u32[]{:S(2)}, u32[]{:S(2)}) collective-permute-start(bf16[8,4096]{1,0:T(8,128)(2,1)S(1)} %get-tuple-element.57), channel_id=1, source_target_pairs={{0,7},{1,6},{2,5},{3,4},{4,3},{5,2},{6,1},{7,0},{8,15},{9,14},{10,... | collective-permute-start | bytes 196616 | tf_op jit(solution)/shard_map/ppermute | solution.py:351
  66.3 9.1 %collective-permute-start.20 = (bf16[8,4096]{1,0:T(8,128)(2,1)S(1)}, bf16[8,4096]{1,0:T(8,128)(2,1)S(1)}, u32[]{:S(2)}, u32[]{:S(2)}) collective-permute-start(bf16[8,4096]{1,0:T(8,128)(2,1)S(1)} %get-tuple-element.62), channel_id=1, source_target_pairs={{0,12},{1,13},{2,14},{3,15},{4,8},{5,9},{6,10},{7,11},{8,4},{9,5},... | collective-permute-start | bytes 196616 | tf_op jit(solution)/shard_map/ppermute | solution.py:351
  69.2 6.2 %collective-permute-start.21 = (bf16[8,4096]{1,0:T(8,128)(2,1)S(1)}, bf16[8,4096]{1,0:T(8,128)(2,1)S(1)}, u32[]{:S(2)}, u32[]{:S(2)}) collective-permute-start(bf16[8,4096]{1,0:T(8,128)(2,1)S(1)} %get-tuple-element.63), channel_id=1, source_target_pairs={{0,1},{1,0},{2,3},{3,2},{4,5},{5,4},{6,7},{7,6},{8,9},{9,8},{10,11... | collective-permute-start | bytes 196616 | tf_op jit(solution)/shard_map/ppermute | solution.py:351
  69.9 7.8 %collective-permute-start.22 = (bf16[8,4096]{1,0:T(8,128)(2,1)S(1)}, bf16[8,4096]{1,0:T(8,128)(2,1)S(1)}, u32[]{:S(2)}, u32[]{:S(2)}) collective-permute-start(bf16[8,4096]{1,0:T(8,128)(2,1)S(1)} %get-tuple-element.64), channel_id=1, source_target_pairs={{0,13},{1,12},{2,15},{3,14},{4,9},{5,8},{6,11},{7,10},{8,5},{9,4},... | collective-permute-start | bytes 196616 | tf_op jit(solution)/shard_map/ppermute | solution.py:351
  71.3 6.5 %collective-permute-start.23 = (bf16[8,4096]{1,0:T(8,128)(2,1)S(1)}, bf16[8,4096]{1,0:T(8,128)(2,1)S(1)}, u32[]{:S(2)}, u32[]{:S(2)}) collective-permute-start(bf16[8,4096]{1,0:T(8,128)(2,1)S(1)} %get-tuple-element.65), channel_id=1, source_target_pairs={{0,2},{1,3},{2,0},{3,1},{4,6},{5,7},{6,4},{7,5},{8,10},{9,11},{10,... | collective-permute-start | bytes 196616 | tf_op jit(solution)/shard_map/ppermute | solution.py:351
  71.6 7.0 %collective-permute-start.27 = (bf16[8,4096]{1,0:T(8,128)(2,1)S(1)}, bf16[8,4096]{1,0:T(8,128)(2,1)S(1)}, u32[]{:S(2)}, u32[]{:S(2)}) collective-permute-start(bf16[8,4096]{1,0:T(8,128)(2,1)S(1)} %get-tuple-element.71), channel_id=1, source_target_pairs={{0,14},{1,15},{2,12},{3,13},{4,10},{5,11},{6,8},{7,9},{8,6},{9,7},... | collective-permute-start | bytes 196616 | tf_op jit(solution)/shard_map/ppermute | solution.py:351
  75.4 4.6 %collective-permute-start.28 = (bf16[8,4096]{1,0:T(8,128)(2,1)S(1)}, bf16[8,4096]{1,0:T(8,128)(2,1)S(1)}, u32[]{:S(2)}, u32[]{:S(2)}) collective-permute-start(bf16[8,4096]{1,0:T(8,128)(2,1)S(1)} %get-tuple-element.72), channel_id=1, source_target_pairs={{0,3},{1,2},{2,1},{3,0},{4,7},{5,6},{6,5},{7,4},{8,11},{9,10},{10,... | collective-permute-start | bytes 196616 | tf_op jit(solution)/shard_map/ppermute | solution.py:351
  75.4 6.9 %collective-permute-start.29 = (bf16[8,4096]{1,0:T(8,128)(2,1)S(1)}, bf16[8,4096]{1,0:T(8,128)(2,1)S(1)}, u32[]{:S(2)}, u32[]{:S(2)}) collective-permute-start(bf16[8,4096]{1,0:T(8,128)(2,1)S(1)} %get-tuple-element.73), channel_id=1, source_target_pairs={{0,15},{1,14},{2,13},{3,12},{4,11},{5,10},{6,9},{7,8},{8,7},{9,6},... | collective-permute-start | bytes 196616 | tf_op jit(solution)/shard_map/ppermute | solution.py:351

commit v23 on v22

--- a/solution.py
+++ b/solution.py
@@ -15,7 +15,7 @@
 ROWS_STEP = 8
 PREP_STEPS = 4
 GROUPS = 4
-HELD = 13
+LEAD = 3
 FIRST = 4
 MOST_PERMUTES = 32
 COLUMNS_STEP = 1024
@@ -327,15 +327,18 @@
     slot_count = max(2, 2 * ((rows + 2 * owners - 1) // (2 * owners)))
     half = owners // 2
     near = [*range(half // 2, half), *range(1, half // 2)]
-    order = [s for pair in zip(range(half, owners), [*near, 0]) for s in pair]
-
+    far = [*range(half, owners)]
+    order = far[:LEAD]
+    for i, s in enumerate(near):
+        order += [s, *far[LEAD + i : LEAD + i + 1]]
+    order.append(0)
     routed, messages = [], []
     for which in (order[:FIRST], order[FIRST:]):
         hits, *packed = pack(which, hidden, adapter_id, adapter_slot, owners, slot_count, held)
         routed.append(hits)
         messages += packed
     keys, rest, lens = prep(base_q, kv_cache, cache_len)
-    messages[HELD] = hold(messages[HELD], rest)
+    messages[-2] = hold(messages[-2], rest)
     size = owners // GROUPS
     arrived = exchange(order, owners)(messages)
     changes = []

time: 86.9 us -> 90.6 us (1.043)
  waiting for transfers between devices: 8.61 us -> 16.3 us
  starting transfers between devices: 57 us -> 51.5 us
  local copies, waits for them, and re-layouts: 0.31 us -> 1.8 us
    ppermute x30, waiting for transfers between devices: 8.61 us -> 16.3 us  [permutes(): lax.ppermute(message, 'owner', [(i, i ^ s) for i in range(owners)])]
    ppermute x30, starting transfers between devices: 57 us -> 51.5 us  [permutes(): lax.ppermute(message, 'owner', [(i, i ^ s) for i in range(owners)])]
    unnamed x24, local copies, waits for them, and re-layouts: 0.05 us -> 1.53 us
  transfers between devices with their start and end apart: 30 -> 30, of which waited for: 5 -> 9; matrix products, arithmetic and copies ran while one was open for 0% -> 0% of each run, Pallas kernels for 14% -> 14%
where the time goes in v23:
time: 90.6 us; the launch traced here: 90.3 us
  starting transfers between devices  51.5 us (57%)
  Pallas kernels  20.6 us (23%)
  waiting for transfers between devices  16.3 us (18%)
  local copies, waits for them, and re-layouts  1.8 us (2%)
    ppermute x30, starting transfers between devices, permutes(): lax.ppermute(message, 'owner', [(i, i ^ s) for i in range(owners)])  51.5 us
    ppermute x30, waiting for transfers between devices, permutes(): lax.ppermute(message, 'owner', [(i, i ^ s) for i in range(owners)])  16.3 us
    pallas_call x2, Pallas kernels, pack(): pl.pallas_call(functools.partial(pack_kernel, which, owners, slot_count,...  8.31 us
    pallas_call x1, Pallas kernels, prep(): pl.pallas_call(functools.partial(prep_kernel, group), grid=(steps,), in_s...  5.14 us
    pallas_call x1, Pallas kernels, attend(): pl.pallas_call(functools.partial(attend_kernel, group, context, len(retur...  4.43 us
    pallas_call x4, Pallas kernels, adapt(): pl.pallas_call(functools.partial(adapt_kernel, count), in_specs=[pl.Block...  2.73 us
  transfers between devices with their start and end apart: 30, of which 9 were waited for; matrix products, arithmetic and copies ran while one was open for 0% of the time, Pallas kernels for 14%

profile of v23, /device:TPU:0, one launch (start us, length us, event | category | flops | bytes accessed | tf_op | source)
XLA Modules:
  0.0 90.3 jit_solution(11828019960914614966)
XLA Ops:
  0.0 3.9 %pack.2 = (bf16[32,128]{1,0:T(8,128)(2,1)}, bf16[8,8320]{1,0:T(8,128)(2,1)}, bf16[8,8320]{1,0:T(8,128)(2,1)}, bf16[8,8320]{1,0:T(8,128)(2,1)}, bf16[8,8320]{1,0:T(8,128)(2,1)}) custom-call(s32[1,32]{1,0:T(1,128)} %bitcast.2, s32[1,128]{1,0:T(1,128)} %bitcast.4, bf16[128,8192]{1,0:T(8,128)(2,1)} %hidden_hbm.3), custom_call_target="tpu_custom_call" | custom-call | tf_op jit(solution)/shard_map/pack/pallas_call | solution.py:96
  3.9 4.1 %collective-permute-start = (bf16[8,8320]{1,0:T(8,128)(2,1)}, bf16[8,8320]{1,0:T(8,128)(2,1)S(1)}, u32[]{:S(2)}, u32[]{:S(2)}) collective-permute-start(bf16[8,8320]{1,0:T(8,128)(2,1)} %get-tuple-element.42), channel_id=1, source_target_pairs={{0,8},{1,9},{2,10},{3,11},{4,12},{5,13},{6,14},{7,15},{8,0},{9,1},... | collective-permute-start | bytes 399368 | tf_op jit(solution)/shard_map/ppermute | solution.py:354
  8.0 3.0 %collective-permute-start.2 = (bf16[8,8320]{1,0:T(8,128)(2,1)}, bf16[8,8320]{1,0:T(8,128)(2,1)S(1)}, u32[]{:S(2)}, u32[]{:S(2)}) collective-permute-start(bf16[8,8320]{1,0:T(8,128)(2,1)} %get-tuple-element.44), channel_id=1, source_target_pairs={{0,10},{1,11},{2,8},{3,9},{4,14},{5,15},{6,12},{7,13},{8,2},{9,3},... | collective-permute-start | bytes 399368 | tf_op jit(solution)/shard_map/ppermute | solution.py:354
  11.0 1.6 %collective-permute-start.3 = (bf16[8,8320]{1,0:T(8,128)(2,1)}, bf16[8,8320]{1,0:T(8,128)(2,1)S(1)}, u32[]{:S(2)}, u32[]{:S(2)}) collective-permute-start(bf16[8,8320]{1,0:T(8,128)(2,1)} %get-tuple-element.45), channel_id=1, source_target_pairs={{0,4},{1,5},{2,6},{3,7},{4,0},{5,1},{6,2},{7,3},{8,12},{9,13},{10,... | collective-permute-start | bytes 399368 | tf_op jit(solution)/shard_map/ppermute | solution.py:354
  12.6 4.5 %pack.3 = (bf16[96,128]{1,0:T(8,128)(2,1)}, bf16[8,8320]{1,0:T(8,128)(2,1)}, bf16[8,8320]{1,0:T(8,128)(2,1)}, bf16[8,8320]{1,0:T(8,128)(2,1)}, bf16[8,8320]{1,0:...) custom-call(s32[1,32]{1,0:T(1,128)} %bitcast.3, ...), custom_call_target="tpu_custom_call" | custom-call | tf_op jit(solution)/shard_map/pack/pallas_call | solution.py:96
  17.0 0.4 collective-permute-start.8
  17.4 3.7 %collective-permute-done.refs_0_ = bf16[8,8320]{1,0:T(8,128)(2,1)S(1)} collective-permute-done((bf16[8,8320]{1,0:T(8,128)(2,1)}, bf16[8,8320]{1,0:T(8,128)(2,1)S(1)}, u32[]{:S(2)}, u32[]{:S(2)}) %collective-permute-start) | collective-permute-done | bytes 133152 | tf_op jit(solution)/shard_map/ppermute | solution.py:354
  21.1 0.0 collective-permute-start.9
  21.1 4.1 %collective-permute-done.1.refs_1_ = bf16[8,8320]{1,0:T(8,128)(2,1)S(1)} collective-permute-done((bf16[8,8320]{1,0:T(8,128)(2,1)}, bf16[8,8320]{1,0:T(8,128)(2,1)S(1)}, u32[]{:S(2)}, u32[]{:S(2)}) %collective-permute-start.1) | collective-permute-done | bytes 133152 | tf_op jit(solution)/shard_map/ppermute | solution.py:354
  25.3 4.3 %collective-permute-start.10 = (bf16[8,8320]{1,0:T(8,128)(2,1)}, bf16[8,8320]{1,0:T(8,128)(2,1)S(1)}, u32[]{:S(2)}, u32[]{:S(2)}) collective-permute-start(bf16[8,8320]{1,0:T(8,128)(2,1)} %get-tuple-element.52), channel_id=1, source_target_pairs={{0,12},{1,13},{2,14},{3,15},{4,8},{5,9},{6,10},{7,11},{8,4},{9,5},... | collective-permute-start | bytes 399368 | tf_op jit(solution)/shard_map/ppermute | solution.py:354
  29.5 1.5 %collective-permute-done.2.refs_2_ = bf16[8,8320]{1,0:T(8,128)(2,1)S(1)} collective-permute-done((bf16[8,8320]{1,0:T(8,128)(2,1)}, bf16[8,8320]{1,0:T(8,128)(2,1)S(1)}, u32[]{:S(2)}, u32[]{:S(2)}) %collective-permute-start.2) | collective-permute-done | bytes 133152 | tf_op jit(solution)/shard_map/ppermute | solution.py:354
  31.0 0.0 collective-permute-start.11
  31.0 1.9 %collective-permute-start.16 = (bf16[8,8320]{1,0:T(8,128)(2,1)}, bf16[8,8320]{1,0:T(8,128)(2,1)S(1)}, u32[]{:S(2)}, u32[]{:S(2)}) collective-permute-start(bf16[8,8320]{1,0:T(8,128)(2,1)} %get-tuple-element.58), channel_id=1, source_target_pairs={{0,13},{1,12},{2,15},{3,14},{4,9},{5,8},{6,11},{7,10},{8,5},{9,4},... | collective-permute-start | bytes 399368 | tf_op jit(solution)/shard_map/ppermute | solution.py:354
  33.0 2.6 %collective-permute-start.17 = (bf16[8,8320]{1,0:T(8,128)(2,1)}, bf16[8,8320]{1,0:T(8,128)(2,1)S(1)}, u32[]{:S(2)}, u32[]{:S(2)}) collective-permute-start(bf16[8,8320]{1,0:T(8,128)(2,1)} %get-tuple-element.59), channel_id=1, source_target_pairs={{0,7},{1,6},{2,5},{3,4},{4,3},{5,2},{6,1},{7,0},{8,15},{9,14},{10,... | collective-permute-start | bytes 399368 | tf_op jit(solution)/shard_map/ppermute | solution.py:354
  35.5 0.1 broadcast_in_dim.7
  35.6 0.1 broadcast_in_dim.8
  35.7 0.1 broadcast_in_dim.9.given_ref
  35.9 5.1 %prep.1 = (bf16[4,128,2048]{2,1,0:T(8,128)(2,1)S(1)}, bf16[4,92,192,128]{3,2,1,0:T(8,128)(2,1)}, s32[16,1,128]{2,1,0:T(1,128)S(1)}) custom-call(bf16[128,4096]{1,0:T(8,128)(2,1)S(1)} %copy-done.2, bf16[128,2,16,512]{3,2,1,0:T(8,128)(2,1)} %kv_ref.1, s32[16,1,128]{2,1,0:T(1,128)S(1)} %broadcast_in_dim.9.given_ref), custom_call_target="tpu_custom_call" | custom-call | tf_op jit(solution)/shard_map/prep/pallas_call | solution.py:184
  41.0 3.7 %collective-permute-start.18 = (bf16[8,8320]{1,0:T(8,128)(2,1)S(1)}, bf16[8,8320]{1,0:T(8,128)(2,1)S(1)}, u32[]{:S(2)}, u32[]{:S(2)}) collective-permute-start(bf16[8,8320]{1,0:T(8,128)(2,1)S(1)} %copy-done.11), channel_id=1, source_target_pairs={{0,14},{1,15},{2,12},{3,13},{4,10},{5,11},{6,8},{7,9},{8,6},{9,7},... | collective-permute-start | bytes 399368 | tf_op jit(solution)/shard_map/ppermute | solution.py:354
  44.7 2.5 %collective-permute-start.24 = (bf16[8,8320]{1,0:T(8,128)(2,1)S(1)}, bf16[8,8320]{1,0:T(8,128)(2,1)S(1)}, u32[]{:S(2)}, u32[]{:S(2)}) collective-permute-start(bf16[8,8320]{1,0:T(8,128)(2,1)S(1)} %copy-done.9), channel_id=1, source_target_pairs={{0,15},{1,14},{2,13},{3,12},{4,11},{5,10},{6,9},{7,8},{8,7},{9,6},... | collective-permute-start | bytes 399368 | tf_op jit(solution)/shard_map/ppermute | solution.py:354
  47.3 1.5 %collective-permute-start.25 = (bf16[8,8320]{1,0:T(8,128)(2,1)S(1)}, bf16[8,8320]{1,0:T(8,128)(2,1)S(1)}, u32[]{:S(2)}, u32[]{:S(2)}) collective-permute-start(bf16[8,8320]{1,0:T(8,128)(2,1)S(1)} %copy-done.8), channel_id=1, source_target_pairs={{0,2},{1,3},{2,0},{3,1},{4,6},{5,7},{6,4},{7,5},{8,10},{9,11},{10,... | collective-permute-start | bytes 399368 | tf_op jit(solution)/shard_map/ppermute | solution.py:354
  48.8 0.4 collective-permute-start.26
  49.1 1.2 %copy-done = bf16[8192,128]{1,0:T(8,128)(2,1)S(1)} copy-done((bf16[8192,128]{1,0:T(8,128)(2,1)S(1)}, bf16[8192,128]{1,0:T(8,128)(2,1)}, u32[]{:S(2)}) %copy-start) | copy-done | bytes 2097176
  50.3 0.3 copy-done.1
  50.6 0.7 adapt.4
  51.3 0.7 adapt.5
  52.0 5.7 %collective-permute-start.4 = (bf16[8,4096]{1,0:T(8,128)(2,1)S(1)}, bf16[8,4096]{1,0:T(8,128)(2,1)S(1)}, u32[]{:S(2)}, u32[]{:S(2)}) collective-permute-start(bf16[8,4096]{1,0:T(8,128)(2,1)S(1)} %get-tuple-element.46), channel_id=1, source_target_pairs={{0,8},{1,9},{2,10},{3,11},{4,12},{5,13},{6,14},{7,15},{8,0},{9,1},... | collective-permute-start | bytes 196616 | tf_op jit(solution)/shard_map/ppermute | solution.py:354
  57.7 2.9 %collective-permute-start.6 = (bf16[8,4096]{1,0:T(8,128)(2,1)S(1)}, bf16[8,4096]{1,0:T(8,128)(2,1)S(1)}, u32[]{:S(2)}, u32[]{:S(2)}) collective-permute-start(bf16[8,4096]{1,0:T(8,128)(2,1)S(1)} %get-tuple-element.48), channel_id=1, source_target_pairs={{0,10},{1,11},{2,8},{3,9},{4,14},{5,15},{6,12},{7,13},{8,2},{9,3},... | collective-permute-start | bytes 196616 | tf_op jit(solution)/shard_map/ppermute | solution.py:354
  60.7 1.4 %collective-permute-start.7 = (bf16[8,4096]{1,0:T(8,128)(2,1)S(1)}, bf16[8,4096]{1,0:T(8,128)(2,1)S(1)}, u32[]{:S(2)}, u32[]{:S(2)}) collective-permute-start(bf16[8,4096]{1,0:T(8,128)(2,1)S(1)} %get-tuple-element.49), channel_id=1, source_target_pairs={{0,4},{1,5},{2,6},{3,7},{4,0},{5,1},{6,2},{7,3},{8,12},{9,13},{10,... | collective-permute-start | bytes 196616 | tf_op jit(solution)/shard_map/ppermute | solution.py:354
  62.1 0.5 collective-permute-start.12
  62.6 0.7 adapt.6
  63.3 0.9 collective-permute-start.13
  64.2 1.8 %collective-permute-done.5.refs_1_ = bf16[8,4096]{1,0:T(8,128)(2,1)S(1)} collective-permute-done((bf16[8,4096]{1,0:T(8,128)(2,1)S(1)}, bf16[8,4096]{1,0:T(8,128)(2,1)S(1)}, u32[]{:S(2)}, u32[]{:S(2)}) %collective-permute-start.5) | collective-permute-done | bytes 65568 | tf_op jit(solution)/shard_map/ppermute | solution.py:354
  66.0 2.4 %collective-permute-start.14 = (bf16[8,4096]{1,0:T(8,128)(2,1)S(1)}, bf16[8,4096]{1,0:T(8,128)(2,1)S(1)}, u32[]{:S(2)}, u32[]{:S(2)}) collective-permute-start(bf16[8,4096]{1,0:T(8,128)(2,1)S(1)} %get-tuple-element.56), channel_id=1, source_target_pairs={{0,12},{1,13},{2,14},{3,15},{4,8},{5,9},{6,10},{7,11},{8,4},{9,5},... | collective-permute-start | bytes 196616 | tf_op jit(solution)/shard_map/ppermute | solution.py:354
  68.4 0.2 collective-permute-done.6.refs_2_
  68.5 0.8 collective-permute-start.15
  69.3 2.4 %collective-permute-start.20 = (bf16[8,4096]{1,0:T(8,128)(2,1)S(1)}, bf16[8,4096]{1,0:T(8,128)(2,1)S(1)}, u32[]{:S(2)}, u32[]{:S(2)}) collective-permute-start(bf16[8,4096]{1,0:T(8,128)(2,1)S(1)} %get-tuple-element.62), channel_id=1, source_target_pairs={{0,13},{1,12},{2,15},{3,14},{4,9},{5,8},{6,11},{7,10},{8,5},{9,4},... | collective-permute-start | bytes 196616 | tf_op jit(solution)/shard_map/ppermute | solution.py:354
  71.8 2.2 %collective-permute-start.21 = (bf16[8,4096]{1,0:T(8,128)(2,1)S(1)}, bf16[8,4096]{1,0:T(8,128)(2,1)S(1)}, u32[]{:S(2)}, u32[]{:S(2)}) collective-permute-start(bf16[8,4096]{1,0:T(8,128)(2,1)S(1)} %get-tuple-element.63), channel_id=1, source_target_pairs={{0,7},{1,6},{2,5},{3,4},{4,3},{5,2},{6,1},{7,0},{8,15},{9,14},{10,... | collective-permute-start | bytes 196616 | tf_op jit(solution)/shard_map/ppermute | solution.py:354
  74.0 0.7 adapt.7
  74.7 2.3 %collective-permute-start.22 = (bf16[8,4096]{1,0:T(8,128)(2,1)S(1)}, bf16[8,4096]{1,0:T(8,128)(2,1)S(1)}, u32[]{:S(2)}, u32[]{:S(2)}) collective-permute-start(bf16[8,4096]{1,0:T(8,128)(2,1)S(1)} %get-tuple-element.64), channel_id=1, source_target_pairs={{0,14},{1,15},{2,12},{3,13},{4,10},{5,11},{6,8},{7,9},{8,6},{9,7},... | collective-permute-start | bytes 196616 | tf_op jit(solution)/shard_map/ppermute | solution.py:354
  77.0 2.6 %collective-permute-start.27 = (bf16[8,4096]{1,0:T(8,128)(2,1)S(1)}, bf16[8,4096]{1,0:T(8,128)(2,1)S(1)}, u32[]{:S(2)}, u32[]{:S(2)}) collective-permute-start(bf16[8,4096]{1,0:T(8,128)(2,1)S(1)} %get-tuple-element.71), channel_id=1, source_target_pairs={{0,15},{1,14},{2,13},{3,12},{4,11},{5,10},{6,9},{7,8},{8,7},{9,6},... | collective-permute-start | bytes 196616 | tf_op jit(solution)/shard_map/ppermute | solution.py:354
  79.6 0.8 collective-permute-start.28
  80.4 0.6 collective-permute-start.29
  81.0 0.8 collective-permute-done.22.refs_10_
  81.8 1.9 %collective-permute-done.27.refs_12_ = bf16[8,4096]{1,0:T(8,128)(2,1)S(1)} collective-permute-done((bf16[8,4096]{1,0:T(8,128)(2,1)S(1)}, bf16[8,4096]{1,0:T(8,128)(2,1)S(1)}, u32[]{:S(2)}, u32[]{:S(2)}) %collective-permute-start.27) | collective-permute-done | bytes 65568 | tf_op jit(solution)/shard_map/ppermute | solution.py:354
  83.7 2.0 %collective-permute-done.28.refs_13_ = bf16[8,4096]{1,0:T(8,128)(2,1)S(1)} collective-permute-done((bf16[8,4096]{1,0:T(8,128)(2,1)S(1)}, bf16[8,4096]{1,0:T(8,128)(2,1)S(1)}, u32[]{:S(2)}, u32[]{:S(2)}) %collective-permute-start.28) | collective-permute-done | bytes 65568 | tf_op jit(solution)/shard_map/ppermute | solution.py:354
  85.6 0.3 collective-permute-done.29.refs_14_
  85.9 4.4 %attend.1 = bf16[128,4096]{1,0:T(8,128)(2,1)} custom-call(bf16[8,4096]{1,0:T(8,128)(2,1)S(1)} %collective-permute-done.4.refs_0_, bf16[8,4096]{1,0:T(8,128)(2,1)S(1)} %collective-permute-done.5.refs_1_, bf16[8,4096]{1,0:T(8,128)(2,1)S(1)} %collective-permute-done.6.refs_2_, bf16[8,4096]{1,0:T(8,128)(2,1)S(1)} %collective-permute-done.7.refs_3_, ...), custom_call_target="tpu_custom_call" | custom-call | tf_op jit(solution)/shard_map/attend/pallas_call | solution.py:304
  (48 shorter events, 0.1 us)
Async XLA Ops:
  0.0 35.5 %copy-start.7 = (s32[128]{0:T(128)S(1)}, s32[128]{0:T(128)}, u32[]{:S(2)}) copy-start(s32[128]{0:T(128)} %param.11) | copy-start | bytes 1540
  0.0 35.8 %copy-start.2 = (bf16[128,4096]{1,0:T(8,128)(2,1)S(1)}, bf16[128,4096]{1,0:T(8,128)(2,1)}, u32[]{:S(2)}) copy-start(bf16[128,4096]{1,0:T(8,128)(2,1)} %base_ref.1) | copy-start | bytes 3145732
  3.9 17.2 %collective-permute-start = (bf16[8,8320]{1,0:T(8,128)(2,1)}, bf16[8,8320]{1,0:T(8,128)(2,1)S(1)}, u32[]{:S(2)}, u32[]{:S(2)}) collective-permute-start(bf16[8,8320]{1,0:T(8,128)(2,1)} %get-tuple-element.42), channel_id=1, source_target_pairs={{0,8},{1,9},{2,10},{3,11},{4,12},{5,13},{6,14},{7,15},{8,0},{9,1},... | collective-permute-start | bytes 399368 | tf_op jit(solution)/shard_map/ppermute | solution.py:354
  8.0 17.3 %collective-permute-start.1 = (bf16[8,8320]{1,0:T(8,128)(2,1)}, bf16[8,8320]{1,0:T(8,128)(2,1)S(1)}, u32[]{:S(2)}, u32[]{:S(2)}) collective-permute-start(bf16[8,8320]{1,0:T(8,128)(2,1)} %get-tuple-element.43), channel_id=1, source_target_pairs={{0,9},{1,8},{2,11},{3,10},{4,13},{5,12},{6,15},{7,14},{8,1},{9,0},... | collective-permute-start | bytes 399368 | tf_op jit(solution)/shard_map/ppermute | solution.py:354
  8.0 23.1 %collective-permute-start.2 = (bf16[8,8320]{1,0:T(8,128)(2,1)}, bf16[8,8320]{1,0:T(8,128)(2,1)S(1)}, u32[]{:S(2)}, u32[]{:S(2)}) collective-permute-start(bf16[8,8320]{1,0:T(8,128)(2,1)} %get-tuple-element.44), channel_id=1, source_target_pairs={{0,10},{1,11},{2,8},{3,9},{4,14},{5,15},{6,12},{7,13},{8,2},{9,3},... | collective-permute-start | bytes 399368 | tf_op jit(solution)/shard_map/ppermute | solution.py:354
  11.0 20.1 %collective-permute-start.3 = (bf16[8,8320]{1,0:T(8,128)(2,1)}, bf16[8,8320]{1,0:T(8,128)(2,1)S(1)}, u32[]{:S(2)}, u32[]{:S(2)}) collective-permute-start(bf16[8,8320]{1,0:T(8,128)(2,1)} %get-tuple-element.45), channel_id=1, source_target_pairs={{0,4},{1,5},{2,6},{3,7},{4,0},{5,1},{6,2},{7,3},{8,12},{9,13},{10,... | collective-permute-start | bytes 399368 | tf_op jit(solution)/shard_map/ppermute | solution.py:354
  17.0 15.9 %collective-permute-start.8 = (bf16[8,8320]{1,0:T(8,128)(2,1)}, bf16[8,8320]{1,0:T(8,128)(2,1)S(1)}, u32[]{:S(2)}, u32[]{:S(2)}) collective-permute-start(bf16[8,8320]{1,0:T(8,128)(2,1)} %get-tuple-element.50), channel_id=1, source_target_pairs={{0,11},{1,10},{2,9},{3,8},{4,15},{5,14},{6,13},{7,12},{8,3},{9,2},... | collective-permute-start | bytes 399368 | tf_op jit(solution)/shard_map/ppermute | solution.py:354
  21.1 19.9 %collective-permute-start.9 = (bf16[8,8320]{1,0:T(8,128)(2,1)}, bf16[8,8320]{1,0:T(8,128)(2,1)S(1)}, u32[]{:S(2)}, u32[]{:S(2)}) collective-permute-start(bf16[8,8320]{1,0:T(8,128)(2,1)} %get-tuple-element.51), channel_id=1, source_target_pairs={{0,5},{1,4},{2,7},{3,6},{4,1},{5,0},{6,3},{7,2},{8,13},{9,12},{10,... | collective-permute-start | bytes 399368 | tf_op jit(solution)/shard_map/ppermute | solution.py:354
  25.3 19.5 %collective-permute-start.10 = (bf16[8,8320]{1,0:T(8,128)(2,1)}, bf16[8,8320]{1,0:T(8,128)(2,1)S(1)}, u32[]{:S(2)}, u32[]{:S(2)}) collective-permute-start(bf16[8,8320]{1,0:T(8,128)(2,1)} %get-tuple-element.52), channel_id=1, source_target_pairs={{0,12},{1,13},{2,14},{3,15},{4,8},{5,9},{6,10},{7,11},{8,4},{9,5},... | collective-permute-start | bytes 399368 | tf_op jit(solution)/shard_map/ppermute | solution.py:354
  31.0 13.7 %collective-permute-start.11 = (bf16[8,8320]{1,0:T(8,128)(2,1)}, bf16[8,8320]{1,0:T(8,128)(2,1)S(1)}, u32[]{:S(2)}, u32[]{:S(2)}) collective-permute-start(bf16[8,8320]{1,0:T(8,128)(2,1)} %get-tuple-element.53), channel_id=1, source_target_pairs={{0,6},{1,7},{2,4},{3,5},{4,2},{5,3},{6,0},{7,1},{8,14},{9,15},{10,... | collective-permute-start | bytes 399368 | tf_op jit(solution)/shard_map/ppermute | solution.py:354
  31.0 16.2 %collective-permute-start.16 = (bf16[8,8320]{1,0:T(8,128)(2,1)}, bf16[8,8320]{1,0:T(8,128)(2,1)S(1)}, u32[]{:S(2)}, u32[]{:S(2)}) collective-permute-start(bf16[8,8320]{1,0:T(8,128)(2,1)} %get-tuple-element.58), channel_id=1, source_target_pairs={{0,13},{1,12},{2,15},{3,14},{4,9},{5,8},{6,11},{7,10},{8,5},{9,4},... | collective-permute-start | bytes 399368 | tf_op jit(solution)/shard_map/ppermute | solution.py:354
  33.0 15.8 %collective-permute-start.17 = (bf16[8,8320]{1,0:T(8,128)(2,1)}, bf16[8,8320]{1,0:T(8,128)(2,1)S(1)}, u32[]{:S(2)}, u32[]{:S(2)}) collective-permute-start(bf16[8,8320]{1,0:T(8,128)(2,1)} %get-tuple-element.59), channel_id=1, source_target_pairs={{0,7},{1,6},{2,5},{3,4},{4,3},{5,2},{6,1},{7,0},{8,15},{9,14},{10,... | collective-permute-start | bytes 399368 | tf_op jit(solution)/shard_map/ppermute | solution.py:354
  35.8 5.2 %copy-start.11 = (bf16[8,8320]{1,0:T(8,128)(2,1)S(1)}, bf16[8,8320]{1,0:T(8,128)(2,1)}, u32[]{:S(2)}) copy-start(bf16[8,8320]{1,0:T(8,128)(2,1)} %get-tuple-element.60) | copy-start | bytes 399364
  35.8 8.9 %copy-start.10 = (bf16[8,8320]{1,0:T(8,128)(2,1)S(1)}, bf16[8,8320]{1,0:T(8,128)(2,1)}, u32[]{:S(2)}) copy-start(bf16[8,8320]{1,0:T(8,128)(2,1)} %get-tuple-element.61) | copy-start | bytes 399364
  35.8 8.9 %copy-start.9 = (bf16[8,8320]{1,0:T(8,128)(2,1)S(1)}, bf16[8,8320]{1,0:T(8,128)(2,1)}, u32[]{:S(2)}) copy-start(bf16[8,8320]{1,0:T(8,128)(2,1)} %get-tuple-element.66) | copy-start | bytes 399364
  35.9 11.4 %copy-start.8 = (bf16[8,8320]{1,0:T(8,128)(2,1)S(1)}, bf16[8,8320]{1,0:T(8,128)(2,1)}, u32[]{:S(2)}) copy-start(bf16[8,8320]{1,0:T(8,128)(2,1)} %get-tuple-element.67) | copy-start | bytes 399364
  35.9 12.9 %copy-start.4 = (bf16[8,8320]{1,0:T(8,128)(2,1)S(1)}, bf16[8,8320]{1,0:T(8,128)(2,1)}, u32[]{:S(2)}) copy-start(bf16[8,8320]{1,0:T(8,128)(2,1)} %get-tuple-element.68.refs_0_) | copy-start | bytes 399364
  41.0 11.0 %collective-permute-start.18 = (bf16[8,8320]{1,0:T(8,128)(2,1)S(1)}, bf16[8,8320]{1,0:T(8,128)(2,1)S(1)}, u32[]{:S(2)}, u32[]{:S(2)}) collective-permute-start(bf16[8,8320]{1,0:T(8,128)(2,1)S(1)} %copy-done.11), channel_id=1, source_target_pairs={{0,14},{1,15},{2,12},{3,13},{4,10},{5,11},{6,8},{7,9},{8,6},{9,7},... | collective-permute-start | bytes 399368 | tf_op jit(solution)/shard_map/ppermute | solution.py:354
  44.7 13.0 %collective-permute-start.19 = (bf16[8,8320]{1,0:T(8,128)(2,1)S(1)}, bf16[8,8320]{1,0:T(8,128)(2,1)S(1)}, u32[]{:S(2)}, u32[]{:S(2)}) collective-permute-start(bf16[8,8320]{1,0:T(8,128)(2,1)S(1)} %copy-done.10), channel_id=1, source_target_pairs={{0,1},{1,0},{2,3},{3,2},{4,5},{5,4},{6,7},{7,6},{8,9},{9,8},{10,11... | collective-permute-start | bytes 399368 | tf_op jit(solution)/shard_map/ppermute | solution.py:354
  44.7 13.0 %collective-permute-start.24 = (bf16[8,8320]{1,0:T(8,128)(2,1)S(1)}, bf16[8,8320]{1,0:T(8,128)(2,1)S(1)}, u32[]{:S(2)}, u32[]{:S(2)}) collective-permute-start(bf16[8,8320]{1,0:T(8,128)(2,1)S(1)} %copy-done.9), channel_id=1, source_target_pairs={{0,15},{1,14},{2,13},{3,12},{4,11},{5,10},{6,9},{7,8},{8,7},{9,6},... | collective-permute-start | bytes 399368 | tf_op jit(solution)/shard_map/ppermute | solution.py:354
  47.3 13.4 %collective-permute-start.25 = (bf16[8,8320]{1,0:T(8,128)(2,1)S(1)}, bf16[8,8320]{1,0:T(8,128)(2,1)S(1)}, u32[]{:S(2)}, u32[]{:S(2)}) collective-permute-start(bf16[8,8320]{1,0:T(8,128)(2,1)S(1)} %copy-done.8), channel_id=1, source_target_pairs={{0,2},{1,3},{2,0},{3,1},{4,6},{5,7},{6,4},{7,5},{8,10},{9,11},{10,... | collective-permute-start | bytes 399368 | tf_op jit(solution)/shard_map/ppermute | solution.py:354
  48.8 1.6 %copy-start = (bf16[8192,128]{1,0:T(8,128)(2,1)S(1)}, bf16[8192,128]{1,0:T(8,128)(2,1)}, u32[]{:S(2)}) copy-start(bf16[8192,128]{1,0:T(8,128)(2,1)} %refs_4_.7) | copy-start | bytes 6291460
  48.8 1.9 %copy-start.1 = (bf16[128,4096]{1,0:T(8,128)(2,1)S(1)}, bf16[128,4096]{1,0:T(8,128)(2,1)}, u32[]{:S(2)}) copy-start(bf16[128,4096]{1,0:T(8,128)(2,1)} %refs_5_.7) | copy-start | bytes 3145732
  48.8 13.3 %collective-permute-start.26 = (bf16[8,8320]{1,0:T(8,128)(2,1)S(1)}, bf16[8,8320]{1,0:T(8,128)(2,1)S(1)}, u32[]{:S(2)}, u32[]{:S(2)}) collective-permute-start(bf16[8,8320]{1,0:T(8,128)(2,1)S(1)} %hold.1), channel_id=1, source_target_pairs={{0,3},{1,2},{2,1},{3,0},{4,7},{5,6},{6,5},{7,4},{8,11},{9,10},{10,... | collective-permute-start | bytes 399368 | tf_op jit(solution)/shard_map/ppermute | solution.py:354
  52.0 22.0 %copy-start.3 = (bf16[8,8320]{1,0:T(8,128)(2,1)S(1)}, bf16[8,8320]{1,0:T(8,128)(2,1)}, u32[]{:S(2)}) copy-start(bf16[8,8320]{1,0:T(8,128)(2,1)} %get-tuple-element.70.refs_3_) | copy-start | bytes 399364
  52.0 11.3 %collective-permute-start.4 = (bf16[8,4096]{1,0:T(8,128)(2,1)S(1)}, bf16[8,4096]{1,0:T(8,128)(2,1)S(1)}, u32[]{:S(2)}, u32[]{:S(2)}) collective-permute-start(bf16[8,4096]{1,0:T(8,128)(2,1)S(1)} %get-tuple-element.46), channel_id=1, source_target_pairs={{0,8},{1,9},{2,10},{3,11},{4,12},{5,13},{6,14},{7,15},{8,0},{9,1},... | collective-permute-start | bytes 196616 | tf_op jit(solution)/shard_map/ppermute | solution.py:354
  57.7 8.3 %collective-permute-start.5 = (bf16[8,4096]{1,0:T(8,128)(2,1)S(1)}, bf16[8,4096]{1,0:T(8,128)(2,1)S(1)}, u32[]{:S(2)}, u32[]{:S(2)}) collective-permute-start(bf16[8,4096]{1,0:T(8,128)(2,1)S(1)} %get-tuple-element.47), channel_id=1, source_target_pairs={{0,9},{1,8},{2,11},{3,10},{4,13},{5,12},{6,15},{7,14},{8,1},{9,0},... | collective-permute-start | bytes 196616 | tf_op jit(solution)/shard_map/ppermute | solution.py:354
  57.7 10.8 %collective-permute-start.6 = (bf16[8,4096]{1,0:T(8,128)(2,1)S(1)}, bf16[8,4096]{1,0:T(8,128)(2,1)S(1)}, u32[]{:S(2)}, u32[]{:S(2)}) collective-permute-start(bf16[8,4096]{1,0:T(8,128)(2,1)S(1)} %get-tuple-element.48), channel_id=1, source_target_pairs={{0,10},{1,11},{2,8},{3,9},{4,14},{5,15},{6,12},{7,13},{8,2},{9,3},... | collective-permute-start | bytes 196616 | tf_op jit(solution)/shard_map/ppermute | solution.py:354
  60.7 8.7 %collective-permute-start.7 = (bf16[8,4096]{1,0:T(8,128)(2,1)S(1)}, bf16[8,4096]{1,0:T(8,128)(2,1)S(1)}, u32[]{:S(2)}, u32[]{:S(2)}) collective-permute-start(bf16[8,4096]{1,0:T(8,128)(2,1)S(1)} %get-tuple-element.49), channel_id=1, source_target_pairs={{0,4},{1,5},{2,6},{3,7},{4,0},{5,1},{6,2},{7,3},{8,12},{9,13},{10,... | collective-permute-start | bytes 196616 | tf_op jit(solution)/shard_map/ppermute | solution.py:354
  62.1 9.7 %collective-permute-start.12 = (bf16[8,4096]{1,0:T(8,128)(2,1)S(1)}, bf16[8,4096]{1,0:T(8,128)(2,1)S(1)}, u32[]{:S(2)}, u32[]{:S(2)}) collective-permute-start(bf16[8,4096]{1,0:T(8,128)(2,1)S(1)} %get-tuple-element.54), channel_id=1, source_target_pairs={{0,11},{1,10},{2,9},{3,8},{4,15},{5,14},{6,13},{7,12},{8,3},{9,2},... | collective-permute-start | bytes 196616 | tf_op jit(solution)/shard_map/ppermute | solution.py:354
  63.3 22.6 %copy-start.5 = (bf16[96,128]{1,0:T(8,128)(2,1)S(1)}, bf16[96,128]{1,0:T(8,128)(2,1)}, u32[]{:S(2)}) copy-start(bf16[96,128]{1,0:T(8,128)(2,1)} %get-tuple-element.76.refs_17_) | copy-start | bytes 73732
  63.3 22.6 %copy-start.6 = (bf16[32,128]{1,0:T(8,128)(2,1)S(1)}, bf16[32,128]{1,0:T(8,128)(2,1)}, u32[]{:S(2)}) copy-start(bf16[32,128]{1,0:T(8,128)(2,1)} %get-tuple-element.75.refs_16_) | copy-start | bytes 24580
  63.3 11.4 %collective-permute-start.13 = (bf16[8,4096]{1,0:T(8,128)(2,1)S(1)}, bf16[8,4096]{1,0:T(8,128)(2,1)S(1)}, u32[]{:S(2)}, u32[]{:S(2)}) collective-permute-start(bf16[8,4096]{1,0:T(8,128)(2,1)S(1)} %get-tuple-element.55), channel_id=1, source_target_pairs={{0,5},{1,4},{2,7},{3,6},{4,1},{5,0},{6,3},{7,2},{8,13},{9,12},{10,... | collective-permute-start | bytes 196616 | tf_op jit(solution)/shard_map/ppermute | solution.py:354
  66.0 11.0 %collective-permute-start.14 = (bf16[8,4096]{1,0:T(8,128)(2,1)S(1)}, bf16[8,4096]{1,0:T(8,128)(2,1)S(1)}, u32[]{:S(2)}, u32[]{:S(2)}) collective-permute-start(bf16[8,4096]{1,0:T(8,128)(2,1)S(1)} %get-tuple-element.56), channel_id=1, source_target_pairs={{0,12},{1,13},{2,14},{3,15},{4,8},{5,9},{6,10},{7,11},{8,4},{9,5},... | collective-permute-start | bytes 196616 | tf_op jit(solution)/shard_map/ppermute | solution.py:354
  68.5 8.5 %collective-permute-start.15 = (bf16[8,4096]{1,0:T(8,128)(2,1)S(1)}, bf16[8,4096]{1,0:T(8,128)(2,1)S(1)}, u32[]{:S(2)}, u32[]{:S(2)}) collective-permute-start(bf16[8,4096]{1,0:T(8,128)(2,1)S(1)} %get-tuple-element.57), channel_id=1, source_target_pairs={{0,6},{1,7},{2,4},{3,5},{4,2},{5,3},{6,0},{7,1},{8,14},{9,15},{10,... | collective-permute-start | bytes 196616 | tf_op jit(solution)/shard_map/ppermute | solution.py:354
  69.3 10.3 %collective-permute-start.20 = (bf16[8,4096]{1,0:T(8,128)(2,1)S(1)}, bf16[8,4096]{1,0:T(8,128)(2,1)S(1)}, u32[]{:S(2)}, u32[]{:S(2)}) collective-permute-start(bf16[8,4096]{1,0:T(8,128)(2,1)S(1)} %get-tuple-element.62), channel_id=1, source_target_pairs={{0,13},{1,12},{2,15},{3,14},{4,9},{5,8},{6,11},{7,10},{8,5},{9,4},... | collective-permute-start | bytes 196616 | tf_op jit(solution)/shard_map/ppermute | solution.py:354
  71.8 8.6 %collective-permute-start.21 = (bf16[8,4096]{1,0:T(8,128)(2,1)S(1)}, bf16[8,4096]{1,0:T(8,128)(2,1)S(1)}, u32[]{:S(2)}, u32[]{:S(2)}) collective-permute-start(bf16[8,4096]{1,0:T(8,128)(2,1)S(1)} %get-tuple-element.63), channel_id=1, source_target_pairs={{0,7},{1,6},{2,5},{3,4},{4,3},{5,2},{6,1},{7,0},{8,15},{9,14},{10,... | collective-permute-start | bytes 196616 | tf_op jit(solution)/shard_map/ppermute | solution.py:354
  74.7 7.1 %collective-permute-start.22 = (bf16[8,4096]{1,0:T(8,128)(2,1)S(1)}, bf16[8,4096]{1,0:T(8,128)(2,1)S(1)}, u32[]{:S(2)}, u32[]{:S(2)}) collective-permute-start(bf16[8,4096]{1,0:T(8,128)(2,1)S(1)} %get-tuple-element.64), channel_id=1, source_target_pairs={{0,14},{1,15},{2,12},{3,13},{4,10},{5,11},{6,8},{7,9},{8,6},{9,7},... | collective-permute-start | bytes 196616 | tf_op jit(solution)/shard_map/ppermute | solution.py:354
  77.0 4.8 %collective-permute-start.23 = (bf16[8,4096]{1,0:T(8,128)(2,1)S(1)}, bf16[8,4096]{1,0:T(8,128)(2,1)S(1)}, u32[]{:S(2)}, u32[]{:S(2)}) collective-permute-start(bf16[8,4096]{1,0:T(8,128)(2,1)S(1)} %get-tuple-element.65), channel_id=1, source_target_pairs={{0,1},{1,0},{2,3},{3,2},{4,5},{5,4},{6,7},{7,6},{8,9},{9,8},{10,11... | collective-permute-start | bytes 196616 | tf_op jit(solution)/shard_map/ppermute | solution.py:354
  77.0 6.7 %collective-permute-start.27 = (bf16[8,4096]{1,0:T(8,128)(2,1)S(1)}, bf16[8,4096]{1,0:T(8,128)(2,1)S(1)}, u32[]{:S(2)}, u32[]{:S(2)}) collective-permute-start(bf16[8,4096]{1,0:T(8,128)(2,1)S(1)} %get-tuple-element.71), channel_id=1, source_target_pairs={{0,15},{1,14},{2,13},{3,12},{4,11},{5,10},{6,9},{7,8},{8,7},{9,6},... | collective-permute-start | bytes 196616 | tf_op jit(solution)/shard_map/ppermute | solution.py:354
  79.6 6.0 %collective-permute-start.28 = (bf16[8,4096]{1,0:T(8,128)(2,1)S(1)}, bf16[8,4096]{1,0:T(8,128)(2,1)S(1)}, u32[]{:S(2)}, u32[]{:S(2)}) collective-permute-start(bf16[8,4096]{1,0:T(8,128)(2,1)S(1)} %get-tuple-element.72), channel_id=1, source_target_pairs={{0,2},{1,3},{2,0},{3,1},{4,6},{5,7},{6,4},{7,5},{8,10},{9,11},{10,... | collective-permute-start | bytes 196616 | tf_op jit(solution)/shard_map/ppermute | solution.py:354
  80.4 5.5 %collective-permute-start.29 = (bf16[8,4096]{1,0:T(8,128)(2,1)S(1)}, bf16[8,4096]{1,0:T(8,128)(2,1)S(1)}, u32[]{:S(2)}, u32[]{:S(2)}) collective-permute-start(bf16[8,4096]{1,0:T(8,128)(2,1)S(1)} %get-tuple-element.73), channel_id=1, source_target_pairs={{0,3},{1,2},{2,1},{3,0},{4,7},{5,6},{6,5},{7,4},{8,11},{9,10},{10,... | collective-permute-start | bytes 196616 | tf_op jit(solution)/shard_map/ppermute | solution.py:354

commit v24 on v23

--- a/solution.py
+++ b/solution.py
@@ -15,7 +15,6 @@
 ROWS_STEP = 8
 PREP_STEPS = 4
 GROUPS = 4
-LEAD = 3
 FIRST = 4
 MOST_PERMUTES = 32
 COLUMNS_STEP = 1024
@@ -328,10 +327,8 @@
     half = owners // 2
     near = [*range(half // 2, half), *range(1, half // 2)]
     far = [*range(half, owners)]
-    order = far[:LEAD]
-    for i, s in enumerate(near):
-        order += [s, *far[LEAD + i : LEAD + i + 1]]
-    order.append(0)
+    order = [s for pair in zip(far, near[: half // 2]) for s in pair]
+    order += [*far[half // 2 :], *near[half // 2 :], 0]
     routed, messages = [], []
     for which in (order[:FIRST], order[FIRST:]):
         hits, *packed = pack(which, hidden, adapter_id, adapter_slot, owners, slot_count, held)

time: 90.6 us -> 87.8 us (0.969)
  waiting for transfers between devices: 16.3 us -> 9.87 us
  starting transfers between devices: 51.5 us -> 56.1 us
  local copies, waits for them, and re-layouts: 1.8 us -> 0.79 us
    ppermute x30, waiting for transfers between devices: 16.3 us -> 9.87 us  [permutes(): lax.ppermute(message, 'owner', [(i, i ^ s) for i in range(owners)])]
    ppermute x30, starting transfers between devices: 51.5 us -> 56.1 us  [permutes(): lax.ppermute(message, 'owner', [(i, i ^ s) for i in range(owners)])]
    unnamed x24, local copies, waits for them, and re-layouts: 1.53 us -> 0.53 us
  transfers between devices with their start and end apart: 30 -> 30, of which waited for: 9 -> 6; matrix products, arithmetic and copies ran while one was open for 0% -> 0% of each run, Pallas kernels for 14% -> 14%
where the time goes in v24:
time: 87.8 us; the launch traced here: 87.5 us
  starting transfers between devices  56.1 us (64%)
  Pallas kernels  20.6 us (23%)
  waiting for transfers between devices  9.87 us (11%)
    ppermute x30, starting transfers between devices, permutes(): lax.ppermute(message, 'owner', [(i, i ^ s) for i in range(owners)])  56.1 us
    ppermute x30, waiting for transfers between devices, permutes(): lax.ppermute(message, 'owner', [(i, i ^ s) for i in range(owners)])  9.87 us
    pallas_call x2, Pallas kernels, pack(): pl.pallas_call(functools.partial(pack_kernel, which, owners, slot_count,...  8.31 us
    pallas_call x1, Pallas kernels, prep(): pl.pallas_call(functools.partial(prep_kernel, group), grid=(steps,), in_s...  5.14 us
    pallas_call x1, Pallas kernels, attend(): pl.pallas_call(functools.partial(attend_kernel, group, context, len(retur...  4.43 us
    pallas_call x4, Pallas kernels, adapt(): pl.pallas_call(functools.partial(adapt_kernel, count), in_specs=[pl.Block...  2.73 us
  transfers between devices with their start and end apart: 30, of which 6 were waited for; matrix products, arithmetic and copies ran while one was open for 0% of the time, Pallas kernels for 14%

profile of v24, /device:TPU:0, one launch (start us, length us, event | category | flops | bytes accessed | tf_op | source)
XLA Modules:
  0.0 87.5 jit_solution(13424257009417594440)
XLA Ops:
  0.0 3.9 %pack.2 = (bf16[32,128]{1,0:T(8,128)(2,1)}, bf16[8,8320]{1,0:T(8,128)(2,1)}, bf16[8,8320]{1,0:T(8,128)(2,1)}, bf16[8,8320]{1,0:T(8,128)(2,1)}, bf16[8,8320]{1,0:T(8,128)(2,1)}) custom-call(s32[1,32]{1,0:T(1,128)} %bitcast.2, s32[1,128]{1,0:T(1,128)} %bitcast.4, bf16[128,8192]{1,0:T(8,128)(2,1)} %hidden_hbm.3), custom_call_target="tpu_custom_call" | custom-call | tf_op jit(solution)/shard_map/pack/pallas_call | solution.py:95
  3.9 4.1 %collective-permute-start = (bf16[8,8320]{1,0:T(8,128)(2,1)}, bf16[8,8320]{1,0:T(8,128)(2,1)S(1)}, u32[]{:S(2)}, u32[]{:S(2)}) collective-permute-start(bf16[8,8320]{1,0:T(8,128)(2,1)} %get-tuple-element.42), channel_id=1, source_target_pairs={{0,8},{1,9},{2,10},{3,11},{4,12},{5,13},{6,14},{7,15},{8,0},{9,1},... | collective-permute-start | bytes 399368 | tf_op jit(solution)/shard_map/ppermute | solution.py:351
  8.0 1.6 %collective-permute-start.1 = (bf16[8,8320]{1,0:T(8,128)(2,1)}, bf16[8,8320]{1,0:T(8,128)(2,1)S(1)}, u32[]{:S(2)}, u32[]{:S(2)}) collective-permute-start(bf16[8,8320]{1,0:T(8,128)(2,1)} %get-tuple-element.43), channel_id=1, source_target_pairs={{0,4},{1,5},{2,6},{3,7},{4,0},{5,1},{6,2},{7,3},{8,12},{9,13},{10,... | collective-permute-start | bytes 399368 | tf_op jit(solution)/shard_map/ppermute | solution.py:351
  9.5 0.0 collective-permute-start.2
  9.5 0.2 collective-permute-start.3
  9.8 4.5 %pack.3 = (bf16[96,128]{1,0:T(8,128)(2,1)}, bf16[8,8320]{1,0:T(8,128)(2,1)}, bf16[8,8320]{1,0:T(8,128)(2,1)}, bf16[8,8320]{1,0:T(8,128)(2,1)}, bf16[8,8320]{1,0:...) custom-call(s32[1,32]{1,0:T(1,128)} %bitcast.3, ...), custom_call_target="tpu_custom_call" | custom-call | tf_op jit(solution)/shard_map/pack/pallas_call | solution.py:95
  14.3 3.8 %collective-permute-start.8 = (bf16[8,8320]{1,0:T(8,128)(2,1)}, bf16[8,8320]{1,0:T(8,128)(2,1)S(1)}, u32[]{:S(2)}, u32[]{:S(2)}) collective-permute-start(bf16[8,8320]{1,0:T(8,128)(2,1)} %get-tuple-element.50), channel_id=1, source_target_pairs={{0,10},{1,11},{2,8},{3,9},{4,14},{5,15},{6,12},{7,13},{8,2},{9,3},... | collective-permute-start | bytes 399368 | tf_op jit(solution)/shard_map/ppermute | solution.py:351
  18.1 1.6 %collective-permute-start.9 = (bf16[8,8320]{1,0:T(8,128)(2,1)}, bf16[8,8320]{1,0:T(8,128)(2,1)S(1)}, u32[]{:S(2)}, u32[]{:S(2)}) collective-permute-start(bf16[8,8320]{1,0:T(8,128)(2,1)} %get-tuple-element.51), channel_id=1, source_target_pairs={{0,6},{1,7},{2,4},{3,5},{4,2},{5,3},{6,0},{7,1},{8,14},{9,15},{10,... | collective-permute-start | bytes 399368 | tf_op jit(solution)/shard_map/ppermute | solution.py:351
  19.7 0.0 collective-permute-done.1.refs_1_
  19.7 0.4 collective-permute-start.10
  20.0 2.2 %collective-permute-start.11 = (bf16[8,8320]{1,0:T(8,128)(2,1)}, bf16[8,8320]{1,0:T(8,128)(2,1)S(1)}, u32[]{:S(2)}, u32[]{:S(2)}) collective-permute-start(bf16[8,8320]{1,0:T(8,128)(2,1)} %get-tuple-element.53), channel_id=1, source_target_pairs={{0,7},{1,6},{2,5},{3,4},{4,3},{5,2},{6,1},{7,0},{8,15},{9,14},{10,... | collective-permute-start | bytes 399368 | tf_op jit(solution)/shard_map/ppermute | solution.py:351
  22.2 2.6 %collective-permute-start.16 = (bf16[8,8320]{1,0:T(8,128)(2,1)}, bf16[8,8320]{1,0:T(8,128)(2,1)S(1)}, u32[]{:S(2)}, u32[]{:S(2)}) collective-permute-start(bf16[8,8320]{1,0:T(8,128)(2,1)} %get-tuple-element.58), channel_id=1, source_target_pairs={{0,12},{1,13},{2,14},{3,15},{4,8},{5,9},{6,10},{7,11},{8,4},{9,5},... | collective-permute-start | bytes 399368 | tf_op jit(solution)/shard_map/ppermute | solution.py:351
  24.8 3.8 %collective-permute-done.8.refs_0_ = bf16[8,8320]{1,0:T(8,128)(2,1)S(1)} collective-permute-done((bf16[8,8320]{1,0:T(8,128)(2,1)}, bf16[8,8320]{1,0:T(8,128)(2,1)S(1)}, u32[]{:S(2)}, u32[]{:S(2)}) %collective-permute-start.8) | collective-permute-done | bytes 133152 | tf_op jit(solution)/shard_map/ppermute | solution.py:351
  28.5 2.6 %collective-permute-start.17 = (bf16[8,8320]{1,0:T(8,128)(2,1)}, bf16[8,8320]{1,0:T(8,128)(2,1)S(1)}, u32[]{:S(2)}, u32[]{:S(2)}) collective-permute-start(bf16[8,8320]{1,0:T(8,128)(2,1)} %get-tuple-element.59), channel_id=1, source_target_pairs={{0,13},{1,12},{2,15},{3,14},{4,9},{5,8},{6,11},{7,10},{8,5},{9,4},... | collective-permute-start | bytes 399368 | tf_op jit(solution)/shard_map/ppermute | solution.py:351
  31.1 0.1 broadcast_in_dim.7
  31.2 0.1 broadcast_in_dim.8
  31.3 0.1 broadcast_in_dim.9.given_ref
  31.4 5.1 %prep.1 = (bf16[4,128,2048]{2,1,0:T(8,128)(2,1)S(1)}, bf16[4,92,192,128]{3,2,1,0:T(8,128)(2,1)}, s32[16,1,128]{2,1,0:T(1,128)S(1)}) custom-call(bf16[128,4096]{1,0:T(8,128)(2,1)S(1)} %copy-done.2, bf16[128,2,16,512]{3,2,1,0:T(8,128)(2,1)} %kv_ref.1, s32[16,1,128]{2,1,0:T(1,128)S(1)} %broadcast_in_dim.9.given_ref), custom_call_target="tpu_custom_call" | custom-call | tf_op jit(solution)/shard_map/prep/pallas_call | solution.py:183
  36.6 0.6 collective-permute-start.18
  37.2 4.2 %collective-permute-start.19 = (bf16[8,8320]{1,0:T(8,128)(2,1)S(1)}, bf16[8,8320]{1,0:T(8,128)(2,1)S(1)}, u32[]{:S(2)}, u32[]{:S(2)}) collective-permute-start(bf16[8,8320]{1,0:T(8,128)(2,1)S(1)} %copy-done.10), channel_id=1, source_target_pairs={{0,15},{1,14},{2,13},{3,12},{4,11},{5,10},{6,9},{7,8},{8,7},{9,6},... | collective-permute-start | bytes 399368 | tf_op jit(solution)/shard_map/ppermute | solution.py:351
  41.4 0.0 collective-permute-start.24
  41.4 0.6 collective-permute-start.25
  42.0 1.4 %collective-permute-start.26 = (bf16[8,8320]{1,0:T(8,128)(2,1)S(1)}, bf16[8,8320]{1,0:T(8,128)(2,1)S(1)}, u32[]{:S(2)}, u32[]{:S(2)}) collective-permute-start(bf16[8,8320]{1,0:T(8,128)(2,1)S(1)} %hold.1), channel_id=1, source_target_pairs={{0,3},{1,2},{2,1},{3,0},{4,7},{5,6},{6,5},{7,4},{8,11},{9,10},{10,... | collective-permute-start | bytes 399368 | tf_op jit(solution)/shard_map/ppermute | solution.py:351
  43.4 0.2 copy-done
  43.6 0.3 copy-done.1
  43.9 0.7 adapt.4
  44.5 0.7 adapt.5
  45.2 0.7 collective-permute-done.18.refs_2_
  45.9 9.5 %collective-permute-start.4 = (bf16[8,4096]{1,0:T(8,128)(2,1)S(1)}, bf16[8,4096]{1,0:T(8,128)(2,1)S(1)}, u32[]{:S(2)}, u32[]{:S(2)}) collective-permute-start(bf16[8,4096]{1,0:T(8,128)(2,1)S(1)} %get-tuple-element.46), channel_id=1, source_target_pairs={{0,8},{1,9},{2,10},{3,11},{4,12},{5,13},{6,14},{7,15},{8,0},{9,1},... | collective-permute-start | bytes 196616 | tf_op jit(solution)/shard_map/ppermute | solution.py:351
  55.4 2.3 %collective-permute-start.6 = (bf16[8,4096]{1,0:T(8,128)(2,1)S(1)}, bf16[8,4096]{1,0:T(8,128)(2,1)S(1)}, u32[]{:S(2)}, u32[]{:S(2)}) collective-permute-start(bf16[8,4096]{1,0:T(8,128)(2,1)S(1)} %get-tuple-element.48), channel_id=1, source_target_pairs={{0,9},{1,8},{2,11},{3,10},{4,13},{5,12},{6,15},{7,14},{8,1},{9,0},... | collective-permute-start | bytes 196616 | tf_op jit(solution)/shard_map/ppermute | solution.py:351
  57.8 2.1 %collective-permute-start.7 = (bf16[8,4096]{1,0:T(8,128)(2,1)S(1)}, bf16[8,4096]{1,0:T(8,128)(2,1)S(1)}, u32[]{:S(2)}, u32[]{:S(2)}) collective-permute-start(bf16[8,4096]{1,0:T(8,128)(2,1)S(1)} %get-tuple-element.49), channel_id=1, source_target_pairs={{0,5},{1,4},{2,7},{3,6},{4,1},{5,0},{6,3},{7,2},{8,13},{9,12},{10,... | collective-permute-start | bytes 196616 | tf_op jit(solution)/shard_map/ppermute | solution.py:351
  59.8 3.3 %collective-permute-start.12 = (bf16[8,4096]{1,0:T(8,128)(2,1)S(1)}, bf16[8,4096]{1,0:T(8,128)(2,1)S(1)}, u32[]{:S(2)}, u32[]{:S(2)}) collective-permute-start(bf16[8,4096]{1,0:T(8,128)(2,1)S(1)} %get-tuple-element.54), channel_id=1, source_target_pairs={{0,10},{1,11},{2,8},{3,9},{4,14},{5,15},{6,12},{7,13},{8,2},{9,3},... | collective-permute-start | bytes 196616 | tf_op jit(solution)/shard_map/ppermute | solution.py:351
  63.2 0.7 adapt.6
  63.9 0.1 collective-permute-start.13
  64.0 0.8 collective-permute-start.14
  64.8 2.3 %collective-permute-start.15 = (bf16[8,4096]{1,0:T(8,128)(2,1)S(1)}, bf16[8,4096]{1,0:T(8,128)(2,1)S(1)}, u32[]{:S(2)}, u32[]{:S(2)}) collective-permute-start(bf16[8,4096]{1,0:T(8,128)(2,1)S(1)} %get-tuple-element.57), channel_id=1, source_target_pairs={{0,7},{1,6},{2,5},{3,4},{4,3},{5,2},{6,1},{7,0},{8,15},{9,14},{10,... | collective-permute-start | bytes 196616 | tf_op jit(solution)/shard_map/ppermute | solution.py:351
  67.1 2.0 %collective-permute-start.20 = (bf16[8,4096]{1,0:T(8,128)(2,1)S(1)}, bf16[8,4096]{1,0:T(8,128)(2,1)S(1)}, u32[]{:S(2)}, u32[]{:S(2)}) collective-permute-start(bf16[8,4096]{1,0:T(8,128)(2,1)S(1)} %get-tuple-element.62), channel_id=1, source_target_pairs={{0,12},{1,13},{2,14},{3,15},{4,8},{5,9},{6,10},{7,11},{8,4},{9,5},... | collective-permute-start | bytes 196616 | tf_op jit(solution)/shard_map/ppermute | solution.py:351
  69.1 1.1 %collective-permute-start.21 = (bf16[8,4096]{1,0:T(8,128)(2,1)S(1)}, bf16[8,4096]{1,0:T(8,128)(2,1)S(1)}, u32[]{:S(2)}, u32[]{:S(2)}) collective-permute-start(bf16[8,4096]{1,0:T(8,128)(2,1)S(1)} %get-tuple-element.63), channel_id=1, source_target_pairs={{0,13},{1,12},{2,15},{3,14},{4,9},{5,8},{6,11},{7,10},{8,5},{9,4},... | collective-permute-start | bytes 196616 | tf_op jit(solution)/shard_map/ppermute | solution.py:351
  70.2 0.7 adapt.7
  70.9 2.3 %collective-permute-start.22 = (bf16[8,4096]{1,0:T(8,128)(2,1)S(1)}, bf16[8,4096]{1,0:T(8,128)(2,1)S(1)}, u32[]{:S(2)}, u32[]{:S(2)}) collective-permute-start(bf16[8,4096]{1,0:T(8,128)(2,1)S(1)} %get-tuple-element.64), channel_id=1, source_target_pairs={{0,14},{1,15},{2,12},{3,13},{4,10},{5,11},{6,8},{7,9},{8,6},{9,7},... | collective-permute-start | bytes 196616 | tf_op jit(solution)/shard_map/ppermute | solution.py:351
  73.2 2.6 %collective-permute-start.23 = (bf16[8,4096]{1,0:T(8,128)(2,1)S(1)}, bf16[8,4096]{1,0:T(8,128)(2,1)S(1)}, u32[]{:S(2)}, u32[]{:S(2)}) collective-permute-start(bf16[8,4096]{1,0:T(8,128)(2,1)S(1)} %get-tuple-element.65), channel_id=1, source_target_pairs={{0,15},{1,14},{2,13},{3,12},{4,11},{5,10},{6,9},{7,8},{8,7},{9,6},... | collective-permute-start | bytes 196616 | tf_op jit(solution)/shard_map/ppermute | solution.py:351
  75.9 0.6 collective-permute-start.28
  76.5 1.2 %collective-permute-start.29 = (bf16[8,4096]{1,0:T(8,128)(2,1)S(1)}, bf16[8,4096]{1,0:T(8,128)(2,1)S(1)}, u32[]{:S(2)}, u32[]{:S(2)}) collective-permute-start(bf16[8,4096]{1,0:T(8,128)(2,1)S(1)} %get-tuple-element.73), channel_id=1, source_target_pairs={{0,3},{1,2},{2,1},{3,0},{4,7},{5,6},{6,5},{7,4},{8,11},{9,10},{10,... | collective-permute-start | bytes 196616 | tf_op jit(solution)/shard_map/ppermute | solution.py:351
  77.7 0.9 collective-permute-done.22.refs_10_
  78.6 1.6 %collective-permute-done.23.refs_11_ = bf16[8,4096]{1,0:T(8,128)(2,1)S(1)} collective-permute-done((bf16[8,4096]{1,0:T(8,128)(2,1)S(1)}, bf16[8,4096]{1,0:T(8,128)(2,1)S(1)}, u32[]{:S(2)}, u32[]{:S(2)}) %collective-permute-start.23) | collective-permute-done | bytes 65568 | tf_op jit(solution)/shard_map/ppermute | solution.py:351
  80.2 1.6 %collective-permute-done.28.refs_13_ = bf16[8,4096]{1,0:T(8,128)(2,1)S(1)} collective-permute-done((bf16[8,4096]{1,0:T(8,128)(2,1)S(1)}, bf16[8,4096]{1,0:T(8,128)(2,1)S(1)}, u32[]{:S(2)}, u32[]{:S(2)}) %collective-permute-start.28) | collective-permute-done | bytes 65568 | tf_op jit(solution)/shard_map/ppermute | solution.py:351
  81.8 1.3 %collective-permute-done.29.refs_14_ = bf16[8,4096]{1,0:T(8,128)(2,1)S(1)} collective-permute-done((bf16[8,4096]{1,0:T(8,128)(2,1)S(1)}, bf16[8,4096]{1,0:T(8,128)(2,1)S(1)}, u32[]{:S(2)}, u32[]{:S(2)}) %collective-permute-start.29) | collective-permute-done | bytes 65568 | tf_op jit(solution)/shard_map/ppermute | solution.py:351
  83.1 4.4 %attend.1 = bf16[128,4096]{1,0:T(8,128)(2,1)} custom-call(bf16[8,4096]{1,0:T(8,128)(2,1)S(1)} %collective-permute-done.4.refs_0_, bf16[8,4096]{1,0:T(8,128)(2,1)S(1)} %collective-permute-done.5.refs_1_, bf16[8,4096]{1,0:T(8,128)(2,1)S(1)} %collective-permute-done.6.refs_2_, bf16[8,4096]{1,0:T(8,128)(2,1)S(1)} %collective-permute-done.7.refs_3_, ...), custom_call_target="tpu_custom_call" | custom-call | tf_op jit(solution)/shard_map/attend/pallas_call | solution.py:303
  (48 shorter events, 0.1 us)
Async XLA Ops:
  0.0 31.1 %copy-start.7 = (s32[128]{0:T(128)S(1)}, s32[128]{0:T(128)}, u32[]{:S(2)}) copy-start(s32[128]{0:T(128)} %param.11) | copy-start | bytes 1540
  0.0 31.4 %copy-start.2 = (bf16[128,4096]{1,0:T(8,128)(2,1)S(1)}, bf16[128,4096]{1,0:T(8,128)(2,1)}, u32[]{:S(2)}) copy-start(bf16[128,4096]{1,0:T(8,128)(2,1)} %base_ref.1) | copy-start | bytes 3145732
  3.9 14.2 %collective-permute-start = (bf16[8,8320]{1,0:T(8,128)(2,1)}, bf16[8,8320]{1,0:T(8,128)(2,1)S(1)}, u32[]{:S(2)}, u32[]{:S(2)}) collective-permute-start(bf16[8,8320]{1,0:T(8,128)(2,1)} %get-tuple-element.42), channel_id=1, source_target_pairs={{0,8},{1,9},{2,10},{3,11},{4,12},{5,13},{6,14},{7,15},{8,0},{9,1},... | collective-permute-start | bytes 399368 | tf_op jit(solution)/shard_map/ppermute | solution.py:351
  8.0 11.7 %collective-permute-start.1 = (bf16[8,8320]{1,0:T(8,128)(2,1)}, bf16[8,8320]{1,0:T(8,128)(2,1)S(1)}, u32[]{:S(2)}, u32[]{:S(2)}) collective-permute-start(bf16[8,8320]{1,0:T(8,128)(2,1)} %get-tuple-element.43), channel_id=1, source_target_pairs={{0,4},{1,5},{2,6},{3,7},{4,0},{5,1},{6,2},{7,3},{8,12},{9,13},{10,... | collective-permute-start | bytes 399368 | tf_op jit(solution)/shard_map/ppermute | solution.py:351
  9.5 10.5 %collective-permute-start.2 = (bf16[8,8320]{1,0:T(8,128)(2,1)}, bf16[8,8320]{1,0:T(8,128)(2,1)S(1)}, u32[]{:S(2)}, u32[]{:S(2)}) collective-permute-start(bf16[8,8320]{1,0:T(8,128)(2,1)} %get-tuple-element.44), channel_id=1, source_target_pairs={{0,9},{1,8},{2,11},{3,10},{4,13},{5,12},{6,15},{7,14},{8,1},{9,0},... | collective-permute-start | bytes 399368 | tf_op jit(solution)/shard_map/ppermute | solution.py:351
  9.5 12.7 %collective-permute-start.3 = (bf16[8,8320]{1,0:T(8,128)(2,1)}, bf16[8,8320]{1,0:T(8,128)(2,1)S(1)}, u32[]{:S(2)}, u32[]{:S(2)}) collective-permute-start(bf16[8,8320]{1,0:T(8,128)(2,1)} %get-tuple-element.45), channel_id=1, source_target_pairs={{0,5},{1,4},{2,7},{3,6},{4,1},{5,0},{6,3},{7,2},{8,13},{9,12},{10,... | collective-permute-start | bytes 399368 | tf_op jit(solution)/shard_map/ppermute | solution.py:351
  14.3 14.3 %collective-permute-start.8 = (bf16[8,8320]{1,0:T(8,128)(2,1)}, bf16[8,8320]{1,0:T(8,128)(2,1)S(1)}, u32[]{:S(2)}, u32[]{:S(2)}) collective-permute-start(bf16[8,8320]{1,0:T(8,128)(2,1)} %get-tuple-element.50), channel_id=1, source_target_pairs={{0,10},{1,11},{2,8},{3,9},{4,14},{5,15},{6,12},{7,13},{8,2},{9,3},... | collective-permute-start | bytes 399368 | tf_op jit(solution)/shard_map/ppermute | solution.py:351
  18.1 18.5 %collective-permute-start.9 = (bf16[8,8320]{1,0:T(8,128)(2,1)}, bf16[8,8320]{1,0:T(8,128)(2,1)S(1)}, u32[]{:S(2)}, u32[]{:S(2)}) collective-permute-start(bf16[8,8320]{1,0:T(8,128)(2,1)} %get-tuple-element.51), channel_id=1, source_target_pairs={{0,6},{1,7},{2,4},{3,5},{4,2},{5,3},{6,0},{7,1},{8,14},{9,15},{10,... | collective-permute-start | bytes 399368 | tf_op jit(solution)/shard_map/ppermute | solution.py:351
  19.7 17.5 %collective-permute-start.10 = (bf16[8,8320]{1,0:T(8,128)(2,1)}, bf16[8,8320]{1,0:T(8,128)(2,1)S(1)}, u32[]{:S(2)}, u32[]{:S(2)}) collective-permute-start(bf16[8,8320]{1,0:T(8,128)(2,1)} %get-tuple-element.52), channel_id=1, source_target_pairs={{0,11},{1,10},{2,9},{3,8},{4,15},{5,14},{6,13},{7,12},{8,3},{9,2},... | collective-permute-start | bytes 399368 | tf_op jit(solution)/shard_map/ppermute | solution.py:351
  20.0 21.4 %collective-permute-start.11 = (bf16[8,8320]{1,0:T(8,128)(2,1)}, bf16[8,8320]{1,0:T(8,128)(2,1)S(1)}, u32[]{:S(2)}, u32[]{:S(2)}) collective-permute-start(bf16[8,8320]{1,0:T(8,128)(2,1)} %get-tuple-element.53), channel_id=1, source_target_pairs={{0,7},{1,6},{2,5},{3,4},{4,3},{5,2},{6,1},{7,0},{8,15},{9,14},{10,... | collective-permute-start | bytes 399368 | tf_op jit(solution)/shard_map/ppermute | solution.py:351
  22.2 19.2 %collective-permute-start.16 = (bf16[8,8320]{1,0:T(8,128)(2,1)}, bf16[8,8320]{1,0:T(8,128)(2,1)S(1)}, u32[]{:S(2)}, u32[]{:S(2)}) collective-permute-start(bf16[8,8320]{1,0:T(8,128)(2,1)} %get-tuple-element.58), channel_id=1, source_target_pairs={{0,12},{1,13},{2,14},{3,15},{4,8},{5,9},{6,10},{7,11},{8,4},{9,5},... | collective-permute-start | bytes 399368 | tf_op jit(solution)/shard_map/ppermute | solution.py:351
  28.5 13.5 %collective-permute-start.17 = (bf16[8,8320]{1,0:T(8,128)(2,1)}, bf16[8,8320]{1,0:T(8,128)(2,1)S(1)}, u32[]{:S(2)}, u32[]{:S(2)}) collective-permute-start(bf16[8,8320]{1,0:T(8,128)(2,1)} %get-tuple-element.59), channel_id=1, source_target_pairs={{0,13},{1,12},{2,15},{3,14},{4,9},{5,8},{6,11},{7,10},{8,5},{9,4},... | collective-permute-start | bytes 399368 | tf_op jit(solution)/shard_map/ppermute | solution.py:351
  31.4 5.2 %copy-start.11 = (bf16[8,8320]{1,0:T(8,128)(2,1)S(1)}, bf16[8,8320]{1,0:T(8,128)(2,1)}, u32[]{:S(2)}) copy-start(bf16[8,8320]{1,0:T(8,128)(2,1)} %get-tuple-element.60) | copy-start | bytes 399364
  31.4 5.8 %copy-start.10 = (bf16[8,8320]{1,0:T(8,128)(2,1)S(1)}, bf16[8,8320]{1,0:T(8,128)(2,1)}, u32[]{:S(2)}) copy-start(bf16[8,8320]{1,0:T(8,128)(2,1)} %get-tuple-element.61) | copy-start | bytes 399364
  31.4 10.0 %copy-start.9 = (bf16[8,8320]{1,0:T(8,128)(2,1)S(1)}, bf16[8,8320]{1,0:T(8,128)(2,1)}, u32[]{:S(2)}) copy-start(bf16[8,8320]{1,0:T(8,128)(2,1)} %get-tuple-element.66) | copy-start | bytes 399364
  31.4 10.0 %copy-start.8 = (bf16[8,8320]{1,0:T(8,128)(2,1)S(1)}, bf16[8,8320]{1,0:T(8,128)(2,1)}, u32[]{:S(2)}) copy-start(bf16[8,8320]{1,0:T(8,128)(2,1)} %get-tuple-element.67) | copy-start | bytes 399364
  31.4 10.6 %copy-start.4 = (bf16[8,8320]{1,0:T(8,128)(2,1)S(1)}, bf16[8,8320]{1,0:T(8,128)(2,1)}, u32[]{:S(2)}) copy-start(bf16[8,8320]{1,0:T(8,128)(2,1)} %get-tuple-element.68.refs_0_) | copy-start | bytes 399364
  36.6 9.3 %collective-permute-start.18 = (bf16[8,8320]{1,0:T(8,128)(2,1)S(1)}, bf16[8,8320]{1,0:T(8,128)(2,1)S(1)}, u32[]{:S(2)}, u32[]{:S(2)}) collective-permute-start(bf16[8,8320]{1,0:T(8,128)(2,1)S(1)} %copy-done.11), channel_id=1, source_target_pairs={{0,14},{1,15},{2,12},{3,13},{4,10},{5,11},{6,8},{7,9},{8,6},{9,7},... | collective-permute-start | bytes 399368 | tf_op jit(solution)/shard_map/ppermute | solution.py:351
  37.2 18.2 %collective-permute-start.19 = (bf16[8,8320]{1,0:T(8,128)(2,1)S(1)}, bf16[8,8320]{1,0:T(8,128)(2,1)S(1)}, u32[]{:S(2)}, u32[]{:S(2)}) collective-permute-start(bf16[8,8320]{1,0:T(8,128)(2,1)S(1)} %copy-done.10), channel_id=1, source_target_pairs={{0,15},{1,14},{2,13},{3,12},{4,11},{5,10},{6,9},{7,8},{8,7},{9,6},... | collective-permute-start | bytes 399368 | tf_op jit(solution)/shard_map/ppermute | solution.py:351
  41.4 14.0 %collective-permute-start.24 = (bf16[8,8320]{1,0:T(8,128)(2,1)S(1)}, bf16[8,8320]{1,0:T(8,128)(2,1)S(1)}, u32[]{:S(2)}, u32[]{:S(2)}) collective-permute-start(bf16[8,8320]{1,0:T(8,128)(2,1)S(1)} %copy-done.9), channel_id=1, source_target_pairs={{0,1},{1,0},{2,3},{3,2},{4,5},{5,4},{6,7},{7,6},{8,9},{9,8},{10,11... | collective-permute-start | bytes 399368 | tf_op jit(solution)/shard_map/ppermute | solution.py:351
  41.4 16.3 %collective-permute-start.25 = (bf16[8,8320]{1,0:T(8,128)(2,1)S(1)}, bf16[8,8320]{1,0:T(8,128)(2,1)S(1)}, u32[]{:S(2)}, u32[]{:S(2)}) collective-permute-start(bf16[8,8320]{1,0:T(8,128)(2,1)S(1)} %copy-done.8), channel_id=1, source_target_pairs={{0,2},{1,3},{2,0},{3,1},{4,6},{5,7},{6,4},{7,5},{8,10},{9,11},{10,... | collective-permute-start | bytes 399368 | tf_op jit(solution)/shard_map/ppermute | solution.py:351
  42.0 1.6 %copy-start = (bf16[8192,128]{1,0:T(8,128)(2,1)S(1)}, bf16[8192,128]{1,0:T(8,128)(2,1)}, u32[]{:S(2)}) copy-start(bf16[8192,128]{1,0:T(8,128)(2,1)} %refs_4_.7) | copy-start | bytes 6291460
  42.0 1.9 %copy-start.1 = (bf16[128,4096]{1,0:T(8,128)(2,1)S(1)}, bf16[128,4096]{1,0:T(8,128)(2,1)}, u32[]{:S(2)}) copy-start(bf16[128,4096]{1,0:T(8,128)(2,1)} %refs_5_.7) | copy-start | bytes 3145732
  42.0 17.8 %collective-permute-start.26 = (bf16[8,8320]{1,0:T(8,128)(2,1)S(1)}, bf16[8,8320]{1,0:T(8,128)(2,1)S(1)}, u32[]{:S(2)}, u32[]{:S(2)}) collective-permute-start(bf16[8,8320]{1,0:T(8,128)(2,1)S(1)} %hold.1), channel_id=1, source_target_pairs={{0,3},{1,2},{2,1},{3,0},{4,7},{5,6},{6,5},{7,4},{8,11},{9,10},{10,... | collective-permute-start | bytes 399368 | tf_op jit(solution)/shard_map/ppermute | solution.py:351
  45.2 25.0 %copy-start.3 = (bf16[8,8320]{1,0:T(8,128)(2,1)S(1)}, bf16[8,8320]{1,0:T(8,128)(2,1)}, u32[]{:S(2)}) copy-start(bf16[8,8320]{1,0:T(8,128)(2,1)} %get-tuple-element.70.refs_3_) | copy-start | bytes 399364
  45.9 18.0 %collective-permute-start.4 = (bf16[8,4096]{1,0:T(8,128)(2,1)S(1)}, bf16[8,4096]{1,0:T(8,128)(2,1)S(1)}, u32[]{:S(2)}, u32[]{:S(2)}) collective-permute-start(bf16[8,4096]{1,0:T(8,128)(2,1)S(1)} %get-tuple-element.46), channel_id=1, source_target_pairs={{0,8},{1,9},{2,10},{3,11},{4,12},{5,13},{6,14},{7,15},{8,0},{9,1},... | collective-permute-start | bytes 196616 | tf_op jit(solution)/shard_map/ppermute | solution.py:351
  55.4 8.6 %collective-permute-start.5 = (bf16[8,4096]{1,0:T(8,128)(2,1)S(1)}, bf16[8,4096]{1,0:T(8,128)(2,1)S(1)}, u32[]{:S(2)}, u32[]{:S(2)}) collective-permute-start(bf16[8,4096]{1,0:T(8,128)(2,1)S(1)} %get-tuple-element.47), channel_id=1, source_target_pairs={{0,4},{1,5},{2,6},{3,7},{4,0},{5,1},{6,2},{7,3},{8,12},{9,13},{10,... | collective-permute-start | bytes 196616 | tf_op jit(solution)/shard_map/ppermute | solution.py:351
  55.4 9.4 %collective-permute-start.6 = (bf16[8,4096]{1,0:T(8,128)(2,1)S(1)}, bf16[8,4096]{1,0:T(8,128)(2,1)S(1)}, u32[]{:S(2)}, u32[]{:S(2)}) collective-permute-start(bf16[8,4096]{1,0:T(8,128)(2,1)S(1)} %get-tuple-element.48), channel_id=1, source_target_pairs={{0,9},{1,8},{2,11},{3,10},{4,13},{5,12},{6,15},{7,14},{8,1},{9,0},... | collective-permute-start | bytes 196616 | tf_op jit(solution)/shard_map/ppermute | solution.py:351
  57.8 9.3 %collective-permute-start.7 = (bf16[8,4096]{1,0:T(8,128)(2,1)S(1)}, bf16[8,4096]{1,0:T(8,128)(2,1)S(1)}, u32[]{:S(2)}, u32[]{:S(2)}) collective-permute-start(bf16[8,4096]{1,0:T(8,128)(2,1)S(1)} %get-tuple-element.49), channel_id=1, source_target_pairs={{0,5},{1,4},{2,7},{3,6},{4,1},{5,0},{6,3},{7,2},{8,13},{9,12},{10,... | collective-permute-start | bytes 196616 | tf_op jit(solution)/shard_map/ppermute | solution.py:351
  59.8 9.3 %collective-permute-start.12 = (bf16[8,4096]{1,0:T(8,128)(2,1)S(1)}, bf16[8,4096]{1,0:T(8,128)(2,1)S(1)}, u32[]{:S(2)}, u32[]{:S(2)}) collective-permute-start(bf16[8,4096]{1,0:T(8,128)(2,1)S(1)} %get-tuple-element.54), channel_id=1, source_target_pairs={{0,10},{1,11},{2,8},{3,9},{4,14},{5,15},{6,12},{7,13},{8,2},{9,3},... | collective-permute-start | bytes 196616 | tf_op jit(solution)/shard_map/ppermute | solution.py:351
  63.9 19.2 %copy-start.5 = (bf16[96,128]{1,0:T(8,128)(2,1)S(1)}, bf16[96,128]{1,0:T(8,128)(2,1)}, u32[]{:S(2)}) copy-start(bf16[96,128]{1,0:T(8,128)(2,1)} %get-tuple-element.76.refs_17_) | copy-start | bytes 73732
  63.9 19.2 %copy-start.6 = (bf16[32,128]{1,0:T(8,128)(2,1)S(1)}, bf16[32,128]{1,0:T(8,128)(2,1)}, u32[]{:S(2)}) copy-start(bf16[32,128]{1,0:T(8,128)(2,1)} %get-tuple-element.75.refs_16_) | copy-start | bytes 24580
  63.9 7.0 %collective-permute-start.13 = (bf16[8,4096]{1,0:T(8,128)(2,1)S(1)}, bf16[8,4096]{1,0:T(8,128)(2,1)S(1)}, u32[]{:S(2)}, u32[]{:S(2)}) collective-permute-start(bf16[8,4096]{1,0:T(8,128)(2,1)S(1)} %get-tuple-element.55), channel_id=1, source_target_pairs={{0,6},{1,7},{2,4},{3,5},{4,2},{5,3},{6,0},{7,1},{8,14},{9,15},{10,... | collective-permute-start | bytes 196616 | tf_op jit(solution)/shard_map/ppermute | solution.py:351
  64.0 9.3 %collective-permute-start.14 = (bf16[8,4096]{1,0:T(8,128)(2,1)S(1)}, bf16[8,4096]{1,0:T(8,128)(2,1)S(1)}, u32[]{:S(2)}, u32[]{:S(2)}) collective-permute-start(bf16[8,4096]{1,0:T(8,128)(2,1)S(1)} %get-tuple-element.56), channel_id=1, source_target_pairs={{0,11},{1,10},{2,9},{3,8},{4,15},{5,14},{6,13},{7,12},{8,3},{9,2},... | collective-permute-start | bytes 196616 | tf_op jit(solution)/shard_map/ppermute | solution.py:351
  64.8 11.0 %collective-permute-start.15 = (bf16[8,4096]{1,0:T(8,128)(2,1)S(1)}, bf16[8,4096]{1,0:T(8,128)(2,1)S(1)}, u32[]{:S(2)}, u32[]{:S(2)}) collective-permute-start(bf16[8,4096]{1,0:T(8,128)(2,1)S(1)} %get-tuple-element.57), channel_id=1, source_target_pairs={{0,7},{1,6},{2,5},{3,4},{4,3},{5,2},{6,1},{7,0},{8,15},{9,14},{10,... | collective-permute-start | bytes 196616 | tf_op jit(solution)/shard_map/ppermute | solution.py:351
  67.1 8.8 %collective-permute-start.20 = (bf16[8,4096]{1,0:T(8,128)(2,1)S(1)}, bf16[8,4096]{1,0:T(8,128)(2,1)S(1)}, u32[]{:S(2)}, u32[]{:S(2)}) collective-permute-start(bf16[8,4096]{1,0:T(8,128)(2,1)S(1)} %get-tuple-element.62), channel_id=1, source_target_pairs={{0,12},{1,13},{2,14},{3,15},{4,8},{5,9},{6,10},{7,11},{8,4},{9,5},... | collective-permute-start | bytes 196616 | tf_op jit(solution)/shard_map/ppermute | solution.py:351
  69.1 7.4 %collective-permute-start.21 = (bf16[8,4096]{1,0:T(8,128)(2,1)S(1)}, bf16[8,4096]{1,0:T(8,128)(2,1)S(1)}, u32[]{:S(2)}, u32[]{:S(2)}) collective-permute-start(bf16[8,4096]{1,0:T(8,128)(2,1)S(1)} %get-tuple-element.63), channel_id=1, source_target_pairs={{0,13},{1,12},{2,15},{3,14},{4,9},{5,8},{6,11},{7,10},{8,5},{9,4},... | collective-permute-start | bytes 196616 | tf_op jit(solution)/shard_map/ppermute | solution.py:351
  70.9 7.7 %collective-permute-start.22 = (bf16[8,4096]{1,0:T(8,128)(2,1)S(1)}, bf16[8,4096]{1,0:T(8,128)(2,1)S(1)}, u32[]{:S(2)}, u32[]{:S(2)}) collective-permute-start(bf16[8,4096]{1,0:T(8,128)(2,1)S(1)} %get-tuple-element.64), channel_id=1, source_target_pairs={{0,14},{1,15},{2,12},{3,13},{4,10},{5,11},{6,8},{7,9},{8,6},{9,7},... | collective-permute-start | bytes 196616 | tf_op jit(solution)/shard_map/ppermute | solution.py:351
  73.2 7.0 %collective-permute-start.23 = (bf16[8,4096]{1,0:T(8,128)(2,1)S(1)}, bf16[8,4096]{1,0:T(8,128)(2,1)S(1)}, u32[]{:S(2)}, u32[]{:S(2)}) collective-permute-start(bf16[8,4096]{1,0:T(8,128)(2,1)S(1)} %get-tuple-element.65), channel_id=1, source_target_pairs={{0,15},{1,14},{2,13},{3,12},{4,11},{5,10},{6,9},{7,8},{8,7},{9,6},... | collective-permute-start | bytes 196616 | tf_op jit(solution)/shard_map/ppermute | solution.py:351
  75.9 4.3 %collective-permute-start.27 = (bf16[8,4096]{1,0:T(8,128)(2,1)S(1)}, bf16[8,4096]{1,0:T(8,128)(2,1)S(1)}, u32[]{:S(2)}, u32[]{:S(2)}) collective-permute-start(bf16[8,4096]{1,0:T(8,128)(2,1)S(1)} %get-tuple-element.71), channel_id=1, source_target_pairs={{0,1},{1,0},{2,3},{3,2},{4,5},{5,4},{6,7},{7,6},{8,9},{9,8},{10,11... | collective-permute-start | bytes 196616 | tf_op jit(solution)/shard_map/ppermute | solution.py:351
  75.9 5.9 %collective-permute-start.28 = (bf16[8,4096]{1,0:T(8,128)(2,1)S(1)}, bf16[8,4096]{1,0:T(8,128)(2,1)S(1)}, u32[]{:S(2)}, u32[]{:S(2)}) collective-permute-start(bf16[8,4096]{1,0:T(8,128)(2,1)S(1)} %get-tuple-element.72), channel_id=1, source_target_pairs={{0,2},{1,3},{2,0},{3,1},{4,6},{5,7},{6,4},{7,5},{8,10},{9,11},{10,... | collective-permute-start | bytes 196616 | tf_op jit(solution)/shard_map/ppermute | solution.py:351
  76.5 6.6 %collective-permute-start.29 = (bf16[8,4096]{1,0:T(8,128)(2,1)S(1)}, bf16[8,4096]{1,0:T(8,128)(2,1)S(1)}, u32[]{:S(2)}, u32[]{:S(2)}) collective-permute-start(bf16[8,4096]{1,0:T(8,128)(2,1)S(1)} %get-tuple-element.73), channel_id=1, source_target_pairs={{0,3},{1,2},{2,1},{3,0},{4,7},{5,6},{6,5},{7,4},{8,11},{9,10},{10,... | collective-permute-start | bytes 196616 | tf_op jit(solution)/shard_map/ppermute | solution.py:351

commit v25 on v22

--- a/solution.py
+++ b/solution.py
@@ -14,7 +14,7 @@
 SCALE = 2.0
 ROWS_STEP = 8
 PREP_STEPS = 4
-GROUPS = 4
+GROUPS = 8
 HELD = 13
 FIRST = 4
 MOST_PERMUTES = 32

time: 86.9 us -> 88.7 us (1.021)
  Pallas kernels: 20.6 us -> 23 us
    pallas_call x4 -> x8, Pallas kernels: 2.74 us -> 5.06 us  [adapt(): pl.pallas_call(functools.partial(adapt_kernel, count), in_specs=[pl.Block...]
  transfers between devices with their start and end apart: 30 -> 30, of which waited for: 5 -> 3; matrix products, arithmetic and copies ran while one was open for 0% -> 0% of each run, Pallas kernels for 14% -> 17%
where the time goes in v25:
time: 88.7 us; the launch traced here: 88.5 us
  starting transfers between devices  56.2 us (63%)
  Pallas kernels  23 us (26%)
  waiting for transfers between devices  8.84 us (10%)
    ppermute x30, starting transfers between devices, permutes(): lax.ppermute(message, 'owner', [(i, i ^ s) for i in range(owners)])  56.2 us
    ppermute x30, waiting for transfers between devices, permutes(): lax.ppermute(message, 'owner', [(i, i ^ s) for i in range(owners)])  8.84 us
    pallas_call x2, Pallas kernels, pack(): pl.pallas_call(functools.partial(pack_kernel, which, owners, slot_count,...  8.28 us
    pallas_call x1, Pallas kernels, prep(): pl.pallas_call(functools.partial(prep_kernel, group), grid=(steps,), in_s...  5.19 us
    pallas_call x8, Pallas kernels, adapt(): pl.pallas_call(functools.partial(adapt_kernel, count), in_specs=[pl.Block...  5.06 us
    pallas_call x1, Pallas kernels, attend(): pl.pallas_call(functools.partial(attend_kernel, group, context, len(retur...  4.47 us
  transfers between devices with their start and end apart: 30, of which 3 were waited for; matrix products, arithmetic and copies ran while one was open for 0% of the time, Pallas kernels for 17%

profile of v25, /device:TPU:0, one launch (start us, length us, event | category | flops | bytes accessed | tf_op | source)
XLA Modules:
  0.0 88.5 jit_solution(6359954032376666130)
XLA Ops:
  0.0 3.9 %pack.2 = (bf16[32,128]{1,0:T(8,128)(2,1)}, bf16[8,8320]{1,0:T(8,128)(2,1)}, bf16[8,8320]{1,0:T(8,128)(2,1)}, bf16[8,8320]{1,0:T(8,128)(2,1)}, bf16[8,8320]{1,0:T(8,128)(2,1)}) custom-call(s32[1,32]{1,0:T(1,128)} %bitcast.2, s32[1,128]{1,0:T(1,128)} %bitcast.4, bf16[128,8192]{1,0:T(8,128)(2,1)} %hidden_hbm.3), custom_call_target="tpu_custom_call" | custom-call | tf_op jit(solution)/shard_map/pack/pallas_call | solution.py:96
  3.9 4.1 %collective-permute-start = (bf16[8,8320]{1,0:T(8,128)(2,1)}, bf16[8,8320]{1,0:T(8,128)(2,1)S(1)}, u32[]{:S(2)}, u32[]{:S(2)}) collective-permute-start(bf16[8,8320]{1,0:T(8,128)(2,1)} %get-tuple-element.42), channel_id=1, source_target_pairs={{0,8},{1,9},{2,10},{3,11},{4,12},{5,13},{6,14},{7,15},{8,0},{9,1},... | collective-permute-start | bytes 399368 | tf_op jit(solution)/shard_map/ppermute | solution.py:351
  8.0 1.6 %collective-permute-start.1 = (bf16[8,8320]{1,0:T(8,128)(2,1)}, bf16[8,8320]{1,0:T(8,128)(2,1)S(1)}, u32[]{:S(2)}, u32[]{:S(2)}) collective-permute-start(bf16[8,8320]{1,0:T(8,128)(2,1)} %get-tuple-element.43), channel_id=1, source_target_pairs={{0,4},{1,5},{2,6},{3,7},{4,0},{5,1},{6,2},{7,3},{8,12},{9,13},{10,... | collective-permute-start | bytes 399368 | tf_op jit(solution)/shard_map/ppermute | solution.py:351
  9.6 0.2 collective-permute-start.5
  9.8 4.4 %pack.3 = (bf16[96,128]{1,0:T(8,128)(2,1)}, bf16[8,8320]{1,0:T(8,128)(2,1)}, bf16[8,8320]{1,0:T(8,128)(2,1)}, bf16[8,8320]{1,0:T(8,128)(2,1)}, bf16[8,8320]{1,0:...) custom-call(s32[1,32]{1,0:T(1,128)} %bitcast.3, ...), custom_call_target="tpu_custom_call" | custom-call | tf_op jit(solution)/shard_map/pack/pallas_call | solution.py:96
  14.2 3.8 %collective-permute-start.8 = (bf16[8,8320]{1,0:T(8,128)(2,1)}, bf16[8,8320]{1,0:T(8,128)(2,1)S(1)}, u32[]{:S(2)}, u32[]{:S(2)}) collective-permute-start(bf16[8,8320]{1,0:T(8,128)(2,1)} %get-tuple-element.50), channel_id=1, source_target_pairs={{0,10},{1,11},{2,8},{3,9},{4,14},{5,15},{6,12},{7,13},{8,2},{9,3},... | collective-permute-start | bytes 399368 | tf_op jit(solution)/shard_map/ppermute | solution.py:351
  18.1 1.6 %collective-permute-start.9 = (bf16[8,8320]{1,0:T(8,128)(2,1)}, bf16[8,8320]{1,0:T(8,128)(2,1)S(1)}, u32[]{:S(2)}, u32[]{:S(2)}) collective-permute-start(bf16[8,8320]{1,0:T(8,128)(2,1)} %get-tuple-element.51), channel_id=1, source_target_pairs={{0,6},{1,7},{2,4},{3,5},{4,2},{5,3},{6,0},{7,1},{8,14},{9,15},{10,... | collective-permute-start | bytes 399368 | tf_op jit(solution)/shard_map/ppermute | solution.py:351
  19.6 0.0 collective-permute-done.1.refs_1_
  19.6 0.4 collective-permute-start.12
  20.0 2.2 %collective-permute-start.13 = (bf16[8,8320]{1,0:T(8,128)(2,1)}, bf16[8,8320]{1,0:T(8,128)(2,1)S(1)}, u32[]{:S(2)}, u32[]{:S(2)}) collective-permute-start(bf16[8,8320]{1,0:T(8,128)(2,1)} %get-tuple-element.55), channel_id=1, source_target_pairs={{0,7},{1,6},{2,5},{3,4},{4,3},{5,2},{6,1},{7,0},{8,15},{9,14},{10,... | collective-permute-start | bytes 399368 | tf_op jit(solution)/shard_map/ppermute | solution.py:351
  22.2 0.0 collective-permute-done.5.refs_1_
  22.2 2.6 %collective-permute-start.16 = (bf16[8,8320]{1,0:T(8,128)(2,1)}, bf16[8,8320]{1,0:T(8,128)(2,1)S(1)}, u32[]{:S(2)}, u32[]{:S(2)}) collective-permute-start(bf16[8,8320]{1,0:T(8,128)(2,1)} %get-tuple-element.58), channel_id=1, source_target_pairs={{0,12},{1,13},{2,14},{3,15},{4,8},{5,9},{6,10},{7,11},{8,4},{9,5},... | collective-permute-start | bytes 399368 | tf_op jit(solution)/shard_map/ppermute | solution.py:351
  24.8 3.8 %collective-permute-done.8.refs_0_ = bf16[8,8320]{1,0:T(8,128)(2,1)S(1)} collective-permute-done((bf16[8,8320]{1,0:T(8,128)(2,1)}, bf16[8,8320]{1,0:T(8,128)(2,1)S(1)}, u32[]{:S(2)}, u32[]{:S(2)}) %collective-permute-start.8) | collective-permute-done | bytes 133152 | tf_op jit(solution)/shard_map/ppermute | solution.py:351
  28.6 0.1 broadcast_in_dim.7
  28.6 0.1 broadcast_in_dim.8
  28.7 0.1 broadcast_in_dim.9.given_ref
  28.9 5.2 %prep.1 = (bf16[4,128,2048]{2,1,0:T(8,128)(2,1)S(1)}, bf16[4,92,192,128]{3,2,1,0:T(8,128)(2,1)}, s32[16,1,128]{2,1,0:T(1,128)S(1)}) custom-call(bf16[128,4096]{1,0:T(8,128)(2,1)S(1)} %copy-done.2, bf16[128,2,16,512]{3,2,1,0:T(8,128)(2,1)} %kv_ref.1, s32[16,1,128]{2,1,0:T(1,128)S(1)} %broadcast_in_dim.9.given_ref), custom_call_target="tpu_custom_call" | custom-call | tf_op jit(solution)/shard_map/prep/pallas_call | solution.py:184
  34.1 0.0 collective-permute-done.9.refs_1_
  34.1 3.3 %collective-permute-start.20 = (bf16[8,8320]{1,0:T(8,128)(2,1)S(1)}, bf16[8,8320]{1,0:T(8,128)(2,1)S(1)}, u32[]{:S(2)}, u32[]{:S(2)}) collective-permute-start(bf16[8,8320]{1,0:T(8,128)(2,1)S(1)} %copy-done.11), channel_id=1, source_target_pairs={{0,13},{1,12},{2,15},{3,14},{4,9},{5,8},{6,11},{7,10},{8,5},{9,4},... | collective-permute-start | bytes 399368 | tf_op jit(solution)/shard_map/ppermute | solution.py:351
  37.4 0.0 collective-permute-done.12.refs_0_
  37.4 0.5 collective-permute-start.21
  37.9 0.0 collective-permute-done.13.refs_1_
  37.9 1.6 %collective-permute-start.24 = (bf16[8,8320]{1,0:T(8,128)(2,1)S(1)}, bf16[8,8320]{1,0:T(8,128)(2,1)S(1)}, u32[]{:S(2)}, u32[]{:S(2)}) collective-permute-start(bf16[8,8320]{1,0:T(8,128)(2,1)S(1)} %copy-done.9), channel_id=1, source_target_pairs={{0,14},{1,15},{2,12},{3,13},{4,10},{5,11},{6,8},{7,9},{8,6},{9,7},... | collective-permute-start | bytes 399368 | tf_op jit(solution)/shard_map/ppermute | solution.py:351
  39.5 2.2 %collective-permute-start.28 = (bf16[8,8320]{1,0:T(8,128)(2,1)S(1)}, bf16[8,8320]{1,0:T(8,128)(2,1)S(1)}, u32[]{:S(2)}, u32[]{:S(2)}) collective-permute-start(bf16[8,8320]{1,0:T(8,128)(2,1)S(1)} %copy-done.8), channel_id=1, source_target_pairs={{0,15},{1,14},{2,13},{3,12},{4,11},{5,10},{6,9},{7,8},{8,7},{9,6},... | collective-permute-start | bytes 399368 | tf_op jit(solution)/shard_map/ppermute | solution.py:351
  41.7 2.2 %collective-permute-start.25 = (bf16[8,8320]{1,0:T(8,128)(2,1)S(1)}, bf16[8,8320]{1,0:T(8,128)(2,1)S(1)}, u32[]{:S(2)}, u32[]{:S(2)}) collective-permute-start(bf16[8,8320]{1,0:T(8,128)(2,1)S(1)} %hold.1), channel_id=1, source_target_pairs={{0,3},{1,2},{2,1},{3,0},{4,7},{5,6},{6,5},{7,4},{8,11},{9,10},{10,... | collective-permute-start | bytes 399368 | tf_op jit(solution)/shard_map/ppermute | solution.py:351
  43.9 0.6 adapt.8
  44.6 0.6 adapt.9
  45.2 0.6 adapt.10
  45.8 5.6 %collective-permute-start.2 = (bf16[8,4096]{1,0:T(8,128)(2,1)S(1)}, bf16[8,4096]{1,0:T(8,128)(2,1)S(1)}, u32[]{:S(2)}, u32[]{:S(2)}) collective-permute-start(bf16[8,4096]{1,0:T(8,128)(2,1)S(1)} %get-tuple-element.44), channel_id=1, source_target_pairs={{0,8},{1,9},{2,10},{3,11},{4,12},{5,13},{6,14},{7,15},{8,0},{9,1},... | collective-permute-start | bytes 196616 | tf_op jit(solution)/shard_map/ppermute | solution.py:351
  51.4 3.4 %collective-permute-start.6 = (bf16[8,4096]{1,0:T(8,128)(2,1)S(1)}, bf16[8,4096]{1,0:T(8,128)(2,1)S(1)}, u32[]{:S(2)}, u32[]{:S(2)}) collective-permute-start(bf16[8,4096]{1,0:T(8,128)(2,1)S(1)} %get-tuple-element.48), channel_id=1, source_target_pairs={{0,9},{1,8},{2,11},{3,10},{4,13},{5,12},{6,15},{7,14},{8,1},{9,0},... | collective-permute-start | bytes 196616 | tf_op jit(solution)/shard_map/ppermute | solution.py:351
  54.9 4.2 %collective-permute-start.7 = (bf16[8,4096]{1,0:T(8,128)(2,1)S(1)}, bf16[8,4096]{1,0:T(8,128)(2,1)S(1)}, u32[]{:S(2)}, u32[]{:S(2)}) collective-permute-start(bf16[8,4096]{1,0:T(8,128)(2,1)S(1)} %get-tuple-element.49), channel_id=1, source_target_pairs={{0,5},{1,4},{2,7},{3,6},{4,1},{5,0},{6,3},{7,2},{8,13},{9,12},{10,... | collective-permute-start | bytes 196616 | tf_op jit(solution)/shard_map/ppermute | solution.py:351
  59.1 0.4 collective-permute-start.10
  59.4 0.6 adapt.11
  60.0 0.6 adapt.12
  60.7 4.1 %collective-permute-start.11 = (bf16[8,4096]{1,0:T(8,128)(2,1)S(1)}, bf16[8,4096]{1,0:T(8,128)(2,1)S(1)}, u32[]{:S(2)}, u32[]{:S(2)}) collective-permute-start(bf16[8,4096]{1,0:T(8,128)(2,1)S(1)} %get-tuple-element.53), channel_id=1, source_target_pairs={{0,6},{1,7},{2,4},{3,5},{4,2},{5,3},{6,0},{7,1},{8,14},{9,15},{10,... | collective-permute-start | bytes 196616 | tf_op jit(solution)/shard_map/ppermute | solution.py:351
  64.8 2.1 %collective-permute-start.15 = (bf16[8,4096]{1,0:T(8,128)(2,1)S(1)}, bf16[8,4096]{1,0:T(8,128)(2,1)S(1)}, u32[]{:S(2)}, u32[]{:S(2)}) collective-permute-start(bf16[8,4096]{1,0:T(8,128)(2,1)S(1)} %get-tuple-element.57), channel_id=1, source_target_pairs={{0,7},{1,6},{2,5},{3,4},{4,3},{5,2},{6,1},{7,0},{8,15},{9,14},{10,... | collective-permute-start | bytes 196616 | tf_op jit(solution)/shard_map/ppermute | solution.py:351
  66.9 2.9 %collective-permute-start.18 = (bf16[8,4096]{1,0:T(8,128)(2,1)S(1)}, bf16[8,4096]{1,0:T(8,128)(2,1)S(1)}, u32[]{:S(2)}, u32[]{:S(2)}) collective-permute-start(bf16[8,4096]{1,0:T(8,128)(2,1)S(1)} %get-tuple-element.60), channel_id=1, source_target_pairs={{0,12},{1,13},{2,14},{3,15},{4,8},{5,9},{6,10},{7,11},{8,4},{9,5},... | collective-permute-start | bytes 196616 | tf_op jit(solution)/shard_map/ppermute | solution.py:351
  69.8 0.6 adapt.13
  70.4 0.6 adapt.15
  71.1 0.6 adapt.14
  71.7 1.1 %collective-permute-start.22 = (bf16[8,4096]{1,0:T(8,128)(2,1)S(1)}, bf16[8,4096]{1,0:T(8,128)(2,1)S(1)}, u32[]{:S(2)}, u32[]{:S(2)}) collective-permute-start(bf16[8,4096]{1,0:T(8,128)(2,1)S(1)} %get-tuple-element.64), channel_id=1, source_target_pairs={{0,13},{1,12},{2,15},{3,14},{4,9},{5,8},{6,11},{7,10},{8,5},{9,4},... | collective-permute-start | bytes 196616 | tf_op jit(solution)/shard_map/ppermute | solution.py:351
  72.8 0.6 collective-permute-start.23
  73.4 3.1 %collective-permute-start.29 = (bf16[8,4096]{1,0:T(8,128)(2,1)S(1)}, bf16[8,4096]{1,0:T(8,128)(2,1)S(1)}, u32[]{:S(2)}, u32[]{:S(2)}) collective-permute-start(bf16[8,4096]{1,0:T(8,128)(2,1)S(1)} %get-tuple-element.73), channel_id=1, source_target_pairs={{0,15},{1,14},{2,13},{3,12},{4,11},{5,10},{6,9},{7,8},{8,7},{9,6},... | collective-permute-start | bytes 196616 | tf_op jit(solution)/shard_map/ppermute | solution.py:351
  76.5 1.0 %collective-permute-start.26 = (bf16[8,4096]{1,0:T(8,128)(2,1)S(1)}, bf16[8,4096]{1,0:T(8,128)(2,1)S(1)}, u32[]{:S(2)}, u32[]{:S(2)}) collective-permute-start(bf16[8,4096]{1,0:T(8,128)(2,1)S(1)} %get-tuple-element.69), channel_id=1, source_target_pairs={{0,14},{1,15},{2,12},{3,13},{4,10},{5,11},{6,8},{7,9},{8,6},{9,7},... | collective-permute-start | bytes 196616 | tf_op jit(solution)/shard_map/ppermute | solution.py:351
  77.5 1.5 %collective-permute-start.27 = (bf16[8,4096]{1,0:T(8,128)(2,1)S(1)}, bf16[8,4096]{1,0:T(8,128)(2,1)S(1)}, u32[]{:S(2)}, u32[]{:S(2)}) collective-permute-start(bf16[8,4096]{1,0:T(8,128)(2,1)S(1)} %get-tuple-element.70), channel_id=1, source_target_pairs={{0,3},{1,2},{2,1},{3,0},{4,7},{5,6},{6,5},{7,4},{8,11},{9,10},{10,... | collective-permute-start | bytes 196616 | tf_op jit(solution)/shard_map/ppermute | solution.py:351
  79.0 1.5 %collective-permute-done.29.refs_14_ = bf16[8,4096]{1,0:T(8,128)(2,1)S(1)} collective-permute-done((bf16[8,4096]{1,0:T(8,128)(2,1)S(1)}, bf16[8,4096]{1,0:T(8,128)(2,1)S(1)}, u32[]{:S(2)}, u32[]{:S(2)}) %collective-permute-start.29) | collective-permute-done | bytes 65568 | tf_op jit(solution)/shard_map/ppermute | solution.py:351
  80.5 3.5 %collective-permute-done.26.refs_12_ = bf16[8,4096]{1,0:T(8,128)(2,1)S(1)} collective-permute-done((bf16[8,4096]{1,0:T(8,128)(2,1)S(1)}, bf16[8,4096]{1,0:T(8,128)(2,1)S(1)}, u32[]{:S(2)}, u32[]{:S(2)}) %collective-permute-start.26) | collective-permute-done | bytes 65568 | tf_op jit(solution)/shard_map/ppermute | solution.py:351
  84.0 4.5 %attend.1 = bf16[128,4096]{1,0:T(8,128)(2,1)} custom-call(bf16[8,4096]{1,0:T(8,128)(2,1)S(1)} %collective-permute-done.2.refs_0_, bf16[8,4096]{1,0:T(8,128)(2,1)S(1)} %collective-permute-done.3.refs_1_, bf16[8,4096]{1,0:T(8,128)(2,1)S(1)} %collective-permute-done.6.refs_2_, bf16[8,4096]{1,0:T(8,128)(2,1)S(1)} %collective-permute-done.7.refs_3_, ...), custom_call_target="tpu_custom_call" | custom-call | tf_op jit(solution)/shard_map/attend/pallas_call | solution.py:304
  (52 shorter events, 0.1 us)
Async XLA Ops:
  0.0 28.6 %copy-start.7 = (s32[128]{0:T(128)S(1)}, s32[128]{0:T(128)}, u32[]{:S(2)}) copy-start(s32[128]{0:T(128)} %param.11) | copy-start | bytes 1540
  0.0 28.8 %copy-start.2 = (bf16[128,4096]{1,0:T(8,128)(2,1)S(1)}, bf16[128,4096]{1,0:T(8,128)(2,1)}, u32[]{:S(2)}) copy-start(bf16[128,4096]{1,0:T(8,128)(2,1)} %base_ref.1) | copy-start | bytes 3145732
  3.9 14.2 %collective-permute-start = (bf16[8,8320]{1,0:T(8,128)(2,1)}, bf16[8,8320]{1,0:T(8,128)(2,1)S(1)}, u32[]{:S(2)}, u32[]{:S(2)}) collective-permute-start(bf16[8,8320]{1,0:T(8,128)(2,1)} %get-tuple-element.42), channel_id=1, source_target_pairs={{0,8},{1,9},{2,10},{3,11},{4,12},{5,13},{6,14},{7,15},{8,0},{9,1},... | collective-permute-start | bytes 399368 | tf_op jit(solution)/shard_map/ppermute | solution.py:351
  8.0 11.7 %collective-permute-start.1 = (bf16[8,8320]{1,0:T(8,128)(2,1)}, bf16[8,8320]{1,0:T(8,128)(2,1)S(1)}, u32[]{:S(2)}, u32[]{:S(2)}) collective-permute-start(bf16[8,8320]{1,0:T(8,128)(2,1)} %get-tuple-element.43), channel_id=1, source_target_pairs={{0,4},{1,5},{2,6},{3,7},{4,0},{5,1},{6,2},{7,3},{8,12},{9,13},{10,... | collective-permute-start | bytes 399368 | tf_op jit(solution)/shard_map/ppermute | solution.py:351
  9.6 10.4 %collective-permute-start.4 = (bf16[8,8320]{1,0:T(8,128)(2,1)}, bf16[8,8320]{1,0:T(8,128)(2,1)S(1)}, u32[]{:S(2)}, u32[]{:S(2)}) collective-permute-start(bf16[8,8320]{1,0:T(8,128)(2,1)} %get-tuple-element.46), channel_id=1, source_target_pairs={{0,9},{1,8},{2,11},{3,10},{4,13},{5,12},{6,15},{7,14},{8,1},{9,0},... | collective-permute-start | bytes 399368 | tf_op jit(solution)/shard_map/ppermute | solution.py:351
  9.6 12.7 %collective-permute-start.5 = (bf16[8,8320]{1,0:T(8,128)(2,1)}, bf16[8,8320]{1,0:T(8,128)(2,1)S(1)}, u32[]{:S(2)}, u32[]{:S(2)}) collective-permute-start(bf16[8,8320]{1,0:T(8,128)(2,1)} %get-tuple-element.47), channel_id=1, source_target_pairs={{0,5},{1,4},{2,7},{3,6},{4,1},{5,0},{6,3},{7,2},{8,13},{9,12},{10,... | collective-permute-start | bytes 399368 | tf_op jit(solution)/shard_map/ppermute | solution.py:351
  14.2 14.3 %collective-permute-start.8 = (bf16[8,8320]{1,0:T(8,128)(2,1)}, bf16[8,8320]{1,0:T(8,128)(2,1)S(1)}, u32[]{:S(2)}, u32[]{:S(2)}) collective-permute-start(bf16[8,8320]{1,0:T(8,128)(2,1)} %get-tuple-element.50), channel_id=1, source_target_pairs={{0,10},{1,11},{2,8},{3,9},{4,14},{5,15},{6,12},{7,13},{8,2},{9,3},... | collective-permute-start | bytes 399368 | tf_op jit(solution)/shard_map/ppermute | solution.py:351
  18.1 16.0 %collective-permute-start.9 = (bf16[8,8320]{1,0:T(8,128)(2,1)}, bf16[8,8320]{1,0:T(8,128)(2,1)S(1)}, u32[]{:S(2)}, u32[]{:S(2)}) collective-permute-start(bf16[8,8320]{1,0:T(8,128)(2,1)} %get-tuple-element.51), channel_id=1, source_target_pairs={{0,6},{1,7},{2,4},{3,5},{4,2},{5,3},{6,0},{7,1},{8,14},{9,15},{10,... | collective-permute-start | bytes 399368 | tf_op jit(solution)/shard_map/ppermute | solution.py:351
  19.6 17.7 %collective-permute-start.12 = (bf16[8,8320]{1,0:T(8,128)(2,1)}, bf16[8,8320]{1,0:T(8,128)(2,1)S(1)}, u32[]{:S(2)}, u32[]{:S(2)}) collective-permute-start(bf16[8,8320]{1,0:T(8,128)(2,1)} %get-tuple-element.54), channel_id=1, source_target_pairs={{0,11},{1,10},{2,9},{3,8},{4,15},{5,14},{6,13},{7,12},{8,3},{9,2},... | collective-permute-start | bytes 399368 | tf_op jit(solution)/shard_map/ppermute | solution.py:351
  20.0 17.9 %collective-permute-start.13 = (bf16[8,8320]{1,0:T(8,128)(2,1)}, bf16[8,8320]{1,0:T(8,128)(2,1)S(1)}, u32[]{:S(2)}, u32[]{:S(2)}) collective-permute-start(bf16[8,8320]{1,0:T(8,128)(2,1)} %get-tuple-element.55), channel_id=1, source_target_pairs={{0,7},{1,6},{2,5},{3,4},{4,3},{5,2},{6,1},{7,0},{8,15},{9,14},{10,... | collective-permute-start | bytes 399368 | tf_op jit(solution)/shard_map/ppermute | solution.py:351
  22.2 17.3 %collective-permute-start.16 = (bf16[8,8320]{1,0:T(8,128)(2,1)}, bf16[8,8320]{1,0:T(8,128)(2,1)S(1)}, u32[]{:S(2)}, u32[]{:S(2)}) collective-permute-start(bf16[8,8320]{1,0:T(8,128)(2,1)} %get-tuple-element.58), channel_id=1, source_target_pairs={{0,12},{1,13},{2,14},{3,15},{4,8},{5,9},{6,10},{7,11},{8,4},{9,5},... | collective-permute-start | bytes 399368 | tf_op jit(solution)/shard_map/ppermute | solution.py:351
  28.5 13.2 %collective-permute-start.17 = (bf16[8,8320]{1,0:T(8,128)(2,1)}, bf16[8,8320]{1,0:T(8,128)(2,1)S(1)}, u32[]{:S(2)}, u32[]{:S(2)}) collective-permute-start(bf16[8,8320]{1,0:T(8,128)(2,1)} %get-tuple-element.59), channel_id=1, source_target_pairs={{0,1},{1,0},{2,3},{3,2},{4,5},{5,4},{6,7},{7,6},{8,9},{9,8},{10,11... | collective-permute-start | bytes 399368 | tf_op jit(solution)/shard_map/ppermute | solution.py:351
  28.8 5.2 %copy-start.11 = (bf16[8,8320]{1,0:T(8,128)(2,1)S(1)}, bf16[8,8320]{1,0:T(8,128)(2,1)}, u32[]{:S(2)}) copy-start(bf16[8,8320]{1,0:T(8,128)(2,1)} %get-tuple-element.62) | copy-start | bytes 399364
  28.8 8.5 %copy-start.10 = (bf16[8,8320]{1,0:T(8,128)(2,1)S(1)}, bf16[8,8320]{1,0:T(8,128)(2,1)}, u32[]{:S(2)}) copy-start(bf16[8,8320]{1,0:T(8,128)(2,1)} %get-tuple-element.63) | copy-start | bytes 399364
  28.9 9.1 %copy-start.9 = (bf16[8,8320]{1,0:T(8,128)(2,1)S(1)}, bf16[8,8320]{1,0:T(8,128)(2,1)}, u32[]{:S(2)}) copy-start(bf16[8,8320]{1,0:T(8,128)(2,1)} %get-tuple-element.66) | copy-start | bytes 399364
  28.9 10.6 %copy-start.8 = (bf16[8,8320]{1,0:T(8,128)(2,1)S(1)}, bf16[8,8320]{1,0:T(8,128)(2,1)}, u32[]{:S(2)}) copy-start(bf16[8,8320]{1,0:T(8,128)(2,1)} %get-tuple-element.71) | copy-start | bytes 399364
  28.9 12.8 %copy-start.3 = (bf16[8,8320]{1,0:T(8,128)(2,1)S(1)}, bf16[8,8320]{1,0:T(8,128)(2,1)}, u32[]{:S(2)}) copy-start(bf16[8,8320]{1,0:T(8,128)(2,1)} %get-tuple-element.67.refs_0_) | copy-start | bytes 399364
  34.1 11.7 %collective-permute-start.20 = (bf16[8,8320]{1,0:T(8,128)(2,1)S(1)}, bf16[8,8320]{1,0:T(8,128)(2,1)S(1)}, u32[]{:S(2)}, u32[]{:S(2)}) collective-permute-start(bf16[8,8320]{1,0:T(8,128)(2,1)S(1)} %copy-done.11), channel_id=1, source_target_pairs={{0,13},{1,12},{2,15},{3,14},{4,9},{5,8},{6,11},{7,10},{8,5},{9,4},... | collective-permute-start | bytes 399368 | tf_op jit(solution)/shard_map/ppermute | solution.py:351
  37.4 14.0 %collective-permute-start.21 = (bf16[8,8320]{1,0:T(8,128)(2,1)S(1)}, bf16[8,8320]{1,0:T(8,128)(2,1)S(1)}, u32[]{:S(2)}, u32[]{:S(2)}) collective-permute-start(bf16[8,8320]{1,0:T(8,128)(2,1)S(1)} %copy-done.10), channel_id=1, source_target_pairs={{0,2},{1,3},{2,0},{3,1},{4,6},{5,7},{6,4},{7,5},{8,10},{9,11},{10,... | collective-permute-start | bytes 399368 | tf_op jit(solution)/shard_map/ppermute | solution.py:351
  37.9 13.5 %collective-permute-start.24 = (bf16[8,8320]{1,0:T(8,128)(2,1)S(1)}, bf16[8,8320]{1,0:T(8,128)(2,1)S(1)}, u32[]{:S(2)}, u32[]{:S(2)}) collective-permute-start(bf16[8,8320]{1,0:T(8,128)(2,1)S(1)} %copy-done.9), channel_id=1, source_target_pairs={{0,14},{1,15},{2,12},{3,13},{4,10},{5,11},{6,8},{7,9},{8,6},{9,7},... | collective-permute-start | bytes 399368 | tf_op jit(solution)/shard_map/ppermute | solution.py:351
  39.5 15.4 %collective-permute-start.28 = (bf16[8,8320]{1,0:T(8,128)(2,1)S(1)}, bf16[8,8320]{1,0:T(8,128)(2,1)S(1)}, u32[]{:S(2)}, u32[]{:S(2)}) collective-permute-start(bf16[8,8320]{1,0:T(8,128)(2,1)S(1)} %copy-done.8), channel_id=1, source_target_pairs={{0,15},{1,14},{2,13},{3,12},{4,11},{5,10},{6,9},{7,8},{8,7},{9,6},... | collective-permute-start | bytes 399368 | tf_op jit(solution)/shard_map/ppermute | solution.py:351
  41.7 2.2 %copy-start = (bf16[8192,128]{1,0:T(8,128)(2,1)S(1)}, bf16[8192,128]{1,0:T(8,128)(2,1)}, u32[]{:S(2)}) copy-start(bf16[8192,128]{1,0:T(8,128)(2,1)} %refs_2_.15) | copy-start | bytes 6291460
  41.7 2.2 %copy-start.1 = (bf16[128,4096]{1,0:T(8,128)(2,1)S(1)}, bf16[128,4096]{1,0:T(8,128)(2,1)}, u32[]{:S(2)}) copy-start(bf16[128,4096]{1,0:T(8,128)(2,1)} %refs_3_.15) | copy-start | bytes 3145732
  41.7 17.4 %collective-permute-start.25 = (bf16[8,8320]{1,0:T(8,128)(2,1)S(1)}, bf16[8,8320]{1,0:T(8,128)(2,1)S(1)}, u32[]{:S(2)}, u32[]{:S(2)}) collective-permute-start(bf16[8,8320]{1,0:T(8,128)(2,1)S(1)} %hold.1), channel_id=1, source_target_pairs={{0,3},{1,2},{2,1},{3,0},{4,7},{5,6},{6,5},{7,4},{8,11},{9,10},{10,... | collective-permute-start | bytes 399368 | tf_op jit(solution)/shard_map/ppermute | solution.py:351
  45.8 14.9 %collective-permute-start.2 = (bf16[8,4096]{1,0:T(8,128)(2,1)S(1)}, bf16[8,4096]{1,0:T(8,128)(2,1)S(1)}, u32[]{:S(2)}, u32[]{:S(2)}) collective-permute-start(bf16[8,4096]{1,0:T(8,128)(2,1)S(1)} %get-tuple-element.44), channel_id=1, source_target_pairs={{0,8},{1,9},{2,10},{3,11},{4,12},{5,13},{6,14},{7,15},{8,0},{9,1},... | collective-permute-start | bytes 196616 | tf_op jit(solution)/shard_map/ppermute | solution.py:351
  51.4 13.4 %collective-permute-start.3 = (bf16[8,4096]{1,0:T(8,128)(2,1)S(1)}, bf16[8,4096]{1,0:T(8,128)(2,1)S(1)}, u32[]{:S(2)}, u32[]{:S(2)}) collective-permute-start(bf16[8,4096]{1,0:T(8,128)(2,1)S(1)} %get-tuple-element.45), channel_id=1, source_target_pairs={{0,4},{1,5},{2,6},{3,7},{4,0},{5,1},{6,2},{7,3},{8,12},{9,13},{10,... | collective-permute-start | bytes 196616 | tf_op jit(solution)/shard_map/ppermute | solution.py:351
  51.4 13.4 %collective-permute-start.6 = (bf16[8,4096]{1,0:T(8,128)(2,1)S(1)}, bf16[8,4096]{1,0:T(8,128)(2,1)S(1)}, u32[]{:S(2)}, u32[]{:S(2)}) collective-permute-start(bf16[8,4096]{1,0:T(8,128)(2,1)S(1)} %get-tuple-element.48), channel_id=1, source_target_pairs={{0,9},{1,8},{2,11},{3,10},{4,13},{5,12},{6,15},{7,14},{8,1},{9,0},... | collective-permute-start | bytes 196616 | tf_op jit(solution)/shard_map/ppermute | solution.py:351
  54.9 12.0 %collective-permute-start.7 = (bf16[8,4096]{1,0:T(8,128)(2,1)S(1)}, bf16[8,4096]{1,0:T(8,128)(2,1)S(1)}, u32[]{:S(2)}, u32[]{:S(2)}) collective-permute-start(bf16[8,4096]{1,0:T(8,128)(2,1)S(1)} %get-tuple-element.49), channel_id=1, source_target_pairs={{0,5},{1,4},{2,7},{3,6},{4,1},{5,0},{6,3},{7,2},{8,13},{9,12},{10,... | collective-permute-start | bytes 196616 | tf_op jit(solution)/shard_map/ppermute | solution.py:351
  59.1 10.7 %collective-permute-start.10 = (bf16[8,4096]{1,0:T(8,128)(2,1)S(1)}, bf16[8,4096]{1,0:T(8,128)(2,1)S(1)}, u32[]{:S(2)}, u32[]{:S(2)}) collective-permute-start(bf16[8,4096]{1,0:T(8,128)(2,1)S(1)} %get-tuple-element.52), channel_id=1, source_target_pairs={{0,10},{1,11},{2,8},{3,9},{4,14},{5,15},{6,12},{7,13},{8,2},{9,3},... | collective-permute-start | bytes 196616 | tf_op jit(solution)/shard_map/ppermute | solution.py:351
  60.7 9.8 %copy-start.4 = (bf16[8,8320]{1,0:T(8,128)(2,1)S(1)}, bf16[8,8320]{1,0:T(8,128)(2,1)}, u32[]{:S(2)}) copy-start(bf16[8,8320]{1,0:T(8,128)(2,1)} %get-tuple-element.72.refs_1_) | copy-start | bytes 399364
  60.7 11.0 %collective-permute-start.11 = (bf16[8,4096]{1,0:T(8,128)(2,1)S(1)}, bf16[8,4096]{1,0:T(8,128)(2,1)S(1)}, u32[]{:S(2)}, u32[]{:S(2)}) collective-permute-start(bf16[8,4096]{1,0:T(8,128)(2,1)S(1)} %get-tuple-element.53), channel_id=1, source_target_pairs={{0,6},{1,7},{2,4},{3,5},{4,2},{5,3},{6,0},{7,1},{8,14},{9,15},{10,... | collective-permute-start | bytes 196616 | tf_op jit(solution)/shard_map/ppermute | solution.py:351
  64.8 8.0 %collective-permute-start.14 = (bf16[8,4096]{1,0:T(8,128)(2,1)S(1)}, bf16[8,4096]{1,0:T(8,128)(2,1)S(1)}, u32[]{:S(2)}, u32[]{:S(2)}) collective-permute-start(bf16[8,4096]{1,0:T(8,128)(2,1)S(1)} %get-tuple-element.56), channel_id=1, source_target_pairs={{0,11},{1,10},{2,9},{3,8},{4,15},{5,14},{6,13},{7,12},{8,3},{9,2},... | collective-permute-start | bytes 196616 | tf_op jit(solution)/shard_map/ppermute | solution.py:351
  64.8 8.6 %collective-permute-start.15 = (bf16[8,4096]{1,0:T(8,128)(2,1)S(1)}, bf16[8,4096]{1,0:T(8,128)(2,1)S(1)}, u32[]{:S(2)}, u32[]{:S(2)}) collective-permute-start(bf16[8,4096]{1,0:T(8,128)(2,1)S(1)} %get-tuple-element.57), channel_id=1, source_target_pairs={{0,7},{1,6},{2,5},{3,4},{4,3},{5,2},{6,1},{7,0},{8,15},{9,14},{10,... | collective-permute-start | bytes 196616 | tf_op jit(solution)/shard_map/ppermute | solution.py:351
  66.9 9.6 %collective-permute-start.18 = (bf16[8,4096]{1,0:T(8,128)(2,1)S(1)}, bf16[8,4096]{1,0:T(8,128)(2,1)S(1)}, u32[]{:S(2)}, u32[]{:S(2)}) collective-permute-start(bf16[8,4096]{1,0:T(8,128)(2,1)S(1)} %get-tuple-element.60), channel_id=1, source_target_pairs={{0,12},{1,13},{2,14},{3,15},{4,8},{5,9},{6,10},{7,11},{8,4},{9,5},... | collective-permute-start | bytes 196616 | tf_op jit(solution)/shard_map/ppermute | solution.py:351
  69.8 7.7 %collective-permute-start.19 = (bf16[8,4096]{1,0:T(8,128)(2,1)S(1)}, bf16[8,4096]{1,0:T(8,128)(2,1)S(1)}, u32[]{:S(2)}, u32[]{:S(2)}) collective-permute-start(bf16[8,4096]{1,0:T(8,128)(2,1)S(1)} %get-tuple-element.61), channel_id=1, source_target_pairs={{0,1},{1,0},{2,3},{3,2},{4,5},{5,4},{6,7},{7,6},{8,9},{9,8},{10,11... | collective-permute-start | bytes 196616 | tf_op jit(solution)/shard_map/ppermute | solution.py:351
  71.1 12.9 %copy-start.5 = (bf16[96,128]{1,0:T(8,128)(2,1)S(1)}, bf16[96,128]{1,0:T(8,128)(2,1)}, u32[]{:S(2)}) copy-start(bf16[96,128]{1,0:T(8,128)(2,1)} %get-tuple-element.76.refs_17_) | copy-start | bytes 73732
  71.1 12.9 %copy-start.6 = (bf16[32,128]{1,0:T(8,128)(2,1)S(1)}, bf16[32,128]{1,0:T(8,128)(2,1)}, u32[]{:S(2)}) copy-start(bf16[32,128]{1,0:T(8,128)(2,1)} %get-tuple-element.75.refs_16_) | copy-start | bytes 24580
  71.7 7.3 %collective-permute-start.22 = (bf16[8,4096]{1,0:T(8,128)(2,1)S(1)}, bf16[8,4096]{1,0:T(8,128)(2,1)S(1)}, u32[]{:S(2)}, u32[]{:S(2)}) collective-permute-start(bf16[8,4096]{1,0:T(8,128)(2,1)S(1)} %get-tuple-element.64), channel_id=1, source_target_pairs={{0,13},{1,12},{2,15},{3,14},{4,9},{5,8},{6,11},{7,10},{8,5},{9,4},... | collective-permute-start | bytes 196616 | tf_op jit(solution)/shard_map/ppermute | solution.py:351
  72.8 6.2 %collective-permute-start.23 = (bf16[8,4096]{1,0:T(8,128)(2,1)S(1)}, bf16[8,4096]{1,0:T(8,128)(2,1)S(1)}, u32[]{:S(2)}, u32[]{:S(2)}) collective-permute-start(bf16[8,4096]{1,0:T(8,128)(2,1)S(1)} %get-tuple-element.65), channel_id=1, source_target_pairs={{0,2},{1,3},{2,0},{3,1},{4,6},{5,7},{6,4},{7,5},{8,10},{9,11},{10,... | collective-permute-start | bytes 196616 | tf_op jit(solution)/shard_map/ppermute | solution.py:351
  73.4 7.1 %collective-permute-start.29 = (bf16[8,4096]{1,0:T(8,128)(2,1)S(1)}, bf16[8,4096]{1,0:T(8,128)(2,1)S(1)}, u32[]{:S(2)}, u32[]{:S(2)}) collective-permute-start(bf16[8,4096]{1,0:T(8,128)(2,1)S(1)} %get-tuple-element.73), channel_id=1, source_target_pairs={{0,15},{1,14},{2,13},{3,12},{4,11},{5,10},{6,9},{7,8},{8,7},{9,6},... | collective-permute-start | bytes 196616 | tf_op jit(solution)/shard_map/ppermute | solution.py:351
  76.5 7.5 %collective-permute-start.26 = (bf16[8,4096]{1,0:T(8,128)(2,1)S(1)}, bf16[8,4096]{1,0:T(8,128)(2,1)S(1)}, u32[]{:S(2)}, u32[]{:S(2)}) collective-permute-start(bf16[8,4096]{1,0:T(8,128)(2,1)S(1)} %get-tuple-element.69), channel_id=1, source_target_pairs={{0,14},{1,15},{2,12},{3,13},{4,10},{5,11},{6,8},{7,9},{8,6},{9,7},... | collective-permute-start | bytes 196616 | tf_op jit(solution)/shard_map/ppermute | solution.py:351
  77.5 6.5 %collective-permute-start.27 = (bf16[8,4096]{1,0:T(8,128)(2,1)S(1)}, bf16[8,4096]{1,0:T(8,128)(2,1)S(1)}, u32[]{:S(2)}, u32[]{:S(2)}) collective-permute-start(bf16[8,4096]{1,0:T(8,128)(2,1)S(1)} %get-tuple-element.70), channel_id=1, source_target_pairs={{0,3},{1,2},{2,1},{3,0},{4,7},{5,6},{6,5},{7,4},{8,11},{9,10},{10,... | collective-permute-start | bytes 196616 | tf_op jit(solution)/shard_map/ppermute | solution.py:351

commit v26 on v25

--- a/solution.py
+++ b/solution.py
@@ -14,7 +14,7 @@
 SCALE = 2.0
 ROWS_STEP = 8
 PREP_STEPS = 4
-GROUPS = 8
+GROUPS = 2
 HELD = 13
 FIRST = 4
 MOST_PERMUTES = 32

time: 88.7 us -> 86.3 us (0.973)
  Pallas kernels: 23 us -> 19.4 us
  starting transfers between devices: 56.2 us -> 57.5 us
    pallas_call x8 -> x2, Pallas kernels: 5.06 us -> 1.51 us  [adapt(): pl.pallas_call(functools.partial(adapt_kernel, count), in_specs=[pl.Block...]
    ppermute x30, starting transfers between devices: 56.2 us -> 57.5 us  [permutes(): lax.ppermute(message, 'owner', [(i, i ^ s) for i in range(owners)])]
  transfers between devices with their start and end apart: 30 -> 30, of which waited for: 3 -> 5; matrix products, arithmetic and copies ran while one was open for 0% -> 0% of each run, Pallas kernels for 17% -> 13%
where the time goes in v26:
time: 86.3 us; the launch traced here: 86.1 us
  starting transfers between devices  57.5 us (67%)
  Pallas kernels  19.4 us (22%)
  waiting for transfers between devices  8.72 us (10%)
    ppermute x30, starting transfers between devices, permutes(): lax.ppermute(message, 'owner', [(i, i ^ s) for i in range(owners)])  57.5 us
    ppermute x30, waiting for transfers between devices, permutes(): lax.ppermute(message, 'owner', [(i, i ^ s) for i in range(owners)])  8.72 us
    pallas_call x2, Pallas kernels, pack(): pl.pallas_call(functools.partial(pack_kernel, which, owners, slot_count,...  8.33 us
    pallas_call x1, Pallas kernels, prep(): pl.pallas_call(functools.partial(prep_kernel, group), grid=(steps,), in_s...  5.14 us
    pallas_call x1, Pallas kernels, attend(): pl.pallas_call(functools.partial(attend_kernel, group, context, len(retur...  4.42 us
  transfers between devices with their start and end apart: 30, of which 5 were waited for; matrix products, arithmetic and copies ran while one was open for 0% of the time, Pallas kernels for 13%

profile of v26, /device:TPU:0, one launch (start us, length us, event | category | flops | bytes accessed | tf_op | source)
XLA Modules:
  0.0 86.1 jit_solution(3844996527456852675)
XLA Ops:
  0.0 3.9 %pack.2 = (bf16[32,128]{1,0:T(8,128)(2,1)}, bf16[8,8320]{1,0:T(8,128)(2,1)}, bf16[8,8320]{1,0:T(8,128)(2,1)}, bf16[8,8320]{1,0:T(8,128)(2,1)}, bf16[8,8320]{1,0:T(8,128)(2,1)}) custom-call(s32[1,32]{1,0:T(1,128)} %bitcast.2, s32[1,128]{1,0:T(1,128)} %bitcast.4, bf16[128,8192]{1,0:T(8,128)(2,1)} %hidden_hbm.3), custom_call_target="tpu_custom_call" | custom-call | tf_op jit(solution)/shard_map/pack/pallas_call | solution.py:96
  3.9 4.1 %collective-permute-start = (bf16[8,8320]{1,0:T(8,128)(2,1)}, bf16[8,8320]{1,0:T(8,128)(2,1)S(1)}, u32[]{:S(2)}, u32[]{:S(2)}) collective-permute-start(bf16[8,8320]{1,0:T(8,128)(2,1)} %get-tuple-element.42), channel_id=1, source_target_pairs={{0,8},{1,9},{2,10},{3,11},{4,12},{5,13},{6,14},{7,15},{8,0},{9,1},... | collective-permute-start | bytes 399368 | tf_op jit(solution)/shard_map/ppermute | solution.py:351
  8.0 1.6 %collective-permute-start.1 = (bf16[8,8320]{1,0:T(8,128)(2,1)}, bf16[8,8320]{1,0:T(8,128)(2,1)S(1)}, u32[]{:S(2)}, u32[]{:S(2)}) collective-permute-start(bf16[8,8320]{1,0:T(8,128)(2,1)} %get-tuple-element.43), channel_id=1, source_target_pairs={{0,4},{1,5},{2,6},{3,7},{4,0},{5,1},{6,2},{7,3},{8,12},{9,13},{10,... | collective-permute-start | bytes 399368 | tf_op jit(solution)/shard_map/ppermute | solution.py:351
  9.5 0.2 collective-permute-start.3
  9.8 4.5 %pack.3 = (bf16[96,128]{1,0:T(8,128)(2,1)}, bf16[8,8320]{1,0:T(8,128)(2,1)}, bf16[8,8320]{1,0:T(8,128)(2,1)}, bf16[8,8320]{1,0:T(8,128)(2,1)}, bf16[8,8320]{1,0:...) custom-call(s32[1,32]{1,0:T(1,128)} %bitcast.3, ...), custom_call_target="tpu_custom_call" | custom-call | tf_op jit(solution)/shard_map/pack/pallas_call | solution.py:96
  14.3 3.8 %collective-permute-start.4 = (bf16[8,8320]{1,0:T(8,128)(2,1)}, bf16[8,8320]{1,0:T(8,128)(2,1)S(1)}, u32[]{:S(2)}, u32[]{:S(2)}) collective-permute-start(bf16[8,8320]{1,0:T(8,128)(2,1)} %get-tuple-element.46), channel_id=1, source_target_pairs={{0,10},{1,11},{2,8},{3,9},{4,14},{5,15},{6,12},{7,13},{8,2},{9,3},... | collective-permute-start | bytes 399368 | tf_op jit(solution)/shard_map/ppermute | solution.py:351
  18.1 1.6 %collective-permute-start.5 = (bf16[8,8320]{1,0:T(8,128)(2,1)}, bf16[8,8320]{1,0:T(8,128)(2,1)S(1)}, u32[]{:S(2)}, u32[]{:S(2)}) collective-permute-start(bf16[8,8320]{1,0:T(8,128)(2,1)} %get-tuple-element.47), channel_id=1, source_target_pairs={{0,6},{1,7},{2,4},{3,5},{4,2},{5,3},{6,0},{7,1},{8,14},{9,15},{10,... | collective-permute-start | bytes 399368 | tf_op jit(solution)/shard_map/ppermute | solution.py:351
  19.7 0.4 collective-permute-start.6
  20.0 2.1 %collective-permute-start.7 = (bf16[8,8320]{1,0:T(8,128)(2,1)}, bf16[8,8320]{1,0:T(8,128)(2,1)S(1)}, u32[]{:S(2)}, u32[]{:S(2)}) collective-permute-start(bf16[8,8320]{1,0:T(8,128)(2,1)} %get-tuple-element.49), channel_id=1, source_target_pairs={{0,7},{1,6},{2,5},{3,4},{4,3},{5,2},{6,1},{7,0},{8,15},{9,14},{10,... | collective-permute-start | bytes 399368 | tf_op jit(solution)/shard_map/ppermute | solution.py:351
  22.2 0.0 collective-permute-done.3.refs_3_
  22.2 2.6 %collective-permute-start.16 = (bf16[8,8320]{1,0:T(8,128)(2,1)}, bf16[8,8320]{1,0:T(8,128)(2,1)S(1)}, u32[]{:S(2)}, u32[]{:S(2)}) collective-permute-start(bf16[8,8320]{1,0:T(8,128)(2,1)} %get-tuple-element.58), channel_id=1, source_target_pairs={{0,12},{1,13},{2,14},{3,15},{4,8},{5,9},{6,10},{7,11},{8,4},{9,5},... | collective-permute-start | bytes 399368 | tf_op jit(solution)/shard_map/ppermute | solution.py:351
  24.8 3.8 %collective-permute-done.4.refs_4_ = bf16[8,8320]{1,0:T(8,128)(2,1)S(1)} collective-permute-done((bf16[8,8320]{1,0:T(8,128)(2,1)}, bf16[8,8320]{1,0:T(8,128)(2,1)S(1)}, u32[]{:S(2)}, u32[]{:S(2)}) %collective-permute-start.4) | collective-permute-done | bytes 133152 | tf_op jit(solution)/shard_map/ppermute | solution.py:351
  28.5 0.1 broadcast_in_dim.7
  28.6 0.1 broadcast_in_dim.8
  28.7 0.1 broadcast_in_dim.9.given_ref
  28.9 5.1 %prep.1 = (bf16[4,128,2048]{2,1,0:T(8,128)(2,1)S(1)}, bf16[4,92,192,128]{3,2,1,0:T(8,128)(2,1)}, s32[16,1,128]{2,1,0:T(1,128)S(1)}) custom-call(bf16[128,4096]{1,0:T(8,128)(2,1)S(1)} %copy-done.2, bf16[128,2,16,512]{3,2,1,0:T(8,128)(2,1)} %kv_ref.1, s32[16,1,128]{2,1,0:T(1,128)S(1)} %broadcast_in_dim.9.given_ref), custom_call_target="tpu_custom_call" | custom-call | tf_op jit(solution)/shard_map/prep/pallas_call | solution.py:184
  34.0 3.3 %collective-permute-start.18 = (bf16[8,8320]{1,0:T(8,128)(2,1)S(1)}, bf16[8,8320]{1,0:T(8,128)(2,1)S(1)}, u32[]{:S(2)}, u32[]{:S(2)}) collective-permute-start(bf16[8,8320]{1,0:T(8,128)(2,1)S(1)} %copy-done.11), channel_id=1, source_target_pairs={{0,13},{1,12},{2,15},{3,14},{4,9},{5,8},{6,11},{7,10},{8,5},{9,4},... | collective-permute-start | bytes 399368 | tf_op jit(solution)/shard_map/ppermute | solution.py:351
  37.3 0.0 collective-permute-done.6.refs_6_
  37.3 0.5 collective-permute-start.19
  37.8 0.0 collective-permute-done.7.refs_7_
  37.9 1.6 %collective-permute-start.20 = (bf16[8,8320]{1,0:T(8,128)(2,1)S(1)}, bf16[8,8320]{1,0:T(8,128)(2,1)S(1)}, u32[]{:S(2)}, u32[]{:S(2)}) collective-permute-start(bf16[8,8320]{1,0:T(8,128)(2,1)S(1)} %copy-done.9), channel_id=1, source_target_pairs={{0,14},{1,15},{2,12},{3,13},{4,10},{5,11},{6,8},{7,9},{8,6},{9,7},... | collective-permute-start | bytes 399368 | tf_op jit(solution)/shard_map/ppermute | solution.py:351
  39.4 2.2 %collective-permute-start.22 = (bf16[8,8320]{1,0:T(8,128)(2,1)S(1)}, bf16[8,8320]{1,0:T(8,128)(2,1)S(1)}, u32[]{:S(2)}, u32[]{:S(2)}) collective-permute-start(bf16[8,8320]{1,0:T(8,128)(2,1)S(1)} %copy-done.8), channel_id=1, source_target_pairs={{0,15},{1,14},{2,13},{3,12},{4,11},{5,10},{6,9},{7,8},{8,7},{9,6},... | collective-permute-start | bytes 399368 | tf_op jit(solution)/shard_map/ppermute | solution.py:351
  41.7 2.2 %collective-permute-start.21 = (bf16[8,8320]{1,0:T(8,128)(2,1)S(1)}, bf16[8,8320]{1,0:T(8,128)(2,1)S(1)}, u32[]{:S(2)}, u32[]{:S(2)}) collective-permute-start(bf16[8,8320]{1,0:T(8,128)(2,1)S(1)} %hold.1), channel_id=1, source_target_pairs={{0,3},{1,2},{2,1},{3,0},{4,7},{5,6},{6,5},{7,4},{8,11},{9,10},{10,... | collective-permute-start | bytes 399368 | tf_op jit(solution)/shard_map/ppermute | solution.py:351
  43.9 0.8 adapt.2
  44.7 6.7 %collective-permute-start.8 = (bf16[8,4096]{1,0:T(8,128)(2,1)S(1)}, bf16[8,4096]{1,0:T(8,128)(2,1)S(1)}, u32[]{:S(2)}, u32[]{:S(2)}) collective-permute-start(bf16[8,4096]{1,0:T(8,128)(2,1)S(1)} %get-tuple-element.50), channel_id=1, source_target_pairs={{0,8},{1,9},{2,10},{3,11},{4,12},{5,13},{6,14},{7,15},{8,0},{9,1},... | collective-permute-start | bytes 196616 | tf_op jit(solution)/shard_map/ppermute | solution.py:351
  51.4 0.0 collective-permute-done.19.refs_3_
  51.4 0.0 collective-permute-start.9
  51.4 0.0 collective-permute-done.20.refs_4_
  51.4 3.4 %collective-permute-start.10 = (bf16[8,4096]{1,0:T(8,128)(2,1)S(1)}, bf16[8,4096]{1,0:T(8,128)(2,1)S(1)}, u32[]{:S(2)}, u32[]{:S(2)}) collective-permute-start(bf16[8,4096]{1,0:T(8,128)(2,1)S(1)} %get-tuple-element.52), channel_id=1, source_target_pairs={{0,9},{1,8},{2,11},{3,10},{4,13},{5,12},{6,15},{7,14},{8,1},{9,0},... | collective-permute-start | bytes 196616 | tf_op jit(solution)/shard_map/ppermute | solution.py:351
  54.8 0.0 collective-permute-done.22.refs_6_
  54.8 4.2 %collective-permute-start.11 = (bf16[8,4096]{1,0:T(8,128)(2,1)S(1)}, bf16[8,4096]{1,0:T(8,128)(2,1)S(1)}, u32[]{:S(2)}, u32[]{:S(2)}) collective-permute-start(bf16[8,4096]{1,0:T(8,128)(2,1)S(1)} %get-tuple-element.53), channel_id=1, source_target_pairs={{0,5},{1,4},{2,7},{3,6},{4,1},{5,0},{6,3},{7,2},{8,13},{9,12},{10,... | collective-permute-start | bytes 196616 | tf_op jit(solution)/shard_map/ppermute | solution.py:351
  59.1 0.4 collective-permute-start.12
  59.4 0.8 adapt.3
  60.2 4.1 %collective-permute-start.13 = (bf16[8,4096]{1,0:T(8,128)(2,1)S(1)}, bf16[8,4096]{1,0:T(8,128)(2,1)S(1)}, u32[]{:S(2)}, u32[]{:S(2)}) collective-permute-start(bf16[8,4096]{1,0:T(8,128)(2,1)S(1)} %get-tuple-element.55), channel_id=1, source_target_pairs={{0,6},{1,7},{2,4},{3,5},{4,2},{5,3},{6,0},{7,1},{8,14},{9,15},{10,... | collective-permute-start | bytes 196616 | tf_op jit(solution)/shard_map/ppermute | solution.py:351
  64.3 2.1 %collective-permute-start.15 = (bf16[8,4096]{1,0:T(8,128)(2,1)S(1)}, bf16[8,4096]{1,0:T(8,128)(2,1)S(1)}, u32[]{:S(2)}, u32[]{:S(2)}) collective-permute-start(bf16[8,4096]{1,0:T(8,128)(2,1)S(1)} %get-tuple-element.57), channel_id=1, source_target_pairs={{0,7},{1,6},{2,5},{3,4},{4,3},{5,2},{6,1},{7,0},{8,15},{9,14},{10,... | collective-permute-start | bytes 196616 | tf_op jit(solution)/shard_map/ppermute | solution.py:351
  66.4 2.9 %collective-permute-start.23 = (bf16[8,4096]{1,0:T(8,128)(2,1)S(1)}, bf16[8,4096]{1,0:T(8,128)(2,1)S(1)}, u32[]{:S(2)}, u32[]{:S(2)}) collective-permute-start(bf16[8,4096]{1,0:T(8,128)(2,1)S(1)} %get-tuple-element.67), channel_id=1, source_target_pairs={{0,12},{1,13},{2,14},{3,15},{4,8},{5,9},{6,10},{7,11},{8,4},{9,5},... | collective-permute-start | bytes 196616 | tf_op jit(solution)/shard_map/ppermute | solution.py:351
  69.3 1.0 %collective-permute-start.25 = (bf16[8,4096]{1,0:T(8,128)(2,1)S(1)}, bf16[8,4096]{1,0:T(8,128)(2,1)S(1)}, u32[]{:S(2)}, u32[]{:S(2)}) collective-permute-start(bf16[8,4096]{1,0:T(8,128)(2,1)S(1)} %get-tuple-element.69), channel_id=1, source_target_pairs={{0,13},{1,12},{2,15},{3,14},{4,9},{5,8},{6,11},{7,10},{8,5},{9,4},... | collective-permute-start | bytes 196616 | tf_op jit(solution)/shard_map/ppermute | solution.py:351
  70.3 1.0 %collective-permute-done.14.refs_6_ = bf16[8,4096]{1,0:T(8,128)(2,1)S(1)} collective-permute-done((bf16[8,4096]{1,0:T(8,128)(2,1)S(1)}, bf16[8,4096]{1,0:T(8,128)(2,1)S(1)}, u32[]{:S(2)}, u32[]{:S(2)}) %collective-permute-start.14) | collective-permute-done | bytes 65568 | tf_op jit(solution)/shard_map/ppermute | solution.py:351
  71.3 0.0 collective-permute-start.26
  71.3 3.4 %collective-permute-start.27 = (bf16[8,4096]{1,0:T(8,128)(2,1)S(1)}, bf16[8,4096]{1,0:T(8,128)(2,1)S(1)}, u32[]{:S(2)}, u32[]{:S(2)}) collective-permute-start(bf16[8,4096]{1,0:T(8,128)(2,1)S(1)} %get-tuple-element.71), channel_id=1, source_target_pairs={{0,14},{1,15},{2,12},{3,13},{4,10},{5,11},{6,8},{7,9},{8,6},{9,7},... | collective-permute-start | bytes 196616 | tf_op jit(solution)/shard_map/ppermute | solution.py:351
  74.7 0.0 collective-permute-done.23.refs_8_
  74.7 0.0 collective-permute-start.28
  74.7 0.0 collective-permute-done.24.refs_9_
  74.7 3.1 %collective-permute-start.29 = (bf16[8,4096]{1,0:T(8,128)(2,1)S(1)}, bf16[8,4096]{1,0:T(8,128)(2,1)S(1)}, u32[]{:S(2)}, u32[]{:S(2)}) collective-permute-start(bf16[8,4096]{1,0:T(8,128)(2,1)S(1)} %get-tuple-element.73), channel_id=1, source_target_pairs={{0,15},{1,14},{2,13},{3,12},{4,11},{5,10},{6,9},{7,8},{8,7},{9,6},... | collective-permute-start | bytes 196616 | tf_op jit(solution)/shard_map/ppermute | solution.py:351
  77.8 0.6 collective-permute-done.27.refs_12_
  78.4 1.3 %collective-permute-done.28.refs_13_ = bf16[8,4096]{1,0:T(8,128)(2,1)S(1)} collective-permute-done((bf16[8,4096]{1,0:T(8,128)(2,1)S(1)}, bf16[8,4096]{1,0:T(8,128)(2,1)S(1)}, u32[]{:S(2)}, u32[]{:S(2)}) %collective-permute-start.28) | collective-permute-done | bytes 65568 | tf_op jit(solution)/shard_map/ppermute | solution.py:351
  79.7 2.0 %collective-permute-done.29.refs_14_ = bf16[8,4096]{1,0:T(8,128)(2,1)S(1)} collective-permute-done((bf16[8,4096]{1,0:T(8,128)(2,1)S(1)}, bf16[8,4096]{1,0:T(8,128)(2,1)S(1)}, u32[]{:S(2)}, u32[]{:S(2)}) %collective-permute-start.29) | collective-permute-done | bytes 65568 | tf_op jit(solution)/shard_map/ppermute | solution.py:351
  81.7 4.4 %attend.1 = bf16[128,4096]{1,0:T(8,128)(2,1)} custom-call(bf16[8,4096]{1,0:T(8,128)(2,1)S(1)} %collective-permute-done.8.refs_0_, bf16[8,4096]{1,0:T(8,128)(2,1)S(1)} %collective-permute-done.9.refs_1_, bf16[8,4096]{1,0:T(8,128)(2,1)S(1)} %collective-permute-done.10.refs_2_, bf16[8,4096]{1,0:T(8,128)(2,1)S(1)} %collective-permute-done.11.refs_3_, ...), custom_call_target="tpu_custom_call" | custom-call | tf_op jit(solution)/shard_map/attend/pallas_call | solution.py:304
  (46 shorter events, 0.1 us)
Async XLA Ops:
  0.0 28.5 %copy-start.7 = (s32[128]{0:T(128)S(1)}, s32[128]{0:T(128)}, u32[]{:S(2)}) copy-start(s32[128]{0:T(128)} %param.11) | copy-start | bytes 1540
  0.0 28.8 %copy-start.2 = (bf16[128,4096]{1,0:T(8,128)(2,1)S(1)}, bf16[128,4096]{1,0:T(8,128)(2,1)}, u32[]{:S(2)}) copy-start(bf16[128,4096]{1,0:T(8,128)(2,1)} %base_ref.1) | copy-start | bytes 3145732
  3.9 14.3 %collective-permute-start = (bf16[8,8320]{1,0:T(8,128)(2,1)}, bf16[8,8320]{1,0:T(8,128)(2,1)S(1)}, u32[]{:S(2)}, u32[]{:S(2)}) collective-permute-start(bf16[8,8320]{1,0:T(8,128)(2,1)} %get-tuple-element.42), channel_id=1, source_target_pairs={{0,8},{1,9},{2,10},{3,11},{4,12},{5,13},{6,14},{7,15},{8,0},{9,1},... | collective-permute-start | bytes 399368 | tf_op jit(solution)/shard_map/ppermute | solution.py:351
  8.0 11.7 %collective-permute-start.1 = (bf16[8,8320]{1,0:T(8,128)(2,1)}, bf16[8,8320]{1,0:T(8,128)(2,1)S(1)}, u32[]{:S(2)}, u32[]{:S(2)}) collective-permute-start(bf16[8,8320]{1,0:T(8,128)(2,1)} %get-tuple-element.43), channel_id=1, source_target_pairs={{0,4},{1,5},{2,6},{3,7},{4,0},{5,1},{6,2},{7,3},{8,12},{9,13},{10,... | collective-permute-start | bytes 399368 | tf_op jit(solution)/shard_map/ppermute | solution.py:351
  9.5 10.5 %collective-permute-start.2 = (bf16[8,8320]{1,0:T(8,128)(2,1)}, bf16[8,8320]{1,0:T(8,128)(2,1)S(1)}, u32[]{:S(2)}, u32[]{:S(2)}) collective-permute-start(bf16[8,8320]{1,0:T(8,128)(2,1)} %get-tuple-element.44), channel_id=1, source_target_pairs={{0,9},{1,8},{2,11},{3,10},{4,13},{5,12},{6,15},{7,14},{8,1},{9,0},... | collective-permute-start | bytes 399368 | tf_op jit(solution)/shard_map/ppermute | solution.py:351
  9.5 12.7 %collective-permute-start.3 = (bf16[8,8320]{1,0:T(8,128)(2,1)}, bf16[8,8320]{1,0:T(8,128)(2,1)S(1)}, u32[]{:S(2)}, u32[]{:S(2)}) collective-permute-start(bf16[8,8320]{1,0:T(8,128)(2,1)} %get-tuple-element.45), channel_id=1, source_target_pairs={{0,5},{1,4},{2,7},{3,6},{4,1},{5,0},{6,3},{7,2},{8,13},{9,12},{10,... | collective-permute-start | bytes 399368 | tf_op jit(solution)/shard_map/ppermute | solution.py:351
  14.3 14.3 %collective-permute-start.4 = (bf16[8,8320]{1,0:T(8,128)(2,1)}, bf16[8,8320]{1,0:T(8,128)(2,1)S(1)}, u32[]{:S(2)}, u32[]{:S(2)}) collective-permute-start(bf16[8,8320]{1,0:T(8,128)(2,1)} %get-tuple-element.46), channel_id=1, source_target_pairs={{0,10},{1,11},{2,8},{3,9},{4,14},{5,15},{6,12},{7,13},{8,2},{9,3},... | collective-permute-start | bytes 399368 | tf_op jit(solution)/shard_map/ppermute | solution.py:351
  18.1 15.9 %collective-permute-start.5 = (bf16[8,8320]{1,0:T(8,128)(2,1)}, bf16[8,8320]{1,0:T(8,128)(2,1)S(1)}, u32[]{:S(2)}, u32[]{:S(2)}) collective-permute-start(bf16[8,8320]{1,0:T(8,128)(2,1)} %get-tuple-element.47), channel_id=1, source_target_pairs={{0,6},{1,7},{2,4},{3,5},{4,2},{5,3},{6,0},{7,1},{8,14},{9,15},{10,... | collective-permute-start | bytes 399368 | tf_op jit(solution)/shard_map/ppermute | solution.py:351
  19.7 17.6 %collective-permute-start.6 = (bf16[8,8320]{1,0:T(8,128)(2,1)}, bf16[8,8320]{1,0:T(8,128)(2,1)S(1)}, u32[]{:S(2)}, u32[]{:S(2)}) collective-permute-start(bf16[8,8320]{1,0:T(8,128)(2,1)} %get-tuple-element.48), channel_id=1, source_target_pairs={{0,11},{1,10},{2,9},{3,8},{4,15},{5,14},{6,13},{7,12},{8,3},{9,2},... | collective-permute-start | bytes 399368 | tf_op jit(solution)/shard_map/ppermute | solution.py:351
  20.0 17.8 %collective-permute-start.7 = (bf16[8,8320]{1,0:T(8,128)(2,1)}, bf16[8,8320]{1,0:T(8,128)(2,1)S(1)}, u32[]{:S(2)}, u32[]{:S(2)}) collective-permute-start(bf16[8,8320]{1,0:T(8,128)(2,1)} %get-tuple-element.49), channel_id=1, source_target_pairs={{0,7},{1,6},{2,5},{3,4},{4,3},{5,2},{6,1},{7,0},{8,15},{9,14},{10,... | collective-permute-start | bytes 399368 | tf_op jit(solution)/shard_map/ppermute | solution.py:351
  22.2 17.2 %collective-permute-start.16 = (bf16[8,8320]{1,0:T(8,128)(2,1)}, bf16[8,8320]{1,0:T(8,128)(2,1)S(1)}, u32[]{:S(2)}, u32[]{:S(2)}) collective-permute-start(bf16[8,8320]{1,0:T(8,128)(2,1)} %get-tuple-element.58), channel_id=1, source_target_pairs={{0,12},{1,13},{2,14},{3,15},{4,8},{5,9},{6,10},{7,11},{8,4},{9,5},... | collective-permute-start | bytes 399368 | tf_op jit(solution)/shard_map/ppermute | solution.py:351
  28.5 13.1 %collective-permute-start.17 = (bf16[8,8320]{1,0:T(8,128)(2,1)}, bf16[8,8320]{1,0:T(8,128)(2,1)S(1)}, u32[]{:S(2)}, u32[]{:S(2)}) collective-permute-start(bf16[8,8320]{1,0:T(8,128)(2,1)} %get-tuple-element.59), channel_id=1, source_target_pairs={{0,1},{1,0},{2,3},{3,2},{4,5},{5,4},{6,7},{7,6},{8,9},{9,8},{10,11... | collective-permute-start | bytes 399368 | tf_op jit(solution)/shard_map/ppermute | solution.py:351
  28.8 5.2 %copy-start.11 = (bf16[8,8320]{1,0:T(8,128)(2,1)S(1)}, bf16[8,8320]{1,0:T(8,128)(2,1)}, u32[]{:S(2)}) copy-start(bf16[8,8320]{1,0:T(8,128)(2,1)} %get-tuple-element.60) | copy-start | bytes 399364
  28.8 8.5 %copy-start.10 = (bf16[8,8320]{1,0:T(8,128)(2,1)S(1)}, bf16[8,8320]{1,0:T(8,128)(2,1)}, u32[]{:S(2)}) copy-start(bf16[8,8320]{1,0:T(8,128)(2,1)} %get-tuple-element.61) | copy-start | bytes 399364
  28.8 9.0 %copy-start.9 = (bf16[8,8320]{1,0:T(8,128)(2,1)S(1)}, bf16[8,8320]{1,0:T(8,128)(2,1)}, u32[]{:S(2)}) copy-start(bf16[8,8320]{1,0:T(8,128)(2,1)} %get-tuple-element.62) | copy-start | bytes 399364
  28.9 10.6 %copy-start.8 = (bf16[8,8320]{1,0:T(8,128)(2,1)S(1)}, bf16[8,8320]{1,0:T(8,128)(2,1)}, u32[]{:S(2)}) copy-start(bf16[8,8320]{1,0:T(8,128)(2,1)} %get-tuple-element.65) | copy-start | bytes 399364
  28.9 12.8 %copy-start.3 = (bf16[8,8320]{1,0:T(8,128)(2,1)S(1)}, bf16[8,8320]{1,0:T(8,128)(2,1)}, u32[]{:S(2)}) copy-start(bf16[8,8320]{1,0:T(8,128)(2,1)} %get-tuple-element.63.refs_0_) | copy-start | bytes 399364
  34.0 10.6 %collective-permute-start.18 = (bf16[8,8320]{1,0:T(8,128)(2,1)S(1)}, bf16[8,8320]{1,0:T(8,128)(2,1)S(1)}, u32[]{:S(2)}, u32[]{:S(2)}) collective-permute-start(bf16[8,8320]{1,0:T(8,128)(2,1)S(1)} %copy-done.11), channel_id=1, source_target_pairs={{0,13},{1,12},{2,15},{3,14},{4,9},{5,8},{6,11},{7,10},{8,5},{9,4},... | collective-permute-start | bytes 399368 | tf_op jit(solution)/shard_map/ppermute | solution.py:351
  37.3 14.1 %collective-permute-start.19 = (bf16[8,8320]{1,0:T(8,128)(2,1)S(1)}, bf16[8,8320]{1,0:T(8,128)(2,1)S(1)}, u32[]{:S(2)}, u32[]{:S(2)}) collective-permute-start(bf16[8,8320]{1,0:T(8,128)(2,1)S(1)} %copy-done.10), channel_id=1, source_target_pairs={{0,2},{1,3},{2,0},{3,1},{4,6},{5,7},{6,4},{7,5},{8,10},{9,11},{10,... | collective-permute-start | bytes 399368 | tf_op jit(solution)/shard_map/ppermute | solution.py:351
  37.9 13.6 %collective-permute-start.20 = (bf16[8,8320]{1,0:T(8,128)(2,1)S(1)}, bf16[8,8320]{1,0:T(8,128)(2,1)S(1)}, u32[]{:S(2)}, u32[]{:S(2)}) collective-permute-start(bf16[8,8320]{1,0:T(8,128)(2,1)S(1)} %copy-done.9), channel_id=1, source_target_pairs={{0,14},{1,15},{2,12},{3,13},{4,10},{5,11},{6,8},{7,9},{8,6},{9,7},... | collective-permute-start | bytes 399368 | tf_op jit(solution)/shard_map/ppermute | solution.py:351
  39.4 15.4 %collective-permute-start.22 = (bf16[8,8320]{1,0:T(8,128)(2,1)S(1)}, bf16[8,8320]{1,0:T(8,128)(2,1)S(1)}, u32[]{:S(2)}, u32[]{:S(2)}) collective-permute-start(bf16[8,8320]{1,0:T(8,128)(2,1)S(1)} %copy-done.8), channel_id=1, source_target_pairs={{0,15},{1,14},{2,13},{3,12},{4,11},{5,10},{6,9},{7,8},{8,7},{9,6},... | collective-permute-start | bytes 399368 | tf_op jit(solution)/shard_map/ppermute | solution.py:351
  41.6 2.2 %copy-start = (bf16[8192,128]{1,0:T(8,128)(2,1)S(1)}, bf16[8192,128]{1,0:T(8,128)(2,1)}, u32[]{:S(2)}) copy-start(bf16[8192,128]{1,0:T(8,128)(2,1)} %refs_8_.3) | copy-start | bytes 6291460
  41.6 2.2 %copy-start.1 = (bf16[128,4096]{1,0:T(8,128)(2,1)S(1)}, bf16[128,4096]{1,0:T(8,128)(2,1)}, u32[]{:S(2)}) copy-start(bf16[128,4096]{1,0:T(8,128)(2,1)} %refs_9_.3) | copy-start | bytes 3145732
  41.6 17.8 %copy-start.4 = (bf16[8,8320]{1,0:T(8,128)(2,1)S(1)}, bf16[8,8320]{1,0:T(8,128)(2,1)}, u32[]{:S(2)}) copy-start(bf16[8,8320]{1,0:T(8,128)(2,1)} %get-tuple-element.66.refs_7_) | copy-start | bytes 399364
  41.7 17.4 %collective-permute-start.21 = (bf16[8,8320]{1,0:T(8,128)(2,1)S(1)}, bf16[8,8320]{1,0:T(8,128)(2,1)S(1)}, u32[]{:S(2)}, u32[]{:S(2)}) collective-permute-start(bf16[8,8320]{1,0:T(8,128)(2,1)S(1)} %hold.1), channel_id=1, source_target_pairs={{0,3},{1,2},{2,1},{3,0},{4,7},{5,6},{6,5},{7,4},{8,11},{9,10},{10,... | collective-permute-start | bytes 399368 | tf_op jit(solution)/shard_map/ppermute | solution.py:351
  44.7 15.5 %collective-permute-start.8 = (bf16[8,4096]{1,0:T(8,128)(2,1)S(1)}, bf16[8,4096]{1,0:T(8,128)(2,1)S(1)}, u32[]{:S(2)}, u32[]{:S(2)}) collective-permute-start(bf16[8,4096]{1,0:T(8,128)(2,1)S(1)} %get-tuple-element.50), channel_id=1, source_target_pairs={{0,8},{1,9},{2,10},{3,11},{4,12},{5,13},{6,14},{7,15},{8,0},{9,1},... | collective-permute-start | bytes 196616 | tf_op jit(solution)/shard_map/ppermute | solution.py:351
  51.4 12.9 %collective-permute-start.9 = (bf16[8,4096]{1,0:T(8,128)(2,1)S(1)}, bf16[8,4096]{1,0:T(8,128)(2,1)S(1)}, u32[]{:S(2)}, u32[]{:S(2)}) collective-permute-start(bf16[8,4096]{1,0:T(8,128)(2,1)S(1)} %get-tuple-element.51), channel_id=1, source_target_pairs={{0,4},{1,5},{2,6},{3,7},{4,0},{5,1},{6,2},{7,3},{8,12},{9,13},{10,... | collective-permute-start | bytes 196616 | tf_op jit(solution)/shard_map/ppermute | solution.py:351
  51.4 12.9 %collective-permute-start.10 = (bf16[8,4096]{1,0:T(8,128)(2,1)S(1)}, bf16[8,4096]{1,0:T(8,128)(2,1)S(1)}, u32[]{:S(2)}, u32[]{:S(2)}) collective-permute-start(bf16[8,4096]{1,0:T(8,128)(2,1)S(1)} %get-tuple-element.52), channel_id=1, source_target_pairs={{0,9},{1,8},{2,11},{3,10},{4,13},{5,12},{6,15},{7,14},{8,1},{9,0},... | collective-permute-start | bytes 196616 | tf_op jit(solution)/shard_map/ppermute | solution.py:351
  54.8 11.5 %collective-permute-start.11 = (bf16[8,4096]{1,0:T(8,128)(2,1)S(1)}, bf16[8,4096]{1,0:T(8,128)(2,1)S(1)}, u32[]{:S(2)}, u32[]{:S(2)}) collective-permute-start(bf16[8,4096]{1,0:T(8,128)(2,1)S(1)} %get-tuple-element.53), channel_id=1, source_target_pairs={{0,5},{1,4},{2,7},{3,6},{4,1},{5,0},{6,3},{7,2},{8,13},{9,12},{10,... | collective-permute-start | bytes 196616 | tf_op jit(solution)/shard_map/ppermute | solution.py:351
  59.1 10.2 %collective-permute-start.12 = (bf16[8,4096]{1,0:T(8,128)(2,1)S(1)}, bf16[8,4096]{1,0:T(8,128)(2,1)S(1)}, u32[]{:S(2)}, u32[]{:S(2)}) collective-permute-start(bf16[8,4096]{1,0:T(8,128)(2,1)S(1)} %get-tuple-element.54), channel_id=1, source_target_pairs={{0,10},{1,11},{2,8},{3,9},{4,14},{5,15},{6,12},{7,13},{8,2},{9,3},... | collective-permute-start | bytes 196616 | tf_op jit(solution)/shard_map/ppermute | solution.py:351
  59.4 22.3 %copy-start.5 = (bf16[96,128]{1,0:T(8,128)(2,1)S(1)}, bf16[96,128]{1,0:T(8,128)(2,1)}, u32[]{:S(2)}) copy-start(bf16[96,128]{1,0:T(8,128)(2,1)} %get-tuple-element.76.refs_17_) | copy-start | bytes 73732
  59.4 22.3 %copy-start.6 = (bf16[32,128]{1,0:T(8,128)(2,1)S(1)}, bf16[32,128]{1,0:T(8,128)(2,1)}, u32[]{:S(2)}) copy-start(bf16[32,128]{1,0:T(8,128)(2,1)} %get-tuple-element.75.refs_16_) | copy-start | bytes 24580
  60.2 9.1 %collective-permute-start.13 = (bf16[8,4096]{1,0:T(8,128)(2,1)S(1)}, bf16[8,4096]{1,0:T(8,128)(2,1)S(1)}, u32[]{:S(2)}, u32[]{:S(2)}) collective-permute-start(bf16[8,4096]{1,0:T(8,128)(2,1)S(1)} %get-tuple-element.55), channel_id=1, source_target_pairs={{0,6},{1,7},{2,4},{3,5},{4,2},{5,3},{6,0},{7,1},{8,14},{9,15},{10,... | collective-permute-start | bytes 196616 | tf_op jit(solution)/shard_map/ppermute | solution.py:351
  64.3 7.1 %collective-permute-start.14 = (bf16[8,4096]{1,0:T(8,128)(2,1)S(1)}, bf16[8,4096]{1,0:T(8,128)(2,1)S(1)}, u32[]{:S(2)}, u32[]{:S(2)}) collective-permute-start(bf16[8,4096]{1,0:T(8,128)(2,1)S(1)} %get-tuple-element.56), channel_id=1, source_target_pairs={{0,11},{1,10},{2,9},{3,8},{4,15},{5,14},{6,13},{7,12},{8,3},{9,2},... | collective-permute-start | bytes 196616 | tf_op jit(solution)/shard_map/ppermute | solution.py:351
  64.3 7.1 %collective-permute-start.15 = (bf16[8,4096]{1,0:T(8,128)(2,1)S(1)}, bf16[8,4096]{1,0:T(8,128)(2,1)S(1)}, u32[]{:S(2)}, u32[]{:S(2)}) collective-permute-start(bf16[8,4096]{1,0:T(8,128)(2,1)S(1)} %get-tuple-element.57), channel_id=1, source_target_pairs={{0,7},{1,6},{2,5},{3,4},{4,3},{5,2},{6,1},{7,0},{8,15},{9,14},{10,... | collective-permute-start | bytes 196616 | tf_op jit(solution)/shard_map/ppermute | solution.py:351
  66.4 8.3 %collective-permute-start.23 = (bf16[8,4096]{1,0:T(8,128)(2,1)S(1)}, bf16[8,4096]{1,0:T(8,128)(2,1)S(1)}, u32[]{:S(2)}, u32[]{:S(2)}) collective-permute-start(bf16[8,4096]{1,0:T(8,128)(2,1)S(1)} %get-tuple-element.67), channel_id=1, source_target_pairs={{0,12},{1,13},{2,14},{3,15},{4,8},{5,9},{6,10},{7,11},{8,4},{9,5},... | collective-permute-start | bytes 196616 | tf_op jit(solution)/shard_map/ppermute | solution.py:351
  69.3 5.4 %collective-permute-start.24 = (bf16[8,4096]{1,0:T(8,128)(2,1)S(1)}, bf16[8,4096]{1,0:T(8,128)(2,1)S(1)}, u32[]{:S(2)}, u32[]{:S(2)}) collective-permute-start(bf16[8,4096]{1,0:T(8,128)(2,1)S(1)} %get-tuple-element.68), channel_id=1, source_target_pairs={{0,1},{1,0},{2,3},{3,2},{4,5},{5,4},{6,7},{7,6},{8,9},{9,8},{10,11... | collective-permute-start | bytes 196616 | tf_op jit(solution)/shard_map/ppermute | solution.py:351
  69.3 8.5 %collective-permute-start.25 = (bf16[8,4096]{1,0:T(8,128)(2,1)S(1)}, bf16[8,4096]{1,0:T(8,128)(2,1)S(1)}, u32[]{:S(2)}, u32[]{:S(2)}) collective-permute-start(bf16[8,4096]{1,0:T(8,128)(2,1)S(1)} %get-tuple-element.69), channel_id=1, source_target_pairs={{0,13},{1,12},{2,15},{3,14},{4,9},{5,8},{6,11},{7,10},{8,5},{9,4},... | collective-permute-start | bytes 196616 | tf_op jit(solution)/shard_map/ppermute | solution.py:351
  71.3 6.5 %collective-permute-start.26 = (bf16[8,4096]{1,0:T(8,128)(2,1)S(1)}, bf16[8,4096]{1,0:T(8,128)(2,1)S(1)}, u32[]{:S(2)}, u32[]{:S(2)}) collective-permute-start(bf16[8,4096]{1,0:T(8,128)(2,1)S(1)} %get-tuple-element.70), channel_id=1, source_target_pairs={{0,2},{1,3},{2,0},{3,1},{4,6},{5,7},{6,4},{7,5},{8,10},{9,11},{10,... | collective-permute-start | bytes 196616 | tf_op jit(solution)/shard_map/ppermute | solution.py:351
  71.3 7.0 %collective-permute-start.27 = (bf16[8,4096]{1,0:T(8,128)(2,1)S(1)}, bf16[8,4096]{1,0:T(8,128)(2,1)S(1)}, u32[]{:S(2)}, u32[]{:S(2)}) collective-permute-start(bf16[8,4096]{1,0:T(8,128)(2,1)S(1)} %get-tuple-element.71), channel_id=1, source_target_pairs={{0,14},{1,15},{2,12},{3,13},{4,10},{5,11},{6,8},{7,9},{8,6},{9,7},... | collective-permute-start | bytes 196616 | tf_op jit(solution)/shard_map/ppermute | solution.py:351
  74.7 4.9 %collective-permute-start.28 = (bf16[8,4096]{1,0:T(8,128)(2,1)S(1)}, bf16[8,4096]{1,0:T(8,128)(2,1)S(1)}, u32[]{:S(2)}, u32[]{:S(2)}) collective-permute-start(bf16[8,4096]{1,0:T(8,128)(2,1)S(1)} %get-tuple-element.72), channel_id=1, source_target_pairs={{0,3},{1,2},{2,1},{3,0},{4,7},{5,6},{6,5},{7,4},{8,11},{9,10},{10,... | collective-permute-start | bytes 196616 | tf_op jit(solution)/shard_map/ppermute | solution.py:351
  74.7 7.0 %collective-permute-start.29 = (bf16[8,4096]{1,0:T(8,128)(2,1)S(1)}, bf16[8,4096]{1,0:T(8,128)(2,1)S(1)}, u32[]{:S(2)}, u32[]{:S(2)}) collective-permute-start(bf16[8,4096]{1,0:T(8,128)(2,1)S(1)} %get-tuple-element.73), channel_id=1, source_target_pairs={{0,15},{1,14},{2,13},{3,12},{4,11},{5,10},{6,9},{7,8},{8,7},{9,6},... | collective-permute-start | bytes 196616 | tf_op jit(solution)/shard_map/ppermute | solution.py:351
